TPU v7x, 32 devices: a whole 2x2x4 slice. The times are simulated.
32 devices in a mesh: groups: 2 (over y), blk: 16 (over z, x, core).
Axes of the slice: x: 2, y: 2, z: 4, core: 2. Of those that a mesh axis runs over, the one named last changes fastest.
Arguments:
- activations: bfloat16 [6144, 8192], P(('groups', 'blk')), parts along dimension 0, may hold values from -6 to 6
- cotangent: bfloat16 [6144, 1024], P(('groups', 'blk')), parts along dimension 0, may hold values from -1.5 to 1.5
- token_layout_row: int32 [6144], P(('groups', 'blk')), parts along dimension 0, may hold values from 0 to 6143, as said below
- tenant_first_row: int32 [64], P('groups'), parts along dimension 0, may hold values from 0 to 6016, as said below
- frozen_value_weight: bfloat16 [8192, 1024], P('blk'), may hold values from -0.1875 to 0.1875
- adapter_down_maps: bfloat16 [96, 16, 8192], P(('groups', 'blk')), parts along dimension 0, may hold values from -0.0625 to 0.0625
- adapter_up_maps: bfloat16 [96, 16, 1024], P(('groups', 'blk')), parts along dimension 0, may hold values from -0.59765625 to 0.59765625
Outputs:
- layout_input_gradient: bfloat16 [12288, 8192], P(('groups', 'blk')), parts along dimension 0
- down_map_gradient: float32 [96, 16, 8192], P(('groups', 'blk')), parts along dimension 0
- up_map_gradient: float32 [96, 16, 1024], P(('groups', 'blk')), parts along dimension 0
There are 2 independent parts, one for each index of `groups`. A program takes and returns all parts, laid end to end along the dimension named above; an argument that names none is the same for every part. Nothing has to cross between parts.
Inputs may be any that keep to these rules, and one draw needn't show every extreme that they name: `token_layout_row`: distinct rows. Each token lies in a block of its tenant, and a tenant's tokens fill its rows in order from its first row, so only its last block has empty rows. Of the tokens of one device at most 24 lie in the 384 rows of any one device, and some device receives exactly 24 from every device. `tenant_first_row`: distinct multiples of 128, rising with the tenant id around the closed order of blocks. Every tenant has one block or more. The blocks of one tenant lie on at most 5 consecutive devices counted cyclically, and some tenant's lie on exactly that many.
All inputs are finite; a program needn't handle non-finite values.
Results may differ from a plain program's by a relative error of at most 0.0029.
Values may be sent and summed in bfloat16 or wider, within the bound.
No kernel may reach another device: no remote copies, remote signals or barrier semaphores. Data moves between devices by JAX's collectives and lax.ppermute only.
A program may use at most 128 MiB of HBM per device.

v0:
```python
import jax
import jax.numpy as jnp
from jax import lax
from jax.sharding import PartitionSpec as P

BLOCK = 128
HOPS = 4
LANES = 128

adapter_scale = 2.0


def moved(value, steps):
    count = lax.axis_size("blk")
    return lax.ppermute(value, "blk", [(i, (i + steps) % count) for i in range(count)])


def dot(a, b, dims, precision=None):
    return lax.dot_general(
        a, b, (dims, ((), ())), preferred_element_type=jnp.float32, precision=precision
    )


def starts_of(blocks, start_ids):
    latest = jnp.max(
        jnp.where(start_ids[None, :] <= blocks[:, None], start_ids[None, :], -1), axis=1
    )
    return jnp.where(latest >= 0, latest, jnp.max(start_ids))


def folded(wide, rank):
    total = wide[:, :LANES]
    for k in range(LANES, wide.shape[1], LANES):
        total = total + wide[:, k : k + LANES]
    fold = jnp.arange(LANES)[:, None] % rank == jnp.arange(rank)[None, :]
    return dot(total, fold.astype(jnp.float32), ((1,), (0,)), lax.Precision.HIGHEST)


def spread(narrow, slot, width):
    rank = narrow.shape[1]
    columns = jnp.arange(width, dtype=jnp.int32)
    tiles = (columns[None, :] % rank == jnp.arange(rank)[:, None]).astype(jnp.bfloat16)
    wide = dot(narrow, tiles, ((1,), (0,)))
    return jnp.where(columns[None, :] // rank == slot[:, None], wide, 0.0).astype(jnp.bfloat16)


def chosen(wide, slot, rank):
    columns = jnp.arange(wide.shape[1], dtype=jnp.int32)
    return folded(jnp.where(columns[None, :] // rank == slot[:, None], wide, 0.0), rank)


def feature_share(act, maps, grad_in, slot):
    rank = grad_in.shape[1]
    rows, width = act.shape[0], maps.shape[0]
    limit = max(8, (24 << 20) // (6 * width))
    pieces = 1
    while rows // pieces > limit or rows % pieces:
        pieces += 1

    def part(act, grad_in, slot):
        hidden = chosen(dot(act, maps, ((1,), (1,))), slot, rank)
        return hidden, dot(spread(grad_in, slot, width), act, ((0,), (0,)))

    if pieces == 1:
        return part(act, grad_in, slot)

    def step(total, xs):
        hidden, down = part(*xs)
        return total + down, hidden

    total, hidden = lax.scan(
        step,
        jnp.zeros((width, act.shape[1]), jnp.float32),
        (
            act.reshape(pieces, rows // pieces, -1),
            grad_in.reshape(pieces, rows // pieces, -1),
            slot.reshape(pieces, rows // pieces),
        ),
    )
    return hidden.reshape(rows, rank), total


def local(
    activations,
    cotangent,
    token_layout_row,
    tenant_first_row,
    frozen_value_weight,
    adapter_down_maps,
    adapter_up_maps,
):
    devices = lax.axis_size("blk")
    device = lax.axis_index("blk")
    tokens = activations.shape[0]
    resident, rank, width = adapter_down_maps.shape
    out_width = cotangent.shape[1]
    resident_rows = resident * BLOCK
    slots = resident * devices
    slot_cap = resident_rows // devices
    start_ids = tenant_first_row // BLOCK

    weight = lax.all_gather(frozen_value_weight, "blk", axis=0, tiled=True)
    rows_all = lax.all_gather(token_layout_row, "blk", axis=0, tiled=True)
    up_all = lax.all_gather(adapter_up_maps, "blk", axis=0, tiled=True)
    up_all = up_all.reshape(slots * rank, out_width)
    act_f = lax.all_to_all(activations, "blk", split_axis=1, concat_axis=0, tiled=True)
    down_flat = adapter_down_maps.reshape(resident * rank, width)
    maps_f = lax.all_to_all(down_flat, "blk", split_axis=1, concat_axis=0, tiled=True)

    target = token_layout_row // resident_rows
    order = jnp.arange(tokens, dtype=jnp.int32)
    before = (target[:, None] == target[None, :]) & (order[None, :] < order[:, None])
    slot = target * slot_cap + jnp.sum(before.astype(jnp.int32), axis=1)
    places = jnp.arange(resident_rows, dtype=jnp.int32)
    send = (places[:, None] == slot[None, :]).astype(jnp.bfloat16)
    send_cot = dot(send, cotangent, ((1,), (0,))).astype(jnp.bfloat16)
    recv_cot = lax.all_to_all(send_cot, "blk", split_axis=0, concat_axis=0, tiled=True)

    first_row = device * resident_rows
    row_of = (rows_all[None, :] - first_row == places[:, None]).astype(jnp.bfloat16)
    mine = (rows_all // resident_rows == device).reshape(devices, tokens)
    earlier = (order[:, None] < order[None, :]).astype(jnp.bfloat16)
    place = dot(mine.astype(jnp.bfloat16), earlier, ((1,), (0,))).astype(jnp.int32)
    place = place + slot_cap * jnp.arange(devices, dtype=jnp.int32)[:, None]
    place = jnp.where(mine, place, -1).reshape(-1)
    place_of = (place[:, None] == places[None, :]).astype(jnp.bfloat16)
    arrange = dot(row_of, place_of, ((1,), (0,))).astype(jnp.bfloat16)
    cot_rows = dot(arrange, recv_cot, ((1,), (0,))).astype(jnp.bfloat16)

    own_slot = starts_of(token_layout_row // BLOCK, start_ids)
    all_up = dot(cotangent, up_all, ((1,), (1,)))
    grad_in = chosen(all_up, own_slot, rank).astype(jnp.bfloat16)
    grad_all = lax.all_gather(grad_in, "blk", axis=0, tiled=True)

    slot_all = starts_of(rows_all // BLOCK, start_ids)
    hidden, down_f = feature_share(act_f, maps_f, grad_all, slot_all)
    down_home = lax.all_to_all(
        (adapter_scale * down_f).astype(jnp.bfloat16), "blk", split_axis=0, concat_axis=1, tiled=True
    )
    down_map_gradient = down_home.astype(jnp.float32).reshape(resident, rank, width)
    hidden = lax.psum(hidden, "blk").astype(jnp.bfloat16)

    first_block = device * resident
    block_numbers = first_block + jnp.arange(resident, dtype=jnp.int32)
    begin = starts_of(block_numbers, start_ids)
    is_local = (begin >= first_block) & (begin <= block_numbers)
    home_slot = jnp.clip(begin - first_block, 0, resident - 1)
    last_map = lax.dynamic_index_in_dim(
        adapter_down_maps, home_slot[resident - 1], 0, keepdims=False
    )
    carried = jnp.zeros_like(last_map)
    for step in range(1, HOPS + 1):
        home = (device - step) % devices
        carried = jnp.where(begin[0] // resident == home, moved(last_map, step), carried)

    grad_rows = dot(row_of, grad_all, ((1,), (0,))).astype(jnp.bfloat16)
    hidden_rows = dot(row_of, hidden, ((1,), (0,))).astype(jnp.bfloat16)
    adapter_rows = []
    up_parts = []
    for b in range(resident):
        rows = slice(b * BLOCK, (b + 1) * BLOCK)
        down = carried
        for k in range(b + 1):
            down = jnp.where(is_local[b] & (home_slot[b] == k), adapter_down_maps[k], down)
        adapter_rows.append(
            (adapter_scale * dot(grad_rows[rows], down, ((1,), (0,)))).astype(jnp.bfloat16)
        )
        up_parts.append(dot(hidden_rows[rows], cot_rows[rows], ((0,), (0,))))
    adapter_rows = jnp.concatenate(adapter_rows, axis=0)

    tail = sum(jnp.where(is_local[b], 0.0, up_parts[b]) for b in range(resident))
    far = jnp.zeros_like(tail)
    for step in range(1, HOPS + 1):
        other = (device + step) % devices * resident
        theirs = starts_of(other[None], start_ids)[0]
        far = far + jnp.where(theirs // resident == device, moved(tail, -step), 0.0)
    up_grads = []
    for k in range(resident):
        total = jnp.where(begin[resident - 1] == first_block + k, far, 0.0)
        for b in range(resident):
            total = total + jnp.where(is_local[b] & (home_slot[b] == k), up_parts[b], 0.0)
        up_grads.append(adapter_scale * total)
    up_map_gradient = jnp.stack(up_grads)

    frozen_rows = dot(cot_rows, weight, ((1,), (1,)))
    layout_input_gradient = (frozen_rows + adapter_rows.astype(jnp.float32)).astype(jnp.bfloat16)
    return (layout_input_gradient, down_map_gradient, up_map_gradient)


def solution(mesh):
    return jax.shard_map(
        local,
        mesh=mesh,
        in_specs=(
            P(("groups", "blk"), None),
            P(("groups", "blk"), None),
            P(("groups", "blk")),
            P("groups"),
            P("blk", None),
            P(("groups", "blk"), None, None),
            P(("groups", "blk"), None, None),
        ),
        out_specs=(
            P(("groups", "blk"), None),
            P(("groups", "blk"), None, None),
            P(("groups", "blk"), None, None),
        ),
        check_vma=False,
    )
```

profile of v0, /device:TPU:1, one launch (start us, length us, event | category | flops | bytes accessed | tf_op | source)
XLA Modules:
  0.0 408.7 jit_solution(8491164162914742561)
XLA Ops:
  7.2 0.7 all-gather.6.cloned.1.call-update
  8.0 0.7 all-gather.4.cloned.1.call-update
  8.7 0.7 and_select_fusion.1
  9.6 1.2 convolution_convert_fusion
  10.8 7.3 %all-to-all-start = ((bf16[16,24,1024]{2,1,0:T(8,128)(2,1)}), bf16[16,24,1024]{2,1,0:T(8,128)(2,1)}, u32[]{:S(2)}, u32[]{:S(2)}) async-start(bf16[16,24,1024]{2,1,0:T(8,128)(2,1)} %bitcast.95), calls=%async_computation | async-start | bytes 1572864 | tf_op jit(solution)/shard_map/all_to_all | solution.py:117
  18.2 2.0 copy.28
  20.2 0.8 fusion.63
  21.1 0.6 compare_and_fusion
  21.7 18.3 %all-to-all-done = bf16[16,24,1024]{2,1,0:T(8,128)(2,1)} async-done(((bf16[16,24,1024]{2,1,0:T(8,128)(2,1)}), bf16[16,24,1024]{2,1,0:T(8,128)(2,1)}, u32[]{:S(2)}, u32[]{:S(2)}) %all-to-all-start) | async-done | bytes 786464 | tf_op jit(solution)/shard_map/all_to_all | solution.py:117
  40.0 5.8 %all-to-all-start.1 = ((bf16[192,16,512]{2,0,1:T(8,128)(2,1)}), bf16[192,16,512]{2,0,1:T(8,128)(2,1)}, u32[]{:S(2)}, u32[]{:S(2)}) async-start(bf16[192,16,512]{2,0,1:T(8,128)(2,1)} %bitcast.91), calls=%async_computation.1 | async-start | bytes 6291456 | tf_op jit(solution)/shard_map/all_to_all | solution.py:106
  45.8 0.7 fusion.69
  48.3 1.4 collective-permute-start
  49.8 1.7 collective-permute-start.1
  51.5 1.2 collective-permute-start.2
  52.7 1.2 collective-permute-start.3
  53.9 0.6 dynamic-slice
  55.1 0.3 dynamic-update-slice
  55.4 164.2 %all-reduce = s32[3072]{0:T(1024)S(1)} all-reduce(s32[3072]{0:T(1024)S(1)} %dynamic-update-slice), channel_id=1, replica_groups=mesh['groups'=2,'blk'=16] {'blk'}, use_global_device_ids=true, to_apply=%add | all-reduce | flops 3072 | bytes 24576
  219.8 0.6 fusion.68
  220.4 0.6 fusion.70
  221.2 0.6 compare_select_fusion.3
  240.0 1.3 copy.24
  246.1 0.6 compare_select_fusion.2
  246.8 3.1 convolution_convert_fusion.1
  249.9 2.1 convolution_select_fusion
  252.3 25.4 %all-gather = bf16[16,192,16]{1,2,0:T(8,128)(2,1)S(1)} all-gather(bf16[1,192,16]{1,2,0:T(8,128)(2,1)S(1)} %fusion.19), channel_id=1, replica_groups=mesh['groups'=2,'blk'=16] {'blk'}, dimensions={0}, use_global_device_ids=true | all-gather | bytes 104448 | tf_op jit(solution)/shard_map/all_gather | solution.py:133
  277.9 3.7 all-to-all-start.3
  281.6 0.8 fusion.15
  282.5 2.1 fusion
  284.6 2.1 fusion.1
  286.6 8.8 %multiply_convert_fusion = bf16[768,512]{1,0:T(8,128)(2,1)} fusion(bf16[3072,512]{1,0:T(8,128)(2,1)} %bitcast.19, bf16[3072,16]{0,1:T(8,128)(2,1)S(1)} %reshape.215, s32[768]{0:T(1024)S(1)} %add_select_fusion.2, s32[3072]{0:T(1024)S(1)} %compare_select_fusion.2, s32[768]{0:T(1024)S(1)} %fusion.50), kind=kOutput, calls=%fused_computation.29 | convolution fusion | flops 2499293184 | bytes 4048896 | tf_op jit(solution)/shard_map/dot_general | solution.py:19
  295.4 4.7 %all-to-all-done.3 = bf16[48,16,512]{2,0,1:T(8,128)(2,1)S(1)} async-done(((bf16[48,16,512]{2,0,1:T(8,128)(2,1)}), bf16[48,16,512]{2,0,1:T(8,128)(2,1)S(1)}, u32[]{:S(2)}, u32[]{:S(2)}) %all-to-all-start.3) | async-done | bytes 786464 | tf_op jit(solution)/shard_map/all_to_all | solution.py:108
  300.1 0.9 copy-done.4
  301.0 5.6 %all-to-all-start.2 = ((bf16[16,48,512]{2,1,0:T(8,128)(2,1)}), bf16[16,48,512]{2,1,0:T(8,128)(2,1)S(1)}, u32[]{:S(2)}, u32[]{:S(2)}) async-start(bf16[16,48,512]{2,1,0:T(8,128)(2,1)} %bitcast.97), calls=%async_computation.2 | async-start | bytes 1572864 | tf_op jit(solution)/shard_map/all_to_all | solution.py:137
  306.6 4.7 %compare_select_fusion = f32[3072,768]{1,0:T(8,128)S(1)} fusion(bf16[3072,512]{1,0:T(8,128)(2,1)} %bitcast.19, bf16[768,512]{1,0:T(8,128)(2,1)} %bitcast.98, s32[768]{0:T(1024)S(1)} %add_select_fusion.2, s32[3072]{0:T(1024)S(1)} %compare_select_fusion.2), kind=kOutput, calls=%fused_computation.1 | convolution fusion | flops 2420637696 | bytes 13384704 | tf_op jit(solution)/shard_map/dot_general | solution.py:19
  311.3 1.1 fusion.12
  312.4 59.6 %all-reduce.2 = bf16[3072,16]{0,1:T(8,128)(2,1)S(1)} all-reduce(f32[3072,16]{0,1:T(8,128)S(1)} %fusion.12), channel_id=1, replica_groups=mesh['groups'=2,'blk'=16] {'blk'}, use_global_device_ids=true, to_apply=%region_6.7 | all-reduce | flops 49152 | bytes 294912 | tf_op jit(solution)/shard_map/psum | solution.py:141
  372.0 0.8 fusion.16
  373.2 2.0 select_add_fusion.1
  375.4 4.3 %collective-permute-start.6 = (f32[16,1024]{1,0:T(8,128)S(1)}, f32[16,1024]{1,0:T(8,128)S(1)}, u32[]{:S(2)}, u32[]{:S(2)}) collective-permute-start(f32[16,1024]{1,0:T(8,128)S(1)} %get-tuple-element.27), channel_id=1, source_target_pairs={{0,13},{1,14},{2,15},{3,0},{4,1},{5,2},{6,3},{7,4},{8,5},{9,6},{10... | collective-permute-start | bytes 196616 | tf_op jit(solution)/shard_map/ppermute | solution.py:15
  379.7 0.3 collective-permute-start.5
  380.0 0.8 collective-permute-start.4
  380.8 2.1 fusion.2
  382.9 2.5 collective-permute-done.6
  385.7 0.7 pad_maximum_fusion
  386.6 0.9 copy.23
  387.5 1.4 reshape.210
  389.0 12.9 %add_convert_fusion = bf16[384,8192]{1,0:T(8,128)(2,1)} fusion(bf16[384,1024]{1,0:T(8,128)(2,1)S(1)} %convolution_convert_fusion.1, bf16[8192,1024]{1,0:T(8,128)(2,1)} %all-gather.4.cloned.1.call-done, bf16[128,8192]{1,0:T(8,128)(2,1)} %fusion.2, bf16[128,8192]{1,0:T(8,128)(2,1)} %fusion.1, bf16[128,8192]{1,0:T(8,128)(2,1)} %fusion), kind=kOutput, calls=%fused_computation | convolution fusion | flops 6467616768 | bytes 30146560 | tf_op jit(solution)/shard_map/dot_general | solution.py:19
  (57 shorter events, 2.9 us)
Async XLA Ops:
  7.2 2.4 copy-start
  7.2 11.0 %copy-start.3 = (bf16[192,8192]{1,0:T(8,128)(2,1)S(1)}, bf16[192,8192]{1,0:T(8,128)(2,1)}, u32[]{:S(2)}) copy-start(bf16[192,8192]{1,0:T(8,128)(2,1)} %param.7) | copy-start | bytes 9437188
  7.2 242.7 %all-gather.6.cloned.1.call-start = ((), (), s32[]{:S(2)}) async-start(), calls=%async_computation.5 | async-start | bytes 1671168 | tf_op jit(solution)/shard_map/all_gather | solution.py:104
  7.9 381.0 %all-gather.4.cloned.1.call-start = ((), (), s32[]{:S(2)}) async-start(), calls=%async_computation.4 | async-start | bytes 17825792 | tf_op jit(solution)/shard_map/all_gather | solution.py:102
  10.8 29.1 %all-to-all-start = ((bf16[16,24,1024]{2,1,0:T(8,128)(2,1)}), bf16[16,24,1024]{2,1,0:T(8,128)(2,1)}, u32[]{:S(2)}, u32[]{:S(2)}) async-start(bf16[16,24,1024]{2,1,0:T(8,128)(2,1)} %bitcast.95), calls=%async_computation | async-start | bytes 1572864 | tf_op jit(solution)/shard_map/all_to_all | solution.py:117
  18.2 2.0 copy-start.6
  40.0 8.3 %copy-start.2 = (bf16[3,16,8192]{2,1,0:T(8,128)(2,1)S(1)}, bf16[3,16,8192]{2,1,0:T(8,128)(2,1)}, u32[]{:S(2)}) copy-start(bf16[3,16,8192]{2,1,0:T(8,128)(2,1)} %param.12) | copy-start | bytes 2359300
  40.0 13.9 %copy-start.7 = (u32[32]{0:T(128)S(1)}, u32[32]{0:T(128)}, u32[]{:S(2)}) copy-start(u32[32]{0:T(128)} %constant.219) | copy-start | bytes 388
  40.0 15.2 %copy-start.5 = (s32[192]{0:T(256)S(1)}, s32[192]{0:T(256)}, u32[]{:S(2)}) copy-start(s32[192]{0:T(256)} %param.9) | copy-start | bytes 2308
  40.0 237.9 %all-to-all-start.1 = ((bf16[192,16,512]{2,0,1:T(8,128)(2,1)}), bf16[192,16,512]{2,0,1:T(8,128)(2,1)}, u32[]{:S(2)}, u32[]{:S(2)}) async-start(bf16[192,16,512]{2,0,1:T(8,128)(2,1)} %bitcast.91), calls=%async_computation.1 | async-start | bytes 6291456 | tf_op jit(solution)/shard_map/all_to_all | solution.py:106
  48.3 198.3 %collective-permute-start = (bf16[16,8192]{1,0:T(8,128)(2,1)S(1)}, bf16[16,8192]{1,0:T(8,128)(2,1)S(1)}, u32[]{:S(2)}, u32[]{:S(2)}) collective-permute-start(bf16[16,8192]{1,0:T(8,128)(2,1)S(1)} %dynamic-slice_bitcast_fusion), channel_id=1, source_target_pairs={{0,4},{1,5},{2,6},{3,7},{4,8},{5,9},{6,10},{7,11},{8,12},{9,13},{1... | collective-permute-start | bytes 786440 | tf_op jit(solution)/shard_map/ppermute | solution.py:15
  49.8 196.9 %collective-permute-start.1 = (bf16[16,8192]{1,0:T(8,128)(2,1)S(1)}, bf16[16,8192]{1,0:T(8,128)(2,1)S(1)}, u32[]{:S(2)}, u32[]{:S(2)}) collective-permute-start(bf16[16,8192]{1,0:T(8,128)(2,1)S(1)} %dynamic-slice_bitcast_fusion), channel_id=1, source_target_pairs={{0,3},{1,4},{2,5},{3,6},{4,7},{5,8},{6,9},{7,10},{8,11},{9,12},{10... | collective-permute-start | bytes 786440 | tf_op jit(solution)/shard_map/ppermute | solution.py:15
  51.5 195.2 %collective-permute-start.2 = (bf16[16,8192]{1,0:T(8,128)(2,1)S(1)}, bf16[16,8192]{1,0:T(8,128)(2,1)S(1)}, u32[]{:S(2)}, u32[]{:S(2)}) collective-permute-start(bf16[16,8192]{1,0:T(8,128)(2,1)S(1)} %dynamic-slice_bitcast_fusion), channel_id=1, source_target_pairs={{0,2},{1,3},{2,4},{3,5},{4,6},{5,7},{6,8},{7,9},{8,10},{9,11},{10,... | collective-permute-start | bytes 786440 | tf_op jit(solution)/shard_map/ppermute | solution.py:15
  52.7 194.0 %collective-permute-start.3 = (bf16[16,8192]{1,0:T(8,128)(2,1)S(1)}, bf16[16,8192]{1,0:T(8,128)(2,1)S(1)}, u32[]{:S(2)}, u32[]{:S(2)}) collective-permute-start(bf16[16,8192]{1,0:T(8,128)(2,1)S(1)} %dynamic-slice_bitcast_fusion), channel_id=1, source_target_pairs={{0,1},{1,2},{2,3},{3,4},{4,5},{5,6},{6,7},{7,8},{8,9},{9,10},{10,1... | collective-permute-start | bytes 786440 | tf_op jit(solution)/shard_map/ppermute | solution.py:15
  277.9 22.2 %all-to-all-start.3 = ((bf16[48,16,512]{2,0,1:T(8,128)(2,1)}), bf16[48,16,512]{2,0,1:T(8,128)(2,1)S(1)}, u32[]{:S(2)}, u32[]{:S(2)}) async-start(bf16[48,16,512]{2,0,1:T(8,128)(2,1)} %copy.24), calls=%async_computation.3 | async-start | bytes 1572864 | tf_op jit(solution)/shard_map/all_to_all | solution.py:108
  300.1 0.9 copy-start.4
  301.0 85.4 %all-to-all-start.2 = ((bf16[16,48,512]{2,1,0:T(8,128)(2,1)}), bf16[16,48,512]{2,1,0:T(8,128)(2,1)S(1)}, u32[]{:S(2)}, u32[]{:S(2)}) async-start(bf16[16,48,512]{2,1,0:T(8,128)(2,1)} %bitcast.97), calls=%async_computation.2 | async-start | bytes 1572864 | tf_op jit(solution)/shard_map/all_to_all | solution.py:137
  375.2 7.7 %collective-permute-start.7 = (f32[16,1024]{1,0:T(8,128)S(1)}, f32[16,1024]{1,0:T(8,128)S(1)}, u32[]{:S(2)}, u32[]{:S(2)}) collective-permute-start(f32[16,1024]{1,0:T(8,128)S(1)} %get-tuple-element.27), channel_id=1, source_target_pairs={{0,12},{1,13},{2,14},{3,15},{4,0},{5,1},{6,2},{7,3},{8,4},{9,5},{1... | collective-permute-start | bytes 196616 | tf_op jit(solution)/shard_map/ppermute | solution.py:15
  375.4 10.0 %collective-permute-start.6 = (f32[16,1024]{1,0:T(8,128)S(1)}, f32[16,1024]{1,0:T(8,128)S(1)}, u32[]{:S(2)}, u32[]{:S(2)}) collective-permute-start(f32[16,1024]{1,0:T(8,128)S(1)} %get-tuple-element.27), channel_id=1, source_target_pairs={{0,13},{1,14},{2,15},{3,0},{4,1},{5,2},{6,3},{7,4},{8,5},{9,6},{10... | collective-permute-start | bytes 196616 | tf_op jit(solution)/shard_map/ppermute | solution.py:15
  379.7 5.7 %collective-permute-start.5 = (f32[16,1024]{1,0:T(8,128)S(1)}, f32[16,1024]{1,0:T(8,128)S(1)}, u32[]{:S(2)}, u32[]{:S(2)}) collective-permute-start(f32[16,1024]{1,0:T(8,128)S(1)} %get-tuple-element.27), channel_id=1, source_target_pairs={{0,14},{1,15},{2,0},{3,1},{4,2},{5,3},{6,4},{7,5},{8,6},{9,7},{10,... | collective-permute-start | bytes 196616 | tf_op jit(solution)/shard_map/ppermute | solution.py:15
  380.0 5.6 %collective-permute-start.4 = (f32[16,1024]{1,0:T(8,128)S(1)}, f32[16,1024]{1,0:T(8,128)S(1)}, u32[]{:S(2)}, u32[]{:S(2)}) collective-permute-start(f32[16,1024]{1,0:T(8,128)S(1)} %get-tuple-element.27), channel_id=1, source_target_pairs={{0,15},{1,0},{2,1},{3,2},{4,3},{5,4},{6,5},{7,6},{8,7},{9,8},{10,9... | collective-permute-start | bytes 196616 | tf_op jit(solution)/shard_map/ppermute | solution.py:15
  389.0 12.9 %copy-start.1 = (bf16[192,1024]{1,0:T(8,128)(2,1)S(1)}, bf16[192,1024]{1,0:T(8,128)(2,1)}, u32[]{:S(2)}) copy-start(bf16[192,1024]{1,0:T(8,128)(2,1)} %param.8) | copy-start | bytes 1179652
Sparse Core Ops, SparseCore 0:
  10.3 63.6 all-gather.5
  76.1 171.2 all-gather.3
where the time goes:
time: 410 us; the launch traced here: 409 us
  blocking collectives  249 us (61%)
  matrix products  44.6 us (11%)
  between operations  39.4 us (10%)
  starting transfers between devices  33.7 us (8%)
  waiting for transfers between devices  27.1 us (7%)
  local copies, waits for them, and re-layouts  9.93 us (2%)
  other arithmetic  4.84 us (1%)
    unnamed x1, blocking collectives  164 us
    psum x1, blocking collectives, local(): hidden = lax.psum(hidden, 'blk').astype(jnp.bfloat16)  59.6 us
    dot_general x17, matrix products, dot(): lax.dot_general(a, b, (dims, ((), ())), preferred_element_type=jnp.float3...  44.6 us
    all_gather x1, blocking collectives, local(): grad_all = lax.all_gather(grad_in, 'blk', axis=0, tiled=True)  25.4 us
    all_to_all x1, waiting for transfers between devices, local(): lax.all_to_all(send_cot, 'blk', split_axis=0, concat_axis=0, tiled=True)  18.3 us
    ppermute x8, starting transfers between devices, moved(): lax.ppermute(value, 'blk', [(i, (i + steps) % count) for i in range(count)])  11.2 us
  transfers between devices with their start and end apart: 14, of which 4 were waited for; matrix products, arithmetic and copies ran while one was open for 11% of the time, Pallas kernels for 0%

commit v1 on v0

--- a/solution.py
+++ b/solution.py
@@ -1,6 +1,8 @@
 import jax
 import jax.numpy as jnp
 from jax import lax
+from jax.experimental import pallas as pl
+from jax.experimental.pallas import tpu as pltpu
 from jax.sharding import PartitionSpec as P
 
 BLOCK = 128
@@ -13,6 +15,73 @@
 def moved(value, steps):
     count = lax.axis_size("blk")
     return lax.ppermute(value, "blk", [(i, (i + steps) % count) for i in range(count)])
+
+
+def to_all(value):
+    count = lax.axis_size("blk")
+    copies = jnp.broadcast_to(value[None], (count,) + value.shape)
+    return lax.all_to_all(copies, "blk", split_axis=0, concat_axis=0)
+
+
+def gathered_half(weight):
+    count, groups = lax.axis_size("blk"), lax.axis_size("groups")
+    part = weight.shape[0] // groups
+    piece = lax.dynamic_slice_in_dim(weight, lax.axis_index("groups") * part, part, 0)
+    same_core = [
+        [g * count + chip * 2 + core for chip in range(count // 2) for g in range(groups)]
+        for core in range(2)
+    ]
+    return lax.all_gather(
+        piece, ("groups", "blk"), axis_index_groups=same_core, axis=0, tiled=True
+    )
+
+
+def half_kernel(side, cot, grad, weight, down, *rest):
+    out = rest[-1]
+    rank = grad.shape[1]
+    frozen = dot(cot[...], weight[...], ((1,), (1,)))
+    for b in range(cot.shape[0] // BLOCK):
+        rows = slice(b * BLOCK, (b + 1) * BLOCK)
+        lora = adapter_scale * dot(
+            grad[rows, :], down[b * rank : (b + 1) * rank, :], ((1,), (0,))
+        )
+        out[rows, :] = (frozen[rows] + lora.astype(jnp.bfloat16).astype(jnp.float32)).astype(
+            jnp.bfloat16
+        )
+
+
+def write_half(side, cot, grad, weight, down, stripe, out=None):
+    rows, depth = cot.shape
+    width = down.shape[1]
+    specs = [
+        pl.BlockSpec((rows, depth), lambda j, side: (0, 0)),
+        pl.BlockSpec(grad.shape, lambda j, side: (0, 0)),
+        pl.BlockSpec((stripe, depth), lambda j, side: (j, 0)),
+        pl.BlockSpec((down.shape[0], stripe), lambda j, side: (0, 2 * j + side[0])),
+    ]
+    args = [side, cot, grad, weight, down]
+    alias = {}
+    if out is not None:
+        specs.append(pl.BlockSpec(memory_space=pl.ANY))
+        args.append(out)
+        alias = {5: 0}
+    return pl.pallas_call(
+        half_kernel,
+        grid_spec=pltpu.PrefetchScalarGridSpec(
+            num_scalar_prefetch=1,
+            grid=(weight.shape[0] // stripe,),
+            in_specs=specs,
+            out_specs=pl.BlockSpec((rows, stripe), lambda j, side: (0, 2 * j + side[0])),
+        ),
+        out_shape=jax.ShapeDtypeStruct((rows, width), jnp.bfloat16),
+        input_output_aliases=alias,
+        cost_estimate=pl.CostEstimate(
+            flops=rows * depth * width,
+            bytes_accessed=weight.size * 2 + rows * width,
+            transcendentals=0,
+        ),
+        compiler_params=pltpu.CompilerParams(vmem_limit_bytes=24 << 20),
+    )(*args)
 
 
 def dot(a, b, dims, precision=None):
@@ -99,8 +168,11 @@
     slot_cap = resident_rows // devices
     start_ids = tenant_first_row // BLOCK
 
-    weight = lax.all_gather(frozen_value_weight, "blk", axis=0, tiled=True)
-    rows_all = lax.all_gather(token_layout_row, "blk", axis=0, tiled=True)
+    core = device % 2
+    own_half = gathered_half(frozen_value_weight)
+    swap = [(i, i ^ 1) for i in range(devices)]
+    other_half = lax.ppermute(own_half, "blk", swap)
+    rows_all = to_all(token_layout_row).reshape(-1)
     up_all = lax.all_gather(adapter_up_maps, "blk", axis=0, tiled=True)
     up_all = up_all.reshape(slots * rank, out_width)
     act_f = lax.all_to_all(activations, "blk", split_axis=1, concat_axis=0, tiled=True)
@@ -130,7 +202,7 @@
     own_slot = starts_of(token_layout_row // BLOCK, start_ids)
     all_up = dot(cotangent, up_all, ((1,), (1,)))
     grad_in = chosen(all_up, own_slot, rank).astype(jnp.bfloat16)
-    grad_all = lax.all_gather(grad_in, "blk", axis=0, tiled=True)
+    grad_all = to_all(grad_in.T).transpose(0, 2, 1).reshape(-1, rank)
 
     slot_all = starts_of(rows_all // BLOCK, start_ids)
     hidden, down_f = feature_share(act_f, maps_f, grad_all, slot_all)
@@ -138,7 +210,10 @@
         (adapter_scale * down_f).astype(jnp.bfloat16), "blk", split_axis=0, concat_axis=1, tiled=True
     )
     down_map_gradient = down_home.astype(jnp.float32).reshape(resident, rank, width)
-    hidden = lax.psum(hidden, "blk").astype(jnp.bfloat16)
+    hidden = hidden.reshape(devices, tokens, rank).transpose(0, 2, 1)
+    hidden = lax.all_to_all(hidden, "blk", split_axis=0, concat_axis=0)
+    hidden = to_all(jnp.sum(hidden, axis=0).astype(jnp.bfloat16))
+    hidden = hidden.transpose(0, 2, 1).reshape(-1, rank)
 
     first_block = device * resident
     block_numbers = first_block + jnp.arange(resident, dtype=jnp.int32)
@@ -155,18 +230,16 @@
 
     grad_rows = dot(row_of, grad_all, ((1,), (0,))).astype(jnp.bfloat16)
     hidden_rows = dot(row_of, hidden, ((1,), (0,))).astype(jnp.bfloat16)
-    adapter_rows = []
+    down_blocks = []
     up_parts = []
     for b in range(resident):
         rows = slice(b * BLOCK, (b + 1) * BLOCK)
         down = carried
         for k in range(b + 1):
             down = jnp.where(is_local[b] & (home_slot[b] == k), adapter_down_maps[k], down)
-        adapter_rows.append(
-            (adapter_scale * dot(grad_rows[rows], down, ((1,), (0,)))).astype(jnp.bfloat16)
-        )
+        down_blocks.append(down)
         up_parts.append(dot(hidden_rows[rows], cot_rows[rows], ((0,), (0,))))
-    adapter_rows = jnp.concatenate(adapter_rows, axis=0)
+    down_blocks = jnp.concatenate(down_blocks, axis=0)
 
     tail = sum(jnp.where(is_local[b], 0.0, up_parts[b]) for b in range(resident))
     far = jnp.zeros_like(tail)
@@ -182,9 +255,28 @@
         up_grads.append(adapter_scale * total)
     up_map_gradient = jnp.stack(up_grads)
 
-    frozen_rows = dot(cot_rows, weight, ((1,), (1,)))
-    layout_input_gradient = (frozen_rows + adapter_rows.astype(jnp.float32)).astype(jnp.bfloat16)
-    return (layout_input_gradient, down_map_gradient, up_map_gradient)
+    stripe = frozen_value_weight.shape[0]
+    if stripe % LANES == 0:
+        own = core.astype(jnp.int32).reshape(1)
+        out = write_half(own, cot_rows, grad_rows, own_half, down_blocks, stripe)
+        out = write_half(1 - own, cot_rows, grad_rows, other_half, down_blocks, stripe, out)
+    else:
+        first = jnp.where(core == 0, own_half, other_half)
+        second = jnp.where(core == 0, other_half, own_half)
+        pairs = [half.reshape(-1, 1, stripe, out_width) for half in (first, second)]
+        weight = jnp.concatenate(pairs, axis=1).reshape(width, out_width)
+        out = dot(cot_rows, weight, ((1,), (1,)))
+        lora = [
+            dot(
+                grad_rows[b * BLOCK : (b + 1) * BLOCK],
+                down_blocks[b * rank : (b + 1) * rank],
+                ((1,), (0,)),
+            )
+            for b in range(resident)
+        ]
+        lora = (adapter_scale * jnp.concatenate(lora, axis=0)).astype(jnp.bfloat16)
+        out = (out + lora.astype(jnp.float32)).astype(jnp.bfloat16)
+    return (out, down_map_gradient, up_map_gradient)
 
 
 def solution(mesh):

time: 410 us -> 370 us (0.902); the launches traced: 409 us -> 363 us
  blocking collectives: 249 us -> 0 us
  waiting for transfers between devices: 27.1 us -> 176 us
  starting transfers between devices: 33.7 us -> 64.5 us
  local copies, waits for them, and re-layouts: 9.93 us -> 26.9 us
  Pallas kernels: 0 us -> 16.6 us
  matrix products: 44.6 us -> 33 us
    unnamed x1 -> x0, blocking collectives: 164 us -> none
    all_gather x1, waiting for transfers between devices: 0.01 us -> 98.9 us  [gathered_half(): lax.all_gather(piece, ('groups', 'blk'), axis_index_groups=same_core, axi...]
    psum x1 -> x0, blocking collectives: 59.6 us -> none  [local(): hidden = lax.psum(hidden, 'blk').astype(jnp.bfloat16)]
    all_gather x1, waiting for transfers between devices: 0.02 us -> 40.8 us  [local(): up_all = lax.all_gather(adapter_up_maps, 'blk', axis=0, tiled=True)]
    all_gather x1 -> x0, blocking collectives: 25.4 us -> none  [local(): grad_all = lax.all_gather(grad_in, 'blk', axis=0, tiled=True)]
    all_to_all x0 -> x4, starting transfers between devices: none -> 20.1 us  [the longest x3 15 us: to_all(): return lax.all_to_all(copies, 'blk', split_axis=0, concat_axis=0)]
    all_to_all x1, waiting for transfers between devices: 18.3 us -> 0.01 us  [local(): lax.all_to_all(send_cot, 'blk', split_axis=0, concat_axis=0, tiled=True)]
    pallas_call x0 -> x2, Pallas kernels: none -> 16.6 us  [write_half(): pl.pallas_call(half_kernel, grid_spec=pltpu.PrefetchScalarGridSpec(num_sc...]
  transfers between devices with their start and end apart: 14 -> 19, of which waited for: 4 -> 8; matrix products, arithmetic and copies ran while one was open for 11% -> 17% of each run, Pallas kernels for 0% -> 2%
where the time goes in v1:
time: 370 us; the launch traced here: 363 us
  waiting for transfers between devices  176 us (48%)
  starting transfers between devices  64.5 us (17%)
  between operations  39.3 us (11%)
  matrix products  33 us (9%)
  local copies, waits for them, and re-layouts  26.9 us (7%)
  Pallas kernels  16.6 us (4%)
  other arithmetic  7.47 us (2%)
    all_gather x1, waiting for transfers between devices, gathered_half(): lax.all_gather(piece, ('groups', 'blk'), axis_index_groups=same_core, axi...  98.9 us
    all_gather x1, waiting for transfers between devices, local(): up_all = lax.all_gather(adapter_up_maps, 'blk', axis=0, tiled=True)  40.8 us
    dot_general x13, matrix products, dot(): lax.dot_general(a, b, (dims, ((), ())), preferred_element_type=jnp.float3...  33 us
    all_to_all x1, waiting for transfers between devices, local(): lax.all_to_all(down_flat, 'blk', split_axis=1, concat_axis=0, tiled=True)  19.2 us
    pallas_call x2, Pallas kernels, write_half(): pl.pallas_call(half_kernel, grid_spec=pltpu.PrefetchScalarGridSpec(num_sc...  16.6 us
    all_to_all x1, starting transfers between devices, local(): lax.all_to_all(send_cot, 'blk', split_axis=0, concat_axis=0, tiled=True)  16.6 us
    all_to_all x3, starting transfers between devices, to_all(): return lax.all_to_all(copies, 'blk', split_axis=0, concat_axis=0)  15 us
    ppermute x8, starting transfers between devices, moved(): lax.ppermute(value, 'blk', [(i, (i + steps) % count) for i in range(count)])  10.9 us
  transfers between devices with their start and end apart: 19, of which 8 were waited for; matrix products, arithmetic and copies ran while one was open for 17% of the time, Pallas kernels for 2%

profile of v1, /device:TPU:1, one launch (start us, length us, event | category | flops | bytes accessed | tf_op | source)
XLA Modules:
  0.0 363.4 jit_solution(17197314842743408587)
XLA Ops:
  7.2 1.2 copy-done
  8.4 0.8 constant_dynamic-slice_fusion
  9.3 1.3 broadcast_in_dim.96
  10.5 7.3 %all-to-all-start = ((s32[16,1,192]{2,1,0:T(1,128)}), s32[16,1,192]{2,1,0:T(1,128)S(1)}, u32[]{:S(2)}, u32[]{:S(2)}) async-start(s32[16,1,192]{2,1,0:T(1,128)} %broadcast_in_dim.96), calls=%async_computation | async-start | bytes 32768 | tf_op jit(solution)/shard_map/all_to_all | solution.py:23
  17.9 1.4 copy.41
  19.3 1.3 copy.36
  20.6 3.1 all-to-all-done
  23.7 4.2 %all-to-all-start.5 = ((bf16[48,16,512]{2,0,1:T(8,128)(2,1)}), bf16[48,16,512]{2,0,1:T(8,128)(2,1)S(1)}, u32[]{:S(2)}, u32[]{:S(2)}) async-start(bf16[48,16,512]{2,0,1:T(8,128)(2,1)} %copy.36), calls=%async_computation.5 | async-start | bytes 1572864 | tf_op jit(solution)/shard_map/all_to_all | solution.py:180
  27.9 3.9 %copy.49 = bf16[24,16,8,512]{3,2,0,1:T(8,128)(2,1)} copy(bf16[24,16,8,512]{3,2,1,0:T(8,128)(2,1)} %bitcast.106) | data formatting | bytes 6291456 | tf_op jit(solution)/shard_map/all_to_all | solution.py:178
  32.7 19.2 %all-to-all-done.5 = bf16[48,16,512]{2,0,1:T(8,128)(2,1)S(1)} async-done(((bf16[48,16,512]{2,0,1:T(8,128)(2,1)}), bf16[48,16,512]{2,0,1:T(8,128)(2,1)S(1)}, u32[]{:S(2)}, u32[]{:S(2)}) %all-to-all-start.5) | async-done | bytes 786464 | tf_op jit(solution)/shard_map/all_to_all | solution.py:180
  52.0 0.9 copy-done.4
  52.9 6.1 %all-to-all-start.3 = ((bf16[192,16,512]{2,0,1:T(8,128)(2,1)}), bf16[192,16,512]{2,0,1:T(8,128)(2,1)}, u32[]{:S(2)}, u32[]{:S(2)}) async-start(bf16[192,16,512]{2,0,1:T(8,128)(2,1)} %bitcast.104), calls=%async_computation.3 | async-start | bytes 6291456 | tf_op jit(solution)/shard_map/all_to_all | solution.py:178
  62.4 1.4 collective-permute-start.1
  63.8 1.7 collective-permute-start.2
  65.5 1.2 collective-permute-start.3
  66.7 1.2 collective-permute-start.4
  93.8 1.2 compare_select_fusion.3
  95.0 1.2 convolution_convert_fusion
  97.3 1.2 compare_select_fusion.2
  98.5 98.9 %all-gather.5.cloned.1.call-done.weight = bf16[4096,1024]{1,0:T(8,128)(2,1)} async-done(((bf16[256,1024]{1,0:T(8,128)(2,1)}), bf16[4096,1024]{1,0:T(8,128)(2,1)}) %all-gather.5.cloned.1.call-update) | async-done | bytes 8388624 | tf_op jit(solution)/shard_map/all_gather | solution.py:34
  198.0 16.6 %all-to-all-start.1 = ((bf16[16,24,1024]{2,1,0:T(8,128)(2,1)}), bf16[16,24,1024]{2,1,0:T(8,128)(2,1)}, u32[]{:S(2)}, u32[]{:S(2)}) async-start(bf16[16,24,1024]{2,1,0:T(8,128)(2,1)} %bitcast.3), calls=%async_computation.1 | async-start | bytes 1572864 | tf_op jit(solution)/shard_map/all_to_all | solution.py:189
  214.7 40.8 %all-gather.3.cloned.1.call-done = bf16[48,16,1024]{2,1,0:T(8,128)(2,1)} async-done(((bf16[3,16,1024]{2,1,0:T(8,128)(2,1)}), bf16[48,16,1024]{2,1,0:T(8,128)(2,1)}) %all-gather.3.cloned.1.call-update) | async-done | bytes 1572880 | tf_op jit(solution)/shard_map/all_gather | solution.py:176
  255.6 2.1 convolution_select_fusion
  257.9 8.5 %compare_select_fusion = f32[3072,768]{1,0:T(8,128)} fusion(bf16[3072,512]{1,0:T(8,128)(2,1)} %bitcast.21, bf16[768,512]{1,0:T(8,128)(2,1)} %bitcast.109, s32[768]{0:T(1024)S(1)} %add_select_fusion.2, s32[3072]{0:T(1024)S(1)} %copy-done.8), kind=kOutput, calls=%fused_computation | convolution fusion | flops 2420637696 | bytes 13384704 | tf_op jit(solution)/shard_map/dot_general | solution.py:88
  267.0 3.8 %all-to-all-start.2 = ((bf16[16,16,192]{2,1,0:T(8,128)(2,1)}), bf16[16,16,192]{2,1,0:T(8,128)(2,1)S(1)}, u32[]{:S(2)}, u32[]{:S(2)}) async-start(bf16[16,16,192]{2,1,0:T(8,128)(2,1)} %broadcast_in_dim.153), calls=%async_computation.2 | async-start | bytes 262144 | tf_op jit(solution)/shard_map/all_to_all | solution.py:23
  270.8 4.9 %fusion.9 = f32[3072,16]{0,1:T(8,128)S(1)} fusion(f32[3072,768]{1,0:T(8,128)} %compare_select_fusion, s32[128]{0:T(128)S(1)} %copy-done.14), kind=kOutput, calls=%fused_computation.15 | convolution fusion | flops 77465600 | bytes 9634304 | tf_op jit(solution)/shard_map/dot_general | solution.py:88
  275.8 0.9 copy.50
  276.7 1.0 all-to-all-done.2
  277.7 5.0 %all-to-all-start.6 = ((f32[16,16,192]{2,1,0:T(8,128)}), f32[16,16,192]{2,1,0:T(8,128)S(1)}, u32[]{:S(2)}, u32[]{:S(2)}) async-start(f32[16,16,192]{2,1,0:T(8,128)} %bitcast.103), calls=%async_computation.6 | async-start | bytes 524288 | tf_op jit(solution)/shard_map/all_to_all | solution.py:214
  282.8 3.2 convolution_convert_fusion.1.cot
  286.2 6.0 %all-to-all-done.6 = f32[16,16,192]{2,1,0:T(8,128)S(1)} async-done(((f32[16,16,192]{2,1,0:T(8,128)}), f32[16,16,192]{2,1,0:T(8,128)S(1)}, u32[]{:S(2)}, u32[]{:S(2)}) %all-to-all-start.6) | async-done | bytes 196640 | tf_op jit(solution)/shard_map/all_to_all | solution.py:214
  292.9 4.0 %all-to-all-start.7 = ((bf16[16,16,192]{2,1,0:T(8,128)(2,1)}), bf16[16,16,192]{2,1,0:T(8,128)(2,1)S(1)}, u32[]{:S(2)}, u32[]{:S(2)}) async-start(bf16[16,16,192]{2,1,0:T(8,128)(2,1)} %broadcast_in_dim.162), calls=%async_computation.7 | async-start | bytes 262144 | tf_op jit(solution)/shard_map/all_to_all | solution.py:23
  296.9 8.8 %multiply_convert_fusion = bf16[768,512]{1,0:T(8,128)(2,1)} fusion(bf16[3072,512]{1,0:T(8,128)(2,1)} %bitcast.21, bf16[3072,16]{0,1:T(8,128)(2,1)S(1)} %reshape.275, s32[768]{0:T(1024)S(1)} %add_select_fusion.2, s32[3072]{0:T(1024)S(1)} %copy-done.9, s32[768]{0:T(1024)S(1)} %copy-done.12), kind=kOutput, calls=%fused_computation.22 | convolution fusion | flops 2499293184 | bytes 4048896 | tf_op jit(solution)/shard_map/dot_general | solution.py:88
  306.3 6.1 %all-to-all-start.4 = ((bf16[16,48,512]{2,1,0:T(8,128)(2,1)}), bf16[16,48,512]{2,1,0:T(8,128)(2,1)S(1)}, u32[]{:S(2)}, u32[]{:S(2)}) async-start(bf16[16,48,512]{2,1,0:T(8,128)(2,1)} %bitcast.110), calls=%async_computation.4 | async-start | bytes 1572864 | tf_op jit(solution)/shard_map/all_to_all | solution.py:209
  312.4 1.6 copy.38
  314.0 1.1 reshape.277
  315.1 0.8 fusion.13
  316.3 2.1 select_add_fusion.1
  318.3 3.2 collective-permute-start.8
  321.6 1.7 collective-permute-start.7
  323.7 0.8 fusion.12.grad
  324.5 2.6 collective-permute-done.8
  327.1 3.8 %collective-permute-done.7 = f32[16,1024]{1,0:T(8,128)S(1)} collective-permute-done((f32[16,1024]{1,0:T(8,128)S(1)}, f32[16,1024]{1,0:T(8,128)S(1)}, u32[]{:S(2)}, u32[]{:S(2)}) %collective-permute-start.7) | collective-permute-done | bytes 65568 | tf_op jit(solution)/shard_map/ppermute | solution.py:17
  331.9 2.1 copy.35
  334.0 2.6 reshape.278
  336.5 3.4 copy-done.1
  339.9 6.7 %shard_map.94.rest_0_ = bf16[384,8192]{1,0:T(8,128)(2,1)} custom-call(s32[1]{0:T(128)} %bitcast.side, bf16[384,1024]{1,0:T(8,128)(2,1)S(1)} %convolution_convert_fusion.1.cot, bf16[384,16]{1,0:T(8,128)(2,1)S(1)} %fusion.12.grad, bf16[4096,1024]{1,0:T(8,128)(2,1)S(1)} %copy-done.1, bf16[48,8192]{1,0:T(8,128)(2,1)S(1)} %pad_maximum_fusion.down), custom_call_target="tpu_custom_call" | custom-call | flops 3221225472 | bytes 11534336 | tf_op jit(solution)/shard_map/pallas_call | solution.py:68
  346.6 10.0 %shard_map.95 = bf16[384,8192]{1,0:T(8,128)(2,1)} custom-call(s32[1]{0:T(128)S(6)} %sub.87.side, bf16[384,1024]{1,0:T(8,128)(2,1)S(1)} %convolution_convert_fusion.1.cot, bf16[384,16]{1,0:T(8,128)(2,1)S(1)} %fusion.12.grad, bf16[4096,1024]{1,0:T(8,128)(2,1)} %collective-permute-done.weight, ...), custom_call_target="tpu_custom_call", output_to_operand_aliasing={{}: (5, {})} | custom-call | flops 3221225472 | bytes 11534336 | tf_op jit(solution)/shard_map/pallas_call | solution.py:68
  (84 shorter events, 11.3 us)
Async XLA Ops:
  7.2 1.2 copy-start
  7.2 190.3 %all-gather.5.cloned.1.call-start = ((), (), s32[]{:S(2)}) async-start(), calls=%async_computation.9 | async-start | bytes 8912896 | tf_op jit(solution)/shard_map/all_gather | solution.py:34
  10.5 13.2 %all-to-all-start = ((s32[16,1,192]{2,1,0:T(1,128)}), s32[16,1,192]{2,1,0:T(1,128)S(1)}, u32[]{:S(2)}, u32[]{:S(2)}) async-start(s32[16,1,192]{2,1,0:T(1,128)} %broadcast_in_dim.96), calls=%async_computation | async-start | bytes 32768 | tf_op jit(solution)/shard_map/all_to_all | solution.py:23
  23.7 28.3 %all-to-all-start.5 = ((bf16[48,16,512]{2,0,1:T(8,128)(2,1)}), bf16[48,16,512]{2,0,1:T(8,128)(2,1)S(1)}, u32[]{:S(2)}, u32[]{:S(2)}) async-start(bf16[48,16,512]{2,0,1:T(8,128)(2,1)} %copy.36), calls=%async_computation.5 | async-start | bytes 1572864 | tf_op jit(solution)/shard_map/all_to_all | solution.py:180
  27.9 3.9 %copy-start.13 = (s32[32]{0:T(128)S(1)}, s32[32]{0:T(128)}, u32[]{:S(2)}) copy-start(s32[32]{0:T(128)} %param.10) | copy-start | bytes 388
  52.0 0.9 copy-start.4
  52.9 9.4 %copy-start.2 = (bf16[3,16,8192]{2,1,0:T(8,128)(2,1)S(1)}, bf16[3,16,8192]{2,1,0:T(8,128)(2,1)}, u32[]{:S(2)}) copy-start(bf16[3,16,8192]{2,1,0:T(8,128)(2,1)} %param.12) | copy-start | bytes 2359300
  52.9 40.6 %copy-start.11 = (s32[192]{0:T(256)S(1)}, s32[192]{0:T(256)}, u32[]{:S(2)}) copy-start(s32[192]{0:T(256)} %param.9) | copy-start | bytes 2308
  52.9 42.1 %copy-start.3 = (bf16[192,1024]{1,0:T(8,128)(2,1)S(1)}, bf16[192,1024]{1,0:T(8,128)(2,1)}, u32[]{:S(2)}) copy-start(bf16[192,1024]{1,0:T(8,128)(2,1)} %param.8) | copy-start | bytes 1179652
  52.9 145.1 %all-to-all-start.3 = ((bf16[192,16,512]{2,0,1:T(8,128)(2,1)}), bf16[192,16,512]{2,0,1:T(8,128)(2,1)}, u32[]{:S(2)}, u32[]{:S(2)}) async-start(bf16[192,16,512]{2,0,1:T(8,128)(2,1)} %bitcast.104), calls=%async_computation.3 | async-start | bytes 6291456 | tf_op jit(solution)/shard_map/all_to_all | solution.py:178
  59.1 196.5 %all-gather.3.cloned.1.call-start = ((), (), s32[]{:S(2)}) async-start(), calls=%async_computation.8 | async-start | bytes 1671168 | tf_op jit(solution)/shard_map/all_gather | solution.py:176
  62.4 135.6 %collective-permute-start.1 = (bf16[16,8192]{1,0:T(8,128)(2,1)S(1)}, bf16[16,8192]{1,0:T(8,128)(2,1)S(1)}, u32[]{:S(2)}, u32[]{:S(2)}) collective-permute-start(bf16[16,8192]{1,0:T(8,128)(2,1)S(1)} %dynamic-slice_bitcast_fusion), channel_id=1, source_target_pairs={{0,4},{1,5},{2,6},{3,7},{4,8},{5,9},{6,10},{7,11},{8,12},{9,13},{1... | collective-permute-start | bytes 786440 | tf_op jit(solution)/shard_map/ppermute | solution.py:17
  63.8 134.1 %collective-permute-start.2 = (bf16[16,8192]{1,0:T(8,128)(2,1)S(1)}, bf16[16,8192]{1,0:T(8,128)(2,1)S(1)}, u32[]{:S(2)}, u32[]{:S(2)}) collective-permute-start(bf16[16,8192]{1,0:T(8,128)(2,1)S(1)} %dynamic-slice_bitcast_fusion), channel_id=1, source_target_pairs={{0,3},{1,4},{2,5},{3,6},{4,7},{5,8},{6,9},{7,10},{8,11},{9,12},{10... | collective-permute-start | bytes 786440 | tf_op jit(solution)/shard_map/ppermute | solution.py:17
  65.5 132.4 %collective-permute-start.3 = (bf16[16,8192]{1,0:T(8,128)(2,1)S(1)}, bf16[16,8192]{1,0:T(8,128)(2,1)S(1)}, u32[]{:S(2)}, u32[]{:S(2)}) collective-permute-start(bf16[16,8192]{1,0:T(8,128)(2,1)S(1)} %dynamic-slice_bitcast_fusion), channel_id=1, source_target_pairs={{0,2},{1,3},{2,4},{3,5},{4,6},{5,7},{6,8},{7,9},{8,10},{9,11},{10,... | collective-permute-start | bytes 786440 | tf_op jit(solution)/shard_map/ppermute | solution.py:17
  66.7 131.2 %collective-permute-start.4 = (bf16[16,8192]{1,0:T(8,128)(2,1)S(1)}, bf16[16,8192]{1,0:T(8,128)(2,1)}, u32[]{:S(2)}, u32[]{:S(2)}) collective-permute-start(bf16[16,8192]{1,0:T(8,128)(2,1)S(1)} %dynamic-slice_bitcast_fusion), channel_id=1, source_target_pairs={{0,1},{1,2},{2,3},{3,4},{4,5},{5,6},{6,7},{7,8},{8,9},{9,10},{10,1... | collective-permute-start | bytes 786440 | tf_op jit(solution)/shard_map/ppermute | solution.py:17
  197.5 149.1 %collective-permute-start = (bf16[4096,1024]{1,0:T(8,128)(2,1)}, bf16[4096,1024]{1,0:T(8,128)(2,1)}, u32[]{:S(2)}, u32[]{:S(2)}) collective-permute-start(bf16[4096,1024]{1,0:T(8,128)(2,1)} %all-gather.5.cloned.1.call-done.weight), channel_id=1, source_target_pairs={{0,1},{1,0},{2,3},{3,2},{4,5},{5,4},{6,7},{7,6},{8,9},{9,8},{10,11... | collective-permute-start | bytes 25165832 | tf_op jit(solution)/shard_map/ppermute | solution.py:174
  198.0 68.3 %all-to-all-start.1 = ((bf16[16,24,1024]{2,1,0:T(8,128)(2,1)}), bf16[16,24,1024]{2,1,0:T(8,128)(2,1)}, u32[]{:S(2)}, u32[]{:S(2)}) async-start(bf16[16,24,1024]{2,1,0:T(8,128)(2,1)} %bitcast.3), calls=%async_computation.1 | async-start | bytes 1572864 | tf_op jit(solution)/shard_map/all_to_all | solution.py:189
  214.6 43.0 %copy-start.14 = (s32[128]{0:T(128)S(1)}, s32[128]{0:T(128)}, u32[]{:S(2)}) copy-start(s32[128]{0:T(128)} %and_select_fusion.2) | copy-start | bytes 1540
  214.6 43.3 %copy-start.8 = (s32[3072]{0:T(1024)S(1)}, s32[3072]{0:T(1024)}, u32[]{:S(2)}) copy-start(s32[3072]{0:T(1024)} %compare_select_fusion.2) | copy-start | bytes 36868
  267.0 10.6 %all-to-all-start.2 = ((bf16[16,16,192]{2,1,0:T(8,128)(2,1)}), bf16[16,16,192]{2,1,0:T(8,128)(2,1)S(1)}, u32[]{:S(2)}, u32[]{:S(2)}) async-start(bf16[16,16,192]{2,1,0:T(8,128)(2,1)} %broadcast_in_dim.153), calls=%async_computation.2 | async-start | bytes 262144 | tf_op jit(solution)/shard_map/all_to_all | solution.py:23
  277.7 14.5 %all-to-all-start.6 = ((f32[16,16,192]{2,1,0:T(8,128)}), f32[16,16,192]{2,1,0:T(8,128)S(1)}, u32[]{:S(2)}, u32[]{:S(2)}) async-start(f32[16,16,192]{2,1,0:T(8,128)} %bitcast.103), calls=%async_computation.6 | async-start | bytes 524288 | tf_op jit(solution)/shard_map/all_to_all | solution.py:214
  282.8 14.1 %copy-start.9 = (s32[3072]{0:T(1024)S(1)}, s32[3072]{0:T(1024)}, u32[]{:S(2)}) copy-start(s32[3072]{0:T(1024)} %compare_select_fusion.2) | copy-start | bytes 36868
  282.8 14.1 %copy-start.12 = (s32[768]{0:T(1024)S(1)}, s32[768]{0:T(1024)}, u32[]{:S(2)}) copy-start(s32[768]{0:T(1024)} %fusion.37) | copy-start | bytes 9220
  286.2 19.5 %copy-start.6 = (bf16[3072,16]{0,1:T(8,128)(2,1)}, bf16[3072,16]{0,1:T(8,128)(2,1)S(1)}, u32[]{:S(2)}) copy-start(bf16[3072,16]{0,1:T(8,128)(2,1)S(1)} %reshape.275) | copy-start | bytes 294916
  292.9 12.8 %all-to-all-start.7 = ((bf16[16,16,192]{2,1,0:T(8,128)(2,1)}), bf16[16,16,192]{2,1,0:T(8,128)(2,1)S(1)}, u32[]{:S(2)}, u32[]{:S(2)}) async-start(bf16[16,16,192]{2,1,0:T(8,128)(2,1)} %broadcast_in_dim.162), calls=%async_computation.7 | async-start | bytes 262144 | tf_op jit(solution)/shard_map/all_to_all | solution.py:23
  296.9 18.2 %copy-start.10 = (s32[3072]{0:T(1024)S(1)}, s32[3072]{0:T(1024)}, u32[]{:S(2)}) copy-start(s32[3072]{0:T(1024)} %get-tuple-element.20) | copy-start | bytes 36868
  305.7 0.7 copy-start.5
  306.3 25.4 %all-to-all-start.4 = ((bf16[16,48,512]{2,1,0:T(8,128)(2,1)}), bf16[16,48,512]{2,1,0:T(8,128)(2,1)S(1)}, u32[]{:S(2)}, u32[]{:S(2)}) async-start(bf16[16,48,512]{2,1,0:T(8,128)(2,1)} %bitcast.110), calls=%async_computation.4 | async-start | bytes 1572864 | tf_op jit(solution)/shard_map/all_to_all | solution.py:209
  315.1 8.6 %copy-start.7 = (bf16[3072,16]{0,1:T(8,128)(2,1)S(1)}, bf16[3072,16]{0,1:T(8,128)(2,1)}, u32[]{:S(2)}) copy-start(bf16[3072,16]{0,1:T(8,128)(2,1)} %copy-done.6) | copy-start | bytes 294916
  318.3 8.8 %collective-permute-start.8 = (f32[16,1024]{1,0:T(8,128)S(1)}, f32[16,1024]{1,0:T(8,128)S(1)}, u32[]{:S(2)}, u32[]{:S(2)}) collective-permute-start(f32[16,1024]{1,0:T(8,128)S(1)} %get-tuple-element.31), channel_id=1, source_target_pairs={{0,12},{1,13},{2,14},{3,15},{4,0},{5,1},{6,2},{7,3},{8,4},{9,5},{1... | collective-permute-start | bytes 196616 | tf_op jit(solution)/shard_map/ppermute | solution.py:17
  321.6 9.3 %collective-permute-start.7 = (f32[16,1024]{1,0:T(8,128)S(1)}, f32[16,1024]{1,0:T(8,128)S(1)}, u32[]{:S(2)}, u32[]{:S(2)}) collective-permute-start(f32[16,1024]{1,0:T(8,128)S(1)} %get-tuple-element.31), channel_id=1, source_target_pairs={{0,13},{1,14},{2,15},{3,0},{4,1},{5,2},{6,3},{7,4},{8,5},{9,6},{10... | collective-permute-start | bytes 196616 | tf_op jit(solution)/shard_map/ppermute | solution.py:17
  323.3 7.6 %collective-permute-start.6 = (f32[16,1024]{1,0:T(8,128)S(1)}, f32[16,1024]{1,0:T(8,128)S(1)}, u32[]{:S(2)}, u32[]{:S(2)}) collective-permute-start(f32[16,1024]{1,0:T(8,128)S(1)} %get-tuple-element.31), channel_id=1, source_target_pairs={{0,14},{1,15},{2,0},{3,1},{4,2},{5,3},{6,4},{7,5},{8,6},{9,7},{10,... | collective-permute-start | bytes 196616 | tf_op jit(solution)/shard_map/ppermute | solution.py:17
  323.5 7.3 %collective-permute-start.5 = (f32[16,1024]{1,0:T(8,128)S(1)}, f32[16,1024]{1,0:T(8,128)S(1)}, u32[]{:S(2)}, u32[]{:S(2)}) collective-permute-start(f32[16,1024]{1,0:T(8,128)S(1)} %get-tuple-element.31), channel_id=1, source_target_pairs={{0,15},{1,0},{2,1},{3,2},{4,3},{5,4},{6,5},{7,6},{8,7},{9,8},{10,9... | collective-permute-start | bytes 196616 | tf_op jit(solution)/shard_map/ppermute | solution.py:17
  336.5 3.4 copy-start.1
Sparse Core Ops, SparseCore 0:
  10.7 186.6 all-gather.4
  199.7 55.7 all-gather.2

commit v2 on v0

v2 whole, which is shorter than its diff:
```python
import jax
import jax.numpy as jnp
from jax import lax
from jax.experimental import pallas as pl
from jax.experimental.pallas import tpu as pltpu
from jax.sharding import PartitionSpec as P

BLOCK = 128
HOPS = 4
LANES = 128
DIGIT = 64

adapter_scale = 2.0


def permuted(value, pairs):
    return lax.ppermute(value, "blk", pairs)


def moved(value, steps):
    count = lax.axis_size("blk")
    return permuted(value, [(i, (i + steps) % count) for i in range(count)])


def to_all(value):
    count = lax.axis_size("blk")
    copies = jnp.broadcast_to(value[None], (count,) + value.shape)
    return lax.all_to_all(copies, "blk", split_axis=0, concat_axis=0)


def dot(a, b, dims):
    return lax.dot_general(a, b, (dims, ((), ())), preferred_element_type=jnp.float32)


def starts_of(blocks, start_ids):
    latest = jnp.max(
        jnp.where(start_ids[None, :] <= blocks[:, None], start_ids[None, :], -1), axis=1
    )
    return jnp.where(latest >= 0, latest, jnp.max(start_ids))


def as_digits(rows):
    return jnp.stack(
        [rows % DIGIT, rows // DIGIT % DIGIT, rows // (DIGIT * DIGIT)]
    ).astype(jnp.bfloat16)


def from_digits(digits):
    low, middle, high = digits.astype(jnp.int32)
    return (high * DIGIT + middle) * DIGIT + low


def ring_shards(weight):
    count, device = lax.axis_size("blk"), lax.axis_index("blk")
    chips = count // 2
    order = list(range(0, chips, 2)) + list(range(chips - 1, 0, -2))
    place = [order.index(chip) for chip in range(chips)]
    chip, core = device // 2, device % 2

    def along(step):
        return [
            (2 * c + k, 2 * order[(place[c] + step) % chips] + k)
            for c in range(chips)
            for k in range(2)
        ]

    def origin(step):
        return jnp.array(order, jnp.int32)[
            (jnp.array(place, jnp.int32)[chip] + step + chips) % chips
        ]

    def both(piece, source, per, part):
        other = permuted(piece, [(i, i ^ 1) for i in range(count)])
        return [
            (piece, (2 * source + core) * per + part),
            (other, (2 * source + 1 - core) * per + part),
        ]

    groups = [both(weight, chip, 1, 0)]
    up = down = weight
    for step in range(1, chips // 2):
        up, down = permuted(up, along(1)), permuted(down, along(-1))
        groups.append(both(up, origin(-step), 1, 0) + both(down, origin(step), 1, 0))
    half = weight.shape[0] // 2
    up, down = permuted(up[:half], along(1)), permuted(down[half:], along(-1))
    far = origin(chips // 2)
    groups.append(both(up, far, 2, 0) + both(down, far, 2, 1))
    return groups


def stripes_kernel(where, cot, grad, down, *rest):
    out = rest[-1]
    rank = grad.shape[1]

    def product(weight):
        frozen = dot(cot[...], weight[...], ((1,), (1,)))
        for b in range(cot.shape[0] // BLOCK):
            rows = slice(b * BLOCK, (b + 1) * BLOCK)
            lora = adapter_scale * dot(
                grad[rows, :], down[b * rank : (b + 1) * rank, :], ((1,), (0,))
            )
            lora = lora.astype(jnp.bfloat16).astype(jnp.float32)
            out[rows, :] = (frozen[rows] + lora).astype(jnp.bfloat16)

    for number in range(where.shape[0]):
        pl.when(pl.program_id(0) == number)(lambda weight=rest[number]: product(weight))


def write_stripes(group, cot, grad, down, out=None):
    rows, depth = cot.shape
    width = down.shape[1]
    count = len(group)
    stripe = group[0][0].shape[0]
    where = jnp.stack([place for _, place in group]).astype(jnp.int32)
    specs = [
        pl.BlockSpec((rows, depth), lambda j, where: (0, 0)),
        pl.BlockSpec(grad.shape, lambda j, where: (0, 0)),
        pl.BlockSpec((down.shape[0], stripe), lambda j, where: (0, where[j])),
    ] + [pl.BlockSpec((stripe, depth), lambda j, where: (0, 0)) for _ in group]
    args = [where, cot, grad, down] + [piece for piece, _ in group]
    alias = {}
    if out is not None:
        specs.append(pl.BlockSpec(memory_space=pl.ANY))
        args.append(out)
        alias = {len(args) - 1: 0}
    return pl.pallas_call(
        stripes_kernel,
        grid_spec=pltpu.PrefetchScalarGridSpec(
            num_scalar_prefetch=1,
            grid=(count,),
            in_specs=specs,
            out_specs=pl.BlockSpec((rows, stripe), lambda j, where: (0, where[j])),
        ),
        out_shape=jax.ShapeDtypeStruct((rows, width), jnp.bfloat16),
        input_output_aliases=alias,
        cost_estimate=pl.CostEstimate(
            flops=2 * rows * depth * stripe * count,
            bytes_accessed=2 * (depth + rows) * stripe * count,
            transcendentals=0,
        ),
        compiler_params=pltpu.CompilerParams(vmem_limit_bytes=32 << 20),
    )(*args)


def small_stripes(groups, cot, grad, down, rank):
    depth = cot.shape[1]
    weight = jnp.zeros((down.shape[1], depth), jnp.bfloat16)
    for piece, place in sum(groups, []):
        weight = lax.dynamic_update_slice(weight, piece, (place * piece.shape[0], 0))
    lora = [
        dot(
            grad[b * BLOCK : (b + 1) * BLOCK], down[b * rank : (b + 1) * rank], ((1,), (0,))
        )
        for b in range(cot.shape[0] // BLOCK)
    ]
    lora = (adapter_scale * jnp.concatenate(lora, axis=0)).astype(jnp.bfloat16)
    out = dot(cot, weight, ((1,), (1,)))
    return (out + lora.astype(jnp.float32)).astype(jnp.bfloat16)


def slot_chunks(width):
    size = min(width, 768)
    while width % size:
        size -= LANES
    return [slice(k, k + size) for k in range(0, width, size)]


def own_rows(slot, first, size, rank):
    index = first // rank + lax.broadcasted_iota(jnp.int32, (size // rank, rank, 1), 0)
    return index == slot[...][None]


def hidden_kernel(act, maps, slot, out):
    rank = out.shape[0]
    tokens = out.shape[1] // act.shape[0]
    rows = jnp.concatenate([act[k, :tokens, :] for k in range(act.shape[0])], axis=0)
    total = jnp.zeros(out.shape, jnp.float32)
    for part in slot_chunks(maps.shape[0]):
        size = part.stop - part.start
        each = dot(maps[part, :], rows, ((1,), (1,))).reshape(size // rank, rank, -1)
        total += jnp.sum(
            jnp.where(own_rows(slot, part.start, size, rank), each, 0.0), axis=0
        )
    out[...] = total


def down_kernel(act, grad, slot, out, total):
    rank = grad.shape[0]
    tokens = grad.shape[1] // act.shape[0]
    rows = jnp.concatenate([act[k, :tokens, :] for k in range(act.shape[0])], axis=0)
    step = pl.program_id(0)

    @pl.when(step == 0)
    def _():
        total[...] = jnp.zeros_like(total)

    wide = grad[...].astype(jnp.float32)[None]
    for part in slot_chunks(total.shape[0]):
        size = part.stop - part.start
        placed = jnp.where(own_rows(slot, part.start, size, rank), wide, 0.0)
        placed = placed.reshape(size, -1).astype(jnp.bfloat16)
        total[part, :] += dot(placed, rows, ((1,), (0,)))

    @pl.when(step == pl.num_programs(0) - 1)
    def _():
        out[...] = (adapter_scale * total[...]).astype(out.dtype)


def feature_calls(devices, tokens, packed, features, width, rank):
    pair = 2
    while pair * tokens % LANES:
        pair *= 2
    grid = (devices // pair,)
    act = pl.BlockSpec((pair, packed, features), lambda j: (j, 0, 0))
    slot = pl.BlockSpec((1, pair * tokens), lambda j: (0, j))
    small = pl.BlockSpec((rank, pair * tokens), lambda j: (0, j))
    whole = pl.BlockSpec((width, features), lambda j: (0, 0))
    every = devices * tokens
    cost = pl.CostEstimate(
        flops=2 * every * width * features,
        bytes_accessed=2 * every * features,
        transcendentals=0,
    )
    params = pltpu.CompilerParams(vmem_limit_bytes=48 << 20)
    hidden = pl.pallas_call(
        hidden_kernel,
        grid=grid,
        in_specs=[act, whole, slot],
        out_specs=small,
        out_shape=jax.ShapeDtypeStruct((rank, every), jnp.float32),
        cost_estimate=cost,
        compiler_params=params,
    )
    down = pl.pallas_call(
        down_kernel,
        grid=grid,
        in_specs=[act, small, slot],
        out_specs=whole,
        out_shape=jax.ShapeDtypeStruct((width, features), jnp.bfloat16),
        scratch_shapes=[pltpu.VMEM((width, features), jnp.float32)],
        cost_estimate=cost,
        compiler_params=params,
    )
    return hidden, down


def local(
    activations,
    cotangent,
    token_layout_row,
    tenant_first_row,
    frozen_value_weight,
    adapter_down_maps,
    adapter_up_maps,
):
    devices = lax.axis_size("blk")
    device = lax.axis_index("blk")
    tokens = activations.shape[0]
    resident, rank, width = adapter_down_maps.shape
    out_width = cotangent.shape[1]
    features = width // devices
    resident_rows = resident * BLOCK
    slots = resident * devices
    slot_cap = resident_rows // devices
    start_ids = tenant_first_row // BLOCK

    groups = ring_shards(frozen_value_weight)

    padded = -(-tokens // LANES) * LANES
    digits = as_digits(jnp.pad(token_layout_row, (0, padded - tokens)))
    digits = digits.reshape(-1, LANES)
    count = digits.shape[0]
    digits = jnp.pad(digits, ((0, resident * rank - count), (0, 0)))
    shared = jnp.concatenate([adapter_up_maps.reshape(-1, out_width), digits], axis=1)
    shared = lax.all_gather(shared, "blk", axis=0, tiled=False)
    up_all = shared[:, :, :out_width].reshape(slots * rank, out_width)
    rows_all = shared[:, :count, out_width:].reshape(devices, 3, padded)[:, :, :tokens]
    rows_all = from_digits(rows_all.transpose(1, 0, 2)).reshape(-1)

    target = token_layout_row // resident_rows
    order = jnp.arange(tokens, dtype=jnp.int32)
    before = (target[:, None] == target[None, :]) & (order[None, :] < order[:, None])
    place = target * slot_cap + jnp.sum(before.astype(jnp.int32), axis=1)
    places = jnp.arange(resident_rows, dtype=jnp.int32)
    send = (places[:, None] == place[None, :]).astype(jnp.bfloat16)
    send_cot = dot(send, cotangent, ((1,), (0,))).astype(jnp.bfloat16)
    send_cot = send_cot.reshape(devices, slot_cap, out_width)
    folds = out_width // features
    packed = [
        activations.reshape(tokens, devices, features).transpose(1, 0, 2),
        adapter_down_maps.reshape(-1, devices, features).transpose(1, 0, 2),
    ] + [send_cot[:, :, k * features : (k + 1) * features] for k in range(folds)]
    packed = jnp.concatenate(packed, axis=1)
    received = lax.all_to_all(packed, "blk", split_axis=0, concat_axis=0)
    maps_f = received[:, tokens : tokens + resident * rank].reshape(slots * rank, features)
    recv_cot = received[:, tokens + resident * rank :]
    recv_cot = [
        recv_cot[:, k * slot_cap : (k + 1) * slot_cap].reshape(resident_rows, features)
        for k in range(folds)
    ]

    first_row = device * resident_rows
    row_of = (rows_all[None, :] - first_row == places[:, None]).astype(jnp.bfloat16)
    mine = (rows_all // resident_rows == device).reshape(devices, tokens)
    earlier = (order[:, None] < order[None, :]).astype(jnp.bfloat16)
    at = dot(mine.astype(jnp.bfloat16), earlier, ((1,), (0,))).astype(jnp.int32)
    at = at + slot_cap * jnp.arange(devices, dtype=jnp.int32)[:, None]
    at = jnp.where(mine, at, -1).reshape(-1)
    arrange = dot(
        row_of, (at[:, None] == places[None, :]).astype(jnp.bfloat16), ((1,), (0,))
    ).astype(jnp.bfloat16)
    cot_rows = jnp.concatenate(
        [dot(arrange, part, ((1,), (0,))).astype(jnp.bfloat16) for part in recv_cot], axis=1
    )

    own_slot = starts_of(token_layout_row // BLOCK, start_ids)
    every_up = dot(up_all, cotangent, ((1,), (1,))).reshape(slots, rank, tokens)
    own = jnp.arange(slots, dtype=jnp.int32)[:, None, None] == own_slot[None, None, :]
    grad_in = jnp.sum(jnp.where(own, every_up, 0.0), axis=0).astype(jnp.bfloat16)
    grad_all = to_all(grad_in).transpose(1, 0, 2).reshape(rank, -1)

    slot_all = starts_of(rows_all // BLOCK, start_ids)[None]
    hidden_call, down_call = feature_calls(
        devices, tokens, packed.shape[1], features, slots * rank, rank
    )
    hidden = hidden_call(received, maps_f, slot_all)
    hidden = hidden.reshape(rank, devices, tokens).transpose(1, 0, 2)
    hidden = lax.all_to_all(hidden, "blk", split_axis=0, concat_axis=0)
    hidden = to_all(jnp.sum(hidden, axis=0).astype(jnp.bfloat16))
    hidden = hidden.transpose(1, 0, 2).reshape(rank, -1)
    down_f = down_call(received, grad_all, slot_all)
    down_home = lax.all_to_all(down_f, "blk", split_axis=0, concat_axis=1, tiled=True)
    down_map_gradient = down_home.astype(jnp.float32).reshape(resident, rank, width)

    first_block = device * resident
    block_numbers = first_block + jnp.arange(resident, dtype=jnp.int32)
    begin = starts_of(block_numbers, start_ids)
    is_local = (begin >= first_block) & (begin <= block_numbers)
    home_slot = jnp.clip(begin - first_block, 0, resident - 1)
    last_map = lax.dynamic_index_in_dim(
        adapter_down_maps, home_slot[resident - 1], 0, keepdims=False
    )
    carried = jnp.zeros_like(last_map)
    for step in range(1, HOPS + 1):
        home = (device - step) % devices
        carried = jnp.where(begin[0] // resident == home, moved(last_map, step), carried)

    grad_rows = dot(row_of, grad_all, ((1,), (1,))).astype(jnp.bfloat16)
    hidden_rows = dot(row_of, hidden, ((1,), (1,))).astype(jnp.bfloat16)
    down_blocks = []
    up_parts = []
    for b in range(resident):
        rows = slice(b * BLOCK, (b + 1) * BLOCK)
        down = carried
        for k in range(b + 1):
            down = jnp.where(is_local[b] & (home_slot[b] == k), adapter_down_maps[k], down)
        down_blocks.append(down)
        up_parts.append(dot(hidden_rows[rows], cot_rows[rows], ((0,), (0,))))
    down_blocks = jnp.concatenate(down_blocks, axis=0)

    tail = sum(jnp.where(is_local[b], 0.0, up_parts[b]) for b in range(resident))
    far = jnp.zeros_like(tail)
    for step in range(1, HOPS + 1):
        other = (device + step) % devices * resident
        theirs = starts_of(other[None], start_ids)[0]
        far = far + jnp.where(theirs // resident == device, moved(tail, -step), 0.0)
    up_grads = []
    for k in range(resident):
        total = jnp.where(begin[resident - 1] == first_block + k, far, 0.0)
        for b in range(resident):
            total = total + jnp.where(is_local[b] & (home_slot[b] == k), up_parts[b], 0.0)
        up_grads.append(adapter_scale * total)
    up_map_gradient = jnp.stack(up_grads)

    if frozen_value_weight.shape[0] % (2 * LANES) == 0:
        out = None
        for group in groups:
            out = write_stripes(group, cot_rows, grad_rows, down_blocks, out)
    else:
        out = small_stripes(groups, cot_rows, grad_rows, down_blocks, rank)
    return (out, down_map_gradient, up_map_gradient)


def solution(mesh):
    return jax.shard_map(
        local,
        mesh=mesh,
        in_specs=(
            P(("groups", "blk"), None),
            P(("groups", "blk"), None),
            P(("groups", "blk")),
            P("groups"),
            P("blk", None),
            P(("groups", "blk"), None, None),
            P(("groups", "blk"), None, None),
        ),
        out_specs=(
            P(("groups", "blk"), None),
            P(("groups", "blk"), None, None),
            P(("groups", "blk"), None, None),
        ),
        check_vma=False,
    )
```

time: 410 us -> 379 us (0.924); the launches traced: 409 us -> 373 us
  blocking collectives: 249 us -> 0 us
  waiting for transfers between devices: 27.1 us -> 159 us
  Pallas kernels: 0 us -> 43.3 us
  starting transfers between devices: 33.7 us -> 72.2 us
  matrix products: 44.6 us -> 10.1 us
  local copies, waits for them, and re-layouts: 9.93 us -> 26.6 us
  between operations: 39.4 us -> 48.6 us
  other arithmetic: 4.84 us -> 13.7 us
    unnamed x1 -> x0, blocking collectives: 164 us -> none
    ppermute x8 -> x25, waiting for transfers between devices: 2.68 us -> 119 us  [permuted(): return lax.ppermute(value, 'blk', pairs)]
    psum x1 -> x0, blocking collectives: 59.6 us -> none  [local(): hidden = lax.psum(hidden, 'blk').astype(jnp.bfloat16)]
    pallas_call x0 -> x7, Pallas kernels: none -> 43.3 us  [the longest x5 28.3 us: write_stripes(): pl.pallas_call(stripes_kernel, grid_spec=pltpu.PrefetchScalarGridSpec(num...]
    ppermute x8 -> x25, starting transfers between devices: 11.2 us -> 46 us  [permuted(): return lax.ppermute(value, 'blk', pairs)]
    dot_general x17 -> x11, matrix products: 44.6 us -> 10.1 us  [dot(): lax.dot_general(a, b, (dims, ((), ())), preferred_element_type=jnp.float32)]
    all_gather x2 -> x1, waiting for transfers between devices: 0.02 us -> 33.9 us  [local(): shared = lax.all_gather(shared, 'blk', axis=0, tiled=False)]
    all_gather x1 -> x0, blocking collectives: 25.4 us -> none  [local(): grad_all = lax.all_gather(grad_in, 'blk', axis=0, tiled=True)]
  transfers between devices with their start and end apart: 14 -> 31, of which waited for: 4 -> 7; matrix products, arithmetic and copies ran while one was open for 11% -> 11% of each run, Pallas kernels for 0% -> 12%
where the time goes in v2:
time: 379 us; the launch traced here: 373 us
  waiting for transfers between devices  159 us (42%)
  starting transfers between devices  72.2 us (19%)
  between operations  48.6 us (13%)
  Pallas kernels  43.3 us (11%)
  local copies, waits for them, and re-layouts  26.6 us (7%)
  other arithmetic  13.7 us (4%)
  matrix products  10.1 us (3%)
    ppermute x25, waiting for transfers between devices, permuted(): return lax.ppermute(value, 'blk', pairs)  119 us
    ppermute x25, starting transfers between devices, permuted(): return lax.ppermute(value, 'blk', pairs)  46 us
    all_gather x1, waiting for transfers between devices, local(): shared = lax.all_gather(shared, 'blk', axis=0, tiled=False)  33.9 us
    pallas_call x5, Pallas kernels, write_stripes(): pl.pallas_call(stripes_kernel, grid_spec=pltpu.PrefetchScalarGridSpec(num...  28.3 us
    dot_general x11, matrix products, dot(): lax.dot_general(a, b, (dims, ((), ())), preferred_element_type=jnp.float32)  10.1 us
    all_to_all x2, starting transfers between devices, to_all(): return lax.all_to_all(copies, 'blk', split_axis=0, concat_axis=0)  9.97 us
  transfers between devices with their start and end apart: 31, of which 7 were waited for; matrix products, arithmetic and copies ran while one was open for 11% of the time, Pallas kernels for 12%

profile of v2, /device:TPU:1, one launch (start us, length us, event | category | flops | bytes accessed | tf_op | source)
XLA Modules:
  0.0 373.4 jit_solution(10418591656522139498)
XLA Ops:
  8.0 1.5 fusion.26
  9.6 2.2 collective-permute-start.4
  11.8 2.3 copy.59
  17.2 4.4 %pad_maximum_fusion = bf16[16,288,512]{2,1,0:T(8,128)(2,1)} fusion(bf16[16,24,512]{2,1,0:T(8,128)(2,1)S(1)} %get-tuple-element.20, bf16[16,24,512]{2,1,0:T(8,128)(2,1)S(1)} %get-tuple-element.19, bf16[16,48,512]{2,1,0:T(8,128)(2,1)S(1)} %bitcast.142, bf16[16,192,512]{2,1,0:T(8,128)(2,1)S(1)} %bitcast.140), kind=kLoop, calls=%fused_computation | loop fusion | flops 18874368 | bytes 9437184 | tf_op jit(solution)/shard_map/concatenate | solution.py:293
  21.6 33.9 %all-gather.3.cloned.1.call-done = bf16[768,1152]{1,0:T(8,128)(2,1)} async-done(((bf16[48,1152]{1,0:T(8,128)(2,1)}), bf16[768,1152]{1,0:T(8,128)(2,1)}) %all-gather.3.cloned.1.call-update) | async-done | bytes 1769488 | tf_op jit(solution)/shard_map/all_gather | solution.py:275
  55.5 1.6 slice.153
  58.3 3.6 all-to-all-start.1
  62.5 6.3 %all-to-all-done.1 = bf16[16,16,192]{2,1,0:T(8,128)(2,1)S(1)} async-done(((bf16[16,16,192]{2,1,0:T(8,128)(2,1)}), bf16[16,16,192]{2,1,0:T(8,128)(2,1)S(1)}, u32[]{:S(2)}, u32[]{:S(2)}) %all-to-all-start.1) | async-done | bytes 98336 | tf_op jit(solution)/shard_map/all_to_all | solution.py:28
  68.8 5.5 %all-to-all-start = ((bf16[16,288,512]{2,1,0:T(8,128)(2,1)}), bf16[16,288,512]{2,1,0:T(8,128)(2,1)}, u32[]{:S(2)}, u32[]{:S(2)}) async-start(bf16[16,288,512]{2,1,0:T(8,128)(2,1)} %pad_maximum_fusion), calls=%async_computation | async-start | bytes 9437184 | tf_op jit(solution)/shard_map/all_to_all | solution.py:294
  77.7 1.4 collective-permute-start
  79.1 1.7 collective-permute-start.1
  80.8 1.2 collective-permute-start.2
  92.1 68.3 %collective-permute-done = bf16[16,8192]{1,0:T(8,128)(2,1)S(1)} collective-permute-done((bf16[16,8192]{1,0:T(8,128)(2,1)}, bf16[16,8192]{1,0:T(8,128)(2,1)S(1)}, u32[]{:S(2)}, u32[]{:S(2)}) %collective-permute-start) | collective-permute-done | bytes 262176 | tf_op jit(solution)/shard_map/ppermute | solution.py:17
  160.4 2.3 collective-permute-start.3
  187.7 22.6 %collective-permute-start.5 = (bf16[512,1024]{1,0:T(8,128)(2,1)}, bf16[512,1024]{1,0:T(8,128)(2,1)}, u32[]{:S(2)}, u32[]{:S(2)}) collective-permute-start(bf16[512,1024]{1,0:T(8,128)(2,1)} %collective-permute-done.4.rest_0_), channel_id=1, source_target_pairs={{0,4},{1,5},{2,0},{3,1},{4,8},{5,9},{6,2},{7,3},{8,12},{9,13},{10,... | collective-permute-start | bytes 3145736 | tf_op jit(solution)/shard_map/ppermute | solution.py:17
  210.5 23.3 %collective-permute-done.5.rest_0_ = bf16[512,1024]{1,0:T(8,128)(2,1)} collective-permute-done((bf16[512,1024]{1,0:T(8,128)(2,1)}, bf16[512,1024]{1,0:T(8,128)(2,1)}, u32[]{:S(2)}, u32[]{:S(2)}) %collective-permute-start.5) | collective-permute-done | bytes 1048608 | tf_op jit(solution)/shard_map/ppermute | solution.py:17
  233.9 1.0 collective-permute-start.6
  236.1 1.3 collective-permute-start.18
  237.5 21.7 %collective-permute-done.11.rest_2_ = bf16[512,1024]{1,0:T(8,128)(2,1)} collective-permute-done((bf16[512,1024]{1,0:T(8,128)(2,1)}, bf16[512,1024]{1,0:T(8,128)(2,1)}, u32[]{:S(2)}, u32[]{:S(2)}) %collective-permute-start.11) | collective-permute-done | bytes 1048608 | tf_op jit(solution)/shard_map/ppermute | solution.py:17
  259.2 2.2 collective-permute-start.16
  261.4 1.9 slice.155
  266.0 2.3 fusion.7
  269.0 1.1 reshape.304.grad
  270.9 1.2 slice.156
  272.1 7.4 %shard_map.226 = f32[16,3072]{1,0:T(8,128)S(1)} custom-call(bf16[16,288,512]{2,1,0:T(8,128)(2,1)} %all-to-all-done.act, bf16[768,512]{1,0:T(8,128)(2,1)S(1)} %bitcast.139, s32[1,3072]{1,0:T(1,128)S(1)} %compare_select_fusion.slot), custom_call_target="tpu_custom_call" | custom-call | flops 2415919104 | bytes 3145728 | tf_op jit(solution)/shard_map/pallas_call | solution.py:326
  280.2 1.7 reshape.306
  281.9 1.8 copy.61
  283.7 4.6 %all-to-all-start.3 = ((f32[16,16,192]{2,1,0:T(8,128)}), f32[16,16,192]{2,1,0:T(8,128)}, u32[]{:S(2)}, u32[]{:S(2)}) async-start(f32[16,16,192]{2,1,0:T(8,128)} %bitcast.151), calls=%async_computation.3 | async-start | bytes 524288 | tf_op jit(solution)/shard_map/all_to_all | solution.py:328
  288.4 1.2 fusion.57
  290.1 1.3 convolution_convert_fusion.2
  291.5 1.5 convolution_convert_fusion.1
  292.9 1.4 collective-permute-start.12
  294.8 1.2 copy-done.2
  296.0 4.0 %shard_map.220.rest_4_ = bf16[384,8192]{1,0:T(8,128)(2,1)} custom-call(s32[2]{0:T(128)S(1)} %pad_add_fusion.4.where, bf16[384,1024]{1,0:T(8,128)(2,1)S(1)} %pad_maximum_fusion.1.cot, bf16[384,16]{1,0:T(8,128)(2,1)S(1)} %fusion.9.grad, bf16[48,8192]{1,0:T(8,128)(2,1)S(1)} %pad_maximum_fusion.2.down, bf16[512,1024]{1,0:T(8,128)(2,1)S(1)} %copy-done.2, ...), custom_call_target="tpu_custom_call" | custom-call | flops 805306368 | bytes 2883584 | tf_op jit(solution)/shard_map/pallas_call | solution.py:126
  300.0 6.6 %shard_map.221.rest_4_ = bf16[384,8192]{1,0:T(8,128)(2,1)} custom-call(s32[4]{0:T(128)S(1)} %pad_add_fusion.3.where, bf16[384,1024]{1,0:T(8,128)(2,1)S(1)} %pad_maximum_fusion.1.cot, bf16[384,16]{1,0:T(8,128)(2,1)S(1)} %fusion.9.grad, bf16[48,8192]{1,0:T(8,128)(2,1)S(1)} %pad_maximum_fusion.2.down, ...), custom_call_target="tpu_custom_call", output_to_operand_aliasing={{}: (8, {})} | custom-call | flops 1610612736 | bytes 5767168 | tf_op jit(solution)/shard_map/pallas_call | solution.py:126
  306.6 7.6 %shard_map.225 = bf16[768,512]{1,0:T(8,128)(2,1)S(1)} custom-call(bf16[16,288,512]{2,1,0:T(8,128)(2,1)} %all-to-all-done.act, bf16[16,3072]{1,0:T(8,128)(2,1)S(1)} %reshape.304.grad, s32[1,3072]{1,0:T(1,128)S(1)} %compare_select_fusion.slot), custom_call_target="tpu_custom_call" | custom-call | flops 2415919104 | bytes 3145728 | tf_op jit(solution)/shard_map/pallas_call | solution.py:331
  315.0 1.0 reduce_sum.29
  316.7 6.4 %all-to-all-start.4 = ((bf16[16,16,192]{2,1,0:T(8,128)(2,1)}), bf16[16,16,192]{2,1,0:T(8,128)(2,1)S(1)}, u32[]{:S(2)}, u32[]{:S(2)}) async-start(bf16[16,16,192]{2,1,0:T(8,128)(2,1)} %broadcast_in_dim.149), calls=%async_computation.4 | async-start | bytes 262144 | tf_op jit(solution)/shard_map/all_to_all | solution.py:28
  323.7 6.6 %shard_map.222.rest_4_ = bf16[384,8192]{1,0:T(8,128)(2,1)} custom-call(s32[4]{0:T(128)S(1)} %pad_add_fusion.2.where, bf16[384,1024]{1,0:T(8,128)(2,1)S(1)} %pad_maximum_fusion.1.cot, bf16[384,16]{1,0:T(8,128)(2,1)S(1)} %fusion.9.grad, bf16[48,8192]{1,0:T(8,128)(2,1)S(1)} %pad_maximum_fusion.2.down, ...), custom_call_target="tpu_custom_call", output_to_operand_aliasing={{}: (8, {})} | custom-call | flops 1610612736 | bytes 5767168 | tf_op jit(solution)/shard_map/pallas_call | solution.py:126
  330.3 6.2 %shard_map.223.rest_4_ = bf16[384,8192]{1,0:T(8,128)(2,1)} custom-call(s32[4]{0:T(128)S(1)} %pad_add_fusion.1.where, bf16[384,1024]{1,0:T(8,128)(2,1)S(1)} %pad_maximum_fusion.1.cot, bf16[384,16]{1,0:T(8,128)(2,1)S(1)} %fusion.9.grad, bf16[48,8192]{1,0:T(8,128)(2,1)S(1)} %pad_maximum_fusion.2.down, ...), custom_call_target="tpu_custom_call", output_to_operand_aliasing={{}: (8, {})} | custom-call | flops 1610612736 | bytes 5767168 | tf_op jit(solution)/shard_map/pallas_call | solution.py:126
  336.5 6.2 %all-to-all-start.2 = ((bf16[16,48,512]{2,1,0:T(8,128)(2,1)}), bf16[16,48,512]{2,1,0:T(8,128)(2,1)}, u32[]{:S(2)}, u32[]{:S(2)}) async-start(bf16[16,48,512]{2,1,0:T(8,128)(2,1)} %bitcast.138), calls=%async_computation.2 | async-start | bytes 1572864 | tf_op jit(solution)/shard_map/all_to_all | solution.py:332
  344.0 2.0 select_add_fusion.1
  346.2 4.3 %collective-permute-start.22 = (f32[16,1024]{1,0:T(8,128)S(1)}, f32[16,1024]{1,0:T(8,128)S(1)}, u32[]{:S(2)}, u32[]{:S(2)}) collective-permute-start(f32[16,1024]{1,0:T(8,128)S(1)} %get-tuple-element.45), channel_id=1, source_target_pairs={{0,14},{1,15},{2,0},{3,1},{4,2},{5,3},{6,4},{7,5},{8,6},{9,7},{10,... | collective-permute-start | bytes 196616 | tf_op jit(solution)/shard_map/ppermute | solution.py:17
  350.5 1.7 collective-permute-start.23
  352.5 4.9 %shard_map.224 = bf16[384,8192]{1,0:T(8,128)(2,1)} custom-call(s32[4]{0:T(128)S(1)} %pad_add_fusion.where, bf16[384,1024]{1,0:T(8,128)(2,1)S(1)} %pad_maximum_fusion.1.cot, bf16[384,16]{1,0:T(8,128)(2,1)S(1)} %fusion.9.grad, bf16[48,8192]{1,0:T(8,128)(2,1)S(1)} %pad_maximum_fusion.2.down, ...), custom_call_target="tpu_custom_call", output_to_operand_aliasing={{}: (8, {})} | custom-call | flops 805306368 | bytes 2883584 | tf_op jit(solution)/shard_map/pallas_call | solution.py:126
  357.4 4.6 %collective-permute-done.23 = f32[16,1024]{1,0:T(8,128)S(1)} collective-permute-done((f32[16,1024]{1,0:T(8,128)S(1)}, f32[16,1024]{1,0:T(8,128)S(1)}, u32[]{:S(2)}, u32[]{:S(2)}) %collective-permute-start.23) | collective-permute-done | bytes 65568 | tf_op jit(solution)/shard_map/ppermute | solution.py:17
  362.9 1.3 convert_bitcast_fusion
  365.1 1.4 reshape.313
  (129 shorter events, 23.1 us)
Async XLA Ops:
  7.2 9.6 %copy-start = (bf16[192,1024]{1,0:T(8,128)(2,1)S(1)}, bf16[192,1024]{1,0:T(8,128)(2,1)}, u32[]{:S(2)}) copy-start(bf16[192,1024]{1,0:T(8,128)(2,1)} %param.22) | copy-start | bytes 1179652
  7.2 48.3 %all-gather.3.cloned.1.call-start = ((), (), s32[]{:S(2)}) async-start(), calls=%async_computation.5 | async-start | bytes 1880064 | tf_op jit(solution)/shard_map/all_gather | solution.py:275
  9.6 178.1 %collective-permute-start.4 = (bf16[512,1024]{1,0:T(8,128)(2,1)}, bf16[512,1024]{1,0:T(8,128)(2,1)}, u32[]{:S(2)}, u32[]{:S(2)}) collective-permute-start(bf16[512,1024]{1,0:T(8,128)(2,1)} %rest_0_.1), channel_id=1, source_target_pairs={{0,4},{1,5},{2,0},{3,1},{4,8},{5,9},{6,2},{7,3},{8,12},{9,13},{10,... | collective-permute-start | bytes 3145736 | tf_op jit(solution)/shard_map/ppermute | solution.py:17
  11.8 198.5 %collective-permute-start.9 = (bf16[512,1024]{1,0:T(8,128)(2,1)}, bf16[512,1024]{1,0:T(8,128)(2,1)}, u32[]{:S(2)}, u32[]{:S(2)}) collective-permute-start(bf16[512,1024]{1,0:T(8,128)(2,1)} %rest_0_.1), channel_id=1, source_target_pairs={{0,2},{1,3},{2,6},{3,7},{4,0},{5,1},{6,10},{7,11},{8,4},{9,5},{10,... | collective-permute-start | bytes 3145736 | tf_op jit(solution)/shard_map/ppermute | solution.py:17
  11.8 2.3 copy-start.9
  14.1 0.7 copy-start.12
  14.1 1.7 copy-start.11
  58.3 10.5 %all-to-all-start.1 = ((bf16[16,16,192]{2,1,0:T(8,128)(2,1)}), bf16[16,16,192]{2,1,0:T(8,128)(2,1)S(1)}, u32[]{:S(2)}, u32[]{:S(2)}) async-start(bf16[16,16,192]{2,1,0:T(8,128)(2,1)} %broadcast_in_dim.141), calls=%async_computation.1 | async-start | bytes 262144 | tf_op jit(solution)/shard_map/all_to_all | solution.py:28
  62.4 19.6 %copy-start.13 = (s32[8]{0:T(128)S(1)}, s32[8]{0:T(128)}, u32[]{:S(2)}) copy-start(s32[8]{0:T(128)} %constant.302.clone) | copy-start | bytes 100
  62.5 24.8 %copy-start.10 = (s32[8]{0:T(128)S(1)}, s32[8]{0:T(128)}, u32[]{:S(2)}) copy-start(s32[8]{0:T(128)} %constant.301.clone) | copy-start | bytes 100
  62.5 125.2 %copy-start.1 = (bf16[512,1024]{1,0:T(8,128)(2,1)S(1)}, bf16[512,1024]{1,0:T(8,128)(2,1)}, u32[]{:S(2)}) copy-start(bf16[512,1024]{1,0:T(8,128)(2,1)} %rest_0_.1) | copy-start | bytes 3145732
  68.8 202.1 %all-to-all-start = ((bf16[16,288,512]{2,1,0:T(8,128)(2,1)}), bf16[16,288,512]{2,1,0:T(8,128)(2,1)}, u32[]{:S(2)}, u32[]{:S(2)}) async-start(bf16[16,288,512]{2,1,0:T(8,128)(2,1)} %pad_maximum_fusion), calls=%async_computation | async-start | bytes 9437184 | tf_op jit(solution)/shard_map/all_to_all | solution.py:294
  77.7 82.7 %collective-permute-start = (bf16[16,8192]{1,0:T(8,128)(2,1)}, bf16[16,8192]{1,0:T(8,128)(2,1)S(1)}, u32[]{:S(2)}, u32[]{:S(2)}) collective-permute-start(bf16[16,8192]{1,0:T(8,128)(2,1)} %dynamic-slice_bitcast_fusion), channel_id=1, source_target_pairs={{0,4},{1,5},{2,6},{3,7},{4,8},{5,9},{6,10},{7,11},{8,12},{9,13},{1... | collective-permute-start | bytes 786440 | tf_op jit(solution)/shard_map/ppermute | solution.py:17
  79.1 108.5 %collective-permute-start.1 = (bf16[16,8192]{1,0:T(8,128)(2,1)}, bf16[16,8192]{1,0:T(8,128)(2,1)S(1)}, u32[]{:S(2)}, u32[]{:S(2)}) collective-permute-start(bf16[16,8192]{1,0:T(8,128)(2,1)} %dynamic-slice_bitcast_fusion), channel_id=1, source_target_pairs={{0,3},{1,4},{2,5},{3,6},{4,7},{5,8},{6,9},{7,10},{8,11},{9,12},{10... | collective-permute-start | bytes 786440 | tf_op jit(solution)/shard_map/ppermute | solution.py:17
  80.8 129.6 %collective-permute-start.2 = (bf16[16,8192]{1,0:T(8,128)(2,1)}, bf16[16,8192]{1,0:T(8,128)(2,1)S(1)}, u32[]{:S(2)}, u32[]{:S(2)}) collective-permute-start(bf16[16,8192]{1,0:T(8,128)(2,1)} %dynamic-slice_bitcast_fusion), channel_id=1, source_target_pairs={{0,2},{1,3},{2,4},{3,5},{4,6},{5,7},{6,8},{7,9},{8,10},{9,11},{10,... | collective-permute-start | bytes 786440 | tf_op jit(solution)/shard_map/ppermute | solution.py:17
  160.4 50.1 %collective-permute-start.3 = (bf16[16,8192]{1,0:T(8,128)(2,1)}, bf16[16,8192]{1,0:T(8,128)(2,1)S(1)}, u32[]{:S(2)}, u32[]{:S(2)}) collective-permute-start(bf16[16,8192]{1,0:T(8,128)(2,1)} %dynamic-slice_bitcast_fusion), channel_id=1, source_target_pairs={{0,1},{1,2},{2,3},{3,4},{4,5},{5,6},{6,7},{7,8},{8,9},{9,10},{10,1... | collective-permute-start | bytes 786440 | tf_op jit(solution)/shard_map/ppermute | solution.py:17
  187.6 101.9 %collective-permute-start.20 = (bf16[512,1024]{1,0:T(8,128)(2,1)S(1)}, bf16[512,1024]{1,0:T(8,128)(2,1)}, u32[]{:S(2)}, u32[]{:S(2)}) collective-permute-start(bf16[512,1024]{1,0:T(8,128)(2,1)S(1)} %copy-done.1), channel_id=1, source_target_pairs={{0,1},{1,0},{2,3},{3,2},{4,5},{5,4},{6,7},{7,6},{8,9},{9,8},{10,11... | collective-permute-start | bytes 3145736 | tf_op jit(solution)/shard_map/ppermute | solution.py:17
  187.7 46.2 %collective-permute-start.5 = (bf16[512,1024]{1,0:T(8,128)(2,1)}, bf16[512,1024]{1,0:T(8,128)(2,1)}, u32[]{:S(2)}, u32[]{:S(2)}) collective-permute-start(bf16[512,1024]{1,0:T(8,128)(2,1)} %collective-permute-done.4.rest_0_), channel_id=1, source_target_pairs={{0,4},{1,5},{2,0},{3,1},{4,8},{5,9},{6,2},{7,3},{8,12},{9,13},{10,... | collective-permute-start | bytes 3145736 | tf_op jit(solution)/shard_map/ppermute | solution.py:17
  210.3 25.2 %collective-permute-start.10 = (bf16[512,1024]{1,0:T(8,128)(2,1)}, bf16[512,1024]{1,0:T(8,128)(2,1)}, u32[]{:S(2)}, u32[]{:S(2)}) collective-permute-start(bf16[512,1024]{1,0:T(8,128)(2,1)} %collective-permute-done.9.rest_2_), channel_id=1, source_target_pairs={{0,2},{1,3},{2,6},{3,7},{4,0},{5,1},{6,10},{7,11},{8,4},{9,5},{10,... | collective-permute-start | bytes 3145736 | tf_op jit(solution)/shard_map/ppermute | solution.py:17
  233.9 29.4 %collective-permute-start.6 = (bf16[512,1024]{1,0:T(8,128)(2,1)}, bf16[512,1024]{1,0:T(8,128)(2,1)S(1)}, u32[]{:S(2)}, u32[]{:S(2)}) collective-permute-start(bf16[512,1024]{1,0:T(8,128)(2,1)} %collective-permute-done.5.rest_0_), channel_id=1, source_target_pairs={{0,4},{1,5},{2,0},{3,1},{4,8},{5,9},{6,2},{7,3},{8,12},{9,13},{10,... | collective-permute-start | bytes 3145736 | tf_op jit(solution)/shard_map/ppermute | solution.py:17
  235.5 23.7 %collective-permute-start.11 = (bf16[512,1024]{1,0:T(8,128)(2,1)}, bf16[512,1024]{1,0:T(8,128)(2,1)}, u32[]{:S(2)}, u32[]{:S(2)}) collective-permute-start(bf16[512,1024]{1,0:T(8,128)(2,1)} %collective-permute-done.10.rest_2_), channel_id=1, source_target_pairs={{0,2},{1,3},{2,6},{3,7},{4,0},{5,1},{6,10},{7,11},{8,4},{9,5},{10,... | collective-permute-start | bytes 3145736 | tf_op jit(solution)/shard_map/ppermute | solution.py:17
  236.1 53.7 %collective-permute-start.18 = (bf16[512,1024]{1,0:T(8,128)(2,1)}, bf16[512,1024]{1,0:T(8,128)(2,1)}, u32[]{:S(2)}, u32[]{:S(2)}) collective-permute-start(bf16[512,1024]{1,0:T(8,128)(2,1)} %collective-permute-done.4.rest_0_), channel_id=1, source_target_pairs={{0,1},{1,0},{2,3},{3,2},{4,5},{5,4},{6,7},{7,6},{8,9},{9,8},{10,11... | collective-permute-start | bytes 3145736 | tf_op jit(solution)/shard_map/ppermute | solution.py:17
  237.4 55.6 %collective-permute-start.19 = (bf16[512,1024]{1,0:T(8,128)(2,1)}, bf16[512,1024]{1,0:T(8,128)(2,1)}, u32[]{:S(2)}, u32[]{:S(2)}) collective-permute-start(bf16[512,1024]{1,0:T(8,128)(2,1)} %collective-permute-done.9.rest_2_), channel_id=1, source_target_pairs={{0,1},{1,0},{2,3},{3,2},{4,5},{5,4},{6,7},{7,6},{8,9},{9,8},{10,11... | collective-permute-start | bytes 3145736 | tf_op jit(solution)/shard_map/ppermute | solution.py:17
  259.2 35.2 %collective-permute-start.16 = (bf16[512,1024]{1,0:T(8,128)(2,1)}, bf16[512,1024]{1,0:T(8,128)(2,1)}, u32[]{:S(2)}, u32[]{:S(2)}) collective-permute-start(bf16[512,1024]{1,0:T(8,128)(2,1)} %collective-permute-done.5.rest_0_), channel_id=1, source_target_pairs={{0,1},{1,0},{2,3},{3,2},{4,5},{5,4},{6,7},{7,6},{8,9},{9,8},{10,11... | collective-permute-start | bytes 3145736 | tf_op jit(solution)/shard_map/ppermute | solution.py:17
  263.3 60.4 %collective-permute-start.17 = (bf16[512,1024]{1,0:T(8,128)(2,1)}, bf16[512,1024]{1,0:T(8,128)(2,1)}, u32[]{:S(2)}, u32[]{:S(2)}) collective-permute-start(bf16[512,1024]{1,0:T(8,128)(2,1)} %collective-permute-done.10.rest_2_), channel_id=1, source_target_pairs={{0,1},{1,0},{2,3},{3,2},{4,5},{5,4},{6,7},{7,6},{8,9},{9,8},{10,11... | collective-permute-start | bytes 3145736 | tf_op jit(solution)/shard_map/ppermute | solution.py:17
  279.5 0.7 copy-start.4
  283.7 31.3 %all-to-all-start.3 = ((f32[16,16,192]{2,1,0:T(8,128)}), f32[16,16,192]{2,1,0:T(8,128)}, u32[]{:S(2)}, u32[]{:S(2)}) async-start(f32[16,16,192]{2,1,0:T(8,128)} %bitcast.151), calls=%async_computation.3 | async-start | bytes 524288 | tf_op jit(solution)/shard_map/all_to_all | solution.py:328
  289.5 40.7 %collective-permute-start.14 = (bf16[512,1024]{1,0:T(8,128)(2,1)S(1)}, bf16[512,1024]{1,0:T(8,128)(2,1)}, u32[]{:S(2)}, u32[]{:S(2)}) collective-permute-start(bf16[512,1024]{1,0:T(8,128)(2,1)S(1)} %collective-permute-done.6.rest_0_), channel_id=1, source_target_pairs={{0,1},{1,0},{2,3},{3,2},{4,5},{5,4},{6,7},{7,6},{8,9},{9,8},{10,11... | collective-permute-start | bytes 3145736 | tf_op jit(solution)/shard_map/ppermute | solution.py:17
  289.8 40.5 %collective-permute-start.15 = (bf16[512,1024]{1,0:T(8,128)(2,1)}, bf16[512,1024]{1,0:T(8,128)(2,1)}, u32[]{:S(2)}, u32[]{:S(2)}) collective-permute-start(bf16[512,1024]{1,0:T(8,128)(2,1)} %collective-permute-done.11.rest_2_), channel_id=1, source_target_pairs={{0,1},{1,0},{2,3},{3,2},{4,5},{5,4},{6,7},{7,6},{8,9},{9,8},{10,11... | collective-permute-start | bytes 3145736 | tf_op jit(solution)/shard_map/ppermute | solution.py:17
  291.4 3.2 copy-start.5
  292.9 1.7 copy-start.7
  292.9 30.1 %collective-permute-start.12 = (bf16[256,1024]{1,0:T(8,128)(2,1)}, bf16[256,1024]{1,0:T(8,128)(2,1)}, u32[]{:S(2)}, u32[]{:S(2)}) collective-permute-start(bf16[256,1024]{1,0:T(8,128)(2,1)} %slice.155), channel_id=1, source_target_pairs={{0,2},{1,3},{2,6},{3,7},{4,0},{5,1},{6,10},{7,11},{8,4},{9,5},{10,... | collective-permute-start | bytes 1572872 | tf_op jit(solution)/shard_map/ppermute | solution.py:17
  294.4 28.9 %collective-permute-start.7 = (bf16[256,1024]{1,0:T(8,128)(2,1)}, bf16[256,1024]{1,0:T(8,128)(2,1)}, u32[]{:S(2)}, u32[]{:S(2)}) collective-permute-start(bf16[256,1024]{1,0:T(8,128)(2,1)} %slice.154), channel_id=1, source_target_pairs={{0,4},{1,5},{2,0},{3,1},{4,8},{5,9},{6,2},{7,3},{8,12},{9,13},{10,... | collective-permute-start | bytes 1572872 | tf_op jit(solution)/shard_map/ppermute | solution.py:17
  294.8 1.2 copy-start.2
  314.2 0.9 copy-start.3
  316.7 19.8 %all-to-all-start.4 = ((bf16[16,16,192]{2,1,0:T(8,128)(2,1)}), bf16[16,16,192]{2,1,0:T(8,128)(2,1)S(1)}, u32[]{:S(2)}, u32[]{:S(2)}) async-start(bf16[16,16,192]{2,1,0:T(8,128)(2,1)} %broadcast_in_dim.149), calls=%async_computation.4 | async-start | bytes 262144 | tf_op jit(solution)/shard_map/all_to_all | solution.py:28
  323.1 29.1 %collective-permute-start.13 = (bf16[256,1024]{1,0:T(8,128)(2,1)}, bf16[256,1024]{1,0:T(8,128)(2,1)}, u32[]{:S(2)}, u32[]{:S(2)}) collective-permute-start(bf16[256,1024]{1,0:T(8,128)(2,1)} %collective-permute-done.12.rest_2_), channel_id=1, source_target_pairs={{0,1},{1,0},{2,3},{3,2},{4,5},{5,4},{6,7},{7,6},{8,9},{9,8},{10,11... | collective-permute-start | bytes 1572872 | tf_op jit(solution)/shard_map/ppermute | solution.py:17
  323.3 29.2 %collective-permute-start.8 = (bf16[256,1024]{1,0:T(8,128)(2,1)}, bf16[256,1024]{1,0:T(8,128)(2,1)}, u32[]{:S(2)}, u32[]{:S(2)}) collective-permute-start(bf16[256,1024]{1,0:T(8,128)(2,1)} %collective-permute-done.7.rest_0_), channel_id=1, source_target_pairs={{0,1},{1,0},{2,3},{3,2},{4,5},{5,4},{6,7},{7,6},{8,9},{9,8},{10,11... | collective-permute-start | bytes 1572872 | tf_op jit(solution)/shard_map/ppermute | solution.py:17
  336.5 7.2 %copy-start.6 = (bf16[384,512]{1,0:T(8,128)(2,1)S(1)}, bf16[384,512]{1,0:T(8,128)(2,1)}, u32[]{:S(2)}) copy-start(bf16[384,512]{1,0:T(8,128)(2,1)} %copy-done.5) | copy-start | bytes 1179652
  336.5 7.2 %copy-start.8 = (bf16[384,512]{1,0:T(8,128)(2,1)S(1)}, bf16[384,512]{1,0:T(8,128)(2,1)}, u32[]{:S(2)}) copy-start(bf16[384,512]{1,0:T(8,128)(2,1)} %copy-done.7) | copy-start | bytes 1179652
  336.5 26.4 %all-to-all-start.2 = ((bf16[16,48,512]{2,1,0:T(8,128)(2,1)}), bf16[16,48,512]{2,1,0:T(8,128)(2,1)}, u32[]{:S(2)}, u32[]{:S(2)}) async-start(bf16[16,48,512]{2,1,0:T(8,128)(2,1)} %bitcast.138), calls=%async_computation.2 | async-start | bytes 1572864 | tf_op jit(solution)/shard_map/all_to_all | solution.py:332
  346.0 11.4 %collective-permute-start.21 = (f32[16,1024]{1,0:T(8,128)S(1)}, f32[16,1024]{1,0:T(8,128)S(1)}, u32[]{:S(2)}, u32[]{:S(2)}) collective-permute-start(f32[16,1024]{1,0:T(8,128)S(1)} %get-tuple-element.45), channel_id=1, source_target_pairs={{0,15},{1,0},{2,1},{3,2},{4,3},{5,4},{6,5},{7,6},{8,7},{9,8},{10,9... | collective-permute-start | bytes 196616 | tf_op jit(solution)/shard_map/ppermute | solution.py:17
  346.2 11.2 %collective-permute-start.22 = (f32[16,1024]{1,0:T(8,128)S(1)}, f32[16,1024]{1,0:T(8,128)S(1)}, u32[]{:S(2)}, u32[]{:S(2)}) collective-permute-start(f32[16,1024]{1,0:T(8,128)S(1)} %get-tuple-element.45), channel_id=1, source_target_pairs={{0,14},{1,15},{2,0},{3,1},{4,2},{5,3},{6,4},{7,5},{8,6},{9,7},{10,... | collective-permute-start | bytes 196616 | tf_op jit(solution)/shard_map/ppermute | solution.py:17
  350.5 11.5 %collective-permute-start.23 = (f32[16,1024]{1,0:T(8,128)S(1)}, f32[16,1024]{1,0:T(8,128)S(1)}, u32[]{:S(2)}, u32[]{:S(2)}) collective-permute-start(f32[16,1024]{1,0:T(8,128)S(1)} %get-tuple-element.45), channel_id=1, source_target_pairs={{0,13},{1,14},{2,15},{3,0},{4,1},{5,2},{6,3},{7,4},{8,5},{9,6},{10... | collective-permute-start | bytes 196616 | tf_op jit(solution)/shard_map/ppermute | solution.py:17
  352.2 9.9 %collective-permute-start.24 = (f32[16,1024]{1,0:T(8,128)S(1)}, f32[16,1024]{1,0:T(8,128)S(1)}, u32[]{:S(2)}, u32[]{:S(2)}) collective-permute-start(f32[16,1024]{1,0:T(8,128)S(1)} %get-tuple-element.45), channel_id=1, source_target_pairs={{0,12},{1,13},{2,14},{3,15},{4,0},{5,1},{6,2},{7,3},{8,4},{9,5},{1... | collective-permute-start | bytes 196616 | tf_op jit(solution)/shard_map/ppermute | solution.py:17
Sparse Core Ops, SparseCore 0:
  10.8 44.6 all-gather.2

commit v3 on v2

--- a/solution.py
+++ b/solution.py
@@ -158,6 +158,53 @@
     return (out + lora.astype(jnp.float32)).astype(jnp.bfloat16)
 
 
+def pack_kernel(rows, act, maps, cot, out):
+    tokens, features = act.shape
+    cap = (out.shape[1] - tokens - maps.shape[0]) * features // cot.shape[1]
+    target = pl.program_id(0)
+    resident_rows = cap * pl.num_programs(0)
+    mine = rows[...] // resident_rows == target
+    first = lax.broadcasted_iota(jnp.int32, (tokens, tokens), 0)
+    later = lax.broadcasted_iota(jnp.int32, (tokens, tokens), 1)
+    earlier = jnp.where(first < later, 1.0, 0.0).astype(jnp.bfloat16)
+    chosen = jnp.broadcast_to(jnp.where(mine, 1.0, 0.0), (8, tokens)).astype(jnp.bfloat16)
+    place = dot(chosen, earlier, ((1,), (0,)))[:1].astype(jnp.int32)
+    place = jnp.where(mine, place, -1)
+    send = lax.broadcasted_iota(jnp.int32, (cap, tokens), 0) == place
+    send = jnp.where(send, 1.0, 0.0).astype(jnp.bfloat16)
+    sent = [
+        dot(send, cot[:, k : k + features], ((1,), (0,)))
+        for k in range(0, cot.shape[1], features)
+    ]
+    out[0, :tokens, :] = act[...]
+    out[0, tokens : tokens + maps.shape[0], :] = maps[...]
+    out[0, tokens + maps.shape[0] :, :] = jnp.concatenate(sent, axis=0).astype(out.dtype)
+
+
+def pack(rows, act, maps, cot, devices, cap):
+    tokens, width = act.shape
+    features = width // devices
+    total = tokens + maps.shape[0] + cap * cot.shape[1] // features
+    return pl.pallas_call(
+        pack_kernel,
+        grid=(devices,),
+        in_specs=[
+            pl.BlockSpec((1, tokens), lambda j: (0, 0)),
+            pl.BlockSpec((tokens, features), lambda j: (0, j)),
+            pl.BlockSpec((maps.shape[0], features), lambda j: (0, j)),
+            pl.BlockSpec(cot.shape, lambda j: (0, 0)),
+        ],
+        out_specs=pl.BlockSpec((1, total, features), lambda j: (j, 0, 0)),
+        out_shape=jax.ShapeDtypeStruct((devices, total, features), act.dtype),
+        cost_estimate=pl.CostEstimate(
+            flops=2 * devices * cap * tokens * cot.shape[1],
+            bytes_accessed=4 * devices * total * features,
+            transcendentals=0,
+        ),
+        compiler_params=pltpu.CompilerParams(vmem_limit_bytes=24 << 20),
+    )(rows[None], act, maps, cot)
+
+
 def slot_chunks(width):
     size = min(width, 768)
     while width % size:
@@ -277,21 +324,31 @@
     rows_all = shared[:, :count, out_width:].reshape(devices, 3, padded)[:, :, :tokens]
     rows_all = from_digits(rows_all.transpose(1, 0, 2)).reshape(-1)
 
-    target = token_layout_row // resident_rows
+    own_slot = starts_of(token_layout_row // BLOCK, start_ids)
+    every_up = dot(up_all, cotangent, ((1,), (1,))).reshape(slots, rank, tokens)
+    own = jnp.arange(slots, dtype=jnp.int32)[:, None, None] == own_slot[None, None, :]
+    grad_in = jnp.sum(jnp.where(own, every_up, 0.0), axis=0).astype(jnp.bfloat16)
+
     order = jnp.arange(tokens, dtype=jnp.int32)
-    before = (target[:, None] == target[None, :]) & (order[None, :] < order[:, None])
-    place = target * slot_cap + jnp.sum(before.astype(jnp.int32), axis=1)
     places = jnp.arange(resident_rows, dtype=jnp.int32)
-    send = (places[:, None] == place[None, :]).astype(jnp.bfloat16)
-    send_cot = dot(send, cotangent, ((1,), (0,))).astype(jnp.bfloat16)
-    send_cot = send_cot.reshape(devices, slot_cap, out_width)
     folds = out_width // features
-    packed = [
-        activations.reshape(tokens, devices, features).transpose(1, 0, 2),
-        adapter_down_maps.reshape(-1, devices, features).transpose(1, 0, 2),
-    ] + [send_cot[:, :, k * features : (k + 1) * features] for k in range(folds)]
-    packed = jnp.concatenate(packed, axis=1)
+    flat_maps = adapter_down_maps.reshape(-1, width)
+    if features % LANES == 0 and slot_cap % 8 == 0:
+        packed = pack(token_layout_row, activations, flat_maps, cotangent, devices, slot_cap)
+    else:
+        target = token_layout_row // resident_rows
+        before = (target[:, None] == target[None, :]) & (order[None, :] < order[:, None])
+        place = target * slot_cap + jnp.sum(before.astype(jnp.int32), axis=1)
+        send = (places[:, None] == place[None, :]).astype(jnp.bfloat16)
+        send_cot = dot(send, cotangent, ((1,), (0,))).astype(jnp.bfloat16)
+        send_cot = send_cot.reshape(devices, slot_cap, out_width)
+        packed = [
+            activations.reshape(tokens, devices, features).transpose(1, 0, 2),
+            flat_maps.reshape(-1, devices, features).transpose(1, 0, 2),
+        ] + [send_cot[:, :, k * features : (k + 1) * features] for k in range(folds)]
+        packed = jnp.concatenate(packed, axis=1)
     received = lax.all_to_all(packed, "blk", split_axis=0, concat_axis=0)
+    grad_in, received = lax.optimization_barrier((grad_in, received))
     maps_f = received[:, tokens : tokens + resident * rank].reshape(slots * rank, features)
     recv_cot = received[:, tokens + resident * rank :]
     recv_cot = [
@@ -313,12 +370,7 @@
         [dot(arrange, part, ((1,), (0,))).astype(jnp.bfloat16) for part in recv_cot], axis=1
     )
 
-    own_slot = starts_of(token_layout_row // BLOCK, start_ids)
-    every_up = dot(up_all, cotangent, ((1,), (1,))).reshape(slots, rank, tokens)
-    own = jnp.arange(slots, dtype=jnp.int32)[:, None, None] == own_slot[None, None, :]
-    grad_in = jnp.sum(jnp.where(own, every_up, 0.0), axis=0).astype(jnp.bfloat16)
     grad_all = to_all(grad_in).transpose(1, 0, 2).reshape(rank, -1)
-
     slot_all = starts_of(rows_all // BLOCK, start_ids)[None]
     hidden_call, down_call = feature_calls(
         devices, tokens, packed.shape[1], features, slots * rank, rank

time: 379 us -> 346 us (0.913)
  waiting for transfers between devices: 159 us -> 107 us
  starting transfers between devices: 72.2 us -> 87.7 us
  Pallas kernels: 43.3 us -> 49.6 us
  other arithmetic: 13.7 us -> 9.32 us
    all_gather x1, waiting for transfers between devices: 33.9 us -> 0.01 us  [local(): shared = lax.all_gather(shared, 'blk', axis=0, tiled=False)]
    all_to_all x2, starting transfers between devices: 9.97 us -> 23.1 us  [to_all(): return lax.all_to_all(copies, 'blk', split_axis=0, concat_axis=0)]
    ppermute x25, waiting for transfers between devices: 119 us -> 107 us  [permuted(): return lax.ppermute(value, 'blk', pairs)]
    all_to_all x2, waiting for transfers between devices: 6.33 us -> 0.01 us  [to_all(): return lax.all_to_all(copies, 'blk', split_axis=0, concat_axis=0)]
    pallas_call x0 -> x1, Pallas kernels: none -> 5.55 us  [pack(): pl.pallas_call(pack_kernel, grid=(devices,), in_specs=[pl.BlockSpec((1, t...]
    unnamed x29 -> x38, local copies, waits for them, and re-layouts: 3.08 us -> 8.08 us
    concatenate x1 -> x0, other arithmetic: 4.44 us -> none  [local(): packed = jnp.concatenate(packed, axis=1)]
    dot_general x11 -> x10, matrix products: 10.1 us -> 9.85 us  [dot(): lax.dot_general(a, b, (dims, ((), ())), preferred_element_type=jnp.float32)]
  transfers between devices with their start and end apart: 31 -> 31, of which waited for: 7 -> 3; matrix products, arithmetic and copies ran while one was open for 11% -> 9% of each run, Pallas kernels for 12% -> 15%
where the time goes in v3:
time: 346 us; the launch traced here: 340 us
  waiting for transfers between devices  107 us (31%)
  starting transfers between devices  87.7 us (25%)
  Pallas kernels  49.6 us (14%)
  between operations  48.9 us (14%)
  local copies, waits for them, and re-layouts  28 us (8%)
  matrix products  9.85 us (3%)
  other arithmetic  9.32 us (3%)
    ppermute x25, waiting for transfers between devices, permuted(): return lax.ppermute(value, 'blk', pairs)  107 us
    ppermute x25, starting transfers between devices, permuted(): return lax.ppermute(value, 'blk', pairs)  47.5 us
    pallas_call x5, Pallas kernels, write_stripes(): pl.pallas_call(stripes_kernel, grid_spec=pltpu.PrefetchScalarGridSpec(num...  28.1 us
    all_to_all x2, starting transfers between devices, to_all(): return lax.all_to_all(copies, 'blk', split_axis=0, concat_axis=0)  23.1 us
    dot_general x10, matrix products, dot(): lax.dot_general(a, b, (dims, ((), ())), preferred_element_type=jnp.float32)  9.85 us
    pallas_call x1, Pallas kernels, local(): down_f = down_call(received, grad_all, slot_all)  8.45 us
    unnamed x38, local copies, waits for them, and re-layouts  8.08 us
    pallas_call x1, Pallas kernels, local(): hidden = hidden_call(received, maps_f, slot_all)  7.42 us
  transfers between devices with their start and end apart: 31, of which 3 were waited for; matrix products, arithmetic and copies ran while one was open for 9% of the time, Pallas kernels for 15%

profile of v3, /device:TPU:1, one launch (start us, length us, event | category | flops | bytes accessed | tf_op | source)
XLA Modules:
  0.0 339.9 jit_solution(15096137078094567614)
XLA Ops:
  7.2 1.4 fusion.44
  12.0 1.0 dynamic-slice_bitcast_fusion
  13.0 2.2 collective-permute-start
  15.2 2.1 collective-permute-start.1
  17.3 1.2 collective-permute-start.2
  18.5 1.3 collective-permute-start.4
  20.0 1.1 copy-done.1
  21.2 1.9 copy-done.3
  23.0 1.0 copy-done.7
  24.7 5.6 %shard_map.220 = bf16[16,288,512]{2,1,0:T(8,128)(2,1)S(1)} custom-call(s32[1,192]{1,0:T(1,128)S(1)} %bitcast.127, bf16[192,8192]{1,0:T(8,128)(2,1)S(1)} %copy-done.3, bf16[48,8192]{1,0:T(8,128)(2,1)S(1)} %bitcast.125, bf16[192,1024]{1,0:T(8,128)(2,1)S(1)} %copy-done.7), custom_call_target="tpu_custom_call" | custom-call | flops 150994944 | bytes 9437184 | tf_op jit(solution)/shard_map/pallas_call | solution.py:188
  30.3 2.2 copy-done
  32.5 5.0 %all-to-all-start = ((bf16[16,288,512]{2,1,0:T(8,128)(2,1)}), bf16[16,288,512]{2,1,0:T(8,128)(2,1)}, u32[]{:S(2)}, u32[]{:S(2)}) async-start(bf16[16,288,512]{2,1,0:T(8,128)(2,1)} %copy-done), calls=%async_computation | async-start | bytes 9437184 | tf_op jit(solution)/shard_map/all_to_all | solution.py:350
  51.2 1.7 collective-permute-start.3
  76.3 1.2 collective-permute-start.5
  77.9 77.8 %collective-permute-done.5.rest_0_ = bf16[512,1024]{1,0:T(8,128)(2,1)} collective-permute-done((bf16[512,1024]{1,0:T(8,128)(2,1)}, bf16[512,1024]{1,0:T(8,128)(2,1)}, u32[]{:S(2)}, u32[]{:S(2)}) %collective-permute-start.5) | collective-permute-done | bytes 1048608 | tf_op jit(solution)/shard_map/ppermute | solution.py:17
  155.8 26.5 %collective-permute-start.6 = (bf16[512,1024]{1,0:T(8,128)(2,1)}, bf16[512,1024]{1,0:T(8,128)(2,1)S(1)}, u32[]{:S(2)}, u32[]{:S(2)}) collective-permute-start(bf16[512,1024]{1,0:T(8,128)(2,1)} %collective-permute-done.5.rest_0_), channel_id=1, source_target_pairs={{0,4},{1,5},{2,0},{3,1},{4,8},{5,9},{6,2},{7,3},{8,12},{9,13},{10,... | collective-permute-start | bytes 3145736 | tf_op jit(solution)/shard_map/ppermute | solution.py:17
  183.0 24.8 %collective-permute-done.11.rest_2_ = bf16[512,1024]{1,0:T(8,128)(2,1)} collective-permute-done((bf16[512,1024]{1,0:T(8,128)(2,1)}, bf16[512,1024]{1,0:T(8,128)(2,1)}, u32[]{:S(2)}, u32[]{:S(2)}) %collective-permute-start.11) | collective-permute-done | bytes 1048608 | tf_op jit(solution)/shard_map/ppermute | solution.py:17
  208.6 1.9 slice.143
  211.4 2.8 slice.141
  215.2 2.0 fusion.8
  218.1 2.3 fusion.7
  220.4 1.2 fusion.55
  222.0 1.1 convolution_convert_fusion
  223.2 2.1 slice.132
  225.9 16.7 %all-to-all-start.1 = ((bf16[16,16,192]{2,1,0:T(8,128)(2,1)}), bf16[16,16,192]{2,1,0:T(8,128)(2,1)S(1)}, u32[]{:S(2)}, u32[]{:S(2)}) async-start(bf16[16,16,192]{2,1,0:T(8,128)(2,1)} %broadcast_in_dim.139), calls=%async_computation.1 | async-start | bytes 262144 | tf_op jit(solution)/shard_map/all_to_all | solution.py:28
  243.1 1.1 copy-done.6
  244.3 7.4 %shard_map.227 = f32[16,3072]{1,0:T(8,128)S(1)} custom-call(bf16[16,288,512]{2,1,0:T(8,128)(2,1)} %all-to-all-done.act, bf16[768,512]{1,0:T(8,128)(2,1)S(1)} %bitcast.126, s32[1,3072]{1,0:T(1,128)S(1)} %compare_select_fusion.slot), custom_call_target="tpu_custom_call" | custom-call | flops 2415919104 | bytes 3145728 | tf_op jit(solution)/shard_map/pallas_call | solution.py:378
  251.8 0.8 copy.49
  252.7 1.1 pad_maximum_fusion.cot
  253.8 6.0 %all-to-all-start.3 = ((f32[16,16,192]{2,1,0:T(8,128)}), f32[16,16,192]{2,1,0:T(8,128)}, u32[]{:S(2)}, u32[]{:S(2)}) async-start(f32[16,16,192]{2,1,0:T(8,128)} %bitcast.123), calls=%async_computation.3 | async-start | bytes 524288 | tf_op jit(solution)/shard_map/all_to_all | solution.py:380
  260.0 1.4 collective-permute-start.12
  262.5 4.0 %shard_map.221.rest_4_ = bf16[384,8192]{1,0:T(8,128)(2,1)} custom-call(s32[2]{0:T(128)S(1)} %pad_add_fusion.4.where, bf16[384,1024]{1,0:T(8,128)(2,1)S(1)} %pad_maximum_fusion.cot, bf16[384,16]{1,0:T(8,128)(2,1)S(1)} %fusion.9.grad, bf16[48,8192]{1,0:T(8,128)(2,1)S(1)} %pad_maximum_fusion.1.down, bf16[512,1024]{1,0:T(8,128)(2,1)S(1)} %copy-done.5, ...), custom_call_target="tpu_custom_call" | custom-call | flops 805306368 | bytes 2883584 | tf_op jit(solution)/shard_map/pallas_call | solution.py:126
  266.5 6.6 %shard_map.222.rest_4_ = bf16[384,8192]{1,0:T(8,128)(2,1)} custom-call(s32[4]{0:T(128)S(1)} %pad_add_fusion.3.where, bf16[384,1024]{1,0:T(8,128)(2,1)S(1)} %pad_maximum_fusion.cot, bf16[384,16]{1,0:T(8,128)(2,1)S(1)} %fusion.9.grad, bf16[48,8192]{1,0:T(8,128)(2,1)S(1)} %pad_maximum_fusion.1.down, ...), custom_call_target="tpu_custom_call", output_to_operand_aliasing={{}: (8, {})} | custom-call | flops 1610612736 | bytes 5767168 | tf_op jit(solution)/shard_map/pallas_call | solution.py:126
  273.1 8.5 %shard_map.226 = bf16[768,512]{1,0:T(8,128)(2,1)} custom-call(bf16[16,288,512]{2,1,0:T(8,128)(2,1)} %all-to-all-done.act, bf16[16,3072]{1,0:T(8,128)(2,1)S(1)} %reshape.291.grad, s32[1,3072]{1,0:T(1,128)S(1)} %compare_select_fusion.slot), custom_call_target="tpu_custom_call" | custom-call | flops 2415919104 | bytes 3145728 | tf_op jit(solution)/shard_map/pallas_call | solution.py:383
  281.5 1.0 reduce_sum.19
  283.2 6.4 %all-to-all-start.4 = ((bf16[16,16,192]{2,1,0:T(8,128)(2,1)}), bf16[16,16,192]{2,1,0:T(8,128)(2,1)S(1)}, u32[]{:S(2)}, u32[]{:S(2)}) async-start(bf16[16,16,192]{2,1,0:T(8,128)(2,1)} %broadcast_in_dim.147), calls=%async_computation.4 | async-start | bytes 262144 | tf_op jit(solution)/shard_map/all_to_all | solution.py:28
  290.2 6.6 %shard_map.223.rest_4_ = bf16[384,8192]{1,0:T(8,128)(2,1)} custom-call(s32[4]{0:T(128)S(1)} %pad_add_fusion.2.where, bf16[384,1024]{1,0:T(8,128)(2,1)S(1)} %pad_maximum_fusion.cot, bf16[384,16]{1,0:T(8,128)(2,1)S(1)} %fusion.9.grad, bf16[48,8192]{1,0:T(8,128)(2,1)S(1)} %pad_maximum_fusion.1.down, ...), custom_call_target="tpu_custom_call", output_to_operand_aliasing={{}: (8, {})} | custom-call | flops 1610612736 | bytes 5767168 | tf_op jit(solution)/shard_map/pallas_call | solution.py:126
  296.8 6.2 %shard_map.224.rest_4_ = bf16[384,8192]{1,0:T(8,128)(2,1)} custom-call(s32[4]{0:T(128)S(1)} %pad_add_fusion.1.where, bf16[384,1024]{1,0:T(8,128)(2,1)S(1)} %pad_maximum_fusion.cot, bf16[384,16]{1,0:T(8,128)(2,1)S(1)} %fusion.9.grad, bf16[48,8192]{1,0:T(8,128)(2,1)S(1)} %pad_maximum_fusion.1.down, ...), custom_call_target="tpu_custom_call", output_to_operand_aliasing={{}: (8, {})} | custom-call | flops 1610612736 | bytes 5767168 | tf_op jit(solution)/shard_map/pallas_call | solution.py:126
  303.0 6.2 %all-to-all-start.2 = ((bf16[16,48,512]{2,1,0:T(8,128)(2,1)}), bf16[16,48,512]{2,1,0:T(8,128)(2,1)}, u32[]{:S(2)}, u32[]{:S(2)}) async-start(bf16[16,48,512]{2,1,0:T(8,128)(2,1)} %bitcast.58), calls=%async_computation.2 | async-start | bytes 1572864 | tf_op jit(solution)/shard_map/all_to_all | solution.py:384
  309.2 0.9 copy.44
  311.4 2.0 select_add_fusion.1
  313.6 4.3 %collective-permute-start.22 = (f32[16,1024]{1,0:T(8,128)S(1)}, f32[16,1024]{1,0:T(8,128)S(1)}, u32[]{:S(2)}, u32[]{:S(2)}) collective-permute-start(f32[16,1024]{1,0:T(8,128)S(1)} %get-tuple-element.45), channel_id=1, source_target_pairs={{0,14},{1,15},{2,0},{3,1},{4,2},{5,3},{6,4},{7,5},{8,6},{9,7},{10,... | collective-permute-start | bytes 196616 | tf_op jit(solution)/shard_map/ppermute | solution.py:17
  317.9 1.7 collective-permute-start.23
  319.9 4.7 %shard_map.225 = bf16[384,8192]{1,0:T(8,128)(2,1)} custom-call(s32[4]{0:T(128)S(1)} %pad_add_fusion.where, bf16[384,1024]{1,0:T(8,128)(2,1)S(1)} %pad_maximum_fusion.cot, bf16[384,16]{1,0:T(8,128)(2,1)S(1)} %fusion.9.grad, bf16[48,8192]{1,0:T(8,128)(2,1)S(1)} %pad_maximum_fusion.1.down, ...), custom_call_target="tpu_custom_call", output_to_operand_aliasing={{}: (8, {})} | custom-call | flops 805306368 | bytes 2883584 | tf_op jit(solution)/shard_map/pallas_call | solution.py:126
  324.6 3.9 %collective-permute-done.23 = f32[16,1024]{1,0:T(8,128)S(1)} collective-permute-done((f32[16,1024]{1,0:T(8,128)S(1)}, f32[16,1024]{1,0:T(8,128)S(1)}, u32[]{:S(2)}, u32[]{:S(2)}) %collective-permute-start.23) | collective-permute-done | bytes 65568 | tf_op jit(solution)/shard_map/ppermute | solution.py:17
  329.4 1.3 convert_bitcast_fusion
  330.7 0.9 copy.42
  331.6 1.4 reshape.300
  (132 shorter events, 18.4 us)
Async XLA Ops:
  13.0 38.2 %collective-permute-start = (bf16[16,8192]{1,0:T(8,128)(2,1)S(1)}, bf16[16,8192]{1,0:T(8,128)(2,1)S(1)}, u32[]{:S(2)}, u32[]{:S(2)}) collective-permute-start(bf16[16,8192]{1,0:T(8,128)(2,1)S(1)} %dynamic-slice_bitcast_fusion), channel_id=1, source_target_pairs={{0,4},{1,5},{2,6},{3,7},{4,8},{5,9},{6,10},{7,11},{8,12},{9,13},{1... | collective-permute-start | bytes 786440 | tf_op jit(solution)/shard_map/ppermute | solution.py:17
  15.2 61.0 %collective-permute-start.1 = (bf16[16,8192]{1,0:T(8,128)(2,1)S(1)}, bf16[16,8192]{1,0:T(8,128)(2,1)S(1)}, u32[]{:S(2)}, u32[]{:S(2)}) collective-permute-start(bf16[16,8192]{1,0:T(8,128)(2,1)S(1)} %dynamic-slice_bitcast_fusion), channel_id=1, source_target_pairs={{0,3},{1,4},{2,5},{3,6},{4,7},{5,8},{6,9},{7,10},{8,11},{9,12},{10... | collective-permute-start | bytes 786440 | tf_op jit(solution)/shard_map/ppermute | solution.py:17
  17.3 60.5 %collective-permute-start.2 = (bf16[16,8192]{1,0:T(8,128)(2,1)S(1)}, bf16[16,8192]{1,0:T(8,128)(2,1)S(1)}, u32[]{:S(2)}, u32[]{:S(2)}) collective-permute-start(bf16[16,8192]{1,0:T(8,128)(2,1)S(1)} %dynamic-slice_bitcast_fusion), channel_id=1, source_target_pairs={{0,2},{1,3},{2,4},{3,5},{4,6},{5,7},{6,8},{7,9},{8,10},{9,11},{10,... | collective-permute-start | bytes 786440 | tf_op jit(solution)/shard_map/ppermute | solution.py:17
  18.5 57.8 %collective-permute-start.4 = (bf16[512,1024]{1,0:T(8,128)(2,1)}, bf16[512,1024]{1,0:T(8,128)(2,1)}, u32[]{:S(2)}, u32[]{:S(2)}) collective-permute-start(bf16[512,1024]{1,0:T(8,128)(2,1)} %rest_0_.1), channel_id=1, source_target_pairs={{0,4},{1,5},{2,0},{3,1},{4,8},{5,9},{6,2},{7,3},{8,12},{9,13},{10,... | collective-permute-start | bytes 3145736 | tf_op jit(solution)/shard_map/ppermute | solution.py:17
  19.8 57.7 %collective-permute-start.9 = (bf16[512,1024]{1,0:T(8,128)(2,1)}, bf16[512,1024]{1,0:T(8,128)(2,1)}, u32[]{:S(2)}, u32[]{:S(2)}) collective-permute-start(bf16[512,1024]{1,0:T(8,128)(2,1)} %rest_0_.1), channel_id=1, source_target_pairs={{0,2},{1,3},{2,6},{3,7},{4,0},{5,1},{6,10},{7,11},{8,4},{9,5},{10,... | collective-permute-start | bytes 3145736 | tf_op jit(solution)/shard_map/ppermute | solution.py:17
  20.0 1.1 copy-start.1
  21.2 1.9 copy-start.3
  30.3 2.2 copy-start
  32.5 5.0 %copy-start.10 = (s32[192]{0:T(256)S(1)}, s32[192]{0:T(256)}, u32[]{:S(2)}) copy-start(s32[192]{0:T(256)} %param.23) | copy-start | bytes 2308
  32.5 5.1 %copy-start.16 = (bf16[3,16,1024]{2,1,0:T(8,128)(2,1)S(1)}, bf16[3,16,1024]{2,1,0:T(8,128)(2,1)}, u32[]{:S(2)}) copy-start(bf16[3,16,1024]{2,1,0:T(8,128)(2,1)} %param.27) | copy-start | bytes 294916
  32.5 5.8 %copy-start.18 = (s32[8]{0:T(128)S(1)}, s32[8]{0:T(128)}, u32[]{:S(2)}) copy-start(s32[8]{0:T(128)} %constant.298.clone) | copy-start | bytes 100
  32.5 11.1 %copy-start.17 = (s32[8]{0:T(128)S(1)}, s32[8]{0:T(128)}, u32[]{:S(2)}) copy-start(s32[8]{0:T(128)} %constant.297.clone) | copy-start | bytes 100
  32.5 43.7 %copy-start.4 = (bf16[512,1024]{1,0:T(8,128)(2,1)S(1)}, bf16[512,1024]{1,0:T(8,128)(2,1)}, u32[]{:S(2)}) copy-start(bf16[512,1024]{1,0:T(8,128)(2,1)} %rest_0_.1) | copy-start | bytes 3145732
  32.5 45.3 %copy-start.2 = (bf16[3,16,8192]{2,1,0:T(8,128)(2,1)S(1)}, bf16[3,16,8192]{2,1,0:T(8,128)(2,1)}, u32[]{:S(2)}) copy-start(bf16[3,16,8192]{2,1,0:T(8,128)(2,1)} %param.26) | copy-start | bytes 2359300
  32.5 187.9 %all-to-all-start = ((bf16[16,288,512]{2,1,0:T(8,128)(2,1)}), bf16[16,288,512]{2,1,0:T(8,128)(2,1)}, u32[]{:S(2)}, u32[]{:S(2)}) async-start(bf16[16,288,512]{2,1,0:T(8,128)(2,1)} %copy-done), calls=%async_computation | async-start | bytes 9437184 | tf_op jit(solution)/shard_map/all_to_all | solution.py:350
  37.5 173.9 %all-gather.3.cloned.1.call-start = ((), (), s32[]{:S(2)}) async-start(), calls=%async_computation.5 | async-start | bytes 1880064 | tf_op jit(solution)/shard_map/all_gather | solution.py:322
  51.2 26.6 %collective-permute-start.3 = (bf16[16,8192]{1,0:T(8,128)(2,1)S(1)}, bf16[16,8192]{1,0:T(8,128)(2,1)S(1)}, u32[]{:S(2)}, u32[]{:S(2)}) collective-permute-start(bf16[16,8192]{1,0:T(8,128)(2,1)S(1)} %dynamic-slice_bitcast_fusion), channel_id=1, source_target_pairs={{0,1},{1,2},{2,3},{3,4},{4,5},{5,6},{6,7},{7,8},{8,9},{9,10},{10,1... | collective-permute-start | bytes 786440 | tf_op jit(solution)/shard_map/ppermute | solution.py:17
  76.2 166.3 %collective-permute-start.20 = (bf16[512,1024]{1,0:T(8,128)(2,1)S(1)}, bf16[512,1024]{1,0:T(8,128)(2,1)}, u32[]{:S(2)}, u32[]{:S(2)}) collective-permute-start(bf16[512,1024]{1,0:T(8,128)(2,1)S(1)} %copy-done.4), channel_id=1, source_target_pairs={{0,1},{1,0},{2,3},{3,2},{4,5},{5,4},{6,7},{7,6},{8,9},{9,8},{10,11... | collective-permute-start | bytes 3145736 | tf_op jit(solution)/shard_map/ppermute | solution.py:17
  76.3 79.5 %collective-permute-start.5 = (bf16[512,1024]{1,0:T(8,128)(2,1)}, bf16[512,1024]{1,0:T(8,128)(2,1)}, u32[]{:S(2)}, u32[]{:S(2)}) collective-permute-start(bf16[512,1024]{1,0:T(8,128)(2,1)} %collective-permute-done.4.rest_0_), channel_id=1, source_target_pairs={{0,4},{1,5},{2,0},{3,1},{4,8},{5,9},{6,2},{7,3},{8,12},{9,13},{10,... | collective-permute-start | bytes 3145736 | tf_op jit(solution)/shard_map/ppermute | solution.py:17
  77.5 104.8 %collective-permute-start.10 = (bf16[512,1024]{1,0:T(8,128)(2,1)}, bf16[512,1024]{1,0:T(8,128)(2,1)}, u32[]{:S(2)}, u32[]{:S(2)}) collective-permute-start(bf16[512,1024]{1,0:T(8,128)(2,1)} %collective-permute-done.9.rest_2_), channel_id=1, source_target_pairs={{0,2},{1,3},{2,6},{3,7},{4,0},{5,1},{6,10},{7,11},{8,4},{9,5},{10,... | collective-permute-start | bytes 3145736 | tf_op jit(solution)/shard_map/ppermute | solution.py:17
  155.8 54.7 %collective-permute-start.6 = (bf16[512,1024]{1,0:T(8,128)(2,1)}, bf16[512,1024]{1,0:T(8,128)(2,1)S(1)}, u32[]{:S(2)}, u32[]{:S(2)}) collective-permute-start(bf16[512,1024]{1,0:T(8,128)(2,1)} %collective-permute-done.5.rest_0_), channel_id=1, source_target_pairs={{0,4},{1,5},{2,0},{3,1},{4,8},{5,9},{6,2},{7,3},{8,12},{9,13},{10,... | collective-permute-start | bytes 3145736 | tf_op jit(solution)/shard_map/ppermute | solution.py:17
  182.3 25.5 %collective-permute-start.11 = (bf16[512,1024]{1,0:T(8,128)(2,1)}, bf16[512,1024]{1,0:T(8,128)(2,1)}, u32[]{:S(2)}, u32[]{:S(2)}) collective-permute-start(bf16[512,1024]{1,0:T(8,128)(2,1)} %collective-permute-done.10.rest_2_), channel_id=1, source_target_pairs={{0,2},{1,3},{2,6},{3,7},{4,0},{5,1},{6,10},{7,11},{8,4},{9,5},{10,... | collective-permute-start | bytes 3145736 | tf_op jit(solution)/shard_map/ppermute | solution.py:17
  182.4 60.3 %collective-permute-start.18 = (bf16[512,1024]{1,0:T(8,128)(2,1)}, bf16[512,1024]{1,0:T(8,128)(2,1)}, u32[]{:S(2)}, u32[]{:S(2)}) collective-permute-start(bf16[512,1024]{1,0:T(8,128)(2,1)} %collective-permute-done.4.rest_0_), channel_id=1, source_target_pairs={{0,1},{1,0},{2,3},{3,2},{4,5},{5,4},{6,7},{7,6},{8,9},{9,8},{10,11... | collective-permute-start | bytes 3145736 | tf_op jit(solution)/shard_map/ppermute | solution.py:17
  182.5 77.5 %collective-permute-start.19 = (bf16[512,1024]{1,0:T(8,128)(2,1)}, bf16[512,1024]{1,0:T(8,128)(2,1)}, u32[]{:S(2)}, u32[]{:S(2)}) collective-permute-start(bf16[512,1024]{1,0:T(8,128)(2,1)} %collective-permute-done.9.rest_2_), channel_id=1, source_target_pairs={{0,1},{1,0},{2,3},{3,2},{4,5},{5,4},{6,7},{7,6},{8,9},{9,8},{10,11... | collective-permute-start | bytes 3145736 | tf_op jit(solution)/shard_map/ppermute | solution.py:17
  207.8 53.6 %collective-permute-start.16 = (bf16[512,1024]{1,0:T(8,128)(2,1)}, bf16[512,1024]{1,0:T(8,128)(2,1)}, u32[]{:S(2)}, u32[]{:S(2)}) collective-permute-start(bf16[512,1024]{1,0:T(8,128)(2,1)} %collective-permute-done.5.rest_0_), channel_id=1, source_target_pairs={{0,1},{1,0},{2,3},{3,2},{4,5},{5,4},{6,7},{7,6},{8,9},{9,8},{10,11... | collective-permute-start | bytes 3145736 | tf_op jit(solution)/shard_map/ppermute | solution.py:17
  210.5 79.7 %collective-permute-start.17 = (bf16[512,1024]{1,0:T(8,128)(2,1)}, bf16[512,1024]{1,0:T(8,128)(2,1)}, u32[]{:S(2)}, u32[]{:S(2)}) collective-permute-start(bf16[512,1024]{1,0:T(8,128)(2,1)} %collective-permute-done.10.rest_2_), channel_id=1, source_target_pairs={{0,1},{1,0},{2,3},{3,2},{4,5},{5,4},{6,7},{7,6},{8,9},{9,8},{10,11... | collective-permute-start | bytes 3145736 | tf_op jit(solution)/shard_map/ppermute | solution.py:17
  211.4 3.8 %copy-start.8 = (bf16[192,1024]{1,0:T(8,128)(2,1)S(1)}, bf16[192,1024]{1,0:T(8,128)(2,1)}, u32[]{:S(2)}) copy-start(bf16[192,1024]{1,0:T(8,128)(2,1)} %cot.1) | copy-start | bytes 1179652
  220.4 1.2 copy-start.14
  222.0 30.6 %copy-start.11 = (bf16[384,512]{1,0:T(8,128)(2,1)}, bf16[384,512]{1,0:T(8,128)(2,1)S(1)}, u32[]{:S(2)}) copy-start(bf16[384,512]{1,0:T(8,128)(2,1)S(1)} %convolution_convert_fusion.1) | copy-start | bytes 1179652
  225.9 27.9 %all-to-all-start.1 = ((bf16[16,16,192]{2,1,0:T(8,128)(2,1)}), bf16[16,16,192]{2,1,0:T(8,128)(2,1)S(1)}, u32[]{:S(2)}, u32[]{:S(2)}) async-start(bf16[16,16,192]{2,1,0:T(8,128)(2,1)} %broadcast_in_dim.139), calls=%async_computation.1 | async-start | bytes 262144 | tf_op jit(solution)/shard_map/all_to_all | solution.py:28
  242.6 54.2 %collective-permute-start.14 = (bf16[512,1024]{1,0:T(8,128)(2,1)S(1)}, bf16[512,1024]{1,0:T(8,128)(2,1)}, u32[]{:S(2)}, u32[]{:S(2)}) collective-permute-start(bf16[512,1024]{1,0:T(8,128)(2,1)S(1)} %collective-permute-done.6.rest_0_), channel_id=1, source_target_pairs={{0,1},{1,0},{2,3},{3,2},{4,5},{5,4},{6,7},{7,6},{8,9},{9,8},{10,11... | collective-permute-start | bytes 3145736 | tf_op jit(solution)/shard_map/ppermute | solution.py:17
  242.7 54.0 %collective-permute-start.15 = (bf16[512,1024]{1,0:T(8,128)(2,1)}, bf16[512,1024]{1,0:T(8,128)(2,1)}, u32[]{:S(2)}, u32[]{:S(2)}) collective-permute-start(bf16[512,1024]{1,0:T(8,128)(2,1)} %collective-permute-done.11.rest_2_), channel_id=1, source_target_pairs={{0,1},{1,0},{2,3},{3,2},{4,5},{5,4},{6,7},{7,6},{8,9},{9,8},{10,11... | collective-permute-start | bytes 3145736 | tf_op jit(solution)/shard_map/ppermute | solution.py:17
  243.1 1.1 copy-start.6
  253.8 27.8 %all-to-all-start.3 = ((f32[16,16,192]{2,1,0:T(8,128)}), f32[16,16,192]{2,1,0:T(8,128)}, u32[]{:S(2)}, u32[]{:S(2)}) async-start(f32[16,16,192]{2,1,0:T(8,128)} %bitcast.123), calls=%async_computation.3 | async-start | bytes 524288 | tf_op jit(solution)/shard_map/all_to_all | solution.py:380
  260.0 2.5 copy-start.5
  260.0 29.6 %collective-permute-start.12 = (bf16[256,1024]{1,0:T(8,128)(2,1)}, bf16[256,1024]{1,0:T(8,128)(2,1)S(1)}, u32[]{:S(2)}, u32[]{:S(2)}) collective-permute-start(bf16[256,1024]{1,0:T(8,128)(2,1)} %slice.143), channel_id=1, source_target_pairs={{0,2},{1,3},{2,6},{3,7},{4,0},{5,1},{6,10},{7,11},{8,4},{9,5},{10,... | collective-permute-start | bytes 1572872 | tf_op jit(solution)/shard_map/ppermute | solution.py:17
  261.4 28.3 %collective-permute-start.7 = (bf16[256,1024]{1,0:T(8,128)(2,1)}, bf16[256,1024]{1,0:T(8,128)(2,1)}, u32[]{:S(2)}, u32[]{:S(2)}) collective-permute-start(bf16[256,1024]{1,0:T(8,128)(2,1)} %slice.142), channel_id=1, source_target_pairs={{0,4},{1,5},{2,0},{3,1},{4,8},{5,9},{6,2},{7,3},{8,12},{9,13},{10,... | collective-permute-start | bytes 1572872 | tf_op jit(solution)/shard_map/ppermute | solution.py:17
  283.2 19.8 %all-to-all-start.4 = ((bf16[16,16,192]{2,1,0:T(8,128)(2,1)}), bf16[16,16,192]{2,1,0:T(8,128)(2,1)S(1)}, u32[]{:S(2)}, u32[]{:S(2)}) async-start(bf16[16,16,192]{2,1,0:T(8,128)(2,1)} %broadcast_in_dim.147), calls=%async_computation.4 | async-start | bytes 262144 | tf_op jit(solution)/shard_map/all_to_all | solution.py:28
  289.6 30.0 %collective-permute-start.13 = (bf16[256,1024]{1,0:T(8,128)(2,1)S(1)}, bf16[256,1024]{1,0:T(8,128)(2,1)}, u32[]{:S(2)}, u32[]{:S(2)}) collective-permute-start(bf16[256,1024]{1,0:T(8,128)(2,1)S(1)} %collective-permute-done.12.rest_2_), channel_id=1, source_target_pairs={{0,1},{1,0},{2,3},{3,2},{4,5},{5,4},{6,7},{7,6},{8,9},{9,8},{10,11... | collective-permute-start | bytes 1572872 | tf_op jit(solution)/shard_map/ppermute | solution.py:17
  289.8 30.1 %collective-permute-start.8 = (bf16[256,1024]{1,0:T(8,128)(2,1)}, bf16[256,1024]{1,0:T(8,128)(2,1)}, u32[]{:S(2)}, u32[]{:S(2)}) collective-permute-start(bf16[256,1024]{1,0:T(8,128)(2,1)} %collective-permute-done.7.rest_0_), channel_id=1, source_target_pairs={{0,1},{1,0},{2,3},{3,2},{4,5},{5,4},{6,7},{7,6},{8,9},{9,8},{10,11... | collective-permute-start | bytes 1572872 | tf_op jit(solution)/shard_map/ppermute | solution.py:17
  303.0 6.2 %copy-start.15 = (bf16[16,16,192]{2,1,0:T(8,128)(2,1)}, bf16[16,16,192]{2,1,0:T(8,128)(2,1)S(1)}, u32[]{:S(2)}) copy-start(bf16[16,16,192]{2,1,0:T(8,128)(2,1)S(1)} %all-to-all-done.4) | copy-start | bytes 294916
  303.0 8.1 %copy-start.12 = (bf16[384,512]{1,0:T(8,128)(2,1)S(1)}, bf16[384,512]{1,0:T(8,128)(2,1)}, u32[]{:S(2)}) copy-start(bf16[384,512]{1,0:T(8,128)(2,1)} %copy-done.11) | copy-start | bytes 1179652
  303.0 8.1 %copy-start.13 = (bf16[384,512]{1,0:T(8,128)(2,1)S(1)}, bf16[384,512]{1,0:T(8,128)(2,1)}, u32[]{:S(2)}) copy-start(bf16[384,512]{1,0:T(8,128)(2,1)} %convolution_convert_fusion) | copy-start | bytes 1179652
  303.0 26.3 %all-to-all-start.2 = ((bf16[16,48,512]{2,1,0:T(8,128)(2,1)}), bf16[16,48,512]{2,1,0:T(8,128)(2,1)}, u32[]{:S(2)}, u32[]{:S(2)}) async-start(bf16[16,48,512]{2,1,0:T(8,128)(2,1)} %bitcast.58), calls=%async_computation.2 | async-start | bytes 1572864 | tf_op jit(solution)/shard_map/all_to_all | solution.py:384
  313.4 11.2 %collective-permute-start.21 = (f32[16,1024]{1,0:T(8,128)S(1)}, f32[16,1024]{1,0:T(8,128)S(1)}, u32[]{:S(2)}, u32[]{:S(2)}) collective-permute-start(f32[16,1024]{1,0:T(8,128)S(1)} %get-tuple-element.45), channel_id=1, source_target_pairs={{0,15},{1,0},{2,1},{3,2},{4,3},{5,4},{6,5},{7,6},{8,7},{9,8},{10,9... | collective-permute-start | bytes 196616 | tf_op jit(solution)/shard_map/ppermute | solution.py:17
  313.6 11.0 %collective-permute-start.22 = (f32[16,1024]{1,0:T(8,128)S(1)}, f32[16,1024]{1,0:T(8,128)S(1)}, u32[]{:S(2)}, u32[]{:S(2)}) collective-permute-start(f32[16,1024]{1,0:T(8,128)S(1)} %get-tuple-element.45), channel_id=1, source_target_pairs={{0,14},{1,15},{2,0},{3,1},{4,2},{5,3},{6,4},{7,5},{8,6},{9,7},{10,... | collective-permute-start | bytes 196616 | tf_op jit(solution)/shard_map/ppermute | solution.py:17
  317.9 10.6 %collective-permute-start.23 = (f32[16,1024]{1,0:T(8,128)S(1)}, f32[16,1024]{1,0:T(8,128)S(1)}, u32[]{:S(2)}, u32[]{:S(2)}) collective-permute-start(f32[16,1024]{1,0:T(8,128)S(1)} %get-tuple-element.45), channel_id=1, source_target_pairs={{0,13},{1,14},{2,15},{3,0},{4,1},{5,2},{6,3},{7,4},{8,5},{9,6},{10... | collective-permute-start | bytes 196616 | tf_op jit(solution)/shard_map/ppermute | solution.py:17
  319.6 9.0 %collective-permute-start.24 = (f32[16,1024]{1,0:T(8,128)S(1)}, f32[16,1024]{1,0:T(8,128)S(1)}, u32[]{:S(2)}, u32[]{:S(2)}) collective-permute-start(f32[16,1024]{1,0:T(8,128)S(1)} %get-tuple-element.45), channel_id=1, source_target_pairs={{0,12},{1,13},{2,14},{3,15},{4,0},{5,1},{6,2},{7,3},{8,4},{9,5},{1... | collective-permute-start | bytes 196616 | tf_op jit(solution)/shard_map/ppermute | solution.py:17
  (2 other events, 1.7 us)
Sparse Core Ops, SparseCore 0:
  41.0 87.7 all-gather.2

commit v4 on v3

--- a/solution.py
+++ b/solution.py
@@ -28,6 +28,18 @@
     return lax.all_to_all(copies, "blk", split_axis=0, concat_axis=0)
 
 
+def after(value, *others):
+    anywhere = pl.BlockSpec(memory_space=pl.ANY)
+    return pl.pallas_call(
+        lambda *refs: None,
+        in_specs=[anywhere] * (1 + len(others)),
+        out_specs=anywhere,
+        out_shape=jax.ShapeDtypeStruct(value.shape, value.dtype),
+        input_output_aliases={0: 0},
+        cost_estimate=pl.CostEstimate(flops=0, bytes_accessed=0, transcendentals=0),
+    )(value, *others)
+
+
 def dot(a, b, dims):
     return lax.dot_general(a, b, (dims, ((), ())), preferred_element_type=jnp.float32)
 
@@ -50,7 +62,7 @@
     return (high * DIGIT + middle) * DIGIT + low
 
 
-def ring_shards(weight):
+def ring_shards(weight, ties):
     count, device = lax.axis_size("blk"), lax.axis_index("blk")
     chips = count // 2
     order = list(range(0, chips, 2)) + list(range(chips - 1, 0, -2))
@@ -81,6 +93,8 @@
     for step in range(1, chips // 2):
         up, down = permuted(up, along(1)), permuted(down, along(-1))
         groups.append(both(up, origin(-step), 1, 0) + both(down, origin(step), 1, 0))
+        if step in ties:
+            up, down = after(up, ties[step]), after(down, ties[step])
     half = weight.shape[0] // 2
     up, down = permuted(up[:half], along(1)), permuted(down[half:], along(-1))
     far = origin(chips // 2)
@@ -158,7 +172,7 @@
     return (out + lora.astype(jnp.float32)).astype(jnp.bfloat16)
 
 
-def pack_kernel(rows, act, maps, cot, out):
+def pack_kernel(rows, act, maps, cot, out, rows_out):
     tokens, features = act.shape
     cap = (out.shape[1] - tokens - maps.shape[0]) * features // cot.shape[1]
     target = pl.program_id(0)
@@ -176,6 +190,7 @@
         dot(send, cot[:, k : k + features], ((1,), (0,)))
         for k in range(0, cot.shape[1], features)
     ]
+    rows_out[...] = rows[...]
     out[0, :tokens, :] = act[...]
     out[0, tokens : tokens + maps.shape[0], :] = maps[...]
     out[0, tokens + maps.shape[0] :, :] = jnp.concatenate(sent, axis=0).astype(out.dtype)
@@ -194,8 +209,14 @@
             pl.BlockSpec((maps.shape[0], features), lambda j: (0, j)),
             pl.BlockSpec(cot.shape, lambda j: (0, 0)),
         ],
-        out_specs=pl.BlockSpec((1, total, features), lambda j: (j, 0, 0)),
-        out_shape=jax.ShapeDtypeStruct((devices, total, features), act.dtype),
+        out_specs=[
+            pl.BlockSpec((1, total, features), lambda j: (j, 0, 0)),
+            pl.BlockSpec((1, tokens), lambda j: (0, 0)),
+        ],
+        out_shape=[
+            jax.ShapeDtypeStruct((devices, total, features), act.dtype),
+            jax.ShapeDtypeStruct((1, tokens), rows.dtype),
+        ],
         cost_estimate=pl.CostEstimate(
             flops=2 * devices * cap * tokens * cot.shape[1],
             bytes_accessed=4 * devices * total * features,
@@ -208,7 +229,7 @@
 def slot_chunks(width):
     size = min(width, 768)
     while width % size:
-        size -= LANES
+        size //= 2
     return [slice(k, k + size) for k in range(0, width, size)]
 
 
@@ -222,9 +243,11 @@
     tokens = out.shape[1] // act.shape[0]
     rows = jnp.concatenate([act[k, :tokens, :] for k in range(act.shape[0])], axis=0)
     total = jnp.zeros(out.shape, jnp.float32)
-    for part in slot_chunks(maps.shape[0]):
+    share = maps.shape[1]
+    for part in slot_chunks(maps.shape[0] * share):
         size = part.stop - part.start
-        each = dot(maps[part, :], rows, ((1,), (1,))).reshape(size // rank, rank, -1)
+        some = maps[part.start // share : part.stop // share].reshape(size, -1)
+        each = dot(some, rows, ((1,), (1,))).reshape(size // rank, rank, -1)
         total += jnp.sum(
             jnp.where(own_rows(slot, part.start, size, rank), each, 0.0), axis=0
         )
@@ -254,6 +277,7 @@
 
 
 def feature_calls(devices, tokens, packed, features, width, rank):
+    share = width // devices
     pair = 2
     while pair * tokens % LANES:
         pair *= 2
@@ -272,7 +296,11 @@
     hidden = pl.pallas_call(
         hidden_kernel,
         grid=grid,
-        in_specs=[act, whole, slot],
+        in_specs=[
+            act,
+            pl.BlockSpec((devices, share, features), lambda j: (0, tokens // share, 0)),
+            slot,
+        ],
         out_specs=small,
         out_shape=jax.ShapeDtypeStruct((rank, every), jnp.float32),
         cost_estimate=cost,
@@ -311,30 +339,15 @@
     slot_cap = resident_rows // devices
     start_ids = tenant_first_row // BLOCK
 
-    groups = ring_shards(frozen_value_weight)
-
-    padded = -(-tokens // LANES) * LANES
-    digits = as_digits(jnp.pad(token_layout_row, (0, padded - tokens)))
-    digits = digits.reshape(-1, LANES)
-    count = digits.shape[0]
-    digits = jnp.pad(digits, ((0, resident * rank - count), (0, 0)))
-    shared = jnp.concatenate([adapter_up_maps.reshape(-1, out_width), digits], axis=1)
-    shared = lax.all_gather(shared, "blk", axis=0, tiled=False)
-    up_all = shared[:, :, :out_width].reshape(slots * rank, out_width)
-    rows_all = shared[:, :count, out_width:].reshape(devices, 3, padded)[:, :, :tokens]
-    rows_all = from_digits(rows_all.transpose(1, 0, 2)).reshape(-1)
-
-    own_slot = starts_of(token_layout_row // BLOCK, start_ids)
-    every_up = dot(up_all, cotangent, ((1,), (1,))).reshape(slots, rank, tokens)
-    own = jnp.arange(slots, dtype=jnp.int32)[:, None, None] == own_slot[None, None, :]
-    grad_in = jnp.sum(jnp.where(own, every_up, 0.0), axis=0).astype(jnp.bfloat16)
-
     order = jnp.arange(tokens, dtype=jnp.int32)
     places = jnp.arange(resident_rows, dtype=jnp.int32)
     folds = out_width // features
     flat_maps = adapter_down_maps.reshape(-1, width)
     if features % LANES == 0 and slot_cap % 8 == 0:
-        packed = pack(token_layout_row, activations, flat_maps, cotangent, devices, slot_cap)
+        packed, rows_sent = pack(
+            token_layout_row, activations, flat_maps, cotangent, devices, slot_cap
+        )
+        rows_sent = rows_sent[0]
     else:
         target = token_layout_row // resident_rows
         before = (target[:, None] == target[None, :]) & (order[None, :] < order[:, None])
@@ -347,14 +360,23 @@
             flat_maps.reshape(-1, devices, features).transpose(1, 0, 2),
         ] + [send_cot[:, :, k * features : (k + 1) * features] for k in range(folds)]
         packed = jnp.concatenate(packed, axis=1)
-    received = lax.all_to_all(packed, "blk", split_axis=0, concat_axis=0)
-    grad_in, received = lax.optimization_barrier((grad_in, received))
-    maps_f = received[:, tokens : tokens + resident * rank].reshape(slots * rank, features)
-    recv_cot = received[:, tokens + resident * rank :]
-    recv_cot = [
-        recv_cot[:, k * slot_cap : (k + 1) * slot_cap].reshape(resident_rows, features)
-        for k in range(folds)
-    ]
+        rows_sent = token_layout_row
+
+    padded = -(-tokens // LANES) * LANES
+    digits = as_digits(jnp.pad(rows_sent, (0, padded - tokens)))
+    digits = digits.reshape(-1, LANES)
+    count = digits.shape[0]
+    digits = jnp.pad(digits, ((0, resident * rank - count), (0, 0)))
+    shared = jnp.concatenate([adapter_up_maps.reshape(-1, out_width), digits], axis=1)
+    shared = lax.all_gather(shared, "blk", axis=0, tiled=False)
+    up_all = shared[:, :, :out_width].reshape(slots * rank, out_width)
+    rows_all = shared[:, :count, out_width:].reshape(devices, 3, padded)[:, :, :tokens]
+    rows_all = from_digits(rows_all.transpose(1, 0, 2)).reshape(-1)
+
+    own_slot = starts_of(token_layout_row // BLOCK, start_ids)
+    every_up = dot(up_all, cotangent, ((1,), (1,))).reshape(slots, rank, tokens)
+    own = jnp.arange(slots, dtype=jnp.int32)[:, None, None] == own_slot[None, None, :]
+    grad_in = jnp.sum(jnp.where(own, every_up, 0.0), axis=0).astype(jnp.bfloat16)
 
     first_row = device * resident_rows
     row_of = (rows_all[None, :] - first_row == places[:, None]).astype(jnp.bfloat16)
@@ -366,16 +388,49 @@
     arrange = dot(
         row_of, (at[:, None] == places[None, :]).astype(jnp.bfloat16), ((1,), (0,))
     ).astype(jnp.bfloat16)
+
+    first_block = device * resident
+    block_numbers = first_block + jnp.arange(resident, dtype=jnp.int32)
+    begin = starts_of(block_numbers, start_ids)
+    is_local = (begin >= first_block) & (begin <= block_numbers)
+    home_slot = jnp.clip(begin - first_block, 0, resident - 1)
+    last_map = lax.dynamic_index_in_dim(
+        adapter_down_maps, home_slot[resident - 1], 0, keepdims=False
+    )
+    last_map = after(last_map, shared)
+    carried = jnp.zeros_like(last_map)
+    for step in range(1, HOPS + 1):
+        home = (device - step) % devices
+        carried = jnp.where(begin[0] // resident == home, moved(last_map, step), carried)
+
+    down_blocks = []
+    for b in range(resident):
+        down = carried
+        for k in range(b + 1):
+            down = jnp.where(is_local[b] & (home_slot[b] == k), adapter_down_maps[k], down)
+        down_blocks.append(down)
+    down_blocks = jnp.concatenate(down_blocks, axis=0)
+    slot_all = starts_of(rows_all // BLOCK, start_ids)[None]
+
+    received = lax.all_to_all(packed, "blk", split_axis=0, concat_axis=0)
+    recv_cot = received[:, tokens + resident * rank :]
+    recv_cot = [
+        recv_cot[:, k * slot_cap : (k + 1) * slot_cap].reshape(resident_rows, features)
+        for k in range(folds)
+    ]
+
     cot_rows = jnp.concatenate(
         [dot(arrange, part, ((1,), (0,))).astype(jnp.bfloat16) for part in recv_cot], axis=1
     )
 
+    grad_in = after(grad_in, received)
     grad_all = to_all(grad_in).transpose(1, 0, 2).reshape(rank, -1)
-    slot_all = starts_of(rows_all // BLOCK, start_ids)[None]
     hidden_call, down_call = feature_calls(
         devices, tokens, packed.shape[1], features, slots * rank, rank
     )
-    hidden = hidden_call(received, maps_f, slot_all)
+    slot_all = after(slot_all, arrange, down_blocks)
+    hidden = hidden_call(received, received, slot_all)
+    slot_all = after(slot_all, hidden)
     hidden = hidden.reshape(rank, devices, tokens).transpose(1, 0, 2)
     hidden = lax.all_to_all(hidden, "blk", split_axis=0, concat_axis=0)
     hidden = to_all(jnp.sum(hidden, axis=0).astype(jnp.bfloat16))
@@ -384,31 +439,13 @@
     down_home = lax.all_to_all(down_f, "blk", split_axis=0, concat_axis=1, tiled=True)
     down_map_gradient = down_home.astype(jnp.float32).reshape(resident, rank, width)
 
-    first_block = device * resident
-    block_numbers = first_block + jnp.arange(resident, dtype=jnp.int32)
-    begin = starts_of(block_numbers, start_ids)
-    is_local = (begin >= first_block) & (begin <= block_numbers)
-    home_slot = jnp.clip(begin - first_block, 0, resident - 1)
-    last_map = lax.dynamic_index_in_dim(
-        adapter_down_maps, home_slot[resident - 1], 0, keepdims=False
-    )
-    carried = jnp.zeros_like(last_map)
-    for step in range(1, HOPS + 1):
-        home = (device - step) % devices
-        carried = jnp.where(begin[0] // resident == home, moved(last_map, step), carried)
-
     grad_rows = dot(row_of, grad_all, ((1,), (1,))).astype(jnp.bfloat16)
+    grad_rows = after(grad_rows, down_f)
     hidden_rows = dot(row_of, hidden, ((1,), (1,))).astype(jnp.bfloat16)
-    down_blocks = []
     up_parts = []
     for b in range(resident):
         rows = slice(b * BLOCK, (b + 1) * BLOCK)
-        down = carried
-        for k in range(b + 1):
-            down = jnp.where(is_local[b] & (home_slot[b] == k), adapter_down_maps[k], down)
-        down_blocks.append(down)
         up_parts.append(dot(hidden_rows[rows], cot_rows[rows], ((0,), (0,))))
-    down_blocks = jnp.concatenate(down_blocks, axis=0)
 
     tail = sum(jnp.where(is_local[b], 0.0, up_parts[b]) for b in range(resident))
     far = jnp.zeros_like(tail)
@@ -424,6 +461,10 @@
         up_grads.append(adapter_scale * total)
     up_map_gradient = jnp.stack(up_grads)
 
+    chips = devices // 2
+    groups = ring_shards(
+        frozen_value_weight, {chips // 2 - 2: down_f, chips // 2 - 1: hidden}
+    )
     if frozen_value_weight.shape[0] % (2 * LANES) == 0:
         out = None
         for group in groups:

time: 346 us -> 353 us (1.020); the launches traced: 340 us -> 351 us
  waiting for transfers between devices: 107 us -> 116 us
  local copies, waits for them, and re-layouts: 28 us -> 31.8 us
    ppermute x25, waiting for transfers between devices: 107 us -> 47.9 us  [permuted(): return lax.ppermute(value, 'blk', pairs)]
    all_gather x1, waiting for transfers between devices: 0.01 us -> 58.1 us  [local(): shared = lax.all_gather(shared, 'blk', axis=0, tiled=False)]
    ppermute x25, starting transfers between devices: 47.5 us -> 28.6 us  [permuted(): return lax.ppermute(value, 'blk', pairs)]
    all_to_all x2, starting transfers between devices: 23.1 us -> 36.9 us  [to_all(): return lax.all_to_all(copies, 'blk', split_axis=0, concat_axis=0)]
    all_to_all x2, waiting for transfers between devices: 0.01 us -> 5.6 us  [to_all(): return lax.all_to_all(copies, 'blk', split_axis=0, concat_axis=0)]
    all_to_all x1, waiting for transfers between devices: 0.01 us -> 3.94 us  [local(): hidden = lax.all_to_all(hidden, 'blk', split_axis=0, concat_axis=0)]
    unnamed x38 -> x50, local copies, waits for them, and re-layouts: 8.08 us -> 8.54 us
    pallas_call x1 -> x10, Pallas kernels: 7.42 us -> 7.73 us  [the longest x1 7.73 us: local(): hidden = hidden_call(received, received, slot_all)]
  transfers between devices with their start and end apart: 31 -> 31, of which waited for: 3 -> 11; matrix products, arithmetic and copies ran while one was open for 9% -> 13% of each run, Pallas kernels for 15% -> 11%
where the time goes in v4:
time: 353 us; the launch traced here: 351 us
  waiting for transfers between devices  116 us (33%)
  starting transfers between devices  84.5 us (24%)
  Pallas kernels  49.6 us (14%)
  between operations  48.4 us (14%)
  local copies, waits for them, and re-layouts  31.8 us (9%)
  matrix products  12.5 us (4%)
  other arithmetic  8.92 us (3%)
    all_gather x1, waiting for transfers between devices, local(): shared = lax.all_gather(shared, 'blk', axis=0, tiled=False)  58.1 us
    ppermute x25, waiting for transfers between devices, permuted(): return lax.ppermute(value, 'blk', pairs)  47.9 us
    all_to_all x2, starting transfers between devices, to_all(): return lax.all_to_all(copies, 'blk', split_axis=0, concat_axis=0)  36.9 us
    ppermute x25, starting transfers between devices, permuted(): return lax.ppermute(value, 'blk', pairs)  28.6 us
    pallas_call x5, Pallas kernels, write_stripes(): pl.pallas_call(stripes_kernel, grid_spec=pltpu.PrefetchScalarGridSpec(num...  27.8 us
    dot_general x10, matrix products, dot(): lax.dot_general(a, b, (dims, ((), ())), preferred_element_type=jnp.float32)  12.5 us
    unnamed x50, local copies, waits for them, and re-layouts  8.54 us
    pallas_call x1, Pallas kernels, local(): down_f = down_call(received, grad_all, slot_all)  8.53 us
  transfers between devices with their start and end apart: 31, of which 11 were waited for; matrix products, arithmetic and copies ran while one was open for 13% of the time, Pallas kernels for 11%

profile of v4, /device:TPU:1, one launch (start us, length us, event | category | flops | bytes accessed | tf_op | source)
XLA Modules:
  0.0 351.2 jit_solution(5342487442124318000)
XLA Ops:
  7.2 2.2 collective-permute-start.4
  10.5 1.9 copy-done.8
  14.1 5.6 %shard_map.220 = (bf16[16,288,512]{2,1,0:T(8,128)(2,1)S(1)}, s32[1,192]{1,0:T(1,128)S(1)}) custom-call(s32[1,192]{1,0:T(1,128)S(1)} %bitcast.126, bf16[192,8192]{1,0:T(8,128)(2,1)S(1)} %copy-done.8, bf16[48,8192]{1,0:T(8,128)(2,1)S(1)} %bitcast.125, bf16[192,1024]{1,0:T(8,128)(2,1)S(1)} %copy-done.11), custom_call_target="tpu_custom_call" | custom-call | flops 150994944 | bytes 9437184 | tf_op jit(solution)/shard_map/pallas_call | solution.py:203
  19.6 2.2 copy-done.6
  22.7 7.4 %all-to-all-start = ((bf16[16,288,512]{2,1,0:T(8,128)(2,1)}), bf16[16,288,512]{2,1,0:T(8,128)(2,1)}, u32[]{:S(2)}, u32[]{:S(2)}) async-start(bf16[16,288,512]{2,1,0:T(8,128)(2,1)} %copy-done.6), calls=%async_computation | async-start | bytes 9437184 | tf_op jit(solution)/shard_map/all_to_all | solution.py:415
  55.6 1.4 collective-permute-start.5
  57.1 58.1 %all-gather.3.cloned.1.call-done = bf16[768,1152]{1,0:T(8,128)(2,1)} async-done(((bf16[48,1152]{1,0:T(8,128)(2,1)}), bf16[768,1152]{1,0:T(8,128)(2,1)}) %all-gather.3.cloned.1.call-update) | async-done | bytes 1769488 | tf_op jit(solution)/shard_map/all_gather | solution.py:371
  116.8 2.8 slice.139
  119.6 2.7 fusion.8.refs_0_
  122.4 1.2 compare_select_fusion.refs_0_
  123.6 16.9 %collective-permute-done.5.refs_0_.rest_0_ = bf16[512,1024]{1,0:T(8,128)(2,1)S(1)} collective-permute-done((bf16[512,1024]{1,0:T(8,128)(2,1)}, bf16[512,1024]{1,0:T(8,128)(2,1)S(1)}, u32[]{:S(2)}, u32[]{:S(2)}) %collective-permute-start.5) | collective-permute-done | bytes 1048608 | tf_op jit(solution)/shard_map/ppermute | solution.py:17
  140.6 3.4 collective-permute-start.3
  144.0 2.3 fusion.7.refs_1_
  146.3 3.7 %collective-permute-done = bf16[16,8192]{1,0:T(8,128)(2,1)S(1)} collective-permute-done((bf16[16,8192]{1,0:T(8,128)(2,1)}, bf16[16,8192]{1,0:T(8,128)(2,1)S(1)}, u32[]{:S(2)}, u32[]{:S(2)}) %collective-permute-start) | collective-permute-done | bytes 262176 | tf_op jit(solution)/shard_map/ppermute | solution.py:17
  150.0 3.4 collective-permute-start.18
  153.4 4.0 %collective-permute-done.1 = bf16[16,8192]{1,0:T(8,128)(2,1)S(1)} collective-permute-done((bf16[16,8192]{1,0:T(8,128)(2,1)}, bf16[16,8192]{1,0:T(8,128)(2,1)S(1)}, u32[]{:S(2)}, u32[]{:S(2)}) %collective-permute-start.1) | collective-permute-done | bytes 262176 | tf_op jit(solution)/shard_map/ppermute | solution.py:17
  157.4 4.4 %collective-permute-done.2 = bf16[16,8192]{1,0:T(8,128)(2,1)} collective-permute-done((bf16[16,8192]{1,0:T(8,128)(2,1)}, bf16[16,8192]{1,0:T(8,128)(2,1)}, u32[]{:S(2)}, u32[]{:S(2)}) %collective-permute-start.2) | collective-permute-done | bytes 262176 | tf_op jit(solution)/shard_map/ppermute | solution.py:17
  161.8 2.0 collective-permute-start.16
  163.8 1.9 collective-permute-start.17
  166.9 1.2 fusion.55
  168.9 1.4 broadcast_in_dim.139
  170.3 32.8 %all-to-all-start.1 = ((bf16[16,16,192]{2,1,0:T(8,128)(2,1)}), bf16[16,16,192]{2,1,0:T(8,128)(2,1)S(1)}, u32[]{:S(2)}, u32[]{:S(2)}) async-start(bf16[16,16,192]{2,1,0:T(8,128)(2,1)} %broadcast_in_dim.139), calls=%async_computation.1 | async-start | bytes 262144 | tf_op jit(solution)/shard_map/all_to_all | solution.py:28
  203.1 7.7 %shard_map.224.refs_1_ = f32[16,3072]{1,0:T(8,128)S(1)} custom-call(bf16[16,288,512]{2,1,0:T(8,128)(2,1)} %all-to-all-done.refs_1_.act.maps, bf16[16,288,512]{2,1,0:T(8,128)(2,1)} %all-to-all-done.refs_1_.act.maps, s32[1,3072]{1,0:T(1,128)S(1)} %copy-done.13), custom_call_target="tpu_custom_call" | custom-call | flops 2415919104 | bytes 3145728 | tf_op jit(solution)/shard_map/pallas_call | solution.py:432
  213.4 8.5 %shard_map.226.refs_1_ = bf16[768,512]{1,0:T(8,128)(2,1)} custom-call(bf16[16,288,512]{2,1,0:T(8,128)(2,1)} %all-to-all-done.refs_1_.act.maps, bf16[16,3072]{1,0:T(8,128)(2,1)S(1)} %reshape.288.grad, s32[1,3072]{1,0:T(1,128)S(1)} %copy-done.14), custom_call_target="tpu_custom_call" | custom-call | flops 2415919104 | bytes 3145728 | tf_op jit(solution)/shard_map/pallas_call | solution.py:438
  222.8 4.3 %shard_map.232.rest_4_ = bf16[384,8192]{1,0:T(8,128)(2,1)} custom-call(s32[2]{0:T(128)S(1)} %pad_add_fusion.4.where, bf16[384,1024]{1,0:T(8,128)(2,1)S(1)} %pad_maximum_fusion.cot, bf16[384,16]{1,0:T(8,128)(2,1)S(1)} %copy-done.4, bf16[48,8192]{1,0:T(8,128)(2,1)S(1)} %copy-done, bf16[512,1024]{1,0:T(8,128)(2,1)} %rest_0_.1, ...), custom_call_target="tpu_custom_call" | custom-call | flops 805306368 | bytes 2883584 | tf_op jit(solution)/shard_map/pallas_call | solution.py:140
  227.2 6.6 %shard_map.233.rest_4_ = bf16[384,8192]{1,0:T(8,128)(2,1)} custom-call(s32[4]{0:T(128)S(1)} %pad_add_fusion.3.where, bf16[384,1024]{1,0:T(8,128)(2,1)S(1)} %pad_maximum_fusion.cot, bf16[384,16]{1,0:T(8,128)(2,1)S(1)} %copy-done.5, bf16[48,8192]{1,0:T(8,128)(2,1)S(1)} %copy-done, ...), custom_call_target="tpu_custom_call", output_to_operand_aliasing={{}: (8, {})} | custom-call | flops 1610612736 | bytes 5767168 | tf_op jit(solution)/shard_map/pallas_call | solution.py:140
  233.8 6.2 %shard_map.234.rest_4_ = bf16[384,8192]{1,0:T(8,128)(2,1)} custom-call(s32[4]{0:T(128)S(1)} %pad_add_fusion.2.where, bf16[384,1024]{1,0:T(8,128)(2,1)S(1)} %pad_maximum_fusion.cot, bf16[384,16]{1,0:T(8,128)(2,1)S(1)} %copy-done.5, bf16[48,8192]{1,0:T(8,128)(2,1)S(1)} %copy-done, ...), custom_call_target="tpu_custom_call", output_to_operand_aliasing={{}: (8, {})} | custom-call | flops 1610612736 | bytes 5767168 | tf_op jit(solution)/shard_map/pallas_call | solution.py:140
  240.0 1.4 collective-permute-start.6
  242.4 1.8 copy.64
  244.2 6.5 %all-to-all-start.2 = ((f32[16,16,192]{2,1,0:T(8,128)}), f32[16,16,192]{2,1,0:T(8,128)}, u32[]{:S(2)}, u32[]{:S(2)}) async-start(f32[16,16,192]{2,1,0:T(8,128)} %bitcast.134), calls=%async_computation.2 | async-start | bytes 524288 | tf_op jit(solution)/shard_map/all_to_all | solution.py:435
  250.7 14.3 %collective-permute-done.6.refs_0_.rest_0_ = bf16[512,1024]{1,0:T(8,128)(2,1)S(1)} collective-permute-done((bf16[512,1024]{1,0:T(8,128)(2,1)}, bf16[512,1024]{1,0:T(8,128)(2,1)S(1)}, u32[]{:S(2)}, u32[]{:S(2)}) %collective-permute-start.6) | collective-permute-done | bytes 1048608 | tf_op jit(solution)/shard_map/ppermute | solution.py:17
  266.2 2.4 collective-permute-start.15
  268.7 3.9 %all-to-all-done.2 = f32[16,16,192]{2,1,0:T(8,128)} async-done(((f32[16,16,192]{2,1,0:T(8,128)}), f32[16,16,192]{2,1,0:T(8,128)}, u32[]{:S(2)}, u32[]{:S(2)}) %all-to-all-start.2) | async-done | bytes 196640 | tf_op jit(solution)/shard_map/all_to_all | solution.py:435
  274.3 4.1 %all-to-all-start.3 = ((bf16[16,16,192]{2,1,0:T(8,128)(2,1)}), bf16[16,16,192]{2,1,0:T(8,128)(2,1)S(1)}, u32[]{:S(2)}, u32[]{:S(2)}) async-start(bf16[16,16,192]{2,1,0:T(8,128)(2,1)} %broadcast_in_dim.145), calls=%async_computation.3 | async-start | bytes 262144 | tf_op jit(solution)/shard_map/all_to_all | solution.py:28
  279.6 5.6 %all-to-all-done.3 = bf16[16,16,192]{2,1,0:T(8,128)(2,1)S(1)} async-done(((bf16[16,16,192]{2,1,0:T(8,128)(2,1)}), bf16[16,16,192]{2,1,0:T(8,128)(2,1)S(1)}, u32[]{:S(2)}, u32[]{:S(2)}) %all-to-all-start.3) | async-done | bytes 98336 | tf_op jit(solution)/shard_map/all_to_all | solution.py:28
  285.2 5.2 %all-to-all-start.4 = ((bf16[16,48,512]{2,1,0:T(8,128)(2,1)}), bf16[16,48,512]{2,1,0:T(8,128)(2,1)}, u32[]{:S(2)}, u32[]{:S(2)}) async-start(bf16[16,48,512]{2,1,0:T(8,128)(2,1)} %bitcast.61), calls=%async_computation.4 | async-start | bytes 1572864 | tf_op jit(solution)/shard_map/all_to_all | solution.py:439
  293.6 6.2 %shard_map.235.rest_4_ = bf16[384,8192]{1,0:T(8,128)(2,1)} custom-call(s32[4]{0:T(128)S(1)} %pad_add_fusion.1.where, bf16[384,1024]{1,0:T(8,128)(2,1)S(1)} %pad_maximum_fusion.cot, bf16[384,16]{1,0:T(8,128)(2,1)S(1)} %copy-done.5, bf16[48,8192]{1,0:T(8,128)(2,1)S(1)} %copy-done, ...), custom_call_target="tpu_custom_call", output_to_operand_aliasing={{}: (8, {})} | custom-call | flops 1610612736 | bytes 5767168 | tf_op jit(solution)/shard_map/pallas_call | solution.py:140
  299.8 1.9 slice.141
  301.7 1.4 collective-permute-start.12
  303.1 1.9 slice.140
  305.1 2.9 select_add_fusion.1
  322.6 4.1 %collective-permute-start.22 = (f32[16,1024]{1,0:T(8,128)S(1)}, f32[16,1024]{1,0:T(8,128)S(1)}, u32[]{:S(2)}, u32[]{:S(2)}) collective-permute-start(f32[16,1024]{1,0:T(8,128)S(1)} %get-tuple-element.45), channel_id=1, source_target_pairs={{0,14},{1,15},{2,0},{3,1},{4,2},{5,3},{6,4},{7,5},{8,6},{9,7},{10,... | collective-permute-start | bytes 196616 | tf_op jit(solution)/shard_map/ppermute | solution.py:17
  328.3 2.6 collective-permute-done.23
  330.9 1.7 collective-permute-done.24
  333.9 1.3 convert_bitcast_fusion
  335.3 2.1 copy.60
  337.4 2.6 reshape.296
  340.0 4.4 %shard_map.236 = bf16[384,8192]{1,0:T(8,128)(2,1)} custom-call(s32[4]{0:T(128)S(1)} %pad_add_fusion.where, bf16[384,1024]{1,0:T(8,128)(2,1)S(1)} %pad_maximum_fusion.cot, bf16[384,16]{1,0:T(8,128)(2,1)S(1)} %copy-done.5, bf16[48,8192]{1,0:T(8,128)(2,1)S(1)} %copy-done, ...), custom_call_target="tpu_custom_call", output_to_operand_aliasing={{}: (8, {})} | custom-call | flops 805306368 | bytes 2883584 | tf_op jit(solution)/shard_map/pallas_call | solution.py:140
  (153 shorter events, 28.2 us)
Async XLA Ops:
  7.2 108.0 %all-gather.3.cloned.1.call-start = ((), (), s32[]{:S(2)}) async-start(), calls=%async_computation.5 | async-start | bytes 1880064 | tf_op jit(solution)/shard_map/all_gather | solution.py:371
  7.2 48.4 %collective-permute-start.4 = (bf16[512,1024]{1,0:T(8,128)(2,1)}, bf16[512,1024]{1,0:T(8,128)(2,1)}, u32[]{:S(2)}, u32[]{:S(2)}) collective-permute-start(bf16[512,1024]{1,0:T(8,128)(2,1)} %rest_0_.1), channel_id=1, source_target_pairs={{0,4},{1,5},{2,0},{3,1},{4,8},{5,9},{6,2},{7,3},{8,12},{9,13},{10,... | collective-permute-start | bytes 3145736 | tf_op jit(solution)/shard_map/ppermute | solution.py:17
  9.4 47.6 %collective-permute-start.9 = (bf16[512,1024]{1,0:T(8,128)(2,1)}, bf16[512,1024]{1,0:T(8,128)(2,1)}, u32[]{:S(2)}, u32[]{:S(2)}) collective-permute-start(bf16[512,1024]{1,0:T(8,128)(2,1)} %rest_0_.1), channel_id=1, source_target_pairs={{0,2},{1,3},{2,6},{3,7},{4,0},{5,1},{6,10},{7,11},{8,4},{9,5},{10,... | collective-permute-start | bytes 3145736 | tf_op jit(solution)/shard_map/ppermute | solution.py:17
  14.1 7.8 %copy-start.21 = (bf16[3,16,1024]{2,1,0:T(8,128)(2,1)S(1)}, bf16[3,16,1024]{2,1,0:T(8,128)(2,1)}, u32[]{:S(2)}) copy-start(bf16[3,16,1024]{2,1,0:T(8,128)(2,1)} %param.27) | copy-start | bytes 294916
  19.6 2.2 copy-start.6
  22.6 7.5 %copy-start.23 = (s32[32]{0:T(128)S(1)}, s32[32]{0:T(128)}, u32[]{:S(2)}) copy-start(s32[32]{0:T(128)} %param.24) | copy-start | bytes 388
  22.6 10.4 %copy-start.24 = (s32[8]{0:T(128)S(1)}, s32[8]{0:T(128)}, u32[]{:S(2)}) copy-start(s32[8]{0:T(128)} %constant.298.clone) | copy-start | bytes 100
  22.6 15.6 %copy-start.22 = (s32[8]{0:T(128)S(1)}, s32[8]{0:T(128)}, u32[]{:S(2)}) copy-start(s32[8]{0:T(128)} %constant.297.clone) | copy-start | bytes 100
  22.7 18.2 %copy-start.16 = (s32[192]{0:T(256)S(1)}, s32[192]{0:T(256)}, u32[]{:S(2)}) copy-start(s32[192]{0:T(256)} %param.23) | copy-start | bytes 2308
  22.7 32.2 %copy-start.3 = (bf16[3,16,8192]{2,1,0:T(8,128)(2,1)S(1)}, bf16[3,16,8192]{2,1,0:T(8,128)(2,1)}, u32[]{:S(2)}) copy-start(bf16[3,16,8192]{2,1,0:T(8,128)(2,1)} %param.26) | copy-start | bytes 2359300
  22.7 144.2 %all-to-all-start = ((bf16[16,288,512]{2,1,0:T(8,128)(2,1)}), bf16[16,288,512]{2,1,0:T(8,128)(2,1)}, u32[]{:S(2)}, u32[]{:S(2)}) async-start(bf16[16,288,512]{2,1,0:T(8,128)(2,1)} %copy-done.6), calls=%async_computation | async-start | bytes 9437184 | tf_op jit(solution)/shard_map/all_to_all | solution.py:415
  55.6 84.9 %collective-permute-start.5 = (bf16[512,1024]{1,0:T(8,128)(2,1)}, bf16[512,1024]{1,0:T(8,128)(2,1)S(1)}, u32[]{:S(2)}, u32[]{:S(2)}) collective-permute-start(bf16[512,1024]{1,0:T(8,128)(2,1)} %collective-permute-done.4.rest_0_), channel_id=1, source_target_pairs={{0,4},{1,5},{2,0},{3,1},{4,8},{5,9},{6,2},{7,3},{8,12},{9,13},{10,... | collective-permute-start | bytes 3145736 | tf_op jit(solution)/shard_map/ppermute | solution.py:17
  57.0 89.2 %collective-permute-start.10 = (bf16[512,1024]{1,0:T(8,128)(2,1)}, bf16[512,1024]{1,0:T(8,128)(2,1)}, u32[]{:S(2)}, u32[]{:S(2)}) collective-permute-start(bf16[512,1024]{1,0:T(8,128)(2,1)} %collective-permute-done.9.rest_2_), channel_id=1, source_target_pairs={{0,2},{1,3},{2,6},{3,7},{4,0},{5,1},{6,10},{7,11},{8,4},{9,5},{10,... | collective-permute-start | bytes 3145736 | tf_op jit(solution)/shard_map/ppermute | solution.py:17
  115.2 34.8 %collective-permute-start = (bf16[16,8192]{1,0:T(8,128)(2,1)}, bf16[16,8192]{1,0:T(8,128)(2,1)S(1)}, u32[]{:S(2)}, u32[]{:S(2)}) collective-permute-start(bf16[16,8192]{1,0:T(8,128)(2,1)} %shard_map.222), channel_id=1, source_target_pairs={{0,4},{1,5},{2,6},{3,7},{4,8},{5,9},{6,10},{7,11},{8,12},{9,13},{1... | collective-permute-start | bytes 786440 | tf_op jit(solution)/shard_map/ppermute | solution.py:17
  115.5 41.9 %collective-permute-start.1 = (bf16[16,8192]{1,0:T(8,128)(2,1)}, bf16[16,8192]{1,0:T(8,128)(2,1)S(1)}, u32[]{:S(2)}, u32[]{:S(2)}) collective-permute-start(bf16[16,8192]{1,0:T(8,128)(2,1)} %shard_map.222), channel_id=1, source_target_pairs={{0,3},{1,4},{2,5},{3,6},{4,7},{5,8},{6,9},{7,10},{8,11},{9,12},{10... | collective-permute-start | bytes 786440 | tf_op jit(solution)/shard_map/ppermute | solution.py:17
  115.7 46.1 %collective-permute-start.2 = (bf16[16,8192]{1,0:T(8,128)(2,1)}, bf16[16,8192]{1,0:T(8,128)(2,1)}, u32[]{:S(2)}, u32[]{:S(2)}) collective-permute-start(bf16[16,8192]{1,0:T(8,128)(2,1)} %shard_map.222), channel_id=1, source_target_pairs={{0,2},{1,3},{2,4},{3,5},{4,6},{5,7},{6,8},{7,9},{8,10},{9,11},{10,... | collective-permute-start | bytes 786440 | tf_op jit(solution)/shard_map/ppermute | solution.py:17
  116.7 2.9 copy-start.12
  119.6 20.9 %copy-start.19 = (bf16[16,8192]{1,0:T(8,128)(2,1)S(1)}, bf16[16,8192]{1,0:T(8,128)(2,1)}, u32[]{:S(2)}) copy-start(bf16[16,8192]{1,0:T(8,128)(2,1)} %shard_map.222) | copy-start | bytes 786436
  140.6 93.2 %copy-start.7 = (bf16[512,1024]{1,0:T(8,128)(2,1)}, bf16[512,1024]{1,0:T(8,128)(2,1)S(1)}, u32[]{:S(2)}) copy-start(bf16[512,1024]{1,0:T(8,128)(2,1)S(1)} %collective-permute-done.5.refs_0_.rest_0_) | copy-start | bytes 3145732
  140.6 23.3 %collective-permute-start.3 = (bf16[16,8192]{1,0:T(8,128)(2,1)S(1)}, bf16[16,8192]{1,0:T(8,128)(2,1)S(1)}, u32[]{:S(2)}, u32[]{:S(2)}) collective-permute-start(bf16[16,8192]{1,0:T(8,128)(2,1)S(1)} %copy-done.19), channel_id=1, source_target_pairs={{0,1},{1,2},{2,3},{3,4},{4,5},{5,6},{6,7},{7,8},{8,9},{9,10},{10,1... | collective-permute-start | bytes 786440 | tf_op jit(solution)/shard_map/ppermute | solution.py:17
  146.3 75.7 %collective-permute-start.20 = (bf16[512,1024]{1,0:T(8,128)(2,1)}, bf16[512,1024]{1,0:T(8,128)(2,1)}, u32[]{:S(2)}, u32[]{:S(2)}) collective-permute-start(bf16[512,1024]{1,0:T(8,128)(2,1)} %rest_0_.1), channel_id=1, source_target_pairs={{0,1},{1,0},{2,3},{3,2},{4,5},{5,4},{6,7},{7,6},{8,9},{9,8},{10,11... | collective-permute-start | bytes 3145736 | tf_op jit(solution)/shard_map/ppermute | solution.py:17
  150.0 77.2 %collective-permute-start.18 = (bf16[512,1024]{1,0:T(8,128)(2,1)}, bf16[512,1024]{1,0:T(8,128)(2,1)}, u32[]{:S(2)}, u32[]{:S(2)}) collective-permute-start(bf16[512,1024]{1,0:T(8,128)(2,1)} %collective-permute-done.4.rest_0_), channel_id=1, source_target_pairs={{0,1},{1,0},{2,3},{3,2},{4,5},{5,4},{6,7},{7,6},{8,9},{9,8},{10,11... | collective-permute-start | bytes 3145736 | tf_op jit(solution)/shard_map/ppermute | solution.py:17
  157.4 69.8 %collective-permute-start.19 = (bf16[512,1024]{1,0:T(8,128)(2,1)}, bf16[512,1024]{1,0:T(8,128)(2,1)}, u32[]{:S(2)}, u32[]{:S(2)}) collective-permute-start(bf16[512,1024]{1,0:T(8,128)(2,1)} %collective-permute-done.9.rest_2_), channel_id=1, source_target_pairs={{0,1},{1,0},{2,3},{3,2},{4,5},{5,4},{6,7},{7,6},{8,9},{9,8},{10,11... | collective-permute-start | bytes 3145736 | tf_op jit(solution)/shard_map/ppermute | solution.py:17
  161.8 72.0 %collective-permute-start.16 = (bf16[512,1024]{1,0:T(8,128)(2,1)S(1)}, bf16[512,1024]{1,0:T(8,128)(2,1)}, u32[]{:S(2)}, u32[]{:S(2)}) collective-permute-start(bf16[512,1024]{1,0:T(8,128)(2,1)S(1)} %collective-permute-done.5.refs_0_.rest_0_), channel_id=1, source_target_pairs={{0,1},{1,0},{2,3},{3,2},{4,5},{5,4},{6,7},{7,6},{8,9},{9,8},{10,11... | collective-permute-start | bytes 3145736 | tf_op jit(solution)/shard_map/ppermute | solution.py:17
  163.8 70.0 %collective-permute-start.17 = (bf16[512,1024]{1,0:T(8,128)(2,1)}, bf16[512,1024]{1,0:T(8,128)(2,1)}, u32[]{:S(2)}, u32[]{:S(2)}) collective-permute-start(bf16[512,1024]{1,0:T(8,128)(2,1)} %collective-permute-done.10.refs_0_.rest_2_), channel_id=1, source_target_pairs={{0,1},{1,0},{2,3},{3,2},{4,5},{5,4},{6,7},{7,6},{8,9},{9,8},{10,11... | collective-permute-start | bytes 3145736 | tf_op jit(solution)/shard_map/ppermute | solution.py:17
  168.8 42.7 %copy-start.17 = (bf16[384,512]{1,0:T(8,128)(2,1)}, bf16[384,512]{1,0:T(8,128)(2,1)S(1)}, u32[]{:S(2)}) copy-start(bf16[384,512]{1,0:T(8,128)(2,1)S(1)} %convolution_convert_fusion) | copy-start | bytes 1179652
  168.8 34.2 %copy-start.13 = (s32[1,3072]{1,0:T(1,128)S(1)}, s32[1,3072]{1,0:T(1,128)}, u32[]{:S(2)}) copy-start(s32[1,3072]{1,0:T(1,128)} %shard_map.223.slot.refs_0_) | copy-start | bytes 36868
  170.3 41.3 %all-to-all-start.1 = ((bf16[16,16,192]{2,1,0:T(8,128)(2,1)}), bf16[16,16,192]{2,1,0:T(8,128)(2,1)S(1)}, u32[]{:S(2)}, u32[]{:S(2)}) async-start(bf16[16,16,192]{2,1,0:T(8,128)(2,1)} %broadcast_in_dim.139), calls=%async_computation.1 | async-start | bytes 262144 | tf_op jit(solution)/shard_map/all_to_all | solution.py:28
  211.5 1.9 copy-start.14
  213.4 8.5 %copy-start = (bf16[48,8192]{1,0:T(8,128)(2,1)S(1)}, bf16[48,8192]{1,0:T(8,128)(2,1)}, u32[]{:S(2)}) copy-start(bf16[48,8192]{1,0:T(8,128)(2,1)} %pad_maximum_fusion.1.refs_2_.down) | copy-start | bytes 2359300
  222.8 4.3 %copy-start.5 = (bf16[384,16]{1,0:T(8,128)(2,1)S(1)}, bf16[384,16]{1,0:T(8,128)(2,1)}, u32[]{:S(2)}) copy-start(bf16[384,16]{1,0:T(8,128)(2,1)} %shard_map.227.grad) | copy-start | bytes 36868
  240.0 25.0 %collective-permute-start.6 = (bf16[512,1024]{1,0:T(8,128)(2,1)}, bf16[512,1024]{1,0:T(8,128)(2,1)S(1)}, u32[]{:S(2)}, u32[]{:S(2)}) collective-permute-start(bf16[512,1024]{1,0:T(8,128)(2,1)} %shard_map.228), channel_id=1, source_target_pairs={{0,4},{1,5},{2,0},{3,1},{4,8},{5,9},{6,2},{7,3},{8,12},{9,13},{10,... | collective-permute-start | bytes 3145736 | tf_op jit(solution)/shard_map/ppermute | solution.py:17
  241.4 24.9 %collective-permute-start.11 = (bf16[512,1024]{1,0:T(8,128)(2,1)}, bf16[512,1024]{1,0:T(8,128)(2,1)}, u32[]{:S(2)}, u32[]{:S(2)}) collective-permute-start(bf16[512,1024]{1,0:T(8,128)(2,1)} %shard_map.230), channel_id=1, source_target_pairs={{0,2},{1,3},{2,6},{3,7},{4,0},{5,1},{6,10},{7,11},{8,4},{9,5},{10,... | collective-permute-start | bytes 3145736 | tf_op jit(solution)/shard_map/ppermute | solution.py:17
  244.2 28.5 %all-to-all-start.2 = ((f32[16,16,192]{2,1,0:T(8,128)}), f32[16,16,192]{2,1,0:T(8,128)}, u32[]{:S(2)}, u32[]{:S(2)}) async-start(f32[16,16,192]{2,1,0:T(8,128)} %bitcast.134), calls=%async_computation.2 | async-start | bytes 524288 | tf_op jit(solution)/shard_map/all_to_all | solution.py:435
  265.1 28.5 %copy-start.1 = (bf16[512,1024]{1,0:T(8,128)(2,1)}, bf16[512,1024]{1,0:T(8,128)(2,1)S(1)}, u32[]{:S(2)}) copy-start(bf16[512,1024]{1,0:T(8,128)(2,1)S(1)} %collective-permute-done.6.refs_0_.rest_0_) | copy-start | bytes 3145732
  265.1 28.5 %collective-permute-start.14 = (bf16[512,1024]{1,0:T(8,128)(2,1)S(1)}, bf16[512,1024]{1,0:T(8,128)(2,1)}, u32[]{:S(2)}, u32[]{:S(2)}) collective-permute-start(bf16[512,1024]{1,0:T(8,128)(2,1)S(1)} %collective-permute-done.6.refs_0_.rest_0_), channel_id=1, source_target_pairs={{0,1},{1,0},{2,3},{3,2},{4,5},{5,4},{6,7},{7,6},{8,9},{9,8},{10,11... | collective-permute-start | bytes 3145736 | tf_op jit(solution)/shard_map/ppermute | solution.py:17
  266.2 27.3 %collective-permute-start.15 = (bf16[512,1024]{1,0:T(8,128)(2,1)}, bf16[512,1024]{1,0:T(8,128)(2,1)}, u32[]{:S(2)}, u32[]{:S(2)}) collective-permute-start(bf16[512,1024]{1,0:T(8,128)(2,1)} %collective-permute-done.11.refs_0_.rest_2_), channel_id=1, source_target_pairs={{0,1},{1,0},{2,3},{3,2},{4,5},{5,4},{6,7},{7,6},{8,9},{9,8},{10,11... | collective-permute-start | bytes 3145736 | tf_op jit(solution)/shard_map/ppermute | solution.py:17
  274.3 10.9 %all-to-all-start.3 = ((bf16[16,16,192]{2,1,0:T(8,128)(2,1)}), bf16[16,16,192]{2,1,0:T(8,128)(2,1)S(1)}, u32[]{:S(2)}, u32[]{:S(2)}) async-start(bf16[16,16,192]{2,1,0:T(8,128)(2,1)} %broadcast_in_dim.145), calls=%async_computation.3 | async-start | bytes 262144 | tf_op jit(solution)/shard_map/all_to_all | solution.py:28
  285.2 48.7 %all-to-all-start.4 = ((bf16[16,48,512]{2,1,0:T(8,128)(2,1)}), bf16[16,48,512]{2,1,0:T(8,128)(2,1)}, u32[]{:S(2)}, u32[]{:S(2)}) async-start(bf16[16,48,512]{2,1,0:T(8,128)(2,1)} %bitcast.61), calls=%async_computation.4 | async-start | bytes 1572864 | tf_op jit(solution)/shard_map/all_to_all | solution.py:439
  290.6 9.2 %copy-start.20 = (bf16[16,3072]{1,0:T(8,128)(2,1)}, bf16[16,3072]{1,0:T(8,128)(2,1)S(1)}, u32[]{:S(2)}) copy-start(bf16[16,3072]{1,0:T(8,128)(2,1)S(1)} %reshape.290.refs_1_) | copy-start | bytes 294916
  301.7 30.9 %collective-permute-start.12 = (bf16[256,1024]{1,0:T(8,128)(2,1)}, bf16[256,1024]{1,0:T(8,128)(2,1)S(1)}, u32[]{:S(2)}, u32[]{:S(2)}) collective-permute-start(bf16[256,1024]{1,0:T(8,128)(2,1)} %slice.141), channel_id=1, source_target_pairs={{0,2},{1,3},{2,6},{3,7},{4,0},{5,1},{6,10},{7,11},{8,4},{9,5},{10,... | collective-permute-start | bytes 1572872 | tf_op jit(solution)/shard_map/ppermute | solution.py:17
  305.0 28.1 %collective-permute-start.7 = (bf16[256,1024]{1,0:T(8,128)(2,1)}, bf16[256,1024]{1,0:T(8,128)(2,1)S(1)}, u32[]{:S(2)}, u32[]{:S(2)}) collective-permute-start(bf16[256,1024]{1,0:T(8,128)(2,1)} %slice.140), channel_id=1, source_target_pairs={{0,4},{1,5},{2,0},{3,1},{4,8},{5,9},{6,2},{7,3},{8,12},{9,13},{10,... | collective-permute-start | bytes 1572872 | tf_op jit(solution)/shard_map/ppermute | solution.py:17
  308.0 19.8 %collective-permute-start.21 = (f32[16,1024]{1,0:T(8,128)S(1)}, f32[16,1024]{1,0:T(8,128)S(1)}, u32[]{:S(2)}, u32[]{:S(2)}) collective-permute-start(f32[16,1024]{1,0:T(8,128)S(1)} %get-tuple-element.45), channel_id=1, source_target_pairs={{0,15},{1,0},{2,1},{3,2},{4,3},{5,4},{6,5},{7,6},{8,7},{9,8},{10,9... | collective-permute-start | bytes 196616 | tf_op jit(solution)/shard_map/ppermute | solution.py:17
  322.6 5.6 %collective-permute-start.22 = (f32[16,1024]{1,0:T(8,128)S(1)}, f32[16,1024]{1,0:T(8,128)S(1)}, u32[]{:S(2)}, u32[]{:S(2)}) collective-permute-start(f32[16,1024]{1,0:T(8,128)S(1)} %get-tuple-element.45), channel_id=1, source_target_pairs={{0,14},{1,15},{2,0},{3,1},{4,2},{5,3},{6,4},{7,5},{8,6},{9,7},{10,... | collective-permute-start | bytes 196616 | tf_op jit(solution)/shard_map/ppermute | solution.py:17
  326.7 4.1 %collective-permute-start.23 = (f32[16,1024]{1,0:T(8,128)S(1)}, f32[16,1024]{1,0:T(8,128)S(1)}, u32[]{:S(2)}, u32[]{:S(2)}) collective-permute-start(f32[16,1024]{1,0:T(8,128)S(1)} %get-tuple-element.45), channel_id=1, source_target_pairs={{0,13},{1,14},{2,15},{3,0},{4,1},{5,2},{6,3},{7,4},{8,5},{9,6},{10... | collective-permute-start | bytes 196616 | tf_op jit(solution)/shard_map/ppermute | solution.py:17
  327.8 4.8 %collective-permute-start.24 = (f32[16,1024]{1,0:T(8,128)S(1)}, f32[16,1024]{1,0:T(8,128)S(1)}, u32[]{:S(2)}, u32[]{:S(2)}) collective-permute-start(f32[16,1024]{1,0:T(8,128)S(1)} %get-tuple-element.45), channel_id=1, source_target_pairs={{0,12},{1,13},{2,14},{3,15},{4,0},{5,1},{6,2},{7,3},{8,4},{9,5},{1... | collective-permute-start | bytes 196616 | tf_op jit(solution)/shard_map/ppermute | solution.py:17
  332.6 7.3 %collective-permute-start.13 = (bf16[256,1024]{1,0:T(8,128)(2,1)S(1)}, bf16[256,1024]{1,0:T(8,128)(2,1)S(1)}, u32[]{:S(2)}, u32[]{:S(2)}) collective-permute-start(bf16[256,1024]{1,0:T(8,128)(2,1)S(1)} %collective-permute-done.12.rest_2_), channel_id=1, source_target_pairs={{0,1},{1,0},{2,3},{3,2},{4,5},{5,4},{6,7},{7,6},{8,9},{9,8},{10,11... | collective-permute-start | bytes 1572872 | tf_op jit(solution)/shard_map/ppermute | solution.py:17
  333.1 6.9 %collective-permute-start.8 = (bf16[256,1024]{1,0:T(8,128)(2,1)S(1)}, bf16[256,1024]{1,0:T(8,128)(2,1)}, u32[]{:S(2)}, u32[]{:S(2)}) collective-permute-start(bf16[256,1024]{1,0:T(8,128)(2,1)S(1)} %collective-permute-done.7.rest_0_), channel_id=1, source_target_pairs={{0,1},{1,0},{2,3},{3,2},{4,5},{5,4},{6,7},{7,6},{8,9},{9,8},{10,11... | collective-permute-start | bytes 1572872 | tf_op jit(solution)/shard_map/ppermute | solution.py:17
  (8 other events, 9.0 us)
Sparse Core Ops, SparseCore 0:
  22.7 92.4 all-gather.2

commit v5 on v2

v5 whole, which is shorter than its diff:
```python
import functools

import jax
import jax.numpy as jnp
from jax import lax
from jax.experimental import pallas as pl
from jax.experimental.pallas import tpu as pltpu
from jax.sharding import PartitionSpec as P

BLOCK = 128
HOPS = 4
LANES = 128
DIGIT = 64
VMEM = 56 << 20

adapter_scale = 2.0


def permuted(value, pairs):
    return lax.ppermute(value, "blk", pairs)


def moved(value, steps):
    count = lax.axis_size("blk")
    return permuted(value, [(i, (i + steps) % count) for i in range(count)])


def to_all(value):
    count = lax.axis_size("blk")
    copies = jnp.broadcast_to(value[None], (count,) + value.shape)
    return lax.all_to_all(copies, "blk", split_axis=0, concat_axis=0)


def after(value, *others):
    anywhere = pl.BlockSpec(memory_space=pl.ANY)
    return pl.pallas_call(
        lambda *refs: None,
        in_specs=[anywhere] * (1 + len(others)),
        out_specs=anywhere,
        out_shape=jax.ShapeDtypeStruct(value.shape, value.dtype),
        input_output_aliases={0: 0},
        cost_estimate=pl.CostEstimate(flops=0, bytes_accessed=0, transcendentals=0),
    )(value, *others)


def dot(a, b, dims):
    return lax.dot_general(a, b, (dims, ((), ())), preferred_element_type=jnp.float32)


def starts_of(blocks, start_ids):
    latest = jnp.max(
        jnp.where(start_ids[None, :] <= blocks[:, None], start_ids[None, :], -1), axis=1
    )
    return jnp.where(latest >= 0, latest, jnp.max(start_ids))


def as_digits(rows):
    return rows % DIGIT, rows // DIGIT % DIGIT, rows // (DIGIT * DIGIT)


def from_digits(digits):
    low, middle, high = [digits[:, k].astype(jnp.int32) for k in range(3)]
    return (high * DIGIT + middle) * DIGIT + low


def ring_shards(weight, ties):
    count, device = lax.axis_size("blk"), lax.axis_index("blk")
    chips = count // 2
    order = list(range(0, chips, 2)) + list(range(chips - 1, 0, -2))
    place = [order.index(chip) for chip in range(chips)]
    chip, core = device // 2, device % 2

    def along(step):
        return [
            (2 * c + k, 2 * order[(place[c] + step) % chips] + k)
            for c in range(chips)
            for k in range(2)
        ]

    def origin(step):
        return jnp.array(order, jnp.int32)[
            (jnp.array(place, jnp.int32)[chip] + step + chips) % chips
        ]

    def both(piece, source, per, part):
        other = permuted(piece, [(i, i ^ 1) for i in range(count)])
        return [
            (piece, (2 * source + core) * per + part),
            (other, (2 * source + 1 - core) * per + part),
        ]

    groups = [both(weight, chip, 1, 0)]
    up = down = weight
    for step in range(1, chips // 2):
        up, down = permuted(up, along(1)), permuted(down, along(-1))
        groups.append(both(up, origin(-step), 1, 0) + both(down, origin(step), 1, 0))
        if step in ties:
            up, down = after(up, ties[step]), after(down, ties[step])
    half = weight.shape[0] // 2
    up, down = permuted(up[:half], along(1)), permuted(down[half:], along(-1))
    far = origin(chips // 2)
    groups.append(both(up, far, 2, 0) + both(down, far, 2, 1))
    return groups


def stripes_kernel(where, cot, grad, down, *rest):
    out = rest[-1]
    rank = grad.shape[1]

    def product(weight):
        frozen = dot(cot[...], weight[...], ((1,), (1,)))
        for b in range(cot.shape[0] // BLOCK):
            rows = slice(b * BLOCK, (b + 1) * BLOCK)
            lora = adapter_scale * dot(
                grad[rows, :], down[b * rank : (b + 1) * rank, :], ((1,), (0,))
            )
            lora = lora.astype(jnp.bfloat16).astype(jnp.float32)
            out[rows, :] = (frozen[rows] + lora).astype(jnp.bfloat16)

    for number in range(where.shape[0]):
        pl.when(pl.program_id(0) == number)(lambda weight=rest[number]: product(weight))


def write_stripes(group, cot, grad, down, out=None):
    rows, depth = cot.shape
    width = down.shape[1]
    count = len(group)
    stripe = group[0][0].shape[0]
    where = jnp.stack([place for _, place in group]).astype(jnp.int32)
    specs = [
        pl.BlockSpec((rows, depth), lambda j, where: (0, 0)),
        pl.BlockSpec(grad.shape, lambda j, where: (0, 0)),
        pl.BlockSpec((down.shape[0], stripe), lambda j, where: (0, where[j])),
    ] + [pl.BlockSpec((stripe, depth), lambda j, where: (0, 0)) for _ in group]
    args = [where, cot, grad, down] + [piece for piece, _ in group]
    alias = {}
    if out is not None:
        specs.append(pl.BlockSpec(memory_space=pl.ANY))
        args.append(out)
        alias = {len(args) - 1: 0}
    return pl.pallas_call(
        stripes_kernel,
        grid_spec=pltpu.PrefetchScalarGridSpec(
            num_scalar_prefetch=1,
            grid=(count,),
            in_specs=specs,
            out_specs=pl.BlockSpec((rows, stripe), lambda j, where: (0, where[j])),
        ),
        out_shape=jax.ShapeDtypeStruct((rows, width), jnp.bfloat16),
        input_output_aliases=alias,
        cost_estimate=pl.CostEstimate(
            flops=2 * rows * depth * stripe * count,
            bytes_accessed=2 * (depth + rows) * stripe * count,
            transcendentals=0,
        ),
        compiler_params=pltpu.CompilerParams(vmem_limit_bytes=VMEM),
    )(*args)


def small_stripes(groups, cot, grad, down, rank):
    depth = cot.shape[1]
    weight = jnp.zeros((down.shape[1], depth), jnp.bfloat16)
    for piece, place in sum(groups, []):
        weight = lax.dynamic_update_slice(weight, piece, (place * piece.shape[0], 0))
    lora = [
        dot(
            grad[b * BLOCK : (b + 1) * BLOCK], down[b * rank : (b + 1) * rank], ((1,), (0,))
        )
        for b in range(cot.shape[0] // BLOCK)
    ]
    lora = (adapter_scale * jnp.concatenate(lora, axis=0)).astype(jnp.bfloat16)
    out = dot(cot, weight, ((1,), (1,)))
    return (out + lora.astype(jnp.float32)).astype(jnp.bfloat16)


def pack_kernel(rows, wide_rows, act, maps, cot, out):
    tokens, features = act.shape
    shared = maps.shape[0]
    cap = shared * features // cot.shape[1]
    target = pl.program_id(0)
    mine = rows[...] // (cap * pl.num_programs(0)) == target
    first = lax.broadcasted_iota(jnp.int32, (tokens, tokens), 0)
    later = lax.broadcasted_iota(jnp.int32, (tokens, tokens), 1)
    earlier = jnp.where(first < later, 1.0, 0.0).astype(jnp.bfloat16)
    chosen = jnp.broadcast_to(jnp.where(mine, 1.0, 0.0), (8, tokens)).astype(jnp.bfloat16)
    place = dot(chosen, earlier, ((1,), (0,)))[:1].astype(jnp.int32)
    place = jnp.where(mine, place, -1)
    send = lax.broadcasted_iota(jnp.int32, (cap, tokens), 0) == place
    send = jnp.where(send, 1.0, 0.0).astype(jnp.bfloat16)
    sent = [
        dot(send, cot[:, k : k + features], ((1,), (0,)))
        for k in range(0, cot.shape[1], features)
    ]
    which = lax.broadcasted_iota(jnp.int32, (16, features), 0)
    low, middle, high = as_digits(wide_rows[...])
    digits = jnp.where(which == 0, low, jnp.where(which == 1, middle, high))
    out[0, :tokens, :] = act[...]
    out[0, tokens : tokens + shared, :] = maps[...]
    out[0, tokens + shared : tokens + 2 * shared, :] = jnp.concatenate(sent, axis=0).astype(
        out.dtype
    )
    out[0, tokens + 2 * shared :, :] = digits.astype(jnp.float32).astype(out.dtype)


def pack(rows, act, maps, cot, devices, cap):
    tokens, width = act.shape
    features = width // devices
    shared = maps.shape[0]
    total = tokens + 2 * shared + 16
    if features % LANES == 0 and cap % 8 == 0 and features >= tokens:
        return pl.pallas_call(
            pack_kernel,
            grid=(devices,),
            in_specs=[
                pl.BlockSpec((1, tokens), lambda j: (0, 0)),
                pl.BlockSpec((1, features), lambda j: (0, 0)),
                pl.BlockSpec((tokens, features), lambda j: (0, j)),
                pl.BlockSpec((shared, features), lambda j: (0, j)),
                pl.BlockSpec(cot.shape, lambda j: (0, 0)),
            ],
            out_specs=pl.BlockSpec((1, total, features), lambda j: (j, 0, 0)),
            out_shape=jax.ShapeDtypeStruct((devices, total, features), act.dtype),
            cost_estimate=pl.CostEstimate(
                flops=2 * devices * cap * tokens * cot.shape[1],
                bytes_accessed=4 * devices * total * features,
                transcendentals=0,
            ),
            compiler_params=pltpu.CompilerParams(vmem_limit_bytes=VMEM),
        )(rows[None], jnp.pad(rows, (0, features - tokens))[None], act, maps, cot)
    target = rows // (cap * devices)
    order = jnp.arange(tokens, dtype=jnp.int32)
    before = (target[:, None] == target[None, :]) & (order[None, :] < order[:, None])
    place = target * cap + jnp.sum(before.astype(jnp.int32), axis=1)
    send = jnp.arange(cap * devices, dtype=jnp.int32)[:, None] == place[None, :]
    sent = dot(send.astype(jnp.bfloat16), cot, ((1,), (0,))).astype(jnp.bfloat16)
    sent = sent.reshape(devices, cap, cot.shape[1])
    digits = jnp.stack(as_digits(rows)).astype(jnp.bfloat16)
    digits = jnp.pad(digits, ((0, 0), (0, -tokens % features))).reshape(-1, features)
    digits = jnp.pad(digits, ((0, 16 - digits.shape[0]), (0, 0)))
    parts = [
        act.reshape(tokens, devices, features).transpose(1, 0, 2),
        maps.reshape(shared, devices, features).transpose(1, 0, 2),
    ]
    parts += [sent[:, :, k : k + features] for k in range(0, cot.shape[1], features)]
    parts += [jnp.broadcast_to(digits[None], (devices,) + digits.shape)]
    return jnp.concatenate(parts, axis=1)


def slot_chunks(width):
    size = min(width, 768)
    while width % size:
        size //= 2
    return [slice(k, k + size) for k in range(0, width, size)]


def slot_of(rows, starts):
    blocks = rows // BLOCK
    latest = jnp.max(jnp.where(starts <= blocks, starts, -1), axis=0, keepdims=True)
    return jnp.where(latest >= 0, latest, jnp.max(starts))


def own_rows(slot, first, size, rank):
    index = first // rank + lax.broadcasted_iota(jnp.int32, (size // rank, rank, 1), 0)
    return index == slot[None]


def exchange_map(rows, devices, places):
    tokens = rows.shape[1]
    cap = places // devices
    target = rows // places
    to = lax.broadcasted_iota(jnp.int32, (devices, tokens), 0) == target
    first = lax.broadcasted_iota(jnp.int32, (tokens, tokens), 0)
    later = lax.broadcasted_iota(jnp.int32, (tokens, tokens), 1)
    earlier = jnp.where(first < later, 1.0, 0.0).astype(jnp.bfloat16)
    ahead = dot(jnp.where(to, 1.0, 0.0).astype(jnp.bfloat16), earlier, ((1,), (0,)))
    ahead = jnp.sum(jnp.where(to, ahead, 0.0), axis=0, keepdims=True).astype(jnp.int32)
    place = target * cap + ahead
    hit = lax.broadcasted_iota(jnp.int32, (places, tokens), 0) == place
    return jnp.where(hit, 1.0, 0.0).astype(jnp.bfloat16)


def hidden_kernel(devices, act, maps, rows, starts, out):
    sources, _, tokens = rows.shape
    rank, places = out.shape[0] // sources, out.shape[1]
    share = maps.shape[1]
    for k in range(sources):
        slot = slot_of(rows[k], starts[...])
        total = jnp.zeros((rank, tokens), jnp.float32)
        for part in slot_chunks(maps.shape[0] * share):
            size = part.stop - part.start
            some = maps[part.start // share : part.stop // share].reshape(size, -1)
            each = dot(some, act[k, :tokens, :], ((1,), (1,))).reshape(size // rank, rank, -1)
            total += jnp.sum(
                jnp.where(own_rows(slot, part.start, size, rank), each, 0.0), axis=0
            )
        high = total.astype(jnp.bfloat16)
        low = (total - high.astype(jnp.float32)).astype(jnp.bfloat16)
        place = exchange_map(rows[k], devices, places)
        out[k * rank : (k + 1) * rank, :] = dot(high, place, ((1,), (1,))) + dot(
            low, place, ((1,), (1,))
        )


def down_kernel(devices, act, grad, rows, starts, out, total):
    sources, _, tokens = rows.shape
    rank, places = grad.shape[0] // sources, grad.shape[1]
    step = pl.program_id(0)

    @pl.when(step == 0)
    def _():
        total[...] = jnp.zeros_like(total)

    for k in range(sources):
        slot = slot_of(rows[k], starts[...])
        place = exchange_map(rows[k], devices, places)
        wide = dot(grad[k * rank : (k + 1) * rank, :], place, ((1,), (0,)))[None]
        for part in slot_chunks(total.shape[0]):
            size = part.stop - part.start
            placed = jnp.where(own_rows(slot, part.start, size, rank), wide, 0.0)
            placed = placed.reshape(size, -1).astype(jnp.bfloat16)
            total[part, :] += dot(placed, act[k, :tokens, :], ((1,), (0,)))

    @pl.when(step == pl.num_programs(0) - 1)
    def _():
        out[...] = (adapter_scale * total[...]).astype(out.dtype)


def feature_calls(received, tokens, share, rank, places, starts):
    devices, packed, features = received.shape
    width = devices * share
    sources = 2
    grid = (devices // sources,)
    act = pl.BlockSpec((sources, packed, features), lambda j: (j, 0, 0))
    maps = pl.BlockSpec((devices, share, features), lambda j: (0, tokens // share, 0))
    rows = pl.BlockSpec((sources, 1, tokens), lambda j: (j, 0, 0))
    begin = pl.BlockSpec((starts, 1), lambda j: (0, 0))
    placed = pl.BlockSpec((sources * rank, places), lambda j: (j, 0))
    cost = pl.CostEstimate(
        flops=2 * devices * tokens * width * features,
        bytes_accessed=2 * devices * tokens * features,
        transcendentals=0,
    )
    params = pltpu.CompilerParams(vmem_limit_bytes=VMEM)
    hidden = pl.pallas_call(
        functools.partial(hidden_kernel, devices),
        grid=grid,
        in_specs=[act, maps, rows, begin],
        out_specs=placed,
        out_shape=jax.ShapeDtypeStruct((devices * rank, places), jnp.float32),
        cost_estimate=cost,
        compiler_params=params,
    )
    down = pl.pallas_call(
        functools.partial(down_kernel, devices),
        grid=grid,
        in_specs=[act, placed, rows, begin],
        out_specs=pl.BlockSpec((width, features), lambda j: (0, 0)),
        out_shape=jax.ShapeDtypeStruct((width, features), jnp.bfloat16),
        scratch_shapes=[pltpu.VMEM((width, features), jnp.float32)],
        cost_estimate=cost,
        compiler_params=params,
    )
    return hidden, down


def local(
    activations,
    cotangent,
    token_layout_row,
    tenant_first_row,
    frozen_value_weight,
    adapter_down_maps,
    adapter_up_maps,
):
    devices = lax.axis_size("blk")
    device = lax.axis_index("blk")
    tokens = activations.shape[0]
    resident, rank, width = adapter_down_maps.shape
    out_width = cotangent.shape[1]
    features = width // devices
    share = resident * rank
    resident_rows = resident * BLOCK
    cap = resident_rows // devices
    start_ids = tenant_first_row // BLOCK

    flat_maps = adapter_down_maps.reshape(share, width)
    packed = pack(token_layout_row, activations, flat_maps, cotangent, devices, cap)
    received = lax.all_to_all(packed, "blk", split_axis=0, concat_axis=0)
    recv_cot = [
        received[:, tokens + share + k * cap : tokens + share + (k + 1) * cap].reshape(
            resident_rows, features
        )
        for k in range(out_width // features)
    ]
    per_digit = -(-tokens // features)
    digits = received[:, tokens + 2 * share : tokens + 2 * share + 3 * per_digit]
    digits = digits.reshape(devices, 3, per_digit * features)[:, :, :tokens]
    rows_all = from_digits(digits)

    first_block = device * resident
    block_numbers = first_block + jnp.arange(resident, dtype=jnp.int32)
    begin = starts_of(block_numbers, start_ids)
    is_local = (begin >= first_block) & (begin <= block_numbers)
    home_slot = jnp.clip(begin - first_block, 0, resident - 1)
    both_maps = jnp.concatenate([adapter_down_maps, adapter_up_maps], axis=2)
    last_map = lax.dynamic_index_in_dim(both_maps, home_slot[resident - 1], 0, keepdims=False)
    carried = jnp.zeros_like(last_map)
    for step in range(1, HOPS + 1):
        home = (device - step) % devices
        carried = jnp.where(begin[0] // resident == home, moved(last_map, step), carried)
    block_maps = []
    for b in range(resident):
        own = carried
        for k in range(b + 1):
            own = jnp.where(is_local[b] & (home_slot[b] == k), both_maps[k], own)
        block_maps.append(own)
    block_maps = jnp.concatenate(block_maps, axis=0)
    down_blocks, up_blocks = block_maps[:, :width], block_maps[:, width:]

    order = jnp.arange(tokens, dtype=jnp.int32)
    mine = rows_all // resident_rows == device
    earlier = (order[:, None] < order[None, :]).astype(jnp.bfloat16)
    ahead = dot(mine.astype(jnp.bfloat16), earlier, ((1,), (0,))).astype(jnp.int32)
    hit = mine[:, None, :] & (ahead[:, None, :] == jnp.arange(cap)[None, :, None])
    row_in = rows_all - device * resident_rows + 1
    row_in = jnp.sum(jnp.where(hit, row_in[:, None, :], 0), axis=2).reshape(-1) - 1
    arrange = row_in[:, None] == jnp.arange(resident_rows, dtype=jnp.int32)[None, :]
    arrange = arrange.astype(jnp.bfloat16)
    in_block = row_in[:, None] // BLOCK == jnp.arange(share, dtype=jnp.int32)[None, :] // rank

    grad_in = sum(
        dot(part, up_blocks[:, k * features : (k + 1) * features], ((1,), (1,)))
        for k, part in enumerate(recv_cot)
    )
    grad_in = jnp.where(in_block, grad_in, 0.0).astype(jnp.bfloat16)
    grad_in = sum(grad_in[:, b * rank : (b + 1) * rank] for b in range(resident))
    grad_sent = grad_in.reshape(devices, cap, rank).transpose(1, 0, 2).reshape(cap, -1)
    grad_all = to_all(grad_sent).reshape(resident_rows, -1).T

    starts = start_ids[:, None]
    hidden_call, down_call = feature_calls(
        received, tokens, share, rank, resident_rows, starts.shape[0]
    )
    rows_all = rows_all[:, None, :]
    shares = hidden_call(received, received, rows_all, starts)
    down_f = down_call(received, grad_all, after(rows_all, shares), starts)
    hidden = shares.T.reshape(devices, cap, -1)
    hidden = lax.all_to_all(hidden, "blk", split_axis=0, concat_axis=0)
    hidden = jnp.sum(hidden, axis=0).astype(jnp.bfloat16)
    hidden = hidden.reshape(cap, devices, rank).transpose(1, 0, 2).reshape(-1, rank)
    down_home = lax.all_to_all(down_f, "blk", split_axis=0, concat_axis=1, tiled=True)
    down_map_gradient = down_home.astype(jnp.float32).reshape(resident, rank, width)

    cot_rows = jnp.concatenate(
        [dot(arrange, part, ((0,), (0,))).astype(jnp.bfloat16) for part in recv_cot], axis=1
    )
    grad_rows = dot(arrange, grad_in, ((0,), (0,))).astype(jnp.bfloat16)
    grad_rows = after(grad_rows, down_f)
    wide = jnp.where(in_block, jnp.concatenate([hidden] * resident, axis=1), 0)
    up_all = [dot(wide, part, ((0,), (0,))) for part in recv_cot]
    up_all = jnp.concatenate(up_all, axis=1).reshape(resident, rank, out_width)
    up_parts = [up_all[b] for b in range(resident)]

    tail = sum(jnp.where(is_local[b], 0.0, up_parts[b]) for b in range(resident))
    far = jnp.zeros_like(tail)
    for step in range(1, HOPS + 1):
        other = (device + step) % devices * resident
        theirs = starts_of(other[None], start_ids)[0]
        far = far + jnp.where(theirs // resident == device, moved(tail, -step), 0.0)
    up_grads = []
    for k in range(resident):
        total = jnp.where(begin[resident - 1] == first_block + k, far, 0.0)
        for b in range(resident):
            total = total + jnp.where(is_local[b] & (home_slot[b] == k), up_parts[b], 0.0)
        up_grads.append(adapter_scale * total)
    up_map_gradient = jnp.stack(up_grads)

    chips = devices // 2
    groups = ring_shards(
        frozen_value_weight, {chips // 2 - 2: shares, chips // 2 - 1: down_f}
    )
    if frozen_value_weight.shape[0] % (2 * LANES) == 0:
        out = None
        for group in groups:
            out = write_stripes(group, cot_rows, grad_rows, down_blocks, out)
    else:
        out = small_stripes(groups, cot_rows, grad_rows, down_blocks, rank)
    return (out, down_map_gradient, up_map_gradient)


def solution(mesh):
    return jax.shard_map(
        local,
        mesh=mesh,
        in_specs=(
            P(("groups", "blk"), None),
            P(("groups", "blk"), None),
            P(("groups", "blk")),
            P("groups"),
            P("blk", None),
            P(("groups", "blk"), None, None),
            P(("groups", "blk"), None, None),
        ),
        out_specs=(
            P(("groups", "blk"), None),
            P(("groups", "blk"), None, None),
            P(("groups", "blk"), None, None),
        ),
        check_vma=False,
    )
```

time: 379 us -> 357 us (0.942)
  waiting for transfers between devices: 159 us -> 131 us
  Pallas kernels: 43.3 us -> 71 us
  starting transfers between devices: 72.2 us -> 86.4 us
  between operations: 48.6 us -> 35.4 us
  local copies, waits for them, and re-layouts: 26.6 us -> 15.9 us
  matrix products: 10.1 us -> 2.31 us
    all_gather x1 -> x0, waiting for transfers between devices: 33.9 us -> none  [local(): shared = lax.all_gather(shared, 'blk', axis=0, tiled=False)]
    pallas_call x2 -> x9, Pallas kernels: 15 us -> 39.5 us  [the longest x1 14.5 us: local(): shares = hidden_call(received, received, rows_all, starts)]
    ppermute x25, starting transfers between devices: 46 us -> 53.8 us  [permuted(): return lax.ppermute(value, 'blk', pairs)]
    dot_general x11 -> x8, matrix products: 10.1 us -> 2.31 us  [dot(): lax.dot_general(a, b, (dims, ((), ())), preferred_element_type=jnp.float32)]
    reshape x7 -> x4, local copies, waits for them, and re-layouts: 7.55 us -> 1.23 us  [the longest x1 0.82 us: local(): grad_all = to_all(grad_sent).reshape(resident_rows, -1).T]
    all_to_all x2 -> x1, starting transfers between devices: 9.97 us -> 15.9 us  [to_all(): return lax.all_to_all(copies, 'blk', split_axis=0, concat_axis=0)]
    ppermute x25, waiting for transfers between devices: 119 us -> 124 us  [permuted(): return lax.ppermute(value, 'blk', pairs)]
    concatenate x4 -> x2, other arithmetic: 6.14 us -> 1.94 us  [the longest x1 0.99 us: local(): jnp.concatenate([dot(arrange, part, ((0,), (0,))).astype(jnp.bfloat16) fo...]
  transfers between devices with their start and end apart: 31 -> 29, of which waited for: 7 -> 10; matrix products, arithmetic and copies ran while one was open for 11% -> 8% of each run, Pallas kernels for 12% -> 13%
where the time goes in v5:
time: 357 us; the launch traced here: 354 us
  waiting for transfers between devices  131 us (37%)
  starting transfers between devices  86.4 us (24%)
  Pallas kernels  71 us (20%)
  between operations  35.4 us (10%)
  local copies, waits for them, and re-layouts  15.9 us (4%)
  other arithmetic  12.4 us (3%)
    ppermute x25, waiting for transfers between devices, permuted(): return lax.ppermute(value, 'blk', pairs)  124 us
    ppermute x25, starting transfers between devices, permuted(): return lax.ppermute(value, 'blk', pairs)  53.8 us
    pallas_call x5, Pallas kernels, write_stripes(): pl.pallas_call(stripes_kernel, grid_spec=pltpu.PrefetchScalarGridSpec(num...  31.5 us
    all_to_all x1, starting transfers between devices, to_all(): return lax.all_to_all(copies, 'blk', split_axis=0, concat_axis=0)  15.9 us
    pallas_call x1, Pallas kernels, local(): shares = hidden_call(received, received, rows_all, starts)  14.5 us
    pallas_call x1, Pallas kernels, pack(): pl.pallas_call(pack_kernel, grid=(devices,), in_specs=[pl.BlockSpec((1, t...  12.7 us
    pallas_call x1, Pallas kernels, local(): down_f = down_call(received, grad_all, after(rows_all, shares), starts)  12.3 us
    all_to_all x1, starting transfers between devices, local(): received = lax.all_to_all(packed, 'blk', split_axis=0, concat_axis=0)  7.46 us
  transfers between devices with their start and end apart: 29, of which 10 were waited for; matrix products, arithmetic and copies ran while one was open for 8% of the time, Pallas kernels for 13%

profile of v5, /device:TPU:1, one launch (start us, length us, event | category | flops | bytes accessed | tf_op | source)
XLA Modules:
  0.0 354.3 jit_solution(12774568977833540620)
XLA Ops:
  0.6 1.3 pad.4
  1.9 12.7 %shard_map.220 = bf16[16,304,512]{2,1,0:T(8,128)(2,1)} custom-call(s32[1,192]{1,0:T(1,128)} %bitcast.140, s32[1,512]{1,0:T(1,128)} %bitcast.139, bf16[192,8192]{1,0:T(8,128)(2,1)} %act.1, bf16[48,8192]{1,0:T(8,128)(2,1)} %bitcast.131, bf16[192,1024]{1,0:T(8,128)(2,1)} %cot.1), custom_call_target="tpu_custom_call" | custom-call | flops 150994944 | bytes 9961472 | tf_op jit(solution)/shard_map/pallas_call | solution.py:211
  14.6 7.5 %all-to-all-start = ((bf16[16,304,512]{2,1,0:T(8,128)(2,1)}), bf16[16,304,512]{2,1,0:T(8,128)(2,1)}, u32[]{:S(2)}, u32[]{:S(2)}) async-start(bf16[16,304,512]{2,1,0:T(8,128)(2,1)} %shard_map.220), calls=%async_computation | async-start | bytes 9961472 | tf_op jit(solution)/shard_map/all_to_all | solution.py:388
  26.5 1.4 collective-permute-start
  28.0 1.7 collective-permute-start.1
  29.7 1.2 collective-permute-start.2
  30.9 1.2 collective-permute-start.3
  54.1 58.9 %collective-permute-done = bf16[16,9216]{1,0:T(8,128)(2,1)S(1)} collective-permute-done((bf16[16,9216]{1,0:T(8,128)(2,1)S(1)}, bf16[16,9216]{1,0:T(8,128)(2,1)S(1)}, u32[]{:S(2)}, u32[]{:S(2)}) %collective-permute-start) | collective-permute-done | bytes 294944 | tf_op jit(solution)/shard_map/ppermute | solution.py:20
  113.0 23.9 %collective-permute-start.4 = (bf16[512,1024]{1,0:T(8,128)(2,1)}, bf16[512,1024]{1,0:T(8,128)(2,1)}, u32[]{:S(2)}, u32[]{:S(2)}) collective-permute-start(bf16[512,1024]{1,0:T(8,128)(2,1)} %rest_0_.1), channel_id=1, source_target_pairs={{0,4},{1,5},{2,0},{3,1},{4,8},{5,9},{6,2},{7,3},{8,12},{9,13},{10,... | collective-permute-start | bytes 3145736 | tf_op jit(solution)/shard_map/ppermute | solution.py:20
  137.0 21.3 %collective-permute-done.4.rest_0_ = bf16[512,1024]{1,0:T(8,128)(2,1)} collective-permute-done((bf16[512,1024]{1,0:T(8,128)(2,1)}, bf16[512,1024]{1,0:T(8,128)(2,1)}, u32[]{:S(2)}, u32[]{:S(2)}) %collective-permute-start.4) | collective-permute-done | bytes 1048608 | tf_op jit(solution)/shard_map/ppermute | solution.py:20
  158.3 3.6 %collective-permute-start.5 = (bf16[512,1024]{1,0:T(8,128)(2,1)}, bf16[512,1024]{1,0:T(8,128)(2,1)S(1)}, u32[]{:S(2)}, u32[]{:S(2)}) collective-permute-start(bf16[512,1024]{1,0:T(8,128)(2,1)} %collective-permute-done.4.rest_0_), channel_id=1, source_target_pairs={{0,4},{1,5},{2,0},{3,1},{4,8},{5,9},{6,2},{7,3},{8,12},{9,13},{10,... | collective-permute-start | bytes 3145736 | tf_op jit(solution)/shard_map/ppermute | solution.py:20
  162.0 2.3 collective-permute-done.9.rest_2_
  164.3 1.5 collective-permute-start.10
  165.8 1.0 pad_maximum_fusion.down
  166.8 2.5 collective-permute-start.18
  169.3 19.2 %collective-permute-done.5.refs_0_.rest_0_ = bf16[512,1024]{1,0:T(8,128)(2,1)S(1)} collective-permute-done((bf16[512,1024]{1,0:T(8,128)(2,1)}, bf16[512,1024]{1,0:T(8,128)(2,1)S(1)}, u32[]{:S(2)}, u32[]{:S(2)}) %collective-permute-start.5) | collective-permute-done | bytes 1048608 | tf_op jit(solution)/shard_map/ppermute | solution.py:20
  189.5 1.2 collective-permute-done.10.refs_0_.rest_2_
  191.1 1.2 fusion.20
  192.9 14.5 %shard_map.221.refs_1_ = f32[256,384]{1,0:T(8,128)} custom-call(bf16[16,304,512]{2,1,0:T(8,128)(2,1)} %all-to-all-done.act.maps, bf16[16,304,512]{2,1,0:T(8,128)(2,1)} %all-to-all-done.act.maps, s32[16,1,192]{2,1,0:T(1,128)} %copy-done.12, s32[32,1]{1,0:T(8,128)} %copy.69.starts), custom_call_target="tpu_custom_call" | custom-call | flops 2415919104 | bytes 3145728 | tf_op jit(solution)/shard_map/pallas_call | solution.py:445
  207.4 1.2 fusion.45
  210.3 15.9 %all-to-all-start.1 = ((bf16[16,24,256]{2,1,0:T(8,128)(2,1)}), bf16[16,24,256]{2,1,0:T(8,128)(2,1)S(1)}, u32[]{:S(2)}, u32[]{:S(2)}) async-start(bf16[16,24,256]{2,1,0:T(8,128)(2,1)} %broadcast_in_dim.122), calls=%async_computation.1 | async-start | bytes 393216 | tf_op jit(solution)/shard_map/all_to_all | solution.py:31
  228.2 1.0 pad_maximum_fusion.2.cot
  229.2 5.3 %all-to-all-done.1 = bf16[16,24,256]{2,1,0:T(8,128)(2,1)S(1)} async-done(((bf16[16,24,256]{2,1,0:T(8,128)(2,1)}), bf16[16,24,256]{2,1,0:T(8,128)(2,1)S(1)}, u32[]{:S(2)}, u32[]{:S(2)}) %all-to-all-start.1) | async-done | bytes 196640 | tf_op jit(solution)/shard_map/all_to_all | solution.py:31
  235.3 12.3 %shard_map.223.refs_1_ = bf16[768,512]{1,0:T(8,128)(2,1)} custom-call(bf16[16,304,512]{2,1,0:T(8,128)(2,1)} %all-to-all-done.act.maps, bf16[256,384]{1,0:T(8,128)(2,1)} %bitcast.136, s32[16,1,192]{2,1,0:T(1,128)} %shard_map.222.rows, s32[32,1]{1,0:T(8,128)} %copy.69.starts), custom_call_target="tpu_custom_call" | custom-call | flops 2415919104 | bytes 3145728 | tf_op jit(solution)/shard_map/pallas_call | solution.py:446
  247.6 4.8 %shard_map.229.rest_4_ = bf16[384,8192]{1,0:T(8,128)(2,1)} custom-call(s32[2]{0:T(128)} %pad_add_fusion.4.where, bf16[384,1024]{1,0:T(8,128)(2,1)} %pad_maximum_fusion.2.cot, bf16[384,16]{1,0:T(8,128)(2,1)} %shard_map.224.grad, bf16[48,8192]{1,0:T(8,128)(2,1)} %pad_maximum_fusion.down, bf16[512,1024]{1,0:T(8,128)(2,1)} %rest_0_.1, ...), custom_call_target="tpu_custom_call" | custom-call | flops 805306368 | bytes 2883584 | tf_op jit(solution)/shard_map/pallas_call | solution.py:141
  252.4 7.1 %shard_map.230.rest_4_ = bf16[384,8192]{1,0:T(8,128)(2,1)} custom-call(s32[4]{0:T(128)} %pad_add_fusion.3.where, bf16[384,1024]{1,0:T(8,128)(2,1)} %pad_maximum_fusion.2.cot, bf16[384,16]{1,0:T(8,128)(2,1)} %shard_map.224.grad, bf16[48,8192]{1,0:T(8,128)(2,1)} %pad_maximum_fusion.down, ...), custom_call_target="tpu_custom_call", output_to_operand_aliasing={{}: (8, {})} | custom-call | flops 1610612736 | bytes 5767168 | tf_op jit(solution)/shard_map/pallas_call | solution.py:141
  259.4 7.1 %shard_map.231.rest_4_ = bf16[384,8192]{1,0:T(8,128)(2,1)} custom-call(s32[4]{0:T(128)} %pad_add_fusion.2.where, bf16[384,1024]{1,0:T(8,128)(2,1)} %pad_maximum_fusion.2.cot, bf16[384,16]{1,0:T(8,128)(2,1)} %shard_map.224.grad, bf16[48,8192]{1,0:T(8,128)(2,1)} %pad_maximum_fusion.down, bf16[512,1024]{1,0:T(8,128)(2,1)} %copy-done.3, ...), custom_call_target="tpu_custom_call", output_to_operand_aliasing={{}: (8, {})} | custom-call | flops 1610612736 | bytes 5767168 | tf_op jit(solution)/shard_map/pallas_call | solution.py:141
  266.9 1.1 collective-permute-start.11
  268.0 0.9 copy.72
  268.9 4.8 %all-to-all-start.3 = ((f32[16,24,256]{2,1,0:T(8,128)}), f32[16,24,256]{2,1,0:T(8,128)S(1)}, u32[]{:S(2)}, u32[]{:S(2)}) async-start(f32[16,24,256]{2,1,0:T(8,128)} %bitcast.132), calls=%async_computation.3 | async-start | bytes 786432 | tf_op jit(solution)/shard_map/all_to_all | solution.py:448
  273.7 16.9 %collective-permute-done.6.refs_0_.rest_0_ = bf16[512,1024]{1,0:T(8,128)(2,1)S(1)} collective-permute-done((bf16[512,1024]{1,0:T(8,128)(2,1)}, bf16[512,1024]{1,0:T(8,128)(2,1)S(1)}, u32[]{:S(2)}, u32[]{:S(2)}) %collective-permute-start.6) | collective-permute-done | bytes 1048608 | tf_op jit(solution)/shard_map/ppermute | solution.py:20
  290.6 2.9 collective-permute-start.14
  293.5 2.1 collective-permute-start.15
  297.6 1.9 all-to-all-done.3
  299.5 4.5 %all-to-all-start.2 = ((bf16[16,48,512]{2,1,0:T(8,128)(2,1)}), bf16[16,48,512]{2,1,0:T(8,128)(2,1)}, u32[]{:S(2)}, u32[]{:S(2)}) async-start(bf16[16,48,512]{2,1,0:T(8,128)(2,1)} %bitcast.54), calls=%async_computation.2 | async-start | bytes 1572864 | tf_op jit(solution)/shard_map/all_to_all | solution.py:451
  305.0 7.1 %shard_map.232.rest_4_ = bf16[384,8192]{1,0:T(8,128)(2,1)} custom-call(s32[4]{0:T(128)} %pad_add_fusion.1.where, bf16[384,1024]{1,0:T(8,128)(2,1)} %pad_maximum_fusion.2.cot, bf16[384,16]{1,0:T(8,128)(2,1)} %shard_map.224.grad, bf16[48,8192]{1,0:T(8,128)(2,1)} %pad_maximum_fusion.down, bf16[512,1024]{1,0:T(8,128)(2,1)} %copy-done.1, ...), custom_call_target="tpu_custom_call", output_to_operand_aliasing={{}: (8, {})} | custom-call | flops 1610612736 | bytes 5767168 | tf_op jit(solution)/shard_map/pallas_call | solution.py:141
  312.0 1.1 slice.168
  313.1 1.4 collective-permute-start.12
  314.5 1.1 slice.167
  316.0 1.9 select_add_fusion.1
  332.7 4.3 %collective-permute-start.22 = (f32[16,1024]{1,0:T(8,128)S(1)}, f32[16,1024]{1,0:T(8,128)S(1)}, u32[]{:S(2)}, u32[]{:S(2)}) collective-permute-start(f32[16,1024]{1,0:T(8,128)S(1)} %get-tuple-element.10), channel_id=1, source_target_pairs={{0,14},{1,15},{2,0},{3,1},{4,2},{5,3},{6,4},{7,5},{8,6},{9,7},{10,... | collective-permute-start | bytes 196616 | tf_op jit(solution)/shard_map/ppermute | solution.py:20
  337.0 1.1 collective-permute-start.23
  339.0 2.1 collective-permute-done.23
  341.1 1.7 collective-permute-done.24
  344.2 1.3 convert_bitcast_fusion
  345.6 0.9 copy.71
  346.5 1.4 reshape.263
  348.8 5.5 %shard_map.233 = bf16[384,8192]{1,0:T(8,128)(2,1)} custom-call(s32[4]{0:T(128)} %pad_add_fusion.where, bf16[384,1024]{1,0:T(8,128)(2,1)} %pad_maximum_fusion.2.cot, bf16[384,16]{1,0:T(8,128)(2,1)} %shard_map.224.grad, bf16[48,8192]{1,0:T(8,128)(2,1)} %pad_maximum_fusion.down, bf16[256,1024]{1,0:T(8,128)(2,1)} %copy-done.10, ...), custom_call_target="tpu_custom_call", output_to_operand_aliasing={{}: (8, {})} | custom-call | flops 805306368 | bytes 2883584 | tf_op jit(solution)/shard_map/pallas_call | solution.py:141
  (121 shorter events, 20.2 us)
Async XLA Ops:
  14.6 7.6 %copy-start.15 = (s32[32]{0:T(128)S(1)}, s32[32]{0:T(128)}, u32[]{:S(2)}) copy-start(s32[32]{0:T(128)} %param.24) | copy-start | bytes 388
  14.6 11.8 %copy-start.8 = (bf16[3,16,8192]{2,1,0:T(8,128)(2,1)S(1)}, bf16[3,16,8192]{2,1,0:T(8,128)(2,1)}, u32[]{:S(2)}) copy-start(bf16[3,16,8192]{2,1,0:T(8,128)(2,1)} %param.26) | copy-start | bytes 2359300
  14.6 176.5 %all-to-all-start = ((bf16[16,304,512]{2,1,0:T(8,128)(2,1)}), bf16[16,304,512]{2,1,0:T(8,128)(2,1)}, u32[]{:S(2)}, u32[]{:S(2)}) async-start(bf16[16,304,512]{2,1,0:T(8,128)(2,1)} %shard_map.220), calls=%async_computation | async-start | bytes 9961472 | tf_op jit(solution)/shard_map/all_to_all | solution.py:388
  22.0 4.4 %copy-start.13 = (bf16[3,16,1024]{2,1,0:T(8,128)(2,1)S(1)}, bf16[3,16,1024]{2,1,0:T(8,128)(2,1)}, u32[]{:S(2)}) copy-start(bf16[3,16,1024]{2,1,0:T(8,128)(2,1)} %param.27) | copy-start | bytes 294916
  22.1 14.6 %copy-start.16 = (s32[8]{0:T(128)S(1)}, s32[8]{0:T(128)}, u32[]{:S(2)}) copy-start(s32[8]{0:T(128)} %constant.262.clone) | copy-start | bytes 100
  22.1 19.8 %copy-start.14 = (s32[8]{0:T(128)S(1)}, s32[8]{0:T(128)}, u32[]{:S(2)}) copy-start(s32[8]{0:T(128)} %constant.261.clone) | copy-start | bytes 100
  26.5 86.5 %collective-permute-start = (bf16[16,9216]{1,0:T(8,128)(2,1)S(1)}, bf16[16,9216]{1,0:T(8,128)(2,1)S(1)}, u32[]{:S(2)}, u32[]{:S(2)}) collective-permute-start(bf16[16,9216]{1,0:T(8,128)(2,1)S(1)} %dynamic-slice_bitcast_fusion), channel_id=1, source_target_pairs={{0,4},{1,5},{2,6},{3,7},{4,8},{5,9},{6,10},{7,11},{8,12},{9,13},{1... | collective-permute-start | bytes 884744 | tf_op jit(solution)/shard_map/ppermute | solution.py:20
  28.0 108.9 %collective-permute-start.1 = (bf16[16,9216]{1,0:T(8,128)(2,1)S(1)}, bf16[16,9216]{1,0:T(8,128)(2,1)S(1)}, u32[]{:S(2)}, u32[]{:S(2)}) collective-permute-start(bf16[16,9216]{1,0:T(8,128)(2,1)S(1)} %dynamic-slice_bitcast_fusion), channel_id=1, source_target_pairs={{0,3},{1,4},{2,5},{3,6},{4,7},{5,8},{6,9},{7,10},{8,11},{9,12},{10... | collective-permute-start | bytes 884744 | tf_op jit(solution)/shard_map/ppermute | solution.py:20
  29.7 107.2 %collective-permute-start.2 = (bf16[16,9216]{1,0:T(8,128)(2,1)S(1)}, bf16[16,9216]{1,0:T(8,128)(2,1)S(1)}, u32[]{:S(2)}, u32[]{:S(2)}) collective-permute-start(bf16[16,9216]{1,0:T(8,128)(2,1)S(1)} %dynamic-slice_bitcast_fusion), channel_id=1, source_target_pairs={{0,2},{1,3},{2,4},{3,5},{4,6},{5,7},{6,8},{7,9},{8,10},{9,11},{10,... | collective-permute-start | bytes 884744 | tf_op jit(solution)/shard_map/ppermute | solution.py:20
  30.9 106.1 %collective-permute-start.3 = (bf16[16,9216]{1,0:T(8,128)(2,1)S(1)}, bf16[16,9216]{1,0:T(8,128)(2,1)S(1)}, u32[]{:S(2)}, u32[]{:S(2)}) collective-permute-start(bf16[16,9216]{1,0:T(8,128)(2,1)S(1)} %dynamic-slice_bitcast_fusion), channel_id=1, source_target_pairs={{0,1},{1,2},{2,3},{3,4},{4,5},{5,6},{6,7},{7,8},{8,9},{9,10},{10,1... | collective-permute-start | bytes 884744 | tf_op jit(solution)/shard_map/ppermute | solution.py:20
  32.1 215.5 %collective-permute-start.20 = (bf16[512,1024]{1,0:T(8,128)(2,1)}, bf16[512,1024]{1,0:T(8,128)(2,1)}, u32[]{:S(2)}, u32[]{:S(2)}) collective-permute-start(bf16[512,1024]{1,0:T(8,128)(2,1)} %rest_0_.1), channel_id=1, source_target_pairs={{0,1},{1,0},{2,3},{3,2},{4,5},{5,4},{6,7},{7,6},{8,9},{9,8},{10,11... | collective-permute-start | bytes 3145736 | tf_op jit(solution)/shard_map/ppermute | solution.py:20
  113.0 45.3 %collective-permute-start.4 = (bf16[512,1024]{1,0:T(8,128)(2,1)}, bf16[512,1024]{1,0:T(8,128)(2,1)}, u32[]{:S(2)}, u32[]{:S(2)}) collective-permute-start(bf16[512,1024]{1,0:T(8,128)(2,1)} %rest_0_.1), channel_id=1, source_target_pairs={{0,4},{1,5},{2,0},{3,1},{4,8},{5,9},{6,2},{7,3},{8,12},{9,13},{10,... | collective-permute-start | bytes 3145736 | tf_op jit(solution)/shard_map/ppermute | solution.py:20
  136.9 27.4 %collective-permute-start.9 = (bf16[512,1024]{1,0:T(8,128)(2,1)}, bf16[512,1024]{1,0:T(8,128)(2,1)}, u32[]{:S(2)}, u32[]{:S(2)}) collective-permute-start(bf16[512,1024]{1,0:T(8,128)(2,1)} %rest_0_.1), channel_id=1, source_target_pairs={{0,2},{1,3},{2,6},{3,7},{4,0},{5,1},{6,10},{7,11},{8,4},{9,5},{10,... | collective-permute-start | bytes 3145736 | tf_op jit(solution)/shard_map/ppermute | solution.py:20
  158.3 30.2 %collective-permute-start.5 = (bf16[512,1024]{1,0:T(8,128)(2,1)}, bf16[512,1024]{1,0:T(8,128)(2,1)S(1)}, u32[]{:S(2)}, u32[]{:S(2)}) collective-permute-start(bf16[512,1024]{1,0:T(8,128)(2,1)} %collective-permute-done.4.rest_0_), channel_id=1, source_target_pairs={{0,4},{1,5},{2,0},{3,1},{4,8},{5,9},{6,2},{7,3},{8,12},{9,13},{10,... | collective-permute-start | bytes 3145736 | tf_op jit(solution)/shard_map/ppermute | solution.py:20
  164.3 26.4 %collective-permute-start.10 = (bf16[512,1024]{1,0:T(8,128)(2,1)}, bf16[512,1024]{1,0:T(8,128)(2,1)}, u32[]{:S(2)}, u32[]{:S(2)}) collective-permute-start(bf16[512,1024]{1,0:T(8,128)(2,1)} %collective-permute-done.9.rest_2_), channel_id=1, source_target_pairs={{0,2},{1,3},{2,6},{3,7},{4,0},{5,1},{6,10},{7,11},{8,4},{9,5},{10,... | collective-permute-start | bytes 3145736 | tf_op jit(solution)/shard_map/ppermute | solution.py:20
  166.8 85.6 %collective-permute-start.18 = (bf16[512,1024]{1,0:T(8,128)(2,1)}, bf16[512,1024]{1,0:T(8,128)(2,1)}, u32[]{:S(2)}, u32[]{:S(2)}) collective-permute-start(bf16[512,1024]{1,0:T(8,128)(2,1)} %collective-permute-done.4.rest_0_), channel_id=1, source_target_pairs={{0,1},{1,0},{2,3},{3,2},{4,5},{5,4},{6,7},{7,6},{8,9},{9,8},{10,11... | collective-permute-start | bytes 3145736 | tf_op jit(solution)/shard_map/ppermute | solution.py:20
  169.3 83.0 %collective-permute-start.19 = (bf16[512,1024]{1,0:T(8,128)(2,1)}, bf16[512,1024]{1,0:T(8,128)(2,1)}, u32[]{:S(2)}, u32[]{:S(2)}) collective-permute-start(bf16[512,1024]{1,0:T(8,128)(2,1)} %collective-permute-done.9.rest_2_), channel_id=1, source_target_pairs={{0,1},{1,0},{2,3},{3,2},{4,5},{5,4},{6,7},{7,6},{8,9},{9,8},{10,11... | collective-permute-start | bytes 3145736 | tf_op jit(solution)/shard_map/ppermute | solution.py:20
  188.5 18.9 %copy-start.3 = (bf16[512,1024]{1,0:T(8,128)(2,1)}, bf16[512,1024]{1,0:T(8,128)(2,1)S(1)}, u32[]{:S(2)}) copy-start(bf16[512,1024]{1,0:T(8,128)(2,1)S(1)} %collective-permute-done.5.refs_0_.rest_0_) | copy-start | bytes 3145732
  188.5 70.9 %collective-permute-start.16 = (bf16[512,1024]{1,0:T(8,128)(2,1)S(1)}, bf16[512,1024]{1,0:T(8,128)(2,1)}, u32[]{:S(2)}, u32[]{:S(2)}) collective-permute-start(bf16[512,1024]{1,0:T(8,128)(2,1)S(1)} %collective-permute-done.5.refs_0_.rest_0_), channel_id=1, source_target_pairs={{0,1},{1,0},{2,3},{3,2},{4,5},{5,4},{6,7},{7,6},{8,9},{9,8},{10,11... | collective-permute-start | bytes 3145736 | tf_op jit(solution)/shard_map/ppermute | solution.py:20
  190.7 68.8 %collective-permute-start.17 = (bf16[512,1024]{1,0:T(8,128)(2,1)}, bf16[512,1024]{1,0:T(8,128)(2,1)}, u32[]{:S(2)}, u32[]{:S(2)}) collective-permute-start(bf16[512,1024]{1,0:T(8,128)(2,1)} %collective-permute-done.10.refs_0_.rest_2_), channel_id=1, source_target_pairs={{0,1},{1,0},{2,3},{3,2},{4,5},{5,4},{6,7},{7,6},{8,9},{9,8},{10,11... | collective-permute-start | bytes 3145736 | tf_op jit(solution)/shard_map/ppermute | solution.py:20
  192.2 0.7 copy-start.12
  208.6 18.6 %copy-start.4 = (bf16[16,24,512]{2,1,0:T(8,128)(2,1)}, bf16[16,24,512]{2,1,0:T(8,128)(2,1)S(1)}, u32[]{:S(2)}) copy-start(bf16[16,24,512]{2,1,0:T(8,128)(2,1)S(1)} %get-tuple-element.23) | copy-start | bytes 1179652
  208.6 19.1 %copy-start.6 = (bf16[16,24,512]{2,1,0:T(8,128)(2,1)}, bf16[16,24,512]{2,1,0:T(8,128)(2,1)S(1)}, u32[]{:S(2)}) copy-start(bf16[16,24,512]{2,1,0:T(8,128)(2,1)S(1)} %get-tuple-element.24) | copy-start | bytes 1179652
  210.3 24.2 %all-to-all-start.1 = ((bf16[16,24,256]{2,1,0:T(8,128)(2,1)}), bf16[16,24,256]{2,1,0:T(8,128)(2,1)S(1)}, u32[]{:S(2)}, u32[]{:S(2)}) async-start(bf16[16,24,256]{2,1,0:T(8,128)(2,1)} %broadcast_in_dim.122), calls=%async_computation.1 | async-start | bytes 393216 | tf_op jit(solution)/shard_map/all_to_all | solution.py:31
  266.5 1.5 copy-start
  266.5 24.1 %collective-permute-start.6 = (bf16[512,1024]{1,0:T(8,128)(2,1)}, bf16[512,1024]{1,0:T(8,128)(2,1)S(1)}, u32[]{:S(2)}, u32[]{:S(2)}) collective-permute-start(bf16[512,1024]{1,0:T(8,128)(2,1)} %shard_map.225), channel_id=1, source_target_pairs={{0,4},{1,5},{2,0},{3,1},{4,8},{5,9},{6,2},{7,3},{8,12},{9,13},{10,... | collective-permute-start | bytes 3145736 | tf_op jit(solution)/shard_map/ppermute | solution.py:20
  266.9 26.6 %collective-permute-start.11 = (bf16[512,1024]{1,0:T(8,128)(2,1)}, bf16[512,1024]{1,0:T(8,128)(2,1)S(1)}, u32[]{:S(2)}, u32[]{:S(2)}) collective-permute-start(bf16[512,1024]{1,0:T(8,128)(2,1)} %shard_map.227), channel_id=1, source_target_pairs={{0,2},{1,3},{2,6},{3,7},{4,0},{5,1},{6,10},{7,11},{8,4},{9,5},{10,... | collective-permute-start | bytes 3145736 | tf_op jit(solution)/shard_map/ppermute | solution.py:20
  268.9 35.6 %copy-start.7 = (bf16[16,24,512]{2,1,0:T(8,128)(2,1)S(1)}, bf16[16,24,512]{2,1,0:T(8,128)(2,1)}, u32[]{:S(2)}) copy-start(bf16[16,24,512]{2,1,0:T(8,128)(2,1)} %copy-done.6) | copy-start | bytes 1179652
  268.9 30.6 %all-to-all-start.3 = ((f32[16,24,256]{2,1,0:T(8,128)}), f32[16,24,256]{2,1,0:T(8,128)S(1)}, u32[]{:S(2)}, u32[]{:S(2)}) async-start(f32[16,24,256]{2,1,0:T(8,128)} %bitcast.132), calls=%async_computation.3 | async-start | bytes 786432 | tf_op jit(solution)/shard_map/all_to_all | solution.py:448
  273.7 31.0 %copy-start.5 = (bf16[16,24,512]{2,1,0:T(8,128)(2,1)S(1)}, bf16[16,24,512]{2,1,0:T(8,128)(2,1)}, u32[]{:S(2)}) copy-start(bf16[16,24,512]{2,1,0:T(8,128)(2,1)} %copy-done.4) | copy-start | bytes 1179652
  290.6 14.3 %copy-start.1 = (bf16[512,1024]{1,0:T(8,128)(2,1)}, bf16[512,1024]{1,0:T(8,128)(2,1)S(1)}, u32[]{:S(2)}) copy-start(bf16[512,1024]{1,0:T(8,128)(2,1)S(1)} %collective-permute-done.6.refs_0_.rest_0_) | copy-start | bytes 3145732
  290.6 14.3 %collective-permute-start.14 = (bf16[512,1024]{1,0:T(8,128)(2,1)S(1)}, bf16[512,1024]{1,0:T(8,128)(2,1)}, u32[]{:S(2)}, u32[]{:S(2)}) collective-permute-start(bf16[512,1024]{1,0:T(8,128)(2,1)S(1)} %collective-permute-done.6.refs_0_.rest_0_), channel_id=1, source_target_pairs={{0,1},{1,0},{2,3},{3,2},{4,5},{5,4},{6,7},{7,6},{8,9},{9,8},{10,11... | collective-permute-start | bytes 3145736 | tf_op jit(solution)/shard_map/ppermute | solution.py:20
  293.5 11.4 %copy-start.2 = (bf16[512,1024]{1,0:T(8,128)(2,1)}, bf16[512,1024]{1,0:T(8,128)(2,1)S(1)}, u32[]{:S(2)}) copy-start(bf16[512,1024]{1,0:T(8,128)(2,1)S(1)} %collective-permute-done.11.refs_0_.rest_2_) | copy-start | bytes 3145732
  293.5 11.4 %collective-permute-start.15 = (bf16[512,1024]{1,0:T(8,128)(2,1)S(1)}, bf16[512,1024]{1,0:T(8,128)(2,1)}, u32[]{:S(2)}, u32[]{:S(2)}) collective-permute-start(bf16[512,1024]{1,0:T(8,128)(2,1)S(1)} %collective-permute-done.11.refs_0_.rest_2_), channel_id=1, source_target_pairs={{0,1},{1,0},{2,3},{3,2},{4,5},{5,4},{6,7},{7,6},{8,9},{9,8},{10,11... | collective-permute-start | bytes 3145736 | tf_op jit(solution)/shard_map/ppermute | solution.py:20
  299.5 44.7 %all-to-all-start.2 = ((bf16[16,48,512]{2,1,0:T(8,128)(2,1)}), bf16[16,48,512]{2,1,0:T(8,128)(2,1)}, u32[]{:S(2)}, u32[]{:S(2)}) async-start(bf16[16,48,512]{2,1,0:T(8,128)(2,1)} %bitcast.54), calls=%async_computation.2 | async-start | bytes 1572864 | tf_op jit(solution)/shard_map/all_to_all | solution.py:451
  313.1 29.8 %collective-permute-start.12 = (bf16[256,1024]{1,0:T(8,128)(2,1)S(1)}, bf16[256,1024]{1,0:T(8,128)(2,1)S(1)}, u32[]{:S(2)}, u32[]{:S(2)}) collective-permute-start(bf16[256,1024]{1,0:T(8,128)(2,1)S(1)} %slice.168), channel_id=1, source_target_pairs={{0,2},{1,3},{2,6},{3,7},{4,0},{5,1},{6,10},{7,11},{8,4},{9,5},{10,... | collective-permute-start | bytes 1572872 | tf_op jit(solution)/shard_map/ppermute | solution.py:20
  315.6 27.8 %collective-permute-start.7 = (bf16[256,1024]{1,0:T(8,128)(2,1)S(1)}, bf16[256,1024]{1,0:T(8,128)(2,1)S(1)}, u32[]{:S(2)}, u32[]{:S(2)}) collective-permute-start(bf16[256,1024]{1,0:T(8,128)(2,1)S(1)} %slice.167), channel_id=1, source_target_pairs={{0,4},{1,5},{2,0},{3,1},{4,8},{5,9},{6,2},{7,3},{8,12},{9,13},{10,... | collective-permute-start | bytes 1572872 | tf_op jit(solution)/shard_map/ppermute | solution.py:20
  317.9 20.2 %collective-permute-start.21 = (f32[16,1024]{1,0:T(8,128)S(1)}, f32[16,1024]{1,0:T(8,128)S(1)}, u32[]{:S(2)}, u32[]{:S(2)}) collective-permute-start(f32[16,1024]{1,0:T(8,128)S(1)} %get-tuple-element.10), channel_id=1, source_target_pairs={{0,15},{1,0},{2,1},{3,2},{4,3},{5,4},{6,5},{7,6},{8,7},{9,8},{10,9... | collective-permute-start | bytes 196616 | tf_op jit(solution)/shard_map/ppermute | solution.py:20
  332.7 6.4 %collective-permute-start.22 = (f32[16,1024]{1,0:T(8,128)S(1)}, f32[16,1024]{1,0:T(8,128)S(1)}, u32[]{:S(2)}, u32[]{:S(2)}) collective-permute-start(f32[16,1024]{1,0:T(8,128)S(1)} %get-tuple-element.10), channel_id=1, source_target_pairs={{0,14},{1,15},{2,0},{3,1},{4,2},{5,3},{6,4},{7,5},{8,6},{9,7},{10,... | collective-permute-start | bytes 196616 | tf_op jit(solution)/shard_map/ppermute | solution.py:20
  337.0 4.1 %collective-permute-start.23 = (f32[16,1024]{1,0:T(8,128)S(1)}, f32[16,1024]{1,0:T(8,128)S(1)}, u32[]{:S(2)}, u32[]{:S(2)}) collective-permute-start(f32[16,1024]{1,0:T(8,128)S(1)} %get-tuple-element.10), channel_id=1, source_target_pairs={{0,13},{1,14},{2,15},{3,0},{4,1},{5,2},{6,3},{7,4},{8,5},{9,6},{10... | collective-permute-start | bytes 196616 | tf_op jit(solution)/shard_map/ppermute | solution.py:20
  338.1 4.7 %collective-permute-start.24 = (f32[16,1024]{1,0:T(8,128)S(1)}, f32[16,1024]{1,0:T(8,128)S(1)}, u32[]{:S(2)}, u32[]{:S(2)}) collective-permute-start(f32[16,1024]{1,0:T(8,128)S(1)} %get-tuple-element.10), channel_id=1, source_target_pairs={{0,12},{1,13},{2,14},{3,15},{4,0},{5,1},{6,2},{7,3},{8,4},{9,5},{1... | collective-permute-start | bytes 196616 | tf_op jit(solution)/shard_map/ppermute | solution.py:20
  342.9 2.7 copy-start.9
  342.9 5.1 %collective-permute-start.13 = (bf16[256,1024]{1,0:T(8,128)(2,1)S(1)}, bf16[256,1024]{1,0:T(8,128)(2,1)S(1)}, u32[]{:S(2)}, u32[]{:S(2)}) collective-permute-start(bf16[256,1024]{1,0:T(8,128)(2,1)S(1)} %collective-permute-done.12.rest_2_), channel_id=1, source_target_pairs={{0,1},{1,0},{2,3},{3,2},{4,5},{5,4},{6,7},{7,6},{8,9},{9,8},{10,11... | collective-permute-start | bytes 1572872 | tf_op jit(solution)/shard_map/ppermute | solution.py:20
  343.4 2.2 copy-start.10
  343.4 4.6 %collective-permute-start.8 = (bf16[256,1024]{1,0:T(8,128)(2,1)S(1)}, bf16[256,1024]{1,0:T(8,128)(2,1)}, u32[]{:S(2)}, u32[]{:S(2)}) collective-permute-start(bf16[256,1024]{1,0:T(8,128)(2,1)S(1)} %collective-permute-done.7.rest_0_), channel_id=1, source_target_pairs={{0,1},{1,0},{2,3},{3,2},{4,5},{5,4},{6,7},{7,6},{8,9},{9,8},{10,11... | collective-permute-start | bytes 1572872 | tf_op jit(solution)/shard_map/ppermute | solution.py:20
  348.0 0.8 copy-start.11

commit v6 on v5

v6 whole, which is shorter than its diff:
```python
import jax
import jax.numpy as jnp
from jax import lax
from jax.experimental import pallas as pl
from jax.experimental.pallas import tpu as pltpu
from jax.sharding import PartitionSpec as P

BLOCK = 128
HOPS = 4
LANES = 128
DIGIT = 64
VMEM = 56 << 20

adapter_scale = 2.0


def moved(value, steps):
    count = lax.axis_size("blk")
    return lax.ppermute(value, "blk", [(i, (i + steps) % count) for i in range(count)])


def to_all(value):
    count = lax.axis_size("blk")
    copies = jnp.broadcast_to(value[None], (count,) + value.shape)
    return lax.all_to_all(copies, "blk", split_axis=0, concat_axis=0)


def after(value, *others):
    anywhere = pl.BlockSpec(memory_space=pl.ANY)
    return pl.pallas_call(
        lambda *refs: None,
        in_specs=[anywhere] * (1 + len(others)),
        out_specs=anywhere,
        out_shape=jax.ShapeDtypeStruct(value.shape, value.dtype),
        input_output_aliases={0: 0},
        cost_estimate=pl.CostEstimate(flops=0, bytes_accessed=0, transcendentals=0),
    )(value, *others)


def dot(a, b, dims):
    return lax.dot_general(a, b, (dims, ((), ())), preferred_element_type=jnp.float32)


def starts_of(blocks, start_ids):
    latest = jnp.max(
        jnp.where(start_ids[None, :] <= blocks[:, None], start_ids[None, :], -1), axis=1
    )
    return jnp.where(latest >= 0, latest, jnp.max(start_ids))


def as_digits(rows, places):
    return (
        rows % DIGIT,
        rows // DIGIT % DIGIT,
        rows // (DIGIT * DIGIT),
        places % DIGIT,
        places // DIGIT,
    )


def from_digits(digits):
    low, middle, high, place, place_high = [digits[:, k].astype(jnp.int32) for k in range(5)]
    return (high * DIGIT + middle) * DIGIT + low, place_high * DIGIT + place


def pack_kernel(rows, act, maps, cot, out, place, digits):
    tokens, features = act.shape
    shared = maps.shape[0]
    cap = shared * features // cot.shape[1]
    devices = pl.num_programs(0)
    step = pl.program_id(0)

    @pl.when(step == 0)
    def _():
        target = rows[...] // (cap * devices)
        to = lax.broadcasted_iota(jnp.int32, (16, features), 0) == target
        first = lax.broadcasted_iota(jnp.int32, (features, features), 0)
        later = lax.broadcasted_iota(jnp.int32, (features, features), 1)
        earlier = jnp.where(first < later, 1.0, 0.0).astype(jnp.bfloat16)
        ahead = dot(jnp.where(to, 1.0, 0.0).astype(jnp.bfloat16), earlier, ((1,), (0,)))
        ahead = jnp.sum(jnp.where(to, ahead, 0.0), axis=0, keepdims=True)
        place[...] = target * cap + ahead.astype(jnp.int32)
        which = lax.broadcasted_iota(jnp.int32, (16, features), 0)
        values = jnp.zeros((16, features), jnp.int32)
        for k, digit in enumerate(as_digits(rows[...], place[...])):
            values = jnp.where(which == k, digit, values)
        digits[...] = values.astype(jnp.float32).astype(out.dtype)

    index = lax.broadcasted_iota(jnp.int32, (cap, tokens), 0) + step * cap
    send = jnp.where(index == place[:, :tokens], 1.0, 0.0).astype(jnp.bfloat16)
    sent = [
        dot(send, cot[:, k : k + features], ((1,), (0,)))
        for k in range(0, cot.shape[1], features)
    ]
    out[0, :tokens, :] = act[...]
    out[0, tokens : tokens + shared, :] = maps[...]
    out[0, tokens + shared : tokens + 2 * shared, :] = jnp.concatenate(sent, axis=0).astype(
        out.dtype
    )
    out[0, tokens + 2 * shared :, :] = digits[...]


def pack(rows, act, maps, cot, devices, cap):
    tokens, width = act.shape
    features = width // devices
    shared = maps.shape[0]
    total = tokens + 2 * shared + 16
    if features % LANES == 0 and cap % 8 == 0 and features >= tokens and devices <= 16:
        padding = jnp.full((features - tokens,), 16 * cap * devices, jnp.int32)
        return pl.pallas_call(
            pack_kernel,
            grid=(devices,),
            in_specs=[
                pl.BlockSpec((1, features), lambda j: (0, 0)),
                pl.BlockSpec((tokens, features), lambda j: (0, j)),
                pl.BlockSpec((shared, features), lambda j: (0, j)),
                pl.BlockSpec(cot.shape, lambda j: (0, 0)),
            ],
            out_specs=pl.BlockSpec((1, total, features), lambda j: (j, 0, 0)),
            out_shape=jax.ShapeDtypeStruct((devices, total, features), act.dtype),
            scratch_shapes=[
                pltpu.VMEM((1, features), jnp.int32),
                pltpu.VMEM((16, features), act.dtype),
            ],
            cost_estimate=pl.CostEstimate(
                flops=2 * devices * cap * tokens * cot.shape[1],
                bytes_accessed=4 * devices * total * features,
                transcendentals=0,
            ),
            compiler_params=pltpu.CompilerParams(vmem_limit_bytes=VMEM),
        )(jnp.concatenate([rows, padding])[None], act, maps, cot)
    target = rows // (cap * devices)
    order = jnp.arange(tokens, dtype=jnp.int32)
    before = (target[:, None] == target[None, :]) & (order[None, :] < order[:, None])
    place = target * cap + jnp.sum(before.astype(jnp.int32), axis=1)
    send = jnp.arange(cap * devices, dtype=jnp.int32)[:, None] == place[None, :]
    sent = dot(send.astype(jnp.bfloat16), cot, ((1,), (0,))).astype(jnp.bfloat16)
    sent = sent.reshape(devices, cap, cot.shape[1])
    digits = jnp.stack(as_digits(rows, place)).astype(jnp.bfloat16)
    digits = jnp.pad(digits, ((0, 0), (0, -tokens % features))).reshape(-1, features)
    digits = jnp.pad(digits, ((0, -digits.shape[0] % 16), (0, 0)))
    parts = [
        act.reshape(tokens, devices, features).transpose(1, 0, 2),
        maps.reshape(shared, devices, features).transpose(1, 0, 2),
    ]
    parts += [sent[:, :, k : k + features] for k in range(0, cot.shape[1], features)]
    parts += [jnp.broadcast_to(digits[None], (devices,) + digits.shape)]
    return jnp.concatenate(parts, axis=1)


def slot_chunks(width):
    size = min(width, 768)
    while width % size:
        size //= 2
    return [slice(k, k + size) for k in range(0, width, size)]


def slot_of(rows, starts):
    blocks = rows // BLOCK
    latest = jnp.max(jnp.where(starts <= blocks, starts, -1), axis=0, keepdims=True)
    return jnp.where(latest >= 0, latest, jnp.max(starts))


def own_rows(slot, first, size, rank):
    index = first // rank + lax.broadcasted_iota(jnp.int32, (size // rank, rank, 1), 0)
    return index == slot[None]


def placing(place, places):
    hit = lax.broadcasted_iota(jnp.int32, (places, place.shape[1]), 0) == place
    return jnp.where(hit, 1.0, 0.0).astype(jnp.bfloat16)


def hidden_kernel(act, maps, rows, spots, starts, out):
    sources, _, tokens = rows.shape
    rank, places = out.shape[0] // sources, out.shape[1]
    share = maps.shape[1]
    for k in range(sources):
        slot = slot_of(rows[k], starts[...])
        total = jnp.zeros((rank, tokens), jnp.float32)
        for part in slot_chunks(maps.shape[0] * share):
            size = part.stop - part.start
            some = maps[part.start // share : part.stop // share].reshape(size, -1)
            each = dot(some, act[k, :tokens, :], ((1,), (1,))).reshape(size // rank, rank, -1)
            total += jnp.sum(
                jnp.where(own_rows(slot, part.start, size, rank), each, 0.0), axis=0
            )
        high = total.astype(jnp.bfloat16)
        low = (total - high.astype(jnp.float32)).astype(jnp.bfloat16)
        place = placing(spots[k], places)
        out[k * rank : (k + 1) * rank, :] = dot(high, place, ((1,), (1,))) + dot(
            low, place, ((1,), (1,))
        )


def down_kernel(act, grad, rows, spots, starts, out, total):
    sources, _, tokens = rows.shape
    rank, places = grad.shape[0] // sources, grad.shape[1]
    step = pl.program_id(0)

    @pl.when(step == 0)
    def _():
        total[...] = jnp.zeros_like(total)

    for k in range(sources):
        slot = slot_of(rows[k], starts[...])
        place = placing(spots[k], places)
        wide = dot(grad[k * rank : (k + 1) * rank, :], place, ((1,), (0,)))[None]
        for part in slot_chunks(total.shape[0]):
            size = part.stop - part.start
            placed = jnp.where(own_rows(slot, part.start, size, rank), wide, 0.0)
            placed = placed.reshape(size, -1).astype(jnp.bfloat16)
            total[part, :] += dot(placed, act[k, :tokens, :], ((1,), (0,)))

    @pl.when(step == pl.num_programs(0) - 1)
    def _():
        out[...] = (adapter_scale * total[...]).astype(out.dtype)


def feature_calls(received, tokens, share, rank, places, starts):
    devices, packed, features = received.shape
    width = devices * share
    sources = 2
    grid = (devices // sources,)
    act = pl.BlockSpec((sources, packed, features), lambda j: (j, 0, 0))
    maps = pl.BlockSpec((devices, share, features), lambda j: (0, tokens // share, 0))
    rows = pl.BlockSpec((sources, 1, tokens), lambda j: (j, 0, 0))
    begin = pl.BlockSpec((starts, 1), lambda j: (0, 0))
    placed = pl.BlockSpec((sources * rank, places), lambda j: (j, 0))
    cost = pl.CostEstimate(
        flops=2 * devices * tokens * width * features,
        bytes_accessed=2 * devices * tokens * features,
        transcendentals=0,
    )
    params = pltpu.CompilerParams(vmem_limit_bytes=VMEM)
    hidden = pl.pallas_call(
        hidden_kernel,
        grid=grid,
        in_specs=[act, maps, rows, rows, begin],
        out_specs=placed,
        out_shape=jax.ShapeDtypeStruct((devices * rank, places), jnp.float32),
        cost_estimate=cost,
        compiler_params=params,
    )
    down = pl.pallas_call(
        down_kernel,
        grid=grid,
        in_specs=[act, placed, rows, rows, begin],
        out_specs=pl.BlockSpec((width, features), lambda j: (0, 0)),
        out_shape=jax.ShapeDtypeStruct((width, features), jnp.bfloat16),
        scratch_shapes=[pltpu.VMEM((width, features), jnp.float32)],
        cost_estimate=cost,
        compiler_params=params,
    )
    return hidden, down


def local(
    activations,
    cotangent,
    token_layout_row,
    tenant_first_row,
    frozen_value_weight,
    adapter_down_maps,
    adapter_up_maps,
):
    devices = lax.axis_size("blk")
    device = lax.axis_index("blk")
    tokens = activations.shape[0]
    resident, rank, width = adapter_down_maps.shape
    out_width = cotangent.shape[1]
    features = width // devices
    share = resident * rank
    resident_rows = resident * BLOCK
    cap = resident_rows // devices
    start_ids = tenant_first_row // BLOCK

    weight = lax.all_gather(frozen_value_weight, "blk", axis=0, tiled=True)

    flat_maps = adapter_down_maps.reshape(share, width)
    packed = pack(token_layout_row, activations, flat_maps, cotangent, devices, cap)
    received = lax.all_to_all(packed, "blk", split_axis=0, concat_axis=0)
    recv_cot = [
        received[:, tokens + share + k * cap : tokens + share + (k + 1) * cap].reshape(
            resident_rows, features
        )
        for k in range(out_width // features)
    ]
    per_digit = -(-tokens // features)
    digits = received[:, tokens + 2 * share : tokens + 2 * share + 5 * per_digit]
    digits = digits.reshape(devices, 5, per_digit * features)[:, :, :tokens]
    rows_all, place_all = from_digits(digits)

    first_block = device * resident
    block_numbers = first_block + jnp.arange(resident, dtype=jnp.int32)
    begin = starts_of(block_numbers, start_ids)
    is_local = (begin >= first_block) & (begin <= block_numbers)
    home_slot = jnp.clip(begin - first_block, 0, resident - 1)
    both_maps = jnp.concatenate([adapter_down_maps, adapter_up_maps], axis=2)
    last_map = lax.dynamic_index_in_dim(both_maps, home_slot[resident - 1], 0, keepdims=False)
    carried = jnp.zeros_like(last_map)
    for step in range(1, HOPS + 1):
        home = (device - step) % devices
        carried = jnp.where(begin[0] // resident == home, moved(last_map, step), carried)
    block_maps = []
    for b in range(resident):
        own = carried
        for k in range(b + 1):
            own = jnp.where(is_local[b] & (home_slot[b] == k), both_maps[k], own)
        block_maps.append(own)
    block_maps = jnp.concatenate(block_maps, axis=0)
    down_blocks, up_blocks = block_maps[:, :width], block_maps[:, width:]

    spots = device * cap + jnp.arange(cap, dtype=jnp.int32)
    hit = place_all[:, None, :] == spots[None, :, None]
    row_in = rows_all - device * resident_rows + 1
    row_in = jnp.sum(jnp.where(hit, row_in[:, None, :], 0), axis=2).reshape(-1) - 1
    arrange = row_in[:, None] == jnp.arange(resident_rows, dtype=jnp.int32)[None, :]
    arrange = arrange.astype(jnp.bfloat16)
    in_block = row_in[:, None] // BLOCK == jnp.arange(share, dtype=jnp.int32)[None, :] // rank

    grad_in = sum(
        dot(part, up_blocks[:, k * features : (k + 1) * features], ((1,), (1,)))
        for k, part in enumerate(recv_cot)
    )
    grad_in = jnp.where(in_block, grad_in, 0.0).astype(jnp.bfloat16)
    grad_in = sum(grad_in[:, b * rank : (b + 1) * rank] for b in range(resident))
    grad_sent = grad_in.reshape(devices, cap, rank).transpose(1, 0, 2).reshape(cap, -1)
    grad_all = to_all(grad_sent).reshape(resident_rows, -1).T

    starts = start_ids[:, None]
    hidden_call, down_call = feature_calls(
        received, tokens, share, rank, resident_rows, starts.shape[0]
    )
    rows_all = rows_all[:, None, :]
    place_all = place_all[:, None, :]
    shares = hidden_call(received, received, rows_all, place_all, starts)
    rows_all = after(rows_all, shares)
    down_f = down_call(received, grad_all, rows_all, place_all, starts)
    hidden = shares.T.reshape(devices, cap, -1)
    hidden = lax.all_to_all(hidden, "blk", split_axis=0, concat_axis=0)
    hidden = jnp.sum(hidden, axis=0).astype(jnp.bfloat16)
    hidden = hidden.reshape(cap, devices, rank).transpose(1, 0, 2).reshape(-1, rank)
    down_home = lax.all_to_all(down_f, "blk", split_axis=0, concat_axis=1, tiled=True)
    down_map_gradient = down_home.astype(jnp.float32).reshape(resident, rank, width)

    cot_rows = jnp.concatenate(
        [dot(arrange, part, ((0,), (0,))).astype(jnp.bfloat16) for part in recv_cot], axis=1
    )
    grad_rows = dot(arrange, grad_in, ((0,), (0,))).astype(jnp.bfloat16)
    lora = [
        dot(
            grad_rows[b * BLOCK : (b + 1) * BLOCK],
            down_blocks[b * rank : (b + 1) * rank],
            ((1,), (0,)),
        )
        for b in range(resident)
    ]
    lora = (adapter_scale * jnp.concatenate(lora, axis=0)).astype(jnp.bfloat16)
    wide = jnp.where(in_block, jnp.concatenate([hidden] * resident, axis=1), 0)
    up_all = [dot(wide, part, ((0,), (0,))) for part in recv_cot]
    up_all = jnp.concatenate(up_all, axis=1).reshape(resident, rank, out_width)
    up_parts = [up_all[b] for b in range(resident)]

    tail = sum(jnp.where(is_local[b], 0.0, up_parts[b]) for b in range(resident))
    far = jnp.zeros_like(tail)
    for step in range(1, HOPS + 1):
        other = (device + step) % devices * resident
        theirs = starts_of(other[None], start_ids)[0]
        far = far + jnp.where(theirs // resident == device, moved(tail, -step), 0.0)
    up_grads = []
    for k in range(resident):
        total = jnp.where(begin[resident - 1] == first_block + k, far, 0.0)
        for b in range(resident):
            total = total + jnp.where(is_local[b] & (home_slot[b] == k), up_parts[b], 0.0)
        up_grads.append(adapter_scale * total)
    up_map_gradient = jnp.stack(up_grads)

    out = dot(cot_rows, weight, ((1,), (1,))) + lora.astype(jnp.float32)
    out = out.astype(jnp.bfloat16)
    return (out, down_map_gradient, up_map_gradient)


def solution(mesh):
    return jax.shard_map(
        local,
        mesh=mesh,
        in_specs=(
            P(("groups", "blk"), None),
            P(("groups", "blk"), None),
            P(("groups", "blk")),
            P("groups"),
            P("blk", None),
            P(("groups", "blk"), None, None),
            P(("groups", "blk"), None, None),
        ),
        out_specs=(
            P(("groups", "blk"), None),
            P(("groups", "blk"), None, None),
            P(("groups", "blk"), None, None),
        ),
        check_vma=False,
    )
```

time: 357 us -> 363 us (1.017); the launches traced: 354 us -> 356 us
  Pallas kernels: 71 us -> 36.4 us
  waiting for transfers between devices: 131 us -> 158 us
  matrix products: 2.31 us -> 25.9 us
  starting transfers between devices: 86.4 us -> 78.1 us
  other arithmetic: 12.4 us -> 6.96 us
  local copies, waits for them, and re-layouts: 15.9 us -> 11.8 us
    ppermute x25 -> x8, starting transfers between devices: 53.8 us -> 9.88 us  [moved(): lax.ppermute(value, 'blk', [(i, (i + steps) % count) for i in range(count)])]
    pallas_call x8 -> x3, Pallas kernels: 71 us -> 36.4 us  [the longest x1 14.5 us: local(): shares = hidden_call(received, received, rows_all, place_all, starts)]
    all_to_all x1, starting transfers between devices: 15.9 us -> 48.7 us  [to_all(): return lax.all_to_all(copies, 'blk', split_axis=0, concat_axis=0)]
    dot_general x8 -> x11, matrix products: 2.31 us -> 25.9 us  [dot(): lax.dot_general(a, b, (dims, ((), ())), preferred_element_type=jnp.float32)]
    ppermute x25 -> x8, waiting for transfers between devices: 124 us -> 146 us  [moved(): lax.ppermute(value, 'blk', [(i, (i + steps) % count) for i in range(count)])]
    all_to_all x1, waiting for transfers between devices: 0.01 us -> 12 us  [local(): received = lax.all_to_all(packed, 'blk', split_axis=0, concat_axis=0)]
    all_to_all x1, waiting for transfers between devices: 5.31 us -> 0.01 us  [to_all(): return lax.all_to_all(copies, 'blk', split_axis=0, concat_axis=0)]
  transfers between devices with their start and end apart: 29 -> 13, of which waited for: 10 -> 5; matrix products, arithmetic and copies ran while one was open for 8% -> 8% of each run, Pallas kernels for 13% -> 10%
where the time goes in v6:
time: 363 us; the launch traced here: 356 us
  waiting for transfers between devices  158 us (44%)
  starting transfers between devices  78.1 us (22%)
  between operations  38.8 us (11%)
  Pallas kernels  36.4 us (10%)
  matrix products  25.9 us (7%)
  local copies, waits for them, and re-layouts  11.8 us (3%)
  other arithmetic  6.96 us (2%)
    ppermute x8, waiting for transfers between devices, moved(): lax.ppermute(value, 'blk', [(i, (i + steps) % count) for i in range(count)])  146 us
    all_to_all x1, starting transfers between devices, to_all(): return lax.all_to_all(copies, 'blk', split_axis=0, concat_axis=0)  48.7 us
    dot_general x11, matrix products, dot(): lax.dot_general(a, b, (dims, ((), ())), preferred_element_type=jnp.float32)  25.9 us
    pallas_call x1, Pallas kernels, local(): shares = hidden_call(received, received, rows_all, place_all, starts)  14.5 us
    all_to_all x1, waiting for transfers between devices, local(): received = lax.all_to_all(packed, 'blk', split_axis=0, concat_axis=0)  12 us
    pallas_call x1, Pallas kernels, pack(): pl.pallas_call(pack_kernel, grid=(devices,), in_specs=[pl.BlockSpec((1, f...  11.8 us
    pallas_call x1, Pallas kernels, local(): down_f = down_call(received, grad_all, rows_all, place_all, starts)  10.1 us
    ppermute x8, starting transfers between devices, moved(): lax.ppermute(value, 'blk', [(i, (i + steps) % count) for i in range(count)])  9.88 us
  transfers between devices with their start and end apart: 13, of which 5 were waited for; matrix products, arithmetic and copies ran while one was open for 8% of the time, Pallas kernels for 10%

profile of v6, /device:TPU:1, one launch (start us, length us, event | category | flops | bytes accessed | tf_op | source)
XLA Modules:
  0.0 356.2 jit_solution(10922496229215651572)
XLA Ops:
  7.2 0.7 all-gather.2.cloned.1.call-update
  7.9 1.3 concatenate.21
  9.2 11.8 %shard_map.94 = bf16[16,304,512]{2,1,0:T(8,128)(2,1)} custom-call(s32[1,512]{1,0:T(1,128)} %bitcast.95, bf16[192,8192]{1,0:T(8,128)(2,1)} %act.1, bf16[48,8192]{1,0:T(8,128)(2,1)} %bitcast.89, bf16[192,1024]{1,0:T(8,128)(2,1)} %cot.1), custom_call_target="tpu_custom_call" | custom-call | flops 150994944 | bytes 9961472 | tf_op jit(solution)/shard_map/pallas_call | solution.py:110
  20.9 7.5 %all-to-all-start = ((bf16[16,304,512]{2,1,0:T(8,128)(2,1)}), bf16[16,304,512]{2,1,0:T(8,128)(2,1)}, u32[]{:S(2)}, u32[]{:S(2)}) async-start(bf16[16,304,512]{2,1,0:T(8,128)(2,1)} %shard_map.94), calls=%async_computation | async-start | bytes 9961472 | tf_op jit(solution)/shard_map/all_to_all | solution.py:282
  28.5 0.7 fusion.36
  29.4 0.6 compare_and_fusion
  30.0 0.7 fusion.50
  32.6 1.7 collective-permute-start.3
  34.3 1.2 collective-permute-start.2
  35.5 0.4 collective-permute-start.1
  35.9 1.2 collective-permute-start
  44.6 0.6 fusion.49
  54.8 0.6 fusion.51
  61.0 0.7 copy.30.starts
  61.7 135.6 %collective-permute-done.2 = bf16[16,9216]{1,0:T(8,128)(2,1)S(1)} collective-permute-done((bf16[16,9216]{1,0:T(8,128)(2,1)S(1)}, bf16[16,9216]{1,0:T(8,128)(2,1)S(1)}, u32[]{:S(2)}, u32[]{:S(2)}) %collective-permute-start.2) | collective-permute-done | bytes 294944 | tf_op jit(solution)/shard_map/ppermute | solution.py:19
  197.2 0.7 collective-permute-done.1
  198.1 12.0 %all-to-all-done.act.maps = bf16[16,304,512]{2,1,0:T(8,128)(2,1)} async-done(((bf16[16,304,512]{2,1,0:T(8,128)(2,1)}), bf16[16,304,512]{2,1,0:T(8,128)(2,1)}, u32[]{:S(2)}, u32[]{:S(2)}) %all-to-all-start) | async-done | bytes 4980768 | tf_op jit(solution)/shard_map/all_to_all | solution.py:282
  210.0 2.0 subtract_add_fusion
  212.1 0.4 select_reduce_fusion
  212.6 1.2 fusion.48
  213.8 0.2 fusion.19
  214.0 0.3 fusion.2
  214.8 0.7 broadcast_in_dim.117
  215.4 48.7 %all-to-all-start.1 = ((bf16[16,24,256]{2,1,0:T(8,128)(2,1)}), bf16[16,24,256]{2,1,0:T(8,128)(2,1)S(1)}, u32[]{:S(2)}, u32[]{:S(2)}) async-start(bf16[16,24,256]{2,1,0:T(8,128)(2,1)} %broadcast_in_dim.117), calls=%async_computation.1 | async-start | bytes 393216 | tf_op jit(solution)/shard_map/all_to_all | solution.py:25
  264.1 14.5 %shard_map.95.refs_1_ = f32[256,384]{1,0:T(8,128)} custom-call(bf16[16,304,512]{2,1,0:T(8,128)(2,1)} %all-to-all-done.act.maps, bf16[16,304,512]{2,1,0:T(8,128)(2,1)} %all-to-all-done.act.maps, s32[16,1,192]{2,1,0:T(1,128)} %get-tuple-element.15.rows.refs_0_, s32[16,1,192]{2,1,0:T(1,128)} %copy-done.1, s32[32,1]{1,0:T(8,128)} %copy.30.starts), custom_call_target="tpu_custom_call" | custom-call | flops 2415919104 | bytes 3145728 | tf_op jit(solution)/shard_map/pallas_call | solution.py:337
  278.6 0.3 convolution_convert_fusion.2
  278.9 1.9 copy.33
  280.8 2.7 fusion.10
  283.6 6.0 %all-to-all-start.3 = ((f32[16,24,256]{2,1,0:T(8,128)}), f32[16,24,256]{2,1,0:T(8,128)S(1)}, u32[]{:S(2)}, u32[]{:S(2)}) async-start(f32[16,24,256]{2,1,0:T(8,128)} %bitcast.29), calls=%async_computation.3 | async-start | bytes 786432 | tf_op jit(solution)/shard_map/all_to_all | solution.py:341
  289.6 2.8 fusion.12
  292.4 2.7 fusion.14
  295.0 0.8 copy.29
  295.9 10.1 %shard_map.97 = bf16[768,512]{1,0:T(8,128)(2,1)} custom-call(bf16[16,304,512]{2,1,0:T(8,128)(2,1)} %all-to-all-done.act.maps, bf16[256,384]{1,0:T(8,128)(2,1)} %bitcast.94, s32[16,1,192]{2,1,0:T(1,128)} %shard_map.96.rows, s32[16,1,192]{2,1,0:T(1,128)} %copy-done.1, s32[32,1]{1,0:T(8,128)} %copy.30.starts), custom_call_target="tpu_custom_call" | custom-call | flops 2415919104 | bytes 3145728 | tf_op jit(solution)/shard_map/pallas_call | solution.py:339
  306.0 6.0 %all-to-all-start.2 = ((bf16[16,48,512]{2,1,0:T(8,128)(2,1)}), bf16[16,48,512]{2,1,0:T(8,128)(2,1)S(1)}, u32[]{:S(2)}, u32[]{:S(2)}) async-start(bf16[16,48,512]{2,1,0:T(8,128)(2,1)} %bitcast.90), calls=%async_computation.2 | async-start | bytes 1572864 | tf_op jit(solution)/shard_map/all_to_all | solution.py:344
  312.0 0.5 convolution_convert_fusion.1
  313.2 0.2 fusion.43
  313.4 1.9 select_add_fusion.1
  315.3 3.2 collective-permute-start.7
  318.5 1.7 collective-permute-start.6
  320.2 0.3 collective-permute-start.5
  320.7 0.5 convolution_convert_fusion
  321.2 5.5 %collective-permute-done.7 = f32[16,1024]{1,0:T(8,128)S(1)} collective-permute-done((f32[16,1024]{1,0:T(8,128)S(1)}, f32[16,1024]{1,0:T(8,128)S(1)}, u32[]{:S(2)}, u32[]{:S(2)}) %collective-permute-start.7) | collective-permute-done | bytes 65568 | tf_op jit(solution)/shard_map/ppermute | solution.py:19
  326.7 3.8 %collective-permute-done.6 = f32[16,1024]{1,0:T(8,128)S(1)} collective-permute-done((f32[16,1024]{1,0:T(8,128)S(1)}, f32[16,1024]{1,0:T(8,128)S(1)}, u32[]{:S(2)}, u32[]{:S(2)}) %collective-permute-start.6) | collective-permute-done | bytes 65568 | tf_op jit(solution)/shard_map/ppermute | solution.py:19
  330.6 0.7 pad_maximum_fusion
  331.3 0.2 convert_bitcast_fusion
  331.5 0.9 copy.32
  332.4 1.4 reshape.228
  333.8 15.5 %add_convert_fusion = bf16[384,8192]{1,0:T(8,128)(2,1)} fusion(bf16[8192,1024]{1,0:T(8,128)(2,1)} %all-gather.2.cloned.1.call-done, f32[128,8192]{1,0:T(8,128)} %fusion.10, f32[128,8192]{1,0:T(8,128)} %fusion.12, f32[128,8192]{1,0:T(8,128)} %fusion.14, bf16[384,512]{1,0:T(8,128)(2,1)S(1)} %convolution_convert_fusion, ...), kind=kOutput, calls=%fused_computation.2 | convolution fusion | flops 6466043904 | bytes 36438016 | tf_op jit(solution)/shard_map/dot_general | solution.py:41
  (44 shorter events, 1.9 us)
Async XLA Ops:
  7.2 326.7 %all-gather.2.cloned.1.call-start = ((), (), s32[]{:S(2)}) async-start(), calls=%async_computation.4 | async-start | bytes 17825792 | tf_op jit(solution)/shard_map/all_gather | solution.py:278
  20.9 7.6 %copy-start.3 = (s32[32]{0:T(128)S(1)}, s32[32]{0:T(128)}, u32[]{:S(2)}) copy-start(s32[32]{0:T(128)} %param.10) | copy-start | bytes 388
  20.9 11.6 %copy-start = (bf16[3,16,8192]{2,1,0:T(8,128)(2,1)S(1)}, bf16[3,16,8192]{2,1,0:T(8,128)(2,1)}, u32[]{:S(2)}) copy-start(bf16[3,16,8192]{2,1,0:T(8,128)(2,1)} %param.12) | copy-start | bytes 2359300
  20.9 11.7 %copy-start.2 = (bf16[3,16,1024]{2,1,0:T(8,128)(2,1)S(1)}, bf16[3,16,1024]{2,1,0:T(8,128)(2,1)}, u32[]{:S(2)}) copy-start(bf16[3,16,1024]{2,1,0:T(8,128)(2,1)} %param.13) | copy-start | bytes 294916
  20.9 189.1 %all-to-all-start = ((bf16[16,304,512]{2,1,0:T(8,128)(2,1)}), bf16[16,304,512]{2,1,0:T(8,128)(2,1)}, u32[]{:S(2)}, u32[]{:S(2)}) async-start(bf16[16,304,512]{2,1,0:T(8,128)(2,1)} %shard_map.94), calls=%async_computation | async-start | bytes 9961472 | tf_op jit(solution)/shard_map/all_to_all | solution.py:282
  32.6 29.0 %collective-permute-start.3 = (bf16[16,9216]{1,0:T(8,128)(2,1)S(1)}, bf16[16,9216]{1,0:T(8,128)(2,1)S(1)}, u32[]{:S(2)}, u32[]{:S(2)}) collective-permute-start(bf16[16,9216]{1,0:T(8,128)(2,1)S(1)} %dynamic-slice_bitcast_fusion), channel_id=1, source_target_pairs={{0,1},{1,2},{2,3},{3,4},{4,5},{5,6},{6,7},{7,8},{8,9},{9,10},{10,1... | collective-permute-start | bytes 884744 | tf_op jit(solution)/shard_map/ppermute | solution.py:19
  34.3 162.9 %collective-permute-start.2 = (bf16[16,9216]{1,0:T(8,128)(2,1)S(1)}, bf16[16,9216]{1,0:T(8,128)(2,1)S(1)}, u32[]{:S(2)}, u32[]{:S(2)}) collective-permute-start(bf16[16,9216]{1,0:T(8,128)(2,1)S(1)} %dynamic-slice_bitcast_fusion), channel_id=1, source_target_pairs={{0,2},{1,3},{2,4},{3,5},{4,6},{5,7},{6,8},{7,9},{8,10},{9,11},{10,... | collective-permute-start | bytes 884744 | tf_op jit(solution)/shard_map/ppermute | solution.py:19
  35.5 162.4 %collective-permute-start.1 = (bf16[16,9216]{1,0:T(8,128)(2,1)S(1)}, bf16[16,9216]{1,0:T(8,128)(2,1)S(1)}, u32[]{:S(2)}, u32[]{:S(2)}) collective-permute-start(bf16[16,9216]{1,0:T(8,128)(2,1)S(1)} %dynamic-slice_bitcast_fusion), channel_id=1, source_target_pairs={{0,3},{1,4},{2,5},{3,6},{4,7},{5,8},{6,9},{7,10},{8,11},{9,12},{10... | collective-permute-start | bytes 884744 | tf_op jit(solution)/shard_map/ppermute | solution.py:19
  35.9 162.0 %collective-permute-start = (bf16[16,9216]{1,0:T(8,128)(2,1)S(1)}, bf16[16,9216]{1,0:T(8,128)(2,1)S(1)}, u32[]{:S(2)}, u32[]{:S(2)}) collective-permute-start(bf16[16,9216]{1,0:T(8,128)(2,1)S(1)} %dynamic-slice_bitcast_fusion), channel_id=1, source_target_pairs={{0,4},{1,5},{2,6},{3,7},{4,8},{5,9},{6,10},{7,11},{8,12},{9,13},{1... | collective-permute-start | bytes 884744 | tf_op jit(solution)/shard_map/ppermute | solution.py:19
  212.0 52.1 %copy-start.1 = (s32[16,1,192]{2,1,0:T(1,128)}, s32[16,1,192]{2,1,0:T(1,128)S(1)}, u32[]{:S(2)}) copy-start(s32[16,1,192]{2,1,0:T(1,128)S(1)} %get-tuple-element.21.spots) | copy-start | bytes 36868
  215.4 68.1 %all-to-all-start.1 = ((bf16[16,24,256]{2,1,0:T(8,128)(2,1)}), bf16[16,24,256]{2,1,0:T(8,128)(2,1)S(1)}, u32[]{:S(2)}, u32[]{:S(2)}) async-start(bf16[16,24,256]{2,1,0:T(8,128)(2,1)} %broadcast_in_dim.117), calls=%async_computation.1 | async-start | bytes 393216 | tf_op jit(solution)/shard_map/all_to_all | solution.py:25
  283.6 22.4 %all-to-all-start.3 = ((f32[16,24,256]{2,1,0:T(8,128)}), f32[16,24,256]{2,1,0:T(8,128)S(1)}, u32[]{:S(2)}, u32[]{:S(2)}) async-start(f32[16,24,256]{2,1,0:T(8,128)} %bitcast.29), calls=%async_computation.3 | async-start | bytes 786432 | tf_op jit(solution)/shard_map/all_to_all | solution.py:341
  306.0 25.3 %all-to-all-start.2 = ((bf16[16,48,512]{2,1,0:T(8,128)(2,1)}), bf16[16,48,512]{2,1,0:T(8,128)(2,1)S(1)}, u32[]{:S(2)}, u32[]{:S(2)}) async-start(bf16[16,48,512]{2,1,0:T(8,128)(2,1)} %bitcast.90), calls=%async_computation.2 | async-start | bytes 1572864 | tf_op jit(solution)/shard_map/all_to_all | solution.py:344
  315.3 11.4 %collective-permute-start.7 = (f32[16,1024]{1,0:T(8,128)S(1)}, f32[16,1024]{1,0:T(8,128)S(1)}, u32[]{:S(2)}, u32[]{:S(2)}) collective-permute-start(f32[16,1024]{1,0:T(8,128)S(1)} %get-tuple-element.10), channel_id=1, source_target_pairs={{0,12},{1,13},{2,14},{3,15},{4,0},{5,1},{6,2},{7,3},{8,4},{9,5},{1... | collective-permute-start | bytes 196616 | tf_op jit(solution)/shard_map/ppermute | solution.py:19
  318.5 12.0 %collective-permute-start.6 = (f32[16,1024]{1,0:T(8,128)S(1)}, f32[16,1024]{1,0:T(8,128)S(1)}, u32[]{:S(2)}, u32[]{:S(2)}) collective-permute-start(f32[16,1024]{1,0:T(8,128)S(1)} %get-tuple-element.10), channel_id=1, source_target_pairs={{0,13},{1,14},{2,15},{3,0},{4,1},{5,2},{6,3},{7,4},{8,5},{9,6},{10... | collective-permute-start | bytes 196616 | tf_op jit(solution)/shard_map/ppermute | solution.py:19
  320.2 10.3 %collective-permute-start.5 = (f32[16,1024]{1,0:T(8,128)S(1)}, f32[16,1024]{1,0:T(8,128)S(1)}, u32[]{:S(2)}, u32[]{:S(2)}) collective-permute-start(f32[16,1024]{1,0:T(8,128)S(1)} %get-tuple-element.10), channel_id=1, source_target_pairs={{0,14},{1,15},{2,0},{3,1},{4,2},{5,3},{6,4},{7,5},{8,6},{9,7},{10,... | collective-permute-start | bytes 196616 | tf_op jit(solution)/shard_map/ppermute | solution.py:19
  320.5 10.0 %collective-permute-start.4 = (f32[16,1024]{1,0:T(8,128)S(1)}, f32[16,1024]{1,0:T(8,128)S(1)}, u32[]{:S(2)}, u32[]{:S(2)}) collective-permute-start(f32[16,1024]{1,0:T(8,128)S(1)} %get-tuple-element.10), channel_id=1, source_target_pairs={{0,15},{1,0},{2,1},{3,2},{4,3},{5,4},{6,5},{7,6},{8,7},{9,8},{10,9... | collective-permute-start | bytes 196616 | tf_op jit(solution)/shard_map/ppermute | solution.py:19
Sparse Core Ops, SparseCore 0:
  10.2 229.9 all-gather.1

commit v7 on v6

--- a/solution.py
+++ b/solution.py
@@ -1,3 +1,5 @@
+import functools
+
 import jax
 import jax.numpy as jnp
 from jax import lax
@@ -63,11 +65,108 @@
     return (high * DIGIT + middle) * DIGIT + low, place_high * DIGIT + place
 
 
+def weight_pieces(weight):
+    count = lax.axis_size("blk")
+    half = weight.shape[0] // 2
+    group = lax.axis_index("groups")
+    mine = lax.dynamic_slice_in_dim(weight, group * half, half, 0)
+    lines = [list(range(k, count, 4)) for k in range(4)]
+    column = lax.all_gather(mine, "blk", axis_index_groups=lines)
+
+    def over(piece, bit):
+        return lax.ppermute(piece, "blk", [(i, i ^ bit) for i in range(count)])
+
+    def groups(piece):
+        return lax.ppermute(piece, "groups", [(0, 1), (1, 0)])
+
+    across = over(column, 2)
+    pieces = []
+    for piece in (column, across):
+        theirs = groups(piece)
+        pieces.append((piece, theirs))
+        pieces.append((over(piece, 1), over(theirs, 1)))
+    return pieces
+
+
+def quarter_kernel(where, cot, grad, down, mine, theirs, *rest):
+    out = rest[-1]
+    rank = grad.shape[1]
+    half = mine.shape[1]
+    lora = [
+        adapter_scale
+        * dot(
+            grad[b * BLOCK : (b + 1) * BLOCK, :],
+            down[b * rank : (b + 1) * rank, :],
+            ((1,), (0,)),
+        )
+        for b in range(cot.shape[0] // BLOCK)
+    ]
+    lora = jnp.concatenate(lora, axis=0).astype(jnp.bfloat16).astype(jnp.float32)
+
+    def product(group):
+        for k, piece in enumerate((mine, theirs) if group == 0 else (theirs, mine)):
+            part = slice(k * half, (k + 1) * half)
+            frozen = dot(cot[...], piece[0], ((1,), (1,)))
+            out[:, part] = (frozen + lora[:, part]).astype(jnp.bfloat16)
+
+    for group in range(2):
+        pl.when(where[1] == group)(functools.partial(product, group))
+
+
+def write_quarter(quarter, first, group, cot, grad, down, out=None):
+    mine, theirs = quarter
+    rows, depth = cot.shape
+    width = down.shape[1]
+    shards, half, _ = mine.shape
+    where = jnp.stack([first, group]).astype(jnp.int32)
+    piece = pl.BlockSpec((1, half, depth), lambda j, where: (j, 0, 0))
+    specs = [
+        pl.BlockSpec((rows, depth), lambda j, where: (0, 0)),
+        pl.BlockSpec(grad.shape, lambda j, where: (0, 0)),
+        pl.BlockSpec((down.shape[0], 2 * half), lambda j, where: (0, 4 * j + where[0])),
+        piece,
+        piece,
+    ]
+    args = [where, cot, grad, down, mine, theirs]
+    alias = {}
+    if out is not None:
+        specs.append(pl.BlockSpec(memory_space=pl.ANY))
+        args.append(out)
+        alias = {len(args) - 1: 0}
+    return pl.pallas_call(
+        quarter_kernel,
+        grid_spec=pltpu.PrefetchScalarGridSpec(
+            num_scalar_prefetch=1,
+            grid=(shards,),
+            in_specs=specs,
+            out_specs=pl.BlockSpec((rows, 2 * half), lambda j, where: (0, 4 * j + where[0])),
+        ),
+        out_shape=jax.ShapeDtypeStruct((rows, width), jnp.bfloat16),
+        input_output_aliases=alias,
+        cost_estimate=pl.CostEstimate(
+            flops=4 * rows * depth * half * shards,
+            bytes_accessed=4 * (depth + rows) * half * shards,
+            transcendentals=0,
+        ),
+        compiler_params=pltpu.CompilerParams(vmem_limit_bytes=VMEM),
+    )(*args)
+
+
+def together(pieces, firsts, group):
+    shards, half, depth = pieces[0][0].shape
+    weight = jnp.zeros((shards, 4, 2, half, depth), jnp.bfloat16)
+    for quarter, first in zip(pieces, firsts):
+        for k, piece in enumerate(quarter):
+            place = (0, first, group if k == 0 else 1 - group, 0, 0)
+            weight = lax.dynamic_update_slice(weight, piece[:, None, None], place)
+    return weight.reshape(-1, depth)
+
+
 def pack_kernel(rows, act, maps, cot, out, place, digits):
-    tokens, features = act.shape
-    shared = maps.shape[0]
+    targets, packed, features = out.shape
+    tokens, shared = act.shape[0], maps.shape[0]
     cap = shared * features // cot.shape[1]
-    devices = pl.num_programs(0)
+    devices = targets * pl.num_programs(0)
     step = pl.program_id(0)
 
     @pl.when(step == 0)
@@ -86,18 +185,19 @@
             values = jnp.where(which == k, digit, values)
         digits[...] = values.astype(jnp.float32).astype(out.dtype)
 
-    index = lax.broadcasted_iota(jnp.int32, (cap, tokens), 0) + step * cap
+    index = lax.broadcasted_iota(jnp.int32, (targets * cap, tokens), 0) + step * targets * cap
     send = jnp.where(index == place[:, :tokens], 1.0, 0.0).astype(jnp.bfloat16)
-    sent = [
-        dot(send, cot[:, k : k + features], ((1,), (0,)))
-        for k in range(0, cot.shape[1], features)
-    ]
-    out[0, :tokens, :] = act[...]
-    out[0, tokens : tokens + shared, :] = maps[...]
-    out[0, tokens + shared : tokens + 2 * shared, :] = jnp.concatenate(sent, axis=0).astype(
-        out.dtype
-    )
-    out[0, tokens + 2 * shared :, :] = digits[...]
+    sent = dot(send, cot[...], ((1,), (0,)))
+    for k in range(targets):
+        part = slice(k * features, (k + 1) * features)
+        some = sent[k * cap : (k + 1) * cap]
+        folds = [some[:, f : f + features] for f in range(0, cot.shape[1], features)]
+        out[k, :tokens, :] = act[:, part]
+        out[k, tokens : tokens + shared, :] = maps[:, part]
+        out[k, tokens + shared : tokens + 2 * shared, :] = jnp.concatenate(
+            folds, axis=0
+        ).astype(out.dtype)
+        out[k, tokens + 2 * shared :, :] = digits[...]
 
 
 def pack(rows, act, maps, cot, devices, cap):
@@ -105,18 +205,19 @@
     features = width // devices
     shared = maps.shape[0]
     total = tokens + 2 * shared + 16
+    targets = 4
     if features % LANES == 0 and cap % 8 == 0 and features >= tokens and devices <= 16:
         padding = jnp.full((features - tokens,), 16 * cap * devices, jnp.int32)
         return pl.pallas_call(
             pack_kernel,
-            grid=(devices,),
+            grid=(devices // targets,),
             in_specs=[
                 pl.BlockSpec((1, features), lambda j: (0, 0)),
-                pl.BlockSpec((tokens, features), lambda j: (0, j)),
-                pl.BlockSpec((shared, features), lambda j: (0, j)),
+                pl.BlockSpec((tokens, targets * features), lambda j: (0, j)),
+                pl.BlockSpec((shared, targets * features), lambda j: (0, j)),
                 pl.BlockSpec(cot.shape, lambda j: (0, 0)),
             ],
-            out_specs=pl.BlockSpec((1, total, features), lambda j: (j, 0, 0)),
+            out_specs=pl.BlockSpec((targets, total, features), lambda j: (j, 0, 0)),
             out_shape=jax.ShapeDtypeStruct((devices, total, features), act.dtype),
             scratch_shapes=[
                 pltpu.VMEM((1, features), jnp.int32),
@@ -171,30 +272,37 @@
     return jnp.where(hit, 1.0, 0.0).astype(jnp.bfloat16)
 
 
+def all_rows(act, tokens):
+    return jnp.concatenate([act[k, :tokens, :] for k in range(act.shape[0])], axis=0)
+
+
+def of_source(sources, width):
+    lane = lax.broadcasted_iota(jnp.int32, (sources, 1, width), 2)
+    return lane // (width // sources) == lax.broadcasted_iota(
+        jnp.int32, (sources, 1, width), 0
+    )
+
+
 def hidden_kernel(act, maps, rows, spots, starts, out):
-    sources, _, tokens = rows.shape
+    sources, share, width = act.shape[0], maps.shape[1], rows.shape[1]
     rank, places = out.shape[0] // sources, out.shape[1]
-    share = maps.shape[1]
-    for k in range(sources):
-        slot = slot_of(rows[k], starts[...])
-        total = jnp.zeros((rank, tokens), jnp.float32)
-        for part in slot_chunks(maps.shape[0] * share):
-            size = part.stop - part.start
-            some = maps[part.start // share : part.stop // share].reshape(size, -1)
-            each = dot(some, act[k, :tokens, :], ((1,), (1,))).reshape(size // rank, rank, -1)
-            total += jnp.sum(
-                jnp.where(own_rows(slot, part.start, size, rank), each, 0.0), axis=0
-            )
-        high = total.astype(jnp.bfloat16)
-        low = (total - high.astype(jnp.float32)).astype(jnp.bfloat16)
-        place = placing(spots[k], places)
-        out[k * rank : (k + 1) * rank, :] = dot(high, place, ((1,), (1,))) + dot(
-            low, place, ((1,), (1,))
-        )
+    slot = slot_of(rows[...], starts[...])
+    every = all_rows(act, width // sources)
+    total = jnp.zeros((rank, width), jnp.float32)
+    for part in slot_chunks(maps.shape[0] * share):
+        size = part.stop - part.start
+        some = maps[part.start // share : part.stop // share].reshape(size, -1)
+        each = dot(some, every, ((1,), (1,))).reshape(size // rank, rank, -1)
+        total += jnp.sum(jnp.where(own_rows(slot, part.start, size, rank), each, 0.0), axis=0)
+    total = jnp.where(of_source(sources, width), total[None], 0.0).reshape(out.shape[0], width)
+    high = total.astype(jnp.bfloat16)
+    low = (total - high.astype(jnp.float32)).astype(jnp.bfloat16)
+    place = placing(spots[...], places)
+    out[...] = dot(high, place, ((1,), (1,))) + dot(low, place, ((1,), (1,)))
 
 
 def down_kernel(act, grad, rows, spots, starts, out, total):
-    sources, _, tokens = rows.shape
+    sources, width = act.shape[0], rows.shape[1]
     rank, places = grad.shape[0] // sources, grad.shape[1]
     step = pl.program_id(0)
 
@@ -202,15 +310,16 @@
     def _():
         total[...] = jnp.zeros_like(total)
 
-    for k in range(sources):
-        slot = slot_of(rows[k], starts[...])
-        place = placing(spots[k], places)
-        wide = dot(grad[k * rank : (k + 1) * rank, :], place, ((1,), (0,)))[None]
-        for part in slot_chunks(total.shape[0]):
-            size = part.stop - part.start
-            placed = jnp.where(own_rows(slot, part.start, size, rank), wide, 0.0)
-            placed = placed.reshape(size, -1).astype(jnp.bfloat16)
-            total[part, :] += dot(placed, act[k, :tokens, :], ((1,), (0,)))
+    slot = slot_of(rows[...], starts[...])
+    every = all_rows(act, width // sources)
+    wide = dot(grad[...], placing(spots[...], places), ((1,), (0,)))
+    wide = wide.reshape(sources, rank, width)
+    wide = jnp.sum(jnp.where(of_source(sources, width), wide, 0.0), axis=0, keepdims=True)
+    for part in slot_chunks(total.shape[0]):
+        size = part.stop - part.start
+        placed = jnp.where(own_rows(slot, part.start, size, rank), wide, 0.0)
+        placed = placed.reshape(size, -1).astype(jnp.bfloat16)
+        total[part, :] += dot(placed, every, ((1,), (0,)))
 
     @pl.when(step == pl.num_programs(0) - 1)
     def _():
@@ -220,11 +329,11 @@
 def feature_calls(received, tokens, share, rank, places, starts):
     devices, packed, features = received.shape
     width = devices * share
-    sources = 2
+    sources = 4
     grid = (devices // sources,)
     act = pl.BlockSpec((sources, packed, features), lambda j: (j, 0, 0))
     maps = pl.BlockSpec((devices, share, features), lambda j: (0, tokens // share, 0))
-    rows = pl.BlockSpec((sources, 1, tokens), lambda j: (j, 0, 0))
+    rows = pl.BlockSpec((1, sources * tokens), lambda j: (0, j))
     begin = pl.BlockSpec((starts, 1), lambda j: (0, 0))
     placed = pl.BlockSpec((sources * rank, places), lambda j: (j, 0))
     cost = pl.CostEstimate(
@@ -275,21 +384,7 @@
     cap = resident_rows // devices
     start_ids = tenant_first_row // BLOCK
 
-    weight = lax.all_gather(frozen_value_weight, "blk", axis=0, tiled=True)
-
-    flat_maps = adapter_down_maps.reshape(share, width)
-    packed = pack(token_layout_row, activations, flat_maps, cotangent, devices, cap)
-    received = lax.all_to_all(packed, "blk", split_axis=0, concat_axis=0)
-    recv_cot = [
-        received[:, tokens + share + k * cap : tokens + share + (k + 1) * cap].reshape(
-            resident_rows, features
-        )
-        for k in range(out_width // features)
-    ]
-    per_digit = -(-tokens // features)
-    digits = received[:, tokens + 2 * share : tokens + 2 * share + 5 * per_digit]
-    digits = digits.reshape(devices, 5, per_digit * features)[:, :, :tokens]
-    rows_all, place_all = from_digits(digits)
+    pieces = weight_pieces(frozen_value_weight)
 
     first_block = device * resident
     block_numbers = first_block + jnp.arange(resident, dtype=jnp.int32)
@@ -311,6 +406,21 @@
     block_maps = jnp.concatenate(block_maps, axis=0)
     down_blocks, up_blocks = block_maps[:, :width], block_maps[:, width:]
 
+    flat_maps = adapter_down_maps.reshape(share, width)
+    packed = pack(token_layout_row, activations, flat_maps, cotangent, devices, cap)
+    packed = after(packed, carried)
+    received = lax.all_to_all(packed, "blk", split_axis=0, concat_axis=0)
+    recv_cot = [
+        received[:, tokens + share + k * cap : tokens + share + (k + 1) * cap].reshape(
+            resident_rows, features
+        )
+        for k in range(out_width // features)
+    ]
+    per_digit = -(-tokens // features)
+    digits = received[:, tokens + 2 * share : tokens + 2 * share + 5 * per_digit]
+    digits = digits.reshape(devices, 5, per_digit * features)[:, :, :tokens]
+    rows_all, place_all = from_digits(digits)
+
     spots = device * cap + jnp.arange(cap, dtype=jnp.int32)
     hit = place_all[:, None, :] == spots[None, :, None]
     row_in = rows_all - device * resident_rows + 1
@@ -332,8 +442,8 @@
     hidden_call, down_call = feature_calls(
         received, tokens, share, rank, resident_rows, starts.shape[0]
     )
-    rows_all = rows_all[:, None, :]
-    place_all = place_all[:, None, :]
+    rows_all, place_all = rows_all.reshape(1, -1), place_all.reshape(1, -1)
+    place_all = after(place_all, pieces[2][0])
     shares = hidden_call(received, received, rows_all, place_all, starts)
     rows_all = after(rows_all, shares)
     down_f = down_call(received, grad_all, rows_all, place_all, starts)
@@ -348,15 +458,7 @@
         [dot(arrange, part, ((0,), (0,))).astype(jnp.bfloat16) for part in recv_cot], axis=1
     )
     grad_rows = dot(arrange, grad_in, ((0,), (0,))).astype(jnp.bfloat16)
-    lora = [
-        dot(
-            grad_rows[b * BLOCK : (b + 1) * BLOCK],
-            down_blocks[b * rank : (b + 1) * rank],
-            ((1,), (0,)),
-        )
-        for b in range(resident)
-    ]
-    lora = (adapter_scale * jnp.concatenate(lora, axis=0)).astype(jnp.bfloat16)
+    grad_rows = after(grad_rows, down_f)
     wide = jnp.where(in_block, jnp.concatenate([hidden] * resident, axis=1), 0)
     up_all = [dot(wide, part, ((0,), (0,))) for part in recv_cot]
     up_all = jnp.concatenate(up_all, axis=1).reshape(resident, rank, out_width)
@@ -376,8 +478,26 @@
         up_grads.append(adapter_scale * total)
     up_map_gradient = jnp.stack(up_grads)
 
-    out = dot(cot_rows, weight, ((1,), (1,))) + lora.astype(jnp.float32)
-    out = out.astype(jnp.bfloat16)
+    group = lax.axis_index("groups")
+    quarter = device % 4
+    firsts = [quarter, quarter ^ 1, quarter ^ 2, quarter ^ 3]
+    if pieces[0][0].shape[1] % LANES == 0:
+        out = None
+        for piece, first in zip(pieces, firsts):
+            out = write_quarter(piece, first, group, cot_rows, grad_rows, down_blocks, out)
+    else:
+        weight = together(pieces, firsts, group)
+        lora = [
+            dot(
+                grad_rows[b * BLOCK : (b + 1) * BLOCK],
+                down_blocks[b * rank : (b + 1) * rank],
+                ((1,), (0,)),
+            )
+            for b in range(resident)
+        ]
+        lora = (adapter_scale * jnp.concatenate(lora, axis=0)).astype(jnp.bfloat16)
+        out = dot(cot_rows, weight, ((1,), (1,))) + lora.astype(jnp.float32)
+        out = out.astype(jnp.bfloat16)
     return (out, down_map_gradient, up_map_gradient)
 
 

time: 363 us -> 397 us (1.094); the launches traced: 356 us -> 394 us
  waiting for transfers between devices: 158 us -> 202 us
  starting transfers between devices: 78.1 us -> 53.3 us
  matrix products: 25.9 us -> 9.35 us
  Pallas kernels: 36.4 us -> 49.9 us
  other arithmetic: 6.96 us -> 18 us
  local copies, waits for them, and re-layouts: 11.8 us -> 22.3 us
    ppermute x8, waiting for transfers between devices: 146 us -> 7.19 us  [moved(): lax.ppermute(value, 'blk', [(i, (i + steps) % count) for i in range(count)])]
    all_gather x1, waiting for transfers between devices: 0.01 us -> 108 us  [weight_pieces(): column = lax.all_gather(mine, 'blk', axis_index_groups=lines)]
    ppermute x0 -> x7, waiting for transfers between devices: none -> 83.1 us  [the longest x2 46.4 us: groups(): return lax.ppermute(piece, 'groups', [(0, 1), (1, 0)])]
    all_to_all x1, starting transfers between devices: 48.7 us -> 14.3 us  [to_all(): return lax.all_to_all(copies, 'blk', split_axis=0, concat_axis=0)]
    pallas_call x1 -> x5, Pallas kernels: 11.8 us -> 34.1 us  [the longest x4 28.7 us: write_quarter(): pl.pallas_call(quarter_kernel, grid_spec=pltpu.PrefetchScalarGridSpec(num...]
    dot_general x11 -> x7, matrix products: 25.9 us -> 9.35 us  [dot(): lax.dot_general(a, b, (dims, ((), ())), preferred_element_type=jnp.float32)]
    all_to_all x1, waiting for transfers between devices: 12 us -> 0.01 us  [local(): received = lax.all_to_all(packed, 'blk', split_axis=0, concat_axis=0)]
    ppermute x0 -> x7, starting transfers between devices: none -> 6.92 us  [the longest x5 4.44 us: over(): return lax.ppermute(piece, 'blk', [(i, i ^ bit) for i in range(count)])]
  transfers between devices with their start and end apart: 13 -> 20, of which waited for: 5 -> 7; matrix products, arithmetic and copies ran while one was open for 8% -> 10% of each run, Pallas kernels for 10% -> 13%
where the time goes in v7:
time: 397 us; the launch traced here: 394 us
  waiting for transfers between devices  202 us (51%)
  starting transfers between devices  53.3 us (13%)
  Pallas kernels  49.9 us (13%)
  between operations  39.3 us (10%)
  local copies, waits for them, and re-layouts  22.3 us (6%)
  other arithmetic  18 us (5%)
  matrix products  9.35 us (2%)
    all_gather x1, waiting for transfers between devices, weight_pieces(): column = lax.all_gather(mine, 'blk', axis_index_groups=lines)  108 us
    ppermute x2, waiting for transfers between devices, groups(): return lax.ppermute(piece, 'groups', [(0, 1), (1, 0)])  46.4 us
    ppermute x5, waiting for transfers between devices, over(): return lax.ppermute(piece, 'blk', [(i, i ^ bit) for i in range(count)])  36.7 us
    pallas_call x4, Pallas kernels, write_quarter(): pl.pallas_call(quarter_kernel, grid_spec=pltpu.PrefetchScalarGridSpec(num...  28.7 us
    all_to_all x1, starting transfers between devices, to_all(): return lax.all_to_all(copies, 'blk', split_axis=0, concat_axis=0)  14.3 us
    ppermute x8, starting transfers between devices, moved(): lax.ppermute(value, 'blk', [(i, (i + steps) % count) for i in range(count)])  12.9 us
    dot_general x7, matrix products, dot(): lax.dot_general(a, b, (dims, ((), ())), preferred_element_type=jnp.float32)  9.35 us
    all_to_all x1, starting transfers between devices, local(): received = lax.all_to_all(packed, 'blk', split_axis=0, concat_axis=0)  8.94 us
  transfers between devices with their start and end apart: 20, of which 7 were waited for; matrix products, arithmetic and copies ran while one was open for 10% of the time, Pallas kernels for 13%

profile of v7, /device:TPU:1, one launch (start us, length us, event | category | flops | bytes accessed | tf_op | source)
XLA Modules:
  0.0 394.4 jit_solution(1157515812020817398)
XLA Ops:
  7.2 1.5 fusion.27
  11.5 1.2 constant_dynamic-update-slice_fusion.1
  14.3 2.2 collective-permute-start
  16.5 2.1 collective-permute-start.1
  18.6 1.2 collective-permute-start.2
  26.0 5.4 %shard_map.94.refs_0_ = bf16[16,304,512]{2,1,0:T(8,128)(2,1)} custom-call(s32[1,512]{1,0:T(1,128)} %bitcast.101, bf16[192,8192]{1,0:T(8,128)(2,1)} %act.1, bf16[48,8192]{1,0:T(8,128)(2,1)} %bitcast.94, bf16[192,1024]{1,0:T(8,128)(2,1)} %cot.1), custom_call_target="tpu_custom_call" | custom-call | flops 150994944 | bytes 9961472 | tf_op jit(solution)/shard_map/pallas_call | solution.py:211
  31.4 2.7 collective-permute-done.1
  34.1 4.5 %collective-permute-done.2 = bf16[16,9216]{1,0:T(8,128)(2,1)S(1)} collective-permute-done((bf16[16,9216]{1,0:T(8,128)(2,1)S(1)}, bf16[16,9216]{1,0:T(8,128)(2,1)S(1)}, u32[]{:S(2)}, u32[]{:S(2)}) %collective-permute-start.2) | collective-permute-done | bytes 294944 | tf_op jit(solution)/shard_map/ppermute | solution.py:21
  39.4 8.9 %all-to-all-start = ((bf16[16,304,512]{2,1,0:T(8,128)(2,1)}), bf16[16,304,512]{2,1,0:T(8,128)(2,1)}, u32[]{:S(2)}, u32[]{:S(2)}) async-start(bf16[16,304,512]{2,1,0:T(8,128)(2,1)} %shard_map.95), calls=%async_computation | async-start | bytes 9961472 | tf_op jit(solution)/shard_map/all_to_all | solution.py:412
  49.3 108.2 %all-gather.3.cloned.1.call-done = bf16[1024,1024]{1,0:T(8,128)(2,1)} async-done(((bf16[256,1024]{1,0:T(8,128)(2,1)}), bf16[1024,1024]{1,0:T(8,128)(2,1)}) %all-gather.3.cloned.1.call-update) | async-done | bytes 2097168 | tf_op jit(solution)/shard_map/all_gather | solution.py:74
  180.3 1.2 collective-permute-start.9
  181.6 36.6 %collective-permute-done.4.refs_1_.mine = bf16[4,256,1024]{2,1,0:T(8,128)(2,1)S(1)} collective-permute-done((bf16[4,256,1024]{2,1,0:T(8,128)(2,1)}, bf16[4,256,1024]{2,1,0:T(8,128)(2,1)S(1)}, u32[]{:S(2)}, u32[]{:S(2)}) %collective-permute-start.4) | collective-permute-done | bytes 2097184 | tf_op jit(solution)/shard_map/ppermute | solution.py:77
  218.2 1.2 collective-permute-start.6
  219.5 1.3 select_select_fusion
  220.8 2.0 pad_maximum_fusion.down
  223.6 3.7 collective-permute-done.9.theirs
  227.4 2.3 collective-permute-start.10
  229.6 42.7 %collective-permute-done.6.theirs = bf16[4,256,1024]{2,1,0:T(8,128)(2,1)} collective-permute-done((bf16[4,256,1024]{2,1,0:T(8,128)(2,1)S(1)}, bf16[4,256,1024]{2,1,0:T(8,128)(2,1)}, u32[]{:S(2)}, u32[]{:S(2)}) %collective-permute-start.6) | collective-permute-done | bytes 2097184 | tf_op jit(solution)/shard_map/ppermute | solution.py:80
  272.3 1.3 collective-permute-start.7
  273.6 1.4 fusion.37
  276.4 8.8 %shard_map.97.refs_1_ = f32[256,384]{1,0:T(8,128)} custom-call(bf16[16,304,512]{2,1,0:T(8,128)(2,1)} %all-to-all-done.act.maps, bf16[16,304,512]{2,1,0:T(8,128)(2,1)} %all-to-all-done.act.maps, s32[1,3072]{1,0:T(1,128)} %reshape.314.rows.refs_0_, s32[1,3072]{1,0:T(1,128)} %shard_map.96.spots, s32[32,1]{1,0:T(8,128)} %copy.40.starts), custom_call_target="tpu_custom_call" | custom-call | flops 2415919104 | bytes 3145728 | tf_op jit(solution)/shard_map/pallas_call | solution.py:447
  285.2 1.9 copy.43
  287.7 1.2 fusion.41
  289.0 1.0 fusion.13
  291.5 14.3 %all-to-all-start.1 = ((bf16[16,24,256]{2,1,0:T(8,128)(2,1)}), bf16[16,24,256]{2,1,0:T(8,128)(2,1)S(1)}, u32[]{:S(2)}, u32[]{:S(2)}) async-start(bf16[16,24,256]{2,1,0:T(8,128)(2,1)} %broadcast_in_dim.115), calls=%async_computation.1 | async-start | bytes 393216 | tf_op jit(solution)/shard_map/all_to_all | solution.py:27
  305.8 2.2 convolution_convert_fusion.1
  308.0 2.2 convolution_convert_fusion
  310.3 3.9 all-to-all-done.1
  314.8 4.1 %all-to-all-start.3 = ((f32[16,24,256]{2,1,0:T(8,128)}), f32[16,24,256]{2,1,0:T(8,128)S(1)}, u32[]{:S(2)}, u32[]{:S(2)}) async-start(f32[16,24,256]{2,1,0:T(8,128)} %bitcast.96), calls=%async_computation.3 | async-start | bytes 786432 | tf_op jit(solution)/shard_map/all_to_all | solution.py:451
  318.9 1.6 convolution_convert_fusion.2
  320.5 1.5 copy.37.refs_0_
  321.9 2.1 pad_maximum_fusion.2.cot
  324.0 1.7 copy.39
  325.7 7.0 %shard_map.99.refs_1_ = bf16[768,512]{1,0:T(8,128)(2,1)} custom-call(bf16[16,304,512]{2,1,0:T(8,128)(2,1)} %all-to-all-done.act.maps, bf16[256,384]{1,0:T(8,128)(2,1)} %bitcast.100, s32[1,3072]{1,0:T(1,128)} %shard_map.98.rows, s32[1,3072]{1,0:T(1,128)} %shard_map.96.spots, s32[32,1]{1,0:T(8,128)} %copy.40.starts), custom_call_target="tpu_custom_call" | custom-call | flops 2415919104 | bytes 3145728 | tf_op jit(solution)/shard_map/pallas_call | solution.py:449
  332.7 7.1 %shard_map.101.rest_0_ = bf16[384,8192]{1,0:T(8,128)(2,1)} custom-call(s32[2]{0:T(128)} %pad_add_fusion.3.where, bf16[384,1024]{1,0:T(8,128)(2,1)} %pad_maximum_fusion.2.cot, bf16[384,16]{1,0:T(8,128)(2,1)} %shard_map.100.grad, bf16[48,8192]{1,0:T(8,128)(2,1)} %pad_maximum_fusion.down, bf16[4,256,1024]{2,1,0:T(8,128)(2,1)} %bitcast.22.mine, ...), custom_call_target="tpu_custom_call" | custom-call | flops 1610612736 | bytes 5767168 | tf_op jit(solution)/shard_map/pallas_call | solution.py:136
  339.8 7.1 %shard_map.102.rest_0_ = bf16[384,8192]{1,0:T(8,128)(2,1)} custom-call(s32[2]{0:T(128)} %pad_add_fusion.2.where, bf16[384,1024]{1,0:T(8,128)(2,1)} %pad_maximum_fusion.2.cot, bf16[384,16]{1,0:T(8,128)(2,1)} %shard_map.100.grad, bf16[48,8192]{1,0:T(8,128)(2,1)} %pad_maximum_fusion.down, ...), custom_call_target="tpu_custom_call", output_to_operand_aliasing={{}: (6, {})} | custom-call | flops 1610612736 | bytes 5767168 | tf_op jit(solution)/shard_map/pallas_call | solution.py:136
  347.7 6.1 %all-to-all-start.2 = ((bf16[16,48,512]{2,1,0:T(8,128)(2,1)}), bf16[16,48,512]{2,1,0:T(8,128)(2,1)}, u32[]{:S(2)}, u32[]{:S(2)}) async-start(bf16[16,48,512]{2,1,0:T(8,128)(2,1)} %bitcast.95), calls=%async_computation.2 | async-start | bytes 1572864 | tf_op jit(solution)/shard_map/all_to_all | solution.py:454
  353.8 7.3 %shard_map.103.rest_0_ = bf16[384,8192]{1,0:T(8,128)(2,1)} custom-call(s32[2]{0:T(128)} %pad_add_fusion.1.where, bf16[384,1024]{1,0:T(8,128)(2,1)} %pad_maximum_fusion.2.cot, bf16[384,16]{1,0:T(8,128)(2,1)} %shard_map.100.grad, bf16[48,8192]{1,0:T(8,128)(2,1)} %pad_maximum_fusion.down, ...), custom_call_target="tpu_custom_call", output_to_operand_aliasing={{}: (6, {})} | custom-call | flops 1610612736 | bytes 5767168 | tf_op jit(solution)/shard_map/pallas_call | solution.py:136
  361.1 1.0 reduce_sum.19
  362.9 1.7 copy.44
  364.6 1.0 reshape.311
  365.5 1.2 fusion.33
  367.6 1.9 select_add_fusion.1
  369.6 4.3 %collective-permute-start.12 = (f32[16,1024]{1,0:T(8,128)S(1)}, f32[16,1024]{1,0:T(8,128)S(1)}, u32[]{:S(2)}, u32[]{:S(2)}) collective-permute-start(f32[16,1024]{1,0:T(8,128)S(1)} %get-tuple-element.10), channel_id=1, source_target_pairs={{0,14},{1,15},{2,0},{3,1},{4,2},{5,3},{6,4},{7,5},{8,6},{9,7},{10,... | collective-permute-start | bytes 196616 | tf_op jit(solution)/shard_map/ppermute | solution.py:21
  373.9 1.7 collective-permute-start.13
  375.9 7.1 %shard_map.104 = bf16[384,8192]{1,0:T(8,128)(2,1)} custom-call(s32[2]{0:T(128)} %pad_add_fusion.where, bf16[384,1024]{1,0:T(8,128)(2,1)} %pad_maximum_fusion.2.cot, bf16[384,16]{1,0:T(8,128)(2,1)} %shard_map.100.grad, bf16[48,8192]{1,0:T(8,128)(2,1)} %pad_maximum_fusion.down, ...), custom_call_target="tpu_custom_call", output_to_operand_aliasing={{}: (6, {})} | custom-call | flops 1610612736 | bytes 5767168 | tf_op jit(solution)/shard_map/pallas_call | solution.py:136
  383.9 1.3 convert_bitcast_fusion
  386.1 1.4 reshape.313
  (92 shorter events, 19.6 us)
Async XLA Ops:
  7.2 41.3 %copy-start = (bf16[512,1024]{1,0:T(8,128)(2,1)S(1)}, bf16[512,1024]{1,0:T(8,128)(2,1)}, u32[]{:S(2)}) copy-start(bf16[512,1024]{1,0:T(8,128)(2,1)} %param.11) | copy-start | bytes 3145732
  7.2 18.2 %copy-start.13 = (s32[192]{0:T(256)S(1)}, s32[192]{0:T(256)}, u32[]{:S(2)}) copy-start(s32[192]{0:T(256)} %param.9) | copy-start | bytes 2308
  14.3 24.3 %copy-start.2 = (bf16[3,16,9216]{2,1,0:T(8,128)(2,1)}, bf16[3,16,9216]{2,1,0:T(8,128)(2,1)S(1)}, u32[]{:S(2)}) copy-start(bf16[3,16,9216]{2,1,0:T(8,128)(2,1)S(1)} %constant_dynamic-update-slice_fusion) | copy-start | bytes 2654212
  14.3 17.1 %collective-permute-start = (bf16[16,9216]{1,0:T(8,128)(2,1)S(1)}, bf16[16,9216]{1,0:T(8,128)(2,1)S(1)}, u32[]{:S(2)}, u32[]{:S(2)}) collective-permute-start(bf16[16,9216]{1,0:T(8,128)(2,1)S(1)} %dynamic-slice_bitcast_fusion), channel_id=1, source_target_pairs={{0,4},{1,5},{2,6},{3,7},{4,8},{5,9},{6,10},{7,11},{8,12},{9,13},{1... | collective-permute-start | bytes 884744 | tf_op jit(solution)/shard_map/ppermute | solution.py:21
  16.5 17.6 %collective-permute-start.1 = (bf16[16,9216]{1,0:T(8,128)(2,1)S(1)}, bf16[16,9216]{1,0:T(8,128)(2,1)S(1)}, u32[]{:S(2)}, u32[]{:S(2)}) collective-permute-start(bf16[16,9216]{1,0:T(8,128)(2,1)S(1)} %dynamic-slice_bitcast_fusion), channel_id=1, source_target_pairs={{0,3},{1,4},{2,5},{3,6},{4,7},{5,8},{6,9},{7,10},{8,11},{9,12},{10... | collective-permute-start | bytes 884744 | tf_op jit(solution)/shard_map/ppermute | solution.py:21
  18.6 19.9 %collective-permute-start.2 = (bf16[16,9216]{1,0:T(8,128)(2,1)S(1)}, bf16[16,9216]{1,0:T(8,128)(2,1)S(1)}, u32[]{:S(2)}, u32[]{:S(2)}) collective-permute-start(bf16[16,9216]{1,0:T(8,128)(2,1)S(1)} %dynamic-slice_bitcast_fusion), channel_id=1, source_target_pairs={{0,2},{1,3},{2,4},{3,5},{4,6},{5,7},{6,8},{7,9},{8,10},{9,11},{10,... | collective-permute-start | bytes 884744 | tf_op jit(solution)/shard_map/ppermute | solution.py:21
  19.8 18.7 %collective-permute-start.3 = (bf16[16,9216]{1,0:T(8,128)(2,1)S(1)}, bf16[16,9216]{1,0:T(8,128)(2,1)S(1)}, u32[]{:S(2)}, u32[]{:S(2)}) collective-permute-start(bf16[16,9216]{1,0:T(8,128)(2,1)S(1)} %dynamic-slice_bitcast_fusion), channel_id=1, source_target_pairs={{0,1},{1,2},{2,3},{3,4},{4,5},{5,6},{6,7},{7,8},{8,9},{9,10},{10,1... | collective-permute-start | bytes 884744 | tf_op jit(solution)/shard_map/ppermute | solution.py:21
  39.4 234.2 %all-to-all-start = ((bf16[16,304,512]{2,1,0:T(8,128)(2,1)}), bf16[16,304,512]{2,1,0:T(8,128)(2,1)}, u32[]{:S(2)}, u32[]{:S(2)}) async-start(bf16[16,304,512]{2,1,0:T(8,128)(2,1)} %shard_map.95), calls=%async_computation | async-start | bytes 9961472 | tf_op jit(solution)/shard_map/all_to_all | solution.py:412
  48.4 109.1 %all-gather.3.cloned.1.call-start = ((), (), s32[]{:S(2)}) async-start(), calls=%async_computation.4 | async-start | bytes 2621440 | tf_op jit(solution)/shard_map/all_gather | solution.py:74
  157.5 60.7 %collective-permute-start.4 = (bf16[4,256,1024]{2,1,0:T(8,128)(2,1)}, bf16[4,256,1024]{2,1,0:T(8,128)(2,1)S(1)}, u32[]{:S(2)}, u32[]{:S(2)}) collective-permute-start(bf16[4,256,1024]{2,1,0:T(8,128)(2,1)} %bitcast.22.mine), channel_id=1, source_target_pairs={{0,2},{1,3},{2,0},{3,1},{4,6},{5,7},{6,4},{7,5},{8,10},{9,11},{10,... | collective-permute-start | bytes 6291464 | tf_op jit(solution)/shard_map/ppermute | solution.py:77
  177.8 112.2 %copy-start.12 = (s32[48]{0:T(128)}, s32[48]{0:T(128)S(1)}, u32[]{:S(2)}) copy-start(s32[48]{0:T(128)S(1)} %and_select_fusion) | copy-start | bytes 580
  180.3 47.0 %collective-permute-start.9 = (bf16[4,256,1024]{2,1,0:T(8,128)(2,1)}, bf16[4,256,1024]{2,1,0:T(8,128)(2,1)}, u32[]{:S(2)}, u32[]{:S(2)}) collective-permute-start(bf16[4,256,1024]{2,1,0:T(8,128)(2,1)} %bitcast.22.mine), channel_id=1, source_target_pairs={{0,16},{16,0},{1,17},{17,1},{2,18},{18,2},{3,19},{19,3},{4,20},{20... | collective-permute-start | bytes 6291464 | tf_op jit(solution)/shard_map/ppermute | solution.py:80
  218.2 58.2 %copy-start.1 = (bf16[4,256,1024]{2,1,0:T(8,128)(2,1)}, bf16[4,256,1024]{2,1,0:T(8,128)(2,1)S(1)}, u32[]{:S(2)}) copy-start(bf16[4,256,1024]{2,1,0:T(8,128)(2,1)S(1)} %collective-permute-done.4.refs_1_.mine) | copy-start | bytes 6291460
  218.2 54.1 %collective-permute-start.6 = (bf16[4,256,1024]{2,1,0:T(8,128)(2,1)S(1)}, bf16[4,256,1024]{2,1,0:T(8,128)(2,1)}, u32[]{:S(2)}, u32[]{:S(2)}) collective-permute-start(bf16[4,256,1024]{2,1,0:T(8,128)(2,1)S(1)} %collective-permute-done.4.refs_1_.mine), channel_id=1, source_target_pairs={{0,16},{16,0},{1,17},{17,1},{2,18},{18,2},{3,19},{19,3},{4,20},{20... | collective-permute-start | bytes 6291464 | tf_op jit(solution)/shard_map/ppermute | solution.py:80
  220.8 51.6 %copy-start.3 = (bf16[16,9216]{1,0:T(8,128)(2,1)}, bf16[16,9216]{1,0:T(8,128)(2,1)S(1)}, u32[]{:S(2)}) copy-start(bf16[16,9216]{1,0:T(8,128)(2,1)S(1)} %get-tuple-element.28) | copy-start | bytes 884740
  222.8 117.0 %collective-permute-start.8 = (bf16[4,256,1024]{2,1,0:T(8,128)(2,1)}, bf16[4,256,1024]{2,1,0:T(8,128)(2,1)}, u32[]{:S(2)}, u32[]{:S(2)}) collective-permute-start(bf16[4,256,1024]{2,1,0:T(8,128)(2,1)} %bitcast.22.mine), channel_id=1, source_target_pairs={{0,1},{1,0},{2,3},{3,2},{4,5},{5,4},{6,7},{7,6},{8,9},{9,8},{10,11... | collective-permute-start | bytes 6291464 | tf_op jit(solution)/shard_map/ppermute | solution.py:77
  223.6 152.0 %collective-permute-start.5 = (bf16[4,256,1024]{2,1,0:T(8,128)(2,1)S(1)}, bf16[4,256,1024]{2,1,0:T(8,128)(2,1)}, u32[]{:S(2)}, u32[]{:S(2)}) collective-permute-start(bf16[4,256,1024]{2,1,0:T(8,128)(2,1)S(1)} %collective-permute-done.4.refs_1_.mine), channel_id=1, source_target_pairs={{0,1},{1,0},{2,3},{3,2},{4,5},{5,4},{6,7},{7,6},{8,9},{9,8},{10,11... | collective-permute-start | bytes 6291464 | tf_op jit(solution)/shard_map/ppermute | solution.py:77
  227.4 112.5 %collective-permute-start.10 = (bf16[4,256,1024]{2,1,0:T(8,128)(2,1)}, bf16[4,256,1024]{2,1,0:T(8,128)(2,1)}, u32[]{:S(2)}, u32[]{:S(2)}) collective-permute-start(bf16[4,256,1024]{2,1,0:T(8,128)(2,1)} %collective-permute-done.9.theirs), channel_id=1, source_target_pairs={{0,1},{1,0},{2,3},{3,2},{4,5},{5,4},{6,7},{7,6},{8,9},{9,8},{10,11... | collective-permute-start | bytes 6291464 | tf_op jit(solution)/shard_map/ppermute | solution.py:77
  272.3 103.6 %collective-permute-start.7 = (bf16[4,256,1024]{2,1,0:T(8,128)(2,1)}, bf16[4,256,1024]{2,1,0:T(8,128)(2,1)}, u32[]{:S(2)}, u32[]{:S(2)}) collective-permute-start(bf16[4,256,1024]{2,1,0:T(8,128)(2,1)} %collective-permute-done.6.theirs), channel_id=1, source_target_pairs={{0,1},{1,0},{2,3},{3,2},{4,5},{5,4},{6,7},{7,6},{8,9},{9,8},{10,11... | collective-permute-start | bytes 6291464 | tf_op jit(solution)/shard_map/ppermute | solution.py:77
  287.7 20.4 %copy-start.11 = (s32[384]{0:T(512)}, s32[384]{0:T(512)S(1)}, u32[]{:S(2)}) copy-start(s32[384]{0:T(512)S(1)} %sub.76) | copy-start | bytes 4612
  287.7 2.4 copy-start.4
  287.7 2.4 copy-start.5
  288.9 1.4 copy-start.6
  289.0 1.4 copy-start.8
  291.5 22.6 %all-to-all-start.1 = ((bf16[16,24,256]{2,1,0:T(8,128)(2,1)}), bf16[16,24,256]{2,1,0:T(8,128)(2,1)S(1)}, u32[]{:S(2)}, u32[]{:S(2)}) async-start(bf16[16,24,256]{2,1,0:T(8,128)(2,1)} %broadcast_in_dim.115), calls=%async_computation.1 | async-start | bytes 393216 | tf_op jit(solution)/shard_map/all_to_all | solution.py:27
  314.1 0.7 copy-start.10
  314.8 32.2 %all-to-all-start.3 = ((f32[16,24,256]{2,1,0:T(8,128)}), f32[16,24,256]{2,1,0:T(8,128)S(1)}, u32[]{:S(2)}, u32[]{:S(2)}) async-start(f32[16,24,256]{2,1,0:T(8,128)} %bitcast.96), calls=%async_computation.3 | async-start | bytes 786432 | tf_op jit(solution)/shard_map/all_to_all | solution.py:451
  347.0 0.8 copy-start.9
  347.7 36.1 %all-to-all-start.2 = ((bf16[16,48,512]{2,1,0:T(8,128)(2,1)}), bf16[16,48,512]{2,1,0:T(8,128)(2,1)}, u32[]{:S(2)}, u32[]{:S(2)}) async-start(bf16[16,48,512]{2,1,0:T(8,128)(2,1)} %bitcast.95), calls=%async_computation.2 | async-start | bytes 1572864 | tf_op jit(solution)/shard_map/all_to_all | solution.py:454
  353.8 12.9 %copy-start.7 = (bf16[16,24,512]{2,1,0:T(8,128)(2,1)S(1)}, bf16[16,24,512]{2,1,0:T(8,128)(2,1)}, u32[]{:S(2)}) copy-start(bf16[16,24,512]{2,1,0:T(8,128)(2,1)} %copy-done.6) | copy-start | bytes 1179652
  369.4 13.6 %collective-permute-start.11 = (f32[16,1024]{1,0:T(8,128)S(1)}, f32[16,1024]{1,0:T(8,128)S(1)}, u32[]{:S(2)}, u32[]{:S(2)}) collective-permute-start(f32[16,1024]{1,0:T(8,128)S(1)} %get-tuple-element.10), channel_id=1, source_target_pairs={{0,15},{1,0},{2,1},{3,2},{4,3},{5,4},{6,5},{7,6},{8,7},{9,8},{10,9... | collective-permute-start | bytes 196616 | tf_op jit(solution)/shard_map/ppermute | solution.py:21
  369.6 13.4 %collective-permute-start.12 = (f32[16,1024]{1,0:T(8,128)S(1)}, f32[16,1024]{1,0:T(8,128)S(1)}, u32[]{:S(2)}, u32[]{:S(2)}) collective-permute-start(f32[16,1024]{1,0:T(8,128)S(1)} %get-tuple-element.10), channel_id=1, source_target_pairs={{0,14},{1,15},{2,0},{3,1},{4,2},{5,3},{6,4},{7,5},{8,6},{9,7},{10,... | collective-permute-start | bytes 196616 | tf_op jit(solution)/shard_map/ppermute | solution.py:21
  373.9 9.1 %collective-permute-start.13 = (f32[16,1024]{1,0:T(8,128)S(1)}, f32[16,1024]{1,0:T(8,128)S(1)}, u32[]{:S(2)}, u32[]{:S(2)}) collective-permute-start(f32[16,1024]{1,0:T(8,128)S(1)} %get-tuple-element.10), channel_id=1, source_target_pairs={{0,13},{1,14},{2,15},{3,0},{4,1},{5,2},{6,3},{7,4},{8,5},{9,6},{10... | collective-permute-start | bytes 196616 | tf_op jit(solution)/shard_map/ppermute | solution.py:21
  375.6 7.5 %collective-permute-start.14 = (f32[16,1024]{1,0:T(8,128)S(1)}, f32[16,1024]{1,0:T(8,128)S(1)}, u32[]{:S(2)}, u32[]{:S(2)}) collective-permute-start(f32[16,1024]{1,0:T(8,128)S(1)} %get-tuple-element.10), channel_id=1, source_target_pairs={{0,12},{1,13},{2,14},{3,15},{4,0},{5,1},{6,2},{7,3},{8,4},{9,5},{1... | collective-permute-start | bytes 196616 | tf_op jit(solution)/shard_map/ppermute | solution.py:21
Sparse Core Ops, SparseCore 0:
  50.8 106.6 all-gather.2

commit v8 on v7

--- a/solution.py
+++ b/solution.py
@@ -36,6 +36,7 @@
         out_shape=jax.ShapeDtypeStruct(value.shape, value.dtype),
         input_output_aliases={0: 0},
         cost_estimate=pl.CostEstimate(flops=0, bytes_accessed=0, transcendentals=0),
+        compiler_params=pltpu.CompilerParams(vmem_limit_bytes=VMEM),
     )(value, *others)
 
 
@@ -89,7 +90,8 @@
 
 
 def quarter_kernel(where, cot, grad, down, mine, theirs, *rest):
-    out = rest[-1]
+    out, token = rest[-2:]
+    token[...] = jnp.zeros_like(token)
     rank = grad.shape[1]
     half = mine.shape[1]
     lora = [
@@ -139,9 +141,15 @@
             num_scalar_prefetch=1,
             grid=(shards,),
             in_specs=specs,
-            out_specs=pl.BlockSpec((rows, 2 * half), lambda j, where: (0, 4 * j + where[0])),
+            out_specs=[
+                pl.BlockSpec((rows, 2 * half), lambda j, where: (0, 4 * j + where[0])),
+                pl.BlockSpec((8, LANES), lambda j, where: (0, 0)),
+            ],
         ),
-        out_shape=jax.ShapeDtypeStruct((rows, width), jnp.bfloat16),
+        out_shape=[
+            jax.ShapeDtypeStruct((rows, width), jnp.bfloat16),
+            jax.ShapeDtypeStruct((8, LANES), jnp.float32),
+        ],
         input_output_aliases=alias,
         cost_estimate=pl.CostEstimate(
             flops=4 * rows * depth * half * shards,
@@ -162,74 +170,50 @@
     return weight.reshape(-1, depth)
 
 
-def pack_kernel(rows, act, maps, cot, out, place, digits):
-    targets, packed, features = out.shape
-    tokens, shared = act.shape[0], maps.shape[0]
-    cap = shared * features // cot.shape[1]
-    devices = targets * pl.num_programs(0)
-    step = pl.program_id(0)
-
-    @pl.when(step == 0)
-    def _():
-        target = rows[...] // (cap * devices)
-        to = lax.broadcasted_iota(jnp.int32, (16, features), 0) == target
-        first = lax.broadcasted_iota(jnp.int32, (features, features), 0)
-        later = lax.broadcasted_iota(jnp.int32, (features, features), 1)
-        earlier = jnp.where(first < later, 1.0, 0.0).astype(jnp.bfloat16)
-        ahead = dot(jnp.where(to, 1.0, 0.0).astype(jnp.bfloat16), earlier, ((1,), (0,)))
-        ahead = jnp.sum(jnp.where(to, ahead, 0.0), axis=0, keepdims=True)
-        place[...] = target * cap + ahead.astype(jnp.int32)
-        which = lax.broadcasted_iota(jnp.int32, (16, features), 0)
-        values = jnp.zeros((16, features), jnp.int32)
-        for k, digit in enumerate(as_digits(rows[...], place[...])):
-            values = jnp.where(which == k, digit, values)
-        digits[...] = values.astype(jnp.float32).astype(out.dtype)
-
-    index = lax.broadcasted_iota(jnp.int32, (targets * cap, tokens), 0) + step * targets * cap
-    send = jnp.where(index == place[:, :tokens], 1.0, 0.0).astype(jnp.bfloat16)
-    sent = dot(send, cot[...], ((1,), (0,)))
-    for k in range(targets):
-        part = slice(k * features, (k + 1) * features)
-        some = sent[k * cap : (k + 1) * cap]
-        folds = [some[:, f : f + features] for f in range(0, cot.shape[1], features)]
-        out[k, :tokens, :] = act[:, part]
-        out[k, tokens : tokens + shared, :] = maps[:, part]
-        out[k, tokens + shared : tokens + 2 * shared, :] = jnp.concatenate(
-            folds, axis=0
-        ).astype(out.dtype)
-        out[k, tokens + 2 * shared :, :] = digits[...]
-
-
-def pack(rows, act, maps, cot, devices, cap):
-    tokens, width = act.shape
-    features = width // devices
-    shared = maps.shape[0]
-    total = tokens + 2 * shared + 16
-    targets = 4
+def rows_kernel(rows, cot, out, place):
+    devices, packed, features = out.shape
+    shared = packed - 16
+    folds = cot.shape[1] // features
+    cap = shared // folds
+    target = rows[...] // (cap * devices)
+    to = lax.broadcasted_iota(jnp.int32, (16, features), 0) == target
+    first = lax.broadcasted_iota(jnp.int32, (features, features), 0)
+    later = lax.broadcasted_iota(jnp.int32, (features, features), 1)
+    earlier = jnp.where(first < later, 1.0, 0.0).astype(jnp.bfloat16)
+    ahead = dot(jnp.where(to, 1.0, 0.0).astype(jnp.bfloat16), earlier, ((1,), (0,)))
+    ahead = jnp.sum(jnp.where(to, ahead, 0.0), axis=0, keepdims=True)
+    place[...] = target * cap + ahead.astype(jnp.int32)
+    which = lax.broadcasted_iota(jnp.int32, (16, features), 0)
+    digits = jnp.zeros((16, features), jnp.int32)
+    for k, digit in enumerate(as_digits(rows[...], place[...])):
+        digits = jnp.where(which == k, digit, digits)
+    digits = digits.astype(jnp.float32).astype(out.dtype)
+    send = placing(place[:, : cot.shape[0]], cap * devices)
+    for f in range(folds):
+        sent = dot(send, cot[:, f * features : (f + 1) * features], ((1,), (0,)))
+        for k in range(devices):
+            some = sent[k * cap : (k + 1) * cap].astype(out.dtype)
+            out[k, f * cap : (f + 1) * cap, :] = some
+    for k in range(devices):
+        out[k, shared:, :] = digits
+
+
+def pack_rows(rows, cot, devices, cap, features):
+    tokens = rows.shape[0]
+    folds = cot.shape[1] // features
     if features % LANES == 0 and cap % 8 == 0 and features >= tokens and devices <= 16:
         padding = jnp.full((features - tokens,), 16 * cap * devices, jnp.int32)
         return pl.pallas_call(
-            pack_kernel,
-            grid=(devices // targets,),
-            in_specs=[
-                pl.BlockSpec((1, features), lambda j: (0, 0)),
-                pl.BlockSpec((tokens, targets * features), lambda j: (0, j)),
-                pl.BlockSpec((shared, targets * features), lambda j: (0, j)),
-                pl.BlockSpec(cot.shape, lambda j: (0, 0)),
-            ],
-            out_specs=pl.BlockSpec((targets, total, features), lambda j: (j, 0, 0)),
-            out_shape=jax.ShapeDtypeStruct((devices, total, features), act.dtype),
-            scratch_shapes=[
-                pltpu.VMEM((1, features), jnp.int32),
-                pltpu.VMEM((16, features), act.dtype),
-            ],
+            rows_kernel,
+            out_shape=jax.ShapeDtypeStruct((devices, folds * cap + 16, features), cot.dtype),
+            scratch_shapes=[pltpu.VMEM((1, features), jnp.int32)],
             cost_estimate=pl.CostEstimate(
                 flops=2 * devices * cap * tokens * cot.shape[1],
-                bytes_accessed=4 * devices * total * features,
+                bytes_accessed=6 * cot.size,
                 transcendentals=0,
             ),
             compiler_params=pltpu.CompilerParams(vmem_limit_bytes=VMEM),
-        )(jnp.concatenate([rows, padding])[None], act, maps, cot)
+        )(jnp.concatenate([rows, padding])[None], cot)
     target = rows // (cap * devices)
     order = jnp.arange(tokens, dtype=jnp.int32)
     before = (target[:, None] == target[None, :]) & (order[None, :] < order[:, None])
@@ -240,13 +224,42 @@
     digits = jnp.stack(as_digits(rows, place)).astype(jnp.bfloat16)
     digits = jnp.pad(digits, ((0, 0), (0, -tokens % features))).reshape(-1, features)
     digits = jnp.pad(digits, ((0, -digits.shape[0] % 16), (0, 0)))
-    parts = [
-        act.reshape(tokens, devices, features).transpose(1, 0, 2),
-        maps.reshape(shared, devices, features).transpose(1, 0, 2),
-    ]
-    parts += [sent[:, :, k : k + features] for k in range(0, cot.shape[1], features)]
+    parts = [sent[:, :, k : k + features] for k in range(0, cot.shape[1], features)]
     parts += [jnp.broadcast_to(digits[None], (devices,) + digits.shape)]
     return jnp.concatenate(parts, axis=1)
+
+
+def features_kernel(act, maps, out):
+    targets, _, features = out.shape
+    tokens = act.shape[0]
+    for k in range(targets):
+        part = slice(k * features, (k + 1) * features)
+        out[k, :tokens, :] = act[:, part]
+        out[k, tokens:, :] = maps[:, part]
+
+
+def pack_features(act, maps, devices):
+    tokens, width = act.shape
+    features = width // devices
+    shared = maps.shape[0]
+    targets = 4
+    if features % LANES == 0:
+        return pl.pallas_call(
+            features_kernel,
+            grid=(devices // targets,),
+            in_specs=[
+                pl.BlockSpec((tokens, targets * features), lambda j: (0, j)),
+                pl.BlockSpec((shared, targets * features), lambda j: (0, j)),
+            ],
+            out_specs=pl.BlockSpec((targets, tokens + shared, features), lambda j: (j, 0, 0)),
+            out_shape=jax.ShapeDtypeStruct((devices, tokens + shared, features), act.dtype),
+            cost_estimate=pl.CostEstimate(
+                flops=0, bytes_accessed=4 * (tokens + shared) * width, transcendentals=0
+            ),
+            compiler_params=pltpu.CompilerParams(vmem_limit_bytes=VMEM),
+        )(act, maps)
+    both = jnp.concatenate([act, maps], axis=0)
+    return both.reshape(tokens + shared, devices, features).transpose(1, 0, 2)
 
 
 def slot_chunks(width):
@@ -386,40 +399,45 @@
 
     pieces = weight_pieces(frozen_value_weight)
 
+    sent_rows = pack_rows(token_layout_row, cotangent, devices, cap, features)
+    got_rows = lax.all_to_all(sent_rows, "blk", split_axis=0, concat_axis=0)
+    recv_cot = [
+        got_rows[:, k * cap : (k + 1) * cap].reshape(resident_rows, features)
+        for k in range(out_width // features)
+    ]
+    per_digit = -(-tokens // features)
+    digits = got_rows[:, share : share + 5 * per_digit]
+    digits = digits.reshape(devices, 5, per_digit * features)[:, :, :tokens]
+    rows_all, place_all = from_digits(digits)
+
     first_block = device * resident
     block_numbers = first_block + jnp.arange(resident, dtype=jnp.int32)
     begin = starts_of(block_numbers, start_ids)
     is_local = (begin >= first_block) & (begin <= block_numbers)
     home_slot = jnp.clip(begin - first_block, 0, resident - 1)
-    both_maps = jnp.concatenate([adapter_down_maps, adapter_up_maps], axis=2)
-    last_map = lax.dynamic_index_in_dim(both_maps, home_slot[resident - 1], 0, keepdims=False)
+    last_map = jnp.concatenate(
+        [
+            lax.dynamic_index_in_dim(maps, home_slot[resident - 1], 0, keepdims=False)
+            for maps in (adapter_down_maps, adapter_up_maps)
+        ],
+        axis=1,
+    )
     carried = jnp.zeros_like(last_map)
     for step in range(1, HOPS + 1):
         home = (device - step) % devices
         carried = jnp.where(begin[0] // resident == home, moved(last_map, step), carried)
-    block_maps = []
-    for b in range(resident):
-        own = carried
-        for k in range(b + 1):
-            own = jnp.where(is_local[b] & (home_slot[b] == k), both_maps[k], own)
-        block_maps.append(own)
-    block_maps = jnp.concatenate(block_maps, axis=0)
-    down_blocks, up_blocks = block_maps[:, :width], block_maps[:, width:]
-
-    flat_maps = adapter_down_maps.reshape(share, width)
-    packed = pack(token_layout_row, activations, flat_maps, cotangent, devices, cap)
-    packed = after(packed, carried)
-    received = lax.all_to_all(packed, "blk", split_axis=0, concat_axis=0)
-    recv_cot = [
-        received[:, tokens + share + k * cap : tokens + share + (k + 1) * cap].reshape(
-            resident_rows, features
-        )
-        for k in range(out_width // features)
-    ]
-    per_digit = -(-tokens // features)
-    digits = received[:, tokens + 2 * share : tokens + 2 * share + 5 * per_digit]
-    digits = digits.reshape(devices, 5, per_digit * features)[:, :, :tokens]
-    rows_all, place_all = from_digits(digits)
+
+    def of_blocks(maps, own):
+        blocks = []
+        for b in range(resident):
+            chosen = own
+            for k in range(b + 1):
+                chosen = jnp.where(is_local[b] & (home_slot[b] == k), maps[k], chosen)
+            blocks.append(chosen)
+        return jnp.concatenate(blocks, axis=0)
+
+    down_blocks = of_blocks(adapter_down_maps, carried[:, :width])
+    up_blocks = of_blocks(adapter_up_maps, carried[:, width:])
 
     spots = device * cap + jnp.arange(cap, dtype=jnp.int32)
     hit = place_all[:, None, :] == spots[None, :, None]
@@ -436,14 +454,47 @@
     grad_in = jnp.where(in_block, grad_in, 0.0).astype(jnp.bfloat16)
     grad_in = sum(grad_in[:, b * rank : (b + 1) * rank] for b in range(resident))
     grad_sent = grad_in.reshape(devices, cap, rank).transpose(1, 0, 2).reshape(cap, -1)
-    grad_all = to_all(grad_sent).reshape(resident_rows, -1).T
+    grad_all = to_all(after(grad_sent, pieces[0][0])).reshape(resident_rows, -1).T
+
+    flat_maps = adapter_down_maps.reshape(share, width)
+    received = after(pack_features(activations, flat_maps, devices), grad_all)
+    received = lax.all_to_all(received, "blk", split_axis=0, concat_axis=0)
+
+    rows_all, place_all = rows_all.reshape(1, -1), place_all.reshape(1, -1)
+
+    cot_rows = jnp.concatenate(
+        [dot(arrange, part, ((0,), (0,))).astype(jnp.bfloat16) for part in recv_cot], axis=1
+    )
+    grad_rows = dot(arrange, grad_in, ((0,), (0,))).astype(jnp.bfloat16)
+    group = lax.axis_index("groups")
+    quarter = device % 4
+    firsts = [quarter, quarter ^ 1, quarter ^ 2, quarter ^ 3]
+    if pieces[0][0].shape[1] % LANES == 0:
+        out = None
+        for number, (piece, first) in enumerate(zip(pieces, firsts)):
+            out, token = write_quarter(
+                piece, first, group, cot_rows, grad_rows, down_blocks, out
+            )
+            if number == 1:
+                place_all = after(place_all, token)
+    else:
+        weight = together(pieces, firsts, group)
+        lora = [
+            dot(
+                grad_rows[b * BLOCK : (b + 1) * BLOCK],
+                down_blocks[b * rank : (b + 1) * rank],
+                ((1,), (0,)),
+            )
+            for b in range(resident)
+        ]
+        lora = (adapter_scale * jnp.concatenate(lora, axis=0)).astype(jnp.bfloat16)
+        out = dot(cot_rows, weight, ((1,), (1,))) + lora.astype(jnp.float32)
+        out = out.astype(jnp.bfloat16)
 
     starts = start_ids[:, None]
     hidden_call, down_call = feature_calls(
         received, tokens, share, rank, resident_rows, starts.shape[0]
     )
-    rows_all, place_all = rows_all.reshape(1, -1), place_all.reshape(1, -1)
-    place_all = after(place_all, pieces[2][0])
     shares = hidden_call(received, received, rows_all, place_all, starts)
     rows_all = after(rows_all, shares)
     down_f = down_call(received, grad_all, rows_all, place_all, starts)
@@ -454,11 +505,6 @@
     down_home = lax.all_to_all(down_f, "blk", split_axis=0, concat_axis=1, tiled=True)
     down_map_gradient = down_home.astype(jnp.float32).reshape(resident, rank, width)
 
-    cot_rows = jnp.concatenate(
-        [dot(arrange, part, ((0,), (0,))).astype(jnp.bfloat16) for part in recv_cot], axis=1
-    )
-    grad_rows = dot(arrange, grad_in, ((0,), (0,))).astype(jnp.bfloat16)
-    grad_rows = after(grad_rows, down_f)
     wide = jnp.where(in_block, jnp.concatenate([hidden] * resident, axis=1), 0)
     up_all = [dot(wide, part, ((0,), (0,))) for part in recv_cot]
     up_all = jnp.concatenate(up_all, axis=1).reshape(resident, rank, out_width)
@@ -478,26 +524,6 @@
         up_grads.append(adapter_scale * total)
     up_map_gradient = jnp.stack(up_grads)
 
-    group = lax.axis_index("groups")
-    quarter = device % 4
-    firsts = [quarter, quarter ^ 1, quarter ^ 2, quarter ^ 3]
-    if pieces[0][0].shape[1] % LANES == 0:
-        out = None
-        for piece, first in zip(pieces, firsts):
-            out = write_quarter(piece, first, group, cot_rows, grad_rows, down_blocks, out)
-    else:
-        weight = together(pieces, firsts, group)
-        lora = [
-            dot(
-                grad_rows[b * BLOCK : (b + 1) * BLOCK],
-                down_blocks[b * rank : (b + 1) * rank],
-                ((1,), (0,)),
-            )
-            for b in range(resident)
-        ]
-        lora = (adapter_scale * jnp.concatenate(lora, axis=0)).astype(jnp.bfloat16)
-        out = dot(cot_rows, weight, ((1,), (1,))) + lora.astype(jnp.float32)
-        out = out.astype(jnp.bfloat16)
     return (out, down_map_gradient, up_map_gradient)
 
 

time: 397 us -> 349 us (0.88)
  waiting for transfers between devices: 202 us -> 173 us
  other arithmetic: 18 us -> 10.4 us
  matrix products: 9.35 us -> 2.92 us
  local copies, waits for them, and re-layouts: 22.3 us -> 15.9 us
    all_gather x1, waiting for transfers between devices: 108 us -> 11 us  [weight_pieces(): column = lax.all_gather(mine, 'blk', axis_index_groups=lines)]
    all_to_all x1 -> x2, waiting for transfers between devices: 0.01 us -> 35.2 us  [the longest x1 35.2 us: local(): got_rows = lax.all_to_all(sent_rows, 'blk', split_axis=0, concat_axis=0)]
    ppermute x2, waiting for transfers between devices: 46.4 us -> 81.4 us  [groups(): return lax.ppermute(piece, 'groups', [(0, 1), (1, 0)])]
    ppermute x8, waiting for transfers between devices: 7.19 us -> 0.02 us  [moved(): lax.ppermute(value, 'blk', [(i, (i + steps) % count) for i in range(count)])]
    dot_general x7, matrix products: 9.35 us -> 2.92 us  [dot(): lax.dot_general(a, b, (dims, ((), ())), preferred_element_type=jnp.float32)]
    ppermute x5, waiting for transfers between devices: 36.7 us -> 41.2 us  [over(): return lax.ppermute(piece, 'blk', [(i, i ^ bit) for i in range(count)])]
    all_to_all x1 -> x2, starting transfers between devices: 8.94 us -> 9.79 us  [the longest x1 5.15 us: local(): received = lax.all_to_all(received, 'blk', split_axis=0, concat_axis=0)]
  transfers between devices with their start and end apart: 20 -> 21, of which waited for: 7 -> 6; matrix products, arithmetic and copies ran while one was open for 10% -> 6% of each run, Pallas kernels for 13% -> 15%
where the time goes in v8:
time: 349 us; the launch traced here: 347 us
  waiting for transfers between devices  173 us (50%)
  starting transfers between devices  55.6 us (16%)
  Pallas kernels  51.2 us (15%)
  between operations  38.3 us (11%)
  local copies, waits for them, and re-layouts  15.9 us (5%)
  other arithmetic  10.4 us (3%)
    ppermute x2, waiting for transfers between devices, groups(): return lax.ppermute(piece, 'groups', [(0, 1), (1, 0)])  81.4 us
    ppermute x5, waiting for transfers between devices, over(): return lax.ppermute(piece, 'blk', [(i, i ^ bit) for i in range(count)])  41.2 us
    all_to_all x1, waiting for transfers between devices, local(): got_rows = lax.all_to_all(sent_rows, 'blk', split_axis=0, concat_axis=0)  35.2 us
    pallas_call x4, Pallas kernels, write_quarter(): pl.pallas_call(quarter_kernel, grid_spec=pltpu.PrefetchScalarGridSpec(num...  28.6 us
    all_to_all x1, starting transfers between devices, to_all(): return lax.all_to_all(copies, 'blk', split_axis=0, concat_axis=0)  13.2 us
    ppermute x8, starting transfers between devices, moved(): lax.ppermute(value, 'blk', [(i, (i + steps) % count) for i in range(count)])  12.9 us
    all_gather x1, waiting for transfers between devices, weight_pieces(): column = lax.all_gather(mine, 'blk', axis_index_groups=lines)  11 us
    pallas_call x1, Pallas kernels, local(): shares = hidden_call(received, received, rows_all, place_all, starts)  8.76 us
  transfers between devices with their start and end apart: 21, of which 6 were waited for; matrix products, arithmetic and copies ran while one was open for 6% of the time, Pallas kernels for 15%

profile of v8, /device:TPU:1, one launch (start us, length us, event | category | flops | bytes accessed | tf_op | source)
XLA Modules:
  0.0 347.0 jit_solution(10174392673849441879)
XLA Ops:
  7.2 1.5 fusion.20
  11.8 1.0 dynamic-slice_bitcast_fusion
  12.8 0.8 dynamic-slice_bitcast_fusion.1
  13.5 2.2 collective-permute-start
  15.7 2.1 collective-permute-start.1
  17.9 1.2 collective-permute-start.2
  19.1 0.9 collective-permute-start.3
  20.0 1.3 concatenate.21
  21.2 2.6 shard_map.94
  23.8 4.6 %all-to-all-start = ((bf16[16,64,512]{2,1,0:T(8,128)(2,1)}), bf16[16,64,512]{2,1,0:T(8,128)(2,1)S(1)}, u32[]{:S(2)}, u32[]{:S(2)}) async-start(bf16[16,64,512]{2,1,0:T(8,128)(2,1)} %shard_map.94), calls=%async_computation | async-start | bytes 2097152 | tf_op jit(solution)/shard_map/all_to_all | solution.py:403
  28.5 0.8 constant_dynamic-slice_fusion
  39.3 0.7 copy-done.2
  40.1 35.2 %all-to-all-done = bf16[16,64,512]{2,1,0:T(8,128)(2,1)S(1)} async-done(((bf16[16,64,512]{2,1,0:T(8,128)(2,1)}), bf16[16,64,512]{2,1,0:T(8,128)(2,1)S(1)}, u32[]{:S(2)}, u32[]{:S(2)}) %all-to-all-start) | async-done | bytes 1048608 | tf_op jit(solution)/shard_map/all_to_all | solution.py:403
  77.0 0.7 reshape.312.refs_0_
  77.8 11.0 %all-gather.3.cloned.1.call-done = bf16[1024,1024]{1,0:T(8,128)(2,1)} async-done(((bf16[256,1024]{1,0:T(8,128)(2,1)}), bf16[1024,1024]{1,0:T(8,128)(2,1)}) %all-gather.3.cloned.1.call-update) | async-done | bytes 2097168 | tf_op jit(solution)/shard_map/all_gather | solution.py:75
  88.8 1.4 broadcast_in_dim.113
  90.2 13.2 %all-to-all-start.1 = ((bf16[16,24,256]{2,1,0:T(8,128)(2,1)}), bf16[16,24,256]{2,1,0:T(8,128)(2,1)S(1)}, u32[]{:S(2)}, u32[]{:S(2)}) async-start(bf16[16,24,256]{2,1,0:T(8,128)(2,1)} %broadcast_in_dim.113), calls=%async_computation.1 | async-start | bytes 393216 | tf_op jit(solution)/shard_map/all_to_all | solution.py:27
  103.3 4.5 %shard_map.99.refs_0_ = bf16[16,240,512]{2,1,0:T(8,128)(2,1)} custom-call(bf16[192,8192]{1,0:T(8,128)(2,1)} %act.1, bf16[48,8192]{1,0:T(8,128)(2,1)} %bitcast.101), custom_call_target="tpu_custom_call" | custom-call | bytes 7864320 | tf_op jit(solution)/shard_map/pallas_call | solution.py:247
  107.9 3.8 %all-to-all-done.1 = bf16[16,24,256]{2,1,0:T(8,128)(2,1)S(1)} async-done(((bf16[16,24,256]{2,1,0:T(8,128)(2,1)}), bf16[16,24,256]{2,1,0:T(8,128)(2,1)S(1)}, u32[]{:S(2)}, u32[]{:S(2)}) %all-to-all-start.1) | async-done | bytes 196640 | tf_op jit(solution)/shard_map/all_to_all | solution.py:27
  111.7 0.8 copy.33
  112.5 5.2 %all-to-all-start.2 = ((bf16[16,240,512]{2,1,0:T(8,128)(2,1)}), bf16[16,240,512]{2,1,0:T(8,128)(2,1)}, u32[]{:S(2)}, u32[]{:S(2)}) async-start(bf16[16,240,512]{2,1,0:T(8,128)(2,1)} %shard_map.101), calls=%async_computation.2 | async-start | bytes 7864320 | tf_op jit(solution)/shard_map/all_to_all | solution.py:461
  117.6 1.2 collective-permute-start.9
  118.9 1.4 collective-permute-start.4
  122.2 0.9 collective-permute-start.8
  123.1 41.7 %collective-permute-done.9.theirs = bf16[4,256,1024]{2,1,0:T(8,128)(2,1)} collective-permute-done((bf16[4,256,1024]{2,1,0:T(8,128)(2,1)}, bf16[4,256,1024]{2,1,0:T(8,128)(2,1)}, u32[]{:S(2)}, u32[]{:S(2)}) %collective-permute-start.9) | collective-permute-done | bytes 2097184 | tf_op jit(solution)/shard_map/ppermute | solution.py:81
  164.8 1.2 collective-permute-start.10
  166.0 41.2 %collective-permute-done.4.mine = bf16[4,256,1024]{2,1,0:T(8,128)(2,1)} collective-permute-done((bf16[4,256,1024]{2,1,0:T(8,128)(2,1)}, bf16[4,256,1024]{2,1,0:T(8,128)(2,1)}, u32[]{:S(2)}, u32[]{:S(2)}) %collective-permute-start.4) | collective-permute-done | bytes 2097184 | tf_op jit(solution)/shard_map/ppermute | solution.py:78
  207.2 1.2 collective-permute-start.6
  208.5 1.0 pad_maximum_fusion.1.down
  210.9 1.0 convolution_convert_fusion.2.grad
  212.8 1.2 collective-permute-start.5
  214.1 39.7 %collective-permute-done.6.theirs = bf16[4,256,1024]{2,1,0:T(8,128)(2,1)} collective-permute-done((bf16[4,256,1024]{2,1,0:T(8,128)(2,1)}, bf16[4,256,1024]{2,1,0:T(8,128)(2,1)}, u32[]{:S(2)}, u32[]{:S(2)}) %collective-permute-start.6) | collective-permute-done | bytes 2097184 | tf_op jit(solution)/shard_map/ppermute | solution.py:81
  253.8 1.8 collective-permute-start.7
  255.5 1.0 pad_maximum_fusion.cot
  256.5 7.1 %shard_map.95 = (bf16[384,8192]{1,0:T(8,128)(2,1)}, f32[8,128]{1,0:T(8,128)}) custom-call(s32[2]{0:T(128)} %pad_add_fusion.3.where, bf16[384,1024]{1,0:T(8,128)(2,1)} %pad_maximum_fusion.cot, bf16[384,16]{1,0:T(8,128)(2,1)} %convolution_convert_fusion.2.grad, bf16[48,8192]{1,0:T(8,128)(2,1)} %pad_maximum_fusion.1.down, bf16[4,256,1024]{2,1,0:T(8,128)(2,1)} %bitcast.112, ...), custom_call_target="tpu_custom_call" | custom-call | flops 1610612736 | bytes 5767168 | tf_op jit(solution)/shard_map/pallas_call | solution.py:138
  263.7 7.1 %shard_map.96 = (bf16[384,8192]{1,0:T(8,128)(2,1)}, f32[8,128]{1,0:T(8,128)}) custom-call(s32[2]{0:T(128)} %pad_add_fusion.2.where, bf16[384,1024]{1,0:T(8,128)(2,1)} %pad_maximum_fusion.cot, bf16[384,16]{1,0:T(8,128)(2,1)} %convolution_convert_fusion.2.grad, bf16[48,8192]{1,0:T(8,128)(2,1)} %pad_maximum_fusion.1.down, ...), custom_call_target="tpu_custom_call", output_to_operand_aliasing={{0}: (6, {})} | custom-call | flops 1610612736 | bytes 5767168 | tf_op jit(solution)/shard_map/pallas_call | solution.py:138
  270.8 8.8 %shard_map.103.refs_1_ = f32[256,384]{1,0:T(8,128)} custom-call(bf16[16,240,512]{2,1,0:T(8,128)(2,1)} %all-to-all-done.2.act.maps, bf16[16,240,512]{2,1,0:T(8,128)(2,1)} %all-to-all-done.2.act.maps, s32[1,3072]{1,0:T(1,128)} %reshape.318.rows.refs_0_, s32[1,3072]{1,0:T(1,128)} %shard_map.102.spots, s32[32,1]{1,0:T(8,128)} %copy.34.starts), custom_call_target="tpu_custom_call" | custom-call | flops 2415919104 | bytes 3145728 | tf_op jit(solution)/shard_map/pallas_call | solution.py:498
  279.6 1.9 copy.37
  281.5 4.7 %all-to-all-start.4 = ((f32[16,24,256]{2,1,0:T(8,128)}), f32[16,24,256]{2,1,0:T(8,128)S(1)}, u32[]{:S(2)}, u32[]{:S(2)}) async-start(f32[16,24,256]{2,1,0:T(8,128)} %bitcast.39), calls=%async_computation.4 | async-start | bytes 786432 | tf_op jit(solution)/shard_map/all_to_all | solution.py:502
  300.5 6.7 %shard_map.105 = bf16[768,512]{1,0:T(8,128)(2,1)} custom-call(bf16[16,240,512]{2,1,0:T(8,128)(2,1)} %all-to-all-done.2.act.maps, bf16[256,384]{1,0:T(8,128)(2,1)} %bitcast.117, s32[1,3072]{1,0:T(1,128)} %shard_map.104.rows, s32[1,3072]{1,0:T(1,128)} %shard_map.102.spots, s32[32,1]{1,0:T(8,128)} %copy.34.starts), custom_call_target="tpu_custom_call" | custom-call | flops 2415919104 | bytes 3145728 | tf_op jit(solution)/shard_map/pallas_call | solution.py:500
  307.2 6.0 %all-to-all-start.3 = ((bf16[16,48,512]{2,1,0:T(8,128)(2,1)}), bf16[16,48,512]{2,1,0:T(8,128)(2,1)S(1)}, u32[]{:S(2)}, u32[]{:S(2)}) async-start(bf16[16,48,512]{2,1,0:T(8,128)(2,1)} %bitcast.114), calls=%async_computation.3 | async-start | bytes 1572864 | tf_op jit(solution)/shard_map/all_to_all | solution.py:505
  313.2 7.2 %shard_map.97 = (bf16[384,8192]{1,0:T(8,128)(2,1)}, f32[8,128]{1,0:T(8,128)}) custom-call(s32[2]{0:T(128)} %pad_add_fusion.1.where, bf16[384,1024]{1,0:T(8,128)(2,1)} %pad_maximum_fusion.cot, bf16[384,16]{1,0:T(8,128)(2,1)} %convolution_convert_fusion.2.grad, bf16[48,8192]{1,0:T(8,128)(2,1)} %pad_maximum_fusion.1.down, ...), custom_call_target="tpu_custom_call", output_to_operand_aliasing={{0}: (6, {})} | custom-call | flops 1610612736 | bytes 5767168 | tf_op jit(solution)/shard_map/pallas_call | solution.py:138
  321.2 1.9 select_add_fusion.1
  323.3 4.3 %collective-permute-start.12 = (f32[16,1024]{1,0:T(8,128)S(1)}, f32[16,1024]{1,0:T(8,128)S(1)}, u32[]{:S(2)}, u32[]{:S(2)}) collective-permute-start(f32[16,1024]{1,0:T(8,128)S(1)} %get-tuple-element.20), channel_id=1, source_target_pairs={{0,14},{1,15},{2,0},{3,1},{4,2},{5,3},{6,4},{7,5},{8,6},{9,7},{10,... | collective-permute-start | bytes 196616 | tf_op jit(solution)/shard_map/ppermute | solution.py:21
  327.6 1.7 collective-permute-start.13
  329.6 7.1 %shard_map.98 = (bf16[384,8192]{1,0:T(8,128)(2,1)}, f32[8,128]{1,0:T(8,128)}) custom-call(s32[2]{0:T(128)} %pad_add_fusion.where, bf16[384,1024]{1,0:T(8,128)(2,1)} %pad_maximum_fusion.cot, bf16[384,16]{1,0:T(8,128)(2,1)} %convolution_convert_fusion.2.grad, bf16[48,8192]{1,0:T(8,128)(2,1)} %pad_maximum_fusion.1.down, ...), custom_call_target="tpu_custom_call", output_to_operand_aliasing={{0}: (6, {})} | custom-call | flops 1610612736 | bytes 5767168 | tf_op jit(solution)/shard_map/pallas_call | solution.py:138
  337.8 0.9 copy.36
  338.7 1.4 reshape.317
  (75 shorter events, 11.7 us)
Async XLA Ops:
  7.2 21.3 %copy-start = (bf16[512,1024]{1,0:T(8,128)(2,1)S(1)}, bf16[512,1024]{1,0:T(8,128)(2,1)}, u32[]{:S(2)}) copy-start(bf16[512,1024]{1,0:T(8,128)(2,1)} %param.11) | copy-start | bytes 3145732
  13.5 25.7 %collective-permute-start = (bf16[16,9216]{1,0:T(8,128)(2,1)S(1)}, bf16[16,9216]{1,0:T(8,128)(2,1)S(1)}, u32[]{:S(2)}, u32[]{:S(2)}) collective-permute-start(bf16[16,9216]{1,0:T(8,128)(2,1)S(1)} %pad_maximum_fusion.2), channel_id=1, source_target_pairs={{0,4},{1,5},{2,6},{3,7},{4,8},{5,9},{6,10},{7,11},{8,12},{9,13},{1... | collective-permute-start | bytes 884744 | tf_op jit(solution)/shard_map/ppermute | solution.py:21
  15.7 23.6 %collective-permute-start.1 = (bf16[16,9216]{1,0:T(8,128)(2,1)S(1)}, bf16[16,9216]{1,0:T(8,128)(2,1)S(1)}, u32[]{:S(2)}, u32[]{:S(2)}) collective-permute-start(bf16[16,9216]{1,0:T(8,128)(2,1)S(1)} %pad_maximum_fusion.2), channel_id=1, source_target_pairs={{0,3},{1,4},{2,5},{3,6},{4,7},{5,8},{6,9},{7,10},{8,11},{9,12},{10... | collective-permute-start | bytes 884744 | tf_op jit(solution)/shard_map/ppermute | solution.py:21
  17.9 21.4 %collective-permute-start.2 = (bf16[16,9216]{1,0:T(8,128)(2,1)S(1)}, bf16[16,9216]{1,0:T(8,128)(2,1)S(1)}, u32[]{:S(2)}, u32[]{:S(2)}) collective-permute-start(bf16[16,9216]{1,0:T(8,128)(2,1)S(1)} %pad_maximum_fusion.2), channel_id=1, source_target_pairs={{0,2},{1,3},{2,4},{3,5},{4,6},{5,7},{6,8},{7,9},{8,10},{9,11},{10,... | collective-permute-start | bytes 884744 | tf_op jit(solution)/shard_map/ppermute | solution.py:21
  19.1 21.0 %collective-permute-start.3 = (bf16[16,9216]{1,0:T(8,128)(2,1)S(1)}, bf16[16,9216]{1,0:T(8,128)(2,1)}, u32[]{:S(2)}, u32[]{:S(2)}) collective-permute-start(bf16[16,9216]{1,0:T(8,128)(2,1)S(1)} %pad_maximum_fusion.2), channel_id=1, source_target_pairs={{0,1},{1,2},{2,3},{3,4},{4,5},{5,6},{6,7},{7,8},{8,9},{9,10},{10,1... | collective-permute-start | bytes 884744 | tf_op jit(solution)/shard_map/ppermute | solution.py:21
  23.8 51.5 %all-to-all-start = ((bf16[16,64,512]{2,1,0:T(8,128)(2,1)}), bf16[16,64,512]{2,1,0:T(8,128)(2,1)S(1)}, u32[]{:S(2)}, u32[]{:S(2)}) async-start(bf16[16,64,512]{2,1,0:T(8,128)(2,1)} %shard_map.94), calls=%async_computation | async-start | bytes 2097152 | tf_op jit(solution)/shard_map/all_to_all | solution.py:403
  28.4 11.7 %copy-start.3 = (bf16[3,16,1024]{2,1,0:T(8,128)(2,1)S(1)}, bf16[3,16,1024]{2,1,0:T(8,128)(2,1)}, u32[]{:S(2)}) copy-start(bf16[3,16,1024]{2,1,0:T(8,128)(2,1)} %param.13) | copy-start | bytes 294916
  28.4 60.3 %all-gather.3.cloned.1.call-start = ((), (), s32[]{:S(2)}) async-start(), calls=%async_computation.5 | async-start | bytes 2621440 | tf_op jit(solution)/shard_map/all_gather | solution.py:75
  39.3 0.7 copy-start.2
  90.2 21.5 %all-to-all-start.1 = ((bf16[16,24,256]{2,1,0:T(8,128)(2,1)}), bf16[16,24,256]{2,1,0:T(8,128)(2,1)S(1)}, u32[]{:S(2)}, u32[]{:S(2)}) async-start(bf16[16,24,256]{2,1,0:T(8,128)(2,1)} %broadcast_in_dim.113), calls=%async_computation.1 | async-start | bytes 393216 | tf_op jit(solution)/shard_map/all_to_all | solution.py:27
  112.5 95.9 %copy-start.1 = (bf16[3,16,8192]{2,1,0:T(8,128)(2,1)S(1)}, bf16[3,16,8192]{2,1,0:T(8,128)(2,1)}, u32[]{:S(2)}) copy-start(bf16[3,16,8192]{2,1,0:T(8,128)(2,1)} %param.12) | copy-start | bytes 2359300
  112.5 158.3 %all-to-all-start.2 = ((bf16[16,240,512]{2,1,0:T(8,128)(2,1)}), bf16[16,240,512]{2,1,0:T(8,128)(2,1)}, u32[]{:S(2)}, u32[]{:S(2)}) async-start(bf16[16,240,512]{2,1,0:T(8,128)(2,1)} %shard_map.101), calls=%async_computation.2 | async-start | bytes 7864320 | tf_op jit(solution)/shard_map/all_to_all | solution.py:461
  117.6 47.2 %collective-permute-start.9 = (bf16[4,256,1024]{2,1,0:T(8,128)(2,1)}, bf16[4,256,1024]{2,1,0:T(8,128)(2,1)}, u32[]{:S(2)}, u32[]{:S(2)}) collective-permute-start(bf16[4,256,1024]{2,1,0:T(8,128)(2,1)} %bitcast.109), channel_id=1, source_target_pairs={{0,16},{16,0},{1,17},{17,1},{2,18},{18,2},{3,19},{19,3},{4,20},{20... | collective-permute-start | bytes 6291464 | tf_op jit(solution)/shard_map/ppermute | solution.py:81
  118.9 88.3 %collective-permute-start.4 = (bf16[4,256,1024]{2,1,0:T(8,128)(2,1)}, bf16[4,256,1024]{2,1,0:T(8,128)(2,1)}, u32[]{:S(2)}, u32[]{:S(2)}) collective-permute-start(bf16[4,256,1024]{2,1,0:T(8,128)(2,1)} %bitcast.110), channel_id=1, source_target_pairs={{0,2},{1,3},{2,0},{3,1},{4,6},{5,7},{6,4},{7,5},{8,10},{9,11},{10,... | collective-permute-start | bytes 6291464 | tf_op jit(solution)/shard_map/ppermute | solution.py:78
  122.2 141.5 %collective-permute-start.8 = (bf16[4,256,1024]{2,1,0:T(8,128)(2,1)}, bf16[4,256,1024]{2,1,0:T(8,128)(2,1)}, u32[]{:S(2)}, u32[]{:S(2)}) collective-permute-start(bf16[4,256,1024]{2,1,0:T(8,128)(2,1)} %bitcast.111), channel_id=1, source_target_pairs={{0,1},{1,0},{2,3},{3,2},{4,5},{5,4},{6,7},{7,6},{8,9},{9,8},{10,11... | collective-permute-start | bytes 6291464 | tf_op jit(solution)/shard_map/ppermute | solution.py:78
  164.8 98.8 %collective-permute-start.10 = (bf16[4,256,1024]{2,1,0:T(8,128)(2,1)}, bf16[4,256,1024]{2,1,0:T(8,128)(2,1)}, u32[]{:S(2)}, u32[]{:S(2)}) collective-permute-start(bf16[4,256,1024]{2,1,0:T(8,128)(2,1)} %collective-permute-done.9.theirs), channel_id=1, source_target_pairs={{0,1},{1,0},{2,3},{3,2},{4,5},{5,4},{6,7},{7,6},{8,9},{9,8},{10,11... | collective-permute-start | bytes 6291464 | tf_op jit(solution)/shard_map/ppermute | solution.py:78
  207.2 46.6 %collective-permute-start.6 = (bf16[4,256,1024]{2,1,0:T(8,128)(2,1)}, bf16[4,256,1024]{2,1,0:T(8,128)(2,1)}, u32[]{:S(2)}, u32[]{:S(2)}) collective-permute-start(bf16[4,256,1024]{2,1,0:T(8,128)(2,1)} %collective-permute-done.4.mine), channel_id=1, source_target_pairs={{0,16},{16,0},{1,17},{17,1},{2,18},{18,2},{3,19},{19,3},{4,20},{20... | collective-permute-start | bytes 6291464 | tf_op jit(solution)/shard_map/ppermute | solution.py:81
  212.8 116.5 %collective-permute-start.5 = (bf16[4,256,1024]{2,1,0:T(8,128)(2,1)}, bf16[4,256,1024]{2,1,0:T(8,128)(2,1)}, u32[]{:S(2)}, u32[]{:S(2)}) collective-permute-start(bf16[4,256,1024]{2,1,0:T(8,128)(2,1)} %collective-permute-done.4.mine), channel_id=1, source_target_pairs={{0,1},{1,0},{2,3},{3,2},{4,5},{5,4},{6,7},{7,6},{8,9},{9,8},{10,11... | collective-permute-start | bytes 6291464 | tf_op jit(solution)/shard_map/ppermute | solution.py:78
  253.8 75.8 %collective-permute-start.7 = (bf16[4,256,1024]{2,1,0:T(8,128)(2,1)}, bf16[4,256,1024]{2,1,0:T(8,128)(2,1)}, u32[]{:S(2)}, u32[]{:S(2)}) collective-permute-start(bf16[4,256,1024]{2,1,0:T(8,128)(2,1)} %collective-permute-done.6.theirs), channel_id=1, source_target_pairs={{0,1},{1,0},{2,3},{3,2},{4,5},{5,4},{6,7},{7,6},{8,9},{9,8},{10,11... | collective-permute-start | bytes 6291464 | tf_op jit(solution)/shard_map/ppermute | solution.py:78
  281.5 25.7 %all-to-all-start.4 = ((f32[16,24,256]{2,1,0:T(8,128)}), f32[16,24,256]{2,1,0:T(8,128)S(1)}, u32[]{:S(2)}, u32[]{:S(2)}) async-start(f32[16,24,256]{2,1,0:T(8,128)} %bitcast.39), calls=%async_computation.4 | async-start | bytes 786432 | tf_op jit(solution)/shard_map/all_to_all | solution.py:502
  307.2 30.4 %all-to-all-start.3 = ((bf16[16,48,512]{2,1,0:T(8,128)(2,1)}), bf16[16,48,512]{2,1,0:T(8,128)(2,1)S(1)}, u32[]{:S(2)}, u32[]{:S(2)}) async-start(bf16[16,48,512]{2,1,0:T(8,128)(2,1)} %bitcast.114), calls=%async_computation.3 | async-start | bytes 1572864 | tf_op jit(solution)/shard_map/all_to_all | solution.py:505
  323.1 13.6 %collective-permute-start.11 = (f32[16,1024]{1,0:T(8,128)S(1)}, f32[16,1024]{1,0:T(8,128)S(1)}, u32[]{:S(2)}, u32[]{:S(2)}) collective-permute-start(f32[16,1024]{1,0:T(8,128)S(1)} %get-tuple-element.20), channel_id=1, source_target_pairs={{0,15},{1,0},{2,1},{3,2},{4,3},{5,4},{6,5},{7,6},{8,7},{9,8},{10,9... | collective-permute-start | bytes 196616 | tf_op jit(solution)/shard_map/ppermute | solution.py:21
  323.3 13.4 %collective-permute-start.12 = (f32[16,1024]{1,0:T(8,128)S(1)}, f32[16,1024]{1,0:T(8,128)S(1)}, u32[]{:S(2)}, u32[]{:S(2)}) collective-permute-start(f32[16,1024]{1,0:T(8,128)S(1)} %get-tuple-element.20), channel_id=1, source_target_pairs={{0,14},{1,15},{2,0},{3,1},{4,2},{5,3},{6,4},{7,5},{8,6},{9,7},{10,... | collective-permute-start | bytes 196616 | tf_op jit(solution)/shard_map/ppermute | solution.py:21
  327.6 9.1 %collective-permute-start.13 = (f32[16,1024]{1,0:T(8,128)S(1)}, f32[16,1024]{1,0:T(8,128)S(1)}, u32[]{:S(2)}, u32[]{:S(2)}) collective-permute-start(f32[16,1024]{1,0:T(8,128)S(1)} %get-tuple-element.20), channel_id=1, source_target_pairs={{0,13},{1,14},{2,15},{3,0},{4,1},{5,2},{6,3},{7,4},{8,5},{9,6},{10... | collective-permute-start | bytes 196616 | tf_op jit(solution)/shard_map/ppermute | solution.py:21
  329.3 7.5 %collective-permute-start.14 = (f32[16,1024]{1,0:T(8,128)S(1)}, f32[16,1024]{1,0:T(8,128)S(1)}, u32[]{:S(2)}, u32[]{:S(2)}) collective-permute-start(f32[16,1024]{1,0:T(8,128)S(1)} %get-tuple-element.20), channel_id=1, source_target_pairs={{0,12},{1,13},{2,14},{3,15},{4,0},{5,1},{6,2},{7,3},{8,4},{9,5},{1... | collective-permute-start | bytes 196616 | tf_op jit(solution)/shard_map/ppermute | solution.py:21
Sparse Core Ops, SparseCore 0:
  31.4 57.2 all-gather.2

commit v9 on v8

--- a/solution.py
+++ b/solution.py
@@ -400,6 +400,7 @@
     pieces = weight_pieces(frozen_value_weight)
 
     sent_rows = pack_rows(token_layout_row, cotangent, devices, cap, features)
+    sent_rows = after(sent_rows, pieces[0][0])
     got_rows = lax.all_to_all(sent_rows, "blk", split_axis=0, concat_axis=0)
     recv_cot = [
         got_rows[:, k * cap : (k + 1) * cap].reshape(resident_rows, features)
@@ -454,11 +455,11 @@
     grad_in = jnp.where(in_block, grad_in, 0.0).astype(jnp.bfloat16)
     grad_in = sum(grad_in[:, b * rank : (b + 1) * rank] for b in range(resident))
     grad_sent = grad_in.reshape(devices, cap, rank).transpose(1, 0, 2).reshape(cap, -1)
-    grad_all = to_all(after(grad_sent, pieces[0][0])).reshape(resident_rows, -1).T
 
     flat_maps = adapter_down_maps.reshape(share, width)
-    received = after(pack_features(activations, flat_maps, devices), grad_all)
+    received = after(pack_features(activations, flat_maps, devices), got_rows)
     received = lax.all_to_all(received, "blk", split_axis=0, concat_axis=0)
+    grad_all = to_all(after(grad_sent, received)).reshape(resident_rows, -1).T
 
     rows_all, place_all = rows_all.reshape(1, -1), place_all.reshape(1, -1)
 
@@ -475,7 +476,7 @@
             out, token = write_quarter(
                 piece, first, group, cot_rows, grad_rows, down_blocks, out
             )
-            if number == 1:
+            if number == 3:
                 place_all = after(place_all, token)
     else:
         weight = together(pieces, firsts, group)

time: 349 us -> 361 us (1.034)
  waiting for transfers between devices: 173 us -> 193 us
  starting transfers between devices: 55.6 us -> 43.2 us
    ppermute x5, waiting for transfers between devices: 41.2 us -> 86.6 us  [over(): return lax.ppermute(piece, 'blk', [(i, i ^ bit) for i in range(count)])]
    ppermute x2, waiting for transfers between devices: 81.4 us -> 41.8 us  [groups(): return lax.ppermute(piece, 'groups', [(0, 1), (1, 0)])]
    all_gather x1, waiting for transfers between devices: 11 us -> 38.5 us  [weight_pieces(): column = lax.all_gather(mine, 'blk', axis_index_groups=lines)]
    all_to_all x1, waiting for transfers between devices: 35.2 us -> 21.9 us  [local(): got_rows = lax.all_to_all(sent_rows, 'blk', split_axis=0, concat_axis=0)]
    all_to_all x1, starting transfers between devices: 13.2 us -> 4.67 us  [to_all(): return lax.all_to_all(copies, 'blk', split_axis=0, concat_axis=0)]
    all_to_all x1, waiting for transfers between devices: 0.01 us -> 4.36 us  [local(): hidden = lax.all_to_all(hidden, 'blk', split_axis=0, concat_axis=0)]
    all_to_all x1, waiting for transfers between devices: 3.78 us -> 0.01 us  [to_all(): return lax.all_to_all(copies, 'blk', split_axis=0, concat_axis=0)]
  transfers between devices with their start and end apart: 21 -> 21, of which waited for: 6 -> 5; matrix products, arithmetic and copies ran while one was open for 6% -> 7% of each run, Pallas kernels for 15% -> 14%
where the time goes in v9:
time: 361 us; the launch traced here: 358 us
  waiting for transfers between devices  193 us (53%)
  Pallas kernels  51.1 us (14%)
  starting transfers between devices  43.2 us (12%)
  between operations  38.8 us (11%)
  local copies, waits for them, and re-layouts  17.4 us (5%)
  other arithmetic  11.4 us (3%)
    ppermute x5, waiting for transfers between devices, over(): return lax.ppermute(piece, 'blk', [(i, i ^ bit) for i in range(count)])  86.6 us
    ppermute x2, waiting for transfers between devices, groups(): return lax.ppermute(piece, 'groups', [(0, 1), (1, 0)])  41.8 us
    all_gather x1, waiting for transfers between devices, weight_pieces(): column = lax.all_gather(mine, 'blk', axis_index_groups=lines)  38.5 us
    pallas_call x4, Pallas kernels, write_quarter(): pl.pallas_call(quarter_kernel, grid_spec=pltpu.PrefetchScalarGridSpec(num...  28.5 us
    all_to_all x1, waiting for transfers between devices, local(): got_rows = lax.all_to_all(sent_rows, 'blk', split_axis=0, concat_axis=0)  21.9 us
    ppermute x8, starting transfers between devices, moved(): lax.ppermute(value, 'blk', [(i, (i + steps) % count) for i in range(count)])  12.1 us
    pallas_call x1, Pallas kernels, local(): shares = hidden_call(received, received, rows_all, place_all, starts)  8.75 us
  transfers between devices with their start and end apart: 21, of which 5 were waited for; matrix products, arithmetic and copies ran while one was open for 7% of the time, Pallas kernels for 14%

profile of v9, /device:TPU:1, one launch (start us, length us, event | category | flops | bytes accessed | tf_op | source)
XLA Modules:
  0.0 357.9 jit_solution(15440847059889854577)
XLA Ops:
  7.2 1.2 copy-done
  8.4 0.8 constant_dynamic-slice_fusion
  9.3 1.4 fusion.20
  14.2 1.3 concatenate.21
  15.5 2.6 shard_map.94.refs_0_
  18.0 0.8 dynamic-slice_bitcast_fusion.1
  18.8 1.0 dynamic-slice_bitcast_fusion
  19.8 38.5 %all-gather.3.cloned.1.call-done = bf16[1024,1024]{1,0:T(8,128)(2,1)} async-done(((bf16[256,1024]{1,0:T(8,128)(2,1)}), bf16[1024,1024]{1,0:T(8,128)(2,1)}) %all-gather.3.cloned.1.call-update) | async-done | bytes 2097168 | tf_op jit(solution)/shard_map/all_gather | solution.py:75
  58.2 4.1 %all-to-all-start = ((bf16[16,64,512]{2,1,0:T(8,128)(2,1)}), bf16[16,64,512]{2,1,0:T(8,128)(2,1)S(1)}, u32[]{:S(2)}, u32[]{:S(2)}) async-start(bf16[16,64,512]{2,1,0:T(8,128)(2,1)} %shard_map.95), calls=%async_computation | async-start | bytes 2097152 | tf_op jit(solution)/shard_map/all_to_all | solution.py:404
  62.4 1.5 collective-permute-start
  63.8 1.7 collective-permute-start.1
  65.6 1.2 collective-permute-start.2
  66.8 1.2 collective-permute-start.3
  77.4 0.7 copy.35.starts
  78.8 4.5 %shard_map.100.refs_0_ = bf16[16,240,512]{2,1,0:T(8,128)(2,1)} custom-call(bf16[192,8192]{1,0:T(8,128)(2,1)} %act.1, bf16[48,8192]{1,0:T(8,128)(2,1)} %bitcast.101), custom_call_target="tpu_custom_call" | custom-call | bytes 7864320 | tf_op jit(solution)/shard_map/pallas_call | solution.py:247
  85.8 21.9 %all-to-all-done.refs_1_ = bf16[16,64,512]{2,1,0:T(8,128)(2,1)S(1)} async-done(((bf16[16,64,512]{2,1,0:T(8,128)(2,1)}), bf16[16,64,512]{2,1,0:T(8,128)(2,1)S(1)}, u32[]{:S(2)}, u32[]{:S(2)}) %all-to-all-start) | async-done | bytes 1048608 | tf_op jit(solution)/shard_map/all_to_all | solution.py:404
  107.7 1.0 copy-done.1
  108.6 5.9 %all-to-all-start.1 = ((bf16[16,240,512]{2,1,0:T(8,128)(2,1)}), bf16[16,240,512]{2,1,0:T(8,128)(2,1)}, u32[]{:S(2)}, u32[]{:S(2)}) async-start(bf16[16,240,512]{2,1,0:T(8,128)(2,1)} %shard_map.101), calls=%async_computation.1 | async-start | bytes 7864320 | tf_op jit(solution)/shard_map/all_to_all | solution.py:461
  114.6 1.0 select_select_fusion
  116.2 1.3 collective-permute-start.9
  117.5 86.6 %collective-permute-done.4.mine = bf16[4,256,1024]{2,1,0:T(8,128)(2,1)} collective-permute-done((bf16[4,256,1024]{2,1,0:T(8,128)(2,1)}, bf16[4,256,1024]{2,1,0:T(8,128)(2,1)}, u32[]{:S(2)}, u32[]{:S(2)}) %collective-permute-start.4) | collective-permute-done | bytes 2097184 | tf_op jit(solution)/shard_map/ppermute | solution.py:78
  204.1 1.2 collective-permute-start.6
  205.3 1.0 pad_maximum_fusion.1.down
  206.3 1.2 collective-permute-start.8
  208.9 41.8 %collective-permute-done.6.theirs = bf16[4,256,1024]{2,1,0:T(8,128)(2,1)} collective-permute-done((bf16[4,256,1024]{2,1,0:T(8,128)(2,1)}, bf16[4,256,1024]{2,1,0:T(8,128)(2,1)}, u32[]{:S(2)}, u32[]{:S(2)}) %collective-permute-start.6) | collective-permute-done | bytes 2097184 | tf_op jit(solution)/shard_map/ppermute | solution.py:81
  250.7 1.8 collective-permute-start.7
  254.7 0.7 reshape.312.refs_0_
  256.4 1.0 pad_maximum_fusion.cot
  257.4 1.0 convolution_convert_fusion.2.grad
  258.4 7.1 %shard_map.96 = (bf16[384,8192]{1,0:T(8,128)(2,1)}, f32[8,128]{1,0:T(8,128)}) custom-call(s32[2]{0:T(128)} %pad_add_fusion.3.where, bf16[384,1024]{1,0:T(8,128)(2,1)} %pad_maximum_fusion.cot, bf16[384,16]{1,0:T(8,128)(2,1)} %convolution_convert_fusion.2.grad, bf16[48,8192]{1,0:T(8,128)(2,1)} %pad_maximum_fusion.1.down, ...), custom_call_target="tpu_custom_call" | custom-call | flops 1610612736 | bytes 5767168 | tf_op jit(solution)/shard_map/pallas_call | solution.py:138
  265.5 7.2 %shard_map.97 = (bf16[384,8192]{1,0:T(8,128)(2,1)}, f32[8,128]{1,0:T(8,128)}) custom-call(s32[2]{0:T(128)} %pad_add_fusion.2.where, bf16[384,1024]{1,0:T(8,128)(2,1)} %pad_maximum_fusion.cot, bf16[384,16]{1,0:T(8,128)(2,1)} %convolution_convert_fusion.2.grad, bf16[48,8192]{1,0:T(8,128)(2,1)} %pad_maximum_fusion.1.down, ...), custom_call_target="tpu_custom_call", output_to_operand_aliasing={{0}: (6, {})} | custom-call | flops 1610612736 | bytes 5767168 | tf_op jit(solution)/shard_map/pallas_call | solution.py:138
  272.7 7.1 %shard_map.98 = (bf16[384,8192]{1,0:T(8,128)(2,1)}, f32[8,128]{1,0:T(8,128)}) custom-call(s32[2]{0:T(128)} %pad_add_fusion.1.where, bf16[384,1024]{1,0:T(8,128)(2,1)} %pad_maximum_fusion.cot, bf16[384,16]{1,0:T(8,128)(2,1)} %convolution_convert_fusion.2.grad, bf16[48,8192]{1,0:T(8,128)(2,1)} %pad_maximum_fusion.1.down, ...), custom_call_target="tpu_custom_call", output_to_operand_aliasing={{0}: (6, {})} | custom-call | flops 1610612736 | bytes 5767168 | tf_op jit(solution)/shard_map/pallas_call | solution.py:138
  279.8 1.4 broadcast_in_dim.113
  281.2 4.7 %all-to-all-start.2 = ((bf16[16,24,256]{2,1,0:T(8,128)(2,1)}), bf16[16,24,256]{2,1,0:T(8,128)(2,1)S(1)}, u32[]{:S(2)}, u32[]{:S(2)}) async-start(bf16[16,24,256]{2,1,0:T(8,128)(2,1)} %broadcast_in_dim.113), calls=%async_computation.2 | async-start | bytes 393216 | tf_op jit(solution)/shard_map/all_to_all | solution.py:27
  285.9 7.1 %shard_map.99 = (bf16[384,8192]{1,0:T(8,128)(2,1)}, f32[8,128]{1,0:T(8,128)}) custom-call(s32[2]{0:T(128)} %pad_add_fusion.where, bf16[384,1024]{1,0:T(8,128)(2,1)} %pad_maximum_fusion.cot, bf16[384,16]{1,0:T(8,128)(2,1)} %convolution_convert_fusion.2.grad, bf16[48,8192]{1,0:T(8,128)(2,1)} %pad_maximum_fusion.1.down, ...), custom_call_target="tpu_custom_call", output_to_operand_aliasing={{0}: (6, {})} | custom-call | flops 1610612736 | bytes 5767168 | tf_op jit(solution)/shard_map/pallas_call | solution.py:138
  293.0 8.7 %shard_map.104.refs_1_ = f32[256,384]{1,0:T(8,128)} custom-call(bf16[16,240,512]{2,1,0:T(8,128)(2,1)} %all-to-all-done.1.refs_1_.act.maps, bf16[16,240,512]{2,1,0:T(8,128)(2,1)} %all-to-all-done.1.refs_1_.act.maps, s32[1,3072]{1,0:T(1,128)} %reshape.318.rows.refs_0_, s32[1,3072]{1,0:T(1,128)} %shard_map.103.spots, s32[32,1]{1,0:T(8,128)} %copy.35.starts), custom_call_target="tpu_custom_call" | custom-call | flops 2415919104 | bytes 3145728 | tf_op jit(solution)/shard_map/pallas_call | solution.py:499
  301.8 1.9 copy.38
  303.7 6.0 %all-to-all-start.4 = ((f32[16,24,256]{2,1,0:T(8,128)}), f32[16,24,256]{2,1,0:T(8,128)S(1)}, u32[]{:S(2)}, u32[]{:S(2)}) async-start(f32[16,24,256]{2,1,0:T(8,128)} %bitcast.39), calls=%async_computation.4 | async-start | bytes 786432 | tf_op jit(solution)/shard_map/all_to_all | solution.py:503
  309.7 0.8 copy.34
  310.6 6.7 %shard_map.106 = bf16[768,512]{1,0:T(8,128)(2,1)} custom-call(bf16[16,240,512]{2,1,0:T(8,128)(2,1)} %all-to-all-done.1.refs_1_.act.maps, bf16[256,384]{1,0:T(8,128)(2,1)} %bitcast.113, s32[1,3072]{1,0:T(1,128)} %shard_map.105.rows, s32[1,3072]{1,0:T(1,128)} %shard_map.103.spots, s32[32,1]{1,0:T(8,128)} %copy.35.starts), custom_call_target="tpu_custom_call" | custom-call | flops 2415919104 | bytes 3145728 | tf_op jit(solution)/shard_map/pallas_call | solution.py:501
  317.3 4.4 %all-to-all-done.4 = f32[16,24,256]{2,1,0:T(8,128)S(1)} async-done(((f32[16,24,256]{2,1,0:T(8,128)}), f32[16,24,256]{2,1,0:T(8,128)S(1)}, u32[]{:S(2)}, u32[]{:S(2)}) %all-to-all-start.4) | async-done | bytes 393248 | tf_op jit(solution)/shard_map/all_to_all | solution.py:503
  321.6 3.8 %all-to-all-start.3 = ((bf16[16,48,512]{2,1,0:T(8,128)(2,1)}), bf16[16,48,512]{2,1,0:T(8,128)(2,1)S(1)}, u32[]{:S(2)}, u32[]{:S(2)}) async-start(bf16[16,48,512]{2,1,0:T(8,128)(2,1)} %bitcast.109), calls=%async_computation.3 | async-start | bytes 1572864 | tf_op jit(solution)/shard_map/all_to_all | solution.py:506
  326.3 2.0 select_add_fusion.1
  328.6 4.3 %collective-permute-start.12 = (f32[16,1024]{1,0:T(8,128)S(1)}, f32[16,1024]{1,0:T(8,128)S(1)}, u32[]{:S(2)}, u32[]{:S(2)}) collective-permute-start(f32[16,1024]{1,0:T(8,128)S(1)} %get-tuple-element.20), channel_id=1, source_target_pairs={{0,14},{1,15},{2,0},{3,1},{4,2},{5,3},{6,4},{7,5},{8,6},{9,7},{10,... | collective-permute-start | bytes 196616 | tf_op jit(solution)/shard_map/ppermute | solution.py:21
  332.9 1.6 collective-permute-start.13
  347.8 0.7 pad_maximum_fusion.3
  348.7 0.9 copy.37
  349.6 1.4 reshape.317
  (78 shorter events, 11.5 us)
Async XLA Ops:
  7.2 1.2 copy-start
  7.2 51.1 %all-gather.3.cloned.1.call-start = ((), (), s32[]{:S(2)}) async-start(), calls=%async_computation.5 | async-start | bytes 2621440 | tf_op jit(solution)/shard_map/all_gather | solution.py:75
  58.2 49.4 %all-to-all-start = ((bf16[16,64,512]{2,1,0:T(8,128)(2,1)}), bf16[16,64,512]{2,1,0:T(8,128)(2,1)S(1)}, u32[]{:S(2)}, u32[]{:S(2)}) async-start(bf16[16,64,512]{2,1,0:T(8,128)(2,1)} %shard_map.95), calls=%async_computation | async-start | bytes 2097152 | tf_op jit(solution)/shard_map/all_to_all | solution.py:404
  62.4 52.2 %collective-permute-start = (bf16[16,9216]{1,0:T(8,128)(2,1)S(1)}, bf16[16,9216]{1,0:T(8,128)(2,1)S(1)}, u32[]{:S(2)}, u32[]{:S(2)}) collective-permute-start(bf16[16,9216]{1,0:T(8,128)(2,1)S(1)} %pad_maximum_fusion.2), channel_id=1, source_target_pairs={{0,4},{1,5},{2,6},{3,7},{4,8},{5,9},{6,10},{7,11},{8,12},{9,13},{1... | collective-permute-start | bytes 884744 | tf_op jit(solution)/shard_map/ppermute | solution.py:21
  63.8 50.8 %collective-permute-start.1 = (bf16[16,9216]{1,0:T(8,128)(2,1)S(1)}, bf16[16,9216]{1,0:T(8,128)(2,1)}, u32[]{:S(2)}, u32[]{:S(2)}) collective-permute-start(bf16[16,9216]{1,0:T(8,128)(2,1)S(1)} %pad_maximum_fusion.2), channel_id=1, source_target_pairs={{0,3},{1,4},{2,5},{3,6},{4,7},{5,8},{6,9},{7,10},{8,11},{9,12},{10... | collective-permute-start | bytes 884744 | tf_op jit(solution)/shard_map/ppermute | solution.py:21
  65.6 49.0 %collective-permute-start.2 = (bf16[16,9216]{1,0:T(8,128)(2,1)S(1)}, bf16[16,9216]{1,0:T(8,128)(2,1)}, u32[]{:S(2)}, u32[]{:S(2)}) collective-permute-start(bf16[16,9216]{1,0:T(8,128)(2,1)S(1)} %pad_maximum_fusion.2), channel_id=1, source_target_pairs={{0,2},{1,3},{2,4},{3,5},{4,6},{5,7},{6,8},{7,9},{8,10},{9,11},{10,... | collective-permute-start | bytes 884744 | tf_op jit(solution)/shard_map/ppermute | solution.py:21
  66.8 47.8 %collective-permute-start.3 = (bf16[16,9216]{1,0:T(8,128)(2,1)S(1)}, bf16[16,9216]{1,0:T(8,128)(2,1)}, u32[]{:S(2)}, u32[]{:S(2)}) collective-permute-start(bf16[16,9216]{1,0:T(8,128)(2,1)S(1)} %pad_maximum_fusion.2), channel_id=1, source_target_pairs={{0,1},{1,2},{2,3},{3,4},{4,5},{5,6},{6,7},{7,8},{8,9},{9,10},{10,1... | collective-permute-start | bytes 884744 | tf_op jit(solution)/shard_map/ppermute | solution.py:21
  107.7 1.0 copy-start.1
  108.6 7.5 %copy-start.3 = (bf16[3,16,8192]{2,1,0:T(8,128)(2,1)S(1)}, bf16[3,16,8192]{2,1,0:T(8,128)(2,1)}, u32[]{:S(2)}) copy-start(bf16[3,16,8192]{2,1,0:T(8,128)(2,1)} %param.12) | copy-start | bytes 2359300
  108.6 171.2 %all-to-all-start.1 = ((bf16[16,240,512]{2,1,0:T(8,128)(2,1)}), bf16[16,240,512]{2,1,0:T(8,128)(2,1)}, u32[]{:S(2)}, u32[]{:S(2)}) async-start(bf16[16,240,512]{2,1,0:T(8,128)(2,1)} %shard_map.101), calls=%async_computation.1 | async-start | bytes 7864320 | tf_op jit(solution)/shard_map/all_to_all | solution.py:461
  114.6 2.9 copy-start.4
  115.7 91.8 %copy-start.2 = (bf16[16,64,512]{2,1,0:T(8,128)(2,1)S(1)}, bf16[16,64,512]{2,1,0:T(8,128)(2,1)}, u32[]{:S(2)}) copy-start(bf16[16,64,512]{2,1,0:T(8,128)(2,1)} %copy-done.1) | copy-start | bytes 3145732
  115.7 88.4 %collective-permute-start.4 = (bf16[4,256,1024]{2,1,0:T(8,128)(2,1)}, bf16[4,256,1024]{2,1,0:T(8,128)(2,1)}, u32[]{:S(2)}, u32[]{:S(2)}) collective-permute-start(bf16[4,256,1024]{2,1,0:T(8,128)(2,1)} %bitcast.3.refs_1_.mine), channel_id=1, source_target_pairs={{0,2},{1,3},{2,0},{3,1},{4,6},{5,7},{6,4},{7,5},{8,10},{9,11},{10,... | collective-permute-start | bytes 6291464 | tf_op jit(solution)/shard_map/ppermute | solution.py:78
  116.2 92.0 %collective-permute-start.9 = (bf16[4,256,1024]{2,1,0:T(8,128)(2,1)}, bf16[4,256,1024]{2,1,0:T(8,128)(2,1)}, u32[]{:S(2)}, u32[]{:S(2)}) collective-permute-start(bf16[4,256,1024]{2,1,0:T(8,128)(2,1)} %bitcast.3.refs_1_.mine), channel_id=1, source_target_pairs={{0,16},{16,0},{1,17},{17,1},{2,18},{18,2},{3,19},{19,3},{4,20},{20... | collective-permute-start | bytes 6291464 | tf_op jit(solution)/shard_map/ppermute | solution.py:81
  204.1 46.6 %collective-permute-start.6 = (bf16[4,256,1024]{2,1,0:T(8,128)(2,1)}, bf16[4,256,1024]{2,1,0:T(8,128)(2,1)}, u32[]{:S(2)}, u32[]{:S(2)}) collective-permute-start(bf16[4,256,1024]{2,1,0:T(8,128)(2,1)} %collective-permute-done.4.mine), channel_id=1, source_target_pairs={{0,16},{16,0},{1,17},{17,1},{2,18},{18,2},{3,19},{19,3},{4,20},{20... | collective-permute-start | bytes 6291464 | tf_op jit(solution)/shard_map/ppermute | solution.py:81
  206.3 59.2 %collective-permute-start.8 = (bf16[4,256,1024]{2,1,0:T(8,128)(2,1)}, bf16[4,256,1024]{2,1,0:T(8,128)(2,1)}, u32[]{:S(2)}, u32[]{:S(2)}) collective-permute-start(bf16[4,256,1024]{2,1,0:T(8,128)(2,1)} %bitcast.3.refs_1_.mine), channel_id=1, source_target_pairs={{0,1},{1,0},{2,3},{3,2},{4,5},{5,4},{6,7},{7,6},{8,9},{9,8},{10,11... | collective-permute-start | bytes 6291464 | tf_op jit(solution)/shard_map/ppermute | solution.py:78
  208.2 57.3 %collective-permute-start.10 = (bf16[4,256,1024]{2,1,0:T(8,128)(2,1)}, bf16[4,256,1024]{2,1,0:T(8,128)(2,1)}, u32[]{:S(2)}, u32[]{:S(2)}) collective-permute-start(bf16[4,256,1024]{2,1,0:T(8,128)(2,1)} %collective-permute-done.9.theirs), channel_id=1, source_target_pairs={{0,1},{1,0},{2,3},{3,2},{4,5},{5,4},{6,7},{7,6},{8,9},{9,8},{10,11... | collective-permute-start | bytes 6291464 | tf_op jit(solution)/shard_map/ppermute | solution.py:78
  208.4 77.5 %collective-permute-start.5 = (bf16[4,256,1024]{2,1,0:T(8,128)(2,1)}, bf16[4,256,1024]{2,1,0:T(8,128)(2,1)}, u32[]{:S(2)}, u32[]{:S(2)}) collective-permute-start(bf16[4,256,1024]{2,1,0:T(8,128)(2,1)} %collective-permute-done.4.mine), channel_id=1, source_target_pairs={{0,1},{1,0},{2,3},{3,2},{4,5},{5,4},{6,7},{7,6},{8,9},{9,8},{10,11... | collective-permute-start | bytes 6291464 | tf_op jit(solution)/shard_map/ppermute | solution.py:78
  250.7 35.2 %collective-permute-start.7 = (bf16[4,256,1024]{2,1,0:T(8,128)(2,1)}, bf16[4,256,1024]{2,1,0:T(8,128)(2,1)}, u32[]{:S(2)}, u32[]{:S(2)}) collective-permute-start(bf16[4,256,1024]{2,1,0:T(8,128)(2,1)} %collective-permute-done.6.theirs), channel_id=1, source_target_pairs={{0,1},{1,0},{2,3},{3,2},{4,5},{5,4},{6,7},{7,6},{8,9},{9,8},{10,11... | collective-permute-start | bytes 6291464 | tf_op jit(solution)/shard_map/ppermute | solution.py:78
  281.2 22.5 %all-to-all-start.2 = ((bf16[16,24,256]{2,1,0:T(8,128)(2,1)}), bf16[16,24,256]{2,1,0:T(8,128)(2,1)S(1)}, u32[]{:S(2)}, u32[]{:S(2)}) async-start(bf16[16,24,256]{2,1,0:T(8,128)(2,1)} %broadcast_in_dim.113), calls=%async_computation.2 | async-start | bytes 393216 | tf_op jit(solution)/shard_map/all_to_all | solution.py:27
  303.7 17.9 %all-to-all-start.4 = ((f32[16,24,256]{2,1,0:T(8,128)}), f32[16,24,256]{2,1,0:T(8,128)S(1)}, u32[]{:S(2)}, u32[]{:S(2)}) async-start(f32[16,24,256]{2,1,0:T(8,128)} %bitcast.39), calls=%async_computation.4 | async-start | bytes 786432 | tf_op jit(solution)/shard_map/all_to_all | solution.py:503
  321.6 26.8 %all-to-all-start.3 = ((bf16[16,48,512]{2,1,0:T(8,128)(2,1)}), bf16[16,48,512]{2,1,0:T(8,128)(2,1)S(1)}, u32[]{:S(2)}, u32[]{:S(2)}) async-start(bf16[16,48,512]{2,1,0:T(8,128)(2,1)} %bitcast.109), calls=%async_computation.3 | async-start | bytes 1572864 | tf_op jit(solution)/shard_map/all_to_all | solution.py:506
  328.3 19.3 %collective-permute-start.11 = (f32[16,1024]{1,0:T(8,128)S(1)}, f32[16,1024]{1,0:T(8,128)S(1)}, u32[]{:S(2)}, u32[]{:S(2)}) collective-permute-start(f32[16,1024]{1,0:T(8,128)S(1)} %get-tuple-element.20), channel_id=1, source_target_pairs={{0,15},{1,0},{2,1},{3,2},{4,3},{5,4},{6,5},{7,6},{8,7},{9,8},{10,9... | collective-permute-start | bytes 196616 | tf_op jit(solution)/shard_map/ppermute | solution.py:21
  328.6 19.1 %collective-permute-start.12 = (f32[16,1024]{1,0:T(8,128)S(1)}, f32[16,1024]{1,0:T(8,128)S(1)}, u32[]{:S(2)}, u32[]{:S(2)}) collective-permute-start(f32[16,1024]{1,0:T(8,128)S(1)} %get-tuple-element.20), channel_id=1, source_target_pairs={{0,14},{1,15},{2,0},{3,1},{4,2},{5,3},{6,4},{7,5},{8,6},{9,7},{10,... | collective-permute-start | bytes 196616 | tf_op jit(solution)/shard_map/ppermute | solution.py:21
  332.9 14.8 %collective-permute-start.13 = (f32[16,1024]{1,0:T(8,128)S(1)}, f32[16,1024]{1,0:T(8,128)S(1)}, u32[]{:S(2)}, u32[]{:S(2)}) collective-permute-start(f32[16,1024]{1,0:T(8,128)S(1)} %get-tuple-element.20), channel_id=1, source_target_pairs={{0,13},{1,14},{2,15},{3,0},{4,1},{5,2},{6,3},{7,4},{8,5},{9,6},{10... | collective-permute-start | bytes 196616 | tf_op jit(solution)/shard_map/ppermute | solution.py:21
  334.5 13.1 %collective-permute-start.14 = (f32[16,1024]{1,0:T(8,128)S(1)}, f32[16,1024]{1,0:T(8,128)S(1)}, u32[]{:S(2)}, u32[]{:S(2)}) collective-permute-start(f32[16,1024]{1,0:T(8,128)S(1)} %get-tuple-element.20), channel_id=1, source_target_pairs={{0,12},{1,13},{2,14},{3,15},{4,0},{5,1},{6,2},{7,3},{8,4},{9,5},{1... | collective-permute-start | bytes 196616 | tf_op jit(solution)/shard_map/ppermute | solution.py:21
Sparse Core Ops, SparseCore 0:
  10.2 48.0 all-gather.2

commit v10 on v9

--- a/solution.py
+++ b/solution.py
@@ -66,13 +66,15 @@
     return (high * DIGIT + middle) * DIGIT + low, place_high * DIGIT + place
 
 
+CHUNKS = 2
+
+
 def weight_pieces(weight):
     count = lax.axis_size("blk")
     half = weight.shape[0] // 2
-    group = lax.axis_index("groups")
-    mine = lax.dynamic_slice_in_dim(weight, group * half, half, 0)
+    size = half // CHUNKS
+    first = lax.axis_index("groups") * half
     lines = [list(range(k, count, 4)) for k in range(4)]
-    column = lax.all_gather(mine, "blk", axis_index_groups=lines)
 
     def over(piece, bit):
         return lax.ppermute(piece, "blk", [(i, i ^ bit) for i in range(count)])
@@ -80,20 +82,26 @@
     def groups(piece):
         return lax.ppermute(piece, "groups", [(0, 1), (1, 0)])
 
-    across = over(column, 2)
+    columns = [
+        lax.all_gather(
+            lax.dynamic_slice_in_dim(weight, first + k * size, size, 0),
+            "blk",
+            axis_index_groups=lines,
+        )
+        for k in range(CHUNKS)
+    ]
     pieces = []
-    for piece in (column, across):
-        theirs = groups(piece)
-        pieces.append((piece, theirs))
-        pieces.append((over(piece, 1), over(theirs, 1)))
+    for mine in (columns, [over(column, 2) for column in columns]):
+        both = mine + [groups(piece) for piece in mine]
+        pieces += [both, [over(piece, 1) for piece in both]]
     return pieces
 
 
-def quarter_kernel(where, cot, grad, down, mine, theirs, *rest):
+def quarter_kernel(where, cot, grad, down, *rest):
+    pieces = rest[: 2 * CHUNKS]
     out, token = rest[-2:]
     token[...] = jnp.zeros_like(token)
     rank = grad.shape[1]
-    half = mine.shape[1]
     lora = [
         adapter_scale
         * dot(
@@ -106,30 +114,27 @@
     lora = jnp.concatenate(lora, axis=0).astype(jnp.bfloat16).astype(jnp.float32)
 
     def product(group):
-        for k, piece in enumerate((mine, theirs) if group == 0 else (theirs, mine)):
-            part = slice(k * half, (k + 1) * half)
-            frozen = dot(cot[...], piece[0], ((1,), (1,)))
-            out[:, part] = (frozen + lora[:, part]).astype(jnp.bfloat16)
+        order = pieces[group * CHUNKS :] + pieces[: group * CHUNKS]
+        weight = jnp.concatenate([piece[0] for piece in order], axis=0)
+        frozen = dot(cot[...], weight, ((1,), (1,)))
+        out[...] = (frozen + lora).astype(jnp.bfloat16)
 
     for group in range(2):
         pl.when(where[1] == group)(functools.partial(product, group))
 
 
 def write_quarter(quarter, first, group, cot, grad, down, out=None):
-    mine, theirs = quarter
     rows, depth = cot.shape
     width = down.shape[1]
-    shards, half, _ = mine.shape
+    shards, part, _ = quarter[0].shape
+    stripe = part * len(quarter)
     where = jnp.stack([first, group]).astype(jnp.int32)
-    piece = pl.BlockSpec((1, half, depth), lambda j, where: (j, 0, 0))
     specs = [
         pl.BlockSpec((rows, depth), lambda j, where: (0, 0)),
         pl.BlockSpec(grad.shape, lambda j, where: (0, 0)),
-        pl.BlockSpec((down.shape[0], 2 * half), lambda j, where: (0, 4 * j + where[0])),
-        piece,
-        piece,
-    ]
-    args = [where, cot, grad, down, mine, theirs]
+        pl.BlockSpec((down.shape[0], stripe), lambda j, where: (0, 4 * j + where[0])),
+    ] + [pl.BlockSpec((1, part, depth), lambda j, where: (j, 0, 0)) for _ in quarter]
+    args = [where, cot, grad, down] + quarter
     alias = {}
     if out is not None:
         specs.append(pl.BlockSpec(memory_space=pl.ANY))
@@ -142,7 +147,7 @@
             grid=(shards,),
             in_specs=specs,
             out_specs=[
-                pl.BlockSpec((rows, 2 * half), lambda j, where: (0, 4 * j + where[0])),
+                pl.BlockSpec((rows, stripe), lambda j, where: (0, 4 * j + where[0])),
                 pl.BlockSpec((8, LANES), lambda j, where: (0, 0)),
             ],
         ),
@@ -152,8 +157,8 @@
         ],
         input_output_aliases=alias,
         cost_estimate=pl.CostEstimate(
-            flops=4 * rows * depth * half * shards,
-            bytes_accessed=4 * (depth + rows) * half * shards,
+            flops=2 * rows * depth * stripe * shards,
+            bytes_accessed=2 * (depth + rows) * stripe * shards,
             transcendentals=0,
         ),
         compiler_params=pltpu.CompilerParams(vmem_limit_bytes=VMEM),
@@ -161,12 +166,13 @@
 
 
 def together(pieces, firsts, group):
-    shards, half, depth = pieces[0][0].shape
-    weight = jnp.zeros((shards, 4, 2, half, depth), jnp.bfloat16)
+    shards, part, depth = pieces[0][0].shape
+    weight = jnp.zeros((shards, 4, 2, CHUNKS, part, depth), jnp.bfloat16)
     for quarter, first in zip(pieces, firsts):
         for k, piece in enumerate(quarter):
-            place = (0, first, group if k == 0 else 1 - group, 0, 0)
-            weight = lax.dynamic_update_slice(weight, piece[:, None, None], place)
+            half = group if k < CHUNKS else 1 - group
+            place = (0, first, half, k % CHUNKS, 0, 0)
+            weight = lax.dynamic_update_slice(weight, piece[:, None, None, None], place)
     return weight.reshape(-1, depth)
 
 
@@ -399,18 +405,6 @@
 
     pieces = weight_pieces(frozen_value_weight)
 
-    sent_rows = pack_rows(token_layout_row, cotangent, devices, cap, features)
-    sent_rows = after(sent_rows, pieces[0][0])
-    got_rows = lax.all_to_all(sent_rows, "blk", split_axis=0, concat_axis=0)
-    recv_cot = [
-        got_rows[:, k * cap : (k + 1) * cap].reshape(resident_rows, features)
-        for k in range(out_width // features)
-    ]
-    per_digit = -(-tokens // features)
-    digits = got_rows[:, share : share + 5 * per_digit]
-    digits = digits.reshape(devices, 5, per_digit * features)[:, :, :tokens]
-    rows_all, place_all = from_digits(digits)
-
     first_block = device * resident
     block_numbers = first_block + jnp.arange(resident, dtype=jnp.int32)
     begin = starts_of(block_numbers, start_ids)
@@ -440,6 +434,20 @@
     down_blocks = of_blocks(adapter_down_maps, carried[:, :width])
     up_blocks = of_blocks(adapter_up_maps, carried[:, width:])
 
+    sent_rows = pack_rows(token_layout_row, cotangent, devices, cap, features)
+    own, _, across, _ = pieces
+    early = [own[CHUNKS - 1], own[CHUNKS], across[0], carried]
+    sent_rows = after(sent_rows, *early)
+    got_rows = lax.all_to_all(sent_rows, "blk", split_axis=0, concat_axis=0)
+    recv_cot = [
+        got_rows[:, k * cap : (k + 1) * cap].reshape(resident_rows, features)
+        for k in range(out_width // features)
+    ]
+    per_digit = -(-tokens // features)
+    digits = got_rows[:, share : share + 5 * per_digit]
+    digits = digits.reshape(devices, 5, per_digit * features)[:, :, :tokens]
+    rows_all, place_all = from_digits(digits)
+
     spots = device * cap + jnp.arange(cap, dtype=jnp.int32)
     hit = place_all[:, None, :] == spots[None, :, None]
     row_in = rows_all - device * resident_rows + 1
@@ -457,7 +465,8 @@
     grad_sent = grad_in.reshape(devices, cap, rank).transpose(1, 0, 2).reshape(cap, -1)
 
     flat_maps = adapter_down_maps.reshape(share, width)
-    received = after(pack_features(activations, flat_maps, devices), got_rows)
+    received = pack_features(activations, flat_maps, devices)
+    received = after(received, got_rows, own[-1], across[CHUNKS - 1])
     received = lax.all_to_all(received, "blk", split_axis=0, concat_axis=0)
     grad_all = to_all(after(grad_sent, received)).reshape(resident_rows, -1).T
 
@@ -470,7 +479,7 @@
     group = lax.axis_index("groups")
     quarter = device % 4
     firsts = [quarter, quarter ^ 1, quarter ^ 2, quarter ^ 3]
-    if pieces[0][0].shape[1] % LANES == 0:
+    if own[0].shape[1] % LANES == 0:
         out = None
         for number, (piece, first) in enumerate(zip(pieces, firsts)):
             out, token = write_quarter(

time: 361 us -> 303 us (0.84)
  waiting for transfers between devices: 193 us -> 112 us
  starting transfers between devices: 43.2 us -> 66.4 us
    ppermute x5 -> x10, waiting for transfers between devices: 86.6 us -> 11.3 us  [over(): return lax.ppermute(piece, 'blk', [(i, i ^ bit) for i in range(count)])]
    all_to_all x1, waiting for transfers between devices: 21.9 us -> 0.01 us  [local(): got_rows = lax.all_to_all(sent_rows, 'blk', split_axis=0, concat_axis=0)]
    ppermute x5 -> x10, starting transfers between devices: 4.05 us -> 19.1 us  [over(): return lax.ppermute(piece, 'blk', [(i, i ^ bit) for i in range(count)])]
    ppermute x2 -> x4, waiting for transfers between devices: 41.8 us -> 52 us  [groups(): return lax.ppermute(piece, 'groups', [(0, 1), (1, 0)])]
    all_gather x1 -> x2, waiting for transfers between devices: 38.5 us -> 44.1 us  [weight_pieces(): lax.all_gather(lax.dynamic_slice_in_dim(weight, first + k * size, size, 0...]
    all_to_all x1, starting transfers between devices: 4.67 us -> 10.1 us  [to_all(): return lax.all_to_all(copies, 'blk', split_axis=0, concat_axis=0)]
  transfers between devices with their start and end apart: 21 -> 29, of which waited for: 5 -> 7; matrix products, arithmetic and copies ran while one was open for 7% -> 8% of each run, Pallas kernels for 14% -> 17%
where the time goes in v10:
time: 303 us; the launch traced here: 300 us
  waiting for transfers between devices  112 us (37%)
  starting transfers between devices  66.4 us (22%)
  Pallas kernels  51.1 us (17%)
  between operations  38.7 us (13%)
  local copies, waits for them, and re-layouts  18.4 us (6%)
  other arithmetic  11 us (4%)
    ppermute x4, waiting for transfers between devices, groups(): return lax.ppermute(piece, 'groups', [(0, 1), (1, 0)])  52 us
    all_gather x2, waiting for transfers between devices, weight_pieces(): lax.all_gather(lax.dynamic_slice_in_dim(weight, first + k * size, size, 0...  44.1 us
    pallas_call x4, Pallas kernels, write_quarter(): pl.pallas_call(quarter_kernel, grid_spec=pltpu.PrefetchScalarGridSpec(num...  28.5 us
    ppermute x10, starting transfers between devices, over(): return lax.ppermute(piece, 'blk', [(i, i ^ bit) for i in range(count)])  19.1 us
    ppermute x8, starting transfers between devices, moved(): lax.ppermute(value, 'blk', [(i, (i + steps) % count) for i in range(count)])  12.9 us
    ppermute x10, waiting for transfers between devices, over(): return lax.ppermute(piece, 'blk', [(i, i ^ bit) for i in range(count)])  11.3 us
    all_to_all x1, starting transfers between devices, to_all(): return lax.all_to_all(copies, 'blk', split_axis=0, concat_axis=0)  10.1 us
    pallas_call x1, Pallas kernels, local(): shares = hidden_call(received, received, rows_all, place_all, starts)  8.75 us
  transfers between devices with their start and end apart: 29, of which 7 were waited for; matrix products, arithmetic and copies ran while one was open for 8% of the time, Pallas kernels for 17%

profile of v10, /device:TPU:1, one launch (start us, length us, event | category | flops | bytes accessed | tf_op | source)
XLA Modules:
  0.0 300.2 jit_solution(4470244095475826769)
XLA Ops:
  7.2 1.8 constant_dynamic-slice_fusion
  9.2 1.4 fusion.20
  13.8 1.0 dynamic-slice_bitcast_fusion
  14.9 2.2 collective-permute-start.2
  17.0 2.1 collective-permute-start.3
  19.2 1.2 collective-permute-start.4
  20.4 0.9 collective-permute-start.5
  24.6 2.6 shard_map.94.refs_0_
  27.2 19.8 %all-gather.7.cloned.1.call-done = bf16[512,1024]{1,0:T(8,128)(2,1)} async-done(((bf16[128,1024]{1,0:T(8,128)(2,1)}), bf16[512,1024]{1,0:T(8,128)(2,1)}) %all-gather.7.cloned.1.call-update) | async-done | bytes 1048592 | tf_op jit(solution)/shard_map/all_gather | solution.py:86
  47.0 12.3 %collective-permute-start.1 = (bf16[4,128,1024]{2,1,0:T(8,128)(2,1)}, bf16[4,128,1024]{2,1,0:T(8,128)(2,1)S(1)}, u32[]{:S(2)}, u32[]{:S(2)}) collective-permute-start(bf16[4,128,1024]{2,1,0:T(8,128)(2,1)} %bitcast.4.rest_0_), channel_id=1, source_target_pairs={{0,2},{1,3},{2,0},{3,1},{4,6},{5,7},{6,4},{7,5},{8,10},{9,11},{10,... | collective-permute-start | bytes 3145736 | tf_op jit(solution)/shard_map/ppermute | solution.py:80
  59.3 1.2 collective-permute-start
  61.3 24.3 %all-gather.5.cloned.1.call-done = bf16[512,1024]{1,0:T(8,128)(2,1)} async-done(((bf16[128,1024]{1,0:T(8,128)(2,1)}), bf16[512,1024]{1,0:T(8,128)(2,1)}) %all-gather.5.cloned.1.call-update) | async-done | bytes 1048592 | tf_op jit(solution)/shard_map/all_gather | solution.py:86
  85.6 1.0 copy-done.3
  86.6 4.9 %all-to-all-start = ((bf16[16,64,512]{2,1,0:T(8,128)(2,1)}), bf16[16,64,512]{2,1,0:T(8,128)(2,1)S(1)}, u32[]{:S(2)}, u32[]{:S(2)}) async-start(bf16[16,64,512]{2,1,0:T(8,128)(2,1)} %shard_map.95), calls=%async_computation | async-start | bytes 2097152 | tf_op jit(solution)/shard_map/all_to_all | solution.py:441
  91.5 1.2 collective-permute-start.16
  92.7 1.4 collective-permute-start.7
  97.7 4.6 %shard_map.100.refs_0_ = bf16[16,240,512]{2,1,0:T(8,128)(2,1)} custom-call(bf16[192,8192]{1,0:T(8,128)(2,1)} %act.1, bf16[48,8192]{1,0:T(8,128)(2,1)} %bitcast.102), custom_call_target="tpu_custom_call" | custom-call | bytes 7864320 | tf_op jit(solution)/shard_map/pallas_call | solution.py:253
  102.3 14.1 %collective-permute-done.16.rest_3_.refs_2_ = bf16[4,128,1024]{2,1,0:T(8,128)(2,1)} collective-permute-done((bf16[4,128,1024]{2,1,0:T(8,128)(2,1)}, bf16[4,128,1024]{2,1,0:T(8,128)(2,1)}, u32[]{:S(2)}, u32[]{:S(2)}) %collective-permute-start.16) | collective-permute-done | bytes 1048608 | tf_op jit(solution)/shard_map/ppermute | solution.py:83
  116.4 11.2 %collective-permute-done.7.rest_1_.refs_3_ = bf16[4,128,1024]{2,1,0:T(8,128)(2,1)} collective-permute-done((bf16[4,128,1024]{2,1,0:T(8,128)(2,1)}, bf16[4,128,1024]{2,1,0:T(8,128)(2,1)}, u32[]{:S(2)}, u32[]{:S(2)}) %collective-permute-start.7) | collective-permute-done | bytes 1048608 | tf_op jit(solution)/shard_map/ppermute | solution.py:80
  127.7 1.0 copy-done
  128.6 5.6 %all-to-all-start.1 = ((bf16[16,240,512]{2,1,0:T(8,128)(2,1)}), bf16[16,240,512]{2,1,0:T(8,128)(2,1)}, u32[]{:S(2)}, u32[]{:S(2)}) async-start(bf16[16,240,512]{2,1,0:T(8,128)(2,1)} %shard_map.101), calls=%async_computation.1 | async-start | bytes 7864320 | tf_op jit(solution)/shard_map/all_to_all | solution.py:470
  141.9 0.9 pad_maximum_fusion.1.down
  143.5 1.2 collective-permute-start.11
  146.4 1.0 collective-permute-start.15
  150.9 17.4 %collective-permute-done.11.rest_3_ = bf16[4,128,1024]{2,1,0:T(8,128)(2,1)} collective-permute-done((bf16[4,128,1024]{2,1,0:T(8,128)(2,1)}, bf16[4,128,1024]{2,1,0:T(8,128)(2,1)}, u32[]{:S(2)}, u32[]{:S(2)}) %collective-permute-start.11) | collective-permute-done | bytes 1048608 | tf_op jit(solution)/shard_map/ppermute | solution.py:83
  168.2 2.0 collective-permute-start.12
  170.2 20.5 %collective-permute-done.9.rest_2_ = bf16[4,128,1024]{2,1,0:T(8,128)(2,1)} collective-permute-done((bf16[4,128,1024]{2,1,0:T(8,128)(2,1)S(1)}, bf16[4,128,1024]{2,1,0:T(8,128)(2,1)}, u32[]{:S(2)}, u32[]{:S(2)}) %collective-permute-start.9) | collective-permute-done | bytes 1048608 | tf_op jit(solution)/shard_map/ppermute | solution.py:83
  190.7 1.2 collective-permute-start.10
  192.4 1.1 pad_maximum_fusion.cot
  193.4 1.0 convolution_convert_fusion.2.grad
  194.4 7.1 %shard_map.96 = (bf16[384,8192]{1,0:T(8,128)(2,1)}, f32[8,128]{1,0:T(8,128)}) custom-call(s32[2]{0:T(128)} %pad_add_fusion.3.where, bf16[384,1024]{1,0:T(8,128)(2,1)} %pad_maximum_fusion.cot, bf16[384,16]{1,0:T(8,128)(2,1)} %convolution_convert_fusion.2.grad, bf16[48,8192]{1,0:T(8,128)(2,1)} %pad_maximum_fusion.1.down, ...), custom_call_target="tpu_custom_call" | custom-call | flops 1610612736 | bytes 5767168 | tf_op jit(solution)/shard_map/pallas_call | solution.py:143
  201.6 7.1 %shard_map.97 = (bf16[384,8192]{1,0:T(8,128)(2,1)}, f32[8,128]{1,0:T(8,128)}) custom-call(s32[2]{0:T(128)} %pad_add_fusion.2.where, bf16[384,1024]{1,0:T(8,128)(2,1)} %pad_maximum_fusion.cot, bf16[384,16]{1,0:T(8,128)(2,1)} %convolution_convert_fusion.2.grad, bf16[48,8192]{1,0:T(8,128)(2,1)} %pad_maximum_fusion.1.down, ...), custom_call_target="tpu_custom_call", output_to_operand_aliasing={{0}: (8, {})} | custom-call | flops 1610612736 | bytes 5767168 | tf_op jit(solution)/shard_map/pallas_call | solution.py:143
  208.7 7.1 %shard_map.98 = (bf16[384,8192]{1,0:T(8,128)(2,1)}, f32[8,128]{1,0:T(8,128)}) custom-call(s32[2]{0:T(128)} %pad_add_fusion.1.where, bf16[384,1024]{1,0:T(8,128)(2,1)} %pad_maximum_fusion.cot, bf16[384,16]{1,0:T(8,128)(2,1)} %convolution_convert_fusion.2.grad, bf16[48,8192]{1,0:T(8,128)(2,1)} %pad_maximum_fusion.1.down, ...), custom_call_target="tpu_custom_call", output_to_operand_aliasing={{0}: (8, {})} | custom-call | flops 1610612736 | bytes 5767168 | tf_op jit(solution)/shard_map/pallas_call | solution.py:143
  215.8 1.4 broadcast_in_dim.113
  217.2 10.1 %all-to-all-start.2 = ((bf16[16,24,256]{2,1,0:T(8,128)(2,1)}), bf16[16,24,256]{2,1,0:T(8,128)(2,1)S(1)}, u32[]{:S(2)}, u32[]{:S(2)}) async-start(bf16[16,24,256]{2,1,0:T(8,128)(2,1)} %broadcast_in_dim.113), calls=%async_computation.2 | async-start | bytes 393216 | tf_op jit(solution)/shard_map/all_to_all | solution.py:27
  227.4 0.9 copy-done.6
  228.3 7.1 %shard_map.99 = (bf16[384,8192]{1,0:T(8,128)(2,1)}, f32[8,128]{1,0:T(8,128)}) custom-call(s32[2]{0:T(128)} %pad_add_fusion.where, bf16[384,1024]{1,0:T(8,128)(2,1)} %pad_maximum_fusion.cot, bf16[384,16]{1,0:T(8,128)(2,1)} %convolution_convert_fusion.2.grad, bf16[48,8192]{1,0:T(8,128)(2,1)} %pad_maximum_fusion.1.down, ...), custom_call_target="tpu_custom_call", output_to_operand_aliasing={{0}: (8, {})} | custom-call | flops 1610612736 | bytes 5767168 | tf_op jit(solution)/shard_map/pallas_call | solution.py:143
  235.5 8.7 %shard_map.104.refs_1_ = f32[256,384]{1,0:T(8,128)} custom-call(bf16[16,240,512]{2,1,0:T(8,128)(2,1)} %all-to-all-done.1.refs_1_.act.maps, bf16[16,240,512]{2,1,0:T(8,128)(2,1)} %all-to-all-done.1.refs_1_.act.maps, s32[1,3072]{1,0:T(1,128)} %reshape.318.rows.refs_0_, s32[1,3072]{1,0:T(1,128)} %shard_map.103.spots, s32[32,1]{1,0:T(8,128)} %copy.35.starts), custom_call_target="tpu_custom_call" | custom-call | flops 2415919104 | bytes 3145728 | tf_op jit(solution)/shard_map/pallas_call | solution.py:508
  244.2 1.9 copy.38
  246.1 6.0 %all-to-all-start.4 = ((f32[16,24,256]{2,1,0:T(8,128)}), f32[16,24,256]{2,1,0:T(8,128)S(1)}, u32[]{:S(2)}, u32[]{:S(2)}) async-start(f32[16,24,256]{2,1,0:T(8,128)} %bitcast.40), calls=%async_computation.4 | async-start | bytes 786432 | tf_op jit(solution)/shard_map/all_to_all | solution.py:512
  252.9 6.7 %shard_map.106 = bf16[768,512]{1,0:T(8,128)(2,1)} custom-call(bf16[16,240,512]{2,1,0:T(8,128)(2,1)} %all-to-all-done.1.refs_1_.act.maps, bf16[256,384]{1,0:T(8,128)(2,1)} %bitcast.114, s32[1,3072]{1,0:T(1,128)} %shard_map.105.rows, s32[1,3072]{1,0:T(1,128)} %shard_map.103.spots, s32[32,1]{1,0:T(8,128)} %copy.35.starts), custom_call_target="tpu_custom_call" | custom-call | flops 2415919104 | bytes 3145728 | tf_op jit(solution)/shard_map/pallas_call | solution.py:510
  259.7 4.4 %all-to-all-done.4 = f32[16,24,256]{2,1,0:T(8,128)S(1)} async-done(((f32[16,24,256]{2,1,0:T(8,128)}), f32[16,24,256]{2,1,0:T(8,128)S(1)}, u32[]{:S(2)}, u32[]{:S(2)}) %all-to-all-start.4) | async-done | bytes 393248 | tf_op jit(solution)/shard_map/all_to_all | solution.py:512
  264.0 3.8 %all-to-all-start.3 = ((bf16[16,48,512]{2,1,0:T(8,128)(2,1)}), bf16[16,48,512]{2,1,0:T(8,128)(2,1)S(1)}, u32[]{:S(2)}, u32[]{:S(2)}) async-start(bf16[16,48,512]{2,1,0:T(8,128)(2,1)} %bitcast.110), calls=%async_computation.3 | async-start | bytes 1572864 | tf_op jit(solution)/shard_map/all_to_all | solution.py:515
  268.7 1.9 select_add_fusion.1
  270.9 4.3 %collective-permute-start.19 = (f32[16,1024]{1,0:T(8,128)S(1)}, f32[16,1024]{1,0:T(8,128)S(1)}, u32[]{:S(2)}, u32[]{:S(2)}) collective-permute-start(f32[16,1024]{1,0:T(8,128)S(1)} %get-tuple-element.20), channel_id=1, source_target_pairs={{0,14},{1,15},{2,0},{3,1},{4,2},{5,3},{6,4},{7,5},{8,6},{9,7},{10,... | collective-permute-start | bytes 196616 | tf_op jit(solution)/shard_map/ppermute | solution.py:21
  275.2 1.6 collective-permute-start.20
  291.1 0.9 copy.37
  292.0 1.4 reshape.317
  (104 shorter events, 16.9 us)
Async XLA Ops:
  7.2 7.6 %copy-start.7 = (bf16[3,16,1024]{2,1,0:T(8,128)(2,1)S(1)}, bf16[3,16,1024]{2,1,0:T(8,128)(2,1)}, u32[]{:S(2)}) copy-start(bf16[3,16,1024]{2,1,0:T(8,128)(2,1)} %param.13) | copy-start | bytes 294916
  7.2 16.8 %copy-start.8 = (s32[192]{0:T(256)S(1)}, s32[192]{0:T(256)}, u32[]{:S(2)}) copy-start(s32[192]{0:T(256)} %param.9) | copy-start | bytes 2308
  7.2 39.8 %all-gather.7.cloned.1.call-start = ((), (), s32[]{:S(2)}) async-start(), calls=%async_computation.6 | async-start | bytes 1310720 | tf_op jit(solution)/shard_map/all_gather | solution.py:86
  9.1 76.5 %all-gather.5.cloned.1.call-start = ((), (), s32[]{:S(2)}) async-start(), calls=%async_computation.5 | async-start | bytes 1310720 | tf_op jit(solution)/shard_map/all_gather | solution.py:86
  14.9 44.5 %collective-permute-start.2 = (bf16[16,9216]{1,0:T(8,128)(2,1)S(1)}, bf16[16,9216]{1,0:T(8,128)(2,1)S(1)}, u32[]{:S(2)}, u32[]{:S(2)}) collective-permute-start(bf16[16,9216]{1,0:T(8,128)(2,1)S(1)} %pad_maximum_fusion.2), channel_id=1, source_target_pairs={{0,4},{1,5},{2,6},{3,7},{4,8},{5,9},{6,10},{7,11},{8,12},{9,13},{1... | collective-permute-start | bytes 884744 | tf_op jit(solution)/shard_map/ppermute | solution.py:21
  17.0 43.5 %collective-permute-start.3 = (bf16[16,9216]{1,0:T(8,128)(2,1)S(1)}, bf16[16,9216]{1,0:T(8,128)(2,1)S(1)}, u32[]{:S(2)}, u32[]{:S(2)}) collective-permute-start(bf16[16,9216]{1,0:T(8,128)(2,1)S(1)} %pad_maximum_fusion.2), channel_id=1, source_target_pairs={{0,3},{1,4},{2,5},{3,6},{4,7},{5,8},{6,9},{7,10},{8,11},{9,12},{10... | collective-permute-start | bytes 884744 | tf_op jit(solution)/shard_map/ppermute | solution.py:21
  19.2 41.4 %collective-permute-start.4 = (bf16[16,9216]{1,0:T(8,128)(2,1)S(1)}, bf16[16,9216]{1,0:T(8,128)(2,1)S(1)}, u32[]{:S(2)}, u32[]{:S(2)}) collective-permute-start(bf16[16,9216]{1,0:T(8,128)(2,1)S(1)} %pad_maximum_fusion.2), channel_id=1, source_target_pairs={{0,2},{1,3},{2,4},{3,5},{4,6},{5,7},{6,8},{7,9},{8,10},{9,11},{10,... | collective-permute-start | bytes 884744 | tf_op jit(solution)/shard_map/ppermute | solution.py:21
  20.4 40.2 %collective-permute-start.5 = (bf16[16,9216]{1,0:T(8,128)(2,1)S(1)}, bf16[16,9216]{1,0:T(8,128)(2,1)S(1)}, u32[]{:S(2)}, u32[]{:S(2)}) collective-permute-start(bf16[16,9216]{1,0:T(8,128)(2,1)S(1)} %pad_maximum_fusion.2), channel_id=1, source_target_pairs={{0,1},{1,2},{2,3},{3,4},{4,5},{5,6},{6,7},{7,8},{8,9},{9,10},{10,1... | collective-permute-start | bytes 884744 | tf_op jit(solution)/shard_map/ppermute | solution.py:21
  47.0 38.6 %collective-permute-start.1 = (bf16[4,128,1024]{2,1,0:T(8,128)(2,1)}, bf16[4,128,1024]{2,1,0:T(8,128)(2,1)S(1)}, u32[]{:S(2)}, u32[]{:S(2)}) collective-permute-start(bf16[4,128,1024]{2,1,0:T(8,128)(2,1)} %bitcast.4.rest_0_), channel_id=1, source_target_pairs={{0,2},{1,3},{2,0},{3,1},{4,6},{5,7},{6,4},{7,5},{8,10},{9,11},{10,... | collective-permute-start | bytes 3145736 | tf_op jit(solution)/shard_map/ppermute | solution.py:80
  59.3 26.3 %collective-permute-start = (bf16[4,128,1024]{2,1,0:T(8,128)(2,1)}, bf16[4,128,1024]{2,1,0:T(8,128)(2,1)}, u32[]{:S(2)}, u32[]{:S(2)}) collective-permute-start(bf16[4,128,1024]{2,1,0:T(8,128)(2,1)} %bitcast.4.rest_0_), channel_id=1, source_target_pairs={{0,16},{16,0},{1,17},{17,1},{2,18},{18,2},{3,19},{19,3},{4,20},{20... | collective-permute-start | bytes 3145736 | tf_op jit(solution)/shard_map/ppermute | solution.py:83
  85.6 1.0 copy-start.3
  86.6 41.1 %all-to-all-start = ((bf16[16,64,512]{2,1,0:T(8,128)(2,1)}), bf16[16,64,512]{2,1,0:T(8,128)(2,1)S(1)}, u32[]{:S(2)}, u32[]{:S(2)}) async-start(bf16[16,64,512]{2,1,0:T(8,128)(2,1)} %shard_map.95), calls=%async_computation | async-start | bytes 2097152 | tf_op jit(solution)/shard_map/all_to_all | solution.py:441
  91.5 24.9 %collective-permute-start.16 = (bf16[4,128,1024]{2,1,0:T(8,128)(2,1)}, bf16[4,128,1024]{2,1,0:T(8,128)(2,1)}, u32[]{:S(2)}, u32[]{:S(2)}) collective-permute-start(bf16[4,128,1024]{2,1,0:T(8,128)(2,1)} %bitcast.3.refs_1_.rest_1_), channel_id=1, source_target_pairs={{0,16},{16,0},{1,17},{17,1},{2,18},{18,2},{3,19},{19,3},{4,20},{20... | collective-permute-start | bytes 3145736 | tf_op jit(solution)/shard_map/ppermute | solution.py:83
  92.7 35.0 %collective-permute-start.7 = (bf16[4,128,1024]{2,1,0:T(8,128)(2,1)}, bf16[4,128,1024]{2,1,0:T(8,128)(2,1)}, u32[]{:S(2)}, u32[]{:S(2)}) collective-permute-start(bf16[4,128,1024]{2,1,0:T(8,128)(2,1)} %bitcast.3.refs_1_.rest_1_), channel_id=1, source_target_pairs={{0,2},{1,3},{2,0},{3,1},{4,6},{5,7},{6,4},{7,5},{8,10},{9,11},{10,... | collective-permute-start | bytes 3145736 | tf_op jit(solution)/shard_map/ppermute | solution.py:80
  127.7 1.0 copy-start
  128.6 13.2 %copy-start.5 = (bf16[16,9216]{1,0:T(8,128)(2,1)S(1)}, bf16[16,9216]{1,0:T(8,128)(2,1)}, u32[]{:S(2)}) copy-start(bf16[16,9216]{1,0:T(8,128)(2,1)} %select_select_fusion.refs_4_) | copy-start | bytes 884740
  128.6 13.2 %copy-start.2 = (bf16[3,16,8192]{2,1,0:T(8,128)(2,1)S(1)}, bf16[3,16,8192]{2,1,0:T(8,128)(2,1)}, u32[]{:S(2)}) copy-start(bf16[3,16,8192]{2,1,0:T(8,128)(2,1)} %param.12) | copy-start | bytes 2359300
  128.6 87.2 %all-to-all-start.1 = ((bf16[16,240,512]{2,1,0:T(8,128)(2,1)}), bf16[16,240,512]{2,1,0:T(8,128)(2,1)}, u32[]{:S(2)}, u32[]{:S(2)}) async-start(bf16[16,240,512]{2,1,0:T(8,128)(2,1)} %shard_map.101), calls=%async_computation.1 | async-start | bytes 7864320 | tf_op jit(solution)/shard_map/all_to_all | solution.py:470
  141.8 2.9 copy-start.4
  141.8 3.2 %copy-start.1 = (bf16[16,64,512]{2,1,0:T(8,128)(2,1)S(1)}, bf16[16,64,512]{2,1,0:T(8,128)(2,1)}, u32[]{:S(2)}) copy-start(bf16[16,64,512]{2,1,0:T(8,128)(2,1)} %copy-done) | copy-start | bytes 3145732
  142.9 3.5 %collective-permute-start.14 = (bf16[4,128,1024]{2,1,0:T(8,128)(2,1)}, bf16[4,128,1024]{2,1,0:T(8,128)(2,1)}, u32[]{:S(2)}, u32[]{:S(2)}) collective-permute-start(bf16[4,128,1024]{2,1,0:T(8,128)(2,1)} %bitcast.3.refs_1_.rest_1_), channel_id=1, source_target_pairs={{0,1},{1,0},{2,3},{3,2},{4,5},{5,4},{6,7},{7,6},{8,9},{9,8},{10,11... | collective-permute-start | bytes 3145736 | tf_op jit(solution)/shard_map/ppermute | solution.py:80
  143.0 7.2 %collective-permute-start.13 = (bf16[4,128,1024]{2,1,0:T(8,128)(2,1)}, bf16[4,128,1024]{2,1,0:T(8,128)(2,1)}, u32[]{:S(2)}, u32[]{:S(2)}) collective-permute-start(bf16[4,128,1024]{2,1,0:T(8,128)(2,1)} %bitcast.4.rest_0_), channel_id=1, source_target_pairs={{0,1},{1,0},{2,3},{3,2},{4,5},{5,4},{6,7},{7,6},{8,9},{9,8},{10,11... | collective-permute-start | bytes 3145736 | tf_op jit(solution)/shard_map/ppermute | solution.py:80
  143.4 7.0 %collective-permute-start.17 = (bf16[4,128,1024]{2,1,0:T(8,128)(2,1)}, bf16[4,128,1024]{2,1,0:T(8,128)(2,1)}, u32[]{:S(2)}, u32[]{:S(2)}) collective-permute-start(bf16[4,128,1024]{2,1,0:T(8,128)(2,1)} %collective-permute-done.16.rest_3_.refs_2_), channel_id=1, source_target_pairs={{0,1},{1,0},{2,3},{3,2},{4,5},{5,4},{6,7},{7,6},{8,9},{9,8},{10,11... | collective-permute-start | bytes 3145736 | tf_op jit(solution)/shard_map/ppermute | solution.py:80
  143.5 24.7 %collective-permute-start.11 = (bf16[4,128,1024]{2,1,0:T(8,128)(2,1)}, bf16[4,128,1024]{2,1,0:T(8,128)(2,1)}, u32[]{:S(2)}, u32[]{:S(2)}) collective-permute-start(bf16[4,128,1024]{2,1,0:T(8,128)(2,1)} %collective-permute-done.7.rest_1_.refs_3_), channel_id=1, source_target_pairs={{0,16},{16,0},{1,17},{17,1},{2,18},{18,2},{3,19},{19,3},{4,20},{20... | collective-permute-start | bytes 3145736 | tf_op jit(solution)/shard_map/ppermute | solution.py:83
  144.7 46.0 %collective-permute-start.9 = (bf16[4,128,1024]{2,1,0:T(8,128)(2,1)S(1)}, bf16[4,128,1024]{2,1,0:T(8,128)(2,1)}, u32[]{:S(2)}, u32[]{:S(2)}) collective-permute-start(bf16[4,128,1024]{2,1,0:T(8,128)(2,1)S(1)} %copy-done.4), channel_id=1, source_target_pairs={{0,16},{16,0},{1,17},{17,1},{2,18},{18,2},{3,19},{19,3},{4,20},{20... | collective-permute-start | bytes 3145736 | tf_op jit(solution)/shard_map/ppermute | solution.py:83
  146.4 55.2 %collective-permute-start.15 = (bf16[4,128,1024]{2,1,0:T(8,128)(2,1)}, bf16[4,128,1024]{2,1,0:T(8,128)(2,1)}, u32[]{:S(2)}, u32[]{:S(2)}) collective-permute-start(bf16[4,128,1024]{2,1,0:T(8,128)(2,1)} %collective-permute-done.refs_2_.rest_2_), channel_id=1, source_target_pairs={{0,1},{1,0},{2,3},{3,2},{4,5},{5,4},{6,7},{7,6},{8,9},{9,8},{10,11... | collective-permute-start | bytes 3145736 | tf_op jit(solution)/shard_map/ppermute | solution.py:80
  150.3 77.1 %collective-permute-start.8 = (bf16[4,128,1024]{2,1,0:T(8,128)(2,1)}, bf16[4,128,1024]{2,1,0:T(8,128)(2,1)S(1)}, u32[]{:S(2)}, u32[]{:S(2)}) collective-permute-start(bf16[4,128,1024]{2,1,0:T(8,128)(2,1)} %collective-permute-done.7.rest_1_.refs_3_), channel_id=1, source_target_pairs={{0,1},{1,0},{2,3},{3,2},{4,5},{5,4},{6,7},{7,6},{8,9},{9,8},{10,11... | collective-permute-start | bytes 3145736 | tf_op jit(solution)/shard_map/ppermute | solution.py:80
  150.4 77.0 %collective-permute-start.6 = (bf16[4,128,1024]{2,1,0:T(8,128)(2,1)S(1)}, bf16[4,128,1024]{2,1,0:T(8,128)(2,1)}, u32[]{:S(2)}, u32[]{:S(2)}) collective-permute-start(bf16[4,128,1024]{2,1,0:T(8,128)(2,1)S(1)} %copy-done.4), channel_id=1, source_target_pairs={{0,1},{1,0},{2,3},{3,2},{4,5},{5,4},{6,7},{7,6},{8,9},{9,8},{10,11... | collective-permute-start | bytes 3145736 | tf_op jit(solution)/shard_map/ppermute | solution.py:80
  168.2 59.2 %collective-permute-start.12 = (bf16[4,128,1024]{2,1,0:T(8,128)(2,1)}, bf16[4,128,1024]{2,1,0:T(8,128)(2,1)}, u32[]{:S(2)}, u32[]{:S(2)}) collective-permute-start(bf16[4,128,1024]{2,1,0:T(8,128)(2,1)} %collective-permute-done.11.rest_3_), channel_id=1, source_target_pairs={{0,1},{1,0},{2,3},{3,2},{4,5},{5,4},{6,7},{7,6},{8,9},{9,8},{10,11... | collective-permute-start | bytes 3145736 | tf_op jit(solution)/shard_map/ppermute | solution.py:80
  190.7 36.7 %collective-permute-start.10 = (bf16[4,128,1024]{2,1,0:T(8,128)(2,1)}, bf16[4,128,1024]{2,1,0:T(8,128)(2,1)}, u32[]{:S(2)}, u32[]{:S(2)}) collective-permute-start(bf16[4,128,1024]{2,1,0:T(8,128)(2,1)} %collective-permute-done.9.rest_2_), channel_id=1, source_target_pairs={{0,1},{1,0},{2,3},{3,2},{4,5},{5,4},{6,7},{7,6},{8,9},{9,8},{10,11... | collective-permute-start | bytes 3145736 | tf_op jit(solution)/shard_map/ppermute | solution.py:80
  217.2 28.9 %all-to-all-start.2 = ((bf16[16,24,256]{2,1,0:T(8,128)(2,1)}), bf16[16,24,256]{2,1,0:T(8,128)(2,1)S(1)}, u32[]{:S(2)}, u32[]{:S(2)}) async-start(bf16[16,24,256]{2,1,0:T(8,128)(2,1)} %broadcast_in_dim.113), calls=%async_computation.2 | async-start | bytes 393216 | tf_op jit(solution)/shard_map/all_to_all | solution.py:27
  227.4 1.0 copy-start.6
  246.1 17.9 %all-to-all-start.4 = ((f32[16,24,256]{2,1,0:T(8,128)}), f32[16,24,256]{2,1,0:T(8,128)S(1)}, u32[]{:S(2)}, u32[]{:S(2)}) async-start(f32[16,24,256]{2,1,0:T(8,128)} %bitcast.40), calls=%async_computation.4 | async-start | bytes 786432 | tf_op jit(solution)/shard_map/all_to_all | solution.py:512
  264.0 26.8 %all-to-all-start.3 = ((bf16[16,48,512]{2,1,0:T(8,128)(2,1)}), bf16[16,48,512]{2,1,0:T(8,128)(2,1)S(1)}, u32[]{:S(2)}, u32[]{:S(2)}) async-start(bf16[16,48,512]{2,1,0:T(8,128)(2,1)} %bitcast.110), calls=%async_computation.3 | async-start | bytes 1572864 | tf_op jit(solution)/shard_map/all_to_all | solution.py:515
  270.6 19.4 %collective-permute-start.18 = (f32[16,1024]{1,0:T(8,128)S(1)}, f32[16,1024]{1,0:T(8,128)S(1)}, u32[]{:S(2)}, u32[]{:S(2)}) collective-permute-start(f32[16,1024]{1,0:T(8,128)S(1)} %get-tuple-element.20), channel_id=1, source_target_pairs={{0,15},{1,0},{2,1},{3,2},{4,3},{5,4},{6,5},{7,6},{8,7},{9,8},{10,9... | collective-permute-start | bytes 196616 | tf_op jit(solution)/shard_map/ppermute | solution.py:21
  270.9 19.1 %collective-permute-start.19 = (f32[16,1024]{1,0:T(8,128)S(1)}, f32[16,1024]{1,0:T(8,128)S(1)}, u32[]{:S(2)}, u32[]{:S(2)}) collective-permute-start(f32[16,1024]{1,0:T(8,128)S(1)} %get-tuple-element.20), channel_id=1, source_target_pairs={{0,14},{1,15},{2,0},{3,1},{4,2},{5,3},{6,4},{7,5},{8,6},{9,7},{10,... | collective-permute-start | bytes 196616 | tf_op jit(solution)/shard_map/ppermute | solution.py:21
  275.2 14.8 %collective-permute-start.20 = (f32[16,1024]{1,0:T(8,128)S(1)}, f32[16,1024]{1,0:T(8,128)S(1)}, u32[]{:S(2)}, u32[]{:S(2)}) collective-permute-start(f32[16,1024]{1,0:T(8,128)S(1)} %get-tuple-element.20), channel_id=1, source_target_pairs={{0,13},{1,14},{2,15},{3,0},{4,1},{5,2},{6,3},{7,4},{8,5},{9,6},{10... | collective-permute-start | bytes 196616 | tf_op jit(solution)/shard_map/ppermute | solution.py:21
  276.8 13.2 %collective-permute-start.21 = (f32[16,1024]{1,0:T(8,128)S(1)}, f32[16,1024]{1,0:T(8,128)S(1)}, u32[]{:S(2)}, u32[]{:S(2)}) collective-permute-start(f32[16,1024]{1,0:T(8,128)S(1)} %get-tuple-element.20), channel_id=1, source_target_pairs={{0,12},{1,13},{2,14},{3,15},{4,0},{5,1},{6,2},{7,3},{8,4},{9,5},{1... | collective-permute-start | bytes 196616 | tf_op jit(solution)/shard_map/ppermute | solution.py:21
Sparse Core Ops, SparseCore 0:
  10.2 36.8 all-gather.6
  48.6 36.9 all-gather.4

commit v11 on v10

--- a/solution.py
+++ b/solution.py
@@ -82,14 +82,10 @@
     def groups(piece):
         return lax.ppermute(piece, "groups", [(0, 1), (1, 0)])
 
-    columns = [
-        lax.all_gather(
-            lax.dynamic_slice_in_dim(weight, first + k * size, size, 0),
-            "blk",
-            axis_index_groups=lines,
-        )
-        for k in range(CHUNKS)
-    ]
+    column = lax.all_gather(
+        lax.dynamic_slice_in_dim(weight, first, half, 0), "blk", axis_index_groups=lines
+    )
+    columns = [column[:, k * size : (k + 1) * size] for k in range(CHUNKS)]
     pieces = []
     for mine in (columns, [over(column, 2) for column in columns]):
         both = mine + [groups(piece) for piece in mine]
@@ -436,8 +432,7 @@
 
     sent_rows = pack_rows(token_layout_row, cotangent, devices, cap, features)
     own, _, across, _ = pieces
-    early = [own[CHUNKS - 1], own[CHUNKS], across[0], carried]
-    sent_rows = after(sent_rows, *early)
+    sent_rows = after(sent_rows, own[0], own[1], carried)
     got_rows = lax.all_to_all(sent_rows, "blk", split_axis=0, concat_axis=0)
     recv_cot = [
         got_rows[:, k * cap : (k + 1) * cap].reshape(resident_rows, features)
@@ -466,7 +461,7 @@
 
     flat_maps = adapter_down_maps.reshape(share, width)
     received = pack_features(activations, flat_maps, devices)
-    received = after(received, got_rows, own[-1], across[CHUNKS - 1])
+    received = after(received, got_rows, own[CHUNKS], across[0])
     received = lax.all_to_all(received, "blk", split_axis=0, concat_axis=0)
     grad_all = to_all(after(grad_sent, received)).reshape(resident_rows, -1).T
 

time: 303 us -> 321 us (1.059)
  local copies, waits for them, and re-layouts: 18.4 us -> 26.5 us
  waiting for transfers between devices: 112 us -> 118 us
  matrix products: 2.91 us -> 6.21 us
    all_gather x2 -> x1, waiting for transfers between devices: 44.1 us -> 11.4 us  [weight_pieces(): lax.all_gather(lax.dynamic_slice_in_dim(weight, first, half, 0), 'blk', a...]
    ppermute x8, waiting for transfers between devices: 0.02 us -> 25 us  [moved(): lax.ppermute(value, 'blk', [(i, (i + steps) % count) for i in range(count)])]
    ppermute x10, waiting for transfers between devices: 11.3 us -> 35.1 us  [over(): return lax.ppermute(piece, 'blk', [(i, i ^ bit) for i in range(count)])]
    all_to_all x1, starting transfers between devices: 4.92 us -> 17 us  [local(): got_rows = lax.all_to_all(sent_rows, 'blk', split_axis=0, concat_axis=0)]
    ppermute x10, starting transfers between devices: 19.1 us -> 7.34 us  [over(): return lax.ppermute(piece, 'blk', [(i, i ^ bit) for i in range(count)])]
    ppermute x4, waiting for transfers between devices: 52 us -> 43.2 us  [groups(): return lax.ppermute(piece, 'groups', [(0, 1), (1, 0)])]
    reshape x3, local copies, waits for them, and re-layouts: 1.02 us -> 4.71 us  [local(): grad_in.reshape(devices, cap, rank).transpose(1, 0, 2).reshape(cap, -1)]
    all_to_all x1, starting transfers between devices: 10.1 us -> 6.57 us  [to_all(): return lax.all_to_all(copies, 'blk', split_axis=0, concat_axis=0)]
  transfers between devices with their start and end apart: 29 -> 28, of which waited for: 7 -> 9; matrix products, arithmetic and copies ran while one was open for 8% -> 11% of each run, Pallas kernels for 17% -> 16%
where the time goes in v11:
time: 321 us; the launch traced here: 318 us
  waiting for transfers between devices  118 us (37%)
  starting transfers between devices  64.2 us (20%)
  Pallas kernels  51.1 us (16%)
  between operations  39.2 us (12%)
  local copies, waits for them, and re-layouts  26.5 us (8%)
  other arithmetic  12.9 us (4%)
  matrix products  6.21 us (2%)
    ppermute x4, waiting for transfers between devices, groups(): return lax.ppermute(piece, 'groups', [(0, 1), (1, 0)])  43.2 us
    ppermute x10, waiting for transfers between devices, over(): return lax.ppermute(piece, 'blk', [(i, i ^ bit) for i in range(count)])  35.1 us
    pallas_call x4, Pallas kernels, write_quarter(): pl.pallas_call(quarter_kernel, grid_spec=pltpu.PrefetchScalarGridSpec(num...  28.5 us
    ppermute x8, waiting for transfers between devices, moved(): lax.ppermute(value, 'blk', [(i, (i + steps) % count) for i in range(count)])  25 us
    all_to_all x1, starting transfers between devices, local(): got_rows = lax.all_to_all(sent_rows, 'blk', split_axis=0, concat_axis=0)  17 us
    ppermute x8, starting transfers between devices, moved(): lax.ppermute(value, 'blk', [(i, (i + steps) % count) for i in range(count)])  12.9 us
    all_gather x1, waiting for transfers between devices, weight_pieces(): lax.all_gather(lax.dynamic_slice_in_dim(weight, first, half, 0), 'blk', a...  11.4 us
    pallas_call x1, Pallas kernels, local(): shares = hidden_call(received, received, rows_all, place_all, starts)  8.75 us
  transfers between devices with their start and end apart: 28, of which 9 were waited for; matrix products, arithmetic and copies ran while one was open for 11% of the time, Pallas kernels for 16%

profile of v11, /device:TPU:1, one launch (start us, length us, event | category | flops | bytes accessed | tf_op | source)
XLA Modules:
  0.0 318.3 jit_solution(5716266168351392213)
XLA Ops:
  7.3 1.1 copy-done
  14.5 2.2 collective-permute-start
  16.7 2.1 collective-permute-start.1
  18.8 1.2 collective-permute-start.2
  24.2 2.6 shard_map.94.refs_0_
  26.7 16.4 %collective-permute-done.1 = bf16[16,9216]{1,0:T(8,128)(2,1)S(1)} collective-permute-done((bf16[16,9216]{1,0:T(8,128)(2,1)S(1)}, bf16[16,9216]{1,0:T(8,128)(2,1)S(1)}, u32[]{:S(2)}, u32[]{:S(2)}) %collective-permute-start.1) | collective-permute-done | bytes 294944 | tf_op jit(solution)/shard_map/ppermute | solution.py:21
  43.1 8.6 %collective-permute-done.2 = bf16[16,9216]{1,0:T(8,128)(2,1)S(1)} collective-permute-done((bf16[16,9216]{1,0:T(8,128)(2,1)S(1)}, bf16[16,9216]{1,0:T(8,128)(2,1)S(1)}, u32[]{:S(2)}, u32[]{:S(2)}) %collective-permute-start.2) | collective-permute-done | bytes 294944 | tf_op jit(solution)/shard_map/ppermute | solution.py:21
  52.5 11.4 %all-gather.3.cloned.1.call-done = bf16[1024,1024]{1,0:T(8,128)(2,1)} async-done(((bf16[256,1024]{1,0:T(8,128)(2,1)}), bf16[1024,1024]{1,0:T(8,128)(2,1)}) %all-gather.3.cloned.1.call-update) | async-done | bytes 2097168 | tf_op jit(solution)/shard_map/all_gather | solution.py:85
  63.8 3.1 fusion.32
  66.9 17.0 %all-to-all-start = ((bf16[16,64,512]{2,1,0:T(8,128)(2,1)}), bf16[16,64,512]{2,1,0:T(8,128)(2,1)S(1)}, u32[]{:S(2)}, u32[]{:S(2)}) async-start(bf16[16,64,512]{2,1,0:T(8,128)(2,1)} %shard_map.95), calls=%async_computation | async-start | bytes 2097152 | tf_op jit(solution)/shard_map/all_to_all | solution.py:436
  84.0 1.2 collective-permute-start.14
  85.2 1.4 collective-permute-start.4
  90.4 4.6 %shard_map.100.refs_0_ = bf16[16,240,512]{2,1,0:T(8,128)(2,1)} custom-call(bf16[192,8192]{1,0:T(8,128)(2,1)} %act.1, bf16[48,8192]{1,0:T(8,128)(2,1)} %bitcast.101), custom_call_target="tpu_custom_call" | custom-call | bytes 7864320 | tf_op jit(solution)/shard_map/pallas_call | solution.py:249
  95.0 13.9 %collective-permute-done.14.rest_2_.refs_2_ = bf16[4,128,1024]{2,1,0:T(8,128)(2,1)} collective-permute-done((bf16[4,128,1024]{2,1,0:T(8,128)(2,1)}, bf16[4,128,1024]{2,1,0:T(8,128)(2,1)}, u32[]{:S(2)}, u32[]{:S(2)}) %collective-permute-start.14) | collective-permute-done | bytes 1048608 | tf_op jit(solution)/shard_map/ppermute | solution.py:83
  108.9 11.1 %collective-permute-done.4.rest_0_.refs_3_ = bf16[4,128,1024]{2,1,0:T(8,128)(2,1)S(1)} collective-permute-done((bf16[4,128,1024]{2,1,0:T(8,128)(2,1)}, bf16[4,128,1024]{2,1,0:T(8,128)(2,1)S(1)}, u32[]{:S(2)}, u32[]{:S(2)}) %collective-permute-start.4) | collective-permute-done | bytes 1048608 | tf_op jit(solution)/shard_map/ppermute | solution.py:80
  122.0 5.6 %all-to-all-start.1 = ((bf16[16,240,512]{2,1,0:T(8,128)(2,1)}), bf16[16,240,512]{2,1,0:T(8,128)(2,1)}, u32[]{:S(2)}, u32[]{:S(2)}) async-start(bf16[16,240,512]{2,1,0:T(8,128)(2,1)} %shard_map.101), calls=%async_computation.1 | async-start | bytes 7864320 | tf_op jit(solution)/shard_map/all_to_all | solution.py:465
  137.4 1.2 collective-permute-start.16
  139.1 1.5 collective-permute-start.6
  143.4 18.9 %collective-permute-done.16.rest_3_ = bf16[4,128,1024]{2,1,0:T(8,128)(2,1)} collective-permute-done((bf16[4,128,1024]{2,1,0:T(8,128)(2,1)}, bf16[4,128,1024]{2,1,0:T(8,128)(2,1)}, u32[]{:S(2)}, u32[]{:S(2)}) %collective-permute-start.16) | collective-permute-done | bytes 1048608 | tf_op jit(solution)/shard_map/ppermute | solution.py:83
  162.3 1.2 collective-permute-start.8
  163.5 23.9 %collective-permute-done.6.rest_1_ = bf16[4,128,1024]{2,1,0:T(8,128)(2,1)} collective-permute-done((bf16[4,128,1024]{2,1,0:T(8,128)(2,1)}, bf16[4,128,1024]{2,1,0:T(8,128)(2,1)}, u32[]{:S(2)}, u32[]{:S(2)}) %collective-permute-start.6) | collective-permute-done | bytes 1048608 | tf_op jit(solution)/shard_map/ppermute | solution.py:80
  187.5 1.2 collective-permute-start.10
  189.8 1.1 fusion.1
  192.5 1.4 add.225.refs_0_
  194.5 1.5 reshape.311
  196.0 1.6 copy.33
  197.6 1.6 reshape.312.refs_0_
  199.3 1.5 convolution_convert_fusion.1
  201.5 10.4 %collective-permute-done.10.rest_3_ = bf16[4,128,1024]{2,1,0:T(8,128)(2,1)} collective-permute-done((bf16[4,128,1024]{2,1,0:T(8,128)(2,1)}, bf16[4,128,1024]{2,1,0:T(8,128)(2,1)}, u32[]{:S(2)}, u32[]{:S(2)}) %collective-permute-start.10) | collective-permute-done | bytes 1048608 | tf_op jit(solution)/shard_map/ppermute | solution.py:83
  211.9 1.5 collective-permute-start.11
  213.4 1.2 convolution_convert_fusion
  216.6 7.1 %shard_map.96 = (bf16[384,8192]{1,0:T(8,128)(2,1)}, f32[8,128]{1,0:T(8,128)}) custom-call(s32[2]{0:T(128)} %pad_add_fusion.3.where, bf16[384,1024]{1,0:T(8,128)(2,1)} %pad_maximum_fusion.cot, bf16[384,16]{1,0:T(8,128)(2,1)} %convolution_convert_fusion.2.grad, bf16[48,8192]{1,0:T(8,128)(2,1)} %pad_maximum_fusion.1.down, ...), custom_call_target="tpu_custom_call" | custom-call | flops 1610612736 | bytes 5767168 | tf_op jit(solution)/shard_map/pallas_call | solution.py:139
  223.7 7.1 %shard_map.97 = (bf16[384,8192]{1,0:T(8,128)(2,1)}, f32[8,128]{1,0:T(8,128)}) custom-call(s32[2]{0:T(128)} %pad_add_fusion.2.where, bf16[384,1024]{1,0:T(8,128)(2,1)} %pad_maximum_fusion.cot, bf16[384,16]{1,0:T(8,128)(2,1)} %convolution_convert_fusion.2.grad, bf16[48,8192]{1,0:T(8,128)(2,1)} %pad_maximum_fusion.1.down, ...), custom_call_target="tpu_custom_call", output_to_operand_aliasing={{0}: (8, {})} | custom-call | flops 1610612736 | bytes 5767168 | tf_op jit(solution)/shard_map/pallas_call | solution.py:139
  230.9 7.1 %shard_map.98 = (bf16[384,8192]{1,0:T(8,128)(2,1)}, f32[8,128]{1,0:T(8,128)}) custom-call(s32[2]{0:T(128)} %pad_add_fusion.1.where, bf16[384,1024]{1,0:T(8,128)(2,1)} %pad_maximum_fusion.cot, bf16[384,16]{1,0:T(8,128)(2,1)} %convolution_convert_fusion.2.grad, bf16[48,8192]{1,0:T(8,128)(2,1)} %pad_maximum_fusion.1.down, ...), custom_call_target="tpu_custom_call", output_to_operand_aliasing={{0}: (8, {})} | custom-call | flops 1610612736 | bytes 5767168 | tf_op jit(solution)/shard_map/pallas_call | solution.py:139
  238.0 1.4 broadcast_in_dim.113
  239.4 6.6 %all-to-all-start.2 = ((bf16[16,24,256]{2,1,0:T(8,128)(2,1)}), bf16[16,24,256]{2,1,0:T(8,128)(2,1)}, u32[]{:S(2)}, u32[]{:S(2)}) async-start(bf16[16,24,256]{2,1,0:T(8,128)(2,1)} %broadcast_in_dim.113), calls=%async_computation.2 | async-start | bytes 393216 | tf_op jit(solution)/shard_map/all_to_all | solution.py:27
  246.0 7.1 %shard_map.99 = (bf16[384,8192]{1,0:T(8,128)(2,1)}, f32[8,128]{1,0:T(8,128)}) custom-call(s32[2]{0:T(128)} %pad_add_fusion.where, bf16[384,1024]{1,0:T(8,128)(2,1)} %pad_maximum_fusion.cot, bf16[384,16]{1,0:T(8,128)(2,1)} %convolution_convert_fusion.2.grad, bf16[48,8192]{1,0:T(8,128)(2,1)} %pad_maximum_fusion.1.down, ...), custom_call_target="tpu_custom_call", output_to_operand_aliasing={{0}: (8, {})} | custom-call | flops 1610612736 | bytes 5767168 | tf_op jit(solution)/shard_map/pallas_call | solution.py:139
  253.1 8.7 %shard_map.104.refs_1_ = f32[256,384]{1,0:T(8,128)} custom-call(bf16[16,240,512]{2,1,0:T(8,128)(2,1)} %all-to-all-done.1.refs_1_.act.maps, bf16[16,240,512]{2,1,0:T(8,128)(2,1)} %all-to-all-done.1.refs_1_.act.maps, s32[1,3072]{1,0:T(1,128)} %reshape.318.rows.refs_0_, s32[1,3072]{1,0:T(1,128)} %shard_map.103.spots, s32[32,1]{1,0:T(8,128)} %copy.35.starts), custom_call_target="tpu_custom_call" | custom-call | flops 2415919104 | bytes 3145728 | tf_op jit(solution)/shard_map/pallas_call | solution.py:503
  261.9 1.9 copy.38
  263.8 6.0 %all-to-all-start.4 = ((f32[16,24,256]{2,1,0:T(8,128)}), f32[16,24,256]{2,1,0:T(8,128)S(1)}, u32[]{:S(2)}, u32[]{:S(2)}) async-start(f32[16,24,256]{2,1,0:T(8,128)} %bitcast.39), calls=%async_computation.4 | async-start | bytes 786432 | tf_op jit(solution)/shard_map/all_to_all | solution.py:507
  269.8 1.7 copy.34
  271.6 6.7 %shard_map.106 = bf16[768,512]{1,0:T(8,128)(2,1)} custom-call(bf16[16,240,512]{2,1,0:T(8,128)(2,1)} %all-to-all-done.1.refs_1_.act.maps, bf16[256,384]{1,0:T(8,128)(2,1)} %bitcast.113, s32[1,3072]{1,0:T(1,128)} %shard_map.105.rows, s32[1,3072]{1,0:T(1,128)} %shard_map.103.spots, s32[32,1]{1,0:T(8,128)} %copy.35.starts), custom_call_target="tpu_custom_call" | custom-call | flops 2415919104 | bytes 3145728 | tf_op jit(solution)/shard_map/pallas_call | solution.py:505
  278.3 3.4 %all-to-all-done.4 = f32[16,24,256]{2,1,0:T(8,128)S(1)} async-done(((f32[16,24,256]{2,1,0:T(8,128)}), f32[16,24,256]{2,1,0:T(8,128)S(1)}, u32[]{:S(2)}, u32[]{:S(2)}) %all-to-all-start.4) | async-done | bytes 393248 | tf_op jit(solution)/shard_map/all_to_all | solution.py:507
  281.7 3.8 %all-to-all-start.3 = ((bf16[16,48,512]{2,1,0:T(8,128)(2,1)}), bf16[16,48,512]{2,1,0:T(8,128)(2,1)S(1)}, u32[]{:S(2)}, u32[]{:S(2)}) async-start(bf16[16,48,512]{2,1,0:T(8,128)(2,1)} %bitcast.110), calls=%async_computation.3 | async-start | bytes 1572864 | tf_op jit(solution)/shard_map/all_to_all | solution.py:510
  286.5 1.9 select_add_fusion.1
  288.6 4.3 %collective-permute-start.19 = (f32[16,1024]{1,0:T(8,128)S(1)}, f32[16,1024]{1,0:T(8,128)S(1)}, u32[]{:S(2)}, u32[]{:S(2)}) collective-permute-start(f32[16,1024]{1,0:T(8,128)S(1)} %get-tuple-element.20), channel_id=1, source_target_pairs={{0,14},{1,15},{2,0},{3,1},{4,2},{5,3},{6,4},{7,5},{8,6},{9,7},{10,... | collective-permute-start | bytes 196616 | tf_op jit(solution)/shard_map/ppermute | solution.py:21
  292.9 1.6 collective-permute-start.20
  310.0 1.4 reshape.317
  (122 shorter events, 27.6 us)
Async XLA Ops:
  7.2 1.2 copy-start
  7.2 2.1 copy-start.18
  7.2 7.2 %copy-start.10 = (bf16[3,16,1024]{2,1,0:T(8,128)(2,1)S(1)}, bf16[3,16,1024]{2,1,0:T(8,128)(2,1)}, u32[]{:S(2)}) copy-start(bf16[3,16,1024]{2,1,0:T(8,128)(2,1)} %param.13) | copy-start | bytes 294916
  7.2 16.4 %copy-start.17 = (s32[192]{0:T(256)S(1)}, s32[192]{0:T(256)}, u32[]{:S(2)}) copy-start(s32[192]{0:T(256)} %param.9) | copy-start | bytes 2308
  7.2 56.6 %all-gather.3.cloned.1.call-start = ((), (), s32[]{:S(2)}) async-start(), calls=%async_computation.5 | async-start | bytes 2621440 | tf_op jit(solution)/shard_map/all_gather | solution.py:85
  14.5 12.2 %collective-permute-start = (bf16[16,9216]{1,0:T(8,128)(2,1)S(1)}, bf16[16,9216]{1,0:T(8,128)(2,1)S(1)}, u32[]{:S(2)}, u32[]{:S(2)}) collective-permute-start(bf16[16,9216]{1,0:T(8,128)(2,1)S(1)} %pad_maximum_fusion.2), channel_id=1, source_target_pairs={{0,4},{1,5},{2,6},{3,7},{4,8},{5,9},{6,10},{7,11},{8,12},{9,13},{1... | collective-permute-start | bytes 884744 | tf_op jit(solution)/shard_map/ppermute | solution.py:21
  16.7 26.4 %collective-permute-start.1 = (bf16[16,9216]{1,0:T(8,128)(2,1)S(1)}, bf16[16,9216]{1,0:T(8,128)(2,1)S(1)}, u32[]{:S(2)}, u32[]{:S(2)}) collective-permute-start(bf16[16,9216]{1,0:T(8,128)(2,1)S(1)} %pad_maximum_fusion.2), channel_id=1, source_target_pairs={{0,3},{1,4},{2,5},{3,6},{4,7},{5,8},{6,9},{7,10},{8,11},{9,12},{10... | collective-permute-start | bytes 884744 | tf_op jit(solution)/shard_map/ppermute | solution.py:21
  18.8 32.9 %collective-permute-start.2 = (bf16[16,9216]{1,0:T(8,128)(2,1)S(1)}, bf16[16,9216]{1,0:T(8,128)(2,1)S(1)}, u32[]{:S(2)}, u32[]{:S(2)}) collective-permute-start(bf16[16,9216]{1,0:T(8,128)(2,1)S(1)} %pad_maximum_fusion.2), channel_id=1, source_target_pairs={{0,2},{1,3},{2,4},{3,5},{4,6},{5,7},{6,8},{7,9},{8,10},{9,11},{10,... | collective-permute-start | bytes 884744 | tf_op jit(solution)/shard_map/ppermute | solution.py:21
  20.0 31.7 %collective-permute-start.3 = (bf16[16,9216]{1,0:T(8,128)(2,1)S(1)}, bf16[16,9216]{1,0:T(8,128)(2,1)S(1)}, u32[]{:S(2)}, u32[]{:S(2)}) collective-permute-start(bf16[16,9216]{1,0:T(8,128)(2,1)S(1)} %pad_maximum_fusion.2), channel_id=1, source_target_pairs={{0,1},{1,2},{2,3},{3,4},{4,5},{5,6},{6,7},{7,8},{8,9},{9,10},{10,1... | collective-permute-start | bytes 884744 | tf_op jit(solution)/shard_map/ppermute | solution.py:21
  66.9 53.1 %all-to-all-start = ((bf16[16,64,512]{2,1,0:T(8,128)(2,1)}), bf16[16,64,512]{2,1,0:T(8,128)(2,1)S(1)}, u32[]{:S(2)}, u32[]{:S(2)}) async-start(bf16[16,64,512]{2,1,0:T(8,128)(2,1)} %shard_map.95), calls=%async_computation | async-start | bytes 2097152 | tf_op jit(solution)/shard_map/all_to_all | solution.py:436
  84.0 24.9 %collective-permute-start.14 = (bf16[4,128,1024]{2,1,0:T(8,128)(2,1)}, bf16[4,128,1024]{2,1,0:T(8,128)(2,1)}, u32[]{:S(2)}, u32[]{:S(2)}) collective-permute-start(bf16[4,128,1024]{2,1,0:T(8,128)(2,1)} %get-tuple-element.32.refs_1_.rest_0_), channel_id=1, source_target_pairs={{0,16},{16,0},{1,17},{17,1},{2,18},{18,2},{3,19},{19,3},{4,20},{20... | collective-permute-start | bytes 3145736 | tf_op jit(solution)/shard_map/ppermute | solution.py:83
  85.2 34.8 %collective-permute-start.4 = (bf16[4,128,1024]{2,1,0:T(8,128)(2,1)}, bf16[4,128,1024]{2,1,0:T(8,128)(2,1)S(1)}, u32[]{:S(2)}, u32[]{:S(2)}) collective-permute-start(bf16[4,128,1024]{2,1,0:T(8,128)(2,1)} %get-tuple-element.32.refs_1_.rest_0_), channel_id=1, source_target_pairs={{0,2},{1,3},{2,0},{3,1},{4,6},{5,7},{6,4},{7,5},{8,10},{9,11},{10,... | collective-permute-start | bytes 3145736 | tf_op jit(solution)/shard_map/ppermute | solution.py:80
  120.0 1.0 copy-start.4
  121.0 1.0 copy-start.1
  122.0 13.7 %copy-start.8 = (bf16[16,9216]{1,0:T(8,128)(2,1)S(1)}, bf16[16,9216]{1,0:T(8,128)(2,1)}, u32[]{:S(2)}) copy-start(bf16[16,9216]{1,0:T(8,128)(2,1)} %select_select_fusion.refs_3_) | copy-start | bytes 884740
  122.0 14.4 %copy-start.3 = (bf16[3,16,8192]{2,1,0:T(8,128)(2,1)S(1)}, bf16[3,16,8192]{2,1,0:T(8,128)(2,1)}, u32[]{:S(2)}) copy-start(bf16[3,16,8192]{2,1,0:T(8,128)(2,1)} %param.12) | copy-start | bytes 2359300
  122.0 116.0 %all-to-all-start.1 = ((bf16[16,240,512]{2,1,0:T(8,128)(2,1)}), bf16[16,240,512]{2,1,0:T(8,128)(2,1)}, u32[]{:S(2)}, u32[]{:S(2)}) async-start(bf16[16,240,512]{2,1,0:T(8,128)(2,1)} %shard_map.101), calls=%async_computation.1 | async-start | bytes 7864320 | tf_op jit(solution)/shard_map/all_to_all | solution.py:465
  136.4 5.1 %copy-start.2 = (bf16[16,64,512]{2,1,0:T(8,128)(2,1)S(1)}, bf16[16,64,512]{2,1,0:T(8,128)(2,1)}, u32[]{:S(2)}) copy-start(bf16[16,64,512]{2,1,0:T(8,128)(2,1)} %copy-done.1) | copy-start | bytes 3145732
  136.4 25.9 %copy-start.5 = (bf16[4,128,1024]{2,1,0:T(8,128)(2,1)S(1)}, bf16[4,128,1024]{2,1,0:T(8,128)(2,1)}, u32[]{:S(2)}) copy-start(bf16[4,128,1024]{2,1,0:T(8,128)(2,1)} %copy-done.4) | copy-start | bytes 3145732
  137.4 24.9 %collective-permute-start.16 = (bf16[4,128,1024]{2,1,0:T(8,128)(2,1)}, bf16[4,128,1024]{2,1,0:T(8,128)(2,1)}, u32[]{:S(2)}, u32[]{:S(2)}) collective-permute-start(bf16[4,128,1024]{2,1,0:T(8,128)(2,1)} %get-tuple-element.31.refs_2_.rest_1_), channel_id=1, source_target_pairs={{0,16},{16,0},{1,17},{17,1},{2,18},{18,2},{3,19},{19,3},{4,20},{20... | collective-permute-start | bytes 3145736 | tf_op jit(solution)/shard_map/ppermute | solution.py:83
  138.6 52.3 %collective-permute-start.12 = (bf16[4,128,1024]{2,1,0:T(8,128)(2,1)}, bf16[4,128,1024]{2,1,0:T(8,128)(2,1)}, u32[]{:S(2)}, u32[]{:S(2)}) collective-permute-start(bf16[4,128,1024]{2,1,0:T(8,128)(2,1)} %get-tuple-element.32.refs_1_.rest_0_), channel_id=1, source_target_pairs={{0,1},{1,0},{2,3},{3,2},{4,5},{5,4},{6,7},{7,6},{8,9},{9,8},{10,11... | collective-permute-start | bytes 3145736 | tf_op jit(solution)/shard_map/ppermute | solution.py:80
  139.1 61.7 %collective-permute-start.13 = (bf16[4,128,1024]{2,1,0:T(8,128)(2,1)}, bf16[4,128,1024]{2,1,0:T(8,128)(2,1)}, u32[]{:S(2)}, u32[]{:S(2)}) collective-permute-start(bf16[4,128,1024]{2,1,0:T(8,128)(2,1)} %get-tuple-element.31.refs_2_.rest_1_), channel_id=1, source_target_pairs={{0,1},{1,0},{2,3},{3,2},{4,5},{5,4},{6,7},{7,6},{8,9},{9,8},{10,11... | collective-permute-start | bytes 3145736 | tf_op jit(solution)/shard_map/ppermute | solution.py:80
  139.1 48.3 %collective-permute-start.6 = (bf16[4,128,1024]{2,1,0:T(8,128)(2,1)}, bf16[4,128,1024]{2,1,0:T(8,128)(2,1)}, u32[]{:S(2)}, u32[]{:S(2)}) collective-permute-start(bf16[4,128,1024]{2,1,0:T(8,128)(2,1)} %get-tuple-element.31.refs_2_.rest_1_), channel_id=1, source_target_pairs={{0,2},{1,3},{2,0},{3,1},{4,6},{5,7},{6,4},{7,5},{8,10},{9,11},{10,... | collective-permute-start | bytes 3145736 | tf_op jit(solution)/shard_map/ppermute | solution.py:80
  140.6 60.2 %collective-permute-start.15 = (bf16[4,128,1024]{2,1,0:T(8,128)(2,1)}, bf16[4,128,1024]{2,1,0:T(8,128)(2,1)}, u32[]{:S(2)}, u32[]{:S(2)}) collective-permute-start(bf16[4,128,1024]{2,1,0:T(8,128)(2,1)} %collective-permute-done.14.rest_2_.refs_2_), channel_id=1, source_target_pairs={{0,1},{1,0},{2,3},{3,2},{4,5},{5,4},{6,7},{7,6},{8,9},{9,8},{10,11... | collective-permute-start | bytes 3145736 | tf_op jit(solution)/shard_map/ppermute | solution.py:80
  143.3 45.4 %copy-start.14 = (s32[384]{0:T(512)S(1)}, s32[384]{0:T(512)}, u32[]{:S(2)}) copy-start(s32[384]{0:T(512)} %sub.76) | copy-start | bytes 4612
  143.4 45.3 %copy-start.6 = (bf16[16,24,512]{2,1,0:T(8,128)(2,1)}, bf16[16,24,512]{2,1,0:T(8,128)(2,1)S(1)}, u32[]{:S(2)}) copy-start(bf16[16,24,512]{2,1,0:T(8,128)(2,1)S(1)} %get-tuple-element.36) | copy-start | bytes 1179652
  162.3 39.1 %collective-permute-start.8 = (bf16[4,128,1024]{2,1,0:T(8,128)(2,1)S(1)}, bf16[4,128,1024]{2,1,0:T(8,128)(2,1)S(1)}, u32[]{:S(2)}, u32[]{:S(2)}) collective-permute-start(bf16[4,128,1024]{2,1,0:T(8,128)(2,1)S(1)} %copy-done.5), channel_id=1, source_target_pairs={{0,16},{16,0},{1,17},{17,1},{2,18},{18,2},{3,19},{19,3},{4,20},{20... | collective-permute-start | bytes 3145736 | tf_op jit(solution)/shard_map/ppermute | solution.py:83
  187.5 24.4 %collective-permute-start.10 = (bf16[4,128,1024]{2,1,0:T(8,128)(2,1)}, bf16[4,128,1024]{2,1,0:T(8,128)(2,1)}, u32[]{:S(2)}, u32[]{:S(2)}) collective-permute-start(bf16[4,128,1024]{2,1,0:T(8,128)(2,1)} %collective-permute-done.6.rest_1_), channel_id=1, source_target_pairs={{0,16},{16,0},{1,17},{17,1},{2,18},{18,2},{3,19},{19,3},{4,20},{20... | collective-permute-start | bytes 3145736 | tf_op jit(solution)/shard_map/ppermute | solution.py:83
  188.7 3.8 %copy-start.12 = (s32[384]{0:T(512)}, s32[384]{0:T(512)S(1)}, u32[]{:S(2)}) copy-start(s32[384]{0:T(512)S(1)} %add_select_fusion) | copy-start | bytes 4612
  190.9 32.9 %collective-permute-start.17 = (bf16[4,128,1024]{2,1,0:T(8,128)(2,1)}, bf16[4,128,1024]{2,1,0:T(8,128)(2,1)}, u32[]{:S(2)}, u32[]{:S(2)}) collective-permute-start(bf16[4,128,1024]{2,1,0:T(8,128)(2,1)} %collective-permute-done.16.rest_3_), channel_id=1, source_target_pairs={{0,1},{1,0},{2,3},{3,2},{4,5},{5,4},{6,7},{7,6},{8,9},{9,8},{10,11... | collective-permute-start | bytes 3145736 | tf_op jit(solution)/shard_map/ppermute | solution.py:80
  199.3 16.3 %copy-start.11 = (bf16[384,16]{0,1:T(8,128)(2,1)S(1)}, bf16[384,16]{0,1:T(8,128)(2,1)}, u32[]{:S(2)}) copy-start(bf16[384,16]{0,1:T(8,128)(2,1)} %slice_add_fusion) | copy-start | bytes 36868
  199.3 16.3 %copy-start.15 = (s32[384]{0:T(512)S(1)}, s32[384]{0:T(512)}, u32[]{:S(2)}) copy-start(s32[384]{0:T(512)} %sub.76) | copy-start | bytes 4612
  200.8 45.2 %collective-permute-start.5 = (bf16[4,128,1024]{2,1,0:T(8,128)(2,1)S(1)}, bf16[4,128,1024]{2,1,0:T(8,128)(2,1)}, u32[]{:S(2)}, u32[]{:S(2)}) collective-permute-start(bf16[4,128,1024]{2,1,0:T(8,128)(2,1)S(1)} %copy-done.5), channel_id=1, source_target_pairs={{0,1},{1,0},{2,3},{3,2},{4,5},{5,4},{6,7},{7,6},{8,9},{9,8},{10,11... | collective-permute-start | bytes 3145736 | tf_op jit(solution)/shard_map/ppermute | solution.py:80
  200.9 45.1 %collective-permute-start.7 = (bf16[4,128,1024]{2,1,0:T(8,128)(2,1)}, bf16[4,128,1024]{2,1,0:T(8,128)(2,1)}, u32[]{:S(2)}, u32[]{:S(2)}) collective-permute-start(bf16[4,128,1024]{2,1,0:T(8,128)(2,1)} %collective-permute-done.6.rest_1_), channel_id=1, source_target_pairs={{0,1},{1,0},{2,3},{3,2},{4,5},{5,4},{6,7},{7,6},{8,9},{9,8},{10,11... | collective-permute-start | bytes 3145736 | tf_op jit(solution)/shard_map/ppermute | solution.py:80
  201.4 22.4 %copy-start.9 = (bf16[4,128,1024]{2,1,0:T(8,128)(2,1)}, bf16[4,128,1024]{2,1,0:T(8,128)(2,1)S(1)}, u32[]{:S(2)}) copy-start(bf16[4,128,1024]{2,1,0:T(8,128)(2,1)S(1)} %collective-permute-done.8.rest_2_) | copy-start | bytes 3145732
  201.4 44.6 %collective-permute-start.9 = (bf16[4,128,1024]{2,1,0:T(8,128)(2,1)S(1)}, bf16[4,128,1024]{2,1,0:T(8,128)(2,1)}, u32[]{:S(2)}, u32[]{:S(2)}) collective-permute-start(bf16[4,128,1024]{2,1,0:T(8,128)(2,1)S(1)} %collective-permute-done.8.rest_2_), channel_id=1, source_target_pairs={{0,1},{1,0},{2,3},{3,2},{4,5},{5,4},{6,7},{7,6},{8,9},{9,8},{10,11... | collective-permute-start | bytes 3145736 | tf_op jit(solution)/shard_map/ppermute | solution.py:80
  211.9 34.2 %collective-permute-start.11 = (bf16[4,128,1024]{2,1,0:T(8,128)(2,1)}, bf16[4,128,1024]{2,1,0:T(8,128)(2,1)}, u32[]{:S(2)}, u32[]{:S(2)}) collective-permute-start(bf16[4,128,1024]{2,1,0:T(8,128)(2,1)} %collective-permute-done.10.rest_3_), channel_id=1, source_target_pairs={{0,1},{1,0},{2,3},{3,2},{4,5},{5,4},{6,7},{7,6},{8,9},{9,8},{10,11... | collective-permute-start | bytes 3145736 | tf_op jit(solution)/shard_map/ppermute | solution.py:80
  239.4 24.4 %all-to-all-start.2 = ((bf16[16,24,256]{2,1,0:T(8,128)(2,1)}), bf16[16,24,256]{2,1,0:T(8,128)(2,1)}, u32[]{:S(2)}, u32[]{:S(2)}) async-start(bf16[16,24,256]{2,1,0:T(8,128)(2,1)} %broadcast_in_dim.113), calls=%async_computation.2 | async-start | bytes 393216 | tf_op jit(solution)/shard_map/all_to_all | solution.py:27
  263.8 17.9 %all-to-all-start.4 = ((f32[16,24,256]{2,1,0:T(8,128)}), f32[16,24,256]{2,1,0:T(8,128)S(1)}, u32[]{:S(2)}, u32[]{:S(2)}) async-start(f32[16,24,256]{2,1,0:T(8,128)} %bitcast.39), calls=%async_computation.4 | async-start | bytes 786432 | tf_op jit(solution)/shard_map/all_to_all | solution.py:507
  278.3 7.7 %copy-start.7 = (bf16[16,24,512]{2,1,0:T(8,128)(2,1)S(1)}, bf16[16,24,512]{2,1,0:T(8,128)(2,1)}, u32[]{:S(2)}) copy-start(bf16[16,24,512]{2,1,0:T(8,128)(2,1)} %copy-done.6) | copy-start | bytes 1179652
  278.3 7.7 %copy-start.13 = (s32[384]{0:T(512)S(1)}, s32[384]{0:T(512)}, u32[]{:S(2)}) copy-start(s32[384]{0:T(512)} %copy-done.12) | copy-start | bytes 4612
  278.3 7.7 %copy-start.16 = (s32[48]{0:T(128)S(1)}, s32[48]{0:T(128)}, u32[]{:S(2)}) copy-start(s32[48]{0:T(128)} %and_select_fusion) | copy-start | bytes 580
  281.7 27.2 %all-to-all-start.3 = ((bf16[16,48,512]{2,1,0:T(8,128)(2,1)}), bf16[16,48,512]{2,1,0:T(8,128)(2,1)S(1)}, u32[]{:S(2)}, u32[]{:S(2)}) async-start(bf16[16,48,512]{2,1,0:T(8,128)(2,1)} %bitcast.110), calls=%async_computation.3 | async-start | bytes 1572864 | tf_op jit(solution)/shard_map/all_to_all | solution.py:510
  288.4 19.7 %collective-permute-start.18 = (f32[16,1024]{1,0:T(8,128)S(1)}, f32[16,1024]{1,0:T(8,128)S(1)}, u32[]{:S(2)}, u32[]{:S(2)}) collective-permute-start(f32[16,1024]{1,0:T(8,128)S(1)} %get-tuple-element.20), channel_id=1, source_target_pairs={{0,15},{1,0},{2,1},{3,2},{4,3},{5,4},{6,5},{7,6},{8,7},{9,8},{10,9... | collective-permute-start | bytes 196616 | tf_op jit(solution)/shard_map/ppermute | solution.py:21
  288.6 19.5 %collective-permute-start.19 = (f32[16,1024]{1,0:T(8,128)S(1)}, f32[16,1024]{1,0:T(8,128)S(1)}, u32[]{:S(2)}, u32[]{:S(2)}) collective-permute-start(f32[16,1024]{1,0:T(8,128)S(1)} %get-tuple-element.20), channel_id=1, source_target_pairs={{0,14},{1,15},{2,0},{3,1},{4,2},{5,3},{6,4},{7,5},{8,6},{9,7},{10,... | collective-permute-start | bytes 196616 | tf_op jit(solution)/shard_map/ppermute | solution.py:21
  292.9 15.2 %collective-permute-start.20 = (f32[16,1024]{1,0:T(8,128)S(1)}, f32[16,1024]{1,0:T(8,128)S(1)}, u32[]{:S(2)}, u32[]{:S(2)}) collective-permute-start(f32[16,1024]{1,0:T(8,128)S(1)} %get-tuple-element.20), channel_id=1, source_target_pairs={{0,13},{1,14},{2,15},{3,0},{4,1},{5,2},{6,3},{7,4},{8,5},{9,6},{10... | collective-permute-start | bytes 196616 | tf_op jit(solution)/shard_map/ppermute | solution.py:21
  294.6 13.5 %collective-permute-start.21 = (f32[16,1024]{1,0:T(8,128)S(1)}, f32[16,1024]{1,0:T(8,128)S(1)}, u32[]{:S(2)}, u32[]{:S(2)}) collective-permute-start(f32[16,1024]{1,0:T(8,128)S(1)} %get-tuple-element.20), channel_id=1, source_target_pairs={{0,12},{1,13},{2,14},{3,15},{4,0},{5,1},{6,2},{7,3},{8,4},{9,5},{1... | collective-permute-start | bytes 196616 | tf_op jit(solution)/shard_map/ppermute | solution.py:21
Sparse Core Ops, SparseCore 0:
  10.2 53.6 all-gather.2

commit v12 on v11

--- a/solution.py
+++ b/solution.py
@@ -66,7 +66,7 @@
     return (high * DIGIT + middle) * DIGIT + low, place_high * DIGIT + place
 
 
-CHUNKS = 2
+CHUNKS = 1
 
 
 def weight_pieces(weight):
@@ -95,8 +95,7 @@
 
 def quarter_kernel(where, cot, grad, down, *rest):
     pieces = rest[: 2 * CHUNKS]
-    out, token = rest[-2:]
-    token[...] = jnp.zeros_like(token)
+    out = rest[-1]
     rank = grad.shape[1]
     lora = [
         adapter_scale
@@ -142,15 +141,9 @@
             num_scalar_prefetch=1,
             grid=(shards,),
             in_specs=specs,
-            out_specs=[
-                pl.BlockSpec((rows, stripe), lambda j, where: (0, 4 * j + where[0])),
-                pl.BlockSpec((8, LANES), lambda j, where: (0, 0)),
-            ],
+            out_specs=pl.BlockSpec((rows, stripe), lambda j, where: (0, 4 * j + where[0])),
         ),
-        out_shape=[
-            jax.ShapeDtypeStruct((rows, width), jnp.bfloat16),
-            jax.ShapeDtypeStruct((8, LANES), jnp.float32),
-        ],
+        out_shape=jax.ShapeDtypeStruct((rows, width), jnp.bfloat16),
         input_output_aliases=alias,
         cost_estimate=pl.CostEstimate(
             flops=2 * rows * depth * stripe * shards,
@@ -172,9 +165,8 @@
     return weight.reshape(-1, depth)
 
 
-def rows_kernel(rows, cot, out, place):
-    devices, packed, features = out.shape
-    shared = packed - 16
+def rows_kernel(rows, cot, out, digits_out, place):
+    devices, shared, features = out.shape
     folds = cot.shape[1] // features
     cap = shared // folds
     target = rows[...] // (cap * devices)
@@ -189,15 +181,13 @@
     digits = jnp.zeros((16, features), jnp.int32)
     for k, digit in enumerate(as_digits(rows[...], place[...])):
         digits = jnp.where(which == k, digit, digits)
-    digits = digits.astype(jnp.float32).astype(out.dtype)
+    digits_out[...] = digits.astype(jnp.float32).astype(out.dtype)
     send = placing(place[:, : cot.shape[0]], cap * devices)
     for f in range(folds):
         sent = dot(send, cot[:, f * features : (f + 1) * features], ((1,), (0,)))
         for k in range(devices):
             some = sent[k * cap : (k + 1) * cap].astype(out.dtype)
             out[k, f * cap : (f + 1) * cap, :] = some
-    for k in range(devices):
-        out[k, shared:, :] = digits
 
 
 def pack_rows(rows, cot, devices, cap, features):
@@ -207,7 +197,10 @@
         padding = jnp.full((features - tokens,), 16 * cap * devices, jnp.int32)
         return pl.pallas_call(
             rows_kernel,
-            out_shape=jax.ShapeDtypeStruct((devices, folds * cap + 16, features), cot.dtype),
+            out_shape=[
+                jax.ShapeDtypeStruct((devices, folds * cap, features), cot.dtype),
+                jax.ShapeDtypeStruct((16, features), cot.dtype),
+            ],
             scratch_shapes=[pltpu.VMEM((1, features), jnp.int32)],
             cost_estimate=pl.CostEstimate(
                 flops=2 * devices * cap * tokens * cot.shape[1],
@@ -227,23 +220,24 @@
     digits = jnp.pad(digits, ((0, 0), (0, -tokens % features))).reshape(-1, features)
     digits = jnp.pad(digits, ((0, -digits.shape[0] % 16), (0, 0)))
     parts = [sent[:, :, k : k + features] for k in range(0, cot.shape[1], features)]
-    parts += [jnp.broadcast_to(digits[None], (devices,) + digits.shape)]
-    return jnp.concatenate(parts, axis=1)
-
-
-def features_kernel(act, maps, out):
+    return jnp.concatenate(parts, axis=1), digits
+
+
+def features_kernel(act, maps, digits, out):
     targets, _, features = out.shape
-    tokens = act.shape[0]
+    tokens, shared = act.shape[0], maps.shape[0]
     for k in range(targets):
         part = slice(k * features, (k + 1) * features)
         out[k, :tokens, :] = act[:, part]
-        out[k, tokens:, :] = maps[:, part]
-
-
-def pack_features(act, maps, devices):
+        out[k, tokens : tokens + shared, :] = maps[:, part]
+        out[k, tokens + shared :, :] = digits[...]
+
+
+def pack_features(act, maps, digits, devices):
     tokens, width = act.shape
     features = width // devices
     shared = maps.shape[0]
+    total = tokens + shared + digits.shape[0]
     targets = 4
     if features % LANES == 0:
         return pl.pallas_call(
@@ -252,16 +246,19 @@
             in_specs=[
                 pl.BlockSpec((tokens, targets * features), lambda j: (0, j)),
                 pl.BlockSpec((shared, targets * features), lambda j: (0, j)),
+                pl.BlockSpec(digits.shape, lambda j: (0, 0)),
             ],
-            out_specs=pl.BlockSpec((targets, tokens + shared, features), lambda j: (j, 0, 0)),
-            out_shape=jax.ShapeDtypeStruct((devices, tokens + shared, features), act.dtype),
+            out_specs=pl.BlockSpec((targets, total, features), lambda j: (j, 0, 0)),
+            out_shape=jax.ShapeDtypeStruct((devices, total, features), act.dtype),
             cost_estimate=pl.CostEstimate(
-                flops=0, bytes_accessed=4 * (tokens + shared) * width, transcendentals=0
+                flops=0, bytes_accessed=4 * total * width, transcendentals=0
             ),
             compiler_params=pltpu.CompilerParams(vmem_limit_bytes=VMEM),
-        )(act, maps)
+        )(act, maps, digits)
     both = jnp.concatenate([act, maps], axis=0)
-    return both.reshape(tokens + shared, devices, features).transpose(1, 0, 2)
+    both = both.reshape(tokens + shared, devices, features).transpose(1, 0, 2)
+    copies = jnp.broadcast_to(digits[None], (devices,) + digits.shape)
+    return jnp.concatenate([both, copies], axis=1)
 
 
 def slot_chunks(width):
@@ -300,7 +297,8 @@
 
 def hidden_kernel(act, maps, rows, spots, starts, out):
     sources, share, width = act.shape[0], maps.shape[1], rows.shape[1]
-    rank, places = out.shape[0] // sources, out.shape[1]
+    _, height, places = out.shape
+    rank = height // sources
     slot = slot_of(rows[...], starts[...])
     every = all_rows(act, width // sources)
     total = jnp.zeros((rank, width), jnp.float32)
@@ -309,11 +307,12 @@
         some = maps[part.start // share : part.stop // share].reshape(size, -1)
         each = dot(some, every, ((1,), (1,))).reshape(size // rank, rank, -1)
         total += jnp.sum(jnp.where(own_rows(slot, part.start, size, rank), each, 0.0), axis=0)
-    total = jnp.where(of_source(sources, width), total[None], 0.0).reshape(out.shape[0], width)
+    total = jnp.where(of_source(sources, width), total[None], 0.0).reshape(height, width)
     high = total.astype(jnp.bfloat16)
     low = (total - high.astype(jnp.float32)).astype(jnp.bfloat16)
     place = placing(spots[...], places)
-    out[...] = dot(high, place, ((1,), (1,))) + dot(low, place, ((1,), (1,)))
+    for k, part in enumerate((high, low)):
+        out[k] = dot(part, place, ((1,), (1,))).astype(out.dtype)
 
 
 def down_kernel(act, grad, rows, spots, starts, out, total):
@@ -361,8 +360,8 @@
         hidden_kernel,
         grid=grid,
         in_specs=[act, maps, rows, rows, begin],
-        out_specs=placed,
-        out_shape=jax.ShapeDtypeStruct((devices * rank, places), jnp.float32),
+        out_specs=pl.BlockSpec((2, sources * rank, places), lambda j: (0, j, 0)),
+        out_shape=jax.ShapeDtypeStruct((2, devices * rank, places), received.dtype),
         cost_estimate=cost,
         compiler_params=params,
     )
@@ -430,18 +429,22 @@
     down_blocks = of_blocks(adapter_down_maps, carried[:, :width])
     up_blocks = of_blocks(adapter_up_maps, carried[:, width:])
 
-    sent_rows = pack_rows(token_layout_row, cotangent, devices, cap, features)
+    sent_cot, digits = pack_rows(token_layout_row, cotangent, devices, cap, features)
+    flat_maps = adapter_down_maps.reshape(share, width)
+    received = pack_features(activations, flat_maps, digits, devices)
+    received = lax.all_to_all(received, "blk", split_axis=0, concat_axis=0)
+    per_digit = -(-tokens // features)
+    digits = received[:, tokens + share : tokens + share + 5 * per_digit]
+    digits = digits.reshape(devices, 5, per_digit * features)[:, :, :tokens]
+    rows_all, place_all = from_digits(digits)
+
     own, _, across, _ = pieces
-    sent_rows = after(sent_rows, own[0], own[1], carried)
-    got_rows = lax.all_to_all(sent_rows, "blk", split_axis=0, concat_axis=0)
+    sent_cot = after(sent_cot, received, own[CHUNKS], across[0])
+    got_cot = lax.all_to_all(sent_cot, "blk", split_axis=0, concat_axis=0)
     recv_cot = [
-        got_rows[:, k * cap : (k + 1) * cap].reshape(resident_rows, features)
+        got_cot[:, k * cap : (k + 1) * cap].reshape(resident_rows, features)
         for k in range(out_width // features)
     ]
-    per_digit = -(-tokens // features)
-    digits = got_rows[:, share : share + 5 * per_digit]
-    digits = digits.reshape(devices, 5, per_digit * features)[:, :, :tokens]
-    rows_all, place_all = from_digits(digits)
 
     spots = device * cap + jnp.arange(cap, dtype=jnp.int32)
     hit = place_all[:, None, :] == spots[None, :, None]
@@ -459,12 +462,6 @@
     grad_in = sum(grad_in[:, b * rank : (b + 1) * rank] for b in range(resident))
     grad_sent = grad_in.reshape(devices, cap, rank).transpose(1, 0, 2).reshape(cap, -1)
 
-    flat_maps = adapter_down_maps.reshape(share, width)
-    received = pack_features(activations, flat_maps, devices)
-    received = after(received, got_rows, own[CHUNKS], across[0])
-    received = lax.all_to_all(received, "blk", split_axis=0, concat_axis=0)
-    grad_all = to_all(after(grad_sent, received)).reshape(resident_rows, -1).T
-
     rows_all, place_all = rows_all.reshape(1, -1), place_all.reshape(1, -1)
 
     cot_rows = jnp.concatenate(
@@ -476,12 +473,8 @@
     firsts = [quarter, quarter ^ 1, quarter ^ 2, quarter ^ 3]
     if own[0].shape[1] % LANES == 0:
         out = None
-        for number, (piece, first) in enumerate(zip(pieces, firsts)):
-            out, token = write_quarter(
-                piece, first, group, cot_rows, grad_rows, down_blocks, out
-            )
-            if number == 3:
-                place_all = after(place_all, token)
+        for piece, first in zip(pieces, firsts):
+            out = write_quarter(piece, first, group, cot_rows, grad_rows, down_blocks, out)
     else:
         weight = together(pieces, firsts, group)
         lora = [
@@ -501,12 +494,18 @@
         received, tokens, share, rank, resident_rows, starts.shape[0]
     )
     shares = hidden_call(received, received, rows_all, place_all, starts)
-    rows_all = after(rows_all, shares)
+
+    shares = shares.reshape(-1, resident_rows).T.reshape(devices, cap, -1)
+    copies = jnp.broadcast_to(grad_sent[None], (devices,) + grad_sent.shape)
+    small = jnp.concatenate([copies, shares], axis=2)
+    small = lax.all_to_all(small, "blk", split_axis=0, concat_axis=0)
+    each = devices * rank
+    grad_all = small[:, :, :each].reshape(resident_rows, each).T
+    hidden = jnp.sum(small[:, :, each:].astype(jnp.float32), axis=0)
+    hidden = (hidden[:, :each] + hidden[:, each:]).astype(jnp.bfloat16)
+    hidden = hidden.reshape(cap, devices, rank).transpose(1, 0, 2).reshape(-1, rank)
+
     down_f = down_call(received, grad_all, rows_all, place_all, starts)
-    hidden = shares.T.reshape(devices, cap, -1)
-    hidden = lax.all_to_all(hidden, "blk", split_axis=0, concat_axis=0)
-    hidden = jnp.sum(hidden, axis=0).astype(jnp.bfloat16)
-    hidden = hidden.reshape(cap, devices, rank).transpose(1, 0, 2).reshape(-1, rank)
     down_home = lax.all_to_all(down_f, "blk", split_axis=0, concat_axis=1, tiled=True)
     down_map_gradient = down_home.astype(jnp.float32).reshape(resident, rank, width)
 

time: 321 us -> 376 us (1.17)
  waiting for transfers between devices: 118 us -> 177 us
  local copies, waits for them, and re-layouts: 26.5 us -> 18.5 us
    all_gather x1, waiting for transfers between devices: 11.4 us -> 62.2 us  [weight_pieces(): lax.all_gather(lax.dynamic_slice_in_dim(weight, first, half, 0), 'blk', a...]
    ppermute x10 -> x5, waiting for transfers between devices: 35.1 us -> 41.7 us  [over(): return lax.ppermute(piece, 'blk', [(i, i ^ bit) for i in range(count)])]
    ppermute x4 -> x2, waiting for transfers between devices: 43.2 us -> 40.8 us  [groups(): return lax.ppermute(piece, 'groups', [(0, 1), (1, 0)])]
    all_to_all x3 -> x2, starting transfers between devices: 29.6 us -> 29.2 us  [the longest x1 23.5 us: local(): got_cot = lax.all_to_all(sent_cot, 'blk', split_axis=0, concat_axis=0)]
  transfers between devices with their start and end apart: 28 -> 20, of which waited for: 9 -> 8; matrix products, arithmetic and copies ran while one was open for 11% -> 10% of each run, Pallas kernels for 16% -> 12%
where the time goes in v12:
time: 376 us; the launch traced here: 370 us
  waiting for transfers between devices  177 us (47%)
  starting transfers between devices  63.6 us (17%)
  Pallas kernels  50.7 us (13%)
  between operations  39.2 us (10%)
  local copies, waits for them, and re-layouts  18.5 us (5%)
  other arithmetic  15.6 us (4%)
  matrix products  6.23 us (2%)
    all_gather x1, waiting for transfers between devices, weight_pieces(): lax.all_gather(lax.dynamic_slice_in_dim(weight, first, half, 0), 'blk', a...  62.2 us
    ppermute x5, waiting for transfers between devices, over(): return lax.ppermute(piece, 'blk', [(i, i ^ bit) for i in range(count)])  41.7 us
    ppermute x2, waiting for transfers between devices, groups(): return lax.ppermute(piece, 'groups', [(0, 1), (1, 0)])  40.8 us
    pallas_call x4, Pallas kernels, write_quarter(): pl.pallas_call(quarter_kernel, grid_spec=pltpu.PrefetchScalarGridSpec(num...  28.5 us
    ppermute x8, waiting for transfers between devices, moved(): lax.ppermute(value, 'blk', [(i, (i + steps) % count) for i in range(count)])  26.7 us
    all_to_all x1, starting transfers between devices, local(): got_cot = lax.all_to_all(sent_cot, 'blk', split_axis=0, concat_axis=0)  23.5 us
    ppermute x8, starting transfers between devices, moved(): lax.ppermute(value, 'blk', [(i, (i + steps) % count) for i in range(count)])  12 us
    pallas_call x1, Pallas kernels, local(): shares = hidden_call(received, received, rows_all, place_all, starts)  8.27 us
  transfers between devices with their start and end apart: 20, of which 8 were waited for; matrix products, arithmetic and copies ran while one was open for 10% of the time, Pallas kernels for 12%

profile of v12, /device:TPU:1, one launch (start us, length us, event | category | flops | bytes accessed | tf_op | source)
XLA Modules:
  0.0 370.3 jit_solution(4179473991554795823)
XLA Ops:
  7.2 1.3 concatenate.24
  8.5 2.5 shard_map.94
  11.0 4.6 %shard_map.95 = bf16[16,256,512]{2,1,0:T(8,128)(2,1)} custom-call(bf16[192,8192]{1,0:T(8,128)(2,1)} %act.1, bf16[48,8192]{1,0:T(8,128)(2,1)} %bitcast.103, bf16[16,512]{1,0:T(8,128)(2,1)} %get-tuple-element.5.digits), custom_call_target="tpu_custom_call" | custom-call | bytes 8388608 | tf_op jit(solution)/shard_map/pallas_call | solution.py:243
  15.6 7.5 %all-to-all-start = ((bf16[16,256,512]{2,1,0:T(8,128)(2,1)}), bf16[16,256,512]{2,1,0:T(8,128)(2,1)}, u32[]{:S(2)}, u32[]{:S(2)}) async-start(bf16[16,256,512]{2,1,0:T(8,128)(2,1)} %shard_map.95), calls=%async_computation | async-start | bytes 8388608 | tf_op jit(solution)/shard_map/all_to_all | solution.py:435
  28.1 1.0 dynamic-slice_bitcast_fusion
  29.1 1.4 collective-permute-start.2
  30.6 1.7 collective-permute-start.3
  32.3 1.2 collective-permute-start.4
  33.4 1.2 collective-permute-start.5
  61.5 62.2 %all-gather.3.cloned.1.call-done = bf16[1024,1024]{1,0:T(8,128)(2,1)} async-done(((bf16[256,1024]{1,0:T(8,128)(2,1)}), bf16[1024,1024]{1,0:T(8,128)(2,1)}) %all-gather.3.cloned.1.call-update) | async-done | bytes 2097168 | tf_op jit(solution)/shard_map/all_gather | solution.py:85
  123.7 11.3 %collective-permute-done.2 = bf16[16,9216]{1,0:T(8,128)(2,1)S(1)} collective-permute-done((bf16[16,9216]{1,0:T(8,128)(2,1)S(1)}, bf16[16,9216]{1,0:T(8,128)(2,1)S(1)}, u32[]{:S(2)}, u32[]{:S(2)}) %collective-permute-start.2) | collective-permute-done | bytes 294944 | tf_op jit(solution)/shard_map/ppermute | solution.py:21
  135.0 8.0 %collective-permute-done.3 = bf16[16,9216]{1,0:T(8,128)(2,1)S(1)} collective-permute-done((bf16[16,9216]{1,0:T(8,128)(2,1)S(1)}, bf16[16,9216]{1,0:T(8,128)(2,1)S(1)}, u32[]{:S(2)}, u32[]{:S(2)}) %collective-permute-start.3) | collective-permute-done | bytes 294944 | tf_op jit(solution)/shard_map/ppermute | solution.py:21
  143.0 5.5 %collective-permute-done.4 = bf16[16,9216]{1,0:T(8,128)(2,1)S(1)} collective-permute-done((bf16[16,9216]{1,0:T(8,128)(2,1)S(1)}, bf16[16,9216]{1,0:T(8,128)(2,1)S(1)}, u32[]{:S(2)}, u32[]{:S(2)}) %collective-permute-start.4) | collective-permute-done | bytes 294944 | tf_op jit(solution)/shard_map/ppermute | solution.py:21
  149.2 1.2 collective-permute-start
  150.4 41.7 %collective-permute-done.1.refs_3_.rest_0_ = bf16[4,256,1024]{2,1,0:T(8,128)(2,1)} collective-permute-done((bf16[4,256,1024]{2,1,0:T(8,128)(2,1)}, bf16[4,256,1024]{2,1,0:T(8,128)(2,1)}, u32[]{:S(2)}, u32[]{:S(2)}) %collective-permute-start.1) | collective-permute-done | bytes 2097184 | tf_op jit(solution)/shard_map/ppermute | solution.py:80
  192.1 1.2 collective-permute-start.7
  193.4 1.2 bitcast_select_fusion.5
  196.3 3.2 collective-permute-start.10
  199.4 40.7 %collective-permute-done.7.rest_1_ = bf16[4,256,1024]{2,1,0:T(8,128)(2,1)} collective-permute-done((bf16[4,256,1024]{2,1,0:T(8,128)(2,1)}, bf16[4,256,1024]{2,1,0:T(8,128)(2,1)}, u32[]{:S(2)}, u32[]{:S(2)}) %collective-permute-start.7) | collective-permute-done | bytes 2097184 | tf_op jit(solution)/shard_map/ppermute | solution.py:83
  240.2 2.3 collective-permute-start.8
  242.5 23.5 %all-to-all-start.1 = ((bf16[16,48,512]{2,1,0:T(8,128)(2,1)}), bf16[16,48,512]{2,1,0:T(8,128)(2,1)}, u32[]{:S(2)}, u32[]{:S(2)}) async-start(bf16[16,48,512]{2,1,0:T(8,128)(2,1)} %shard_map.96), calls=%async_computation.1 | async-start | bytes 1572864 | tf_op jit(solution)/shard_map/all_to_all | solution.py:443
  266.0 1.4 fusion.29
  269.3 8.3 %shard_map.101 = bf16[2,256,384]{2,1,0:T(8,128)(2,1)} custom-call(bf16[16,256,512]{2,1,0:T(8,128)(2,1)} %all-to-all-done.refs_1_.act.maps, bf16[16,256,512]{2,1,0:T(8,128)(2,1)} %all-to-all-done.refs_1_.act.maps, s32[1,3072]{1,0:T(1,128)} %reshape.319.rows, s32[1,3072]{1,0:T(1,128)} %add.228.spots, s32[32,1]{1,0:T(8,128)} %copy.28.starts), custom_call_target="tpu_custom_call" | custom-call | flops 2415919104 | bytes 3145728 | tf_op jit(solution)/shard_map/pallas_call | solution.py:496
  277.6 1.9 copy.29
  279.5 5.2 %all-to-all-done.1 = bf16[16,48,512]{2,1,0:T(8,128)(2,1)} async-done(((bf16[16,48,512]{2,1,0:T(8,128)(2,1)}), bf16[16,48,512]{2,1,0:T(8,128)(2,1)}, u32[]{:S(2)}, u32[]{:S(2)}) %all-to-all-start.1) | async-done | bytes 786464 | tf_op jit(solution)/shard_map/all_to_all | solution.py:443
  284.7 1.2 fusion.33
  286.6 1.0 fusion.9
  287.7 1.1 fusion.1
  289.5 1.6 copy.27
  291.1 1.0 broadcast_in_dim.114
  292.2 1.9 pad_maximum_fusion.2
  294.0 5.8 %all-to-all-start.2 = ((bf16[16,24,768]{2,1,0:T(8,128)(2,1)}), bf16[16,24,768]{2,1,0:T(8,128)(2,1)}, u32[]{:S(2)}, u32[]{:S(2)}) async-start(bf16[16,24,768]{2,1,0:T(8,128)(2,1)} %pad_maximum_fusion.2), calls=%async_computation.2 | async-start | bytes 1179648 | tf_op jit(solution)/shard_map/all_to_all | solution.py:501
  299.8 1.2 convolution_convert_fusion.1
  301.1 1.5 convolution_convert_fusion
  302.6 1.0 pad_maximum_fusion.cot
  303.6 1.0 convolution_convert_fusion.2.grad
  304.6 7.1 %shard_map.97.rest_2_ = bf16[384,8192]{1,0:T(8,128)(2,1)} custom-call(s32[2]{0:T(128)} %pad_add_fusion.3.where, bf16[384,1024]{1,0:T(8,128)(2,1)} %pad_maximum_fusion.cot, bf16[384,16]{1,0:T(8,128)(2,1)} %convolution_convert_fusion.2.grad, bf16[48,8192]{1,0:T(8,128)(2,1)} %pad_maximum_fusion.1.down, bf16[4,256,1024]{2,1,0:T(8,128)(2,1)} %bitcast.4.rest_0_, ...), custom_call_target="tpu_custom_call" | custom-call | flops 1610612736 | bytes 5767168 | tf_op jit(solution)/shard_map/pallas_call | solution.py:138
  311.7 7.1 %shard_map.98.rest_2_ = bf16[384,8192]{1,0:T(8,128)(2,1)} custom-call(s32[2]{0:T(128)} %pad_add_fusion.2.where, bf16[384,1024]{1,0:T(8,128)(2,1)} %pad_maximum_fusion.cot, bf16[384,16]{1,0:T(8,128)(2,1)} %convolution_convert_fusion.2.grad, bf16[48,8192]{1,0:T(8,128)(2,1)} %pad_maximum_fusion.1.down, ...), custom_call_target="tpu_custom_call", output_to_operand_aliasing={{}: (6, {})} | custom-call | flops 1610612736 | bytes 5767168 | tf_op jit(solution)/shard_map/pallas_call | solution.py:138
  318.9 7.1 %shard_map.99.rest_2_ = bf16[384,8192]{1,0:T(8,128)(2,1)} custom-call(s32[2]{0:T(128)} %pad_add_fusion.1.where, bf16[384,1024]{1,0:T(8,128)(2,1)} %pad_maximum_fusion.cot, bf16[384,16]{1,0:T(8,128)(2,1)} %convolution_convert_fusion.2.grad, bf16[48,8192]{1,0:T(8,128)(2,1)} %pad_maximum_fusion.1.down, ...), custom_call_target="tpu_custom_call", output_to_operand_aliasing={{}: (6, {})} | custom-call | flops 1610612736 | bytes 5767168 | tf_op jit(solution)/shard_map/pallas_call | solution.py:138
  327.8 6.8 %shard_map.102 = bf16[768,512]{1,0:T(8,128)(2,1)} custom-call(bf16[16,256,512]{2,1,0:T(8,128)(2,1)} %all-to-all-done.refs_1_.act.maps, bf16[256,384]{1,0:T(8,128)(2,1)} %bitcast.116, s32[1,3072]{1,0:T(1,128)} %reshape.319.rows, s32[1,3072]{1,0:T(1,128)} %add.228.spots, s32[32,1]{1,0:T(8,128)} %copy.28.starts), custom_call_target="tpu_custom_call" | custom-call | flops 2415919104 | bytes 3145728 | tf_op jit(solution)/shard_map/pallas_call | solution.py:508
  334.5 6.1 %all-to-all-start.3 = ((bf16[16,48,512]{2,1,0:T(8,128)(2,1)}), bf16[16,48,512]{2,1,0:T(8,128)(2,1)S(1)}, u32[]{:S(2)}, u32[]{:S(2)}) async-start(bf16[16,48,512]{2,1,0:T(8,128)(2,1)} %bitcast.111), calls=%async_computation.3 | async-start | bytes 1572864 | tf_op jit(solution)/shard_map/all_to_all | solution.py:509
  340.7 1.1 convert_reduce_fusion
  342.6 2.0 select_add_fusion.1
  344.8 4.3 %collective-permute-start.12 = (f32[16,1024]{1,0:T(8,128)S(1)}, f32[16,1024]{1,0:T(8,128)S(1)}, u32[]{:S(2)}, u32[]{:S(2)}) collective-permute-start(f32[16,1024]{1,0:T(8,128)S(1)} %get-tuple-element.14), channel_id=1, source_target_pairs={{0,14},{1,15},{2,0},{3,1},{4,2},{5,3},{6,4},{7,5},{8,6},{9,7},{10,... | collective-permute-start | bytes 196616 | tf_op jit(solution)/shard_map/ppermute | solution.py:21
  349.1 1.7 collective-permute-start.13
  351.1 7.1 %shard_map.100 = bf16[384,8192]{1,0:T(8,128)(2,1)} custom-call(s32[2]{0:T(128)} %pad_add_fusion.where, bf16[384,1024]{1,0:T(8,128)(2,1)} %pad_maximum_fusion.cot, bf16[384,16]{1,0:T(8,128)(2,1)} %convolution_convert_fusion.2.grad, bf16[48,8192]{1,0:T(8,128)(2,1)} %pad_maximum_fusion.1.down, ...), custom_call_target="tpu_custom_call", output_to_operand_aliasing={{}: (6, {})} | custom-call | flops 1610612736 | bytes 5767168 | tf_op jit(solution)/shard_map/pallas_call | solution.py:138
  358.2 1.9 collective-permute-done.13
  362.0 1.4 reshape.318
  (89 shorter events, 17.9 us)
Async XLA Ops:
  7.2 16.0 %copy-start = (bf16[512,1024]{1,0:T(8,128)(2,1)S(1)}, bf16[512,1024]{1,0:T(8,128)(2,1)}, u32[]{:S(2)}) copy-start(bf16[512,1024]{1,0:T(8,128)(2,1)} %param.11) | copy-start | bytes 3145732
  15.6 8.4 %copy-start.11 = (s32[32]{0:T(128)S(1)}, s32[32]{0:T(128)}, u32[]{:S(2)}) copy-start(s32[32]{0:T(128)} %param.10) | copy-start | bytes 388
  15.6 12.5 %copy-start.4 = (bf16[3,16,1024]{2,1,0:T(8,128)(2,1)S(1)}, bf16[3,16,1024]{2,1,0:T(8,128)(2,1)}, u32[]{:S(2)}) copy-start(bf16[3,16,1024]{2,1,0:T(8,128)(2,1)} %param.13) | copy-start | bytes 294916
  15.6 226.9 %all-to-all-start = ((bf16[16,256,512]{2,1,0:T(8,128)(2,1)}), bf16[16,256,512]{2,1,0:T(8,128)(2,1)}, u32[]{:S(2)}, u32[]{:S(2)}) async-start(bf16[16,256,512]{2,1,0:T(8,128)(2,1)} %shard_map.95), calls=%async_computation | async-start | bytes 8388608 | tf_op jit(solution)/shard_map/all_to_all | solution.py:435
  23.1 100.6 %all-gather.3.cloned.1.call-start = ((), (), s32[]{:S(2)}) async-start(), calls=%async_computation.4 | async-start | bytes 2621440 | tf_op jit(solution)/shard_map/all_gather | solution.py:85
  29.1 105.9 %collective-permute-start.2 = (bf16[16,9216]{1,0:T(8,128)(2,1)S(1)}, bf16[16,9216]{1,0:T(8,128)(2,1)S(1)}, u32[]{:S(2)}, u32[]{:S(2)}) collective-permute-start(bf16[16,9216]{1,0:T(8,128)(2,1)S(1)} %pad_maximum_fusion.3), channel_id=1, source_target_pairs={{0,4},{1,5},{2,6},{3,7},{4,8},{5,9},{6,10},{7,11},{8,12},{9,13},{1... | collective-permute-start | bytes 884744 | tf_op jit(solution)/shard_map/ppermute | solution.py:21
  30.6 112.4 %collective-permute-start.3 = (bf16[16,9216]{1,0:T(8,128)(2,1)S(1)}, bf16[16,9216]{1,0:T(8,128)(2,1)S(1)}, u32[]{:S(2)}, u32[]{:S(2)}) collective-permute-start(bf16[16,9216]{1,0:T(8,128)(2,1)S(1)} %pad_maximum_fusion.3), channel_id=1, source_target_pairs={{0,3},{1,4},{2,5},{3,6},{4,7},{5,8},{6,9},{7,10},{8,11},{9,12},{10... | collective-permute-start | bytes 884744 | tf_op jit(solution)/shard_map/ppermute | solution.py:21
  32.3 116.2 %collective-permute-start.4 = (bf16[16,9216]{1,0:T(8,128)(2,1)S(1)}, bf16[16,9216]{1,0:T(8,128)(2,1)S(1)}, u32[]{:S(2)}, u32[]{:S(2)}) collective-permute-start(bf16[16,9216]{1,0:T(8,128)(2,1)S(1)} %pad_maximum_fusion.3), channel_id=1, source_target_pairs={{0,2},{1,3},{2,4},{3,5},{4,6},{5,7},{6,8},{7,9},{8,10},{9,11},{10,... | collective-permute-start | bytes 884744 | tf_op jit(solution)/shard_map/ppermute | solution.py:21
  33.4 115.0 %collective-permute-start.5 = (bf16[16,9216]{1,0:T(8,128)(2,1)S(1)}, bf16[16,9216]{1,0:T(8,128)(2,1)S(1)}, u32[]{:S(2)}, u32[]{:S(2)}) collective-permute-start(bf16[16,9216]{1,0:T(8,128)(2,1)S(1)} %pad_maximum_fusion.3), channel_id=1, source_target_pairs={{0,1},{1,2},{2,3},{3,4},{4,5},{5,6},{6,7},{7,8},{8,9},{9,10},{10,1... | collective-permute-start | bytes 884744 | tf_op jit(solution)/shard_map/ppermute | solution.py:21
  58.9 228.8 %copy-start.9 = (s32[48]{0:T(128)}, s32[48]{0:T(128)S(1)}, u32[]{:S(2)}) copy-start(s32[48]{0:T(128)S(1)} %and_select_fusion.1) | copy-start | bytes 580
  123.7 68.5 %collective-permute-start.1 = (bf16[4,256,1024]{2,1,0:T(8,128)(2,1)}, bf16[4,256,1024]{2,1,0:T(8,128)(2,1)}, u32[]{:S(2)}, u32[]{:S(2)}) collective-permute-start(bf16[4,256,1024]{2,1,0:T(8,128)(2,1)} %bitcast.4.rest_0_), channel_id=1, source_target_pairs={{0,2},{1,3},{2,0},{3,1},{4,6},{5,7},{6,4},{7,5},{8,10},{9,11},{10,... | collective-permute-start | bytes 6291464 | tf_op jit(solution)/shard_map/ppermute | solution.py:80
  149.2 47.0 %collective-permute-start = (bf16[4,256,1024]{2,1,0:T(8,128)(2,1)}, bf16[4,256,1024]{2,1,0:T(8,128)(2,1)S(1)}, u32[]{:S(2)}, u32[]{:S(2)}) collective-permute-start(bf16[4,256,1024]{2,1,0:T(8,128)(2,1)} %bitcast.4.rest_0_), channel_id=1, source_target_pairs={{0,16},{16,0},{1,17},{17,1},{2,18},{18,2},{3,19},{19,3},{4,20},{20... | collective-permute-start | bytes 6291464 | tf_op jit(solution)/shard_map/ppermute | solution.py:83
  192.1 48.0 %collective-permute-start.7 = (bf16[4,256,1024]{2,1,0:T(8,128)(2,1)}, bf16[4,256,1024]{2,1,0:T(8,128)(2,1)}, u32[]{:S(2)}, u32[]{:S(2)}) collective-permute-start(bf16[4,256,1024]{2,1,0:T(8,128)(2,1)} %collective-permute-done.1.refs_3_.rest_0_), channel_id=1, source_target_pairs={{0,16},{16,0},{1,17},{17,1},{2,18},{18,2},{3,19},{19,3},{4,20},{20... | collective-permute-start | bytes 6291464 | tf_op jit(solution)/shard_map/ppermute | solution.py:83
  195.5 116.2 %collective-permute-start.9 = (bf16[4,256,1024]{2,1,0:T(8,128)(2,1)}, bf16[4,256,1024]{2,1,0:T(8,128)(2,1)}, u32[]{:S(2)}, u32[]{:S(2)}) collective-permute-start(bf16[4,256,1024]{2,1,0:T(8,128)(2,1)} %bitcast.4.rest_0_), channel_id=1, source_target_pairs={{0,1},{1,0},{2,3},{3,2},{4,5},{5,4},{6,7},{7,6},{8,9},{9,8},{10,11... | collective-permute-start | bytes 6291464 | tf_op jit(solution)/shard_map/ppermute | solution.py:80
  196.2 154.5 %collective-permute-start.6 = (bf16[4,256,1024]{2,1,0:T(8,128)(2,1)}, bf16[4,256,1024]{2,1,0:T(8,128)(2,1)}, u32[]{:S(2)}, u32[]{:S(2)}) collective-permute-start(bf16[4,256,1024]{2,1,0:T(8,128)(2,1)} %collective-permute-done.1.refs_3_.rest_0_), channel_id=1, source_target_pairs={{0,1},{1,0},{2,3},{3,2},{4,5},{5,4},{6,7},{7,6},{8,9},{9,8},{10,11... | collective-permute-start | bytes 6291464 | tf_op jit(solution)/shard_map/ppermute | solution.py:80
  196.3 46.3 %copy-start.1 = (bf16[4,256,1024]{2,1,0:T(8,128)(2,1)}, bf16[4,256,1024]{2,1,0:T(8,128)(2,1)S(1)}, u32[]{:S(2)}) copy-start(bf16[4,256,1024]{2,1,0:T(8,128)(2,1)S(1)} %collective-permute-done.refs_2_.rest_1_) | copy-start | bytes 6291460
  196.3 115.4 %collective-permute-start.10 = (bf16[4,256,1024]{2,1,0:T(8,128)(2,1)S(1)}, bf16[4,256,1024]{2,1,0:T(8,128)(2,1)}, u32[]{:S(2)}, u32[]{:S(2)}) collective-permute-start(bf16[4,256,1024]{2,1,0:T(8,128)(2,1)S(1)} %collective-permute-done.refs_2_.rest_1_), channel_id=1, source_target_pairs={{0,1},{1,0},{2,3},{3,2},{4,5},{5,4},{6,7},{7,6},{8,9},{9,8},{10,11... | collective-permute-start | bytes 6291464 | tf_op jit(solution)/shard_map/ppermute | solution.py:80
  240.2 110.9 %collective-permute-start.8 = (bf16[4,256,1024]{2,1,0:T(8,128)(2,1)}, bf16[4,256,1024]{2,1,0:T(8,128)(2,1)}, u32[]{:S(2)}, u32[]{:S(2)}) collective-permute-start(bf16[4,256,1024]{2,1,0:T(8,128)(2,1)} %collective-permute-done.7.rest_1_), channel_id=1, source_target_pairs={{0,1},{1,0},{2,3},{3,2},{4,5},{5,4},{6,7},{7,6},{8,9},{9,8},{10,11... | collective-permute-start | bytes 6291464 | tf_op jit(solution)/shard_map/ppermute | solution.py:80
  242.5 42.1 %all-to-all-start.1 = ((bf16[16,48,512]{2,1,0:T(8,128)(2,1)}), bf16[16,48,512]{2,1,0:T(8,128)(2,1)}, u32[]{:S(2)}, u32[]{:S(2)}) async-start(bf16[16,48,512]{2,1,0:T(8,128)(2,1)} %shard_map.96), calls=%async_computation.1 | async-start | bytes 1572864 | tf_op jit(solution)/shard_map/all_to_all | solution.py:443
  269.3 8.3 %copy-start.7 = (s32[384]{0:T(512)}, s32[384]{0:T(512)S(1)}, u32[]{:S(2)}) copy-start(s32[384]{0:T(512)S(1)} %sub.69) | copy-start | bytes 4612
  285.8 0.8 copy-start.2
  288.7 2.4 copy-start.5
  294.0 9.5 %copy-start.6 = (bf16[384,16]{0,1:T(8,128)(2,1)S(1)}, bf16[384,16]{0,1:T(8,128)(2,1)}, u32[]{:S(2)}) copy-start(bf16[384,16]{0,1:T(8,128)(2,1)} %copy-done.5) | copy-start | bytes 36868
  294.0 31.9 %all-to-all-start.2 = ((bf16[16,24,768]{2,1,0:T(8,128)(2,1)}), bf16[16,24,768]{2,1,0:T(8,128)(2,1)}, u32[]{:S(2)}, u32[]{:S(2)}) async-start(bf16[16,24,768]{2,1,0:T(8,128)(2,1)} %pad_maximum_fusion.2), calls=%async_computation.2 | async-start | bytes 1179648 | tf_op jit(solution)/shard_map/all_to_all | solution.py:501
  299.8 3.7 %copy-start.8 = (s32[384]{0:T(512)S(1)}, s32[384]{0:T(512)}, u32[]{:S(2)}) copy-start(s32[384]{0:T(512)} %copy-done.7) | copy-start | bytes 4612
  334.5 7.6 %copy-start.3 = (bf16[16,24,512]{2,1,0:T(8,128)(2,1)S(1)}, bf16[16,24,512]{2,1,0:T(8,128)(2,1)}, u32[]{:S(2)}) copy-start(bf16[16,24,512]{2,1,0:T(8,128)(2,1)} %copy-done.2) | copy-start | bytes 1179652
  334.5 7.6 %copy-start.10 = (s32[48]{0:T(128)S(1)}, s32[48]{0:T(128)}, u32[]{:S(2)}) copy-start(s32[48]{0:T(128)} %copy-done.9) | copy-start | bytes 580
  334.5 26.3 %all-to-all-start.3 = ((bf16[16,48,512]{2,1,0:T(8,128)(2,1)}), bf16[16,48,512]{2,1,0:T(8,128)(2,1)S(1)}, u32[]{:S(2)}, u32[]{:S(2)}) async-start(bf16[16,48,512]{2,1,0:T(8,128)(2,1)} %bitcast.111), calls=%async_computation.3 | async-start | bytes 1572864 | tf_op jit(solution)/shard_map/all_to_all | solution.py:509
  344.6 13.6 %collective-permute-start.11 = (f32[16,1024]{1,0:T(8,128)S(1)}, f32[16,1024]{1,0:T(8,128)S(1)}, u32[]{:S(2)}, u32[]{:S(2)}) collective-permute-start(f32[16,1024]{1,0:T(8,128)S(1)} %get-tuple-element.14), channel_id=1, source_target_pairs={{0,15},{1,0},{2,1},{3,2},{4,3},{5,4},{6,5},{7,6},{8,7},{9,8},{10,9... | collective-permute-start | bytes 196616 | tf_op jit(solution)/shard_map/ppermute | solution.py:21
  344.8 13.4 %collective-permute-start.12 = (f32[16,1024]{1,0:T(8,128)S(1)}, f32[16,1024]{1,0:T(8,128)S(1)}, u32[]{:S(2)}, u32[]{:S(2)}) collective-permute-start(f32[16,1024]{1,0:T(8,128)S(1)} %get-tuple-element.14), channel_id=1, source_target_pairs={{0,14},{1,15},{2,0},{3,1},{4,2},{5,3},{6,4},{7,5},{8,6},{9,7},{10,... | collective-permute-start | bytes 196616 | tf_op jit(solution)/shard_map/ppermute | solution.py:21
  349.1 11.0 %collective-permute-start.13 = (f32[16,1024]{1,0:T(8,128)S(1)}, f32[16,1024]{1,0:T(8,128)S(1)}, u32[]{:S(2)}, u32[]{:S(2)}) collective-permute-start(f32[16,1024]{1,0:T(8,128)S(1)} %get-tuple-element.14), channel_id=1, source_target_pairs={{0,13},{1,14},{2,15},{3,0},{4,1},{5,2},{6,3},{7,4},{8,5},{9,6},{10... | collective-permute-start | bytes 196616 | tf_op jit(solution)/shard_map/ppermute | solution.py:21
  350.8 9.3 %collective-permute-start.14 = (f32[16,1024]{1,0:T(8,128)S(1)}, f32[16,1024]{1,0:T(8,128)S(1)}, u32[]{:S(2)}, u32[]{:S(2)}) collective-permute-start(f32[16,1024]{1,0:T(8,128)S(1)} %get-tuple-element.14), channel_id=1, source_target_pairs={{0,12},{1,13},{2,14},{3,15},{4,0},{5,1},{6,2},{7,3},{8,4},{9,5},{1... | collective-permute-start | bytes 196616 | tf_op jit(solution)/shard_map/ppermute | solution.py:21
Sparse Core Ops, SparseCore 0:
  25.5 98.1 all-gather.2

commit v13 on v12

--- a/solution.py
+++ b/solution.py
@@ -66,15 +66,16 @@
     return (high * DIGIT + middle) * DIGIT + low, place_high * DIGIT + place
 
 
-CHUNKS = 1
-
-
-def weight_pieces(weight):
+def weight_column(weight):
     count = lax.axis_size("blk")
     half = weight.shape[0] // 2
-    size = half // CHUNKS
-    first = lax.axis_index("groups") * half
     lines = [list(range(k, count, 4)) for k in range(4)]
+    mine = lax.dynamic_slice_in_dim(weight, lax.axis_index("groups") * half, half, 0)
+    return lax.all_gather(mine, "blk", axis_index_groups=lines)
+
+
+def weight_quarters(column, late):
+    count = lax.axis_size("blk")
 
     def over(piece, bit):
         return lax.ppermute(piece, "blk", [(i, i ^ bit) for i in range(count)])
@@ -82,19 +83,19 @@
     def groups(piece):
         return lax.ppermute(piece, "groups", [(0, 1), (1, 0)])
 
-    column = lax.all_gather(
-        lax.dynamic_slice_in_dim(weight, first, half, 0), "blk", axis_index_groups=lines
-    )
-    columns = [column[:, k * size : (k + 1) * size] for k in range(CHUNKS)]
-    pieces = []
-    for mine in (columns, [over(column, 2) for column in columns]):
-        both = mine + [groups(piece) for piece in mine]
-        pieces += [both, [over(piece, 1) for piece in both]]
-    return pieces
+    theirs = groups(column)
+    across = over(column, 2)
+    across_theirs = groups(across)
+    return [
+        [column, theirs],
+        [over(column, 1), over(theirs, 1)],
+        [across, across_theirs],
+        [over(across, 1), over(after(across_theirs, late), 1)],
+    ]
 
 
 def quarter_kernel(where, cot, grad, down, *rest):
-    pieces = rest[: 2 * CHUNKS]
+    pieces = rest[:2]
     out = rest[-1]
     rank = grad.shape[1]
     lora = [
@@ -109,7 +110,7 @@
     lora = jnp.concatenate(lora, axis=0).astype(jnp.bfloat16).astype(jnp.float32)
 
     def product(group):
-        order = pieces[group * CHUNKS :] + pieces[: group * CHUNKS]
+        order = pieces[group:] + pieces[:group]
         weight = jnp.concatenate([piece[0] for piece in order], axis=0)
         frozen = dot(cot[...], weight, ((1,), (1,)))
         out[...] = (frozen + lora).astype(jnp.bfloat16)
@@ -156,12 +157,11 @@
 
 def together(pieces, firsts, group):
     shards, part, depth = pieces[0][0].shape
-    weight = jnp.zeros((shards, 4, 2, CHUNKS, part, depth), jnp.bfloat16)
+    weight = jnp.zeros((shards, 4, 2, part, depth), jnp.bfloat16)
     for quarter, first in zip(pieces, firsts):
         for k, piece in enumerate(quarter):
-            half = group if k < CHUNKS else 1 - group
-            place = (0, first, half, k % CHUNKS, 0, 0)
-            weight = lax.dynamic_update_slice(weight, piece[:, None, None, None], place)
+            place = (0, first, group if k == 0 else 1 - group, 0, 0)
+            weight = lax.dynamic_update_slice(weight, piece[:, None, None], place)
     return weight.reshape(-1, depth)
 
 
@@ -223,21 +223,22 @@
     return jnp.concatenate(parts, axis=1), digits
 
 
-def features_kernel(act, maps, digits, out):
+def features_kernel(act, maps, cot, digits, out):
     targets, _, features = out.shape
     tokens, shared = act.shape[0], maps.shape[0]
     for k in range(targets):
         part = slice(k * features, (k + 1) * features)
         out[k, :tokens, :] = act[:, part]
         out[k, tokens : tokens + shared, :] = maps[:, part]
-        out[k, tokens + shared :, :] = digits[...]
-
-
-def pack_features(act, maps, digits, devices):
+        out[k, tokens + shared : tokens + 2 * shared, :] = cot[k]
+        out[k, tokens + 2 * shared :, :] = digits[...]
+
+
+def pack_features(act, maps, cot, digits, devices):
     tokens, width = act.shape
     features = width // devices
     shared = maps.shape[0]
-    total = tokens + shared + digits.shape[0]
+    total = tokens + 2 * shared + digits.shape[0]
     targets = 4
     if features % LANES == 0:
         return pl.pallas_call(
@@ -246,6 +247,7 @@
             in_specs=[
                 pl.BlockSpec((tokens, targets * features), lambda j: (0, j)),
                 pl.BlockSpec((shared, targets * features), lambda j: (0, j)),
+                pl.BlockSpec((targets, shared, features), lambda j: (j, 0, 0)),
                 pl.BlockSpec(digits.shape, lambda j: (0, 0)),
             ],
             out_specs=pl.BlockSpec((targets, total, features), lambda j: (j, 0, 0)),
@@ -254,11 +256,11 @@
                 flops=0, bytes_accessed=4 * total * width, transcendentals=0
             ),
             compiler_params=pltpu.CompilerParams(vmem_limit_bytes=VMEM),
-        )(act, maps, digits)
+        )(act, maps, cot, digits)
     both = jnp.concatenate([act, maps], axis=0)
     both = both.reshape(tokens + shared, devices, features).transpose(1, 0, 2)
     copies = jnp.broadcast_to(digits[None], (devices,) + digits.shape)
-    return jnp.concatenate([both, copies], axis=1)
+    return jnp.concatenate([both, cot, copies], axis=1)
 
 
 def slot_chunks(width):
@@ -398,7 +400,7 @@
     cap = resident_rows // devices
     start_ids = tenant_first_row // BLOCK
 
-    pieces = weight_pieces(frozen_value_weight)
+    column = weight_column(frozen_value_weight)
 
     first_block = device * resident
     block_numbers = first_block + jnp.arange(resident, dtype=jnp.int32)
@@ -431,20 +433,19 @@
 
     sent_cot, digits = pack_rows(token_layout_row, cotangent, devices, cap, features)
     flat_maps = adapter_down_maps.reshape(share, width)
-    received = pack_features(activations, flat_maps, digits, devices)
+    received = pack_features(activations, flat_maps, sent_cot, digits, devices)
+    received = after(received, column, carried)
     received = lax.all_to_all(received, "blk", split_axis=0, concat_axis=0)
+    recv_cot = [
+        received[:, tokens + share + k * cap : tokens + share + (k + 1) * cap].reshape(
+            resident_rows, features
+        )
+        for k in range(out_width // features)
+    ]
     per_digit = -(-tokens // features)
-    digits = received[:, tokens + share : tokens + share + 5 * per_digit]
+    digits = received[:, tokens + 2 * share : tokens + 2 * share + 5 * per_digit]
     digits = digits.reshape(devices, 5, per_digit * features)[:, :, :tokens]
     rows_all, place_all = from_digits(digits)
-
-    own, _, across, _ = pieces
-    sent_cot = after(sent_cot, received, own[CHUNKS], across[0])
-    got_cot = lax.all_to_all(sent_cot, "blk", split_axis=0, concat_axis=0)
-    recv_cot = [
-        got_cot[:, k * cap : (k + 1) * cap].reshape(resident_rows, features)
-        for k in range(out_width // features)
-    ]
 
     spots = device * cap + jnp.arange(cap, dtype=jnp.int32)
     hit = place_all[:, None, :] == spots[None, :, None]
@@ -468,12 +469,55 @@
         [dot(arrange, part, ((0,), (0,))).astype(jnp.bfloat16) for part in recv_cot], axis=1
     )
     grad_rows = dot(arrange, grad_in, ((0,), (0,))).astype(jnp.bfloat16)
+
+    starts = start_ids[:, None]
+    hidden_call, down_call = feature_calls(
+        received, tokens, share, rank, resident_rows, starts.shape[0]
+    )
+    shares = hidden_call(received, received, rows_all, place_all, starts)
+
+    shares = shares.reshape(-1, resident_rows).T.reshape(devices, cap, -1)
+    copies = jnp.broadcast_to(grad_sent[None], (devices,) + grad_sent.shape)
+    small = jnp.concatenate([copies, shares], axis=2)
+    small = lax.all_to_all(small, "blk", split_axis=0, concat_axis=0)
+    each = devices * rank
+    grad_all = small[:, :, :each].reshape(resident_rows, each).T
+    hidden = jnp.sum(small[:, :, each:].astype(jnp.float32), axis=0)
+    hidden = (hidden[:, :each] + hidden[:, each:]).astype(jnp.bfloat16)
+    hidden = hidden.reshape(cap, devices, rank).transpose(1, 0, 2).reshape(-1, rank)
+
+    down_f = down_call(received, grad_all, rows_all, place_all, starts)
+    down_home = lax.all_to_all(down_f, "blk", split_axis=0, concat_axis=1, tiled=True)
+    down_map_gradient = down_home.astype(jnp.float32).reshape(resident, rank, width)
+
+    wide = jnp.where(in_block, jnp.concatenate([hidden] * resident, axis=1), 0)
+    up_all = [dot(wide, part, ((0,), (0,))) for part in recv_cot]
+    up_all = jnp.concatenate(up_all, axis=1).reshape(resident, rank, out_width)
+    up_parts = [up_all[b] for b in range(resident)]
+
+    tail = sum(jnp.where(is_local[b], 0.0, up_parts[b]) for b in range(resident))
+    far = jnp.zeros_like(tail)
+    for step in range(1, HOPS + 1):
+        other = (device + step) % devices * resident
+        theirs = starts_of(other[None], start_ids)[0]
+        far = far + jnp.where(theirs // resident == device, moved(tail, -step), 0.0)
+    up_grads = []
+    for k in range(resident):
+        total = jnp.where(begin[resident - 1] == first_block + k, far, 0.0)
+        for b in range(resident):
+            total = total + jnp.where(is_local[b] & (home_slot[b] == k), up_parts[b], 0.0)
+        up_grads.append(adapter_scale * total)
+    up_map_gradient = jnp.stack(up_grads)
+
+    pieces = weight_quarters(column, shares)
     group = lax.axis_index("groups")
     quarter = device % 4
     firsts = [quarter, quarter ^ 1, quarter ^ 2, quarter ^ 3]
-    if own[0].shape[1] % LANES == 0:
+    if column.shape[1] % LANES == 0:
         out = None
-        for piece, first in zip(pieces, firsts):
+        for number, (piece, first) in enumerate(zip(pieces, firsts)):
+            if number == 2:
+                grad_rows = after(grad_rows, down_f)
             out = write_quarter(piece, first, group, cot_rows, grad_rows, down_blocks, out)
     else:
         weight = together(pieces, firsts, group)
@@ -488,45 +532,6 @@
         lora = (adapter_scale * jnp.concatenate(lora, axis=0)).astype(jnp.bfloat16)
         out = dot(cot_rows, weight, ((1,), (1,))) + lora.astype(jnp.float32)
         out = out.astype(jnp.bfloat16)
-
-    starts = start_ids[:, None]
-    hidden_call, down_call = feature_calls(
-        received, tokens, share, rank, resident_rows, starts.shape[0]
-    )
-    shares = hidden_call(received, received, rows_all, place_all, starts)
-
-    shares = shares.reshape(-1, resident_rows).T.reshape(devices, cap, -1)
-    copies = jnp.broadcast_to(grad_sent[None], (devices,) + grad_sent.shape)
-    small = jnp.concatenate([copies, shares], axis=2)
-    small = lax.all_to_all(small, "blk", split_axis=0, concat_axis=0)
-    each = devices * rank
-    grad_all = small[:, :, :each].reshape(resident_rows, each).T
-    hidden = jnp.sum(small[:, :, each:].astype(jnp.float32), axis=0)
-    hidden = (hidden[:, :each] + hidden[:, each:]).astype(jnp.bfloat16)
-    hidden = hidden.reshape(cap, devices, rank).transpose(1, 0, 2).reshape(-1, rank)
-
-    down_f = down_call(received, grad_all, rows_all, place_all, starts)
-    down_home = lax.all_to_all(down_f, "blk", split_axis=0, concat_axis=1, tiled=True)
-    down_map_gradient = down_home.astype(jnp.float32).reshape(resident, rank, width)
-
-    wide = jnp.where(in_block, jnp.concatenate([hidden] * resident, axis=1), 0)
-    up_all = [dot(wide, part, ((0,), (0,))) for part in recv_cot]
-    up_all = jnp.concatenate(up_all, axis=1).reshape(resident, rank, out_width)
-    up_parts = [up_all[b] for b in range(resident)]
-
-    tail = sum(jnp.where(is_local[b], 0.0, up_parts[b]) for b in range(resident))
-    far = jnp.zeros_like(tail)
-    for step in range(1, HOPS + 1):
-        other = (device + step) % devices * resident
-        theirs = starts_of(other[None], start_ids)[0]
-        far = far + jnp.where(theirs // resident == device, moved(tail, -step), 0.0)
-    up_grads = []
-    for k in range(resident):
-        total = jnp.where(begin[resident - 1] == first_block + k, far, 0.0)
-        for b in range(resident):
-            total = total + jnp.where(is_local[b] & (home_slot[b] == k), up_parts[b], 0.0)
-        up_grads.append(adapter_scale * total)
-    up_map_gradient = jnp.stack(up_grads)
 
     return (out, down_map_gradient, up_map_gradient)
 

time: 376 us -> 309 us (0.82)
  waiting for transfers between devices: 177 us -> 118 us
  starting transfers between devices: 63.6 us -> 53.7 us
    all_gather x1, waiting for transfers between devices: 62.2 us -> 10.1 us  [weight_column(): return lax.all_gather(mine, 'blk', axis_index_groups=lines)]
    ppermute x5, waiting for transfers between devices: 41.7 us -> 83.1 us  [over(): return lax.ppermute(piece, 'blk', [(i, i ^ bit) for i in range(count)])]
    ppermute x2, waiting for transfers between devices: 40.8 us -> 0.01 us  [groups(): return lax.ppermute(piece, 'groups', [(0, 1), (1, 0)])]
    all_to_all x1 -> x0, starting transfers between devices: 23.5 us -> none  [local(): got_cot = lax.all_to_all(sent_cot, 'blk', split_axis=0, concat_axis=0)]
    all_to_all x1, starting transfers between devices: 7.46 us -> 17.2 us  [local(): received = lax.all_to_all(received, 'blk', split_axis=0, concat_axis=0)]
    all_to_all x1, starting transfers between devices: 5.77 us -> 11.2 us  [local(): small = lax.all_to_all(small, 'blk', split_axis=0, concat_axis=0)]
    all_to_all x1 -> x0, waiting for transfers between devices: 5.15 us -> none  [local(): got_cot = lax.all_to_all(sent_cot, 'blk', split_axis=0, concat_axis=0)]
  transfers between devices with their start and end apart: 20 -> 19, of which waited for: 8 -> 6; matrix products, arithmetic and copies ran while one was open for 10% -> 14% of each run, Pallas kernels for 12% -> 14%
where the time goes in v13:
time: 309 us; the launch traced here: 307 us
  waiting for transfers between devices  118 us (38%)
  starting transfers between devices  53.7 us (17%)
  Pallas kernels  51.4 us (17%)
  between operations  38.9 us (13%)
  local copies, waits for them, and re-layouts  20.9 us (7%)
  other arithmetic  17.5 us (6%)
  matrix products  6.91 us (2%)
    ppermute x5, waiting for transfers between devices, over(): return lax.ppermute(piece, 'blk', [(i, i ^ bit) for i in range(count)])  83.1 us
    pallas_call x4, Pallas kernels, write_quarter(): pl.pallas_call(quarter_kernel, grid_spec=pltpu.PrefetchScalarGridSpec(num...  28.6 us
    ppermute x8, waiting for transfers between devices, moved(): lax.ppermute(value, 'blk', [(i, (i + steps) % count) for i in range(count)])  24.5 us
    all_to_all x1, starting transfers between devices, local(): received = lax.all_to_all(received, 'blk', split_axis=0, concat_axis=0)  17.2 us
    ppermute x8, starting transfers between devices, moved(): lax.ppermute(value, 'blk', [(i, (i + steps) % count) for i in range(count)])  13.1 us
    all_to_all x1, starting transfers between devices, local(): small = lax.all_to_all(small, 'blk', split_axis=0, concat_axis=0)  11.2 us
    all_gather x1, waiting for transfers between devices, weight_column(): return lax.all_gather(mine, 'blk', axis_index_groups=lines)  10.1 us
    pallas_call x1, Pallas kernels, local(): shares = hidden_call(received, received, rows_all, place_all, starts)  8.3 us
  transfers between devices with their start and end apart: 19, of which 6 were waited for; matrix products, arithmetic and copies ran while one was open for 14% of the time, Pallas kernels for 14%

profile of v13, /device:TPU:1, one launch (start us, length us, event | category | flops | bytes accessed | tf_op | source)
XLA Modules:
  0.0 307.0 jit_solution(2454373248755062565)
XLA Ops:
  7.3 1.1 copy-done
  9.3 1.4 fusion.19
  14.1 1.0 dynamic-slice_bitcast_fusion
  15.2 2.2 collective-permute-start
  17.3 2.1 collective-permute-start.1
  19.5 1.2 collective-permute-start.2
  24.8 2.5 shard_map.94
  27.3 5.1 %shard_map.95.refs_0_ = bf16[16,304,512]{2,1,0:T(8,128)(2,1)} custom-call(bf16[192,8192]{1,0:T(8,128)(2,1)} %act.1, bf16[48,8192]{1,0:T(8,128)(2,1)} %bitcast.108, bf16[16,48,512]{2,1,0:T(8,128)(2,1)} %get-tuple-element.5.cot, bf16[16,512]{1,0:T(8,128)(2,1)} %get-tuple-element.6.digits), custom_call_target="tpu_custom_call" | custom-call | bytes 9961472 | tf_op jit(solution)/shard_map/pallas_call | solution.py:244
  32.4 12.7 %collective-permute-done.1 = bf16[16,9216]{1,0:T(8,128)(2,1)S(1)} collective-permute-done((bf16[16,9216]{1,0:T(8,128)(2,1)S(1)}, bf16[16,9216]{1,0:T(8,128)(2,1)S(1)}, u32[]{:S(2)}, u32[]{:S(2)}) %collective-permute-start.1) | collective-permute-done | bytes 294944 | tf_op jit(solution)/shard_map/ppermute | solution.py:21
  45.1 8.6 %collective-permute-done.2 = bf16[16,9216]{1,0:T(8,128)(2,1)S(1)} collective-permute-done((bf16[16,9216]{1,0:T(8,128)(2,1)S(1)}, bf16[16,9216]{1,0:T(8,128)(2,1)S(1)}, u32[]{:S(2)}, u32[]{:S(2)}) %collective-permute-start.2) | collective-permute-done | bytes 294944 | tf_op jit(solution)/shard_map/ppermute | solution.py:21
  54.4 10.1 %all-gather.3.cloned.1.call-done = bf16[1024,1024]{1,0:T(8,128)(2,1)} async-done(((bf16[256,1024]{1,0:T(8,128)(2,1)}), bf16[1024,1024]{1,0:T(8,128)(2,1)}) %all-gather.3.cloned.1.call-update) | async-done | bytes 2097168 | tf_op jit(solution)/shard_map/all_gather | solution.py:74
  64.5 17.2 %all-to-all-start = ((bf16[16,304,512]{2,1,0:T(8,128)(2,1)}), bf16[16,304,512]{2,1,0:T(8,128)(2,1)}, u32[]{:S(2)}, u32[]{:S(2)}) async-start(bf16[16,304,512]{2,1,0:T(8,128)(2,1)} %shard_map.96), calls=%async_computation | async-start | bytes 9961472 | tf_op jit(solution)/shard_map/all_to_all | solution.py:438
  93.8 1.2 collective-permute-start.9
  95.0 1.4 collective-permute-start.4
  96.4 1.2 bitcast_select_fusion.5
  97.6 0.9 pad_maximum_fusion.1.down
  99.4 83.1 %collective-permute-done.4.rest_0_ = bf16[4,256,1024]{2,1,0:T(8,128)(2,1)} collective-permute-done((bf16[4,256,1024]{2,1,0:T(8,128)(2,1)S(1)}, bf16[4,256,1024]{2,1,0:T(8,128)(2,1)}, u32[]{:S(2)}, u32[]{:S(2)}) %collective-permute-start.4) | collective-permute-done | bytes 2097184 | tf_op jit(solution)/shard_map/ppermute | solution.py:81
  182.5 1.2 collective-permute-start.6
  183.7 1.2 collective-permute-start.5
  184.9 1.3 fusion.27
  188.0 2.0 fusion.31
  190.0 8.3 %shard_map.97 = bf16[2,256,384]{2,1,0:T(8,128)(2,1)} custom-call(bf16[16,304,512]{2,1,0:T(8,128)(2,1)} %all-to-all-done.act.maps, bf16[16,304,512]{2,1,0:T(8,128)(2,1)} %all-to-all-done.act.maps, s32[1,3072]{1,0:T(1,128)} %reshape.319.rows, s32[1,3072]{1,0:T(1,128)} %add.228.spots, s32[32,1]{1,0:T(8,128)} %copy.41.starts), custom_call_target="tpu_custom_call" | custom-call | flops 2415919104 | bytes 3145728 | tf_op jit(solution)/shard_map/pallas_call | solution.py:477
  198.3 1.9 copy.42
  200.3 1.2 fusion.8
  201.6 1.1 fusion.1
  203.4 1.6 copy.40
  205.1 1.0 broadcast_in_dim.114
  206.1 1.9 pad_maximum_fusion.2
  208.0 11.2 %all-to-all-start.1 = ((bf16[16,24,768]{2,1,0:T(8,128)(2,1)}), bf16[16,24,768]{2,1,0:T(8,128)(2,1)}, u32[]{:S(2)}, u32[]{:S(2)}) async-start(bf16[16,24,768]{2,1,0:T(8,128)(2,1)} %pad_maximum_fusion.2), calls=%async_computation.1 | async-start | bytes 1179648 | tf_op jit(solution)/shard_map/all_to_all | solution.py:482
  219.2 1.6 convolution_convert_fusion.2
  220.7 1.5 copy.39.refs_0_.grad
  222.2 1.5 convolution_convert_fusion.1
  223.7 1.2 convolution_convert_fusion
  224.9 1.0 pad_maximum_fusion.cot
  225.9 7.1 %shard_map.101.rest_2_ = bf16[384,8192]{1,0:T(8,128)(2,1)} custom-call(s32[2]{0:T(128)} %pad_add_fusion.3.where, bf16[384,1024]{1,0:T(8,128)(2,1)} %pad_maximum_fusion.cot, bf16[384,16]{1,0:T(8,128)(2,1)} %copy.39.refs_0_.grad, bf16[48,8192]{1,0:T(8,128)(2,1)} %pad_maximum_fusion.1.down, bf16[4,256,1024]{2,1,0:T(8,128)(2,1)} %bitcast.104, ...), custom_call_target="tpu_custom_call" | custom-call | flops 1610612736 | bytes 5767168 | tf_op jit(solution)/shard_map/pallas_call | solution.py:139
  233.0 7.1 %shard_map.102.rest_2_ = bf16[384,8192]{1,0:T(8,128)(2,1)} custom-call(s32[2]{0:T(128)} %pad_add_fusion.2.where, bf16[384,1024]{1,0:T(8,128)(2,1)} %pad_maximum_fusion.cot, bf16[384,16]{1,0:T(8,128)(2,1)} %copy.39.refs_0_.grad, bf16[48,8192]{1,0:T(8,128)(2,1)} %pad_maximum_fusion.1.down, ...), custom_call_target="tpu_custom_call", output_to_operand_aliasing={{}: (6, {})} | custom-call | flops 1610612736 | bytes 5767168 | tf_op jit(solution)/shard_map/pallas_call | solution.py:139
  240.2 0.9 slice.216
  241.9 6.9 %shard_map.98.refs_1_ = bf16[768,512]{1,0:T(8,128)(2,1)} custom-call(bf16[16,304,512]{2,1,0:T(8,128)(2,1)} %all-to-all-done.act.maps, bf16[256,384]{1,0:T(8,128)(2,1)} %bitcast.121, s32[1,3072]{1,0:T(1,128)} %reshape.319.rows, s32[1,3072]{1,0:T(1,128)} %add.228.spots, s32[32,1]{1,0:T(8,128)} %copy.41.starts), custom_call_target="tpu_custom_call" | custom-call | flops 2415919104 | bytes 3145728 | tf_op jit(solution)/shard_map/pallas_call | solution.py:489
  248.9 7.1 %shard_map.103.rest_2_ = bf16[384,8192]{1,0:T(8,128)(2,1)} custom-call(s32[2]{0:T(128)} %pad_add_fusion.1.where, bf16[384,1024]{1,0:T(8,128)(2,1)} %pad_maximum_fusion.cot, bf16[384,16]{1,0:T(8,128)(2,1)} %shard_map.99.grad, bf16[48,8192]{1,0:T(8,128)(2,1)} %pad_maximum_fusion.1.down, ...), custom_call_target="tpu_custom_call", output_to_operand_aliasing={{}: (6, {})} | custom-call | flops 1610612736 | bytes 5767168 | tf_op jit(solution)/shard_map/pallas_call | solution.py:139
  256.2 6.0 %all-to-all-start.2 = ((bf16[16,48,512]{2,1,0:T(8,128)(2,1)}), bf16[16,48,512]{2,1,0:T(8,128)(2,1)S(1)}, u32[]{:S(2)}, u32[]{:S(2)}) async-start(bf16[16,48,512]{2,1,0:T(8,128)(2,1)} %bitcast.35), calls=%async_computation.2 | async-start | bytes 1572864 | tf_op jit(solution)/shard_map/all_to_all | solution.py:490
  262.2 1.1 convert_reduce_fusion
  264.2 2.0 select_add_fusion.1
  279.5 4.4 %collective-permute-start.12 = (f32[16,1024]{1,0:T(8,128)S(1)}, f32[16,1024]{1,0:T(8,128)S(1)}, u32[]{:S(2)}, u32[]{:S(2)}) collective-permute-start(f32[16,1024]{1,0:T(8,128)S(1)} %get-tuple-element.14), channel_id=1, source_target_pairs={{0,14},{1,15},{2,0},{3,1},{4,2},{5,3},{6,4},{7,5},{8,6},{9,7},{10,... | collective-permute-start | bytes 196616 | tf_op jit(solution)/shard_map/ppermute | solution.py:21
  283.9 1.7 collective-permute-start.13
  286.4 1.4 collective-permute-done.13
  287.9 1.8 collective-permute-done.14
  291.6 1.4 reshape.318
  293.0 7.1 %shard_map.104 = bf16[384,8192]{1,0:T(8,128)(2,1)} custom-call(s32[2]{0:T(128)} %pad_add_fusion.where, bf16[384,1024]{1,0:T(8,128)(2,1)} %pad_maximum_fusion.cot, bf16[384,16]{1,0:T(8,128)(2,1)} %shard_map.99.grad, bf16[48,8192]{1,0:T(8,128)(2,1)} %pad_maximum_fusion.1.down, ...), custom_call_target="tpu_custom_call", output_to_operand_aliasing={{}: (6, {})} | custom-call | flops 1610612736 | bytes 5767168 | tf_op jit(solution)/shard_map/pallas_call | solution.py:139
  (87 shorter events, 18.3 us)
Async XLA Ops:
  7.2 1.2 copy-start
  7.2 7.9 %copy-start.4 = (bf16[3,16,1024]{2,1,0:T(8,128)(2,1)S(1)}, bf16[3,16,1024]{2,1,0:T(8,128)(2,1)}, u32[]{:S(2)}) copy-start(bf16[3,16,1024]{2,1,0:T(8,128)(2,1)} %param.13) | copy-start | bytes 294916
  7.2 17.0 %copy-start.9 = (s32[192]{0:T(256)S(1)}, s32[192]{0:T(256)}, u32[]{:S(2)}) copy-start(s32[192]{0:T(256)} %param.9) | copy-start | bytes 2308
  7.2 57.3 %all-gather.3.cloned.1.call-start = ((), (), s32[]{:S(2)}) async-start(), calls=%async_computation.3 | async-start | bytes 2621440 | tf_op jit(solution)/shard_map/all_gather | solution.py:74
  15.2 17.2 %collective-permute-start = (bf16[16,9216]{1,0:T(8,128)(2,1)S(1)}, bf16[16,9216]{1,0:T(8,128)(2,1)S(1)}, u32[]{:S(2)}, u32[]{:S(2)}) collective-permute-start(bf16[16,9216]{1,0:T(8,128)(2,1)S(1)} %pad_maximum_fusion.3), channel_id=1, source_target_pairs={{0,4},{1,5},{2,6},{3,7},{4,8},{5,9},{6,10},{7,11},{8,12},{9,13},{1... | collective-permute-start | bytes 884744 | tf_op jit(solution)/shard_map/ppermute | solution.py:21
  17.3 27.7 %collective-permute-start.1 = (bf16[16,9216]{1,0:T(8,128)(2,1)S(1)}, bf16[16,9216]{1,0:T(8,128)(2,1)S(1)}, u32[]{:S(2)}, u32[]{:S(2)}) collective-permute-start(bf16[16,9216]{1,0:T(8,128)(2,1)S(1)} %pad_maximum_fusion.3), channel_id=1, source_target_pairs={{0,3},{1,4},{2,5},{3,6},{4,7},{5,8},{6,9},{7,10},{8,11},{9,12},{10... | collective-permute-start | bytes 884744 | tf_op jit(solution)/shard_map/ppermute | solution.py:21
  19.5 34.2 %collective-permute-start.2 = (bf16[16,9216]{1,0:T(8,128)(2,1)S(1)}, bf16[16,9216]{1,0:T(8,128)(2,1)S(1)}, u32[]{:S(2)}, u32[]{:S(2)}) collective-permute-start(bf16[16,9216]{1,0:T(8,128)(2,1)S(1)} %pad_maximum_fusion.3), channel_id=1, source_target_pairs={{0,2},{1,3},{2,4},{3,5},{4,6},{5,7},{6,8},{7,9},{8,10},{9,11},{10,... | collective-permute-start | bytes 884744 | tf_op jit(solution)/shard_map/ppermute | solution.py:21
  20.7 33.0 %collective-permute-start.3 = (bf16[16,9216]{1,0:T(8,128)(2,1)S(1)}, bf16[16,9216]{1,0:T(8,128)(2,1)S(1)}, u32[]{:S(2)}, u32[]{:S(2)}) collective-permute-start(bf16[16,9216]{1,0:T(8,128)(2,1)S(1)} %pad_maximum_fusion.3), channel_id=1, source_target_pairs={{0,1},{1,2},{2,3},{3,4},{4,5},{5,6},{6,7},{7,8},{8,9},{9,10},{10,1... | collective-permute-start | bytes 884744 | tf_op jit(solution)/shard_map/ppermute | solution.py:21
  64.5 28.6 %copy-start.3 = (bf16[16,9216]{1,0:T(8,128)(2,1)S(1)}, bf16[16,9216]{1,0:T(8,128)(2,1)}, u32[]{:S(2)}) copy-start(bf16[16,9216]{1,0:T(8,128)(2,1)} %select_select_fusion.refs_2_) | copy-start | bytes 884740
  64.5 29.2 %copy-start.1 = (bf16[1024,1024]{1,0:T(8,128)(2,1)S(1)}, bf16[1024,1024]{1,0:T(8,128)(2,1)}, u32[]{:S(2)}) copy-start(bf16[1024,1024]{1,0:T(8,128)(2,1)} %all-gather.3.cloned.1.call-done) | copy-start | bytes 6291460
  64.5 120.4 %all-to-all-start = ((bf16[16,304,512]{2,1,0:T(8,128)(2,1)}), bf16[16,304,512]{2,1,0:T(8,128)(2,1)}, u32[]{:S(2)}, u32[]{:S(2)}) async-start(bf16[16,304,512]{2,1,0:T(8,128)(2,1)} %shard_map.96), calls=%async_computation | async-start | bytes 9961472 | tf_op jit(solution)/shard_map/all_to_all | solution.py:438
  93.8 91.1 %collective-permute-start.9 = (bf16[4,256,1024]{2,1,0:T(8,128)(2,1)S(1)}, bf16[4,256,1024]{2,1,0:T(8,128)(2,1)}, u32[]{:S(2)}, u32[]{:S(2)}) collective-permute-start(bf16[4,256,1024]{2,1,0:T(8,128)(2,1)S(1)} %bitcast.105), channel_id=1, source_target_pairs={{0,16},{16,0},{1,17},{17,1},{2,18},{18,2},{3,19},{19,3},{4,20},{20... | collective-permute-start | bytes 6291464 | tf_op jit(solution)/shard_map/ppermute | solution.py:84
  95.0 87.5 %collective-permute-start.4 = (bf16[4,256,1024]{2,1,0:T(8,128)(2,1)S(1)}, bf16[4,256,1024]{2,1,0:T(8,128)(2,1)}, u32[]{:S(2)}, u32[]{:S(2)}) collective-permute-start(bf16[4,256,1024]{2,1,0:T(8,128)(2,1)S(1)} %bitcast.106), channel_id=1, source_target_pairs={{0,2},{1,3},{2,0},{3,1},{4,6},{5,7},{6,4},{7,5},{8,10},{9,11},{10,... | collective-permute-start | bytes 6291464 | tf_op jit(solution)/shard_map/ppermute | solution.py:81
  98.5 134.5 %collective-permute-start.8 = (bf16[4,256,1024]{2,1,0:T(8,128)(2,1)S(1)}, bf16[4,256,1024]{2,1,0:T(8,128)(2,1)}, u32[]{:S(2)}, u32[]{:S(2)}) collective-permute-start(bf16[4,256,1024]{2,1,0:T(8,128)(2,1)S(1)} %bitcast.107), channel_id=1, source_target_pairs={{0,1},{1,0},{2,3},{3,2},{4,5},{5,4},{6,7},{7,6},{8,9},{9,8},{10,11... | collective-permute-start | bytes 6291464 | tf_op jit(solution)/shard_map/ppermute | solution.py:81
  182.5 66.4 %collective-permute-start.6 = (bf16[4,256,1024]{2,1,0:T(8,128)(2,1)}, bf16[4,256,1024]{2,1,0:T(8,128)(2,1)}, u32[]{:S(2)}, u32[]{:S(2)}) collective-permute-start(bf16[4,256,1024]{2,1,0:T(8,128)(2,1)} %collective-permute-done.4.rest_0_), channel_id=1, source_target_pairs={{0,16},{16,0},{1,17},{17,1},{2,18},{18,2},{3,19},{19,3},{4,20},{20... | collective-permute-start | bytes 6291464 | tf_op jit(solution)/shard_map/ppermute | solution.py:84
  183.7 109.3 %collective-permute-start.5 = (bf16[4,256,1024]{2,1,0:T(8,128)(2,1)}, bf16[4,256,1024]{2,1,0:T(8,128)(2,1)}, u32[]{:S(2)}, u32[]{:S(2)}) collective-permute-start(bf16[4,256,1024]{2,1,0:T(8,128)(2,1)} %collective-permute-done.4.rest_0_), channel_id=1, source_target_pairs={{0,1},{1,0},{2,3},{3,2},{4,5},{5,4},{6,7},{7,6},{8,9},{9,8},{10,11... | collective-permute-start | bytes 6291464 | tf_op jit(solution)/shard_map/ppermute | solution.py:81
  184.9 48.1 %collective-permute-start.10 = (bf16[4,256,1024]{2,1,0:T(8,128)(2,1)}, bf16[4,256,1024]{2,1,0:T(8,128)(2,1)}, u32[]{:S(2)}, u32[]{:S(2)}) collective-permute-start(bf16[4,256,1024]{2,1,0:T(8,128)(2,1)} %collective-permute-done.9.rest_1_), channel_id=1, source_target_pairs={{0,1},{1,0},{2,3},{3,2},{4,5},{5,4},{6,7},{7,6},{8,9},{9,8},{10,11... | collective-permute-start | bytes 6291464 | tf_op jit(solution)/shard_map/ppermute | solution.py:81
  200.3 1.3 copy-start.7
  202.7 2.4 copy-start.5
  206.1 13.1 %copy-start.6 = (bf16[384,16]{0,1:T(8,128)(2,1)S(1)}, bf16[384,16]{0,1:T(8,128)(2,1)}, u32[]{:S(2)}) copy-start(bf16[384,16]{0,1:T(8,128)(2,1)} %copy-done.5) | copy-start | bytes 36868
  208.0 32.2 %all-to-all-start.1 = ((bf16[16,24,768]{2,1,0:T(8,128)(2,1)}), bf16[16,24,768]{2,1,0:T(8,128)(2,1)}, u32[]{:S(2)}, u32[]{:S(2)}) async-start(bf16[16,24,768]{2,1,0:T(8,128)(2,1)} %pad_maximum_fusion.2), calls=%async_computation.1 | async-start | bytes 1179648 | tf_op jit(solution)/shard_map/all_to_all | solution.py:482
  256.0 7.7 %copy-start.8 = (s32[48]{0:T(128)S(1)}, s32[48]{0:T(128)}, u32[]{:S(2)}) copy-start(s32[48]{0:T(128)} %and_select_fusion) | copy-start | bytes 580
  256.0 8.0 %copy-start.2 = (bf16[16,24,512]{2,1,0:T(8,128)(2,1)S(1)}, bf16[16,24,512]{2,1,0:T(8,128)(2,1)}, u32[]{:S(2)}) copy-start(bf16[16,24,512]{2,1,0:T(8,128)(2,1)} %get-tuple-element.25) | copy-start | bytes 1179652
  256.0 37.0 %collective-permute-start.7 = (bf16[4,256,1024]{2,1,0:T(8,128)(2,1)}, bf16[4,256,1024]{2,1,0:T(8,128)(2,1)}, u32[]{:S(2)}, u32[]{:S(2)}) collective-permute-start(bf16[4,256,1024]{2,1,0:T(8,128)(2,1)} %shard_map.100), channel_id=1, source_target_pairs={{0,1},{1,0},{2,3},{3,2},{4,5},{5,4},{6,7},{7,6},{8,9},{9,8},{10,11... | collective-permute-start | bytes 6291464 | tf_op jit(solution)/shard_map/ppermute | solution.py:81
  256.2 34.3 %all-to-all-start.2 = ((bf16[16,48,512]{2,1,0:T(8,128)(2,1)}), bf16[16,48,512]{2,1,0:T(8,128)(2,1)S(1)}, u32[]{:S(2)}, u32[]{:S(2)}) async-start(bf16[16,48,512]{2,1,0:T(8,128)(2,1)} %bitcast.35), calls=%async_computation.2 | async-start | bytes 1572864 | tf_op jit(solution)/shard_map/all_to_all | solution.py:490
  266.2 19.4 %collective-permute-start.11 = (f32[16,1024]{1,0:T(8,128)S(1)}, f32[16,1024]{1,0:T(8,128)S(1)}, u32[]{:S(2)}, u32[]{:S(2)}) collective-permute-start(f32[16,1024]{1,0:T(8,128)S(1)} %get-tuple-element.14), channel_id=1, source_target_pairs={{0,15},{1,0},{2,1},{3,2},{4,3},{5,4},{6,5},{7,6},{8,7},{9,8},{10,9... | collective-permute-start | bytes 196616 | tf_op jit(solution)/shard_map/ppermute | solution.py:21
  279.5 6.9 %collective-permute-start.12 = (f32[16,1024]{1,0:T(8,128)S(1)}, f32[16,1024]{1,0:T(8,128)S(1)}, u32[]{:S(2)}, u32[]{:S(2)}) collective-permute-start(f32[16,1024]{1,0:T(8,128)S(1)} %get-tuple-element.14), channel_id=1, source_target_pairs={{0,14},{1,15},{2,0},{3,1},{4,2},{5,3},{6,4},{7,5},{8,6},{9,7},{10,... | collective-permute-start | bytes 196616 | tf_op jit(solution)/shard_map/ppermute | solution.py:21
  283.9 4.0 %collective-permute-start.13 = (f32[16,1024]{1,0:T(8,128)S(1)}, f32[16,1024]{1,0:T(8,128)S(1)}, u32[]{:S(2)}, u32[]{:S(2)}) collective-permute-start(f32[16,1024]{1,0:T(8,128)S(1)} %get-tuple-element.14), channel_id=1, source_target_pairs={{0,13},{1,14},{2,15},{3,0},{4,1},{5,2},{6,3},{7,4},{8,5},{9,6},{10... | collective-permute-start | bytes 196616 | tf_op jit(solution)/shard_map/ppermute | solution.py:21
  285.5 4.1 %collective-permute-start.14 = (f32[16,1024]{1,0:T(8,128)S(1)}, f32[16,1024]{1,0:T(8,128)S(1)}, u32[]{:S(2)}, u32[]{:S(2)}) collective-permute-start(f32[16,1024]{1,0:T(8,128)S(1)} %get-tuple-element.14), channel_id=1, source_target_pairs={{0,12},{1,13},{2,14},{3,15},{4,0},{5,1},{6,2},{7,3},{8,4},{9,5},{1... | collective-permute-start | bytes 196616 | tf_op jit(solution)/shard_map/ppermute | solution.py:21
Sparse Core Ops, SparseCore 0:
  9.6 54.8 all-gather.2

commit v14 on v11

--- a/solution.py
+++ b/solution.py
@@ -66,15 +66,16 @@
     return (high * DIGIT + middle) * DIGIT + low, place_high * DIGIT + place
 
 
-CHUNKS = 2
-
-
-def weight_pieces(weight):
+def weight_column(weight):
     count = lax.axis_size("blk")
     half = weight.shape[0] // 2
-    size = half // CHUNKS
-    first = lax.axis_index("groups") * half
     lines = [list(range(k, count, 4)) for k in range(4)]
+    mine = lax.dynamic_slice_in_dim(weight, lax.axis_index("groups") * half, half, 0)
+    return lax.all_gather(mine, "blk", axis_index_groups=lines)
+
+
+def weight_quarters(column):
+    count = lax.axis_size("blk")
 
     def over(piece, bit):
         return lax.ppermute(piece, "blk", [(i, i ^ bit) for i in range(count)])
@@ -82,38 +83,33 @@
     def groups(piece):
         return lax.ppermute(piece, "groups", [(0, 1), (1, 0)])
 
-    column = lax.all_gather(
-        lax.dynamic_slice_in_dim(weight, first, half, 0), "blk", axis_index_groups=lines
-    )
-    columns = [column[:, k * size : (k + 1) * size] for k in range(CHUNKS)]
-    pieces = []
-    for mine in (columns, [over(column, 2) for column in columns]):
-        both = mine + [groups(piece) for piece in mine]
-        pieces += [both, [over(piece, 1) for piece in both]]
-    return pieces
-
-
-def quarter_kernel(where, cot, grad, down, *rest):
-    pieces = rest[: 2 * CHUNKS]
+    own = [column, groups(column)]
+    across = over(column, 2)
+    across = [across, groups(across)]
+
+    def quarter(number, late=None):
+        mine, theirs = across if number >= 2 else own
+        if number % 2 == 0:
+            return [mine, theirs]
+        if late is not None:
+            theirs = after(theirs, late)
+        return [over(mine, 1), over(theirs, 1)]
+
+    return quarter
+
+
+def quarter_kernel(where, cot, grad, down, mine, theirs, *rest):
     out, token = rest[-2:]
     token[...] = jnp.zeros_like(token)
-    rank = grad.shape[1]
-    lora = [
-        adapter_scale
-        * dot(
-            grad[b * BLOCK : (b + 1) * BLOCK, :],
-            down[b * rank : (b + 1) * rank, :],
-            ((1,), (0,)),
-        )
-        for b in range(cot.shape[0] // BLOCK)
-    ]
-    lora = jnp.concatenate(lora, axis=0).astype(jnp.bfloat16).astype(jnp.float32)
+    half = mine.shape[1]
+    lora = adapter_scale * dot(grad[...], down[...], ((1,), (0,)))
+    lora = lora.astype(jnp.bfloat16).astype(jnp.float32)
 
     def product(group):
-        order = pieces[group * CHUNKS :] + pieces[: group * CHUNKS]
-        weight = jnp.concatenate([piece[0] for piece in order], axis=0)
-        frozen = dot(cot[...], weight, ((1,), (1,)))
-        out[...] = (frozen + lora).astype(jnp.bfloat16)
+        for k, piece in enumerate((mine, theirs) if group == 0 else (theirs, mine)):
+            part = slice(k * half, (k + 1) * half)
+            frozen = dot(cot[...], piece[0], ((1,), (1,)))
+            out[:, part] = (frozen + lora[:, part]).astype(jnp.bfloat16)
 
     for group in range(2):
         pl.when(where[1] == group)(functools.partial(product, group))
@@ -163,12 +159,11 @@
 
 def together(pieces, firsts, group):
     shards, part, depth = pieces[0][0].shape
-    weight = jnp.zeros((shards, 4, 2, CHUNKS, part, depth), jnp.bfloat16)
+    weight = jnp.zeros((shards, 4, 2, part, depth), jnp.bfloat16)
     for quarter, first in zip(pieces, firsts):
         for k, piece in enumerate(quarter):
-            half = group if k < CHUNKS else 1 - group
-            place = (0, first, half, k % CHUNKS, 0, 0)
-            weight = lax.dynamic_update_slice(weight, piece[:, None, None, None], place)
+            place = (0, first, group if k == 0 else 1 - group, 0, 0)
+            weight = lax.dynamic_update_slice(weight, piece[:, None, None], place)
     return weight.reshape(-1, depth)
 
 
@@ -300,7 +295,8 @@
 
 def hidden_kernel(act, maps, rows, spots, starts, out):
     sources, share, width = act.shape[0], maps.shape[1], rows.shape[1]
-    rank, places = out.shape[0] // sources, out.shape[1]
+    _, height, places = out.shape
+    rank = height // sources
     slot = slot_of(rows[...], starts[...])
     every = all_rows(act, width // sources)
     total = jnp.zeros((rank, width), jnp.float32)
@@ -309,11 +305,12 @@
         some = maps[part.start // share : part.stop // share].reshape(size, -1)
         each = dot(some, every, ((1,), (1,))).reshape(size // rank, rank, -1)
         total += jnp.sum(jnp.where(own_rows(slot, part.start, size, rank), each, 0.0), axis=0)
-    total = jnp.where(of_source(sources, width), total[None], 0.0).reshape(out.shape[0], width)
+    total = jnp.where(of_source(sources, width), total[None], 0.0).reshape(height, width)
     high = total.astype(jnp.bfloat16)
     low = (total - high.astype(jnp.float32)).astype(jnp.bfloat16)
     place = placing(spots[...], places)
-    out[...] = dot(high, place, ((1,), (1,))) + dot(low, place, ((1,), (1,)))
+    for k, part in enumerate((high, low)):
+        out[k] = dot(part, place, ((1,), (1,))).astype(out.dtype)
 
 
 def down_kernel(act, grad, rows, spots, starts, out, total):
@@ -361,8 +358,8 @@
         hidden_kernel,
         grid=grid,
         in_specs=[act, maps, rows, rows, begin],
-        out_specs=placed,
-        out_shape=jax.ShapeDtypeStruct((devices * rank, places), jnp.float32),
+        out_specs=pl.BlockSpec((2, sources * rank, places), lambda j: (0, j, 0)),
+        out_shape=jax.ShapeDtypeStruct((2, devices * rank, places), received.dtype),
         cost_estimate=cost,
         compiler_params=params,
     )
@@ -399,7 +396,7 @@
     cap = resident_rows // devices
     start_ids = tenant_first_row // BLOCK
 
-    pieces = weight_pieces(frozen_value_weight)
+    column = weight_column(frozen_value_weight)
 
     first_block = device * resident
     block_numbers = first_block + jnp.arange(resident, dtype=jnp.int32)
@@ -431,8 +428,6 @@
     up_blocks = of_blocks(adapter_up_maps, carried[:, width:])
 
     sent_rows = pack_rows(token_layout_row, cotangent, devices, cap, features)
-    own, _, across, _ = pieces
-    sent_rows = after(sent_rows, own[0], own[1], carried)
     got_rows = lax.all_to_all(sent_rows, "blk", split_axis=0, concat_axis=0)
     recv_cot = [
         got_rows[:, k * cap : (k + 1) * cap].reshape(resident_rows, features)
@@ -443,6 +438,10 @@
     digits = digits.reshape(devices, 5, per_digit * features)[:, :, :tokens]
     rows_all, place_all = from_digits(digits)
 
+    flat_maps = adapter_down_maps.reshape(share, width)
+    received = after(pack_features(activations, flat_maps, devices), got_rows)
+    received = lax.all_to_all(received, "blk", split_axis=0, concat_axis=0)
+
     spots = device * cap + jnp.arange(cap, dtype=jnp.int32)
     hit = place_all[:, None, :] == spots[None, :, None]
     row_in = rows_all - device * resident_rows + 1
@@ -459,54 +458,45 @@
     grad_in = sum(grad_in[:, b * rank : (b + 1) * rank] for b in range(resident))
     grad_sent = grad_in.reshape(devices, cap, rank).transpose(1, 0, 2).reshape(cap, -1)
 
-    flat_maps = adapter_down_maps.reshape(share, width)
-    received = pack_features(activations, flat_maps, devices)
-    received = after(received, got_rows, own[CHUNKS], across[0])
-    received = lax.all_to_all(received, "blk", split_axis=0, concat_axis=0)
-    grad_all = to_all(after(grad_sent, received)).reshape(resident_rows, -1).T
-
     rows_all, place_all = rows_all.reshape(1, -1), place_all.reshape(1, -1)
 
     cot_rows = jnp.concatenate(
         [dot(arrange, part, ((0,), (0,))).astype(jnp.bfloat16) for part in recv_cot], axis=1
     )
     grad_rows = dot(arrange, grad_in, ((0,), (0,))).astype(jnp.bfloat16)
+
+    in_rows = jnp.arange(resident_rows, dtype=jnp.int32)[:, None] // BLOCK
+    in_rows = in_rows == jnp.arange(share, dtype=jnp.int32)[None, :] // rank
+    grad_wide = jnp.where(in_rows, jnp.concatenate([grad_rows] * resident, axis=1), 0)
     group = lax.axis_index("groups")
-    quarter = device % 4
-    firsts = [quarter, quarter ^ 1, quarter ^ 2, quarter ^ 3]
-    if own[0].shape[1] % LANES == 0:
+    firsts = [(device % 4) ^ k for k in range(4)]
+    pieces = weight_quarters(column)
+    tiled = column.shape[1] % LANES == 0
+    if tiled:
         out = None
-        for number, (piece, first) in enumerate(zip(pieces, firsts)):
+        for quarter in (0, 1):
             out, token = write_quarter(
-                piece, first, group, cot_rows, grad_rows, down_blocks, out
+                pieces(quarter), firsts[quarter], group, cot_rows, grad_wide, down_blocks, out
             )
-            if number == 3:
-                place_all = after(place_all, token)
-    else:
-        weight = together(pieces, firsts, group)
-        lora = [
-            dot(
-                grad_rows[b * BLOCK : (b + 1) * BLOCK],
-                down_blocks[b * rank : (b + 1) * rank],
-                ((1,), (0,)),
-            )
-            for b in range(resident)
-        ]
-        lora = (adapter_scale * jnp.concatenate(lora, axis=0)).astype(jnp.bfloat16)
-        out = dot(cot_rows, weight, ((1,), (1,))) + lora.astype(jnp.float32)
-        out = out.astype(jnp.bfloat16)
+        place_all = after(place_all, token)
 
     starts = start_ids[:, None]
     hidden_call, down_call = feature_calls(
         received, tokens, share, rank, resident_rows, starts.shape[0]
     )
     shares = hidden_call(received, received, rows_all, place_all, starts)
-    rows_all = after(rows_all, shares)
+
+    shares = shares.reshape(-1, resident_rows).T.reshape(devices, cap, -1)
+    copies = jnp.broadcast_to(grad_sent[None], (devices,) + grad_sent.shape)
+    small = jnp.concatenate([copies, shares], axis=2)
+    small = lax.all_to_all(small, "blk", split_axis=0, concat_axis=0)
+    each = devices * rank
+    grad_all = small[:, :, :each].reshape(resident_rows, each).T
+    hidden = jnp.sum(small[:, :, each:].astype(jnp.float32), axis=0)
+    hidden = (hidden[:, :each] + hidden[:, each:]).astype(jnp.bfloat16)
+    hidden = hidden.reshape(cap, devices, rank).transpose(1, 0, 2).reshape(-1, rank)
+
     down_f = down_call(received, grad_all, rows_all, place_all, starts)
-    hidden = shares.T.reshape(devices, cap, -1)
-    hidden = lax.all_to_all(hidden, "blk", split_axis=0, concat_axis=0)
-    hidden = jnp.sum(hidden, axis=0).astype(jnp.bfloat16)
-    hidden = hidden.reshape(cap, devices, rank).transpose(1, 0, 2).reshape(-1, rank)
     down_home = lax.all_to_all(down_f, "blk", split_axis=0, concat_axis=1, tiled=True)
     down_map_gradient = down_home.astype(jnp.float32).reshape(resident, rank, width)
 
@@ -529,6 +519,17 @@
         up_grads.append(adapter_scale * total)
     up_map_gradient = jnp.stack(up_grads)
 
+    if tiled:
+        late = after(grad_wide, down_f)
+        for quarter in (2, 3):
+            out, _ = write_quarter(
+                pieces(quarter, shares), firsts[quarter], group, cot_rows, late, down_blocks, out
+            )
+    else:
+        weight = together([pieces(k, shares) for k in range(4)], firsts, group)
+        lora = adapter_scale * dot(grad_wide, down_blocks, ((1,), (0,)))
+        out = dot(cot_rows, weight, ((1,), (1,)))
+        out = (out + lora.astype(jnp.bfloat16).astype(jnp.float32)).astype(jnp.bfloat16)
     return (out, down_map_gradient, up_map_gradient)
 
 

time: 321 us -> 324 us (level)
  starting transfers between devices: 64.2 us -> 103 us
  waiting for transfers between devices: 118 us -> 98.1 us
  local copies, waits for them, and re-layouts: 26.5 us -> 17.6 us
  matrix products: 6.21 us -> 2.3 us
    ppermute x4 -> x2, waiting for transfers between devices: 43.2 us -> 4.86 us  [groups(): return lax.ppermute(piece, 'groups', [(0, 1), (1, 0)])]
    ppermute x10 -> x5, starting transfers between devices: 7.34 us -> 41.3 us  [over(): return lax.ppermute(piece, 'blk', [(i, i ^ bit) for i in range(count)])]
    all_to_all x1, starting transfers between devices: 5.56 us -> 30.7 us  [local(): received = lax.all_to_all(received, 'blk', split_axis=0, concat_axis=0)]
    ppermute x8, waiting for transfers between devices: 25 us -> 3.27 us  [moved(): lax.ppermute(value, 'blk', [(i, (i + steps) % count) for i in range(count)])]
    all_gather x1, waiting for transfers between devices: 11.4 us -> 25.7 us  [weight_column(): return lax.all_gather(mine, 'blk', axis_index_groups=lines)]
    all_to_all x2 -> x1, waiting for transfers between devices: 3.43 us -> 14.5 us  [local(): small = lax.all_to_all(small, 'blk', split_axis=0, concat_axis=0)]
    all_to_all x1, starting transfers between devices: 17 us -> 7.32 us  [local(): got_rows = lax.all_to_all(sent_rows, 'blk', split_axis=0, concat_axis=0)]
    ppermute x10 -> x5, waiting for transfers between devices: 35.1 us -> 44.4 us  [over(): return lax.ppermute(piece, 'blk', [(i, i ^ bit) for i in range(count)])]
  transfers between devices with their start and end apart: 28 -> 20, of which waited for: 9 -> 7; matrix products, arithmetic and copies ran while one was open for 11% -> 9% of each run, Pallas kernels for 16% -> 13%
where the time goes in v14:
time: 324 us; the launch traced here: 323 us
  starting transfers between devices  103 us (32%)
  waiting for transfers between devices  98.1 us (30%)
  Pallas kernels  50.7 us (16%)
  between operations  38.4 us (12%)
  local copies, waits for them, and re-layouts  17.6 us (5%)
  other arithmetic  12.5 us (4%)
    ppermute x5, waiting for transfers between devices, over(): return lax.ppermute(piece, 'blk', [(i, i ^ bit) for i in range(count)])  44.4 us
    ppermute x5, starting transfers between devices, over(): return lax.ppermute(piece, 'blk', [(i, i ^ bit) for i in range(count)])  41.3 us
    all_to_all x1, starting transfers between devices, local(): received = lax.all_to_all(received, 'blk', split_axis=0, concat_axis=0)  30.7 us
    pallas_call x4, Pallas kernels, write_quarter(): pl.pallas_call(quarter_kernel, grid_spec=pltpu.PrefetchScalarGridSpec(num...  28.6 us
    all_gather x1, waiting for transfers between devices, weight_column(): return lax.all_gather(mine, 'blk', axis_index_groups=lines)  25.7 us
    all_to_all x1, waiting for transfers between devices, local(): small = lax.all_to_all(small, 'blk', split_axis=0, concat_axis=0)  14.5 us
    ppermute x8, starting transfers between devices, moved(): lax.ppermute(value, 'blk', [(i, (i + steps) % count) for i in range(count)])  12 us
    pallas_call x1, Pallas kernels, local(): shares = hidden_call(received, received, rows_all, place_all, starts)  8.25 us
  transfers between devices with their start and end apart: 20, of which 7 were waited for; matrix products, arithmetic and copies ran while one was open for 9% of the time, Pallas kernels for 13%

profile of v14, /device:TPU:1, one launch (start us, length us, event | category | flops | bytes accessed | tf_op | source)
XLA Modules:
  0.0 322.6 jit_solution(18387172191207280986)
XLA Ops:
  7.2 1.4 concatenate.27
  8.5 2.6 shard_map.94
  11.1 7.3 %all-to-all-start = ((bf16[16,64,512]{2,1,0:T(8,128)(2,1)}), bf16[16,64,512]{2,1,0:T(8,128)(2,1)S(1)}, u32[]{:S(2)}, u32[]{:S(2)}) async-start(bf16[16,64,512]{2,1,0:T(8,128)(2,1)} %shard_map.94), calls=%async_computation | async-start | bytes 2097152 | tf_op jit(solution)/shard_map/all_to_all | solution.py:431
  18.6 0.7 fusion.24
  22.4 1.0 dynamic-slice_bitcast_fusion
  23.4 1.4 collective-permute-start
  24.9 1.7 collective-permute-start.1
  26.6 1.2 collective-permute-start.2
  27.8 1.2 collective-permute-start.3
  29.0 0.8 constant_dynamic-slice_fusion
  40.5 4.6 %shard_map.95.refs_0_ = bf16[16,240,512]{2,1,0:T(8,128)(2,1)} custom-call(bf16[192,8192]{1,0:T(8,128)(2,1)} %act.1, bf16[48,8192]{1,0:T(8,128)(2,1)} %bitcast.104), custom_call_target="tpu_custom_call" | custom-call | bytes 7864320 | tf_op jit(solution)/shard_map/pallas_call | solution.py:244
  46.3 5.4 %all-to-all-done.refs_1_ = bf16[16,64,512]{2,1,0:T(8,128)(2,1)S(1)} async-done(((bf16[16,64,512]{2,1,0:T(8,128)(2,1)}), bf16[16,64,512]{2,1,0:T(8,128)(2,1)S(1)}, u32[]{:S(2)}, u32[]{:S(2)}) %all-to-all-start) | async-done | bytes 1048608 | tf_op jit(solution)/shard_map/all_to_all | solution.py:431
  51.7 1.0 copy-done.2
  52.7 30.7 %all-to-all-start.1 = ((bf16[16,240,512]{2,1,0:T(8,128)(2,1)}), bf16[16,240,512]{2,1,0:T(8,128)(2,1)}, u32[]{:S(2)}, u32[]{:S(2)}) async-start(bf16[16,240,512]{2,1,0:T(8,128)(2,1)} %shard_map.96), calls=%async_computation.1 | async-start | bytes 7864320 | tf_op jit(solution)/shard_map/all_to_all | solution.py:443
  83.5 1.0 copy-done.4
  84.6 25.7 %all-gather.3.cloned.1.call-done = bf16[1024,1024]{1,0:T(8,128)(2,1)} async-done(((bf16[256,1024]{1,0:T(8,128)(2,1)}), bf16[1024,1024]{1,0:T(8,128)(2,1)}) %all-gather.3.cloned.1.call-update) | async-done | bytes 2097168 | tf_op jit(solution)/shard_map/all_gather | solution.py:74
  110.3 1.3 collective-permute-start.5
  111.5 0.9 pad_maximum_fusion.1.down
  113.2 38.0 %collective-permute-start.7 = (bf16[4,256,1024]{2,1,0:T(8,128)(2,1)}, bf16[4,256,1024]{2,1,0:T(8,128)(2,1)}, u32[]{:S(2)}, u32[]{:S(2)}) collective-permute-start(bf16[4,256,1024]{2,1,0:T(8,128)(2,1)} %bitcast.26.mine), channel_id=1, source_target_pairs={{0,2},{1,3},{2,0},{3,1},{4,6},{5,7},{6,4},{7,5},{8,10},{9,11},{10,... | collective-permute-start | bytes 6291464 | tf_op jit(solution)/shard_map/ppermute | solution.py:81
  151.3 1.1 collective-permute-start.4
  152.4 4.9 %collective-permute-done.5.theirs = bf16[4,256,1024]{2,1,0:T(8,128)(2,1)} collective-permute-done((bf16[4,256,1024]{2,1,0:T(8,128)(2,1)}, bf16[4,256,1024]{2,1,0:T(8,128)(2,1)}, u32[]{:S(2)}, u32[]{:S(2)}) %collective-permute-start.5) | collective-permute-done | bytes 2097184 | tf_op jit(solution)/shard_map/ppermute | solution.py:84
  157.2 1.4 collective-permute-start.6
  161.2 0.8 compare_select_fusion.1.grad.refs_0_
  163.0 44.4 %collective-permute-done.7.mine = bf16[4,256,1024]{2,1,0:T(8,128)(2,1)} collective-permute-done((bf16[4,256,1024]{2,1,0:T(8,128)(2,1)}, bf16[4,256,1024]{2,1,0:T(8,128)(2,1)}, u32[]{:S(2)}, u32[]{:S(2)}) %collective-permute-start.7) | collective-permute-done | bytes 2097184 | tf_op jit(solution)/shard_map/ppermute | solution.py:81
  207.6 1.0 pad_maximum_fusion.cot
  208.6 7.2 %shard_map.97 = (bf16[384,8192]{1,0:T(8,128)(2,1)}, f32[8,128]{1,0:T(8,128)}) custom-call(s32[2]{0:T(128)} %pad_add_fusion.2.where, bf16[384,1024]{1,0:T(8,128)(2,1)} %pad_maximum_fusion.cot, bf16[384,48]{1,0:T(8,128)(2,1)} %compare_select_fusion.1.grad.refs_0_, bf16[48,8192]{1,0:T(8,128)(2,1)} %pad_maximum_fusion.1.down, ...), custom_call_target="tpu_custom_call" | custom-call | flops 1610612736 | bytes 5767168 | tf_op jit(solution)/shard_map/pallas_call | solution.py:135
  215.8 7.1 %shard_map.98 = (bf16[384,8192]{1,0:T(8,128)(2,1)}, f32[8,128]{1,0:T(8,128)}) custom-call(s32[2]{0:T(128)} %pad_add_fusion.1.where, bf16[384,1024]{1,0:T(8,128)(2,1)} %pad_maximum_fusion.cot, bf16[384,48]{1,0:T(8,128)(2,1)} %compare_select_fusion.1.grad.refs_0_, bf16[48,8192]{1,0:T(8,128)(2,1)} %pad_maximum_fusion.1.down, ...), custom_call_target="tpu_custom_call", output_to_operand_aliasing={{0}: (6, {})} | custom-call | flops 1610612736 | bytes 5767168 | tf_op jit(solution)/shard_map/pallas_call | solution.py:135
  222.9 8.3 %shard_map.100 = bf16[2,256,384]{2,1,0:T(8,128)(2,1)} custom-call(bf16[16,240,512]{2,1,0:T(8,128)(2,1)} %all-to-all-done.1.act.maps, bf16[16,240,512]{2,1,0:T(8,128)(2,1)} %all-to-all-done.1.act.maps, s32[1,3072]{1,0:T(1,128)} %reshape.356.rows, s32[1,3072]{1,0:T(1,128)} %shard_map.99.spots, s32[32,1]{1,0:T(8,128)} %copy.61.starts), custom_call_target="tpu_custom_call" | custom-call | flops 2415919104 | bytes 3145728 | tf_op jit(solution)/shard_map/pallas_call | solution.py:487
  231.2 1.2 copy.62
  232.4 0.9 pad_maximum_fusion.2
  233.3 5.5 %all-to-all-start.2 = ((bf16[16,24,768]{2,1,0:T(8,128)(2,1)}), bf16[16,24,768]{2,1,0:T(8,128)(2,1)}, u32[]{:S(2)}, u32[]{:S(2)}) async-start(bf16[16,24,768]{2,1,0:T(8,128)(2,1)} %pad_maximum_fusion.2), calls=%async_computation.2 | async-start | bytes 1179648 | tf_op jit(solution)/shard_map/all_to_all | solution.py:492
  239.7 14.5 %all-to-all-done.2 = bf16[16,24,768]{2,1,0:T(8,128)(2,1)} async-done(((bf16[16,24,768]{2,1,0:T(8,128)(2,1)}), bf16[16,24,768]{2,1,0:T(8,128)(2,1)}, u32[]{:S(2)}, u32[]{:S(2)}) %all-to-all-start.2) | async-done | bytes 589856 | tf_op jit(solution)/shard_map/all_to_all | solution.py:492
  254.1 1.6 slice.217
  255.8 1.7 copy.63
  257.5 6.7 %shard_map.101.refs_1_ = bf16[768,512]{1,0:T(8,128)(2,1)} custom-call(bf16[16,240,512]{2,1,0:T(8,128)(2,1)} %all-to-all-done.1.act.maps, bf16[256,384]{1,0:T(8,128)(2,1)} %bitcast.118, s32[1,3072]{1,0:T(1,128)} %reshape.356.rows, s32[1,3072]{1,0:T(1,128)} %shard_map.99.spots, s32[32,1]{1,0:T(8,128)} %copy.61.starts), custom_call_target="tpu_custom_call" | custom-call | flops 2415919104 | bytes 3145728 | tf_op jit(solution)/shard_map/pallas_call | solution.py:499
  264.2 1.3 copy-done.1
  265.5 7.2 %shard_map.104 = (bf16[384,8192]{1,0:T(8,128)(2,1)}, f32[8,128]{1,0:T(8,128)}) custom-call(s32[2]{0:T(128)} %pad_add_fusion.3.where, bf16[384,1024]{1,0:T(8,128)(2,1)} %pad_maximum_fusion.cot, bf16[384,48]{1,0:T(8,128)(2,1)} %shard_map.102.grad, bf16[48,8192]{1,0:T(8,128)(2,1)} %pad_maximum_fusion.1.down, ...), custom_call_target="tpu_custom_call", output_to_operand_aliasing={{0}: (6, {})} | custom-call | flops 1610612736 | bytes 5767168 | tf_op jit(solution)/shard_map/pallas_call | solution.py:135
  273.2 1.1 convert_reduce_fusion
  274.7 4.6 %all-to-all-start.3 = ((bf16[16,48,512]{2,1,0:T(8,128)(2,1)}), bf16[16,48,512]{2,1,0:T(8,128)(2,1)S(1)}, u32[]{:S(2)}, u32[]{:S(2)}) async-start(bf16[16,48,512]{2,1,0:T(8,128)(2,1)} %bitcast.36), calls=%async_computation.3 | async-start | bytes 1572864 | tf_op jit(solution)/shard_map/all_to_all | solution.py:500
  280.0 1.9 select_add_fusion.1
  295.1 4.4 %collective-permute-start.12 = (f32[16,1024]{1,0:T(8,128)S(1)}, f32[16,1024]{1,0:T(8,128)S(1)}, u32[]{:S(2)}, u32[]{:S(2)}) collective-permute-start(f32[16,1024]{1,0:T(8,128)S(1)} %get-tuple-element.20), channel_id=1, source_target_pairs={{0,14},{1,15},{2,0},{3,1},{4,2},{5,3},{6,4},{7,5},{8,6},{9,7},{10,... | collective-permute-start | bytes 196616 | tf_op jit(solution)/shard_map/ppermute | solution.py:21
  299.5 1.7 collective-permute-start.13
  302.0 1.4 collective-permute-done.13
  303.4 1.8 collective-permute-done.14
  305.4 0.7 pad_maximum_fusion.4
  306.3 0.9 copy.65
  307.2 1.4 reshape.355
  308.6 7.1 %shard_map.105 = (bf16[384,8192]{1,0:T(8,128)(2,1)}, f32[8,128]{1,0:T(8,128)}) custom-call(s32[2]{0:T(128)} %pad_add_fusion.where, bf16[384,1024]{1,0:T(8,128)(2,1)} %pad_maximum_fusion.cot, bf16[384,48]{1,0:T(8,128)(2,1)} %shard_map.102.grad, bf16[48,8192]{1,0:T(8,128)(2,1)} %pad_maximum_fusion.1.down, ...), custom_call_target="tpu_custom_call", output_to_operand_aliasing={{0}: (6, {})} | custom-call | flops 1610612736 | bytes 5767168 | tf_op jit(solution)/shard_map/pallas_call | solution.py:135
  (101 shorter events, 12.8 us)
Async XLA Ops:
  7.2 21.8 %copy-start = (bf16[512,1024]{1,0:T(8,128)(2,1)S(1)}, bf16[512,1024]{1,0:T(8,128)(2,1)}, u32[]{:S(2)}) copy-start(bf16[512,1024]{1,0:T(8,128)(2,1)} %param.11) | copy-start | bytes 3145732
  7.2 11.4 %copy-start.13 = (s32[32]{0:T(128)S(1)}, s32[32]{0:T(128)}, u32[]{:S(2)}) copy-start(s32[32]{0:T(128)} %param.10) | copy-start | bytes 388
  8.5 14.8 %copy-start.10 = (bf16[3,16,1024]{2,1,0:T(8,128)(2,1)S(1)}, bf16[3,16,1024]{2,1,0:T(8,128)(2,1)}, u32[]{:S(2)}) copy-start(bf16[3,16,1024]{2,1,0:T(8,128)(2,1)} %param.13) | copy-start | bytes 294916
  11.1 40.6 %all-to-all-start = ((bf16[16,64,512]{2,1,0:T(8,128)(2,1)}), bf16[16,64,512]{2,1,0:T(8,128)(2,1)S(1)}, u32[]{:S(2)}, u32[]{:S(2)}) async-start(bf16[16,64,512]{2,1,0:T(8,128)(2,1)} %shard_map.94), calls=%async_computation | async-start | bytes 2097152 | tf_op jit(solution)/shard_map/all_to_all | solution.py:431
  18.5 91.8 %all-gather.3.cloned.1.call-start = ((), (), s32[]{:S(2)}) async-start(), calls=%async_computation.4 | async-start | bytes 2621440 | tf_op jit(solution)/shard_map/all_gather | solution.py:74
  23.4 59.9 %collective-permute-start = (bf16[16,9216]{1,0:T(8,128)(2,1)S(1)}, bf16[16,9216]{1,0:T(8,128)(2,1)S(1)}, u32[]{:S(2)}, u32[]{:S(2)}) collective-permute-start(bf16[16,9216]{1,0:T(8,128)(2,1)S(1)} %pad_maximum_fusion.3), channel_id=1, source_target_pairs={{0,4},{1,5},{2,6},{3,7},{4,8},{5,9},{6,10},{7,11},{8,12},{9,13},{1... | collective-permute-start | bytes 884744 | tf_op jit(solution)/shard_map/ppermute | solution.py:21
  24.9 58.5 %collective-permute-start.1 = (bf16[16,9216]{1,0:T(8,128)(2,1)S(1)}, bf16[16,9216]{1,0:T(8,128)(2,1)S(1)}, u32[]{:S(2)}, u32[]{:S(2)}) collective-permute-start(bf16[16,9216]{1,0:T(8,128)(2,1)S(1)} %pad_maximum_fusion.3), channel_id=1, source_target_pairs={{0,3},{1,4},{2,5},{3,6},{4,7},{5,8},{6,9},{7,10},{8,11},{9,12},{10... | collective-permute-start | bytes 884744 | tf_op jit(solution)/shard_map/ppermute | solution.py:21
  26.6 56.8 %collective-permute-start.2 = (bf16[16,9216]{1,0:T(8,128)(2,1)S(1)}, bf16[16,9216]{1,0:T(8,128)(2,1)S(1)}, u32[]{:S(2)}, u32[]{:S(2)}) collective-permute-start(bf16[16,9216]{1,0:T(8,128)(2,1)S(1)} %pad_maximum_fusion.3), channel_id=1, source_target_pairs={{0,2},{1,3},{2,4},{3,5},{4,6},{5,7},{6,8},{7,9},{8,10},{9,11},{10,... | collective-permute-start | bytes 884744 | tf_op jit(solution)/shard_map/ppermute | solution.py:21
  27.8 55.6 %collective-permute-start.3 = (bf16[16,9216]{1,0:T(8,128)(2,1)S(1)}, bf16[16,9216]{1,0:T(8,128)(2,1)}, u32[]{:S(2)}, u32[]{:S(2)}) collective-permute-start(bf16[16,9216]{1,0:T(8,128)(2,1)S(1)} %pad_maximum_fusion.3), channel_id=1, source_target_pairs={{0,1},{1,2},{2,3},{3,4},{4,5},{5,6},{6,7},{7,8},{8,9},{9,10},{10,1... | collective-permute-start | bytes 884744 | tf_op jit(solution)/shard_map/ppermute | solution.py:21
  45.0 116.2 %copy-start.11 = (s32[48]{0:T(128)}, s32[48]{0:T(128)S(1)}, u32[]{:S(2)}) copy-start(s32[48]{0:T(128)S(1)} %and_select_fusion.1) | copy-start | bytes 580
  51.7 1.0 copy-start.2
  52.7 170.2 %all-to-all-start.1 = ((bf16[16,240,512]{2,1,0:T(8,128)(2,1)}), bf16[16,240,512]{2,1,0:T(8,128)(2,1)}, u32[]{:S(2)}, u32[]{:S(2)}) async-start(bf16[16,240,512]{2,1,0:T(8,128)(2,1)} %shard_map.96), calls=%async_computation.1 | async-start | bytes 7864320 | tf_op jit(solution)/shard_map/all_to_all | solution.py:443
  83.4 1.1 copy-start.4
  83.5 29.0 %copy-start.3 = (bf16[16,64,512]{2,1,0:T(8,128)(2,1)S(1)}, bf16[16,64,512]{2,1,0:T(8,128)(2,1)}, u32[]{:S(2)}) copy-start(bf16[16,64,512]{2,1,0:T(8,128)(2,1)} %copy-done.2) | copy-start | bytes 3145732
  110.3 47.0 %collective-permute-start.5 = (bf16[4,256,1024]{2,1,0:T(8,128)(2,1)}, bf16[4,256,1024]{2,1,0:T(8,128)(2,1)}, u32[]{:S(2)}, u32[]{:S(2)}) collective-permute-start(bf16[4,256,1024]{2,1,0:T(8,128)(2,1)} %bitcast.26.mine), channel_id=1, source_target_pairs={{0,16},{16,0},{1,17},{17,1},{2,18},{18,2},{3,19},{19,3},{4,20},{20... | collective-permute-start | bytes 6291464 | tf_op jit(solution)/shard_map/ppermute | solution.py:84
  113.2 49.8 %copy-start.6 = (bf16[16,24,512]{2,1,0:T(8,128)(2,1)}, bf16[16,24,512]{2,1,0:T(8,128)(2,1)S(1)}, u32[]{:S(2)}) copy-start(bf16[16,24,512]{2,1,0:T(8,128)(2,1)S(1)} %get-tuple-element.34) | copy-start | bytes 1179652
  113.2 49.8 %copy-start.8 = (bf16[16,24,512]{2,1,0:T(8,128)(2,1)}, bf16[16,24,512]{2,1,0:T(8,128)(2,1)S(1)}, u32[]{:S(2)}) copy-start(bf16[16,24,512]{2,1,0:T(8,128)(2,1)S(1)} %get-tuple-element.35) | copy-start | bytes 1179652
  113.2 94.1 %collective-permute-start.7 = (bf16[4,256,1024]{2,1,0:T(8,128)(2,1)}, bf16[4,256,1024]{2,1,0:T(8,128)(2,1)}, u32[]{:S(2)}, u32[]{:S(2)}) collective-permute-start(bf16[4,256,1024]{2,1,0:T(8,128)(2,1)} %bitcast.26.mine), channel_id=1, source_target_pairs={{0,2},{1,3},{2,0},{3,1},{4,6},{5,7},{6,4},{7,5},{8,10},{9,11},{10,... | collective-permute-start | bytes 6291464 | tf_op jit(solution)/shard_map/ppermute | solution.py:81
  151.3 64.4 %collective-permute-start.4 = (bf16[4,256,1024]{2,1,0:T(8,128)(2,1)}, bf16[4,256,1024]{2,1,0:T(8,128)(2,1)}, u32[]{:S(2)}, u32[]{:S(2)}) collective-permute-start(bf16[4,256,1024]{2,1,0:T(8,128)(2,1)} %bitcast.26.mine), channel_id=1, source_target_pairs={{0,1},{1,0},{2,3},{3,2},{4,5},{5,4},{6,7},{7,6},{8,9},{9,8},{10,11... | collective-permute-start | bytes 6291464 | tf_op jit(solution)/shard_map/ppermute | solution.py:81
  157.2 58.5 %collective-permute-start.6 = (bf16[4,256,1024]{2,1,0:T(8,128)(2,1)}, bf16[4,256,1024]{2,1,0:T(8,128)(2,1)}, u32[]{:S(2)}, u32[]{:S(2)}) collective-permute-start(bf16[4,256,1024]{2,1,0:T(8,128)(2,1)} %collective-permute-done.5.theirs), channel_id=1, source_target_pairs={{0,1},{1,0},{2,3},{3,2},{4,5},{5,4},{6,7},{7,6},{8,9},{9,8},{10,11... | collective-permute-start | bytes 6291464 | tf_op jit(solution)/shard_map/ppermute | solution.py:81
  207.4 56.9 %collective-permute-start.9 = (bf16[4,256,1024]{2,1,0:T(8,128)(2,1)}, bf16[4,256,1024]{2,1,0:T(8,128)(2,1)S(1)}, u32[]{:S(2)}, u32[]{:S(2)}) collective-permute-start(bf16[4,256,1024]{2,1,0:T(8,128)(2,1)} %collective-permute-done.7.mine), channel_id=1, source_target_pairs={{0,16},{16,0},{1,17},{17,1},{2,18},{18,2},{3,19},{19,3},{4,20},{20... | collective-permute-start | bytes 6291464 | tf_op jit(solution)/shard_map/ppermute | solution.py:84
  232.3 31.9 %copy-start.5 = (bf16[512,384]{0,1:T(8,128)(2,1)}, bf16[512,384]{0,1:T(8,128)(2,1)S(1)}, u32[]{:S(2)}) copy-start(bf16[512,384]{0,1:T(8,128)(2,1)S(1)} %copy.62) | copy-start | bytes 1179652
  233.3 20.9 %all-to-all-start.2 = ((bf16[16,24,768]{2,1,0:T(8,128)(2,1)}), bf16[16,24,768]{2,1,0:T(8,128)(2,1)}, u32[]{:S(2)}, u32[]{:S(2)}) async-start(bf16[16,24,768]{2,1,0:T(8,128)(2,1)} %pad_maximum_fusion.2), calls=%async_computation.2 | async-start | bytes 1179648 | tf_op jit(solution)/shard_map/all_to_all | solution.py:492
  239.4 69.2 %collective-permute-start.8 = (bf16[4,256,1024]{2,1,0:T(8,128)(2,1)}, bf16[4,256,1024]{2,1,0:T(8,128)(2,1)}, u32[]{:S(2)}, u32[]{:S(2)}) collective-permute-start(bf16[4,256,1024]{2,1,0:T(8,128)(2,1)} %collective-permute-done.7.mine), channel_id=1, source_target_pairs={{0,1},{1,0},{2,3},{3,2},{4,5},{5,4},{6,7},{7,6},{8,9},{9,8},{10,11... | collective-permute-start | bytes 6291464 | tf_op jit(solution)/shard_map/ppermute | solution.py:81
  264.2 1.3 copy-start.1
  272.7 6.8 %copy-start.9 = (bf16[16,24,512]{2,1,0:T(8,128)(2,1)S(1)}, bf16[16,24,512]{2,1,0:T(8,128)(2,1)}, u32[]{:S(2)}) copy-start(bf16[16,24,512]{2,1,0:T(8,128)(2,1)} %copy-done.8) | copy-start | bytes 1179652
  272.7 6.8 %copy-start.12 = (s32[48]{0:T(128)S(1)}, s32[48]{0:T(128)}, u32[]{:S(2)}) copy-start(s32[48]{0:T(128)} %copy-done.11) | copy-start | bytes 580
  272.7 7.1 %copy-start.7 = (bf16[16,24,512]{2,1,0:T(8,128)(2,1)S(1)}, bf16[16,24,512]{2,1,0:T(8,128)(2,1)}, u32[]{:S(2)}) copy-start(bf16[16,24,512]{2,1,0:T(8,128)(2,1)} %copy-done.6) | copy-start | bytes 1179652
  272.7 35.9 %collective-permute-start.10 = (bf16[4,256,1024]{2,1,0:T(8,128)(2,1)}, bf16[4,256,1024]{2,1,0:T(8,128)(2,1)}, u32[]{:S(2)}, u32[]{:S(2)}) collective-permute-start(bf16[4,256,1024]{2,1,0:T(8,128)(2,1)} %shard_map.103), channel_id=1, source_target_pairs={{0,1},{1,0},{2,3},{3,2},{4,5},{5,4},{6,7},{7,6},{8,9},{9,8},{10,11... | collective-permute-start | bytes 6291464 | tf_op jit(solution)/shard_map/ppermute | solution.py:81
  274.7 31.3 %all-to-all-start.3 = ((bf16[16,48,512]{2,1,0:T(8,128)(2,1)}), bf16[16,48,512]{2,1,0:T(8,128)(2,1)S(1)}, u32[]{:S(2)}, u32[]{:S(2)}) async-start(bf16[16,48,512]{2,1,0:T(8,128)(2,1)} %bitcast.36), calls=%async_computation.3 | async-start | bytes 1572864 | tf_op jit(solution)/shard_map/all_to_all | solution.py:500
  281.9 19.2 %collective-permute-start.11 = (f32[16,1024]{1,0:T(8,128)S(1)}, f32[16,1024]{1,0:T(8,128)S(1)}, u32[]{:S(2)}, u32[]{:S(2)}) collective-permute-start(f32[16,1024]{1,0:T(8,128)S(1)} %get-tuple-element.20), channel_id=1, source_target_pairs={{0,15},{1,0},{2,1},{3,2},{4,3},{5,4},{6,5},{7,6},{8,7},{9,8},{10,9... | collective-permute-start | bytes 196616 | tf_op jit(solution)/shard_map/ppermute | solution.py:21
  295.1 6.9 %collective-permute-start.12 = (f32[16,1024]{1,0:T(8,128)S(1)}, f32[16,1024]{1,0:T(8,128)S(1)}, u32[]{:S(2)}, u32[]{:S(2)}) collective-permute-start(f32[16,1024]{1,0:T(8,128)S(1)} %get-tuple-element.20), channel_id=1, source_target_pairs={{0,14},{1,15},{2,0},{3,1},{4,2},{5,3},{6,4},{7,5},{8,6},{9,7},{10,... | collective-permute-start | bytes 196616 | tf_op jit(solution)/shard_map/ppermute | solution.py:21
  299.5 4.0 %collective-permute-start.13 = (f32[16,1024]{1,0:T(8,128)S(1)}, f32[16,1024]{1,0:T(8,128)S(1)}, u32[]{:S(2)}, u32[]{:S(2)}) collective-permute-start(f32[16,1024]{1,0:T(8,128)S(1)} %get-tuple-element.20), channel_id=1, source_target_pairs={{0,13},{1,14},{2,15},{3,0},{4,1},{5,2},{6,3},{7,4},{8,5},{9,6},{10... | collective-permute-start | bytes 196616 | tf_op jit(solution)/shard_map/ppermute | solution.py:21
  301.1 4.1 %collective-permute-start.14 = (f32[16,1024]{1,0:T(8,128)S(1)}, f32[16,1024]{1,0:T(8,128)S(1)}, u32[]{:S(2)}, u32[]{:S(2)}) collective-permute-start(f32[16,1024]{1,0:T(8,128)S(1)} %get-tuple-element.20), channel_id=1, source_target_pairs={{0,12},{1,13},{2,14},{3,15},{4,0},{5,1},{6,2},{7,3},{8,4},{9,5},{1... | collective-permute-start | bytes 196616 | tf_op jit(solution)/shard_map/ppermute | solution.py:21
Sparse Core Ops, SparseCore 0:
  30.0 80.2 all-gather.2

commit v15 on v14

--- a/solution.py
+++ b/solution.py
@@ -74,8 +74,12 @@
     return lax.all_gather(mine, "blk", axis_index_groups=lines)
 
 
+CHUNKS = 2
+
+
 def weight_quarters(column):
     count = lax.axis_size("blk")
+    size = column.shape[1] // CHUNKS
 
     def over(piece, bit):
         return lax.ppermute(piece, "blk", [(i, i ^ bit) for i in range(count)])
@@ -83,33 +87,26 @@
     def groups(piece):
         return lax.ppermute(piece, "groups", [(0, 1), (1, 0)])
 
-    own = [column, groups(column)]
-    across = over(column, 2)
-    across = [across, groups(across)]
-
-    def quarter(number, late=None):
-        mine, theirs = across if number >= 2 else own
-        if number % 2 == 0:
-            return [mine, theirs]
-        if late is not None:
-            theirs = after(theirs, late)
-        return [over(mine, 1), over(theirs, 1)]
-
-    return quarter
-
-
-def quarter_kernel(where, cot, grad, down, mine, theirs, *rest):
+    mine = [column[:, k * size : (k + 1) * size] for k in range(CHUNKS)]
+    quarters = []
+    for side in (mine, [over(piece, 2) for piece in mine]):
+        both = side + [groups(piece) for piece in side]
+        quarters += [both, [over(piece, 1) for piece in both]]
+    return quarters
+
+
+def quarter_kernel(where, cot, grad, down, *rest):
+    pieces = rest[: 2 * CHUNKS]
     out, token = rest[-2:]
     token[...] = jnp.zeros_like(token)
-    half = mine.shape[1]
     lora = adapter_scale * dot(grad[...], down[...], ((1,), (0,)))
     lora = lora.astype(jnp.bfloat16).astype(jnp.float32)
 
     def product(group):
-        for k, piece in enumerate((mine, theirs) if group == 0 else (theirs, mine)):
-            part = slice(k * half, (k + 1) * half)
-            frozen = dot(cot[...], piece[0], ((1,), (1,)))
-            out[:, part] = (frozen + lora[:, part]).astype(jnp.bfloat16)
+        order = pieces[group * CHUNKS :] + pieces[: group * CHUNKS]
+        weight = jnp.concatenate([piece[0] for piece in order], axis=0)
+        frozen = dot(cot[...], weight, ((1,), (1,)))
+        out[...] = (frozen + lora).astype(jnp.bfloat16)
 
     for group in range(2):
         pl.when(where[1] == group)(functools.partial(product, group))
@@ -159,11 +156,12 @@
 
 def together(pieces, firsts, group):
     shards, part, depth = pieces[0][0].shape
-    weight = jnp.zeros((shards, 4, 2, part, depth), jnp.bfloat16)
+    weight = jnp.zeros((shards, 4, 2, CHUNKS, part, depth), jnp.bfloat16)
     for quarter, first in zip(pieces, firsts):
         for k, piece in enumerate(quarter):
-            place = (0, first, group if k == 0 else 1 - group, 0, 0)
-            weight = lax.dynamic_update_slice(weight, piece[:, None, None], place)
+            half = group if k < CHUNKS else 1 - group
+            place = (0, first, half, k % CHUNKS, 0, 0)
+            weight = lax.dynamic_update_slice(weight, piece[:, None, None, None], place)
     return weight.reshape(-1, depth)
 
 
@@ -396,7 +394,7 @@
     cap = resident_rows // devices
     start_ids = tenant_first_row // BLOCK
 
-    column = weight_column(frozen_value_weight)
+    quarters = weight_quarters(weight_column(frozen_value_weight))
 
     first_block = device * resident
     block_numbers = first_block + jnp.arange(resident, dtype=jnp.int32)
@@ -428,6 +426,8 @@
     up_blocks = of_blocks(adapter_up_maps, carried[:, width:])
 
     sent_rows = pack_rows(token_layout_row, cotangent, devices, cap, features)
+    own, _, across, _ = quarters
+    sent_rows = after(sent_rows, carried, own[CHUNKS], across[0])
     got_rows = lax.all_to_all(sent_rows, "blk", split_axis=0, concat_axis=0)
     recv_cot = [
         got_rows[:, k * cap : (k + 1) * cap].reshape(resident_rows, features)
@@ -439,7 +439,8 @@
     rows_all, place_all = from_digits(digits)
 
     flat_maps = adapter_down_maps.reshape(share, width)
-    received = after(pack_features(activations, flat_maps, devices), got_rows)
+    received = pack_features(activations, flat_maps, devices)
+    received = after(received, got_rows, own[-1], across[CHUNKS - 1])
     received = lax.all_to_all(received, "blk", split_axis=0, concat_axis=0)
 
     spots = device * cap + jnp.arange(cap, dtype=jnp.int32)
@@ -470,15 +471,18 @@
     grad_wide = jnp.where(in_rows, jnp.concatenate([grad_rows] * resident, axis=1), 0)
     group = lax.axis_index("groups")
     firsts = [(device % 4) ^ k for k in range(4)]
-    pieces = weight_quarters(column)
-    tiled = column.shape[1] % LANES == 0
-    if tiled:
+    if own[0].shape[1] % LANES == 0:
         out = None
-        for quarter in (0, 1):
+        for quarter, first in zip(quarters, firsts):
             out, token = write_quarter(
-                pieces(quarter), firsts[quarter], group, cot_rows, grad_wide, down_blocks, out
+                quarter, first, group, cot_rows, grad_wide, down_blocks, out
             )
         place_all = after(place_all, token)
+    else:
+        weight = together(quarters, firsts, group)
+        lora = adapter_scale * dot(grad_wide, down_blocks, ((1,), (0,)))
+        out = dot(cot_rows, weight, ((1,), (1,)))
+        out = (out + lora.astype(jnp.bfloat16).astype(jnp.float32)).astype(jnp.bfloat16)
 
     starts = start_ids[:, None]
     hidden_call, down_call = feature_calls(
@@ -519,17 +523,6 @@
         up_grads.append(adapter_scale * total)
     up_map_gradient = jnp.stack(up_grads)
 
-    if tiled:
-        late = after(grad_wide, down_f)
-        for quarter in (2, 3):
-            out, _ = write_quarter(
-                pieces(quarter, shares), firsts[quarter], group, cot_rows, late, down_blocks, out
-            )
-    else:
-        weight = together([pieces(k, shares) for k in range(4)], firsts, group)
-        lora = adapter_scale * dot(grad_wide, down_blocks, ((1,), (0,)))
-        out = dot(cot_rows, weight, ((1,), (1,)))
-        out = (out + lora.astype(jnp.bfloat16).astype(jnp.float32)).astype(jnp.bfloat16)
     return (out, down_map_gradient, up_map_gradient)
 
 

time: 324 us -> 326 us (level)
  starting transfers between devices: 103 us -> 49.9 us
  waiting for transfers between devices: 98.1 us -> 127 us
  blocking collectives: 0 us -> 23.2 us
    ppermute x2 -> x4, waiting for transfers between devices: 4.86 us -> 56.7 us  [groups(): return lax.ppermute(piece, 'groups', [(0, 1), (1, 0)])]
    all_to_all x1, starting transfers between devices: 30.7 us -> 5.63 us  [local(): received = lax.all_to_all(received, 'blk', split_axis=0, concat_axis=0)]
    all_to_all x0 -> x1, blocking collectives: none -> 23.2 us  [local(): small = lax.all_to_all(small, 'blk', split_axis=0, concat_axis=0)]
    ppermute x5 -> x10, starting transfers between devices: 41.3 us -> 18.5 us  [over(): return lax.ppermute(piece, 'blk', [(i, i ^ bit) for i in range(count)])]
    all_to_all x1 -> x0, waiting for transfers between devices: 14.5 us -> none  [local(): small = lax.all_to_all(small, 'blk', split_axis=0, concat_axis=0)]
    ppermute x5 -> x10, waiting for transfers between devices: 44.4 us -> 32.8 us  [over(): return lax.ppermute(piece, 'blk', [(i, i ^ bit) for i in range(count)])]
    all_gather x1, waiting for transfers between devices: 25.7 us -> 37.1 us  [weight_column(): return lax.all_gather(mine, 'blk', axis_index_groups=lines)]
    all_to_all x1 -> x0, starting transfers between devices: 5.53 us -> none  [local(): small = lax.all_to_all(small, 'blk', split_axis=0, concat_axis=0)]
  transfers between devices with their start and end apart: 20 -> 26, of which waited for: 7 -> 6; matrix products, arithmetic and copies ran while one was open for 9% -> 7% of each run, Pallas kernels for 13% -> 11%
where the time goes in v15:
time: 326 us; the launch traced here: 324 us
  waiting for transfers between devices  127 us (39%)
  Pallas kernels  50.6 us (16%)
  starting transfers between devices  49.9 us (15%)
  between operations  39.8 us (12%)
  blocking collectives  23.2 us (7%)
  local copies, waits for them, and re-layouts  19.8 us (6%)
  other arithmetic  11.5 us (4%)
    ppermute x4, waiting for transfers between devices, groups(): return lax.ppermute(piece, 'groups', [(0, 1), (1, 0)])  56.7 us
    all_gather x1, waiting for transfers between devices, weight_column(): return lax.all_gather(mine, 'blk', axis_index_groups=lines)  37.1 us
    ppermute x10, waiting for transfers between devices, over(): return lax.ppermute(piece, 'blk', [(i, i ^ bit) for i in range(count)])  32.8 us
    pallas_call x4, Pallas kernels, write_quarter(): pl.pallas_call(quarter_kernel, grid_spec=pltpu.PrefetchScalarGridSpec(num...  28.5 us
    all_to_all x1, blocking collectives, local(): small = lax.all_to_all(small, 'blk', split_axis=0, concat_axis=0)  23.2 us
    ppermute x10, starting transfers between devices, over(): return lax.ppermute(piece, 'blk', [(i, i ^ bit) for i in range(count)])  18.5 us
    ppermute x8, starting transfers between devices, moved(): lax.ppermute(value, 'blk', [(i, (i + steps) % count) for i in range(count)])  12.9 us
    pallas_call x1, Pallas kernels, local(): shares = hidden_call(received, received, rows_all, place_all, starts)  8.25 us
  transfers between devices with their start and end apart: 26, of which 6 were waited for; matrix products, arithmetic and copies ran while one was open for 7% of the time, Pallas kernels for 11%

profile of v15, /device:TPU:1, one launch (start us, length us, event | category | flops | bytes accessed | tf_op | source)
XLA Modules:
  0.0 323.7 jit_solution(13995721280645225070)
XLA Ops:
  7.3 1.1 copy-done
  8.4 0.8 constant_dynamic-slice_fusion
  9.3 0.8 fusion.24
  13.7 1.0 dynamic-slice_bitcast_fusion
  14.7 2.2 collective-permute-start
  16.9 2.1 collective-permute-start.1
  19.0 1.2 collective-permute-start.2
  20.2 0.9 collective-permute-start.3
  24.4 2.6 shard_map.94.refs_0_
  26.9 37.1 %all-gather.3.cloned.1.call-done = bf16[1024,1024]{1,0:T(8,128)(2,1)} async-done(((bf16[256,1024]{1,0:T(8,128)(2,1)}), bf16[1024,1024]{1,0:T(8,128)(2,1)}) %all-gather.3.cloned.1.call-update) | async-done | bytes 2097168 | tf_op jit(solution)/shard_map/all_gather | solution.py:74
  64.1 3.0 fusion.36
  67.1 13.7 %collective-permute-start.5 = (bf16[4,128,1024]{2,1,0:T(8,128)(2,1)}, bf16[4,128,1024]{2,1,0:T(8,128)(2,1)}, u32[]{:S(2)}, u32[]{:S(2)}) collective-permute-start(bf16[4,128,1024]{2,1,0:T(8,128)(2,1)} %get-tuple-element.32.rest_0_), channel_id=1, source_target_pairs={{0,2},{1,3},{2,0},{3,1},{4,6},{5,7},{6,4},{7,5},{8,10},{9,11},{10,... | collective-permute-start | bytes 3145736 | tf_op jit(solution)/shard_map/ppermute | solution.py:85
  80.8 1.2 collective-permute-start.4
  82.0 0.8 select_select_fusion.refs_1_
  82.8 21.4 %collective-permute-done.5.refs_3_.rest_0_ = bf16[4,128,1024]{2,1,0:T(8,128)(2,1)} collective-permute-done((bf16[4,128,1024]{2,1,0:T(8,128)(2,1)}, bf16[4,128,1024]{2,1,0:T(8,128)(2,1)}, u32[]{:S(2)}, u32[]{:S(2)}) %collective-permute-start.5) | collective-permute-done | bytes 1048608 | tf_op jit(solution)/shard_map/ppermute | solution.py:85
  104.2 0.8 collective-permute-done.4.refs_2_.rest_2_
  105.0 5.1 %all-to-all-start = ((bf16[16,64,512]{2,1,0:T(8,128)(2,1)}), bf16[16,64,512]{2,1,0:T(8,128)(2,1)S(1)}, u32[]{:S(2)}, u32[]{:S(2)}) async-start(bf16[16,64,512]{2,1,0:T(8,128)(2,1)} %shard_map.95), calls=%async_computation | async-start | bytes 2097152 | tf_op jit(solution)/shard_map/all_to_all | solution.py:431
  110.1 1.2 collective-permute-start.16
  111.3 1.4 collective-permute-start.7
  112.7 4.6 %shard_map.100.refs_0_ = bf16[16,240,512]{2,1,0:T(8,128)(2,1)} custom-call(bf16[192,8192]{1,0:T(8,128)(2,1)} %act.1, bf16[48,8192]{1,0:T(8,128)(2,1)} %bitcast.104), custom_call_target="tpu_custom_call" | custom-call | bytes 7864320 | tf_op jit(solution)/shard_map/pallas_call | solution.py:242
  119.2 15.7 %collective-permute-done.16.rest_3_.refs_2_ = bf16[4,128,1024]{2,1,0:T(8,128)(2,1)} collective-permute-done((bf16[4,128,1024]{2,1,0:T(8,128)(2,1)}, bf16[4,128,1024]{2,1,0:T(8,128)(2,1)}, u32[]{:S(2)}, u32[]{:S(2)}) %collective-permute-start.16) | collective-permute-done | bytes 1048608 | tf_op jit(solution)/shard_map/ppermute | solution.py:88
  134.9 11.4 %collective-permute-done.7.rest_1_.refs_3_ = bf16[4,128,1024]{2,1,0:T(8,128)(2,1)} collective-permute-done((bf16[4,128,1024]{2,1,0:T(8,128)(2,1)}, bf16[4,128,1024]{2,1,0:T(8,128)(2,1)}, u32[]{:S(2)}, u32[]{:S(2)}) %collective-permute-start.7) | collective-permute-done | bytes 1048608 | tf_op jit(solution)/shard_map/ppermute | solution.py:85
  146.3 1.0 copy-done.1
  147.3 5.6 %all-to-all-start.1 = ((bf16[16,240,512]{2,1,0:T(8,128)(2,1)}), bf16[16,240,512]{2,1,0:T(8,128)(2,1)}, u32[]{:S(2)}, u32[]{:S(2)}) async-start(bf16[16,240,512]{2,1,0:T(8,128)(2,1)} %shard_map.101), calls=%async_computation.1 | async-start | bytes 7864320 | tf_op jit(solution)/shard_map/all_to_all | solution.py:444
  162.7 0.9 pad_maximum_fusion.1.down
  164.3 1.2 collective-permute-start.11
  167.5 1.0 collective-permute-start.17
  171.2 40.2 %collective-permute-done.9.rest_2_ = bf16[4,128,1024]{2,1,0:T(8,128)(2,1)} collective-permute-done((bf16[4,128,1024]{2,1,0:T(8,128)(2,1)}, bf16[4,128,1024]{2,1,0:T(8,128)(2,1)}, u32[]{:S(2)}, u32[]{:S(2)}) %collective-permute-start.9) | collective-permute-done | bytes 1048608 | tf_op jit(solution)/shard_map/ppermute | solution.py:88
  211.4 1.2 collective-permute-start.10
  213.1 1.0 pad_maximum_fusion.cot
  214.1 0.8 compare_select_fusion.1.grad
  214.9 7.1 %shard_map.96 = (bf16[384,8192]{1,0:T(8,128)(2,1)}, f32[8,128]{1,0:T(8,128)}) custom-call(s32[2]{0:T(128)} %pad_add_fusion.3.where, bf16[384,1024]{1,0:T(8,128)(2,1)} %pad_maximum_fusion.cot, bf16[384,48]{1,0:T(8,128)(2,1)} %compare_select_fusion.1.grad, bf16[48,8192]{1,0:T(8,128)(2,1)} %pad_maximum_fusion.1.down, ...), custom_call_target="tpu_custom_call" | custom-call | flops 1610612736 | bytes 5767168 | tf_op jit(solution)/shard_map/pallas_call | solution.py:132
  222.0 1.0 copy-done.7
  223.0 7.1 %shard_map.97 = (bf16[384,8192]{1,0:T(8,128)(2,1)}, f32[8,128]{1,0:T(8,128)}) custom-call(s32[2]{0:T(128)} %pad_add_fusion.2.where, bf16[384,1024]{1,0:T(8,128)(2,1)} %pad_maximum_fusion.cot, bf16[384,48]{1,0:T(8,128)(2,1)} %compare_select_fusion.1.grad, bf16[48,8192]{1,0:T(8,128)(2,1)} %pad_maximum_fusion.1.down, ...), custom_call_target="tpu_custom_call", output_to_operand_aliasing={{0}: (8, {})} | custom-call | flops 1610612736 | bytes 5767168 | tf_op jit(solution)/shard_map/pallas_call | solution.py:132
  230.1 7.1 %shard_map.98 = (bf16[384,8192]{1,0:T(8,128)(2,1)}, f32[8,128]{1,0:T(8,128)}) custom-call(s32[2]{0:T(128)} %pad_add_fusion.1.where, bf16[384,1024]{1,0:T(8,128)(2,1)} %pad_maximum_fusion.cot, bf16[384,48]{1,0:T(8,128)(2,1)} %compare_select_fusion.1.grad, bf16[48,8192]{1,0:T(8,128)(2,1)} %pad_maximum_fusion.1.down, ...), custom_call_target="tpu_custom_call", output_to_operand_aliasing={{0}: (8, {})} | custom-call | flops 1610612736 | bytes 5767168 | tf_op jit(solution)/shard_map/pallas_call | solution.py:132
  237.3 0.9 copy-done.5
  239.3 7.1 %shard_map.99 = (bf16[384,8192]{1,0:T(8,128)(2,1)}, f32[8,128]{1,0:T(8,128)}) custom-call(s32[2]{0:T(128)} %pad_add_fusion.where, bf16[384,1024]{1,0:T(8,128)(2,1)} %pad_maximum_fusion.cot, bf16[384,48]{1,0:T(8,128)(2,1)} %compare_select_fusion.1.grad, bf16[48,8192]{1,0:T(8,128)(2,1)} %pad_maximum_fusion.1.down, ...), custom_call_target="tpu_custom_call", output_to_operand_aliasing={{0}: (8, {})} | custom-call | flops 1610612736 | bytes 5767168 | tf_op jit(solution)/shard_map/pallas_call | solution.py:132
  246.4 8.3 %shard_map.103 = bf16[2,256,384]{2,1,0:T(8,128)(2,1)} custom-call(bf16[16,240,512]{2,1,0:T(8,128)(2,1)} %all-to-all-done.1.act.maps, bf16[16,240,512]{2,1,0:T(8,128)(2,1)} %all-to-all-done.1.act.maps, s32[1,3072]{1,0:T(1,128)} %reshape.356.rows, s32[1,3072]{1,0:T(1,128)} %shard_map.102.spots, s32[32,1]{1,0:T(8,128)} %copy.57.starts), custom_call_target="tpu_custom_call" | custom-call | flops 2415919104 | bytes 3145728 | tf_op jit(solution)/shard_map/pallas_call | solution.py:491
  254.7 1.2 copy.58
  255.9 23.2 %all_to_all.28 = bf16[16,24,768]{2,1,0:T(8,128)(2,1)S(1)} all-to-all(bf16[16,24,768]{2,1,0:T(8,128)(2,1)S(1)} %pad_maximum_fusion.2), channel_id=1, replica_groups=mesh['groups'=2,'blk'=16] {'blk'}, dimensions={0} | all-to-all | bytes 1179648 | tf_op jit(solution)/shard_map/all_to_all | solution.py:496
  279.1 0.8 copy.59
  279.9 6.7 %shard_map.104 = bf16[768,512]{1,0:T(8,128)(2,1)} custom-call(bf16[16,240,512]{2,1,0:T(8,128)(2,1)} %all-to-all-done.1.act.maps, bf16[256,384]{1,0:T(8,128)(2,1)} %bitcast.119, s32[1,3072]{1,0:T(1,128)} %reshape.356.rows, s32[1,3072]{1,0:T(1,128)} %shard_map.102.spots, s32[32,1]{1,0:T(8,128)} %copy.57.starts), custom_call_target="tpu_custom_call" | custom-call | flops 2415919104 | bytes 3145728 | tf_op jit(solution)/shard_map/pallas_call | solution.py:503
  286.6 3.8 %all-to-all-start.3 = ((bf16[16,48,512]{2,1,0:T(8,128)(2,1)}), bf16[16,48,512]{2,1,0:T(8,128)(2,1)S(1)}, u32[]{:S(2)}, u32[]{:S(2)}) async-start(bf16[16,48,512]{2,1,0:T(8,128)(2,1)} %bitcast.113), calls=%async_computation.3 | async-start | bytes 1572864 | tf_op jit(solution)/shard_map/all_to_all | solution.py:504
  291.6 1.9 select_add_fusion.1
  293.9 4.3 %collective-permute-start.19 = (f32[16,1024]{1,0:T(8,128)S(1)}, f32[16,1024]{1,0:T(8,128)S(1)}, u32[]{:S(2)}, u32[]{:S(2)}) collective-permute-start(f32[16,1024]{1,0:T(8,128)S(1)} %get-tuple-element.20), channel_id=1, source_target_pairs={{0,14},{1,15},{2,0},{3,1},{4,2},{5,3},{6,4},{7,5},{8,6},{9,7},{10,... | collective-permute-start | bytes 196616 | tf_op jit(solution)/shard_map/ppermute | solution.py:21
  298.2 1.6 collective-permute-start.20
  314.5 0.9 copy.61
  315.4 1.4 reshape.355
  (113 shorter events, 16.4 us)
Async XLA Ops:
  7.2 1.2 copy-start
  7.2 2.1 copy-start.12
  7.2 6.5 %copy-start.10 = (bf16[3,16,1024]{2,1,0:T(8,128)(2,1)S(1)}, bf16[3,16,1024]{2,1,0:T(8,128)(2,1)}, u32[]{:S(2)}) copy-start(bf16[3,16,1024]{2,1,0:T(8,128)(2,1)} %param.13) | copy-start | bytes 294916
  7.2 16.6 %copy-start.11 = (s32[192]{0:T(256)S(1)}, s32[192]{0:T(256)}, u32[]{:S(2)}) copy-start(s32[192]{0:T(256)} %param.9) | copy-start | bytes 2308
  7.2 56.9 %all-gather.3.cloned.1.call-start = ((), (), s32[]{:S(2)}) async-start(), calls=%async_computation.4 | async-start | bytes 2621440 | tf_op jit(solution)/shard_map/all_gather | solution.py:74
  14.7 66.1 %collective-permute-start = (bf16[16,9216]{1,0:T(8,128)(2,1)S(1)}, bf16[16,9216]{1,0:T(8,128)(2,1)S(1)}, u32[]{:S(2)}, u32[]{:S(2)}) collective-permute-start(bf16[16,9216]{1,0:T(8,128)(2,1)S(1)} %pad_maximum_fusion.3), channel_id=1, source_target_pairs={{0,4},{1,5},{2,6},{3,7},{4,8},{5,9},{6,10},{7,11},{8,12},{9,13},{1... | collective-permute-start | bytes 884744 | tf_op jit(solution)/shard_map/ppermute | solution.py:21
  16.9 65.1 %collective-permute-start.1 = (bf16[16,9216]{1,0:T(8,128)(2,1)S(1)}, bf16[16,9216]{1,0:T(8,128)(2,1)S(1)}, u32[]{:S(2)}, u32[]{:S(2)}) collective-permute-start(bf16[16,9216]{1,0:T(8,128)(2,1)S(1)} %pad_maximum_fusion.3), channel_id=1, source_target_pairs={{0,3},{1,4},{2,5},{3,6},{4,7},{5,8},{6,9},{7,10},{8,11},{9,12},{10... | collective-permute-start | bytes 884744 | tf_op jit(solution)/shard_map/ppermute | solution.py:21
  19.0 63.0 %collective-permute-start.2 = (bf16[16,9216]{1,0:T(8,128)(2,1)S(1)}, bf16[16,9216]{1,0:T(8,128)(2,1)S(1)}, u32[]{:S(2)}, u32[]{:S(2)}) collective-permute-start(bf16[16,9216]{1,0:T(8,128)(2,1)S(1)} %pad_maximum_fusion.3), channel_id=1, source_target_pairs={{0,2},{1,3},{2,4},{3,5},{4,6},{5,7},{6,8},{7,9},{8,10},{9,11},{10,... | collective-permute-start | bytes 884744 | tf_op jit(solution)/shard_map/ppermute | solution.py:21
  20.2 61.8 %collective-permute-start.3 = (bf16[16,9216]{1,0:T(8,128)(2,1)S(1)}, bf16[16,9216]{1,0:T(8,128)(2,1)S(1)}, u32[]{:S(2)}, u32[]{:S(2)}) collective-permute-start(bf16[16,9216]{1,0:T(8,128)(2,1)S(1)} %pad_maximum_fusion.3), channel_id=1, source_target_pairs={{0,1},{1,2},{2,3},{3,4},{4,5},{5,6},{6,7},{7,8},{8,9},{9,10},{10,1... | collective-permute-start | bytes 884744 | tf_op jit(solution)/shard_map/ppermute | solution.py:21
  67.1 37.1 %collective-permute-start.5 = (bf16[4,128,1024]{2,1,0:T(8,128)(2,1)}, bf16[4,128,1024]{2,1,0:T(8,128)(2,1)}, u32[]{:S(2)}, u32[]{:S(2)}) collective-permute-start(bf16[4,128,1024]{2,1,0:T(8,128)(2,1)} %get-tuple-element.32.rest_0_), channel_id=1, source_target_pairs={{0,2},{1,3},{2,0},{3,1},{4,6},{5,7},{6,4},{7,5},{8,10},{9,11},{10,... | collective-permute-start | bytes 3145736 | tf_op jit(solution)/shard_map/ppermute | solution.py:85
  80.8 24.3 %collective-permute-start.4 = (bf16[4,128,1024]{2,1,0:T(8,128)(2,1)}, bf16[4,128,1024]{2,1,0:T(8,128)(2,1)}, u32[]{:S(2)}, u32[]{:S(2)}) collective-permute-start(bf16[4,128,1024]{2,1,0:T(8,128)(2,1)} %get-tuple-element.32.rest_0_), channel_id=1, source_target_pairs={{0,16},{16,0},{1,17},{17,1},{2,18},{18,2},{3,19},{19,3},{4,20},{20... | collective-permute-start | bytes 3145736 | tf_op jit(solution)/shard_map/ppermute | solution.py:88
  105.0 41.2 %all-to-all-start = ((bf16[16,64,512]{2,1,0:T(8,128)(2,1)}), bf16[16,64,512]{2,1,0:T(8,128)(2,1)S(1)}, u32[]{:S(2)}, u32[]{:S(2)}) async-start(bf16[16,64,512]{2,1,0:T(8,128)(2,1)} %shard_map.95), calls=%async_computation | async-start | bytes 2097152 | tf_op jit(solution)/shard_map/all_to_all | solution.py:431
  110.1 24.8 %collective-permute-start.16 = (bf16[4,128,1024]{2,1,0:T(8,128)(2,1)}, bf16[4,128,1024]{2,1,0:T(8,128)(2,1)}, u32[]{:S(2)}, u32[]{:S(2)}) collective-permute-start(bf16[4,128,1024]{2,1,0:T(8,128)(2,1)} %get-tuple-element.31.rest_1_), channel_id=1, source_target_pairs={{0,16},{16,0},{1,17},{17,1},{2,18},{18,2},{3,19},{19,3},{4,20},{20... | collective-permute-start | bytes 3145736 | tf_op jit(solution)/shard_map/ppermute | solution.py:88
  111.3 34.9 %collective-permute-start.7 = (bf16[4,128,1024]{2,1,0:T(8,128)(2,1)}, bf16[4,128,1024]{2,1,0:T(8,128)(2,1)}, u32[]{:S(2)}, u32[]{:S(2)}) collective-permute-start(bf16[4,128,1024]{2,1,0:T(8,128)(2,1)} %get-tuple-element.31.rest_1_), channel_id=1, source_target_pairs={{0,2},{1,3},{2,0},{3,1},{4,6},{5,7},{6,4},{7,5},{8,10},{9,11},{10,... | collective-permute-start | bytes 3145736 | tf_op jit(solution)/shard_map/ppermute | solution.py:85
  146.3 1.0 copy-start.1
  147.3 15.3 %copy-start.4 = (bf16[16,9216]{1,0:T(8,128)(2,1)S(1)}, bf16[16,9216]{1,0:T(8,128)(2,1)}, u32[]{:S(2)}) copy-start(bf16[16,9216]{1,0:T(8,128)(2,1)} %select_select_fusion.refs_1_) | copy-start | bytes 884740
  147.3 15.3 %copy-start.3 = (bf16[3,16,8192]{2,1,0:T(8,128)(2,1)S(1)}, bf16[3,16,8192]{2,1,0:T(8,128)(2,1)}, u32[]{:S(2)}) copy-start(bf16[3,16,8192]{2,1,0:T(8,128)(2,1)} %param.12) | copy-start | bytes 2359300
  147.3 99.2 %all-to-all-start.1 = ((bf16[16,240,512]{2,1,0:T(8,128)(2,1)}), bf16[16,240,512]{2,1,0:T(8,128)(2,1)}, u32[]{:S(2)}, u32[]{:S(2)}) async-start(bf16[16,240,512]{2,1,0:T(8,128)(2,1)} %shard_map.101), calls=%async_computation.1 | async-start | bytes 7864320 | tf_op jit(solution)/shard_map/all_to_all | solution.py:444
  162.6 3.2 copy-start.2
  163.6 3.9 %collective-permute-start.13 = (bf16[4,128,1024]{2,1,0:T(8,128)(2,1)}, bf16[4,128,1024]{2,1,0:T(8,128)(2,1)}, u32[]{:S(2)}, u32[]{:S(2)}) collective-permute-start(bf16[4,128,1024]{2,1,0:T(8,128)(2,1)} %get-tuple-element.32.rest_0_), channel_id=1, source_target_pairs={{0,1},{1,0},{2,3},{3,2},{4,5},{5,4},{6,7},{7,6},{8,9},{9,8},{10,11... | collective-permute-start | bytes 3145736 | tf_op jit(solution)/shard_map/ppermute | solution.py:85
  163.7 6.9 %collective-permute-start.14 = (bf16[4,128,1024]{2,1,0:T(8,128)(2,1)}, bf16[4,128,1024]{2,1,0:T(8,128)(2,1)}, u32[]{:S(2)}, u32[]{:S(2)}) collective-permute-start(bf16[4,128,1024]{2,1,0:T(8,128)(2,1)} %get-tuple-element.31.rest_1_), channel_id=1, source_target_pairs={{0,1},{1,0},{2,3},{3,2},{4,5},{5,4},{6,7},{7,6},{8,9},{9,8},{10,11... | collective-permute-start | bytes 3145736 | tf_op jit(solution)/shard_map/ppermute | solution.py:85
  164.1 6.6 %collective-permute-start.15 = (bf16[4,128,1024]{2,1,0:T(8,128)(2,1)}, bf16[4,128,1024]{2,1,0:T(8,128)(2,1)}, u32[]{:S(2)}, u32[]{:S(2)}) collective-permute-start(bf16[4,128,1024]{2,1,0:T(8,128)(2,1)} %collective-permute-done.4.refs_2_.rest_2_), channel_id=1, source_target_pairs={{0,1},{1,0},{2,3},{3,2},{4,5},{5,4},{6,7},{7,6},{8,9},{9,8},{10,11... | collective-permute-start | bytes 3145736 | tf_op jit(solution)/shard_map/ppermute | solution.py:85
  164.3 48.4 %collective-permute-start.11 = (bf16[4,128,1024]{2,1,0:T(8,128)(2,1)}, bf16[4,128,1024]{2,1,0:T(8,128)(2,1)}, u32[]{:S(2)}, u32[]{:S(2)}) collective-permute-start(bf16[4,128,1024]{2,1,0:T(8,128)(2,1)} %collective-permute-done.7.rest_1_.refs_3_), channel_id=1, source_target_pairs={{0,16},{16,0},{1,17},{17,1},{2,18},{18,2},{3,19},{19,3},{4,20},{20... | collective-permute-start | bytes 3145736 | tf_op jit(solution)/shard_map/ppermute | solution.py:88
  165.5 45.9 %collective-permute-start.9 = (bf16[4,128,1024]{2,1,0:T(8,128)(2,1)}, bf16[4,128,1024]{2,1,0:T(8,128)(2,1)}, u32[]{:S(2)}, u32[]{:S(2)}) collective-permute-start(bf16[4,128,1024]{2,1,0:T(8,128)(2,1)} %collective-permute-done.5.refs_3_.rest_0_), channel_id=1, source_target_pairs={{0,16},{16,0},{1,17},{17,1},{2,18},{18,2},{3,19},{19,3},{4,20},{20... | collective-permute-start | bytes 3145736 | tf_op jit(solution)/shard_map/ppermute | solution.py:88
  167.5 54.5 %collective-permute-start.17 = (bf16[4,128,1024]{2,1,0:T(8,128)(2,1)}, bf16[4,128,1024]{2,1,0:T(8,128)(2,1)S(1)}, u32[]{:S(2)}, u32[]{:S(2)}) collective-permute-start(bf16[4,128,1024]{2,1,0:T(8,128)(2,1)} %collective-permute-done.16.rest_3_.refs_2_), channel_id=1, source_target_pairs={{0,1},{1,0},{2,3},{3,2},{4,5},{5,4},{6,7},{7,6},{8,9},{9,8},{10,11... | collective-permute-start | bytes 3145736 | tf_op jit(solution)/shard_map/ppermute | solution.py:85
  170.6 66.6 %collective-permute-start.6 = (bf16[4,128,1024]{2,1,0:T(8,128)(2,1)}, bf16[4,128,1024]{2,1,0:T(8,128)(2,1)S(1)}, u32[]{:S(2)}, u32[]{:S(2)}) collective-permute-start(bf16[4,128,1024]{2,1,0:T(8,128)(2,1)} %collective-permute-done.5.refs_3_.rest_0_), channel_id=1, source_target_pairs={{0,1},{1,0},{2,3},{3,2},{4,5},{5,4},{6,7},{7,6},{8,9},{9,8},{10,11... | collective-permute-start | bytes 3145736 | tf_op jit(solution)/shard_map/ppermute | solution.py:85
  170.7 66.6 %collective-permute-start.8 = (bf16[4,128,1024]{2,1,0:T(8,128)(2,1)}, bf16[4,128,1024]{2,1,0:T(8,128)(2,1)S(1)}, u32[]{:S(2)}, u32[]{:S(2)}) collective-permute-start(bf16[4,128,1024]{2,1,0:T(8,128)(2,1)} %collective-permute-done.7.rest_1_.refs_3_), channel_id=1, source_target_pairs={{0,1},{1,0},{2,3},{3,2},{4,5},{5,4},{6,7},{7,6},{8,9},{9,8},{10,11... | collective-permute-start | bytes 3145736 | tf_op jit(solution)/shard_map/ppermute | solution.py:85
  211.4 25.9 %collective-permute-start.10 = (bf16[4,128,1024]{2,1,0:T(8,128)(2,1)}, bf16[4,128,1024]{2,1,0:T(8,128)(2,1)S(1)}, u32[]{:S(2)}, u32[]{:S(2)}) collective-permute-start(bf16[4,128,1024]{2,1,0:T(8,128)(2,1)} %collective-permute-done.9.rest_2_), channel_id=1, source_target_pairs={{0,1},{1,0},{2,3},{3,2},{4,5},{5,4},{6,7},{7,6},{8,9},{9,8},{10,11... | collective-permute-start | bytes 3145736 | tf_op jit(solution)/shard_map/ppermute | solution.py:85
  212.6 24.7 %collective-permute-start.12 = (bf16[4,128,1024]{2,1,0:T(8,128)(2,1)}, bf16[4,128,1024]{2,1,0:T(8,128)(2,1)S(1)}, u32[]{:S(2)}, u32[]{:S(2)}) collective-permute-start(bf16[4,128,1024]{2,1,0:T(8,128)(2,1)} %collective-permute-done.11.rest_3_), channel_id=1, source_target_pairs={{0,1},{1,0},{2,3},{3,2},{4,5},{5,4},{6,7},{7,6},{8,9},{9,8},{10,11... | collective-permute-start | bytes 3145736 | tf_op jit(solution)/shard_map/ppermute | solution.py:85
  222.0 1.0 copy-start.7
  237.3 1.0 copy-start.5
  237.3 1.4 copy-start.6
  237.3 1.6 copy-start.8
  237.3 1.9 copy-start.9
  286.6 27.7 %all-to-all-start.3 = ((bf16[16,48,512]{2,1,0:T(8,128)(2,1)}), bf16[16,48,512]{2,1,0:T(8,128)(2,1)S(1)}, u32[]{:S(2)}, u32[]{:S(2)}) async-start(bf16[16,48,512]{2,1,0:T(8,128)(2,1)} %bitcast.113), calls=%async_computation.3 | async-start | bytes 1572864 | tf_op jit(solution)/shard_map/all_to_all | solution.py:504
  293.6 19.9 %collective-permute-start.18 = (f32[16,1024]{1,0:T(8,128)S(1)}, f32[16,1024]{1,0:T(8,128)S(1)}, u32[]{:S(2)}, u32[]{:S(2)}) collective-permute-start(f32[16,1024]{1,0:T(8,128)S(1)} %get-tuple-element.20), channel_id=1, source_target_pairs={{0,15},{1,0},{2,1},{3,2},{4,3},{5,4},{6,5},{7,6},{8,7},{9,8},{10,9... | collective-permute-start | bytes 196616 | tf_op jit(solution)/shard_map/ppermute | solution.py:21
  293.9 19.6 %collective-permute-start.19 = (f32[16,1024]{1,0:T(8,128)S(1)}, f32[16,1024]{1,0:T(8,128)S(1)}, u32[]{:S(2)}, u32[]{:S(2)}) collective-permute-start(f32[16,1024]{1,0:T(8,128)S(1)} %get-tuple-element.20), channel_id=1, source_target_pairs={{0,14},{1,15},{2,0},{3,1},{4,2},{5,3},{6,4},{7,5},{8,6},{9,7},{10,... | collective-permute-start | bytes 196616 | tf_op jit(solution)/shard_map/ppermute | solution.py:21
  298.2 15.3 %collective-permute-start.20 = (f32[16,1024]{1,0:T(8,128)S(1)}, f32[16,1024]{1,0:T(8,128)S(1)}, u32[]{:S(2)}, u32[]{:S(2)}) collective-permute-start(f32[16,1024]{1,0:T(8,128)S(1)} %get-tuple-element.20), channel_id=1, source_target_pairs={{0,13},{1,14},{2,15},{3,0},{4,1},{5,2},{6,3},{7,4},{8,5},{9,6},{10... | collective-permute-start | bytes 196616 | tf_op jit(solution)/shard_map/ppermute | solution.py:21
  299.8 13.7 %collective-permute-start.21 = (f32[16,1024]{1,0:T(8,128)S(1)}, f32[16,1024]{1,0:T(8,128)S(1)}, u32[]{:S(2)}, u32[]{:S(2)}) collective-permute-start(f32[16,1024]{1,0:T(8,128)S(1)} %get-tuple-element.20), channel_id=1, source_target_pairs={{0,12},{1,13},{2,14},{3,15},{4,0},{5,1},{6,2},{7,3},{8,4},{9,5},{1... | collective-permute-start | bytes 196616 | tf_op jit(solution)/shard_map/ppermute | solution.py:21
Sparse Core Ops, SparseCore 0:
  10.2 53.8 all-gather.2

commit v16 on v11

--- a/solution.py
+++ b/solution.py
@@ -69,12 +69,23 @@
 CHUNKS = 2
 
 
+def near_lines(count):
+    return count // 4 <= 4
+
+
+def line_order():
+    count = lax.axis_size("blk")
+    shards = jnp.arange(count // 4, dtype=jnp.int32)
+    if near_lines(count):
+        return (lax.axis_index("blk") // 4 - shards) % (count // 4)
+    return shards
+
+
 def weight_pieces(weight):
     count = lax.axis_size("blk")
     half = weight.shape[0] // 2
     size = half // CHUNKS
     first = lax.axis_index("groups") * half
-    lines = [list(range(k, count, 4)) for k in range(4)]
 
     def over(piece, bit):
         return lax.ppermute(piece, "blk", [(i, i ^ bit) for i in range(count)])
@@ -82,10 +93,14 @@
     def groups(piece):
         return lax.ppermute(piece, "groups", [(0, 1), (1, 0)])
 
-    column = lax.all_gather(
-        lax.dynamic_slice_in_dim(weight, first, half, 0), "blk", axis_index_groups=lines
-    )
-    columns = [column[:, k * size : (k + 1) * size] for k in range(CHUNKS)]
+    def column(chunk):
+        mine = lax.dynamic_slice_in_dim(weight, first + chunk * size, size, 0)
+        if near_lines(count):
+            return jnp.stack([mine] + [moved(mine, 4 * k) for k in range(1, count // 4)])
+        lines = [list(range(k, count, 4)) for k in range(4)]
+        return lax.all_gather(mine, "blk", axis_index_groups=lines)
+
+    columns = [column(k) for k in range(CHUNKS)]
     pieces = []
     for mine in (columns, [over(column, 2) for column in columns]):
         both = mine + [groups(piece) for piece in mine]
@@ -116,7 +131,7 @@
         out[...] = (frozen + lora).astype(jnp.bfloat16)
 
     for group in range(2):
-        pl.when(where[1] == group)(functools.partial(product, group))
+        pl.when(where[where.shape[0] - 1] == group)(functools.partial(product, group))
 
 
 def write_quarter(quarter, first, group, cot, grad, down, out=None):
@@ -124,11 +139,11 @@
     width = down.shape[1]
     shards, part, _ = quarter[0].shape
     stripe = part * len(quarter)
-    where = jnp.stack([first, group]).astype(jnp.int32)
+    where = jnp.concatenate([4 * line_order() + first, group[None]]).astype(jnp.int32)
     specs = [
         pl.BlockSpec((rows, depth), lambda j, where: (0, 0)),
         pl.BlockSpec(grad.shape, lambda j, where: (0, 0)),
-        pl.BlockSpec((down.shape[0], stripe), lambda j, where: (0, 4 * j + where[0])),
+        pl.BlockSpec((down.shape[0], stripe), lambda j, where: (0, where[j])),
     ] + [pl.BlockSpec((1, part, depth), lambda j, where: (j, 0, 0)) for _ in quarter]
     args = [where, cot, grad, down] + quarter
     alias = {}
@@ -143,7 +158,7 @@
             grid=(shards,),
             in_specs=specs,
             out_specs=[
-                pl.BlockSpec((rows, stripe), lambda j, where: (0, 4 * j + where[0])),
+                pl.BlockSpec((rows, stripe), lambda j, where: (0, where[j])),
                 pl.BlockSpec((8, LANES), lambda j, where: (0, 0)),
             ],
         ),
@@ -164,11 +179,18 @@
 def together(pieces, firsts, group):
     shards, part, depth = pieces[0][0].shape
     weight = jnp.zeros((shards, 4, 2, CHUNKS, part, depth), jnp.bfloat16)
+    order = line_order()
     for quarter, first in zip(pieces, firsts):
         for k, piece in enumerate(quarter):
             half = group if k < CHUNKS else 1 - group
-            place = (0, first, half, k % CHUNKS, 0, 0)
-            weight = lax.dynamic_update_slice(weight, piece[:, None, None, None], place)
+            if not near_lines(4 * shards):
+                place = (0, first, half, k % CHUNKS, 0, 0)
+                weight = lax.dynamic_update_slice(weight, piece[:, None, None, None], place)
+                continue
+            for j in range(shards):
+                place = (order[j], first, half, k % CHUNKS, 0, 0)
+                shard = piece[j][None, None, None, None]
+                weight = lax.dynamic_update_slice(weight, shard, place)
     return weight.reshape(-1, depth)
 
 
@@ -432,7 +454,8 @@
 
     sent_rows = pack_rows(token_layout_row, cotangent, devices, cap, features)
     own, _, across, _ = pieces
-    sent_rows = after(sent_rows, own[0], own[1], carried)
+    early = [own[CHUNKS - 1], own[CHUNKS], across[0], carried]
+    sent_rows = after(sent_rows, *early)
     got_rows = lax.all_to_all(sent_rows, "blk", split_axis=0, concat_axis=0)
     recv_cot = [
         got_rows[:, k * cap : (k + 1) * cap].reshape(resident_rows, features)
@@ -461,7 +484,7 @@
 
     flat_maps = adapter_down_maps.reshape(share, width)
     received = pack_features(activations, flat_maps, devices)
-    received = after(received, got_rows, own[CHUNKS], across[0])
+    received = after(received, got_rows)
     received = lax.all_to_all(received, "blk", split_axis=0, concat_axis=0)
     grad_all = to_all(after(grad_sent, received)).reshape(resident_rows, -1).T
 
@@ -480,7 +503,7 @@
             out, token = write_quarter(
                 piece, first, group, cot_rows, grad_rows, down_blocks, out
             )
-            if number == 3:
+            if number == 2:
                 place_all = after(place_all, token)
     else:
         weight = together(pieces, firsts, group)

time: 321 us -> 304 us (0.947)
  starting transfers between devices: 64.2 us -> 103 us
  waiting for transfers between devices: 118 us -> 83.8 us
  between operations: 39.2 us -> 25.4 us
  local copies, waits for them, and re-layouts: 26.5 us -> 18.6 us
    ppermute x8 -> x14, starting transfers between devices: 12.9 us -> 40.2 us  [moved(): lax.ppermute(value, 'blk', [(i, (i + steps) % count) for i in range(count)])]
    ppermute x4, waiting for transfers between devices: 43.2 us -> 22.3 us  [groups(): return lax.ppermute(piece, 'groups', [(0, 1), (1, 0)])]
    all_to_all x1, waiting for transfers between devices: 0.01 us -> 18.6 us  [local(): got_rows = lax.all_to_all(sent_rows, 'blk', split_axis=0, concat_axis=0)]
    ppermute x8 -> x14, waiting for transfers between devices: 25 us -> 7.55 us  [moved(): lax.ppermute(value, 'blk', [(i, (i + steps) % count) for i in range(count)])]
    ppermute x10, starting transfers between devices: 7.34 us -> 19.4 us  [over(): return lax.ppermute(piece, 'blk', [(i, i ^ bit) for i in range(count)])]
    all_gather x1 -> x0, waiting for transfers between devices: 11.4 us -> none  [weight_pieces(): lax.all_gather(lax.dynamic_slice_in_dim(weight, first, half, 0), 'blk', a...]
    all_to_all x1, starting transfers between devices: 17 us -> 9.14 us  [local(): got_rows = lax.all_to_all(sent_rows, 'blk', split_axis=0, concat_axis=0)]
    all_to_all x1, starting transfers between devices: 6.57 us -> 12.8 us  [to_all(): return lax.all_to_all(copies, 'blk', split_axis=0, concat_axis=0)]
  transfers between devices with their start and end apart: 28 -> 33, of which waited for: 9 -> 8; matrix products, arithmetic and copies ran while one was open for 11% -> 11% of each run, Pallas kernels for 16% -> 17%
where the time goes in v16:
time: 304 us; the launch traced here: 302 us
  starting transfers between devices  103 us (34%)
  waiting for transfers between devices  83.8 us (28%)
  Pallas kernels  51.2 us (17%)
  between operations  25.4 us (8%)
  local copies, waits for them, and re-layouts  18.6 us (6%)
  other arithmetic  15.2 us (5%)
  matrix products  5.19 us (2%)
    ppermute x14, starting transfers between devices, moved(): lax.ppermute(value, 'blk', [(i, (i + steps) % count) for i in range(count)])  40.2 us
    ppermute x10, waiting for transfers between devices, over(): return lax.ppermute(piece, 'blk', [(i, i ^ bit) for i in range(count)])  32.1 us
    pallas_call x4, Pallas kernels, write_quarter(): pl.pallas_call(quarter_kernel, grid_spec=pltpu.PrefetchScalarGridSpec(num...  28.5 us
    ppermute x4, waiting for transfers between devices, groups(): return lax.ppermute(piece, 'groups', [(0, 1), (1, 0)])  22.3 us
    ppermute x10, starting transfers between devices, over(): return lax.ppermute(piece, 'blk', [(i, i ^ bit) for i in range(count)])  19.4 us
    all_to_all x1, waiting for transfers between devices, local(): got_rows = lax.all_to_all(sent_rows, 'blk', split_axis=0, concat_axis=0)  18.6 us
    all_to_all x1, starting transfers between devices, to_all(): return lax.all_to_all(copies, 'blk', split_axis=0, concat_axis=0)  12.8 us
    all_to_all x1, starting transfers between devices, local(): got_rows = lax.all_to_all(sent_rows, 'blk', split_axis=0, concat_axis=0)  9.14 us
  transfers between devices with their start and end apart: 33, of which 8 were waited for; matrix products, arithmetic and copies ran while one was open for 11% of the time, Pallas kernels for 17%

profile of v16, /device:TPU:1, one launch (start us, length us, event | category | flops | bytes accessed | tf_op | source)
XLA Modules:
  0.0 302.4 jit_solution(6615706283074274363)
XLA Ops:
  0.6 1.1 constant_dynamic-slice_fusion
  1.7 2.2 collective-permute-start.3
  3.9 2.3 collective-permute-start.4
  6.2 1.1 collective-permute-start.5
  7.7 1.5 fusion.22
  14.4 2.9 collective-permute-start.2
  19.8 5.0 %collective-permute-done.4 = bf16[128,1024]{1,0:T(8,128)(2,1)S(1)} collective-permute-done((bf16[128,1024]{1,0:T(8,128)(2,1)S(1)}, bf16[128,1024]{1,0:T(8,128)(2,1)S(1)}, u32[]{:S(2)}, u32[]{:S(2)}) %collective-permute-start.4) | collective-permute-done | bytes 262176 | tf_op jit(solution)/shard_map/ppermute | solution.py:21
  24.7 1.5 collective-permute-start.10
  26.2 16.1 %collective-permute-start.11 = (bf16[16,9216]{1,0:T(8,128)(2,1)S(1)}, bf16[16,9216]{1,0:T(8,128)(2,1)S(1)}, u32[]{:S(2)}, u32[]{:S(2)}) collective-permute-start(bf16[16,9216]{1,0:T(8,128)(2,1)S(1)} %pad_maximum_fusion.4), channel_id=1, source_target_pairs={{0,1},{1,2},{2,3},{3,4},{4,5},{5,6},{6,7},{7,8},{8,9},{9,10},{10,1... | collective-permute-start | bytes 884744 | tf_op jit(solution)/shard_map/ppermute | solution.py:21
  42.3 1.6 collective-permute-start.8
  43.9 2.6 collective-permute-done.1
  46.5 5.7 %collective-permute-start.9 = (bf16[16,9216]{1,0:T(8,128)(2,1)S(1)}, bf16[16,9216]{1,0:T(8,128)(2,1)S(1)}, u32[]{:S(2)}, u32[]{:S(2)}) collective-permute-start(bf16[16,9216]{1,0:T(8,128)(2,1)S(1)} %pad_maximum_fusion.4), channel_id=1, source_target_pairs={{0,3},{1,4},{2,5},{3,6},{4,7},{5,8},{6,9},{7,10},{8,11},{9,12},{10... | collective-permute-start | bytes 884744 | tf_op jit(solution)/shard_map/ppermute | solution.py:21
  52.7 2.6 shard_map.94.refs_0_
  55.5 14.6 %collective-permute-start.7 = (bf16[4,128,1024]{2,1,0:T(8,128)(2,1)S(1)}, bf16[4,128,1024]{2,1,0:T(8,128)(2,1)S(1)}, u32[]{:S(2)}, u32[]{:S(2)}) collective-permute-start(bf16[4,128,1024]{2,1,0:T(8,128)(2,1)S(1)} %pad_maximum_fusion.1.rest_0_), channel_id=1, source_target_pairs={{0,2},{1,3},{2,0},{3,1},{4,6},{5,7},{6,4},{7,5},{8,10},{9,11},{10,... | collective-permute-start | bytes 3145736 | tf_op jit(solution)/shard_map/ppermute | solution.py:91
  70.0 2.1 pad_maximum_fusion.refs_1_.rest_1_
  72.1 1.2 collective-permute-start.6
  74.1 18.6 %collective-permute-done.7.refs_3_.rest_0_ = bf16[4,128,1024]{2,1,0:T(8,128)(2,1)S(1)} collective-permute-done((bf16[4,128,1024]{2,1,0:T(8,128)(2,1)S(1)}, bf16[4,128,1024]{2,1,0:T(8,128)(2,1)S(1)}, u32[]{:S(2)}, u32[]{:S(2)}) %collective-permute-start.7) | collective-permute-done | bytes 1048608 | tf_op jit(solution)/shard_map/ppermute | solution.py:91
  92.7 3.3 %collective-permute-done.6.refs_2_.rest_2_ = bf16[4,128,1024]{2,1,0:T(8,128)(2,1)} collective-permute-done((bf16[4,128,1024]{2,1,0:T(8,128)(2,1)S(1)}, bf16[4,128,1024]{2,1,0:T(8,128)(2,1)}, u32[]{:S(2)}, u32[]{:S(2)}) %collective-permute-start.6) | collective-permute-done | bytes 1048608 | tf_op jit(solution)/shard_map/ppermute | solution.py:94
  96.0 9.1 %all-to-all-start = ((bf16[16,64,512]{2,1,0:T(8,128)(2,1)}), bf16[16,64,512]{2,1,0:T(8,128)(2,1)S(1)}, u32[]{:S(2)}, u32[]{:S(2)}) async-start(bf16[16,64,512]{2,1,0:T(8,128)(2,1)} %shard_map.95), calls=%async_computation | async-start | bytes 2097152 | tf_op jit(solution)/shard_map/all_to_all | solution.py:459
  105.1 4.6 %shard_map.100.refs_0_ = bf16[16,240,512]{2,1,0:T(8,128)(2,1)} custom-call(bf16[192,8192]{1,0:T(8,128)(2,1)} %act.1, bf16[48,8192]{1,0:T(8,128)(2,1)} %bitcast.104), custom_call_target="tpu_custom_call" | custom-call | bytes 7864320 | tf_op jit(solution)/shard_map/pallas_call | solution.py:271
  109.7 18.6 %all-to-all-done.refs_1_ = bf16[16,64,512]{2,1,0:T(8,128)(2,1)S(1)} async-done(((bf16[16,64,512]{2,1,0:T(8,128)(2,1)}), bf16[16,64,512]{2,1,0:T(8,128)(2,1)S(1)}, u32[]{:S(2)}, u32[]{:S(2)}) %all-to-all-start) | async-done | bytes 1048608 | tf_op jit(solution)/shard_map/all_to_all | solution.py:459
  129.3 6.7 %all-to-all-start.1 = ((bf16[16,240,512]{2,1,0:T(8,128)(2,1)}), bf16[16,240,512]{2,1,0:T(8,128)(2,1)}, u32[]{:S(2)}, u32[]{:S(2)}) async-start(bf16[16,240,512]{2,1,0:T(8,128)(2,1)} %shard_map.101), calls=%async_computation.1 | async-start | bytes 7864320 | tf_op jit(solution)/shard_map/all_to_all | solution.py:488
  147.3 1.2 collective-permute-start.22
  149.0 1.5 collective-permute-start.13
  153.0 19.0 %collective-permute-done.22.rest_3_ = bf16[4,128,1024]{2,1,0:T(8,128)(2,1)} collective-permute-done((bf16[4,128,1024]{2,1,0:T(8,128)(2,1)S(1)}, bf16[4,128,1024]{2,1,0:T(8,128)(2,1)}, u32[]{:S(2)}, u32[]{:S(2)}) %collective-permute-start.22) | collective-permute-done | bytes 1048608 | tf_op jit(solution)/shard_map/ppermute | solution.py:94
  175.7 1.0 fusion.9
  176.7 1.1 fusion.1
  177.9 1.4 add.281.refs_0_
  181.0 1.2 collective-permute-start.15
  182.2 13.5 %collective-permute-done.13.rest_1_ = bf16[4,128,1024]{2,1,0:T(8,128)(2,1)} collective-permute-done((bf16[4,128,1024]{2,1,0:T(8,128)(2,1)S(1)}, bf16[4,128,1024]{2,1,0:T(8,128)(2,1)}, u32[]{:S(2)}, u32[]{:S(2)}) %collective-permute-start.13) | collective-permute-done | bytes 1048608 | tf_op jit(solution)/shard_map/ppermute | solution.py:91
  195.8 1.2 collective-permute-start.17
  197.0 1.2 convolution_convert_fusion.1
  200.7 7.1 %shard_map.96 = (bf16[384,8192]{1,0:T(8,128)(2,1)}, f32[8,128]{1,0:T(8,128)}) custom-call(s32[5]{0:T(128)} %pad_add_fusion.3.where, bf16[384,1024]{1,0:T(8,128)(2,1)} %pad_maximum_fusion.2.cot, bf16[384,16]{1,0:T(8,128)(2,1)} %convolution_convert_fusion.2.grad, bf16[48,8192]{1,0:T(8,128)(2,1)} %pad_maximum_fusion.3.down, bf16[4,128,1024]{2,1,0:T(8,128)(2,1)} %copy-done.11, ...), custom_call_target="tpu_custom_call" | custom-call | flops 1610612736 | bytes 5767168 | tf_op jit(solution)/shard_map/pallas_call | solution.py:154
  207.8 7.1 %shard_map.97 = (bf16[384,8192]{1,0:T(8,128)(2,1)}, f32[8,128]{1,0:T(8,128)}) custom-call(s32[5]{0:T(128)} %pad_add_fusion.2.where, bf16[384,1024]{1,0:T(8,128)(2,1)} %pad_maximum_fusion.2.cot, bf16[384,16]{1,0:T(8,128)(2,1)} %convolution_convert_fusion.2.grad, bf16[48,8192]{1,0:T(8,128)(2,1)} %pad_maximum_fusion.3.down, ...), custom_call_target="tpu_custom_call", output_to_operand_aliasing={{0}: (8, {})} | custom-call | flops 1610612736 | bytes 5767168 | tf_op jit(solution)/shard_map/pallas_call | solution.py:154
  215.0 1.4 broadcast_in_dim.120
  216.4 12.8 %all-to-all-start.2 = ((bf16[16,24,256]{2,1,0:T(8,128)(2,1)}), bf16[16,24,256]{2,1,0:T(8,128)(2,1)S(1)}, u32[]{:S(2)}, u32[]{:S(2)}) async-start(bf16[16,24,256]{2,1,0:T(8,128)(2,1)} %broadcast_in_dim.120), calls=%async_computation.2 | async-start | bytes 393216 | tf_op jit(solution)/shard_map/all_to_all | solution.py:27
  229.2 7.1 %shard_map.98 = (bf16[384,8192]{1,0:T(8,128)(2,1)}, f32[8,128]{1,0:T(8,128)}) custom-call(s32[5]{0:T(128)} %pad_add_fusion.1.where, bf16[384,1024]{1,0:T(8,128)(2,1)} %pad_maximum_fusion.2.cot, bf16[384,16]{1,0:T(8,128)(2,1)} %convolution_convert_fusion.2.grad, bf16[48,8192]{1,0:T(8,128)(2,1)} %pad_maximum_fusion.3.down, ...), custom_call_target="tpu_custom_call", output_to_operand_aliasing={{0}: (8, {})} | custom-call | flops 1610612736 | bytes 5767168 | tf_op jit(solution)/shard_map/pallas_call | solution.py:154
  236.4 8.8 %shard_map.104.refs_1_ = f32[256,384]{1,0:T(8,128)} custom-call(bf16[16,240,512]{2,1,0:T(8,128)(2,1)} %all-to-all-done.1.refs_1_.act.maps, bf16[16,240,512]{2,1,0:T(8,128)(2,1)} %all-to-all-done.1.refs_1_.act.maps, s32[1,3072]{1,0:T(1,128)} %reshape.318.rows.refs_0_, s32[1,3072]{1,0:T(1,128)} %shard_map.103.spots, s32[32,1]{1,0:T(8,128)} %copy.35.starts), custom_call_target="tpu_custom_call" | custom-call | flops 2415919104 | bytes 3145728 | tf_op jit(solution)/shard_map/pallas_call | solution.py:526
  245.1 2.0 copy.38
  247.1 6.0 %all-to-all-start.4 = ((f32[16,24,256]{2,1,0:T(8,128)}), f32[16,24,256]{2,1,0:T(8,128)S(1)}, u32[]{:S(2)}, u32[]{:S(2)}) async-start(f32[16,24,256]{2,1,0:T(8,128)} %bitcast.42), calls=%async_computation.4 | async-start | bytes 786432 | tf_op jit(solution)/shard_map/all_to_all | solution.py:530
  255.1 6.8 %shard_map.106 = bf16[768,512]{1,0:T(8,128)(2,1)} custom-call(bf16[16,240,512]{2,1,0:T(8,128)(2,1)} %all-to-all-done.1.refs_1_.act.maps, bf16[256,384]{1,0:T(8,128)(2,1)} %bitcast.123, s32[1,3072]{1,0:T(1,128)} %shard_map.105.rows, s32[1,3072]{1,0:T(1,128)} %shard_map.103.spots, s32[32,1]{1,0:T(8,128)} %copy.35.starts), custom_call_target="tpu_custom_call" | custom-call | flops 2415919104 | bytes 3145728 | tf_op jit(solution)/shard_map/pallas_call | solution.py:528
  261.9 3.2 %all-to-all-done.4 = f32[16,24,256]{2,1,0:T(8,128)S(1)} async-done(((f32[16,24,256]{2,1,0:T(8,128)}), f32[16,24,256]{2,1,0:T(8,128)S(1)}, u32[]{:S(2)}, u32[]{:S(2)}) %all-to-all-start.4) | async-done | bytes 393248 | tf_op jit(solution)/shard_map/all_to_all | solution.py:530
  265.1 3.8 %all-to-all-start.3 = ((bf16[16,48,512]{2,1,0:T(8,128)(2,1)}), bf16[16,48,512]{2,1,0:T(8,128)(2,1)S(1)}, u32[]{:S(2)}, u32[]{:S(2)}) async-start(bf16[16,48,512]{2,1,0:T(8,128)(2,1)} %bitcast.114), calls=%async_computation.3 | async-start | bytes 1572864 | tf_op jit(solution)/shard_map/all_to_all | solution.py:533
  283.4 1.9 select_add_fusion.1
  285.6 4.3 %collective-permute-start.25 = (f32[16,1024]{1,0:T(8,128)S(1)}, f32[16,1024]{1,0:T(8,128)S(1)}, u32[]{:S(2)}, u32[]{:S(2)}) collective-permute-start(f32[16,1024]{1,0:T(8,128)S(1)} %get-tuple-element.20), channel_id=1, source_target_pairs={{0,14},{1,15},{2,0},{3,1},{4,2},{5,3},{6,4},{7,5},{8,6},{9,7},{10,... | collective-permute-start | bytes 196616 | tf_op jit(solution)/shard_map/ppermute | solution.py:21
  289.9 1.6 collective-permute-start.26
  291.8 7.1 %shard_map.99 = (bf16[384,8192]{1,0:T(8,128)(2,1)}, f32[8,128]{1,0:T(8,128)}) custom-call(s32[5]{0:T(128)} %pad_add_fusion.where, bf16[384,1024]{1,0:T(8,128)(2,1)} %pad_maximum_fusion.2.cot, bf16[384,16]{1,0:T(8,128)(2,1)} %convolution_convert_fusion.2.grad, bf16[48,8192]{1,0:T(8,128)(2,1)} %pad_maximum_fusion.3.down, ...), custom_call_target="tpu_custom_call", output_to_operand_aliasing={{0}: (8, {})} | custom-call | flops 1610612736 | bytes 5767168 | tf_op jit(solution)/shard_map/pallas_call | solution.py:154
  300.9 1.4 reshape.317
  (136 shorter events, 27.3 us)
Async XLA Ops:
  0.6 51.5 %copy-start.18 = (s32[192]{0:T(256)S(1)}, s32[192]{0:T(256)}, u32[]{:S(2)}) copy-start(s32[192]{0:T(256)} %param.9) | copy-start | bytes 2308
  1.7 12.6 %collective-permute-start.3 = (bf16[128,1024]{1,0:T(8,128)(2,1)S(1)}, bf16[128,1024]{1,0:T(8,128)(2,1)S(1)}, u32[]{:S(2)}, u32[]{:S(2)}) collective-permute-start(bf16[128,1024]{1,0:T(8,128)(2,1)S(1)} %get-tuple-element.38), channel_id=1, source_target_pairs={{0,4},{1,5},{2,6},{3,7},{4,8},{5,9},{6,10},{7,11},{8,12},{9,13},{1... | collective-permute-start | bytes 786440 | tf_op jit(solution)/shard_map/ppermute | solution.py:21
  3.9 20.8 %collective-permute-start.4 = (bf16[128,1024]{1,0:T(8,128)(2,1)S(1)}, bf16[128,1024]{1,0:T(8,128)(2,1)S(1)}, u32[]{:S(2)}, u32[]{:S(2)}) collective-permute-start(bf16[128,1024]{1,0:T(8,128)(2,1)S(1)} %get-tuple-element.38), channel_id=1, source_target_pairs={{0,8},{1,9},{2,10},{3,11},{4,12},{5,13},{6,14},{7,15},{8,0},{9,1},... | collective-permute-start | bytes 786440 | tf_op jit(solution)/shard_map/ppermute | solution.py:21
  6.2 20.0 %collective-permute-start.5 = (bf16[128,1024]{1,0:T(8,128)(2,1)S(1)}, bf16[128,1024]{1,0:T(8,128)(2,1)S(1)}, u32[]{:S(2)}, u32[]{:S(2)}) collective-permute-start(bf16[128,1024]{1,0:T(8,128)(2,1)S(1)} %get-tuple-element.38), channel_id=1, source_target_pairs={{0,12},{1,13},{2,14},{3,15},{4,0},{5,1},{6,2},{7,3},{8,4},{9,5},{1... | collective-permute-start | bytes 786440 | tf_op jit(solution)/shard_map/ppermute | solution.py:21
  7.3 35.1 %collective-permute-start = (bf16[128,1024]{1,0:T(8,128)(2,1)S(1)}, bf16[128,1024]{1,0:T(8,128)(2,1)S(1)}, u32[]{:S(2)}, u32[]{:S(2)}) collective-permute-start(bf16[128,1024]{1,0:T(8,128)(2,1)S(1)} %get-tuple-element.39), channel_id=1, source_target_pairs={{0,4},{1,5},{2,6},{3,7},{4,8},{5,9},{6,10},{7,11},{8,12},{9,13},{1... | collective-permute-start | bytes 786440 | tf_op jit(solution)/shard_map/ppermute | solution.py:21
  7.7 38.8 %collective-permute-start.1 = (bf16[128,1024]{1,0:T(8,128)(2,1)S(1)}, bf16[128,1024]{1,0:T(8,128)(2,1)S(1)}, u32[]{:S(2)}, u32[]{:S(2)}) collective-permute-start(bf16[128,1024]{1,0:T(8,128)(2,1)S(1)} %get-tuple-element.39), channel_id=1, source_target_pairs={{0,8},{1,9},{2,10},{3,11},{4,12},{5,13},{6,14},{7,15},{8,0},{9,1},... | collective-permute-start | bytes 786440 | tf_op jit(solution)/shard_map/ppermute | solution.py:21
  14.4 41.1 %collective-permute-start.2 = (bf16[128,1024]{1,0:T(8,128)(2,1)S(1)}, bf16[128,1024]{1,0:T(8,128)(2,1)}, u32[]{:S(2)}, u32[]{:S(2)}) collective-permute-start(bf16[128,1024]{1,0:T(8,128)(2,1)S(1)} %get-tuple-element.39), channel_id=1, source_target_pairs={{0,12},{1,13},{2,14},{3,15},{4,0},{5,1},{6,2},{7,3},{8,4},{9,5},{1... | collective-permute-start | bytes 786440 | tf_op jit(solution)/shard_map/ppermute | solution.py:21
  24.7 47.3 %collective-permute-start.10 = (bf16[16,9216]{1,0:T(8,128)(2,1)S(1)}, bf16[16,9216]{1,0:T(8,128)(2,1)S(1)}, u32[]{:S(2)}, u32[]{:S(2)}) collective-permute-start(bf16[16,9216]{1,0:T(8,128)(2,1)S(1)} %pad_maximum_fusion.4), channel_id=1, source_target_pairs={{0,2},{1,3},{2,4},{3,5},{4,6},{5,7},{6,8},{7,9},{8,10},{9,11},{10,... | collective-permute-start | bytes 884744 | tf_op jit(solution)/shard_map/ppermute | solution.py:21
  26.2 47.1 %collective-permute-start.11 = (bf16[16,9216]{1,0:T(8,128)(2,1)S(1)}, bf16[16,9216]{1,0:T(8,128)(2,1)S(1)}, u32[]{:S(2)}, u32[]{:S(2)}) collective-permute-start(bf16[16,9216]{1,0:T(8,128)(2,1)S(1)} %pad_maximum_fusion.4), channel_id=1, source_target_pairs={{0,1},{1,2},{2,3},{3,4},{4,5},{5,6},{6,7},{7,8},{8,9},{9,10},{10,1... | collective-permute-start | bytes 884744 | tf_op jit(solution)/shard_map/ppermute | solution.py:21
  42.3 31.0 %collective-permute-start.8 = (bf16[16,9216]{1,0:T(8,128)(2,1)S(1)}, bf16[16,9216]{1,0:T(8,128)(2,1)S(1)}, u32[]{:S(2)}, u32[]{:S(2)}) collective-permute-start(bf16[16,9216]{1,0:T(8,128)(2,1)S(1)} %pad_maximum_fusion.4), channel_id=1, source_target_pairs={{0,4},{1,5},{2,6},{3,7},{4,8},{5,9},{6,10},{7,11},{8,12},{9,13},{1... | collective-permute-start | bytes 884744 | tf_op jit(solution)/shard_map/ppermute | solution.py:21
  46.5 26.9 %collective-permute-start.9 = (bf16[16,9216]{1,0:T(8,128)(2,1)S(1)}, bf16[16,9216]{1,0:T(8,128)(2,1)S(1)}, u32[]{:S(2)}, u32[]{:S(2)}) collective-permute-start(bf16[16,9216]{1,0:T(8,128)(2,1)S(1)} %pad_maximum_fusion.4), channel_id=1, source_target_pairs={{0,3},{1,4},{2,5},{3,6},{4,7},{5,8},{6,9},{7,10},{8,11},{9,12},{10... | collective-permute-start | bytes 884744 | tf_op jit(solution)/shard_map/ppermute | solution.py:21
  55.4 18.7 %copy-start.11 = (bf16[4,128,1024]{2,1,0:T(8,128)(2,1)}, bf16[4,128,1024]{2,1,0:T(8,128)(2,1)S(1)}, u32[]{:S(2)}) copy-start(bf16[4,128,1024]{2,1,0:T(8,128)(2,1)S(1)} %pad_maximum_fusion.1.rest_0_) | copy-start | bytes 3145732
  55.5 37.2 %collective-permute-start.7 = (bf16[4,128,1024]{2,1,0:T(8,128)(2,1)S(1)}, bf16[4,128,1024]{2,1,0:T(8,128)(2,1)S(1)}, u32[]{:S(2)}, u32[]{:S(2)}) collective-permute-start(bf16[4,128,1024]{2,1,0:T(8,128)(2,1)S(1)} %pad_maximum_fusion.1.rest_0_), channel_id=1, source_target_pairs={{0,2},{1,3},{2,0},{3,1},{4,6},{5,7},{6,4},{7,5},{8,10},{9,11},{10,... | collective-permute-start | bytes 3145736 | tf_op jit(solution)/shard_map/ppermute | solution.py:91
  72.1 23.9 %collective-permute-start.6 = (bf16[4,128,1024]{2,1,0:T(8,128)(2,1)S(1)}, bf16[4,128,1024]{2,1,0:T(8,128)(2,1)}, u32[]{:S(2)}, u32[]{:S(2)}) collective-permute-start(bf16[4,128,1024]{2,1,0:T(8,128)(2,1)S(1)} %pad_maximum_fusion.1.rest_0_), channel_id=1, source_target_pairs={{0,16},{16,0},{1,17},{17,1},{2,18},{18,2},{3,19},{19,3},{4,20},{20... | collective-permute-start | bytes 3145736 | tf_op jit(solution)/shard_map/ppermute | solution.py:94
  92.7 3.3 %copy-start.3 = (bf16[4,128,1024]{2,1,0:T(8,128)(2,1)}, bf16[4,128,1024]{2,1,0:T(8,128)(2,1)S(1)}, u32[]{:S(2)}) copy-start(bf16[4,128,1024]{2,1,0:T(8,128)(2,1)S(1)} %collective-permute-done.7.refs_3_.rest_0_) | copy-start | bytes 3145732
  96.0 32.3 %all-to-all-start = ((bf16[16,64,512]{2,1,0:T(8,128)(2,1)}), bf16[16,64,512]{2,1,0:T(8,128)(2,1)S(1)}, u32[]{:S(2)}, u32[]{:S(2)}) async-start(bf16[16,64,512]{2,1,0:T(8,128)(2,1)} %shard_map.95), calls=%async_computation | async-start | bytes 2097152 | tf_op jit(solution)/shard_map/all_to_all | solution.py:459
  129.3 18.0 %copy-start.6 = (bf16[4,128,1024]{2,1,0:T(8,128)(2,1)S(1)}, bf16[4,128,1024]{2,1,0:T(8,128)(2,1)}, u32[]{:S(2)}) copy-start(bf16[4,128,1024]{2,1,0:T(8,128)(2,1)} %pad_maximum_fusion.refs_1_.rest_1_) | copy-start | bytes 3145732
  129.3 21.3 %copy-start.2 = (bf16[3,16,8192]{2,1,0:T(8,128)(2,1)S(1)}, bf16[3,16,8192]{2,1,0:T(8,128)(2,1)}, u32[]{:S(2)}) copy-start(bf16[3,16,8192]{2,1,0:T(8,128)(2,1)} %param.12) | copy-start | bytes 2359300
  129.3 21.3 %copy-start.10 = (bf16[16,9216]{1,0:T(8,128)(2,1)S(1)}, bf16[16,9216]{1,0:T(8,128)(2,1)}, u32[]{:S(2)}) copy-start(bf16[16,9216]{1,0:T(8,128)(2,1)} %select_select_fusion.refs_4_) | copy-start | bytes 884740
  129.3 85.7 %all-to-all-start.1 = ((bf16[16,240,512]{2,1,0:T(8,128)(2,1)}), bf16[16,240,512]{2,1,0:T(8,128)(2,1)}, u32[]{:S(2)}, u32[]{:S(2)}) async-start(bf16[16,240,512]{2,1,0:T(8,128)(2,1)} %shard_map.101), calls=%async_computation.1 | async-start | bytes 7864320 | tf_op jit(solution)/shard_map/all_to_all | solution.py:488
  136.0 14.6 %copy-start.12 = (bf16[3,16,1024]{2,1,0:T(8,128)(2,1)S(1)}, bf16[3,16,1024]{2,1,0:T(8,128)(2,1)}, u32[]{:S(2)}) copy-start(bf16[3,16,1024]{2,1,0:T(8,128)(2,1)} %param.13) | copy-start | bytes 294916
  147.3 25.7 %copy-start.1 = (bf16[16,64,512]{2,1,0:T(8,128)(2,1)S(1)}, bf16[16,64,512]{2,1,0:T(8,128)(2,1)}, u32[]{:S(2)}) copy-start(bf16[16,64,512]{2,1,0:T(8,128)(2,1)} %copy-done) | copy-start | bytes 3145732
  147.3 24.7 %collective-permute-start.22 = (bf16[4,128,1024]{2,1,0:T(8,128)(2,1)S(1)}, bf16[4,128,1024]{2,1,0:T(8,128)(2,1)}, u32[]{:S(2)}, u32[]{:S(2)}) collective-permute-start(bf16[4,128,1024]{2,1,0:T(8,128)(2,1)S(1)} %copy-done.6), channel_id=1, source_target_pairs={{0,16},{16,0},{1,17},{17,1},{2,18},{18,2},{3,19},{19,3},{4,20},{20... | collective-permute-start | bytes 3145736 | tf_op jit(solution)/shard_map/ppermute | solution.py:94
  148.5 32.5 %collective-permute-start.20 = (bf16[4,128,1024]{2,1,0:T(8,128)(2,1)S(1)}, bf16[4,128,1024]{2,1,0:T(8,128)(2,1)}, u32[]{:S(2)}, u32[]{:S(2)}) collective-permute-start(bf16[4,128,1024]{2,1,0:T(8,128)(2,1)S(1)} %copy-done.6), channel_id=1, source_target_pairs={{0,1},{1,0},{2,3},{3,2},{4,5},{5,4},{6,7},{7,6},{8,9},{9,8},{10,11... | collective-permute-start | bytes 3145736 | tf_op jit(solution)/shard_map/ppermute | solution.py:91
  148.9 58.9 %collective-permute-start.19 = (bf16[4,128,1024]{2,1,0:T(8,128)(2,1)}, bf16[4,128,1024]{2,1,0:T(8,128)(2,1)}, u32[]{:S(2)}, u32[]{:S(2)}) collective-permute-start(bf16[4,128,1024]{2,1,0:T(8,128)(2,1)} %copy-done.11), channel_id=1, source_target_pairs={{0,1},{1,0},{2,3},{3,2},{4,5},{5,4},{6,7},{7,6},{8,9},{9,8},{10,11... | collective-permute-start | bytes 3145736 | tf_op jit(solution)/shard_map/ppermute | solution.py:91
  149.0 46.8 %collective-permute-start.13 = (bf16[4,128,1024]{2,1,0:T(8,128)(2,1)S(1)}, bf16[4,128,1024]{2,1,0:T(8,128)(2,1)}, u32[]{:S(2)}, u32[]{:S(2)}) collective-permute-start(bf16[4,128,1024]{2,1,0:T(8,128)(2,1)S(1)} %copy-done.6), channel_id=1, source_target_pairs={{0,2},{1,3},{2,0},{3,1},{4,6},{5,7},{6,4},{7,5},{8,10},{9,11},{10,... | collective-permute-start | bytes 3145736 | tf_op jit(solution)/shard_map/ppermute | solution.py:91
  152.2 55.6 %collective-permute-start.21 = (bf16[4,128,1024]{2,1,0:T(8,128)(2,1)}, bf16[4,128,1024]{2,1,0:T(8,128)(2,1)}, u32[]{:S(2)}, u32[]{:S(2)}) collective-permute-start(bf16[4,128,1024]{2,1,0:T(8,128)(2,1)} %collective-permute-done.6.refs_2_.rest_2_), channel_id=1, source_target_pairs={{0,1},{1,0},{2,3},{3,2},{4,5},{5,4},{6,7},{7,6},{8,9},{9,8},{10,11... | collective-permute-start | bytes 3145736 | tf_op jit(solution)/shard_map/ppermute | solution.py:91
  172.0 35.9 %collective-permute-start.23 = (bf16[4,128,1024]{2,1,0:T(8,128)(2,1)}, bf16[4,128,1024]{2,1,0:T(8,128)(2,1)}, u32[]{:S(2)}, u32[]{:S(2)}) collective-permute-start(bf16[4,128,1024]{2,1,0:T(8,128)(2,1)} %collective-permute-done.22.rest_3_), channel_id=1, source_target_pairs={{0,1},{1,0},{2,3},{3,2},{4,5},{5,4},{6,7},{7,6},{8,9},{9,8},{10,11... | collective-permute-start | bytes 3145736 | tf_op jit(solution)/shard_map/ppermute | solution.py:91
  174.1 6.9 %copy-start.4 = (bf16[4,128,1024]{2,1,0:T(8,128)(2,1)S(1)}, bf16[4,128,1024]{2,1,0:T(8,128)(2,1)}, u32[]{:S(2)}) copy-start(bf16[4,128,1024]{2,1,0:T(8,128)(2,1)} %copy-done.3) | copy-start | bytes 3145732
  174.9 23.3 %copy-start.16 = (s32[384]{0:T(512)S(1)}, s32[384]{0:T(512)}, u32[]{:S(2)}) copy-start(s32[384]{0:T(512)} %copy-done.15) | copy-start | bytes 4612
  176.7 21.5 %copy-start.8 = (bf16[16,24,512]{2,1,0:T(8,128)(2,1)S(1)}, bf16[16,24,512]{2,1,0:T(8,128)(2,1)}, u32[]{:S(2)}) copy-start(bf16[16,24,512]{2,1,0:T(8,128)(2,1)} %copy-done.7) | copy-start | bytes 1179652
  181.0 48.2 %collective-permute-start.15 = (bf16[4,128,1024]{2,1,0:T(8,128)(2,1)S(1)}, bf16[4,128,1024]{2,1,0:T(8,128)(2,1)}, u32[]{:S(2)}, u32[]{:S(2)}) collective-permute-start(bf16[4,128,1024]{2,1,0:T(8,128)(2,1)S(1)} %copy-done.4), channel_id=1, source_target_pairs={{0,16},{16,0},{1,17},{17,1},{2,18},{18,2},{3,19},{19,3},{4,20},{20... | collective-permute-start | bytes 3145736 | tf_op jit(solution)/shard_map/ppermute | solution.py:94
  195.8 33.4 %collective-permute-start.17 = (bf16[4,128,1024]{2,1,0:T(8,128)(2,1)}, bf16[4,128,1024]{2,1,0:T(8,128)(2,1)}, u32[]{:S(2)}, u32[]{:S(2)}) collective-permute-start(bf16[4,128,1024]{2,1,0:T(8,128)(2,1)} %collective-permute-done.13.rest_1_), channel_id=1, source_target_pairs={{0,16},{16,0},{1,17},{17,1},{2,18},{18,2},{3,19},{19,3},{4,20},{20... | collective-permute-start | bytes 3145736 | tf_op jit(solution)/shard_map/ppermute | solution.py:94
  216.4 30.8 %all-to-all-start.2 = ((bf16[16,24,256]{2,1,0:T(8,128)(2,1)}), bf16[16,24,256]{2,1,0:T(8,128)(2,1)S(1)}, u32[]{:S(2)}, u32[]{:S(2)}) async-start(bf16[16,24,256]{2,1,0:T(8,128)(2,1)} %broadcast_in_dim.120), calls=%async_computation.2 | async-start | bytes 393216 | tf_op jit(solution)/shard_map/all_to_all | solution.py:27
  245.1 8.1 %copy-start.5 = (bf16[4,128,1024]{2,1,0:T(8,128)(2,1)S(1)}, bf16[4,128,1024]{2,1,0:T(8,128)(2,1)}, u32[]{:S(2)}) copy-start(bf16[4,128,1024]{2,1,0:T(8,128)(2,1)} %copy-done.3) | copy-start | bytes 3145732
  247.1 17.9 %all-to-all-start.4 = ((f32[16,24,256]{2,1,0:T(8,128)}), f32[16,24,256]{2,1,0:T(8,128)S(1)}, u32[]{:S(2)}, u32[]{:S(2)}) async-start(f32[16,24,256]{2,1,0:T(8,128)} %bitcast.42), calls=%async_computation.4 | async-start | bytes 786432 | tf_op jit(solution)/shard_map/all_to_all | solution.py:530
  253.2 32.4 %collective-permute-start.12 = (bf16[4,128,1024]{2,1,0:T(8,128)(2,1)S(1)}, bf16[4,128,1024]{2,1,0:T(8,128)(2,1)}, u32[]{:S(2)}, u32[]{:S(2)}) collective-permute-start(bf16[4,128,1024]{2,1,0:T(8,128)(2,1)S(1)} %copy-done.5), channel_id=1, source_target_pairs={{0,1},{1,0},{2,3},{3,2},{4,5},{5,4},{6,7},{7,6},{8,9},{9,8},{10,11... | collective-permute-start | bytes 3145736 | tf_op jit(solution)/shard_map/ppermute | solution.py:91
  253.4 36.6 %collective-permute-start.14 = (bf16[4,128,1024]{2,1,0:T(8,128)(2,1)}, bf16[4,128,1024]{2,1,0:T(8,128)(2,1)}, u32[]{:S(2)}, u32[]{:S(2)}) collective-permute-start(bf16[4,128,1024]{2,1,0:T(8,128)(2,1)} %collective-permute-done.13.rest_1_), channel_id=1, source_target_pairs={{0,1},{1,0},{2,3},{3,2},{4,5},{5,4},{6,7},{7,6},{8,9},{9,8},{10,11... | collective-permute-start | bytes 3145736 | tf_op jit(solution)/shard_map/ppermute | solution.py:91
  253.8 37.8 %collective-permute-start.16 = (bf16[4,128,1024]{2,1,0:T(8,128)(2,1)}, bf16[4,128,1024]{2,1,0:T(8,128)(2,1)}, u32[]{:S(2)}, u32[]{:S(2)}) collective-permute-start(bf16[4,128,1024]{2,1,0:T(8,128)(2,1)} %collective-permute-done.15.rest_2_), channel_id=1, source_target_pairs={{0,1},{1,0},{2,3},{3,2},{4,5},{5,4},{6,7},{7,6},{8,9},{9,8},{10,11... | collective-permute-start | bytes 3145736 | tf_op jit(solution)/shard_map/ppermute | solution.py:91
  253.9 37.9 %collective-permute-start.18 = (bf16[4,128,1024]{2,1,0:T(8,128)(2,1)}, bf16[4,128,1024]{2,1,0:T(8,128)(2,1)}, u32[]{:S(2)}, u32[]{:S(2)}) collective-permute-start(bf16[4,128,1024]{2,1,0:T(8,128)(2,1)} %collective-permute-done.17.rest_3_), channel_id=1, source_target_pairs={{0,1},{1,0},{2,3},{3,2},{4,5},{5,4},{6,7},{7,6},{8,9},{9,8},{10,11... | collective-permute-start | bytes 3145736 | tf_op jit(solution)/shard_map/ppermute | solution.py:91
  261.9 21.1 %copy-start.14 = (s32[384]{0:T(512)S(1)}, s32[384]{0:T(512)}, u32[]{:S(2)}) copy-start(s32[384]{0:T(512)} %copy-done.13) | copy-start | bytes 4612
  261.9 21.1 %copy-start.17 = (s32[48]{0:T(128)S(1)}, s32[48]{0:T(128)}, u32[]{:S(2)}) copy-start(s32[48]{0:T(128)} %and_select_fusion) | copy-start | bytes 580
  261.9 21.4 %copy-start.9 = (bf16[16,24,512]{2,1,0:T(8,128)(2,1)S(1)}, bf16[16,24,512]{2,1,0:T(8,128)(2,1)}, u32[]{:S(2)}) copy-start(bf16[16,24,512]{2,1,0:T(8,128)(2,1)} %copy-done.7) | copy-start | bytes 1179652
  265.1 34.7 %all-to-all-start.3 = ((bf16[16,48,512]{2,1,0:T(8,128)(2,1)}), bf16[16,48,512]{2,1,0:T(8,128)(2,1)S(1)}, u32[]{:S(2)}, u32[]{:S(2)}) async-start(bf16[16,48,512]{2,1,0:T(8,128)(2,1)} %bitcast.114), calls=%async_computation.3 | async-start | bytes 1572864 | tf_op jit(solution)/shard_map/all_to_all | solution.py:533
  285.4 13.6 %collective-permute-start.24 = (f32[16,1024]{1,0:T(8,128)S(1)}, f32[16,1024]{1,0:T(8,128)S(1)}, u32[]{:S(2)}, u32[]{:S(2)}) collective-permute-start(f32[16,1024]{1,0:T(8,128)S(1)} %get-tuple-element.20), channel_id=1, source_target_pairs={{0,15},{1,0},{2,1},{3,2},{4,3},{5,4},{6,5},{7,6},{8,7},{9,8},{10,9... | collective-permute-start | bytes 196616 | tf_op jit(solution)/shard_map/ppermute | solution.py:21
  285.6 13.3 %collective-permute-start.25 = (f32[16,1024]{1,0:T(8,128)S(1)}, f32[16,1024]{1,0:T(8,128)S(1)}, u32[]{:S(2)}, u32[]{:S(2)}) collective-permute-start(f32[16,1024]{1,0:T(8,128)S(1)} %get-tuple-element.20), channel_id=1, source_target_pairs={{0,14},{1,15},{2,0},{3,1},{4,2},{5,3},{6,4},{7,5},{8,6},{9,7},{10,... | collective-permute-start | bytes 196616 | tf_op jit(solution)/shard_map/ppermute | solution.py:21
  289.9 9.0 %collective-permute-start.26 = (f32[16,1024]{1,0:T(8,128)S(1)}, f32[16,1024]{1,0:T(8,128)S(1)}, u32[]{:S(2)}, u32[]{:S(2)}) collective-permute-start(f32[16,1024]{1,0:T(8,128)S(1)} %get-tuple-element.20), channel_id=1, source_target_pairs={{0,13},{1,14},{2,15},{3,0},{4,1},{5,2},{6,3},{7,4},{8,5},{9,6},{10... | collective-permute-start | bytes 196616 | tf_op jit(solution)/shard_map/ppermute | solution.py:21
  291.6 7.4 %collective-permute-start.27 = (f32[16,1024]{1,0:T(8,128)S(1)}, f32[16,1024]{1,0:T(8,128)S(1)}, u32[]{:S(2)}, u32[]{:S(2)}) collective-permute-start(f32[16,1024]{1,0:T(8,128)S(1)} %get-tuple-element.20), channel_id=1, source_target_pairs={{0,12},{1,13},{2,14},{3,15},{4,0},{5,1},{6,2},{7,3},{8,4},{9,5},{1... | collective-permute-start | bytes 196616 | tf_op jit(solution)/shard_map/ppermute | solution.py:21
  (4 other events, 5.3 us)

commit v17 on v16

--- a/solution.py
+++ b/solution.py
@@ -454,8 +454,7 @@
 
     sent_rows = pack_rows(token_layout_row, cotangent, devices, cap, features)
     own, _, across, _ = pieces
-    early = [own[CHUNKS - 1], own[CHUNKS], across[0], carried]
-    sent_rows = after(sent_rows, *early)
+    sent_rows = after(sent_rows, *own[:CHUNKS], carried)
     got_rows = lax.all_to_all(sent_rows, "blk", split_axis=0, concat_axis=0)
     recv_cot = [
         got_rows[:, k * cap : (k + 1) * cap].reshape(resident_rows, features)
@@ -484,7 +483,7 @@
 
     flat_maps = adapter_down_maps.reshape(share, width)
     received = pack_features(activations, flat_maps, devices)
-    received = after(received, got_rows)
+    received = after(received, got_rows, own[CHUNKS], across[0])
     received = lax.all_to_all(received, "blk", split_axis=0, concat_axis=0)
     grad_all = to_all(after(grad_sent, received)).reshape(resident_rows, -1).T
 
@@ -499,12 +498,11 @@
     firsts = [quarter, quarter ^ 1, quarter ^ 2, quarter ^ 3]
     if own[0].shape[1] % LANES == 0:
         out = None
-        for number, (piece, first) in enumerate(zip(pieces, firsts)):
+        for piece, first in zip(pieces[:2], firsts):
             out, token = write_quarter(
                 piece, first, group, cot_rows, grad_rows, down_blocks, out
             )
-            if number == 2:
-                place_all = after(place_all, token)
+        place_all = after(place_all, token)
     else:
         weight = together(pieces, firsts, group)
         lora = [
@@ -552,6 +550,10 @@
         up_grads.append(adapter_scale * total)
     up_map_gradient = jnp.stack(up_grads)
 
+    if own[0].shape[1] % LANES == 0:
+        late = after(grad_rows, down_f)
+        for piece, first in zip(pieces[2:], firsts[2:]):
+            out, _ = write_quarter(piece, first, group, cot_rows, late, down_blocks, out)
     return (out, down_map_gradient, up_map_gradient)
 
 

time: 304 us -> 299 us (0.984)
  starting transfers between devices: 103 us -> 99.1 us
    all_to_all x1, waiting for transfers between devices: 18.6 us -> 0.01 us  [local(): got_rows = lax.all_to_all(sent_rows, 'blk', split_axis=0, concat_axis=0)]
    ppermute x4, waiting for transfers between devices: 22.3 us -> 38.4 us  [groups(): return lax.ppermute(piece, 'groups', [(0, 1), (1, 0)])]
    ppermute x10, starting transfers between devices: 19.4 us -> 5.74 us  [over(): return lax.ppermute(piece, 'blk', [(i, i ^ bit) for i in range(count)])]
    ppermute x10, waiting for transfers between devices: 32.1 us -> 21.9 us  [over(): return lax.ppermute(piece, 'blk', [(i, i ^ bit) for i in range(count)])]
    ppermute x14, waiting for transfers between devices: 7.55 us -> 17.3 us  [moved(): lax.ppermute(value, 'blk', [(i, (i + steps) % count) for i in range(count)])]
    ppermute x14, starting transfers between devices: 40.2 us -> 48.8 us  [moved(): lax.ppermute(value, 'blk', [(i, (i + steps) % count) for i in range(count)])]
    all_to_all x1, starting transfers between devices: 9.14 us -> 3.68 us  [local(): got_rows = lax.all_to_all(sent_rows, 'blk', split_axis=0, concat_axis=0)]
    all_to_all x1, starting transfers between devices: 12.8 us -> 18.2 us  [to_all(): return lax.all_to_all(copies, 'blk', split_axis=0, concat_axis=0)]
  transfers between devices with their start and end apart: 33 -> 33, of which waited for: 8 -> 7; matrix products, arithmetic and copies ran while one was open for 11% -> 11% of each run, Pallas kernels for 17% -> 17%
where the time goes in v17:
time: 299 us; the launch traced here: 297 us
  starting transfers between devices  99.1 us (33%)
  waiting for transfers between devices  82 us (27%)
  Pallas kernels  51.3 us (17%)
  between operations  24.9 us (8%)
  local copies, waits for them, and re-layouts  19.7 us (7%)
  other arithmetic  15.3 us (5%)
  matrix products  4.72 us (2%)
    ppermute x14, starting transfers between devices, moved(): lax.ppermute(value, 'blk', [(i, (i + steps) % count) for i in range(count)])  48.8 us
    ppermute x4, waiting for transfers between devices, groups(): return lax.ppermute(piece, 'groups', [(0, 1), (1, 0)])  38.4 us
    pallas_call x4, Pallas kernels, write_quarter(): pl.pallas_call(quarter_kernel, grid_spec=pltpu.PrefetchScalarGridSpec(num...  28.7 us
    ppermute x10, waiting for transfers between devices, over(): return lax.ppermute(piece, 'blk', [(i, i ^ bit) for i in range(count)])  21.9 us
    all_to_all x1, starting transfers between devices, to_all(): return lax.all_to_all(copies, 'blk', split_axis=0, concat_axis=0)  18.2 us
    ppermute x14, waiting for transfers between devices, moved(): lax.ppermute(value, 'blk', [(i, (i + steps) % count) for i in range(count)])  17.3 us
    pallas_call x1, Pallas kernels, local(): shares = hidden_call(received, received, rows_all, place_all, starts)  8.75 us
    pallas_call x1, Pallas kernels, local(): down_f = down_call(received, grad_all, rows_all, place_all, starts)  6.77 us
  transfers between devices with their start and end apart: 33, of which 7 were waited for; matrix products, arithmetic and copies ran while one was open for 11% of the time, Pallas kernels for 17%

profile of v17, /device:TPU:1, one launch (start us, length us, event | category | flops | bytes accessed | tf_op | source)
XLA Modules:
  0.0 297.1 jit_solution(7168285044568567924)
XLA Ops:
  0.6 1.1 constant_dynamic-slice_fusion
  1.7 2.2 collective-permute-start.3
  3.9 2.3 collective-permute-start.4
  6.2 1.1 collective-permute-start.5
  7.7 1.4 fusion.20
  14.0 2.9 collective-permute-start.2
  19.5 5.3 %collective-permute-done.4 = bf16[128,1024]{1,0:T(8,128)(2,1)S(1)} collective-permute-done((bf16[128,1024]{1,0:T(8,128)(2,1)S(1)}, bf16[128,1024]{1,0:T(8,128)(2,1)S(1)}, u32[]{:S(2)}, u32[]{:S(2)}) %collective-permute-start.4) | collective-permute-done | bytes 262176 | tf_op jit(solution)/shard_map/ppermute | solution.py:21
  24.7 2.3 collective-permute-start.6
  27.1 15.4 %collective-permute-start.7 = (bf16[16,9216]{1,0:T(8,128)(2,1)S(1)}, bf16[16,9216]{1,0:T(8,128)(2,1)S(1)}, u32[]{:S(2)}, u32[]{:S(2)}) collective-permute-start(bf16[16,9216]{1,0:T(8,128)(2,1)S(1)} %pad_maximum_fusion.4), channel_id=1, source_target_pairs={{0,3},{1,4},{2,5},{3,6},{4,7},{5,8},{6,9},{7,10},{8,11},{9,12},{10... | collective-permute-start | bytes 884744 | tf_op jit(solution)/shard_map/ppermute | solution.py:21
  42.5 1.5 collective-permute-start.8
  43.9 12.0 %collective-permute-done.1 = bf16[128,1024]{1,0:T(8,128)(2,1)S(1)} collective-permute-done((bf16[128,1024]{1,0:T(8,128)(2,1)S(1)}, bf16[128,1024]{1,0:T(8,128)(2,1)S(1)}, u32[]{:S(2)}, u32[]{:S(2)}) %collective-permute-start.1) | collective-permute-done | bytes 262176 | tf_op jit(solution)/shard_map/ppermute | solution.py:21
  56.0 14.3 %collective-permute-start.9 = (bf16[16,9216]{1,0:T(8,128)(2,1)S(1)}, bf16[16,9216]{1,0:T(8,128)(2,1)S(1)}, u32[]{:S(2)}, u32[]{:S(2)}) collective-permute-start(bf16[16,9216]{1,0:T(8,128)(2,1)S(1)} %pad_maximum_fusion.4), channel_id=1, source_target_pairs={{0,1},{1,2},{2,3},{3,4},{4,5},{5,6},{6,7},{7,8},{8,9},{9,10},{10,1... | collective-permute-start | bytes 884744 | tf_op jit(solution)/shard_map/ppermute | solution.py:21
  70.9 2.6 shard_map.94.refs_0_
  73.4 1.1 pad_maximum_fusion.1.refs_2_.rest_1_
  74.5 2.1 pad_maximum_fusion.refs_1_.rest_0_
  77.4 3.7 %all-to-all-start = ((bf16[16,64,512]{2,1,0:T(8,128)(2,1)}), bf16[16,64,512]{2,1,0:T(8,128)(2,1)S(1)}, u32[]{:S(2)}, u32[]{:S(2)}) async-start(bf16[16,64,512]{2,1,0:T(8,128)(2,1)} %shard_map.95), calls=%async_computation | async-start | bytes 2097152 | tf_op jit(solution)/shard_map/all_to_all | solution.py:458
  81.1 1.3 collective-permute-start.10
  83.3 4.5 %shard_map.96.refs_0_ = bf16[16,240,512]{2,1,0:T(8,128)(2,1)} custom-call(bf16[192,8192]{1,0:T(8,128)(2,1)} %act.1, bf16[48,8192]{1,0:T(8,128)(2,1)} %bitcast.104), custom_call_target="tpu_custom_call" | custom-call | bytes 7864320 | tf_op jit(solution)/shard_map/pallas_call | solution.py:271
  87.8 18.6 %collective-permute-done.10.refs_2_.rest_2_ = bf16[4,128,1024]{2,1,0:T(8,128)(2,1)} collective-permute-done((bf16[4,128,1024]{2,1,0:T(8,128)(2,1)S(1)}, bf16[4,128,1024]{2,1,0:T(8,128)(2,1)}, u32[]{:S(2)}, u32[]{:S(2)}) %collective-permute-start.10) | collective-permute-done | bytes 1048608 | tf_op jit(solution)/shard_map/ppermute | solution.py:94
  106.4 10.3 %collective-permute-done.11.refs_3_.rest_0_ = bf16[4,128,1024]{2,1,0:T(8,128)(2,1)S(1)} collective-permute-done((bf16[4,128,1024]{2,1,0:T(8,128)(2,1)S(1)}, bf16[4,128,1024]{2,1,0:T(8,128)(2,1)S(1)}, u32[]{:S(2)}, u32[]{:S(2)}) %collective-permute-start.11) | collective-permute-done | bytes 1048608 | tf_op jit(solution)/shard_map/ppermute | solution.py:91
  116.7 1.1 copy-done.4
  118.7 5.6 %all-to-all-start.1 = ((bf16[16,240,512]{2,1,0:T(8,128)(2,1)}), bf16[16,240,512]{2,1,0:T(8,128)(2,1)}, u32[]{:S(2)}, u32[]{:S(2)}) async-start(bf16[16,240,512]{2,1,0:T(8,128)(2,1)} %shard_map.97), calls=%async_computation.1 | async-start | bytes 7864320 | tf_op jit(solution)/shard_map/all_to_all | solution.py:487
  134.8 1.2 collective-permute-start.15
  136.6 1.5 collective-permute-start.18
  139.9 19.8 %collective-permute-done.15.rest_3_ = bf16[4,128,1024]{2,1,0:T(8,128)(2,1)} collective-permute-done((bf16[4,128,1024]{2,1,0:T(8,128)(2,1)}, bf16[4,128,1024]{2,1,0:T(8,128)(2,1)}, u32[]{:S(2)}, u32[]{:S(2)}) %collective-permute-start.15) | collective-permute-done | bytes 1048608 | tf_op jit(solution)/shard_map/ppermute | solution.py:94
  163.2 1.2 fusion.1
  166.2 1.4 add.275.refs_0_
  169.2 1.5 convolution_convert_fusion.1
  171.2 1.3 collective-permute-start.20
  172.5 11.7 %collective-permute-done.18.rest_1_ = bf16[4,128,1024]{2,1,0:T(8,128)(2,1)} collective-permute-done((bf16[4,128,1024]{2,1,0:T(8,128)(2,1)}, bf16[4,128,1024]{2,1,0:T(8,128)(2,1)}, u32[]{:S(2)}, u32[]{:S(2)}) %collective-permute-start.18) | collective-permute-done | bytes 1048608 | tf_op jit(solution)/shard_map/ppermute | solution.py:91
  184.2 1.2 collective-permute-start.22
  185.4 1.0 pad_maximum_fusion.2.cot
  186.4 7.1 %shard_map.99 = (bf16[384,8192]{1,0:T(8,128)(2,1)}, f32[8,128]{1,0:T(8,128)}) custom-call(s32[5]{0:T(128)} %pad_add_fusion.2.where, bf16[384,1024]{1,0:T(8,128)(2,1)} %pad_maximum_fusion.2.cot, bf16[384,16]{1,0:T(8,128)(2,1)} %copy.41.grad.refs_0_, bf16[48,8192]{1,0:T(8,128)(2,1)} %pad_maximum_fusion.3.down, ...), custom_call_target="tpu_custom_call" | custom-call | flops 1610612736 | bytes 5767168 | tf_op jit(solution)/shard_map/pallas_call | solution.py:154
  193.5 4.4 %all-to-all-done.1.refs_1_.act.maps = bf16[16,240,512]{2,1,0:T(8,128)(2,1)} async-done(((bf16[16,240,512]{2,1,0:T(8,128)(2,1)}), bf16[16,240,512]{2,1,0:T(8,128)(2,1)}, u32[]{:S(2)}, u32[]{:S(2)}) %all-to-all-start.1) | async-done | bytes 3932192 | tf_op jit(solution)/shard_map/all_to_all | solution.py:487
  197.9 1.4 broadcast_in_dim.120
  199.3 18.2 %all-to-all-start.2 = ((bf16[16,24,256]{2,1,0:T(8,128)(2,1)}), bf16[16,24,256]{2,1,0:T(8,128)(2,1)S(1)}, u32[]{:S(2)}, u32[]{:S(2)}) async-start(bf16[16,24,256]{2,1,0:T(8,128)(2,1)} %broadcast_in_dim.120), calls=%async_computation.2 | async-start | bytes 393216 | tf_op jit(solution)/shard_map/all_to_all | solution.py:27
  217.5 7.1 %shard_map.100 = (bf16[384,8192]{1,0:T(8,128)(2,1)}, f32[8,128]{1,0:T(8,128)}) custom-call(s32[5]{0:T(128)} %pad_add_fusion.1.where, bf16[384,1024]{1,0:T(8,128)(2,1)} %pad_maximum_fusion.2.cot, bf16[384,16]{1,0:T(8,128)(2,1)} %copy.41.grad.refs_0_, bf16[48,8192]{1,0:T(8,128)(2,1)} %pad_maximum_fusion.3.down, ...), custom_call_target="tpu_custom_call", output_to_operand_aliasing={{0}: (8, {})} | custom-call | flops 1610612736 | bytes 5767168 | tf_op jit(solution)/shard_map/pallas_call | solution.py:154
  224.7 8.7 %shard_map.102.refs_1_ = f32[256,384]{1,0:T(8,128)} custom-call(bf16[16,240,512]{2,1,0:T(8,128)(2,1)} %all-to-all-done.1.refs_1_.act.maps, bf16[16,240,512]{2,1,0:T(8,128)(2,1)} %all-to-all-done.1.refs_1_.act.maps, s32[1,3072]{1,0:T(1,128)} %reshape.318.rows.refs_0_, s32[1,3072]{1,0:T(1,128)} %shard_map.101.spots, s32[32,1]{1,0:T(8,128)} %copy.46.starts), custom_call_target="tpu_custom_call" | custom-call | flops 2415919104 | bytes 3145728 | tf_op jit(solution)/shard_map/pallas_call | solution.py:524
  233.4 1.9 copy.49
  235.3 6.0 %all-to-all-start.4 = ((f32[16,24,256]{2,1,0:T(8,128)}), f32[16,24,256]{2,1,0:T(8,128)S(1)}, u32[]{:S(2)}, u32[]{:S(2)}) async-start(f32[16,24,256]{2,1,0:T(8,128)} %bitcast.42), calls=%async_computation.4 | async-start | bytes 786432 | tf_op jit(solution)/shard_map/all_to_all | solution.py:528
  257.3 6.8 %shard_map.104.refs_1_ = bf16[768,512]{1,0:T(8,128)(2,1)} custom-call(bf16[16,240,512]{2,1,0:T(8,128)(2,1)} %all-to-all-done.1.refs_1_.act.maps, bf16[256,384]{1,0:T(8,128)(2,1)} %bitcast.123, s32[1,3072]{1,0:T(1,128)} %shard_map.103.rows, s32[1,3072]{1,0:T(1,128)} %shard_map.101.spots, s32[32,1]{1,0:T(8,128)} %copy.46.starts), custom_call_target="tpu_custom_call" | custom-call | flops 2415919104 | bytes 3145728 | tf_op jit(solution)/shard_map/pallas_call | solution.py:526
  264.1 6.0 %all-to-all-start.3 = ((bf16[16,48,512]{2,1,0:T(8,128)(2,1)}), bf16[16,48,512]{2,1,0:T(8,128)(2,1)S(1)}, u32[]{:S(2)}, u32[]{:S(2)}) async-start(bf16[16,48,512]{2,1,0:T(8,128)(2,1)} %bitcast.111), calls=%async_computation.3 | async-start | bytes 1572864 | tf_op jit(solution)/shard_map/all_to_all | solution.py:531
  270.1 7.3 %shard_map.106 = (bf16[384,8192]{1,0:T(8,128)(2,1)}, f32[8,128]{1,0:T(8,128)}) custom-call(s32[5]{0:T(128)} %pad_add_fusion.3.where, bf16[384,1024]{1,0:T(8,128)(2,1)} %pad_maximum_fusion.2.cot, bf16[384,16]{1,0:T(8,128)(2,1)} %shard_map.105.grad, bf16[48,8192]{1,0:T(8,128)(2,1)} %pad_maximum_fusion.3.down, ...), custom_call_target="tpu_custom_call", output_to_operand_aliasing={{0}: (8, {})} | custom-call | flops 1610612736 | bytes 5767168 | tf_op jit(solution)/shard_map/pallas_call | solution.py:154
  278.3 1.9 select_add_fusion.1
  280.3 4.3 %collective-permute-start.25 = (f32[16,1024]{1,0:T(8,128)S(1)}, f32[16,1024]{1,0:T(8,128)S(1)}, u32[]{:S(2)}, u32[]{:S(2)}) collective-permute-start(f32[16,1024]{1,0:T(8,128)S(1)} %get-tuple-element.20), channel_id=1, source_target_pairs={{0,14},{1,15},{2,0},{3,1},{4,2},{5,3},{6,4},{7,5},{8,6},{9,7},{10,... | collective-permute-start | bytes 196616 | tf_op jit(solution)/shard_map/ppermute | solution.py:21
  284.6 1.7 collective-permute-start.26
  286.6 7.1 %shard_map.107 = (bf16[384,8192]{1,0:T(8,128)(2,1)}, f32[8,128]{1,0:T(8,128)}) custom-call(s32[5]{0:T(128)} %pad_add_fusion.where, bf16[384,1024]{1,0:T(8,128)(2,1)} %pad_maximum_fusion.2.cot, bf16[384,16]{1,0:T(8,128)(2,1)} %shard_map.105.grad, bf16[48,8192]{1,0:T(8,128)(2,1)} %pad_maximum_fusion.3.down, ...), custom_call_target="tpu_custom_call", output_to_operand_aliasing={{0}: (8, {})} | custom-call | flops 1610612736 | bytes 5767168 | tf_op jit(solution)/shard_map/pallas_call | solution.py:154
  295.7 1.4 reshape.317
  (134 shorter events, 26.6 us)
Async XLA Ops:
  0.6 69.7 %copy-start.16 = (s32[192]{0:T(256)S(1)}, s32[192]{0:T(256)}, u32[]{:S(2)}) copy-start(s32[192]{0:T(256)} %param.9) | copy-start | bytes 2308
  1.7 12.3 %collective-permute-start.3 = (bf16[128,1024]{1,0:T(8,128)(2,1)S(1)}, bf16[128,1024]{1,0:T(8,128)(2,1)S(1)}, u32[]{:S(2)}, u32[]{:S(2)}) collective-permute-start(bf16[128,1024]{1,0:T(8,128)(2,1)S(1)} %get-tuple-element.38), channel_id=1, source_target_pairs={{0,4},{1,5},{2,6},{3,7},{4,8},{5,9},{6,10},{7,11},{8,12},{9,13},{1... | collective-permute-start | bytes 786440 | tf_op jit(solution)/shard_map/ppermute | solution.py:21
  3.9 20.8 %collective-permute-start.4 = (bf16[128,1024]{1,0:T(8,128)(2,1)S(1)}, bf16[128,1024]{1,0:T(8,128)(2,1)S(1)}, u32[]{:S(2)}, u32[]{:S(2)}) collective-permute-start(bf16[128,1024]{1,0:T(8,128)(2,1)S(1)} %get-tuple-element.38), channel_id=1, source_target_pairs={{0,8},{1,9},{2,10},{3,11},{4,12},{5,13},{6,14},{7,15},{8,0},{9,1},... | collective-permute-start | bytes 786440 | tf_op jit(solution)/shard_map/ppermute | solution.py:21
  6.2 20.9 %collective-permute-start.5 = (bf16[128,1024]{1,0:T(8,128)(2,1)S(1)}, bf16[128,1024]{1,0:T(8,128)(2,1)S(1)}, u32[]{:S(2)}, u32[]{:S(2)}) collective-permute-start(bf16[128,1024]{1,0:T(8,128)(2,1)S(1)} %get-tuple-element.38), channel_id=1, source_target_pairs={{0,12},{1,13},{2,14},{3,15},{4,0},{5,1},{6,2},{7,3},{8,4},{9,5},{1... | collective-permute-start | bytes 786440 | tf_op jit(solution)/shard_map/ppermute | solution.py:21
  7.3 35.2 %collective-permute-start = (bf16[128,1024]{1,0:T(8,128)(2,1)S(1)}, bf16[128,1024]{1,0:T(8,128)(2,1)S(1)}, u32[]{:S(2)}, u32[]{:S(2)}) collective-permute-start(bf16[128,1024]{1,0:T(8,128)(2,1)S(1)} %get-tuple-element.39), channel_id=1, source_target_pairs={{0,4},{1,5},{2,6},{3,7},{4,8},{5,9},{6,10},{7,11},{8,12},{9,13},{1... | collective-permute-start | bytes 786440 | tf_op jit(solution)/shard_map/ppermute | solution.py:21
  7.7 48.3 %collective-permute-start.1 = (bf16[128,1024]{1,0:T(8,128)(2,1)S(1)}, bf16[128,1024]{1,0:T(8,128)(2,1)S(1)}, u32[]{:S(2)}, u32[]{:S(2)}) collective-permute-start(bf16[128,1024]{1,0:T(8,128)(2,1)S(1)} %get-tuple-element.39), channel_id=1, source_target_pairs={{0,8},{1,9},{2,10},{3,11},{4,12},{5,13},{6,14},{7,15},{8,0},{9,1},... | collective-permute-start | bytes 786440 | tf_op jit(solution)/shard_map/ppermute | solution.py:21
  14.0 60.5 %collective-permute-start.2 = (bf16[128,1024]{1,0:T(8,128)(2,1)S(1)}, bf16[128,1024]{1,0:T(8,128)(2,1)}, u32[]{:S(2)}, u32[]{:S(2)}) collective-permute-start(bf16[128,1024]{1,0:T(8,128)(2,1)S(1)} %get-tuple-element.39), channel_id=1, source_target_pairs={{0,12},{1,13},{2,14},{3,15},{4,0},{5,1},{6,2},{7,3},{8,4},{9,5},{1... | collective-permute-start | bytes 786440 | tf_op jit(solution)/shard_map/ppermute | solution.py:21
  24.7 51.9 %collective-permute-start.6 = (bf16[16,9216]{1,0:T(8,128)(2,1)S(1)}, bf16[16,9216]{1,0:T(8,128)(2,1)S(1)}, u32[]{:S(2)}, u32[]{:S(2)}) collective-permute-start(bf16[16,9216]{1,0:T(8,128)(2,1)S(1)} %pad_maximum_fusion.4), channel_id=1, source_target_pairs={{0,4},{1,5},{2,6},{3,7},{4,8},{5,9},{6,10},{7,11},{8,12},{9,13},{1... | collective-permute-start | bytes 884744 | tf_op jit(solution)/shard_map/ppermute | solution.py:21
  27.1 49.5 %collective-permute-start.7 = (bf16[16,9216]{1,0:T(8,128)(2,1)S(1)}, bf16[16,9216]{1,0:T(8,128)(2,1)S(1)}, u32[]{:S(2)}, u32[]{:S(2)}) collective-permute-start(bf16[16,9216]{1,0:T(8,128)(2,1)S(1)} %pad_maximum_fusion.4), channel_id=1, source_target_pairs={{0,3},{1,4},{2,5},{3,6},{4,7},{5,8},{6,9},{7,10},{8,11},{9,12},{10... | collective-permute-start | bytes 884744 | tf_op jit(solution)/shard_map/ppermute | solution.py:21
  42.5 34.1 %collective-permute-start.8 = (bf16[16,9216]{1,0:T(8,128)(2,1)S(1)}, bf16[16,9216]{1,0:T(8,128)(2,1)S(1)}, u32[]{:S(2)}, u32[]{:S(2)}) collective-permute-start(bf16[16,9216]{1,0:T(8,128)(2,1)S(1)} %pad_maximum_fusion.4), channel_id=1, source_target_pairs={{0,2},{1,3},{2,4},{3,5},{4,6},{5,7},{6,8},{7,9},{8,10},{9,11},{10,... | collective-permute-start | bytes 884744 | tf_op jit(solution)/shard_map/ppermute | solution.py:21
  56.0 20.6 %collective-permute-start.9 = (bf16[16,9216]{1,0:T(8,128)(2,1)S(1)}, bf16[16,9216]{1,0:T(8,128)(2,1)S(1)}, u32[]{:S(2)}, u32[]{:S(2)}) collective-permute-start(bf16[16,9216]{1,0:T(8,128)(2,1)S(1)} %pad_maximum_fusion.4), channel_id=1, source_target_pairs={{0,1},{1,2},{2,3},{3,4},{4,5},{5,6},{6,7},{7,8},{8,9},{9,10},{10,1... | collective-permute-start | bytes 884744 | tf_op jit(solution)/shard_map/ppermute | solution.py:21
  77.4 3.7 %copy-start.3 = (bf16[4,128,1024]{2,1,0:T(8,128)(2,1)S(1)}, bf16[4,128,1024]{2,1,0:T(8,128)(2,1)}, u32[]{:S(2)}) copy-start(bf16[4,128,1024]{2,1,0:T(8,128)(2,1)} %pad_maximum_fusion.refs_1_.rest_0_) | copy-start | bytes 3145732
  77.4 39.3 %all-to-all-start = ((bf16[16,64,512]{2,1,0:T(8,128)(2,1)}), bf16[16,64,512]{2,1,0:T(8,128)(2,1)S(1)}, u32[]{:S(2)}, u32[]{:S(2)}) async-start(bf16[16,64,512]{2,1,0:T(8,128)(2,1)} %shard_map.95), calls=%async_computation | async-start | bytes 2097152 | tf_op jit(solution)/shard_map/all_to_all | solution.py:458
  81.1 25.3 %collective-permute-start.10 = (bf16[4,128,1024]{2,1,0:T(8,128)(2,1)S(1)}, bf16[4,128,1024]{2,1,0:T(8,128)(2,1)}, u32[]{:S(2)}, u32[]{:S(2)}) collective-permute-start(bf16[4,128,1024]{2,1,0:T(8,128)(2,1)S(1)} %copy-done.3), channel_id=1, source_target_pairs={{0,16},{16,0},{1,17},{17,1},{2,18},{18,2},{3,19},{19,3},{4,20},{20... | collective-permute-start | bytes 3145736 | tf_op jit(solution)/shard_map/ppermute | solution.py:94
  82.4 34.2 %collective-permute-start.11 = (bf16[4,128,1024]{2,1,0:T(8,128)(2,1)S(1)}, bf16[4,128,1024]{2,1,0:T(8,128)(2,1)S(1)}, u32[]{:S(2)}, u32[]{:S(2)}) collective-permute-start(bf16[4,128,1024]{2,1,0:T(8,128)(2,1)S(1)} %copy-done.3), channel_id=1, source_target_pairs={{0,2},{1,3},{2,0},{3,1},{4,6},{5,7},{6,4},{7,5},{8,10},{9,11},{10,... | collective-permute-start | bytes 3145736 | tf_op jit(solution)/shard_map/ppermute | solution.py:91
  116.6 1.1 copy-start.4
  117.7 1.0 copy-start
  118.7 19.4 %copy-start.2 = (bf16[3,16,8192]{2,1,0:T(8,128)(2,1)S(1)}, bf16[3,16,8192]{2,1,0:T(8,128)(2,1)}, u32[]{:S(2)}) copy-start(bf16[3,16,8192]{2,1,0:T(8,128)(2,1)} %param.12) | copy-start | bytes 2359300
  118.7 19.4 %copy-start.8 = (bf16[16,9216]{1,0:T(8,128)(2,1)S(1)}, bf16[16,9216]{1,0:T(8,128)(2,1)}, u32[]{:S(2)}) copy-start(bf16[16,9216]{1,0:T(8,128)(2,1)} %select_select_fusion.refs_3_) | copy-start | bytes 884740
  118.7 79.2 %all-to-all-start.1 = ((bf16[16,240,512]{2,1,0:T(8,128)(2,1)}), bf16[16,240,512]{2,1,0:T(8,128)(2,1)}, u32[]{:S(2)}, u32[]{:S(2)}) async-start(bf16[16,240,512]{2,1,0:T(8,128)(2,1)} %shard_map.97), calls=%async_computation.1 | async-start | bytes 7864320 | tf_op jit(solution)/shard_map/all_to_all | solution.py:487
  124.2 13.9 %copy-start.10 = (bf16[3,16,1024]{2,1,0:T(8,128)(2,1)S(1)}, bf16[3,16,1024]{2,1,0:T(8,128)(2,1)}, u32[]{:S(2)}) copy-start(bf16[3,16,1024]{2,1,0:T(8,128)(2,1)} %param.13) | copy-start | bytes 294916
  134.8 25.9 %copy-start.1 = (bf16[16,64,512]{2,1,0:T(8,128)(2,1)S(1)}, bf16[16,64,512]{2,1,0:T(8,128)(2,1)}, u32[]{:S(2)}) copy-start(bf16[16,64,512]{2,1,0:T(8,128)(2,1)} %copy-done) | copy-start | bytes 3145732
  134.8 24.9 %collective-permute-start.15 = (bf16[4,128,1024]{2,1,0:T(8,128)(2,1)}, bf16[4,128,1024]{2,1,0:T(8,128)(2,1)}, u32[]{:S(2)}, u32[]{:S(2)}) collective-permute-start(bf16[4,128,1024]{2,1,0:T(8,128)(2,1)} %pad_maximum_fusion.1.refs_2_.rest_1_), channel_id=1, source_target_pairs={{0,16},{16,0},{1,17},{17,1},{2,18},{18,2},{3,19},{19,3},{4,20},{20... | collective-permute-start | bytes 3145736 | tf_op jit(solution)/shard_map/ppermute | solution.py:94
  136.1 35.1 %collective-permute-start.13 = (bf16[4,128,1024]{2,1,0:T(8,128)(2,1)}, bf16[4,128,1024]{2,1,0:T(8,128)(2,1)}, u32[]{:S(2)}, u32[]{:S(2)}) collective-permute-start(bf16[4,128,1024]{2,1,0:T(8,128)(2,1)} %pad_maximum_fusion.1.refs_2_.rest_1_), channel_id=1, source_target_pairs={{0,1},{1,0},{2,3},{3,2},{4,5},{5,4},{6,7},{7,6},{8,9},{9,8},{10,11... | collective-permute-start | bytes 3145736 | tf_op jit(solution)/shard_map/ppermute | solution.py:91
  136.5 81.0 %collective-permute-start.12 = (bf16[4,128,1024]{2,1,0:T(8,128)(2,1)S(1)}, bf16[4,128,1024]{2,1,0:T(8,128)(2,1)}, u32[]{:S(2)}, u32[]{:S(2)}) collective-permute-start(bf16[4,128,1024]{2,1,0:T(8,128)(2,1)S(1)} %copy-done.3), channel_id=1, source_target_pairs={{0,1},{1,0},{2,3},{3,2},{4,5},{5,4},{6,7},{7,6},{8,9},{9,8},{10,11... | collective-permute-start | bytes 3145736 | tf_op jit(solution)/shard_map/ppermute | solution.py:91
  136.6 47.6 %collective-permute-start.18 = (bf16[4,128,1024]{2,1,0:T(8,128)(2,1)}, bf16[4,128,1024]{2,1,0:T(8,128)(2,1)}, u32[]{:S(2)}, u32[]{:S(2)}) collective-permute-start(bf16[4,128,1024]{2,1,0:T(8,128)(2,1)} %pad_maximum_fusion.1.refs_2_.rest_1_), channel_id=1, source_target_pairs={{0,2},{1,3},{2,0},{3,1},{4,6},{5,7},{6,4},{7,5},{8,10},{9,11},{10,... | collective-permute-start | bytes 3145736 | tf_op jit(solution)/shard_map/ppermute | solution.py:91
  138.2 23.9 %copy-start.9 = (bf16[48,1024]{1,0:T(8,128)(2,1)}, bf16[48,1024]{1,0:T(8,128)(2,1)S(1)}, u32[]{:S(2)}) copy-start(bf16[48,1024]{1,0:T(8,128)(2,1)S(1)} %pad_maximum_fusion.6) | copy-start | bytes 294916
  139.2 78.3 %collective-permute-start.14 = (bf16[4,128,1024]{2,1,0:T(8,128)(2,1)}, bf16[4,128,1024]{2,1,0:T(8,128)(2,1)}, u32[]{:S(2)}, u32[]{:S(2)}) collective-permute-start(bf16[4,128,1024]{2,1,0:T(8,128)(2,1)} %collective-permute-done.10.refs_2_.rest_2_), channel_id=1, source_target_pairs={{0,1},{1,0},{2,3},{3,2},{4,5},{5,4},{6,7},{7,6},{8,9},{9,8},{10,11... | collective-permute-start | bytes 3145736 | tf_op jit(solution)/shard_map/ppermute | solution.py:91
  159.7 57.8 %collective-permute-start.16 = (bf16[4,128,1024]{2,1,0:T(8,128)(2,1)}, bf16[4,128,1024]{2,1,0:T(8,128)(2,1)}, u32[]{:S(2)}, u32[]{:S(2)}) collective-permute-start(bf16[4,128,1024]{2,1,0:T(8,128)(2,1)} %collective-permute-done.15.rest_3_), channel_id=1, source_target_pairs={{0,1},{1,0},{2,3},{3,2},{4,5},{5,4},{6,7},{7,6},{8,9},{9,8},{10,11... | collective-permute-start | bytes 3145736 | tf_op jit(solution)/shard_map/ppermute | solution.py:91
  162.0 2.3 copy-start.11
  163.1 7.6 %copy-start.14 = (s32[384]{0:T(512)S(1)}, s32[384]{0:T(512)}, u32[]{:S(2)}) copy-start(s32[384]{0:T(512)} %copy-done.13) | copy-start | bytes 4612
  163.1 8.1 %copy-start.5 = (bf16[4,128,1024]{2,1,0:T(8,128)(2,1)S(1)}, bf16[4,128,1024]{2,1,0:T(8,128)(2,1)}, u32[]{:S(2)}) copy-start(bf16[4,128,1024]{2,1,0:T(8,128)(2,1)} %copy-done.4) | copy-start | bytes 3145732
  171.2 84.2 %collective-permute-start.20 = (bf16[4,128,1024]{2,1,0:T(8,128)(2,1)S(1)}, bf16[4,128,1024]{2,1,0:T(8,128)(2,1)}, u32[]{:S(2)}, u32[]{:S(2)}) collective-permute-start(bf16[4,128,1024]{2,1,0:T(8,128)(2,1)S(1)} %copy-done.5), channel_id=1, source_target_pairs={{0,16},{16,0},{1,17},{17,1},{2,18},{18,2},{3,19},{19,3},{4,20},{20... | collective-permute-start | bytes 3145736 | tf_op jit(solution)/shard_map/ppermute | solution.py:94
  184.2 71.3 %collective-permute-start.22 = (bf16[4,128,1024]{2,1,0:T(8,128)(2,1)}, bf16[4,128,1024]{2,1,0:T(8,128)(2,1)}, u32[]{:S(2)}, u32[]{:S(2)}) collective-permute-start(bf16[4,128,1024]{2,1,0:T(8,128)(2,1)} %collective-permute-done.18.rest_1_), channel_id=1, source_target_pairs={{0,16},{16,0},{1,17},{17,1},{2,18},{18,2},{3,19},{19,3},{4,20},{20... | collective-permute-start | bytes 3145736 | tf_op jit(solution)/shard_map/ppermute | solution.py:94
  199.3 36.0 %all-to-all-start.2 = ((bf16[16,24,256]{2,1,0:T(8,128)(2,1)}), bf16[16,24,256]{2,1,0:T(8,128)(2,1)S(1)}, u32[]{:S(2)}, u32[]{:S(2)}) async-start(bf16[16,24,256]{2,1,0:T(8,128)(2,1)} %broadcast_in_dim.120), calls=%async_computation.2 | async-start | bytes 393216 | tf_op jit(solution)/shard_map/all_to_all | solution.py:27
  235.3 28.8 %all-to-all-start.4 = ((f32[16,24,256]{2,1,0:T(8,128)}), f32[16,24,256]{2,1,0:T(8,128)S(1)}, u32[]{:S(2)}, u32[]{:S(2)}) async-start(f32[16,24,256]{2,1,0:T(8,128)} %bitcast.42), calls=%async_computation.4 | async-start | bytes 786432 | tf_op jit(solution)/shard_map/all_to_all | solution.py:528
  254.8 25.5 %collective-permute-start.17 = (bf16[4,128,1024]{2,1,0:T(8,128)(2,1)S(1)}, bf16[4,128,1024]{2,1,0:T(8,128)(2,1)}, u32[]{:S(2)}, u32[]{:S(2)}) collective-permute-start(bf16[4,128,1024]{2,1,0:T(8,128)(2,1)S(1)} %copy-done.5), channel_id=1, source_target_pairs={{0,1},{1,0},{2,3},{3,2},{4,5},{5,4},{6,7},{7,6},{8,9},{9,8},{10,11... | collective-permute-start | bytes 3145736 | tf_op jit(solution)/shard_map/ppermute | solution.py:91
  255.0 29.7 %collective-permute-start.19 = (bf16[4,128,1024]{2,1,0:T(8,128)(2,1)}, bf16[4,128,1024]{2,1,0:T(8,128)(2,1)}, u32[]{:S(2)}, u32[]{:S(2)}) collective-permute-start(bf16[4,128,1024]{2,1,0:T(8,128)(2,1)} %collective-permute-done.18.rest_1_), channel_id=1, source_target_pairs={{0,1},{1,0},{2,3},{3,2},{4,5},{5,4},{6,7},{7,6},{8,9},{9,8},{10,11... | collective-permute-start | bytes 3145736 | tf_op jit(solution)/shard_map/ppermute | solution.py:91
  255.4 31.0 %collective-permute-start.21 = (bf16[4,128,1024]{2,1,0:T(8,128)(2,1)}, bf16[4,128,1024]{2,1,0:T(8,128)(2,1)}, u32[]{:S(2)}, u32[]{:S(2)}) collective-permute-start(bf16[4,128,1024]{2,1,0:T(8,128)(2,1)} %collective-permute-done.20.rest_2_), channel_id=1, source_target_pairs={{0,1},{1,0},{2,3},{3,2},{4,5},{5,4},{6,7},{7,6},{8,9},{9,8},{10,11... | collective-permute-start | bytes 3145736 | tf_op jit(solution)/shard_map/ppermute | solution.py:91
  255.5 31.1 %collective-permute-start.23 = (bf16[4,128,1024]{2,1,0:T(8,128)(2,1)}, bf16[4,128,1024]{2,1,0:T(8,128)(2,1)}, u32[]{:S(2)}, u32[]{:S(2)}) collective-permute-start(bf16[4,128,1024]{2,1,0:T(8,128)(2,1)} %collective-permute-done.22.rest_3_), channel_id=1, source_target_pairs={{0,1},{1,0},{2,3},{3,2},{4,5},{5,4},{6,7},{7,6},{8,9},{9,8},{10,11... | collective-permute-start | bytes 3145736 | tf_op jit(solution)/shard_map/ppermute | solution.py:91
  264.1 30.5 %all-to-all-start.3 = ((bf16[16,48,512]{2,1,0:T(8,128)(2,1)}), bf16[16,48,512]{2,1,0:T(8,128)(2,1)S(1)}, u32[]{:S(2)}, u32[]{:S(2)}) async-start(bf16[16,48,512]{2,1,0:T(8,128)(2,1)} %bitcast.111), calls=%async_computation.3 | async-start | bytes 1572864 | tf_op jit(solution)/shard_map/all_to_all | solution.py:531
  270.1 7.8 %copy-start.12 = (s32[384]{0:T(512)S(1)}, s32[384]{0:T(512)}, u32[]{:S(2)}) copy-start(s32[384]{0:T(512)} %copy-done.11) | copy-start | bytes 4612
  270.1 7.8 %copy-start.15 = (s32[48]{0:T(128)S(1)}, s32[48]{0:T(128)}, u32[]{:S(2)}) copy-start(s32[48]{0:T(128)} %and_select_fusion) | copy-start | bytes 580
  270.1 8.0 %copy-start.7 = (bf16[16,24,512]{2,1,0:T(8,128)(2,1)S(1)}, bf16[16,24,512]{2,1,0:T(8,128)(2,1)}, u32[]{:S(2)}) copy-start(bf16[16,24,512]{2,1,0:T(8,128)(2,1)} %copy-done.6) | copy-start | bytes 1179652
  280.1 13.6 %collective-permute-start.24 = (f32[16,1024]{1,0:T(8,128)S(1)}, f32[16,1024]{1,0:T(8,128)S(1)}, u32[]{:S(2)}, u32[]{:S(2)}) collective-permute-start(f32[16,1024]{1,0:T(8,128)S(1)} %get-tuple-element.20), channel_id=1, source_target_pairs={{0,15},{1,0},{2,1},{3,2},{4,3},{5,4},{6,5},{7,6},{8,7},{9,8},{10,9... | collective-permute-start | bytes 196616 | tf_op jit(solution)/shard_map/ppermute | solution.py:21
  280.3 13.4 %collective-permute-start.25 = (f32[16,1024]{1,0:T(8,128)S(1)}, f32[16,1024]{1,0:T(8,128)S(1)}, u32[]{:S(2)}, u32[]{:S(2)}) collective-permute-start(f32[16,1024]{1,0:T(8,128)S(1)} %get-tuple-element.20), channel_id=1, source_target_pairs={{0,14},{1,15},{2,0},{3,1},{4,2},{5,3},{6,4},{7,5},{8,6},{9,7},{10,... | collective-permute-start | bytes 196616 | tf_op jit(solution)/shard_map/ppermute | solution.py:21
  284.6 9.1 %collective-permute-start.26 = (f32[16,1024]{1,0:T(8,128)S(1)}, f32[16,1024]{1,0:T(8,128)S(1)}, u32[]{:S(2)}, u32[]{:S(2)}) collective-permute-start(f32[16,1024]{1,0:T(8,128)S(1)} %get-tuple-element.20), channel_id=1, source_target_pairs={{0,13},{1,14},{2,15},{3,0},{4,1},{5,2},{6,3},{7,4},{8,5},{9,6},{10... | collective-permute-start | bytes 196616 | tf_op jit(solution)/shard_map/ppermute | solution.py:21
  286.3 7.4 %collective-permute-start.27 = (f32[16,1024]{1,0:T(8,128)S(1)}, f32[16,1024]{1,0:T(8,128)S(1)}, u32[]{:S(2)}, u32[]{:S(2)}) collective-permute-start(f32[16,1024]{1,0:T(8,128)S(1)} %get-tuple-element.20), channel_id=1, source_target_pairs={{0,12},{1,13},{2,14},{3,15},{4,0},{5,1},{6,2},{7,3},{8,4},{9,5},{1... | collective-permute-start | bytes 196616 | tf_op jit(solution)/shard_map/ppermute | solution.py:21
  (2 other events, 1.3 us)

commit v18 on v17

--- a/solution.py
+++ b/solution.py
@@ -77,7 +77,7 @@
     count = lax.axis_size("blk")
     shards = jnp.arange(count // 4, dtype=jnp.int32)
     if near_lines(count):
-        return (lax.axis_index("blk") // 4 - shards) % (count // 4)
+        return lax.rem(lax.div(lax.axis_index("blk"), 4) + count // 4 - shards, count // 4)
     return shards
 
 
@@ -426,8 +426,14 @@
     first_block = device * resident
     block_numbers = first_block + jnp.arange(resident, dtype=jnp.int32)
     begin = starts_of(block_numbers, start_ids)
+    hops = jnp.arange(1, HOPS + 1, dtype=jnp.int32)
     is_local = (begin >= first_block) & (begin <= block_numbers)
     home_slot = jnp.clip(begin - first_block, 0, resident - 1)
+    own_slots = jnp.arange(resident, dtype=jnp.int32)
+    chosen_slot = is_local[:, None] & (home_slot[:, None] == own_slots[None, :])
+    others = lax.rem(device + hops, devices) * resident
+    to_me = lax.div(starts_of(others, start_ids), resident) == device
+    continues = begin[resident - 1] == first_block + own_slots
     last_map = jnp.concatenate(
         [
             lax.dynamic_index_in_dim(maps, home_slot[resident - 1], 0, keepdims=False)
@@ -435,17 +441,18 @@
         ],
         axis=1,
     )
+    homes = lax.rem(device + devices - hops, devices)
+    from_home = lax.div(begin[:1], resident) == homes
     carried = jnp.zeros_like(last_map)
     for step in range(1, HOPS + 1):
-        home = (device - step) % devices
-        carried = jnp.where(begin[0] // resident == home, moved(last_map, step), carried)
+        carried = jnp.where(from_home[step - 1], moved(last_map, step), carried)
 
     def of_blocks(maps, own):
         blocks = []
         for b in range(resident):
             chosen = own
             for k in range(b + 1):
-                chosen = jnp.where(is_local[b] & (home_slot[b] == k), maps[k], chosen)
+                chosen = jnp.where(chosen_slot[b, k], maps[k], chosen)
             blocks.append(chosen)
         return jnp.concatenate(blocks, axis=0)
 
@@ -483,7 +490,7 @@
 
     flat_maps = adapter_down_maps.reshape(share, width)
     received = pack_features(activations, flat_maps, devices)
-    received = after(received, got_rows, own[CHUNKS], across[0])
+    received = after(received, got_rows)
     received = lax.all_to_all(received, "blk", split_axis=0, concat_axis=0)
     grad_all = to_all(after(grad_sent, received)).reshape(resident_rows, -1).T
 
@@ -494,7 +501,7 @@
     )
     grad_rows = dot(arrange, grad_in, ((0,), (0,))).astype(jnp.bfloat16)
     group = lax.axis_index("groups")
-    quarter = device % 4
+    quarter = lax.rem(device, 4)
     firsts = [quarter, quarter ^ 1, quarter ^ 2, quarter ^ 3]
     if own[0].shape[1] % LANES == 0:
         out = None
@@ -539,14 +546,12 @@
     tail = sum(jnp.where(is_local[b], 0.0, up_parts[b]) for b in range(resident))
     far = jnp.zeros_like(tail)
     for step in range(1, HOPS + 1):
-        other = (device + step) % devices * resident
-        theirs = starts_of(other[None], start_ids)[0]
-        far = far + jnp.where(theirs // resident == device, moved(tail, -step), 0.0)
+        far = far + jnp.where(to_me[step - 1], moved(tail, -step), 0.0)
     up_grads = []
     for k in range(resident):
-        total = jnp.where(begin[resident - 1] == first_block + k, far, 0.0)
+        total = jnp.where(continues[k], far, 0.0)
         for b in range(resident):
-            total = total + jnp.where(is_local[b] & (home_slot[b] == k), up_parts[b], 0.0)
+            total = total + jnp.where(chosen_slot[b, k], up_parts[b], 0.0)
         up_grads.append(adapter_scale * total)
     up_map_gradient = jnp.stack(up_grads)
 

time: 299 us -> 304 us (1.017)
  between operations: 24.9 us -> 3.64 us
  waiting for transfers between devices: 82 us -> 103 us
  other arithmetic: 15.3 us -> 35.1 us
  starting transfers between devices: 99.1 us -> 88.3 us
    all_to_all x1, waiting for transfers between devices: 0.01 us -> 17.9 us  [local(): got_rows = lax.all_to_all(sent_rows, 'blk', split_axis=0, concat_axis=0)]
    all_to_all x1, starting transfers between devices: 18.2 us -> 5.72 us  [to_all(): return lax.all_to_all(copies, 'blk', split_axis=0, concat_axis=0)]
    ppermute x10, waiting for transfers between devices: 21.9 us -> 32.3 us  [over(): return lax.ppermute(piece, 'blk', [(i, i ^ bit) for i in range(count)])]
    select_n x3, other arithmetic: 0.86 us -> 11 us  [the longest x2 7.79 us: of_blocks(): chosen = jnp.where(chosen_slot[b, k], maps[k], chosen)]
    another operation x3, other arithmetic: 0.79 us -> 10.7 us  [local(): up_map_gradient = jnp.stack(up_grads)]
    all_to_all x1, starting transfers between devices: 3.68 us -> 11.2 us  [local(): got_rows = lax.all_to_all(sent_rows, 'blk', split_axis=0, concat_axis=0)]
    ppermute x4, waiting for transfers between devices: 38.4 us -> 31.9 us  [groups(): return lax.ppermute(piece, 'groups', [(0, 1), (1, 0)])]
    ppermute x14, starting transfers between devices: 48.8 us -> 43.5 us  [moved(): lax.ppermute(value, 'blk', [(i, (i + steps) % count) for i in range(count)])]
  transfers between devices with their start and end apart: 33 -> 33, of which waited for: 7 -> 9; matrix products, arithmetic and copies ran while one was open for 11% -> 16% of each run, Pallas kernels for 17% -> 17%
where the time goes in v18:
time: 304 us; the launch traced here: 302 us
  waiting for transfers between devices  103 us (34%)
  starting transfers between devices  88.3 us (29%)
  Pallas kernels  51.2 us (17%)
  other arithmetic  35.1 us (12%)
  local copies, waits for them, and re-layouts  19 us (6%)
  between operations  3.64 us (1%)
    ppermute x14, starting transfers between devices, moved(): lax.ppermute(value, 'blk', [(i, (i + steps) % count) for i in range(count)])  43.5 us
    ppermute x10, waiting for transfers between devices, over(): return lax.ppermute(piece, 'blk', [(i, i ^ bit) for i in range(count)])  32.3 us
    ppermute x4, waiting for transfers between devices, groups(): return lax.ppermute(piece, 'groups', [(0, 1), (1, 0)])  31.9 us
    pallas_call x4, Pallas kernels, write_quarter(): pl.pallas_call(quarter_kernel, grid_spec=pltpu.PrefetchScalarGridSpec(num...  28.5 us
    ppermute x14, waiting for transfers between devices, moved(): lax.ppermute(value, 'blk', [(i, (i + steps) % count) for i in range(count)])  19.7 us
    all_to_all x1, waiting for transfers between devices, local(): got_rows = lax.all_to_all(sent_rows, 'blk', split_axis=0, concat_axis=0)  17.9 us
    all_to_all x1, starting transfers between devices, local(): got_rows = lax.all_to_all(sent_rows, 'blk', split_axis=0, concat_axis=0)  11.2 us
    another operation x3, other arithmetic, local(): up_map_gradient = jnp.stack(up_grads)  10.7 us
  transfers between devices with their start and end apart: 33, of which 9 were waited for; matrix products, arithmetic and copies ran while one was open for 16% of the time, Pallas kernels for 17%

profile of v18, /device:TPU:1, one launch (start us, length us, event | category | flops | bytes accessed | tf_op | source)
XLA Modules:
  0.0 301.9 jit_solution(4759560137558437028)
XLA Ops:
  0.7 1.1 constant_dynamic-slice_fusion
  1.8 2.2 collective-permute-start.3
  3.9 2.3 collective-permute-start.4
  6.2 1.1 collective-permute-start.5
  7.8 1.3 fusion.35
  15.6 3.1 %collective-permute-start.6 = (bf16[16,9216]{1,0:T(8,128)(2,1)S(1)}, bf16[16,9216]{1,0:T(8,128)(2,1)S(1)}, u32[]{:S(2)}, u32[]{:S(2)}) collective-permute-start(bf16[16,9216]{1,0:T(8,128)(2,1)S(1)} %pad_maximum_fusion.4), channel_id=1, source_target_pairs={{0,4},{1,5},{2,6},{3,7},{4,8},{5,9},{6,10},{7,11},{8,12},{9,13},{1... | collective-permute-start | bytes 884744 | tf_op jit(solution)/shard_map/ppermute | solution.py:21
  18.7 6.0 %collective-permute-done.4 = bf16[128,1024]{1,0:T(8,128)(2,1)S(1)} collective-permute-done((bf16[128,1024]{1,0:T(8,128)(2,1)S(1)}, bf16[128,1024]{1,0:T(8,128)(2,1)S(1)}, u32[]{:S(2)}, u32[]{:S(2)}) %collective-permute-start.4) | collective-permute-done | bytes 262176 | tf_op jit(solution)/shard_map/ppermute | solution.py:21
  24.7 10.1 %collective-permute-start.7 = (bf16[16,9216]{1,0:T(8,128)(2,1)S(1)}, bf16[16,9216]{1,0:T(8,128)(2,1)S(1)}, u32[]{:S(2)}, u32[]{:S(2)}) collective-permute-start(bf16[16,9216]{1,0:T(8,128)(2,1)S(1)} %pad_maximum_fusion.4), channel_id=1, source_target_pairs={{0,3},{1,4},{2,5},{3,6},{4,7},{5,8},{6,9},{7,10},{8,11},{9,12},{10... | collective-permute-start | bytes 884744 | tf_op jit(solution)/shard_map/ppermute | solution.py:21
  34.8 1.2 collective-permute-start.8
  36.0 16.5 %collective-permute-start.9 = (bf16[16,9216]{1,0:T(8,128)(2,1)S(1)}, bf16[16,9216]{1,0:T(8,128)(2,1)S(1)}, u32[]{:S(2)}, u32[]{:S(2)}) collective-permute-start(bf16[16,9216]{1,0:T(8,128)(2,1)S(1)} %pad_maximum_fusion.4), channel_id=1, source_target_pairs={{0,1},{1,2},{2,3},{3,4},{4,5},{5,6},{6,7},{7,8},{8,9},{9,10},{10,1... | collective-permute-start | bytes 884744 | tf_op jit(solution)/shard_map/ppermute | solution.py:21
  52.6 3.4 %collective-permute-done.1 = bf16[128,1024]{1,0:T(8,128)(2,1)S(1)} collective-permute-done((bf16[128,1024]{1,0:T(8,128)(2,1)S(1)}, bf16[128,1024]{1,0:T(8,128)(2,1)S(1)}, u32[]{:S(2)}, u32[]{:S(2)}) %collective-permute-start.1) | collective-permute-done | bytes 262176 | tf_op jit(solution)/shard_map/ppermute | solution.py:21
  57.2 2.6 shard_map.94.refs_0_
  59.8 1.2 pad_maximum_fusion.1.refs_2_.rest_1_
  61.0 10.3 %collective-permute-done.2 = bf16[128,1024]{1,0:T(8,128)(2,1)S(1)} collective-permute-done((bf16[128,1024]{1,0:T(8,128)(2,1)S(1)}, bf16[128,1024]{1,0:T(8,128)(2,1)S(1)}, u32[]{:S(2)}, u32[]{:S(2)}) %collective-permute-start.2) | collective-permute-done | bytes 262176 | tf_op jit(solution)/shard_map/ppermute | solution.py:21
  71.3 1.1 pad_maximum_fusion.refs_1_.rest_0_
  72.5 3.2 %select_select_fusion.refs_3_ = bf16[16,9216]{1,0:T(8,128)(2,1)} fusion(bf16[16,9216]{1,0:T(8,128)(2,1)S(1)} %collective-permute-done.6, bf16[16,9216]{1,0:T(8,128)(2,1)S(1)} %collective-permute-done.7, bf16[16,9216]{1,0:T(8,128)(2,1)S(1)} %collective-permute-done.8, bf16[16,9216]{1,0:T(8,128)(2,1)S(1)} %collective-permute-done.9, pred[]{:T(512)} %bitcast.17, ...), kind=kLoop, calls=%fused_computation.17 | loop fusion | flops 589824 | bytes 1474564 | tf_op jit(solution)/shard_map/jit(_where)/select_n | solution.py:448
  75.7 11.2 %all-to-all-start = ((bf16[16,64,512]{2,1,0:T(8,128)(2,1)}), bf16[16,64,512]{2,1,0:T(8,128)(2,1)S(1)}, u32[]{:S(2)}, u32[]{:S(2)}) async-start(bf16[16,64,512]{2,1,0:T(8,128)(2,1)} %shard_map.95), calls=%async_computation | async-start | bytes 2097152 | tf_op jit(solution)/shard_map/all_to_all | solution.py:465
  87.6 4.6 %shard_map.96.refs_0_ = bf16[16,240,512]{2,1,0:T(8,128)(2,1)} custom-call(bf16[192,8192]{1,0:T(8,128)(2,1)} %act.1, bf16[48,8192]{1,0:T(8,128)(2,1)} %bitcast.106), custom_call_target="tpu_custom_call" | custom-call | bytes 7864320 | tf_op jit(solution)/shard_map/pallas_call | solution.py:271
  92.2 17.9 %all-to-all-done.refs_1_ = bf16[16,64,512]{2,1,0:T(8,128)(2,1)S(1)} async-done(((bf16[16,64,512]{2,1,0:T(8,128)(2,1)}), bf16[16,64,512]{2,1,0:T(8,128)(2,1)S(1)}, u32[]{:S(2)}, u32[]{:S(2)}) %all-to-all-start) | async-done | bytes 1048608 | tf_op jit(solution)/shard_map/all_to_all | solution.py:465
  111.0 6.8 %all-to-all-start.1 = ((bf16[16,240,512]{2,1,0:T(8,128)(2,1)}), bf16[16,240,512]{2,1,0:T(8,128)(2,1)}, u32[]{:S(2)}, u32[]{:S(2)}) async-start(bf16[16,240,512]{2,1,0:T(8,128)(2,1)} %shard_map.97), calls=%async_computation.1 | async-start | bytes 7864320 | tf_op jit(solution)/shard_map/all_to_all | solution.py:494
  121.1 1.2 collective-permute-start.14
  123.3 1.6 collective-permute-start.18
  124.9 3.8 %bitcast_select_fusion.11 = (bf16[16,1024]{1,0:T(8,128)(2,1)S(1)}, bf16[16,1024]{1,0:T(8,128)(2,1)S(1)}, bf16[16,1024]{1,0:T(8,128)(2,1)S(1)}) fusion(pred[]{:T(512)} %bitcast.20, bf16[16,9216]{1,0:T(8,128)(2,1)S(1)} %copy-done.4, bf16[3,16,1024]{2,1,0:T(8,128)(2,1)S(1)} %copy-done.6, pred[]{:T(512)} %bitcast.24, pred[]{:T(512)} %bitcast.22, pred[]{:T(512)} %bitcast.28, ...), kind=kLoop, calls=%fused_computation.48 | loop fusion | flops 98304 | bytes 229382 | tf_op jit(solution)/shard_map/jit(_where)/select_n | solution.py:455
  128.8 4.0 %bitcast_select_fusion.5 = (bf16[16,8192]{1,0:T(8,128)(2,1)S(1)}, bf16[16,8192]{1,0:T(8,128)(2,1)S(1)}, bf16[16,8192]{1,0:T(8,128)(2,1)S(1)}) fusion(pred[]{:T(512)} %bitcast.20, bf16[16,9216]{1,0:T(8,128)(2,1)S(1)} %copy-done.4, bf16[3,16,8192]{2,1,0:T(8,128)(2,1)S(1)} %copy-done.2, pred[]{:T(512)} %bitcast.24, pred[]{:T(512)} %bitcast.22, pred[]{:T(512)} %bitcast.28, ...), kind=kLoop, calls=%fused_computation.23 | loop fusion | flops 786432 | bytes 1835014 | tf_op jit(solution)/shard_map/jit(_where)/select_n | solution.py:455
  135.1 10.9 %collective-permute-done.14.rest_3_ = bf16[4,128,1024]{2,1,0:T(8,128)(2,1)} collective-permute-done((bf16[4,128,1024]{2,1,0:T(8,128)(2,1)}, bf16[4,128,1024]{2,1,0:T(8,128)(2,1)}, u32[]{:S(2)}, u32[]{:S(2)}) %collective-permute-start.14) | collective-permute-done | bytes 1048608 | tf_op jit(solution)/shard_map/ppermute | solution.py:94
  146.0 1.5 collective-permute-start.10
  147.5 20.9 %collective-permute-done.12.rest_2_ = bf16[4,128,1024]{2,1,0:T(8,128)(2,1)} collective-permute-done((bf16[4,128,1024]{2,1,0:T(8,128)(2,1)S(1)}, bf16[4,128,1024]{2,1,0:T(8,128)(2,1)}, u32[]{:S(2)}, u32[]{:S(2)}) %collective-permute-start.12) | collective-permute-done | bytes 1048608 | tf_op jit(solution)/shard_map/ppermute | solution.py:94
  173.9 3.9 %collective-permute-done.18.rest_1_ = bf16[4,128,1024]{2,1,0:T(8,128)(2,1)} collective-permute-done((bf16[4,128,1024]{2,1,0:T(8,128)(2,1)}, bf16[4,128,1024]{2,1,0:T(8,128)(2,1)}, u32[]{:S(2)}, u32[]{:S(2)}) %collective-permute-start.18) | collective-permute-done | bytes 1048608 | tf_op jit(solution)/shard_map/ppermute | solution.py:91
  177.8 1.2 collective-permute-start.22
  179.0 28.4 %collective-permute-done.16.rest_0_ = bf16[4,128,1024]{2,1,0:T(8,128)(2,1)} collective-permute-done((bf16[4,128,1024]{2,1,0:T(8,128)(2,1)S(1)}, bf16[4,128,1024]{2,1,0:T(8,128)(2,1)}, u32[]{:S(2)}, u32[]{:S(2)}) %collective-permute-start.16) | collective-permute-done | bytes 1048608 | tf_op jit(solution)/shard_map/ppermute | solution.py:91
  207.4 1.2 collective-permute-start.20
  209.6 7.1 %shard_map.99 = (bf16[384,8192]{1,0:T(8,128)(2,1)}, f32[8,128]{1,0:T(8,128)}) custom-call(s32[5]{0:T(128)} %pad_add_fusion.2.where, bf16[384,1024]{1,0:T(8,128)(2,1)} %pad_maximum_fusion.2.cot, bf16[384,16]{1,0:T(8,128)(2,1)} %copy.41.grad.refs_0_, bf16[48,8192]{1,0:T(8,128)(2,1)} %pad_maximum_fusion.3.down, ...), custom_call_target="tpu_custom_call" | custom-call | flops 1610612736 | bytes 5767168 | tf_op jit(solution)/shard_map/pallas_call | solution.py:154
  216.8 1.4 broadcast_in_dim.120
  218.2 5.7 %all-to-all-start.2 = ((bf16[16,24,256]{2,1,0:T(8,128)(2,1)}), bf16[16,24,256]{2,1,0:T(8,128)(2,1)S(1)}, u32[]{:S(2)}, u32[]{:S(2)}) async-start(bf16[16,24,256]{2,1,0:T(8,128)(2,1)} %broadcast_in_dim.120), calls=%async_computation.2 | async-start | bytes 393216 | tf_op jit(solution)/shard_map/all_to_all | solution.py:27
  223.9 7.2 %shard_map.100 = (bf16[384,8192]{1,0:T(8,128)(2,1)}, f32[8,128]{1,0:T(8,128)}) custom-call(s32[5]{0:T(128)} %pad_add_fusion.1.where, bf16[384,1024]{1,0:T(8,128)(2,1)} %pad_maximum_fusion.2.cot, bf16[384,16]{1,0:T(8,128)(2,1)} %copy.41.grad.refs_0_, bf16[48,8192]{1,0:T(8,128)(2,1)} %pad_maximum_fusion.3.down, ...), custom_call_target="tpu_custom_call", output_to_operand_aliasing={{0}: (8, {})} | custom-call | flops 1610612736 | bytes 5767168 | tf_op jit(solution)/shard_map/pallas_call | solution.py:154
  231.0 8.7 %shard_map.102.refs_1_ = f32[256,384]{1,0:T(8,128)} custom-call(bf16[16,240,512]{2,1,0:T(8,128)(2,1)} %all-to-all-done.1.refs_1_.act.maps, bf16[16,240,512]{2,1,0:T(8,128)(2,1)} %all-to-all-done.1.refs_1_.act.maps, s32[1,3072]{1,0:T(1,128)} %reshape.257.rows.refs_0_, s32[1,3072]{1,0:T(1,128)} %shard_map.101.spots, s32[32,1]{1,0:T(8,128)} %copy.46.starts), custom_call_target="tpu_custom_call" | custom-call | flops 2415919104 | bytes 3145728 | tf_op jit(solution)/shard_map/pallas_call | solution.py:531
  239.8 1.9 copy.49
  241.7 6.0 %all-to-all-start.4 = ((f32[16,24,256]{2,1,0:T(8,128)}), f32[16,24,256]{2,1,0:T(8,128)S(1)}, u32[]{:S(2)}, u32[]{:S(2)}) async-start(f32[16,24,256]{2,1,0:T(8,128)} %bitcast.44), calls=%async_computation.4 | async-start | bytes 786432 | tf_op jit(solution)/shard_map/all_to_all | solution.py:535
  252.1 6.8 %shard_map.104.refs_1_ = bf16[768,512]{1,0:T(8,128)(2,1)} custom-call(bf16[16,240,512]{2,1,0:T(8,128)(2,1)} %all-to-all-done.1.refs_1_.act.maps, bf16[256,384]{1,0:T(8,128)(2,1)} %bitcast.126, s32[1,3072]{1,0:T(1,128)} %shard_map.103.rows, s32[1,3072]{1,0:T(1,128)} %shard_map.101.spots, s32[32,1]{1,0:T(8,128)} %copy.46.starts), custom_call_target="tpu_custom_call" | custom-call | flops 2415919104 | bytes 3145728 | tf_op jit(solution)/shard_map/pallas_call | solution.py:533
  259.6 5.3 %all-to-all-start.3 = ((bf16[16,48,512]{2,1,0:T(8,128)(2,1)}), bf16[16,48,512]{2,1,0:T(8,128)(2,1)S(1)}, u32[]{:S(2)}, u32[]{:S(2)}) async-start(bf16[16,48,512]{2,1,0:T(8,128)(2,1)} %bitcast.113), calls=%async_computation.3 | async-start | bytes 1572864 | tf_op jit(solution)/shard_map/all_to_all | solution.py:538
  264.9 7.1 %shard_map.106 = (bf16[384,8192]{1,0:T(8,128)(2,1)}, f32[8,128]{1,0:T(8,128)}) custom-call(s32[5]{0:T(128)} %pad_add_fusion.3.where, bf16[384,1024]{1,0:T(8,128)(2,1)} %pad_maximum_fusion.2.cot, bf16[384,16]{1,0:T(8,128)(2,1)} %shard_map.105.grad, bf16[48,8192]{1,0:T(8,128)(2,1)} %pad_maximum_fusion.3.down, ...), custom_call_target="tpu_custom_call", output_to_operand_aliasing={{0}: (8, {})} | custom-call | flops 1610612736 | bytes 5767168 | tf_op jit(solution)/shard_map/pallas_call | solution.py:154
  272.9 2.0 select_add_fusion.1
  275.1 4.3 %collective-permute-start.25 = (f32[16,1024]{1,0:T(8,128)S(1)}, f32[16,1024]{1,0:T(8,128)S(1)}, u32[]{:S(2)}, u32[]{:S(2)}) collective-permute-start(f32[16,1024]{1,0:T(8,128)S(1)} %get-tuple-element.15), channel_id=1, source_target_pairs={{0,14},{1,15},{2,0},{3,1},{4,2},{5,3},{6,4},{7,5},{8,6},{9,7},{10,... | collective-permute-start | bytes 196616 | tf_op jit(solution)/shard_map/ppermute | solution.py:21
  279.5 1.7 collective-permute-start.26
  281.4 7.1 %shard_map.107 = (bf16[384,8192]{1,0:T(8,128)(2,1)}, f32[8,128]{1,0:T(8,128)}) custom-call(s32[5]{0:T(128)} %pad_add_fusion.where, bf16[384,1024]{1,0:T(8,128)(2,1)} %pad_maximum_fusion.2.cot, bf16[384,16]{1,0:T(8,128)(2,1)} %shard_map.105.grad, bf16[48,8192]{1,0:T(8,128)(2,1)} %pad_maximum_fusion.3.down, ...), custom_call_target="tpu_custom_call", output_to_operand_aliasing={{0}: (8, {})} | custom-call | flops 1610612736 | bytes 5767168 | tf_op jit(solution)/shard_map/pallas_call | solution.py:154
  288.6 5.0 %multiply_bitcast_fusion.2 = (f32[1,16,1024]{2,1,0:T(8,128)S(1)}, f32[16,1024]{1,0:T(8,128)S(1)}) fusion(f32[16,1024]{1,0:T(8,128)S(1)} %get-tuple-element.18, f32[16,1024]{1,0:T(8,128)S(1)} %get-tuple-element.17, f32[16,1024]{1,0:T(8,128)S(1)} %get-tuple-element.16, pred[]{:T(512)} %bitcast.40, pred[]{:T(512)} %bitcast.28, pred[]{:T(512)} %bitcast.24, ...), kind=kLoop, calls=%fused_computation.37 | loop fusion | flops 245760 | bytes 589832 | tf_op jit(solution)/shard_map/stack | solution.py:556
  293.6 5.1 %multiply_bitcast_fusion.1 = (f32[1,16,1024]{2,1,0:T(8,128)S(1)}, f32[1,16,1024]{2,1,0:T(8,128)S(1)}) fusion(f32[16,1024]{1,0:T(8,128)S(1)} %get-tuple-element.18, f32[16,1024]{1,0:T(8,128)S(1)} %get-tuple-element.17, f32[16,1024]{1,0:T(8,128)S(1)} %get-tuple-element.16, f32[16,1024]{1,0:T(8,128)S(1)} %get-tuple-element.14, pred[]{:T(512)} %bitcast.53, ...), kind=kLoop, calls=%fused_computation.36 | loop fusion | flops 262144 | bytes 393224 | tf_op jit(solution)/shard_map/stack | solution.py:556
  300.5 1.4 reshape.256
  (126 shorter events, 28.4 us)
Async XLA Ops:
  0.6 12.8 %copy-start.6 = (bf16[3,16,1024]{2,1,0:T(8,128)(2,1)S(1)}, bf16[3,16,1024]{2,1,0:T(8,128)(2,1)}, u32[]{:S(2)}) copy-start(bf16[3,16,1024]{2,1,0:T(8,128)(2,1)} %param.13) | copy-start | bytes 294916
  0.6 56.0 %copy-start.7 = (s32[192]{0:T(256)S(1)}, s32[192]{0:T(256)}, u32[]{:S(2)}) copy-start(s32[192]{0:T(256)} %param.9) | copy-start | bytes 2308
  1.8 13.8 %collective-permute-start.3 = (bf16[128,1024]{1,0:T(8,128)(2,1)S(1)}, bf16[128,1024]{1,0:T(8,128)(2,1)S(1)}, u32[]{:S(2)}, u32[]{:S(2)}) collective-permute-start(bf16[128,1024]{1,0:T(8,128)(2,1)S(1)} %get-tuple-element.34), channel_id=1, source_target_pairs={{0,4},{1,5},{2,6},{3,7},{4,8},{5,9},{6,10},{7,11},{8,12},{9,13},{1... | collective-permute-start | bytes 786440 | tf_op jit(solution)/shard_map/ppermute | solution.py:21
  3.9 20.8 %collective-permute-start.4 = (bf16[128,1024]{1,0:T(8,128)(2,1)S(1)}, bf16[128,1024]{1,0:T(8,128)(2,1)S(1)}, u32[]{:S(2)}, u32[]{:S(2)}) collective-permute-start(bf16[128,1024]{1,0:T(8,128)(2,1)S(1)} %get-tuple-element.34), channel_id=1, source_target_pairs={{0,8},{1,9},{2,10},{3,11},{4,12},{5,13},{6,14},{7,15},{8,0},{9,1},... | collective-permute-start | bytes 786440 | tf_op jit(solution)/shard_map/ppermute | solution.py:21
  6.2 28.6 %collective-permute-start.5 = (bf16[128,1024]{1,0:T(8,128)(2,1)S(1)}, bf16[128,1024]{1,0:T(8,128)(2,1)S(1)}, u32[]{:S(2)}, u32[]{:S(2)}) collective-permute-start(bf16[128,1024]{1,0:T(8,128)(2,1)S(1)} %get-tuple-element.34), channel_id=1, source_target_pairs={{0,12},{1,13},{2,14},{3,15},{4,0},{5,1},{6,2},{7,3},{8,4},{9,5},{1... | collective-permute-start | bytes 786440 | tf_op jit(solution)/shard_map/ppermute | solution.py:21
  7.3 28.7 %collective-permute-start = (bf16[128,1024]{1,0:T(8,128)(2,1)S(1)}, bf16[128,1024]{1,0:T(8,128)(2,1)S(1)}, u32[]{:S(2)}, u32[]{:S(2)}) collective-permute-start(bf16[128,1024]{1,0:T(8,128)(2,1)S(1)} %get-tuple-element.35), channel_id=1, source_target_pairs={{0,4},{1,5},{2,6},{3,7},{4,8},{5,9},{6,10},{7,11},{8,12},{9,13},{1... | collective-permute-start | bytes 786440 | tf_op jit(solution)/shard_map/ppermute | solution.py:21
  7.7 48.2 %collective-permute-start.1 = (bf16[128,1024]{1,0:T(8,128)(2,1)S(1)}, bf16[128,1024]{1,0:T(8,128)(2,1)S(1)}, u32[]{:S(2)}, u32[]{:S(2)}) collective-permute-start(bf16[128,1024]{1,0:T(8,128)(2,1)S(1)} %get-tuple-element.35), channel_id=1, source_target_pairs={{0,8},{1,9},{2,10},{3,11},{4,12},{5,13},{6,14},{7,15},{8,0},{9,1},... | collective-permute-start | bytes 786440 | tf_op jit(solution)/shard_map/ppermute | solution.py:21
  15.6 56.8 %collective-permute-start.6 = (bf16[16,9216]{1,0:T(8,128)(2,1)S(1)}, bf16[16,9216]{1,0:T(8,128)(2,1)S(1)}, u32[]{:S(2)}, u32[]{:S(2)}) collective-permute-start(bf16[16,9216]{1,0:T(8,128)(2,1)S(1)} %pad_maximum_fusion.4), channel_id=1, source_target_pairs={{0,4},{1,5},{2,6},{3,7},{4,8},{5,9},{6,10},{7,11},{8,12},{9,13},{1... | collective-permute-start | bytes 884744 | tf_op jit(solution)/shard_map/ppermute | solution.py:21
  24.7 47.7 %collective-permute-start.7 = (bf16[16,9216]{1,0:T(8,128)(2,1)S(1)}, bf16[16,9216]{1,0:T(8,128)(2,1)S(1)}, u32[]{:S(2)}, u32[]{:S(2)}) collective-permute-start(bf16[16,9216]{1,0:T(8,128)(2,1)S(1)} %pad_maximum_fusion.4), channel_id=1, source_target_pairs={{0,3},{1,4},{2,5},{3,6},{4,7},{5,8},{6,9},{7,10},{8,11},{9,12},{10... | collective-permute-start | bytes 884744 | tf_op jit(solution)/shard_map/ppermute | solution.py:21
  34.8 37.6 %collective-permute-start.8 = (bf16[16,9216]{1,0:T(8,128)(2,1)S(1)}, bf16[16,9216]{1,0:T(8,128)(2,1)S(1)}, u32[]{:S(2)}, u32[]{:S(2)}) collective-permute-start(bf16[16,9216]{1,0:T(8,128)(2,1)S(1)} %pad_maximum_fusion.4), channel_id=1, source_target_pairs={{0,2},{1,3},{2,4},{3,5},{4,6},{5,7},{6,8},{7,9},{8,10},{9,11},{10,... | collective-permute-start | bytes 884744 | tf_op jit(solution)/shard_map/ppermute | solution.py:21
  36.0 36.4 %collective-permute-start.9 = (bf16[16,9216]{1,0:T(8,128)(2,1)S(1)}, bf16[16,9216]{1,0:T(8,128)(2,1)S(1)}, u32[]{:S(2)}, u32[]{:S(2)}) collective-permute-start(bf16[16,9216]{1,0:T(8,128)(2,1)S(1)} %pad_maximum_fusion.4), channel_id=1, source_target_pairs={{0,1},{1,2},{2,3},{3,4},{4,5},{5,6},{6,7},{7,8},{8,9},{9,10},{10,1... | collective-permute-start | bytes 884744 | tf_op jit(solution)/shard_map/ppermute | solution.py:21
  56.0 15.3 %collective-permute-start.2 = (bf16[128,1024]{1,0:T(8,128)(2,1)S(1)}, bf16[128,1024]{1,0:T(8,128)(2,1)S(1)}, u32[]{:S(2)}, u32[]{:S(2)}) collective-permute-start(bf16[128,1024]{1,0:T(8,128)(2,1)S(1)} %get-tuple-element.35), channel_id=1, source_target_pairs={{0,12},{1,13},{2,14},{3,15},{4,0},{5,1},{6,2},{7,3},{8,4},{9,5},{1... | collective-permute-start | bytes 786440 | tf_op jit(solution)/shard_map/ppermute | solution.py:21
  75.7 34.4 %all-to-all-start = ((bf16[16,64,512]{2,1,0:T(8,128)(2,1)}), bf16[16,64,512]{2,1,0:T(8,128)(2,1)S(1)}, u32[]{:S(2)}, u32[]{:S(2)}) async-start(bf16[16,64,512]{2,1,0:T(8,128)(2,1)} %shard_map.95), calls=%async_computation | async-start | bytes 2097152 | tf_op jit(solution)/shard_map/all_to_all | solution.py:465
  110.1 1.0 copy-start
  111.0 11.3 %copy-start.3 = (bf16[4,128,1024]{2,1,0:T(8,128)(2,1)S(1)}, bf16[4,128,1024]{2,1,0:T(8,128)(2,1)}, u32[]{:S(2)}) copy-start(bf16[4,128,1024]{2,1,0:T(8,128)(2,1)} %pad_maximum_fusion.refs_1_.rest_0_) | copy-start | bytes 3145732
  111.0 13.9 %copy-start.4 = (bf16[16,9216]{1,0:T(8,128)(2,1)S(1)}, bf16[16,9216]{1,0:T(8,128)(2,1)}, u32[]{:S(2)}) copy-start(bf16[16,9216]{1,0:T(8,128)(2,1)} %select_select_fusion.refs_3_) | copy-start | bytes 884740
  111.0 17.7 %copy-start.2 = (bf16[3,16,8192]{2,1,0:T(8,128)(2,1)S(1)}, bf16[3,16,8192]{2,1,0:T(8,128)(2,1)}, u32[]{:S(2)}) copy-start(bf16[3,16,8192]{2,1,0:T(8,128)(2,1)} %param.12) | copy-start | bytes 2359300
  111.0 105.7 %all-to-all-start.1 = ((bf16[16,240,512]{2,1,0:T(8,128)(2,1)}), bf16[16,240,512]{2,1,0:T(8,128)(2,1)}, u32[]{:S(2)}, u32[]{:S(2)}) async-start(bf16[16,240,512]{2,1,0:T(8,128)(2,1)} %shard_map.97), calls=%async_computation.1 | async-start | bytes 7864320 | tf_op jit(solution)/shard_map/all_to_all | solution.py:494
  121.1 24.9 %collective-permute-start.14 = (bf16[4,128,1024]{2,1,0:T(8,128)(2,1)}, bf16[4,128,1024]{2,1,0:T(8,128)(2,1)}, u32[]{:S(2)}, u32[]{:S(2)}) collective-permute-start(bf16[4,128,1024]{2,1,0:T(8,128)(2,1)} %pad_maximum_fusion.1.refs_2_.rest_1_), channel_id=1, source_target_pairs={{0,16},{16,0},{1,17},{17,1},{2,18},{18,2},{3,19},{19,3},{4,20},{20... | collective-permute-start | bytes 3145736 | tf_op jit(solution)/shard_map/ppermute | solution.py:94
  122.3 46.2 %collective-permute-start.12 = (bf16[4,128,1024]{2,1,0:T(8,128)(2,1)S(1)}, bf16[4,128,1024]{2,1,0:T(8,128)(2,1)}, u32[]{:S(2)}, u32[]{:S(2)}) collective-permute-start(bf16[4,128,1024]{2,1,0:T(8,128)(2,1)S(1)} %copy-done.3), channel_id=1, source_target_pairs={{0,16},{16,0},{1,17},{17,1},{2,18},{18,2},{3,19},{19,3},{4,20},{20... | collective-permute-start | bytes 3145736 | tf_op jit(solution)/shard_map/ppermute | solution.py:94
  122.5 46.9 %collective-permute-start.11 = (bf16[4,128,1024]{2,1,0:T(8,128)(2,1)}, bf16[4,128,1024]{2,1,0:T(8,128)(2,1)}, u32[]{:S(2)}, u32[]{:S(2)}) collective-permute-start(bf16[4,128,1024]{2,1,0:T(8,128)(2,1)} %pad_maximum_fusion.1.refs_2_.rest_1_), channel_id=1, source_target_pairs={{0,1},{1,0},{2,3},{3,2},{4,5},{5,4},{6,7},{7,6},{8,9},{9,8},{10,11... | collective-permute-start | bytes 3145736 | tf_op jit(solution)/shard_map/ppermute | solution.py:91
  123.3 54.5 %collective-permute-start.18 = (bf16[4,128,1024]{2,1,0:T(8,128)(2,1)}, bf16[4,128,1024]{2,1,0:T(8,128)(2,1)}, u32[]{:S(2)}, u32[]{:S(2)}) collective-permute-start(bf16[4,128,1024]{2,1,0:T(8,128)(2,1)} %pad_maximum_fusion.1.refs_2_.rest_1_), channel_id=1, source_target_pairs={{0,2},{1,3},{2,0},{3,1},{4,6},{5,7},{6,4},{7,5},{8,10},{9,11},{10,... | collective-permute-start | bytes 3145736 | tf_op jit(solution)/shard_map/ppermute | solution.py:91
  124.9 82.5 %collective-permute-start.16 = (bf16[4,128,1024]{2,1,0:T(8,128)(2,1)S(1)}, bf16[4,128,1024]{2,1,0:T(8,128)(2,1)}, u32[]{:S(2)}, u32[]{:S(2)}) collective-permute-start(bf16[4,128,1024]{2,1,0:T(8,128)(2,1)S(1)} %copy-done.3), channel_id=1, source_target_pairs={{0,2},{1,3},{2,0},{3,1},{4,6},{5,7},{6,4},{7,5},{8,10},{9,11},{10,... | collective-permute-start | bytes 3145736 | tf_op jit(solution)/shard_map/ppermute | solution.py:91
  128.7 4.9 %copy-start.1 = (bf16[16,64,512]{2,1,0:T(8,128)(2,1)S(1)}, bf16[16,64,512]{2,1,0:T(8,128)(2,1)}, u32[]{:S(2)}) copy-start(bf16[16,64,512]{2,1,0:T(8,128)(2,1)} %copy-done) | copy-start | bytes 3145732
  146.0 77.9 %collective-permute-start.10 = (bf16[4,128,1024]{2,1,0:T(8,128)(2,1)S(1)}, bf16[4,128,1024]{2,1,0:T(8,128)(2,1)}, u32[]{:S(2)}, u32[]{:S(2)}) collective-permute-start(bf16[4,128,1024]{2,1,0:T(8,128)(2,1)S(1)} %copy-done.3), channel_id=1, source_target_pairs={{0,1},{1,0},{2,3},{3,2},{4,5},{5,4},{6,7},{7,6},{8,9},{9,8},{10,11... | collective-permute-start | bytes 3145736 | tf_op jit(solution)/shard_map/ppermute | solution.py:91
  168.5 55.4 %collective-permute-start.15 = (bf16[4,128,1024]{2,1,0:T(8,128)(2,1)}, bf16[4,128,1024]{2,1,0:T(8,128)(2,1)}, u32[]{:S(2)}, u32[]{:S(2)}) collective-permute-start(bf16[4,128,1024]{2,1,0:T(8,128)(2,1)} %collective-permute-done.14.rest_3_), channel_id=1, source_target_pairs={{0,1},{1,0},{2,3},{3,2},{4,5},{5,4},{6,7},{7,6},{8,9},{9,8},{10,11... | collective-permute-start | bytes 3145736 | tf_op jit(solution)/shard_map/ppermute | solution.py:91
  169.4 54.4 %collective-permute-start.13 = (bf16[4,128,1024]{2,1,0:T(8,128)(2,1)}, bf16[4,128,1024]{2,1,0:T(8,128)(2,1)}, u32[]{:S(2)}, u32[]{:S(2)}) collective-permute-start(bf16[4,128,1024]{2,1,0:T(8,128)(2,1)} %collective-permute-done.12.rest_2_), channel_id=1, source_target_pairs={{0,1},{1,0},{2,3},{3,2},{4,5},{5,4},{6,7},{7,6},{8,9},{9,8},{10,11... | collective-permute-start | bytes 3145736 | tf_op jit(solution)/shard_map/ppermute | solution.py:91
  177.8 72.4 %collective-permute-start.22 = (bf16[4,128,1024]{2,1,0:T(8,128)(2,1)}, bf16[4,128,1024]{2,1,0:T(8,128)(2,1)}, u32[]{:S(2)}, u32[]{:S(2)}) collective-permute-start(bf16[4,128,1024]{2,1,0:T(8,128)(2,1)} %collective-permute-done.18.rest_1_), channel_id=1, source_target_pairs={{0,16},{16,0},{1,17},{17,1},{2,18},{18,2},{3,19},{19,3},{4,20},{20... | collective-permute-start | bytes 3145736 | tf_op jit(solution)/shard_map/ppermute | solution.py:94
  207.4 42.9 %collective-permute-start.20 = (bf16[4,128,1024]{2,1,0:T(8,128)(2,1)}, bf16[4,128,1024]{2,1,0:T(8,128)(2,1)S(1)}, u32[]{:S(2)}, u32[]{:S(2)}) collective-permute-start(bf16[4,128,1024]{2,1,0:T(8,128)(2,1)} %collective-permute-done.16.rest_0_), channel_id=1, source_target_pairs={{0,16},{16,0},{1,17},{17,1},{2,18},{18,2},{3,19},{19,3},{4,20},{20... | collective-permute-start | bytes 3145736 | tf_op jit(solution)/shard_map/ppermute | solution.py:94
  218.2 23.6 %all-to-all-start.2 = ((bf16[16,24,256]{2,1,0:T(8,128)(2,1)}), bf16[16,24,256]{2,1,0:T(8,128)(2,1)S(1)}, u32[]{:S(2)}, u32[]{:S(2)}) async-start(bf16[16,24,256]{2,1,0:T(8,128)(2,1)} %broadcast_in_dim.120), calls=%async_computation.2 | async-start | bytes 393216 | tf_op jit(solution)/shard_map/all_to_all | solution.py:27
  241.7 17.9 %all-to-all-start.4 = ((f32[16,24,256]{2,1,0:T(8,128)}), f32[16,24,256]{2,1,0:T(8,128)S(1)}, u32[]{:S(2)}, u32[]{:S(2)}) async-start(f32[16,24,256]{2,1,0:T(8,128)} %bitcast.44), calls=%async_computation.4 | async-start | bytes 786432 | tf_op jit(solution)/shard_map/all_to_all | solution.py:535
  249.7 25.4 %collective-permute-start.19 = (bf16[4,128,1024]{2,1,0:T(8,128)(2,1)}, bf16[4,128,1024]{2,1,0:T(8,128)(2,1)}, u32[]{:S(2)}, u32[]{:S(2)}) collective-permute-start(bf16[4,128,1024]{2,1,0:T(8,128)(2,1)} %collective-permute-done.18.rest_1_), channel_id=1, source_target_pairs={{0,1},{1,0},{2,3},{3,2},{4,5},{5,4},{6,7},{7,6},{8,9},{9,8},{10,11... | collective-permute-start | bytes 3145736 | tf_op jit(solution)/shard_map/ppermute | solution.py:91
  249.8 29.7 %collective-permute-start.17 = (bf16[4,128,1024]{2,1,0:T(8,128)(2,1)}, bf16[4,128,1024]{2,1,0:T(8,128)(2,1)}, u32[]{:S(2)}, u32[]{:S(2)}) collective-permute-start(bf16[4,128,1024]{2,1,0:T(8,128)(2,1)} %collective-permute-done.16.rest_0_), channel_id=1, source_target_pairs={{0,1},{1,0},{2,3},{3,2},{4,5},{5,4},{6,7},{7,6},{8,9},{9,8},{10,11... | collective-permute-start | bytes 3145736 | tf_op jit(solution)/shard_map/ppermute | solution.py:91
  250.2 30.9 %collective-permute-start.23 = (bf16[4,128,1024]{2,1,0:T(8,128)(2,1)}, bf16[4,128,1024]{2,1,0:T(8,128)(2,1)}, u32[]{:S(2)}, u32[]{:S(2)}) collective-permute-start(bf16[4,128,1024]{2,1,0:T(8,128)(2,1)} %collective-permute-done.22.rest_3_), channel_id=1, source_target_pairs={{0,1},{1,0},{2,3},{3,2},{4,5},{5,4},{6,7},{7,6},{8,9},{9,8},{10,11... | collective-permute-start | bytes 3145736 | tf_op jit(solution)/shard_map/ppermute | solution.py:91
  250.3 8.6 %copy-start.5 = (bf16[4,128,1024]{2,1,0:T(8,128)(2,1)}, bf16[4,128,1024]{2,1,0:T(8,128)(2,1)S(1)}, u32[]{:S(2)}) copy-start(bf16[4,128,1024]{2,1,0:T(8,128)(2,1)S(1)} %collective-permute-done.20.rest_2_) | copy-start | bytes 3145732
  250.3 31.1 %collective-permute-start.21 = (bf16[4,128,1024]{2,1,0:T(8,128)(2,1)S(1)}, bf16[4,128,1024]{2,1,0:T(8,128)(2,1)}, u32[]{:S(2)}, u32[]{:S(2)}) collective-permute-start(bf16[4,128,1024]{2,1,0:T(8,128)(2,1)S(1)} %collective-permute-done.20.rest_2_), channel_id=1, source_target_pairs={{0,1},{1,0},{2,3},{3,2},{4,5},{5,4},{6,7},{7,6},{8,9},{9,8},{10,11... | collective-permute-start | bytes 3145736 | tf_op jit(solution)/shard_map/ppermute | solution.py:91
  259.6 39.7 %all-to-all-start.3 = ((bf16[16,48,512]{2,1,0:T(8,128)(2,1)}), bf16[16,48,512]{2,1,0:T(8,128)(2,1)S(1)}, u32[]{:S(2)}, u32[]{:S(2)}) async-start(bf16[16,48,512]{2,1,0:T(8,128)(2,1)} %bitcast.113), calls=%async_computation.3 | async-start | bytes 1572864 | tf_op jit(solution)/shard_map/all_to_all | solution.py:538
  275.0 13.6 %collective-permute-start.24 = (f32[16,1024]{1,0:T(8,128)S(1)}, f32[16,1024]{1,0:T(8,128)S(1)}, u32[]{:S(2)}, u32[]{:S(2)}) collective-permute-start(f32[16,1024]{1,0:T(8,128)S(1)} %get-tuple-element.15), channel_id=1, source_target_pairs={{0,15},{1,0},{2,1},{3,2},{4,3},{5,4},{6,5},{7,6},{8,7},{9,8},{10,9... | collective-permute-start | bytes 196616 | tf_op jit(solution)/shard_map/ppermute | solution.py:21
  275.1 13.4 %collective-permute-start.25 = (f32[16,1024]{1,0:T(8,128)S(1)}, f32[16,1024]{1,0:T(8,128)S(1)}, u32[]{:S(2)}, u32[]{:S(2)}) collective-permute-start(f32[16,1024]{1,0:T(8,128)S(1)} %get-tuple-element.15), channel_id=1, source_target_pairs={{0,14},{1,15},{2,0},{3,1},{4,2},{5,3},{6,4},{7,5},{8,6},{9,7},{10,... | collective-permute-start | bytes 196616 | tf_op jit(solution)/shard_map/ppermute | solution.py:21
  279.5 9.1 %collective-permute-start.26 = (f32[16,1024]{1,0:T(8,128)S(1)}, f32[16,1024]{1,0:T(8,128)S(1)}, u32[]{:S(2)}, u32[]{:S(2)}) collective-permute-start(f32[16,1024]{1,0:T(8,128)S(1)} %get-tuple-element.15), channel_id=1, source_target_pairs={{0,13},{1,14},{2,15},{3,0},{4,1},{5,2},{6,3},{7,4},{8,5},{9,6},{10... | collective-permute-start | bytes 196616 | tf_op jit(solution)/shard_map/ppermute | solution.py:21
  281.2 7.4 %collective-permute-start.27 = (f32[16,1024]{1,0:T(8,128)S(1)}, f32[16,1024]{1,0:T(8,128)S(1)}, u32[]{:S(2)}, u32[]{:S(2)}) collective-permute-start(f32[16,1024]{1,0:T(8,128)S(1)} %get-tuple-element.15), channel_id=1, source_target_pairs={{0,12},{1,13},{2,14},{3,15},{4,0},{5,1},{6,2},{7,3},{8,4},{9,5},{1... | collective-permute-start | bytes 196616 | tf_op jit(solution)/shard_map/ppermute | solution.py:21

commit v19 on v18

--- a/solution.py
+++ b/solution.py
@@ -101,11 +101,15 @@
         return lax.all_gather(mine, "blk", axis_index_groups=lines)
 
     columns = [column(k) for k in range(CHUNKS)]
-    pieces = []
-    for mine in (columns, [over(column, 2) for column in columns]):
+    own = columns + [groups(piece) for piece in columns]
+    across = [over(piece, 2) for piece in columns]
+
+    def rest(late):
+        mine = [after(piece, late) for piece in across]
         both = mine + [groups(piece) for piece in mine]
-        pieces += [both, [over(piece, 1) for piece in both]]
-    return pieces
+        return [both, [over(piece, 1) for piece in both]]
+
+    return [own, [over(piece, 1) for piece in own]], rest
 
 
 def quarter_kernel(where, cot, grad, down, *rest):
@@ -421,7 +425,7 @@
     cap = resident_rows // devices
     start_ids = tenant_first_row // BLOCK
 
-    pieces = weight_pieces(frozen_value_weight)
+    pieces, rest_of_pieces = weight_pieces(frozen_value_weight)
 
     first_block = device * resident
     block_numbers = first_block + jnp.arange(resident, dtype=jnp.int32)
@@ -429,11 +433,19 @@
     hops = jnp.arange(1, HOPS + 1, dtype=jnp.int32)
     is_local = (begin >= first_block) & (begin <= block_numbers)
     home_slot = jnp.clip(begin - first_block, 0, resident - 1)
-    own_slots = jnp.arange(resident, dtype=jnp.int32)
-    chosen_slot = is_local[:, None] & (home_slot[:, None] == own_slots[None, :])
+    row, place_in = jnp.arange(share, dtype=jnp.int32), jnp.arange(HOPS * rank, dtype=jnp.int32)
+    same = row[:, None] % rank == row[None, :] % rank
+    same_far = row[:, None] % rank == place_in[None, :] % rank
     others = lax.rem(device + hops, devices) * resident
     to_me = lax.div(starts_of(others, start_ids), resident) == device
-    continues = begin[resident - 1] == first_block + own_slots
+    home_of = jnp.where(is_local, home_slot, -1)
+    home_of = jnp.broadcast_to(home_of[:, None], (resident, rank)).reshape(-1)
+    from_own = same & (home_of[:, None] == row[None, :] // rank)
+    to_own = same & (home_of[None, :] == row[:, None] // rank)
+    remote = same[:rank] & (home_of < 0)[None, :]
+    continues = (begin[resident - 1] - first_block) == row // rank
+    to_me = jnp.broadcast_to(to_me[:, None], (HOPS, rank)).reshape(-1)
+    from_tails = same_far & continues[:, None] & to_me[None, :]
     last_map = jnp.concatenate(
         [
             lax.dynamic_index_in_dim(maps, home_slot[resident - 1], 0, keepdims=False)
@@ -443,25 +455,21 @@
     )
     homes = lax.rem(device + devices - hops, devices)
     from_home = lax.div(begin[:1], resident) == homes
-    carried = jnp.zeros_like(last_map)
-    for step in range(1, HOPS + 1):
-        carried = jnp.where(from_home[step - 1], moved(last_map, step), carried)
-
-    def of_blocks(maps, own):
-        blocks = []
-        for b in range(resident):
-            chosen = own
-            for k in range(b + 1):
-                chosen = jnp.where(chosen_slot[b, k], maps[k], chosen)
-            blocks.append(chosen)
-        return jnp.concatenate(blocks, axis=0)
-
-    down_blocks = of_blocks(adapter_down_maps, carried[:, :width])
-    up_blocks = of_blocks(adapter_up_maps, carried[:, width:])
+    from_home = jnp.broadcast_to(from_home[:, None], (HOPS, rank)).reshape(-1)
+    from_far = same_far & (home_of < 0)[:, None] & from_home[None, :]
+    carried = [moved(last_map, step) for step in range(1, HOPS + 1)]
+    every_carried = jnp.concatenate(carried, axis=0)
+
+    def of_blocks(maps, far):
+        own = dot(from_own.astype(jnp.bfloat16), maps.reshape(share, -1), ((1,), (0,)))
+        return (own + dot(from_far.astype(jnp.bfloat16), far, ((1,), (0,)))).astype(jnp.bfloat16)
+
+    down_blocks = of_blocks(adapter_down_maps, every_carried[:, :width])
+    up_blocks = of_blocks(adapter_up_maps, every_carried[:, width:])
 
     sent_rows = pack_rows(token_layout_row, cotangent, devices, cap, features)
-    own, _, across, _ = pieces
-    sent_rows = after(sent_rows, *own[:CHUNKS], carried)
+    own = pieces[0]
+    sent_rows = after(sent_rows, *own[:CHUNKS], *carried)
     got_rows = lax.all_to_all(sent_rows, "blk", split_axis=0, concat_axis=0)
     recv_cot = [
         got_rows[:, k * cap : (k + 1) * cap].reshape(resident_rows, features)
@@ -503,15 +511,47 @@
     group = lax.axis_index("groups")
     quarter = lax.rem(device, 4)
     firsts = [quarter, quarter ^ 1, quarter ^ 2, quarter ^ 3]
-    if own[0].shape[1] % LANES == 0:
+    tiled = own[0].shape[1] % LANES == 0
+    if tiled:
         out = None
-        for piece, first in zip(pieces[:2], firsts):
+        for piece, first in zip(pieces, firsts):
             out, token = write_quarter(
                 piece, first, group, cot_rows, grad_rows, down_blocks, out
             )
         place_all = after(place_all, token)
+
+    starts = start_ids[:, None]
+    hidden_call, down_call = feature_calls(
+        received, tokens, share, rank, resident_rows, starts.shape[0]
+    )
+    shares = hidden_call(received, received, rows_all, place_all, starts)
+    rows_all = after(rows_all, shares)
+    down_f = down_call(received, grad_all, rows_all, place_all, starts)
+    hidden = shares.T.reshape(devices, cap, -1)
+    hidden = lax.all_to_all(hidden, "blk", split_axis=0, concat_axis=0)
+    hidden = jnp.sum(hidden, axis=0).astype(jnp.bfloat16)
+    hidden = hidden.reshape(cap, devices, rank).transpose(1, 0, 2).reshape(-1, rank)
+    down_home = lax.all_to_all(down_f, "blk", split_axis=0, concat_axis=1, tiled=True)
+    down_map_gradient = down_home.astype(jnp.float32).reshape(resident, rank, width)
+
+    wide = jnp.where(in_block, jnp.concatenate([hidden] * resident, axis=1), 0)
+    up_all = [dot(wide, part, ((0,), (0,))) for part in recv_cot]
+    up_all = jnp.concatenate(up_all, axis=1)
+
+    exact = lax.Precision.HIGHEST
+    tail = jnp.dot(remote.astype(jnp.float32), up_all, precision=exact)
+    tails = jnp.concatenate([moved(tail, -step) for step in range(1, HOPS + 1)], axis=0)
+    up_grads = jnp.dot(to_own.astype(jnp.float32), up_all, precision=exact)
+    up_grads = up_grads + jnp.dot(from_tails.astype(jnp.float32), tails, precision=exact)
+    up_map_gradient = (adapter_scale * up_grads).reshape(resident, rank, out_width)
+
+    others = rest_of_pieces(shares)
+    if tiled:
+        late = after(grad_rows, down_f)
+        for piece, first in zip(others, firsts[2:]):
+            out, _ = write_quarter(piece, first, group, cot_rows, late, down_blocks, out)
     else:
-        weight = together(pieces, firsts, group)
+        weight = together(pieces + others, firsts, group)
         lora = [
             dot(
                 grad_rows[b * BLOCK : (b + 1) * BLOCK],
@@ -523,42 +563,6 @@
         lora = (adapter_scale * jnp.concatenate(lora, axis=0)).astype(jnp.bfloat16)
         out = dot(cot_rows, weight, ((1,), (1,))) + lora.astype(jnp.float32)
         out = out.astype(jnp.bfloat16)
-
-    starts = start_ids[:, None]
-    hidden_call, down_call = feature_calls(
-        received, tokens, share, rank, resident_rows, starts.shape[0]
-    )
-    shares = hidden_call(received, received, rows_all, place_all, starts)
-    rows_all = after(rows_all, shares)
-    down_f = down_call(received, grad_all, rows_all, place_all, starts)
-    hidden = shares.T.reshape(devices, cap, -1)
-    hidden = lax.all_to_all(hidden, "blk", split_axis=0, concat_axis=0)
-    hidden = jnp.sum(hidden, axis=0).astype(jnp.bfloat16)
-    hidden = hidden.reshape(cap, devices, rank).transpose(1, 0, 2).reshape(-1, rank)
-    down_home = lax.all_to_all(down_f, "blk", split_axis=0, concat_axis=1, tiled=True)
-    down_map_gradient = down_home.astype(jnp.float32).reshape(resident, rank, width)
-
-    wide = jnp.where(in_block, jnp.concatenate([hidden] * resident, axis=1), 0)
-    up_all = [dot(wide, part, ((0,), (0,))) for part in recv_cot]
-    up_all = jnp.concatenate(up_all, axis=1).reshape(resident, rank, out_width)
-    up_parts = [up_all[b] for b in range(resident)]
-
-    tail = sum(jnp.where(is_local[b], 0.0, up_parts[b]) for b in range(resident))
-    far = jnp.zeros_like(tail)
-    for step in range(1, HOPS + 1):
-        far = far + jnp.where(to_me[step - 1], moved(tail, -step), 0.0)
-    up_grads = []
-    for k in range(resident):
-        total = jnp.where(continues[k], far, 0.0)
-        for b in range(resident):
-            total = total + jnp.where(chosen_slot[b, k], up_parts[b], 0.0)
-        up_grads.append(adapter_scale * total)
-    up_map_gradient = jnp.stack(up_grads)
-
-    if own[0].shape[1] % LANES == 0:
-        late = after(grad_rows, down_f)
-        for piece, first in zip(pieces[2:], firsts[2:]):
-            out, _ = write_quarter(piece, first, group, cot_rows, late, down_blocks, out)
     return (out, down_map_gradient, up_map_gradient)
 
 

time: 304 us -> 315 us (1.036)
  starting transfers between devices: 88.3 us -> 123 us
  other arithmetic: 35.1 us -> 10.8 us
  waiting for transfers between devices: 103 us -> 97.1 us
  matrix products: 2.19 us -> 5.83 us
    all_to_all x1, waiting for transfers between devices: 0.01 us -> 32.5 us  [local(): received = lax.all_to_all(received, 'blk', split_axis=0, concat_axis=0)]
    ppermute x10, waiting for transfers between devices: 32.3 us -> 0.03 us  [over(): return lax.ppermute(piece, 'blk', [(i, i ^ bit) for i in range(count)])]
    all_to_all x1, starting transfers between devices: 5.72 us -> 18.1 us  [to_all(): return lax.all_to_all(copies, 'blk', split_axis=0, concat_axis=0)]
    another operation x3 -> x0, other arithmetic: 10.7 us -> none  [local(): up_map_gradient = jnp.stack(up_grads)]
    select_n x3, other arithmetic: 11 us -> 0.65 us  [the longest x1 0.64 us: local(): home_of = jnp.where(is_local, home_slot, -1)]
    all_to_all x1, starting transfers between devices: 11.2 us -> 21.4 us  [local(): got_rows = lax.all_to_all(sent_rows, 'blk', split_axis=0, concat_axis=0)]
    ppermute x14, starting transfers between devices: 43.5 us -> 51.2 us  [moved(): lax.ppermute(value, 'blk', [(i, (i + steps) % count) for i in range(count)])]
    all_to_all x1, waiting for transfers between devices: 17.9 us -> 10.9 us  [local(): got_rows = lax.all_to_all(sent_rows, 'blk', split_axis=0, concat_axis=0)]
  transfers between devices with their start and end apart: 33 -> 33, of which waited for: 9 -> 11; matrix products, arithmetic and copies ran while one was open for 16% -> 10% of each run, Pallas kernels for 17% -> 14%
where the time goes in v19:
time: 315 us; the launch traced here: 312 us
  starting transfers between devices  123 us (39%)
  waiting for transfers between devices  97.1 us (31%)
  Pallas kernels  51.2 us (16%)
  local copies, waits for them, and re-layouts  19.8 us (6%)
  other arithmetic  10.8 us (3%)
  matrix products  5.83 us (2%)
  between operations  4.38 us (1%)
    ppermute x14, starting transfers between devices, moved(): lax.ppermute(value, 'blk', [(i, (i + steps) % count) for i in range(count)])  51.2 us
    ppermute x4, waiting for transfers between devices, groups(): return lax.ppermute(piece, 'groups', [(0, 1), (1, 0)])  33.1 us
    all_to_all x1, waiting for transfers between devices, local(): received = lax.all_to_all(received, 'blk', split_axis=0, concat_axis=0)  32.5 us
    pallas_call x4, Pallas kernels, write_quarter(): pl.pallas_call(quarter_kernel, grid_spec=pltpu.PrefetchScalarGridSpec(num...  28.5 us
    all_to_all x1, starting transfers between devices, local(): got_rows = lax.all_to_all(sent_rows, 'blk', split_axis=0, concat_axis=0)  21.4 us
    ppermute x14, waiting for transfers between devices, moved(): lax.ppermute(value, 'blk', [(i, (i + steps) % count) for i in range(count)])  19.5 us
    all_to_all x1, starting transfers between devices, to_all(): return lax.all_to_all(copies, 'blk', split_axis=0, concat_axis=0)  18.1 us
    ppermute x10, starting transfers between devices, over(): return lax.ppermute(piece, 'blk', [(i, i ^ bit) for i in range(count)])  11.1 us
  transfers between devices with their start and end apart: 33, of which 11 were waited for; matrix products, arithmetic and copies ran while one was open for 10% of the time, Pallas kernels for 14%

profile of v19, /device:TPU:1, one launch (start us, length us, event | category | flops | bytes accessed | tf_op | source)
XLA Modules:
  0.0 312.5 jit_solution(15378668319188786258)
XLA Ops:
  0.7 1.1 constant_dynamic-slice_fusion
  1.8 2.2 collective-permute-start.3
  3.9 2.3 collective-permute-start.4
  6.3 1.1 collective-permute-start.5
  7.8 1.3 fusion.84
  12.5 1.0 dynamic-slice_bitcast_fusion
  14.2 3.2 %collective-permute-start.6 = (bf16[16,9216]{1,0:T(8,128)(2,1)S(1)}, bf16[16,9216]{1,0:T(8,128)(2,1)S(1)}, u32[]{:S(2)}, u32[]{:S(2)}) collective-permute-start(bf16[16,9216]{1,0:T(8,128)(2,1)S(1)} %pad_maximum_fusion.3), channel_id=1, source_target_pairs={{0,1},{1,2},{2,3},{3,4},{4,5},{5,6},{6,7},{7,8},{8,9},{9,10},{10,1... | collective-permute-start | bytes 884744 | tf_op jit(solution)/shard_map/ppermute | solution.py:21
  17.4 7.3 %collective-permute-done.4 = bf16[128,1024]{1,0:T(8,128)(2,1)S(1)} collective-permute-done((bf16[128,1024]{1,0:T(8,128)(2,1)S(1)}, bf16[128,1024]{1,0:T(8,128)(2,1)S(1)}, u32[]{:S(2)}, u32[]{:S(2)}) %collective-permute-start.4) | collective-permute-done | bytes 262176 | tf_op jit(solution)/shard_map/ppermute | solution.py:21
  24.7 1.5 collective-permute-start.7
  26.2 21.8 %collective-permute-start.8 = (bf16[16,9216]{1,0:T(8,128)(2,1)S(1)}, bf16[16,9216]{1,0:T(8,128)(2,1)S(1)}, u32[]{:S(2)}, u32[]{:S(2)}) collective-permute-start(bf16[16,9216]{1,0:T(8,128)(2,1)S(1)} %pad_maximum_fusion.3), channel_id=1, source_target_pairs={{0,3},{1,4},{2,5},{3,6},{4,7},{5,8},{6,9},{7,10},{8,11},{9,12},{10... | collective-permute-start | bytes 884744 | tf_op jit(solution)/shard_map/ppermute | solution.py:21
  48.0 8.1 %collective-permute-done.1 = bf16[128,1024]{1,0:T(8,128)(2,1)} collective-permute-done((bf16[128,1024]{1,0:T(8,128)(2,1)S(1)}, bf16[128,1024]{1,0:T(8,128)(2,1)}, u32[]{:S(2)}, u32[]{:S(2)}) %collective-permute-start.1) | collective-permute-done | bytes 262176 | tf_op jit(solution)/shard_map/ppermute | solution.py:21
  57.3 2.6 shard_map.94.refs_0_
  59.9 1.1 pad_maximum_fusion.1.refs_2_.rest_1_
  61.4 2.2 pad_maximum_fusion.refs_1_.rest_0_
  65.3 21.4 %all-to-all-start = ((bf16[16,64,512]{2,1,0:T(8,128)(2,1)}), bf16[16,64,512]{2,1,0:T(8,128)(2,1)S(1)}, u32[]{:S(2)}, u32[]{:S(2)}) async-start(bf16[16,64,512]{2,1,0:T(8,128)(2,1)} %shard_map.95), calls=%async_computation | async-start | bytes 2097152 | tf_op jit(solution)/shard_map/all_to_all | solution.py:473
  88.5 4.6 %shard_map.96.refs_0_ = bf16[16,240,512]{2,1,0:T(8,128)(2,1)} custom-call(bf16[192,8192]{1,0:T(8,128)(2,1)} %act.1, bf16[48,8192]{1,0:T(8,128)(2,1)} %bitcast.51), custom_call_target="tpu_custom_call" | custom-call | bytes 7864320 | tf_op jit(solution)/shard_map/pallas_call | solution.py:275
  95.0 1.3 collective-permute-start.14
  97.2 1.6 collective-permute-start.18
  98.9 10.9 %all-to-all-done.refs_1_ = bf16[16,64,512]{2,1,0:T(8,128)(2,1)S(1)} async-done(((bf16[16,64,512]{2,1,0:T(8,128)(2,1)}), bf16[16,64,512]{2,1,0:T(8,128)(2,1)S(1)}, u32[]{:S(2)}, u32[]{:S(2)}) %all-to-all-start) | async-done | bytes 1048608 | tf_op jit(solution)/shard_map/all_to_all | solution.py:473
  110.8 6.9 %all-to-all-start.1 = ((bf16[16,240,512]{2,1,0:T(8,128)(2,1)}), bf16[16,240,512]{2,1,0:T(8,128)(2,1)}, u32[]{:S(2)}, u32[]{:S(2)}) async-start(bf16[16,240,512]{2,1,0:T(8,128)(2,1)} %shard_map.97), calls=%async_computation.1 | async-start | bytes 7864320 | tf_op jit(solution)/shard_map/all_to_all | solution.py:502
  118.9 1.3 fusion.down
  120.2 1.2 collective-permute-start.15
  121.5 21.1 %collective-permute-done.12.rest_2_ = bf16[4,128,1024]{2,1,0:T(8,128)(2,1)} collective-permute-done((bf16[4,128,1024]{2,1,0:T(8,128)(2,1)}, bf16[4,128,1024]{2,1,0:T(8,128)(2,1)}, u32[]{:S(2)}, u32[]{:S(2)}) %collective-permute-start.12) | collective-permute-done | bytes 1048608 | tf_op jit(solution)/shard_map/ppermute | solution.py:94
  149.3 1.4 collective-permute-start.16
  150.7 1.0 pad_maximum_fusion.2.cot
  151.7 7.1 %shard_map.99 = (bf16[384,8192]{1,0:T(8,128)(2,1)}, f32[8,128]{1,0:T(8,128)}) custom-call(s32[5]{0:T(128)} %pad_add_fusion.2.where, bf16[384,1024]{1,0:T(8,128)(2,1)} %pad_maximum_fusion.2.cot, bf16[384,16]{1,0:T(8,128)(2,1)} %copy.43.grad.refs_0_, bf16[48,8192]{1,0:T(8,128)(2,1)} %fusion.down, bf16[4,128,1024]{2,1,0:T(8,128)(2,1)} %pad_maximum_fusion.refs_1_.rest_0_, ...), custom_call_target="tpu_custom_call" | custom-call | flops 1610612736 | bytes 5767168 | tf_op jit(solution)/shard_map/pallas_call | solution.py:158
  158.8 32.5 %all-to-all-done.1.refs_1_.act.maps = bf16[16,240,512]{2,1,0:T(8,128)(2,1)} async-done(((bf16[16,240,512]{2,1,0:T(8,128)(2,1)}), bf16[16,240,512]{2,1,0:T(8,128)(2,1)}, u32[]{:S(2)}, u32[]{:S(2)}) %all-to-all-start.1) | async-done | bytes 3932192 | tf_op jit(solution)/shard_map/all_to_all | solution.py:502
  191.4 1.4 broadcast_in_dim.124
  192.8 18.1 %all-to-all-start.2 = ((bf16[16,24,256]{2,1,0:T(8,128)(2,1)}), bf16[16,24,256]{2,1,0:T(8,128)(2,1)S(1)}, u32[]{:S(2)}, u32[]{:S(2)}) async-start(bf16[16,24,256]{2,1,0:T(8,128)(2,1)} %broadcast_in_dim.124), calls=%async_computation.2 | async-start | bytes 393216 | tf_op jit(solution)/shard_map/all_to_all | solution.py:27
  210.9 7.1 %shard_map.100 = (bf16[384,8192]{1,0:T(8,128)(2,1)}, f32[8,128]{1,0:T(8,128)}) custom-call(s32[5]{0:T(128)} %pad_add_fusion.1.where, bf16[384,1024]{1,0:T(8,128)(2,1)} %pad_maximum_fusion.2.cot, bf16[384,16]{1,0:T(8,128)(2,1)} %copy.43.grad.refs_0_, bf16[48,8192]{1,0:T(8,128)(2,1)} %fusion.down, ...), custom_call_target="tpu_custom_call", output_to_operand_aliasing={{0}: (8, {})} | custom-call | flops 1610612736 | bytes 5767168 | tf_op jit(solution)/shard_map/pallas_call | solution.py:158
  218.0 8.7 %shard_map.102.refs_1_ = f32[256,384]{1,0:T(8,128)} custom-call(bf16[16,240,512]{2,1,0:T(8,128)(2,1)} %all-to-all-done.1.refs_1_.act.maps, bf16[16,240,512]{2,1,0:T(8,128)(2,1)} %all-to-all-done.1.refs_1_.act.maps, s32[1,3072]{1,0:T(1,128)} %reshape.374.rows.refs_0_, s32[1,3072]{1,0:T(1,128)} %shard_map.101.spots, s32[32,1]{1,0:T(8,128)} %copy.48.starts), custom_call_target="tpu_custom_call" | custom-call | flops 2415919104 | bytes 3145728 | tf_op jit(solution)/shard_map/pallas_call | solution.py:527
  226.8 1.9 copy.51
  228.7 6.0 %all-to-all-start.4 = ((f32[16,24,256]{2,1,0:T(8,128)}), f32[16,24,256]{2,1,0:T(8,128)S(1)}, u32[]{:S(2)}, u32[]{:S(2)}) async-start(f32[16,24,256]{2,1,0:T(8,128)} %bitcast.25), calls=%async_computation.4 | async-start | bytes 786432 | tf_op jit(solution)/shard_map/all_to_all | solution.py:531
  235.6 1.3 collective-permute-start.22
  238.9 6.7 %shard_map.104.refs_1_ = bf16[768,512]{1,0:T(8,128)(2,1)} custom-call(bf16[16,240,512]{2,1,0:T(8,128)(2,1)} %all-to-all-done.1.refs_1_.act.maps, bf16[256,384]{1,0:T(8,128)(2,1)} %bitcast.69, s32[1,3072]{1,0:T(1,128)} %shard_map.103.rows, s32[1,3072]{1,0:T(1,128)} %shard_map.101.spots, s32[32,1]{1,0:T(8,128)} %copy.48.starts), custom_call_target="tpu_custom_call" | custom-call | flops 2415919104 | bytes 3145728 | tf_op jit(solution)/shard_map/pallas_call | solution.py:529
  245.6 1.0 all-to-all-done.4
  246.7 5.7 %all-to-all-start.3 = ((bf16[16,48,512]{2,1,0:T(8,128)(2,1)}), bf16[16,48,512]{2,1,0:T(8,128)(2,1)S(1)}, u32[]{:S(2)}, u32[]{:S(2)}) async-start(bf16[16,48,512]{2,1,0:T(8,128)(2,1)} %bitcast.59), calls=%async_computation.3 | async-start | bytes 1572864 | tf_op jit(solution)/shard_map/all_to_all | solution.py:534
  254.2 4.4 %collective-permute-start.19 = (bf16[4,128,1024]{2,1,0:T(8,128)(2,1)}, bf16[4,128,1024]{2,1,0:T(8,128)(2,1)}, u32[]{:S(2)}, u32[]{:S(2)}) collective-permute-start(bf16[4,128,1024]{2,1,0:T(8,128)(2,1)} %shard_map.107.rest_1_), channel_id=1, source_target_pairs={{0,1},{1,0},{2,3},{3,2},{4,5},{5,4},{6,7},{7,6},{8,9},{9,8},{10,11... | collective-permute-start | bytes 3145736 | tf_op jit(solution)/shard_map/ppermute | solution.py:91
  258.5 1.5 collective-permute-done.24
  260.0 11.2 %collective-permute-start.25 = (f32[16,1024]{1,0:T(8,128)S(1)}, f32[16,1024]{1,0:T(8,128)S(1)}, u32[]{:S(2)}, u32[]{:S(2)}) collective-permute-start(f32[16,1024]{1,0:T(8,128)S(1)} %fusion.16), channel_id=1, source_target_pairs={{0,14},{1,15},{2,0},{3,1},{4,2},{5,3},{6,4},{7,5},{8,6},{9,7},{10,... | collective-permute-start | bytes 196616 | tf_op jit(solution)/shard_map/ppermute | solution.py:21
  271.2 12.0 %collective-permute-done.20.rest_2_ = bf16[4,128,1024]{2,1,0:T(8,128)(2,1)} collective-permute-done((bf16[4,128,1024]{2,1,0:T(8,128)(2,1)}, bf16[4,128,1024]{2,1,0:T(8,128)(2,1)}, u32[]{:S(2)}, u32[]{:S(2)}) %collective-permute-start.20) | collective-permute-done | bytes 1048608 | tf_op jit(solution)/shard_map/ppermute | solution.py:94
  284.2 4.0 %collective-permute-start.26 = (f32[16,1024]{1,0:T(8,128)S(1)}, f32[16,1024]{1,0:T(8,128)S(1)}, u32[]{:S(2)}, u32[]{:S(2)}) collective-permute-start(f32[16,1024]{1,0:T(8,128)S(1)} %fusion.16), channel_id=1, source_target_pairs={{0,13},{1,14},{2,15},{3,0},{4,1},{5,2},{6,3},{7,4},{8,5},{9,6},{10... | collective-permute-start | bytes 196616 | tf_op jit(solution)/shard_map/ppermute | solution.py:21
  288.8 1.1 collective-permute-done.26
  289.8 3.5 %collective-permute-start.27 = (f32[16,1024]{1,0:T(8,128)S(1)}, f32[16,1024]{1,0:T(8,128)S(1)}, u32[]{:S(2)}, u32[]{:S(2)}) collective-permute-start(f32[16,1024]{1,0:T(8,128)S(1)} %fusion.16), channel_id=1, source_target_pairs={{0,12},{1,13},{2,14},{3,15},{4,0},{5,1},{6,2},{7,3},{8,4},{9,5},{1... | collective-permute-start | bytes 196616 | tf_op jit(solution)/shard_map/ppermute | solution.py:21
  293.6 1.0 collective-permute-done.27
  295.6 7.1 %shard_map.108 = (bf16[384,8192]{1,0:T(8,128)(2,1)}, f32[8,128]{1,0:T(8,128)}) custom-call(s32[5]{0:T(128)} %pad_add_fusion.3.where, bf16[384,1024]{1,0:T(8,128)(2,1)} %pad_maximum_fusion.2.cot, bf16[384,16]{1,0:T(8,128)(2,1)} %shard_map.105.grad, bf16[48,8192]{1,0:T(8,128)(2,1)} %fusion.down, ...), custom_call_target="tpu_custom_call", output_to_operand_aliasing={{0}: (8, {})} | custom-call | flops 1610612736 | bytes 5767168 | tf_op jit(solution)/shard_map/pallas_call | solution.py:158
  303.9 1.4 reshape.373
  305.3 7.1 %shard_map.109 = (bf16[384,8192]{1,0:T(8,128)(2,1)}, f32[8,128]{1,0:T(8,128)}) custom-call(s32[5]{0:T(128)} %pad_add_fusion.where, bf16[384,1024]{1,0:T(8,128)(2,1)} %pad_maximum_fusion.2.cot, bf16[384,16]{1,0:T(8,128)(2,1)} %shard_map.105.grad, bf16[48,8192]{1,0:T(8,128)(2,1)} %fusion.down, ...), custom_call_target="tpu_custom_call", output_to_operand_aliasing={{0}: (8, {})} | custom-call | flops 1610612736 | bytes 5767168 | tf_op jit(solution)/shard_map/pallas_call | solution.py:158
  (147 shorter events, 26.5 us)
Async XLA Ops:
  0.6 12.8 %copy-start = (bf16[3,16,1024]{2,1,0:T(8,128)(2,1)S(1)}, bf16[3,16,1024]{2,1,0:T(8,128)(2,1)}, u32[]{:S(2)}) copy-start(bf16[3,16,1024]{2,1,0:T(8,128)(2,1)} %param.13) | copy-start | bytes 294916
  0.6 55.4 %copy-start.14 = (s32[192]{0:T(256)S(1)}, s32[192]{0:T(256)}, u32[]{:S(2)}) copy-start(s32[192]{0:T(256)} %param.9) | copy-start | bytes 2308
  1.8 12.4 %collective-permute-start.3 = (bf16[128,1024]{1,0:T(8,128)(2,1)S(1)}, bf16[128,1024]{1,0:T(8,128)(2,1)S(1)}, u32[]{:S(2)}, u32[]{:S(2)}) collective-permute-start(bf16[128,1024]{1,0:T(8,128)(2,1)S(1)} %get-tuple-element.25), channel_id=1, source_target_pairs={{0,4},{1,5},{2,6},{3,7},{4,8},{5,9},{6,10},{7,11},{8,12},{9,13},{1... | collective-permute-start | bytes 786440 | tf_op jit(solution)/shard_map/ppermute | solution.py:21
  3.9 20.8 %collective-permute-start.4 = (bf16[128,1024]{1,0:T(8,128)(2,1)S(1)}, bf16[128,1024]{1,0:T(8,128)(2,1)S(1)}, u32[]{:S(2)}, u32[]{:S(2)}) collective-permute-start(bf16[128,1024]{1,0:T(8,128)(2,1)S(1)} %get-tuple-element.25), channel_id=1, source_target_pairs={{0,8},{1,9},{2,10},{3,11},{4,12},{5,13},{6,14},{7,15},{8,0},{9,1},... | collective-permute-start | bytes 786440 | tf_op jit(solution)/shard_map/ppermute | solution.py:21
  6.3 19.9 %collective-permute-start.5 = (bf16[128,1024]{1,0:T(8,128)(2,1)S(1)}, bf16[128,1024]{1,0:T(8,128)(2,1)S(1)}, u32[]{:S(2)}, u32[]{:S(2)}) collective-permute-start(bf16[128,1024]{1,0:T(8,128)(2,1)S(1)} %get-tuple-element.25), channel_id=1, source_target_pairs={{0,12},{1,13},{2,14},{3,15},{4,0},{5,1},{6,2},{7,3},{8,4},{9,5},{1... | collective-permute-start | bytes 786440 | tf_op jit(solution)/shard_map/ppermute | solution.py:21
  7.3 40.6 %collective-permute-start = (bf16[128,1024]{1,0:T(8,128)(2,1)S(1)}, bf16[128,1024]{1,0:T(8,128)(2,1)S(1)}, u32[]{:S(2)}, u32[]{:S(2)}) collective-permute-start(bf16[128,1024]{1,0:T(8,128)(2,1)S(1)} %get-tuple-element.26), channel_id=1, source_target_pairs={{0,4},{1,5},{2,6},{3,7},{4,8},{5,9},{6,10},{7,11},{8,12},{9,13},{1... | collective-permute-start | bytes 786440 | tf_op jit(solution)/shard_map/ppermute | solution.py:21
  7.7 48.4 %collective-permute-start.1 = (bf16[128,1024]{1,0:T(8,128)(2,1)S(1)}, bf16[128,1024]{1,0:T(8,128)(2,1)}, u32[]{:S(2)}, u32[]{:S(2)}) collective-permute-start(bf16[128,1024]{1,0:T(8,128)(2,1)S(1)} %get-tuple-element.26), channel_id=1, source_target_pairs={{0,8},{1,9},{2,10},{3,11},{4,12},{5,13},{6,14},{7,15},{8,0},{9,1},... | collective-permute-start | bytes 786440 | tf_op jit(solution)/shard_map/ppermute | solution.py:21
  14.2 49.4 %collective-permute-start.6 = (bf16[16,9216]{1,0:T(8,128)(2,1)S(1)}, bf16[16,9216]{1,0:T(8,128)(2,1)S(1)}, u32[]{:S(2)}, u32[]{:S(2)}) collective-permute-start(bf16[16,9216]{1,0:T(8,128)(2,1)S(1)} %pad_maximum_fusion.3), channel_id=1, source_target_pairs={{0,1},{1,2},{2,3},{3,4},{4,5},{5,6},{6,7},{7,8},{8,9},{9,10},{10,1... | collective-permute-start | bytes 884744 | tf_op jit(solution)/shard_map/ppermute | solution.py:21
  24.7 38.9 %collective-permute-start.7 = (bf16[16,9216]{1,0:T(8,128)(2,1)S(1)}, bf16[16,9216]{1,0:T(8,128)(2,1)S(1)}, u32[]{:S(2)}, u32[]{:S(2)}) collective-permute-start(bf16[16,9216]{1,0:T(8,128)(2,1)S(1)} %pad_maximum_fusion.3), channel_id=1, source_target_pairs={{0,2},{1,3},{2,4},{3,5},{4,6},{5,7},{6,8},{7,9},{8,10},{9,11},{10,... | collective-permute-start | bytes 884744 | tf_op jit(solution)/shard_map/ppermute | solution.py:21
  26.2 37.5 %collective-permute-start.8 = (bf16[16,9216]{1,0:T(8,128)(2,1)S(1)}, bf16[16,9216]{1,0:T(8,128)(2,1)S(1)}, u32[]{:S(2)}, u32[]{:S(2)}) collective-permute-start(bf16[16,9216]{1,0:T(8,128)(2,1)S(1)} %pad_maximum_fusion.3), channel_id=1, source_target_pairs={{0,3},{1,4},{2,5},{3,6},{4,7},{5,8},{6,9},{7,10},{8,11},{9,12},{10... | collective-permute-start | bytes 884744 | tf_op jit(solution)/shard_map/ppermute | solution.py:21
  47.9 15.7 %collective-permute-start.9 = (bf16[16,9216]{1,0:T(8,128)(2,1)S(1)}, bf16[16,9216]{1,0:T(8,128)(2,1)S(1)}, u32[]{:S(2)}, u32[]{:S(2)}) collective-permute-start(bf16[16,9216]{1,0:T(8,128)(2,1)S(1)} %pad_maximum_fusion.3), channel_id=1, source_target_pairs={{0,4},{1,5},{2,6},{3,7},{4,8},{5,9},{6,10},{7,11},{8,12},{9,13},{1... | collective-permute-start | bytes 884744 | tf_op jit(solution)/shard_map/ppermute | solution.py:21
  56.1 5.3 %collective-permute-start.2 = (bf16[128,1024]{1,0:T(8,128)(2,1)S(1)}, bf16[128,1024]{1,0:T(8,128)(2,1)}, u32[]{:S(2)}, u32[]{:S(2)}) collective-permute-start(bf16[128,1024]{1,0:T(8,128)(2,1)S(1)} %get-tuple-element.26), channel_id=1, source_target_pairs={{0,12},{1,13},{2,14},{3,15},{4,0},{5,1},{6,2},{7,3},{8,4},{9,5},{1... | collective-permute-start | bytes 786440 | tf_op jit(solution)/shard_map/ppermute | solution.py:21
  63.6 0.7 copy-start.6
  63.6 0.8 copy-start.8
  63.7 0.9 copy-start.10
  64.5 0.7 copy-start.12
  65.3 44.5 %all-to-all-start = ((bf16[16,64,512]{2,1,0:T(8,128)(2,1)}), bf16[16,64,512]{2,1,0:T(8,128)(2,1)S(1)}, u32[]{:S(2)}, u32[]{:S(2)}) async-start(bf16[16,64,512]{2,1,0:T(8,128)(2,1)} %shard_map.95), calls=%async_computation | async-start | bytes 2097152 | tf_op jit(solution)/shard_map/all_to_all | solution.py:473
  88.5 6.1 %copy-start.3 = (bf16[3,16,8192]{2,1,0:T(8,128)(2,1)S(1)}, bf16[3,16,8192]{2,1,0:T(8,128)(2,1)}, u32[]{:S(2)}) copy-start(bf16[3,16,8192]{2,1,0:T(8,128)(2,1)} %param.12) | copy-start | bytes 2359300
  95.0 25.2 %collective-permute-start.14 = (bf16[4,128,1024]{2,1,0:T(8,128)(2,1)}, bf16[4,128,1024]{2,1,0:T(8,128)(2,1)}, u32[]{:S(2)}, u32[]{:S(2)}) collective-permute-start(bf16[4,128,1024]{2,1,0:T(8,128)(2,1)} %pad_maximum_fusion.1.refs_2_.rest_1_), channel_id=1, source_target_pairs={{0,16},{16,0},{1,17},{17,1},{2,18},{18,2},{3,19},{19,3},{4,20},{20... | collective-permute-start | bytes 3145736 | tf_op jit(solution)/shard_map/ppermute | solution.py:94
  96.3 46.2 %collective-permute-start.12 = (bf16[4,128,1024]{2,1,0:T(8,128)(2,1)}, bf16[4,128,1024]{2,1,0:T(8,128)(2,1)}, u32[]{:S(2)}, u32[]{:S(2)}) collective-permute-start(bf16[4,128,1024]{2,1,0:T(8,128)(2,1)} %pad_maximum_fusion.refs_1_.rest_0_), channel_id=1, source_target_pairs={{0,16},{16,0},{1,17},{17,1},{2,18},{18,2},{3,19},{19,3},{4,20},{20... | collective-permute-start | bytes 3145736 | tf_op jit(solution)/shard_map/ppermute | solution.py:94
  96.6 52.7 %collective-permute-start.11 = (bf16[4,128,1024]{2,1,0:T(8,128)(2,1)}, bf16[4,128,1024]{2,1,0:T(8,128)(2,1)}, u32[]{:S(2)}, u32[]{:S(2)}) collective-permute-start(bf16[4,128,1024]{2,1,0:T(8,128)(2,1)} %pad_maximum_fusion.1.refs_2_.rest_1_), channel_id=1, source_target_pairs={{0,1},{1,0},{2,3},{3,2},{4,5},{5,4},{6,7},{7,6},{8,9},{9,8},{10,11... | collective-permute-start | bytes 3145736 | tf_op jit(solution)/shard_map/ppermute | solution.py:91
  97.2 113.7 %collective-permute-start.10 = (bf16[4,128,1024]{2,1,0:T(8,128)(2,1)}, bf16[4,128,1024]{2,1,0:T(8,128)(2,1)}, u32[]{:S(2)}, u32[]{:S(2)}) collective-permute-start(bf16[4,128,1024]{2,1,0:T(8,128)(2,1)} %pad_maximum_fusion.refs_1_.rest_0_), channel_id=1, source_target_pairs={{0,1},{1,0},{2,3},{3,2},{4,5},{5,4},{6,7},{7,6},{8,9},{9,8},{10,11... | collective-permute-start | bytes 3145736 | tf_op jit(solution)/shard_map/ppermute | solution.py:91
  97.2 138.3 %collective-permute-start.18 = (bf16[4,128,1024]{2,1,0:T(8,128)(2,1)}, bf16[4,128,1024]{2,1,0:T(8,128)(2,1)}, u32[]{:S(2)}, u32[]{:S(2)}) collective-permute-start(bf16[4,128,1024]{2,1,0:T(8,128)(2,1)} %pad_maximum_fusion.1.refs_2_.rest_1_), channel_id=1, source_target_pairs={{0,2},{1,3},{2,0},{3,1},{4,6},{5,7},{6,4},{7,5},{8,10},{9,11},{10,... | collective-permute-start | bytes 3145736 | tf_op jit(solution)/shard_map/ppermute | solution.py:91
  109.8 1.0 copy-start.1
  110.8 6.9 %copy-start.7 = (bf16[16,9216]{1,0:T(8,128)(2,1)S(1)}, bf16[16,9216]{1,0:T(8,128)(2,1)}, u32[]{:S(2)}) copy-start(bf16[16,9216]{1,0:T(8,128)(2,1)} %copy-done.6) | copy-start | bytes 884740
  110.8 6.9 %copy-start.9 = (bf16[16,9216]{1,0:T(8,128)(2,1)S(1)}, bf16[16,9216]{1,0:T(8,128)(2,1)}, u32[]{:S(2)}) copy-start(bf16[16,9216]{1,0:T(8,128)(2,1)} %copy-done.8) | copy-start | bytes 884740
  110.8 7.0 %copy-start.11 = (bf16[16,9216]{1,0:T(8,128)(2,1)S(1)}, bf16[16,9216]{1,0:T(8,128)(2,1)}, u32[]{:S(2)}) copy-start(bf16[16,9216]{1,0:T(8,128)(2,1)} %copy-done.10) | copy-start | bytes 884740
  110.8 80.6 %all-to-all-start.1 = ((bf16[16,240,512]{2,1,0:T(8,128)(2,1)}), bf16[16,240,512]{2,1,0:T(8,128)(2,1)}, u32[]{:S(2)}, u32[]{:S(2)}) async-start(bf16[16,240,512]{2,1,0:T(8,128)(2,1)} %shard_map.97), calls=%async_computation.1 | async-start | bytes 7864320 | tf_op jit(solution)/shard_map/all_to_all | solution.py:502
  117.7 1.0 copy-start.13
  118.9 24.6 %copy-start.2 = (bf16[16,64,512]{2,1,0:T(8,128)(2,1)S(1)}, bf16[16,64,512]{2,1,0:T(8,128)(2,1)}, u32[]{:S(2)}) copy-start(bf16[16,64,512]{2,1,0:T(8,128)(2,1)} %copy-done.1) | copy-start | bytes 3145732
  120.2 90.7 %collective-permute-start.15 = (bf16[4,128,1024]{2,1,0:T(8,128)(2,1)}, bf16[4,128,1024]{2,1,0:T(8,128)(2,1)}, u32[]{:S(2)}, u32[]{:S(2)}) collective-permute-start(bf16[4,128,1024]{2,1,0:T(8,128)(2,1)} %collective-permute-done.14.rest_3_), channel_id=1, source_target_pairs={{0,1},{1,0},{2,3},{3,2},{4,5},{5,4},{6,7},{7,6},{8,9},{9,8},{10,11... | collective-permute-start | bytes 3145736 | tf_op jit(solution)/shard_map/ppermute | solution.py:91
  142.6 68.3 %collective-permute-start.13 = (bf16[4,128,1024]{2,1,0:T(8,128)(2,1)}, bf16[4,128,1024]{2,1,0:T(8,128)(2,1)}, u32[]{:S(2)}, u32[]{:S(2)}) collective-permute-start(bf16[4,128,1024]{2,1,0:T(8,128)(2,1)} %collective-permute-done.12.rest_2_), channel_id=1, source_target_pairs={{0,1},{1,0},{2,3},{3,2},{4,5},{5,4},{6,7},{7,6},{8,9},{9,8},{10,11... | collective-permute-start | bytes 3145736 | tf_op jit(solution)/shard_map/ppermute | solution.py:91
  149.3 87.6 %collective-permute-start.16 = (bf16[4,128,1024]{2,1,0:T(8,128)(2,1)}, bf16[4,128,1024]{2,1,0:T(8,128)(2,1)S(1)}, u32[]{:S(2)}, u32[]{:S(2)}) collective-permute-start(bf16[4,128,1024]{2,1,0:T(8,128)(2,1)} %pad_maximum_fusion.refs_1_.rest_0_), channel_id=1, source_target_pairs={{0,2},{1,3},{2,0},{3,1},{4,6},{5,7},{6,4},{7,5},{8,10},{9,11},{10,... | collective-permute-start | bytes 3145736 | tf_op jit(solution)/shard_map/ppermute | solution.py:91
  192.8 36.0 %all-to-all-start.2 = ((bf16[16,24,256]{2,1,0:T(8,128)(2,1)}), bf16[16,24,256]{2,1,0:T(8,128)(2,1)S(1)}, u32[]{:S(2)}, u32[]{:S(2)}) async-start(bf16[16,24,256]{2,1,0:T(8,128)(2,1)} %broadcast_in_dim.124), calls=%async_computation.2 | async-start | bytes 393216 | tf_op jit(solution)/shard_map/all_to_all | solution.py:27
  228.7 17.9 %all-to-all-start.4 = ((f32[16,24,256]{2,1,0:T(8,128)}), f32[16,24,256]{2,1,0:T(8,128)S(1)}, u32[]{:S(2)}, u32[]{:S(2)}) async-start(f32[16,24,256]{2,1,0:T(8,128)} %bitcast.25), calls=%async_computation.4 | async-start | bytes 786432 | tf_op jit(solution)/shard_map/all_to_all | solution.py:531
  235.6 35.6 %collective-permute-start.22 = (bf16[4,128,1024]{2,1,0:T(8,128)(2,1)}, bf16[4,128,1024]{2,1,0:T(8,128)(2,1)}, u32[]{:S(2)}, u32[]{:S(2)}) collective-permute-start(bf16[4,128,1024]{2,1,0:T(8,128)(2,1)} %shard_map.107.rest_1_), channel_id=1, source_target_pairs={{0,16},{16,0},{1,17},{17,1},{2,18},{18,2},{3,19},{19,3},{4,20},{20... | collective-permute-start | bytes 3145736 | tf_op jit(solution)/shard_map/ppermute | solution.py:94
  236.8 1.0 copy-start.4
  237.8 45.3 %collective-permute-start.20 = (bf16[4,128,1024]{2,1,0:T(8,128)(2,1)}, bf16[4,128,1024]{2,1,0:T(8,128)(2,1)}, u32[]{:S(2)}, u32[]{:S(2)}) collective-permute-start(bf16[4,128,1024]{2,1,0:T(8,128)(2,1)} %shard_map.106.rest_0_), channel_id=1, source_target_pairs={{0,16},{16,0},{1,17},{17,1},{2,18},{18,2},{3,19},{19,3},{4,20},{20... | collective-permute-start | bytes 3145736 | tf_op jit(solution)/shard_map/ppermute | solution.py:94
  246.7 11.9 %copy-start.5 = (bf16[4,128,1024]{2,1,0:T(8,128)(2,1)S(1)}, bf16[4,128,1024]{2,1,0:T(8,128)(2,1)}, u32[]{:S(2)}) copy-start(bf16[4,128,1024]{2,1,0:T(8,128)(2,1)} %shard_map.106.rest_0_) | copy-start | bytes 3145732
  246.7 56.1 %all-to-all-start.3 = ((bf16[16,48,512]{2,1,0:T(8,128)(2,1)}), bf16[16,48,512]{2,1,0:T(8,128)(2,1)S(1)}, u32[]{:S(2)}, u32[]{:S(2)}) async-start(bf16[16,48,512]{2,1,0:T(8,128)(2,1)} %bitcast.59), calls=%async_computation.3 | async-start | bytes 1572864 | tf_op jit(solution)/shard_map/all_to_all | solution.py:534
  253.4 6.6 %collective-permute-start.24 = (f32[16,1024]{1,0:T(8,128)S(1)}, f32[16,1024]{1,0:T(8,128)S(1)}, u32[]{:S(2)}, u32[]{:S(2)}) collective-permute-start(f32[16,1024]{1,0:T(8,128)S(1)} %fusion.16), channel_id=1, source_target_pairs={{0,15},{1,0},{2,1},{3,2},{4,3},{5,4},{6,5},{7,6},{8,7},{9,8},{10,9... | collective-permute-start | bytes 196616 | tf_op jit(solution)/shard_map/ppermute | solution.py:21
  254.2 51.2 %collective-permute-start.19 = (bf16[4,128,1024]{2,1,0:T(8,128)(2,1)}, bf16[4,128,1024]{2,1,0:T(8,128)(2,1)}, u32[]{:S(2)}, u32[]{:S(2)}) collective-permute-start(bf16[4,128,1024]{2,1,0:T(8,128)(2,1)} %shard_map.107.rest_1_), channel_id=1, source_target_pairs={{0,1},{1,0},{2,3},{3,2},{4,5},{5,4},{6,7},{7,6},{8,9},{9,8},{10,11... | collective-permute-start | bytes 3145736 | tf_op jit(solution)/shard_map/ppermute | solution.py:91
  258.5 46.8 %collective-permute-start.17 = (bf16[4,128,1024]{2,1,0:T(8,128)(2,1)S(1)}, bf16[4,128,1024]{2,1,0:T(8,128)(2,1)}, u32[]{:S(2)}, u32[]{:S(2)}) collective-permute-start(bf16[4,128,1024]{2,1,0:T(8,128)(2,1)S(1)} %copy-done.5), channel_id=1, source_target_pairs={{0,1},{1,0},{2,3},{3,2},{4,5},{5,4},{6,7},{7,6},{8,9},{9,8},{10,11... | collective-permute-start | bytes 3145736 | tf_op jit(solution)/shard_map/ppermute | solution.py:91
  260.0 24.2 %collective-permute-start.25 = (f32[16,1024]{1,0:T(8,128)S(1)}, f32[16,1024]{1,0:T(8,128)S(1)}, u32[]{:S(2)}, u32[]{:S(2)}) collective-permute-start(f32[16,1024]{1,0:T(8,128)S(1)} %fusion.16), channel_id=1, source_target_pairs={{0,14},{1,15},{2,0},{3,1},{4,2},{5,3},{6,4},{7,5},{8,6},{9,7},{10,... | collective-permute-start | bytes 196616 | tf_op jit(solution)/shard_map/ppermute | solution.py:21
  271.2 34.2 %collective-permute-start.23 = (bf16[4,128,1024]{2,1,0:T(8,128)(2,1)}, bf16[4,128,1024]{2,1,0:T(8,128)(2,1)}, u32[]{:S(2)}, u32[]{:S(2)}) collective-permute-start(bf16[4,128,1024]{2,1,0:T(8,128)(2,1)} %collective-permute-done.22.rest_3_), channel_id=1, source_target_pairs={{0,1},{1,0},{2,3},{3,2},{4,5},{5,4},{6,7},{7,6},{8,9},{9,8},{10,11... | collective-permute-start | bytes 3145736 | tf_op jit(solution)/shard_map/ppermute | solution.py:91
  283.1 22.2 %collective-permute-start.21 = (bf16[4,128,1024]{2,1,0:T(8,128)(2,1)}, bf16[4,128,1024]{2,1,0:T(8,128)(2,1)}, u32[]{:S(2)}, u32[]{:S(2)}) collective-permute-start(bf16[4,128,1024]{2,1,0:T(8,128)(2,1)} %collective-permute-done.20.rest_2_), channel_id=1, source_target_pairs={{0,1},{1,0},{2,3},{3,2},{4,5},{5,4},{6,7},{7,6},{8,9},{9,8},{10,11... | collective-permute-start | bytes 3145736 | tf_op jit(solution)/shard_map/ppermute | solution.py:91
  284.2 5.7 %collective-permute-start.26 = (f32[16,1024]{1,0:T(8,128)S(1)}, f32[16,1024]{1,0:T(8,128)S(1)}, u32[]{:S(2)}, u32[]{:S(2)}) collective-permute-start(f32[16,1024]{1,0:T(8,128)S(1)} %fusion.16), channel_id=1, source_target_pairs={{0,13},{1,14},{2,15},{3,0},{4,1},{5,2},{6,3},{7,4},{8,5},{9,6},{10... | collective-permute-start | bytes 196616 | tf_op jit(solution)/shard_map/ppermute | solution.py:21
  289.8 4.8 %collective-permute-start.27 = (f32[16,1024]{1,0:T(8,128)S(1)}, f32[16,1024]{1,0:T(8,128)S(1)}, u32[]{:S(2)}, u32[]{:S(2)}) collective-permute-start(f32[16,1024]{1,0:T(8,128)S(1)} %fusion.16), channel_id=1, source_target_pairs={{0,12},{1,13},{2,14},{3,15},{4,0},{5,1},{6,2},{7,3},{8,4},{9,5},{1... | collective-permute-start | bytes 196616 | tf_op jit(solution)/shard_map/ppermute | solution.py:21

commit v20 on v19

--- a/solution.py
+++ b/solution.py
@@ -436,8 +436,8 @@
     row, place_in = jnp.arange(share, dtype=jnp.int32), jnp.arange(HOPS * rank, dtype=jnp.int32)
     same = row[:, None] % rank == row[None, :] % rank
     same_far = row[:, None] % rank == place_in[None, :] % rank
-    others = lax.rem(device + hops, devices) * resident
-    to_me = lax.div(starts_of(others, start_ids), resident) == device
+    next_ones = lax.rem(device + hops, devices) * resident
+    to_me = lax.div(starts_of(next_ones, start_ids), resident) == device
     home_of = jnp.where(is_local, home_slot, -1)
     home_of = jnp.broadcast_to(home_of[:, None], (resident, rank)).reshape(-1)
     from_own = same & (home_of[:, None] == row[None, :] // rank)
@@ -513,12 +513,16 @@
     firsts = [quarter, quarter ^ 1, quarter ^ 2, quarter ^ 3]
     tiled = own[0].shape[1] % LANES == 0
     if tiled:
-        out = None
-        for piece, first in zip(pieces, firsts):
-            out, token = write_quarter(
-                piece, first, group, cot_rows, grad_rows, down_blocks, out
-            )
+        out, first_done = write_quarter(
+            pieces[0], firsts[0], group, cot_rows, grad_rows, down_blocks
+        )
+        others = rest_of_pieces(first_done)
+        out, token = write_quarter(
+            pieces[1], firsts[1], group, cot_rows, grad_rows, down_blocks, out
+        )
         place_all = after(place_all, token)
+    else:
+        others = rest_of_pieces(place_all)
 
     starts = start_ids[:, None]
     hidden_call, down_call = feature_calls(
@@ -540,12 +544,13 @@
 
     exact = lax.Precision.HIGHEST
     tail = jnp.dot(remote.astype(jnp.float32), up_all, precision=exact)
+    if tiled:
+        tail = after(tail, *others[1])
     tails = jnp.concatenate([moved(tail, -step) for step in range(1, HOPS + 1)], axis=0)
     up_grads = jnp.dot(to_own.astype(jnp.float32), up_all, precision=exact)
     up_grads = up_grads + jnp.dot(from_tails.astype(jnp.float32), tails, precision=exact)
     up_map_gradient = (adapter_scale * up_grads).reshape(resident, rank, out_width)
 
-    others = rest_of_pieces(shares)
     if tiled:
         late = after(grad_rows, down_f)
         for piece, first in zip(others, firsts[2:]):

time: 315 us -> 291 us (0.924)
  starting transfers between devices: 123 us -> 99.7 us
  waiting for transfers between devices: 97.1 us -> 88 us
  matrix products: 5.83 us -> 10.4 us
    ppermute x4, waiting for transfers between devices: 33.1 us -> 8.91 us  [groups(): return lax.ppermute(piece, 'groups', [(0, 1), (1, 0)])]
    ppermute x10, waiting for transfers between devices: 0.03 us -> 22.3 us  [over(): return lax.ppermute(piece, 'blk', [(i, i ^ bit) for i in range(count)])]
    all_to_all x1, waiting for transfers between devices: 32.5 us -> 19 us  [local(): received = lax.all_to_all(received, 'blk', split_axis=0, concat_axis=0)]
    ppermute x14, starting transfers between devices: 51.2 us -> 38.9 us  [moved(): lax.ppermute(value, 'blk', [(i, (i + steps) % count) for i in range(count)])]
    ppermute x10, starting transfers between devices: 11.1 us -> 4.57 us  [over(): return lax.ppermute(piece, 'blk', [(i, i ^ bit) for i in range(count)])]
    all_to_all x1, waiting for transfers between devices: 10.9 us -> 16.6 us  [local(): got_rows = lax.all_to_all(sent_rows, 'blk', split_axis=0, concat_axis=0)]
    dot_general x11, matrix products: 4.37 us -> 8.33 us  [dot(): lax.dot_general(a, b, (dims, ((), ())), preferred_element_type=jnp.float32)]
    all_to_all x1, starting transfers between devices: 21.4 us -> 17.7 us  [local(): got_rows = lax.all_to_all(sent_rows, 'blk', split_axis=0, concat_axis=0)]
  transfers between devices with their start and end apart: 33 -> 33, of which waited for: 11 -> 9; matrix products, arithmetic and copies ran while one was open for 10% -> 12% of each run, Pallas kernels for 14% -> 18%
where the time goes in v20:
time: 291 us; the launch traced here: 289 us
  starting transfers between devices  99.7 us (34%)
  waiting for transfers between devices  88 us (30%)
  Pallas kernels  51.2 us (18%)
  local copies, waits for them, and re-layouts  22.6 us (8%)
  other arithmetic  12.8 us (4%)
  matrix products  10.4 us (4%)
  between operations  4.41 us (2%)
    ppermute x14, starting transfers between devices, moved(): lax.ppermute(value, 'blk', [(i, (i + steps) % count) for i in range(count)])  38.9 us
    pallas_call x4, Pallas kernels, write_quarter(): pl.pallas_call(quarter_kernel, grid_spec=pltpu.PrefetchScalarGridSpec(num...  28.5 us
    ppermute x10, waiting for transfers between devices, over(): return lax.ppermute(piece, 'blk', [(i, i ^ bit) for i in range(count)])  22.3 us
    all_to_all x1, waiting for transfers between devices, local(): received = lax.all_to_all(received, 'blk', split_axis=0, concat_axis=0)  19 us
    all_to_all x1, starting transfers between devices, to_all(): return lax.all_to_all(copies, 'blk', split_axis=0, concat_axis=0)  18.2 us
    all_to_all x1, starting transfers between devices, local(): got_rows = lax.all_to_all(sent_rows, 'blk', split_axis=0, concat_axis=0)  17.7 us
    ppermute x14, waiting for transfers between devices, moved(): lax.ppermute(value, 'blk', [(i, (i + steps) % count) for i in range(count)])  17.6 us
    all_to_all x1, waiting for transfers between devices, local(): got_rows = lax.all_to_all(sent_rows, 'blk', split_axis=0, concat_axis=0)  16.6 us
  transfers between devices with their start and end apart: 33, of which 9 were waited for; matrix products, arithmetic and copies ran while one was open for 12% of the time, Pallas kernels for 18%

profile of v20, /device:TPU:1, one launch (start us, length us, event | category | flops | bytes accessed | tf_op | source)
XLA Modules:
  0.0 289.2 jit_solution(15900145545064726898)
XLA Ops:
  0.7 1.1 constant_dynamic-slice_fusion
  1.8 2.2 collective-permute-start.3
  3.9 2.3 collective-permute-start.4
  6.3 1.1 collective-permute-start.5
  7.8 1.3 fusion.84
  15.7 3.2 %collective-permute-start.6 = (bf16[16,9216]{1,0:T(8,128)(2,1)S(1)}, bf16[16,9216]{1,0:T(8,128)(2,1)S(1)}, u32[]{:S(2)}, u32[]{:S(2)}) collective-permute-start(bf16[16,9216]{1,0:T(8,128)(2,1)S(1)} %pad_maximum_fusion.3), channel_id=1, source_target_pairs={{0,1},{1,2},{2,3},{3,4},{4,5},{5,6},{6,7},{7,8},{8,9},{9,10},{10,1... | collective-permute-start | bytes 884744 | tf_op jit(solution)/shard_map/ppermute | solution.py:21
  18.9 5.8 %collective-permute-done.4 = bf16[128,1024]{1,0:T(8,128)(2,1)S(1)} collective-permute-done((bf16[128,1024]{1,0:T(8,128)(2,1)S(1)}, bf16[128,1024]{1,0:T(8,128)(2,1)S(1)}, u32[]{:S(2)}, u32[]{:S(2)}) %collective-permute-start.4) | collective-permute-done | bytes 262176 | tf_op jit(solution)/shard_map/ppermute | solution.py:21
  24.7 1.5 collective-permute-start.7
  26.2 21.8 %collective-permute-start.8 = (bf16[16,9216]{1,0:T(8,128)(2,1)S(1)}, bf16[16,9216]{1,0:T(8,128)(2,1)S(1)}, u32[]{:S(2)}, u32[]{:S(2)}) collective-permute-start(bf16[16,9216]{1,0:T(8,128)(2,1)S(1)} %pad_maximum_fusion.3), channel_id=1, source_target_pairs={{0,3},{1,4},{2,5},{3,6},{4,7},{5,8},{6,9},{7,10},{8,11},{9,12},{10... | collective-permute-start | bytes 884744 | tf_op jit(solution)/shard_map/ppermute | solution.py:21
  48.0 8.0 %collective-permute-done.1 = bf16[128,1024]{1,0:T(8,128)(2,1)S(1)} collective-permute-done((bf16[128,1024]{1,0:T(8,128)(2,1)S(1)}, bf16[128,1024]{1,0:T(8,128)(2,1)S(1)}, u32[]{:S(2)}, u32[]{:S(2)}) %collective-permute-start.1) | collective-permute-done | bytes 262176 | tf_op jit(solution)/shard_map/ppermute | solution.py:21
  56.9 4.6 %shard_map.96.refs_0_ = bf16[16,240,512]{2,1,0:T(8,128)(2,1)} custom-call(bf16[192,8192]{1,0:T(8,128)(2,1)} %act.1, bf16[48,8192]{1,0:T(8,128)(2,1)} %bitcast.50), custom_call_target="tpu_custom_call" | custom-call | bytes 7864320 | tf_op jit(solution)/shard_map/pallas_call | solution.py:275
  61.5 2.6 shard_map.94.refs_0_
  64.0 1.1 pad_maximum_fusion.1.refs_2_.rest_1_
  65.1 2.1 pad_maximum_fusion.refs_1_.rest_0_
  68.9 17.7 %all-to-all-start = ((bf16[16,64,512]{2,1,0:T(8,128)(2,1)}), bf16[16,64,512]{2,1,0:T(8,128)(2,1)S(1)}, u32[]{:S(2)}, u32[]{:S(2)}) async-start(bf16[16,64,512]{2,1,0:T(8,128)(2,1)} %shard_map.95), calls=%async_computation | async-start | bytes 2097152 | tf_op jit(solution)/shard_map/all_to_all | solution.py:473
  88.6 1.3 collective-permute-start.14
  90.8 1.7 collective-permute-start.18
  93.2 16.6 %all-to-all-done.refs_1_ = bf16[16,64,512]{2,1,0:T(8,128)(2,1)S(1)} async-done(((bf16[16,64,512]{2,1,0:T(8,128)(2,1)}), bf16[16,64,512]{2,1,0:T(8,128)(2,1)S(1)}, u32[]{:S(2)}, u32[]{:S(2)}) %all-to-all-start) | async-done | bytes 1048608 | tf_op jit(solution)/shard_map/all_to_all | solution.py:473
  110.7 6.9 %all-to-all-start.1 = ((bf16[16,240,512]{2,1,0:T(8,128)(2,1)}), bf16[16,240,512]{2,1,0:T(8,128)(2,1)}, u32[]{:S(2)}, u32[]{:S(2)}) async-start(bf16[16,240,512]{2,1,0:T(8,128)(2,1)} %shard_map.97), calls=%async_computation.1 | async-start | bytes 7864320 | tf_op jit(solution)/shard_map/all_to_all | solution.py:502
  117.7 1.0 constant_dynamic-update-slice_fusion
  118.7 1.0 copy-done.10
  120.0 2.6 fusion.down
  126.0 1.0 pad_maximum_fusion.2.cot
  127.2 8.9 %collective-permute-done.12.rest_2_ = bf16[4,128,1024]{2,1,0:T(8,128)(2,1)} collective-permute-done((bf16[4,128,1024]{2,1,0:T(8,128)(2,1)}, bf16[4,128,1024]{2,1,0:T(8,128)(2,1)}, u32[]{:S(2)}, u32[]{:S(2)}) %collective-permute-start.12) | collective-permute-done | bytes 1048608 | tf_op jit(solution)/shard_map/ppermute | solution.py:94
  137.0 7.1 %shard_map.99 = (bf16[384,8192]{1,0:T(8,128)(2,1)}, f32[8,128]{1,0:T(8,128)}) custom-call(s32[5]{0:T(128)} %pad_add_fusion.2.where, bf16[384,1024]{1,0:T(8,128)(2,1)} %pad_maximum_fusion.2.cot, bf16[384,16]{1,0:T(8,128)(2,1)} %copy.44.grad.refs_0_, bf16[48,8192]{1,0:T(8,128)(2,1)} %fusion.down, bf16[4,128,1024]{2,1,0:T(8,128)(2,1)} %pad_maximum_fusion.refs_1_.rest_0_, ...), custom_call_target="tpu_custom_call" | custom-call | flops 1610612736 | bytes 5767168 | tf_op jit(solution)/shard_map/pallas_call | solution.py:158
  144.2 22.2 %collective-permute-done.16.refs_0_ = bf16[4,128,1024]{2,1,0:T(8,128)(2,1)} collective-permute-done((bf16[4,128,1024]{2,1,0:T(8,128)(2,1)}, bf16[4,128,1024]{2,1,0:T(8,128)(2,1)}, u32[]{:S(2)}, u32[]{:S(2)}) %collective-permute-start.16) | collective-permute-done | bytes 1048608 | tf_op jit(solution)/shard_map/ppermute | solution.py:91
  166.4 1.3 collective-permute-start.22
  172.2 19.0 %all-to-all-done.1.refs_1_.act.maps = bf16[16,240,512]{2,1,0:T(8,128)(2,1)} async-done(((bf16[16,240,512]{2,1,0:T(8,128)(2,1)}), bf16[16,240,512]{2,1,0:T(8,128)(2,1)}, u32[]{:S(2)}, u32[]{:S(2)}) %all-to-all-start.1) | async-done | bytes 3932192 | tf_op jit(solution)/shard_map/all_to_all | solution.py:502
  191.3 1.4 broadcast_in_dim.124
  192.7 18.2 %all-to-all-start.2 = ((bf16[16,24,256]{2,1,0:T(8,128)(2,1)}), bf16[16,24,256]{2,1,0:T(8,128)(2,1)S(1)}, u32[]{:S(2)}, u32[]{:S(2)}) async-start(bf16[16,24,256]{2,1,0:T(8,128)(2,1)} %broadcast_in_dim.124), calls=%async_computation.2 | async-start | bytes 393216 | tf_op jit(solution)/shard_map/all_to_all | solution.py:27
  211.8 7.1 %shard_map.100 = (bf16[384,8192]{1,0:T(8,128)(2,1)}, f32[8,128]{1,0:T(8,128)}) custom-call(s32[5]{0:T(128)} %pad_add_fusion.1.where, bf16[384,1024]{1,0:T(8,128)(2,1)} %pad_maximum_fusion.2.cot, bf16[384,16]{1,0:T(8,128)(2,1)} %copy.44.grad.refs_0_, bf16[48,8192]{1,0:T(8,128)(2,1)} %fusion.down, ...), custom_call_target="tpu_custom_call", output_to_operand_aliasing={{0}: (8, {})} | custom-call | flops 1610612736 | bytes 5767168 | tf_op jit(solution)/shard_map/pallas_call | solution.py:158
  219.5 8.7 %shard_map.102.refs_1_ = f32[256,384]{1,0:T(8,128)} custom-call(bf16[16,240,512]{2,1,0:T(8,128)(2,1)} %all-to-all-done.1.refs_1_.act.maps, bf16[16,240,512]{2,1,0:T(8,128)(2,1)} %all-to-all-done.1.refs_1_.act.maps, s32[1,3072]{1,0:T(1,128)} %reshape.374.rows.refs_0_, s32[1,3072]{1,0:T(1,128)} %shard_map.101.spots, s32[32,1]{1,0:T(8,128)} %copy.49.starts), custom_call_target="tpu_custom_call" | custom-call | flops 2415919104 | bytes 3145728 | tf_op jit(solution)/shard_map/pallas_call | solution.py:531
  228.2 1.9 copy.52
  230.2 6.0 %all-to-all-start.4 = ((f32[16,24,256]{2,1,0:T(8,128)}), f32[16,24,256]{2,1,0:T(8,128)}, u32[]{:S(2)}, u32[]{:S(2)}) async-start(f32[16,24,256]{2,1,0:T(8,128)} %bitcast.59), calls=%async_computation.4 | async-start | bytes 786432 | tf_op jit(solution)/shard_map/all_to_all | solution.py:535
  237.8 6.8 %shard_map.104.refs_1_ = bf16[768,512]{1,0:T(8,128)(2,1)} custom-call(bf16[16,240,512]{2,1,0:T(8,128)(2,1)} %all-to-all-done.1.refs_1_.act.maps, bf16[256,384]{1,0:T(8,128)(2,1)} %bitcast.71, s32[1,3072]{1,0:T(1,128)} %shard_map.103.rows, s32[1,3072]{1,0:T(1,128)} %shard_map.101.spots, s32[32,1]{1,0:T(8,128)} %copy.49.starts), custom_call_target="tpu_custom_call" | custom-call | flops 2415919104 | bytes 3145728 | tf_op jit(solution)/shard_map/pallas_call | solution.py:533
  244.6 3.6 %all-to-all-done.4 = f32[16,24,256]{2,1,0:T(8,128)} async-done(((f32[16,24,256]{2,1,0:T(8,128)}), f32[16,24,256]{2,1,0:T(8,128)}, u32[]{:S(2)}, u32[]{:S(2)}) %all-to-all-start.4) | async-done | bytes 393248 | tf_op jit(solution)/shard_map/all_to_all | solution.py:535
  248.2 4.4 %all-to-all-start.3 = ((bf16[16,48,512]{2,1,0:T(8,128)(2,1)}), bf16[16,48,512]{2,1,0:T(8,128)(2,1)}, u32[]{:S(2)}, u32[]{:S(2)}) async-start(bf16[16,48,512]{2,1,0:T(8,128)(2,1)} %bitcast.58), calls=%async_computation.3 | async-start | bytes 1572864 | tf_op jit(solution)/shard_map/all_to_all | solution.py:538
  253.4 7.1 %shard_map.108 = (bf16[384,8192]{1,0:T(8,128)(2,1)}, f32[8,128]{1,0:T(8,128)}) custom-call(s32[5]{0:T(128)} %pad_add_fusion.3.where, bf16[384,1024]{1,0:T(8,128)(2,1)} %pad_maximum_fusion.2.cot, bf16[384,16]{1,0:T(8,128)(2,1)} %shard_map.105.grad, bf16[48,8192]{1,0:T(8,128)(2,1)} %fusion.down, ...), custom_call_target="tpu_custom_call", output_to_operand_aliasing={{0}: (8, {})} | custom-call | flops 1610612736 | bytes 5767168 | tf_op jit(solution)/shard_map/pallas_call | solution.py:158
  262.2 7.1 %shard_map.109 = (bf16[384,8192]{1,0:T(8,128)(2,1)}, f32[8,128]{1,0:T(8,128)}) custom-call(s32[5]{0:T(128)} %pad_add_fusion.where, bf16[384,1024]{1,0:T(8,128)(2,1)} %pad_maximum_fusion.2.cot, bf16[384,16]{1,0:T(8,128)(2,1)} %shard_map.105.grad, bf16[48,8192]{1,0:T(8,128)(2,1)} %fusion.down, ...), custom_call_target="tpu_custom_call", output_to_operand_aliasing={{0}: (8, {})} | custom-call | flops 1610612736 | bytes 5767168 | tf_op jit(solution)/shard_map/pallas_call | solution.py:158
  269.3 1.0 reduce_sum.19
  270.8 1.2 fusion.78
  272.0 1.2 fusion.79
  274.3 4.3 %collective-permute-start.25 = (f32[16,1024]{1,0:T(8,128)}, f32[16,1024]{1,0:T(8,128)S(1)}, u32[]{:S(2)}, u32[]{:S(2)}) collective-permute-start(f32[16,1024]{1,0:T(8,128)} %shard_map.110), channel_id=1, source_target_pairs={{0,14},{1,15},{2,0},{3,1},{4,2},{5,3},{6,4},{7,5},{8,6},{9,7},{10,... | collective-permute-start | bytes 196616 | tf_op jit(solution)/shard_map/ppermute | solution.py:21
  278.6 1.6 collective-permute-start.26
  280.8 2.0 collective-permute-done.26
  282.8 1.8 collective-permute-done.27
  285.5 1.3 convert_bitcast_fusion
  287.8 1.4 reshape.373
  (160 shorter events, 29.6 us)
Async XLA Ops:
  0.6 13.5 %copy-start = (bf16[3,16,1024]{2,1,0:T(8,128)(2,1)S(1)}, bf16[3,16,1024]{2,1,0:T(8,128)(2,1)}, u32[]{:S(2)}) copy-start(bf16[3,16,1024]{2,1,0:T(8,128)(2,1)} %param.13) | copy-start | bytes 294916
  0.6 55.6 %copy-start.20 = (s32[192]{0:T(256)S(1)}, s32[192]{0:T(256)}, u32[]{:S(2)}) copy-start(s32[192]{0:T(256)} %param.9) | copy-start | bytes 2308
  1.8 13.9 %collective-permute-start.3 = (bf16[128,1024]{1,0:T(8,128)(2,1)S(1)}, bf16[128,1024]{1,0:T(8,128)(2,1)S(1)}, u32[]{:S(2)}, u32[]{:S(2)}) collective-permute-start(bf16[128,1024]{1,0:T(8,128)(2,1)S(1)} %get-tuple-element.27), channel_id=1, source_target_pairs={{0,4},{1,5},{2,6},{3,7},{4,8},{5,9},{6,10},{7,11},{8,12},{9,13},{1... | collective-permute-start | bytes 786440 | tf_op jit(solution)/shard_map/ppermute | solution.py:21
  3.9 20.8 %collective-permute-start.4 = (bf16[128,1024]{1,0:T(8,128)(2,1)S(1)}, bf16[128,1024]{1,0:T(8,128)(2,1)S(1)}, u32[]{:S(2)}, u32[]{:S(2)}) collective-permute-start(bf16[128,1024]{1,0:T(8,128)(2,1)S(1)} %get-tuple-element.27), channel_id=1, source_target_pairs={{0,8},{1,9},{2,10},{3,11},{4,12},{5,13},{6,14},{7,15},{8,0},{9,1},... | collective-permute-start | bytes 786440 | tf_op jit(solution)/shard_map/ppermute | solution.py:21
  6.3 19.9 %collective-permute-start.5 = (bf16[128,1024]{1,0:T(8,128)(2,1)S(1)}, bf16[128,1024]{1,0:T(8,128)(2,1)S(1)}, u32[]{:S(2)}, u32[]{:S(2)}) collective-permute-start(bf16[128,1024]{1,0:T(8,128)(2,1)S(1)} %get-tuple-element.27), channel_id=1, source_target_pairs={{0,12},{1,13},{2,14},{3,15},{4,0},{5,1},{6,2},{7,3},{8,4},{9,5},{1... | collective-permute-start | bytes 786440 | tf_op jit(solution)/shard_map/ppermute | solution.py:21
  7.3 40.6 %collective-permute-start = (bf16[128,1024]{1,0:T(8,128)(2,1)S(1)}, bf16[128,1024]{1,0:T(8,128)(2,1)S(1)}, u32[]{:S(2)}, u32[]{:S(2)}) collective-permute-start(bf16[128,1024]{1,0:T(8,128)(2,1)S(1)} %get-tuple-element.28), channel_id=1, source_target_pairs={{0,4},{1,5},{2,6},{3,7},{4,8},{5,9},{6,10},{7,11},{8,12},{9,13},{1... | collective-permute-start | bytes 786440 | tf_op jit(solution)/shard_map/ppermute | solution.py:21
  7.7 48.2 %collective-permute-start.1 = (bf16[128,1024]{1,0:T(8,128)(2,1)S(1)}, bf16[128,1024]{1,0:T(8,128)(2,1)S(1)}, u32[]{:S(2)}, u32[]{:S(2)}) collective-permute-start(bf16[128,1024]{1,0:T(8,128)(2,1)S(1)} %get-tuple-element.28), channel_id=1, source_target_pairs={{0,8},{1,9},{2,10},{3,11},{4,12},{5,13},{6,14},{7,15},{8,0},{9,1},... | collective-permute-start | bytes 786440 | tf_op jit(solution)/shard_map/ppermute | solution.py:21
  15.7 51.5 %collective-permute-start.6 = (bf16[16,9216]{1,0:T(8,128)(2,1)S(1)}, bf16[16,9216]{1,0:T(8,128)(2,1)S(1)}, u32[]{:S(2)}, u32[]{:S(2)}) collective-permute-start(bf16[16,9216]{1,0:T(8,128)(2,1)S(1)} %pad_maximum_fusion.3), channel_id=1, source_target_pairs={{0,1},{1,2},{2,3},{3,4},{4,5},{5,6},{6,7},{7,8},{8,9},{9,10},{10,1... | collective-permute-start | bytes 884744 | tf_op jit(solution)/shard_map/ppermute | solution.py:21
  24.7 42.5 %collective-permute-start.7 = (bf16[16,9216]{1,0:T(8,128)(2,1)S(1)}, bf16[16,9216]{1,0:T(8,128)(2,1)S(1)}, u32[]{:S(2)}, u32[]{:S(2)}) collective-permute-start(bf16[16,9216]{1,0:T(8,128)(2,1)S(1)} %pad_maximum_fusion.3), channel_id=1, source_target_pairs={{0,2},{1,3},{2,4},{3,5},{4,6},{5,7},{6,8},{7,9},{8,10},{9,11},{10,... | collective-permute-start | bytes 884744 | tf_op jit(solution)/shard_map/ppermute | solution.py:21
  26.2 41.1 %collective-permute-start.8 = (bf16[16,9216]{1,0:T(8,128)(2,1)S(1)}, bf16[16,9216]{1,0:T(8,128)(2,1)S(1)}, u32[]{:S(2)}, u32[]{:S(2)}) collective-permute-start(bf16[16,9216]{1,0:T(8,128)(2,1)S(1)} %pad_maximum_fusion.3), channel_id=1, source_target_pairs={{0,3},{1,4},{2,5},{3,6},{4,7},{5,8},{6,9},{7,10},{8,11},{9,12},{10... | collective-permute-start | bytes 884744 | tf_op jit(solution)/shard_map/ppermute | solution.py:21
  47.9 19.3 %collective-permute-start.9 = (bf16[16,9216]{1,0:T(8,128)(2,1)S(1)}, bf16[16,9216]{1,0:T(8,128)(2,1)S(1)}, u32[]{:S(2)}, u32[]{:S(2)}) collective-permute-start(bf16[16,9216]{1,0:T(8,128)(2,1)S(1)} %pad_maximum_fusion.3), channel_id=1, source_target_pairs={{0,4},{1,5},{2,6},{3,7},{4,8},{5,9},{6,10},{7,11},{8,12},{9,13},{1... | collective-permute-start | bytes 884744 | tf_op jit(solution)/shard_map/ppermute | solution.py:21
  56.0 9.2 %collective-permute-start.2 = (bf16[128,1024]{1,0:T(8,128)(2,1)S(1)}, bf16[128,1024]{1,0:T(8,128)(2,1)}, u32[]{:S(2)}, u32[]{:S(2)}) collective-permute-start(bf16[128,1024]{1,0:T(8,128)(2,1)S(1)} %get-tuple-element.28), channel_id=1, source_target_pairs={{0,12},{1,13},{2,14},{3,15},{4,0},{5,1},{6,2},{7,3},{8,4},{9,5},{1... | collective-permute-start | bytes 786440 | tf_op jit(solution)/shard_map/ppermute | solution.py:21
  68.9 19.3 %copy-start.3 = (bf16[3,16,8192]{2,1,0:T(8,128)(2,1)S(1)}, bf16[3,16,8192]{2,1,0:T(8,128)(2,1)}, u32[]{:S(2)}) copy-start(bf16[3,16,8192]{2,1,0:T(8,128)(2,1)} %param.12) | copy-start | bytes 2359300
  68.9 40.9 %all-to-all-start = ((bf16[16,64,512]{2,1,0:T(8,128)(2,1)}), bf16[16,64,512]{2,1,0:T(8,128)(2,1)S(1)}, u32[]{:S(2)}, u32[]{:S(2)}) async-start(bf16[16,64,512]{2,1,0:T(8,128)(2,1)} %shard_map.95), calls=%async_computation | async-start | bytes 2097152 | tf_op jit(solution)/shard_map/all_to_all | solution.py:473
  86.6 5.9 %copy-start.16 = (bf16[16,9216]{1,0:T(8,128)(2,1)S(1)}, bf16[16,9216]{1,0:T(8,128)(2,1)}, u32[]{:S(2)}) copy-start(bf16[16,9216]{1,0:T(8,128)(2,1)} %copy-done.15) | copy-start | bytes 884740
  88.6 38.5 %collective-permute-start.14 = (bf16[4,128,1024]{2,1,0:T(8,128)(2,1)}, bf16[4,128,1024]{2,1,0:T(8,128)(2,1)}, u32[]{:S(2)}, u32[]{:S(2)}) collective-permute-start(bf16[4,128,1024]{2,1,0:T(8,128)(2,1)} %pad_maximum_fusion.1.refs_2_.rest_1_), channel_id=1, source_target_pairs={{0,16},{16,0},{1,17},{17,1},{2,18},{18,2},{3,19},{19,3},{4,20},{20... | collective-permute-start | bytes 3145736 | tf_op jit(solution)/shard_map/ppermute | solution.py:94
  89.9 46.2 %collective-permute-start.12 = (bf16[4,128,1024]{2,1,0:T(8,128)(2,1)}, bf16[4,128,1024]{2,1,0:T(8,128)(2,1)}, u32[]{:S(2)}, u32[]{:S(2)}) collective-permute-start(bf16[4,128,1024]{2,1,0:T(8,128)(2,1)} %pad_maximum_fusion.refs_1_.rest_0_), channel_id=1, source_target_pairs={{0,16},{16,0},{1,17},{17,1},{2,18},{18,2},{3,19},{19,3},{4,20},{20... | collective-permute-start | bytes 3145736 | tf_op jit(solution)/shard_map/ppermute | solution.py:94
  90.1 77.5 %collective-permute-start.11 = (bf16[4,128,1024]{2,1,0:T(8,128)(2,1)}, bf16[4,128,1024]{2,1,0:T(8,128)(2,1)}, u32[]{:S(2)}, u32[]{:S(2)}) collective-permute-start(bf16[4,128,1024]{2,1,0:T(8,128)(2,1)} %pad_maximum_fusion.1.refs_2_.rest_1_), channel_id=1, source_target_pairs={{0,1},{1,0},{2,3},{3,2},{4,5},{5,4},{6,7},{7,6},{8,9},{9,8},{10,11... | collective-permute-start | bytes 3145736 | tf_op jit(solution)/shard_map/ppermute | solution.py:91
  90.8 46.3 %collective-permute-start.18 = (bf16[4,128,1024]{2,1,0:T(8,128)(2,1)}, bf16[4,128,1024]{2,1,0:T(8,128)(2,1)}, u32[]{:S(2)}, u32[]{:S(2)}) collective-permute-start(bf16[4,128,1024]{2,1,0:T(8,128)(2,1)} %pad_maximum_fusion.1.refs_2_.rest_1_), channel_id=1, source_target_pairs={{0,2},{1,3},{2,0},{3,1},{4,6},{5,7},{6,4},{7,5},{8,10},{9,11},{10,... | collective-permute-start | bytes 3145736 | tf_op jit(solution)/shard_map/ppermute | solution.py:91
  92.4 74.0 %collective-permute-start.16 = (bf16[4,128,1024]{2,1,0:T(8,128)(2,1)}, bf16[4,128,1024]{2,1,0:T(8,128)(2,1)}, u32[]{:S(2)}, u32[]{:S(2)}) collective-permute-start(bf16[4,128,1024]{2,1,0:T(8,128)(2,1)} %pad_maximum_fusion.refs_1_.rest_0_), channel_id=1, source_target_pairs={{0,2},{1,3},{2,0},{3,1},{4,6},{5,7},{6,4},{7,5},{8,10},{9,11},{10,... | collective-permute-start | bytes 3145736 | tf_op jit(solution)/shard_map/ppermute | solution.py:91
  110.7 6.9 %copy-start.9 = (bf16[64,9216]{1,0:T(8,128)(2,1)S(1)}, bf16[64,9216]{1,0:T(8,128)(2,1)}, u32[]{:S(2)}) copy-start(bf16[64,9216]{1,0:T(8,128)(2,1)} %constant_dynamic-update-slice_fusion.3) | copy-start | bytes 3538948
  110.7 6.9 %copy-start.12 = (bf16[16,9216]{1,0:T(8,128)(2,1)S(1)}, bf16[16,9216]{1,0:T(8,128)(2,1)}, u32[]{:S(2)}) copy-start(bf16[16,9216]{1,0:T(8,128)(2,1)} %copy-done.11) | copy-start | bytes 884740
  110.7 7.0 %copy-start.14 = (bf16[16,9216]{1,0:T(8,128)(2,1)S(1)}, bf16[16,9216]{1,0:T(8,128)(2,1)}, u32[]{:S(2)}) copy-start(bf16[16,9216]{1,0:T(8,128)(2,1)} %copy-done.13) | copy-start | bytes 884740
  110.7 80.5 %all-to-all-start.1 = ((bf16[16,240,512]{2,1,0:T(8,128)(2,1)}), bf16[16,240,512]{2,1,0:T(8,128)(2,1)}, u32[]{:S(2)}, u32[]{:S(2)}) async-start(bf16[16,240,512]{2,1,0:T(8,128)(2,1)} %shard_map.97), calls=%async_computation.1 | async-start | bytes 7864320 | tf_op jit(solution)/shard_map/all_to_all | solution.py:502
  117.6 2.1 copy-start.19
  118.7 1.0 copy-start.10
  120.0 2.6 copy-start.2
  123.4 3.6 %copy-start.7 = (bf16[16,24,512]{2,1,0:T(8,128)(2,1)}, bf16[16,24,512]{2,1,0:T(8,128)(2,1)S(1)}, u32[]{:S(2)}) copy-start(bf16[16,24,512]{2,1,0:T(8,128)(2,1)S(1)} %get-tuple-element.23) | copy-start | bytes 1179652
  123.4 3.6 %copy-start.8 = (bf16[16,24,512]{2,1,0:T(8,128)(2,1)}, bf16[16,24,512]{2,1,0:T(8,128)(2,1)S(1)}, u32[]{:S(2)}) copy-start(bf16[16,24,512]{2,1,0:T(8,128)(2,1)S(1)} %get-tuple-element.24) | copy-start | bytes 1179652
  127.0 83.8 %collective-permute-start.10 = (bf16[4,128,1024]{2,1,0:T(8,128)(2,1)}, bf16[4,128,1024]{2,1,0:T(8,128)(2,1)S(1)}, u32[]{:S(2)}, u32[]{:S(2)}) collective-permute-start(bf16[4,128,1024]{2,1,0:T(8,128)(2,1)} %pad_maximum_fusion.refs_1_.rest_0_), channel_id=1, source_target_pairs={{0,1},{1,0},{2,3},{3,2},{4,5},{5,4},{6,7},{7,6},{8,9},{9,8},{10,11... | collective-permute-start | bytes 3145736 | tf_op jit(solution)/shard_map/ppermute | solution.py:91
  136.1 74.9 %collective-permute-start.15 = (bf16[4,128,1024]{2,1,0:T(8,128)(2,1)}, bf16[4,128,1024]{2,1,0:T(8,128)(2,1)}, u32[]{:S(2)}, u32[]{:S(2)}) collective-permute-start(bf16[4,128,1024]{2,1,0:T(8,128)(2,1)} %collective-permute-done.14.rest_3_), channel_id=1, source_target_pairs={{0,1},{1,0},{2,3},{3,2},{4,5},{5,4},{6,7},{7,6},{8,9},{9,8},{10,11... | collective-permute-start | bytes 3145736 | tf_op jit(solution)/shard_map/ppermute | solution.py:91
  137.0 74.4 %collective-permute-start.13 = (bf16[4,128,1024]{2,1,0:T(8,128)(2,1)}, bf16[4,128,1024]{2,1,0:T(8,128)(2,1)}, u32[]{:S(2)}, u32[]{:S(2)}) collective-permute-start(bf16[4,128,1024]{2,1,0:T(8,128)(2,1)} %collective-permute-done.12.rest_2_), channel_id=1, source_target_pairs={{0,1},{1,0},{2,3},{3,2},{4,5},{5,4},{6,7},{7,6},{8,9},{9,8},{10,11... | collective-permute-start | bytes 3145736 | tf_op jit(solution)/shard_map/ppermute | solution.py:91
  166.4 52.5 %collective-permute-start.22 = (bf16[4,128,1024]{2,1,0:T(8,128)(2,1)}, bf16[4,128,1024]{2,1,0:T(8,128)(2,1)}, u32[]{:S(2)}, u32[]{:S(2)}) collective-permute-start(bf16[4,128,1024]{2,1,0:T(8,128)(2,1)} %shard_map.107.rest_1_), channel_id=1, source_target_pairs={{0,16},{16,0},{1,17},{17,1},{2,18},{18,2},{3,19},{19,3},{4,20},{20... | collective-permute-start | bytes 3145736 | tf_op jit(solution)/shard_map/ppermute | solution.py:94
  167.6 51.5 %collective-permute-start.20 = (bf16[4,128,1024]{2,1,0:T(8,128)(2,1)}, bf16[4,128,1024]{2,1,0:T(8,128)(2,1)}, u32[]{:S(2)}, u32[]{:S(2)}) collective-permute-start(bf16[4,128,1024]{2,1,0:T(8,128)(2,1)} %shard_map.106.rest_0_), channel_id=1, source_target_pairs={{0,16},{16,0},{1,17},{17,1},{2,18},{18,2},{3,19},{19,3},{4,20},{20... | collective-permute-start | bytes 3145736 | tf_op jit(solution)/shard_map/ppermute | solution.py:94
  192.7 37.5 %all-to-all-start.2 = ((bf16[16,24,256]{2,1,0:T(8,128)(2,1)}), bf16[16,24,256]{2,1,0:T(8,128)(2,1)S(1)}, u32[]{:S(2)}, u32[]{:S(2)}) async-start(bf16[16,24,256]{2,1,0:T(8,128)(2,1)} %broadcast_in_dim.124), calls=%async_computation.2 | async-start | bytes 393216 | tf_op jit(solution)/shard_map/all_to_all | solution.py:27
  210.9 49.7 %collective-permute-start.19 = (bf16[4,128,1024]{2,1,0:T(8,128)(2,1)}, bf16[4,128,1024]{2,1,0:T(8,128)(2,1)S(1)}, u32[]{:S(2)}, u32[]{:S(2)}) collective-permute-start(bf16[4,128,1024]{2,1,0:T(8,128)(2,1)} %shard_map.107.rest_1_), channel_id=1, source_target_pairs={{0,1},{1,0},{2,3},{3,2},{4,5},{5,4},{6,7},{7,6},{8,9},{9,8},{10,11... | collective-permute-start | bytes 3145736 | tf_op jit(solution)/shard_map/ppermute | solution.py:91
  211.0 49.5 %collective-permute-start.17 = (bf16[4,128,1024]{2,1,0:T(8,128)(2,1)}, bf16[4,128,1024]{2,1,0:T(8,128)(2,1)S(1)}, u32[]{:S(2)}, u32[]{:S(2)}) collective-permute-start(bf16[4,128,1024]{2,1,0:T(8,128)(2,1)} %shard_map.106.rest_0_), channel_id=1, source_target_pairs={{0,1},{1,0},{2,3},{3,2},{4,5},{5,4},{6,7},{7,6},{8,9},{9,8},{10,11... | collective-permute-start | bytes 3145736 | tf_op jit(solution)/shard_map/ppermute | solution.py:91
  218.9 41.7 %collective-permute-start.23 = (bf16[4,128,1024]{2,1,0:T(8,128)(2,1)}, bf16[4,128,1024]{2,1,0:T(8,128)(2,1)S(1)}, u32[]{:S(2)}, u32[]{:S(2)}) collective-permute-start(bf16[4,128,1024]{2,1,0:T(8,128)(2,1)} %collective-permute-done.22.rest_3_), channel_id=1, source_target_pairs={{0,1},{1,0},{2,3},{3,2},{4,5},{5,4},{6,7},{7,6},{8,9},{9,8},{10,11... | collective-permute-start | bytes 3145736 | tf_op jit(solution)/shard_map/ppermute | solution.py:91
  219.1 41.5 %collective-permute-start.21 = (bf16[4,128,1024]{2,1,0:T(8,128)(2,1)}, bf16[4,128,1024]{2,1,0:T(8,128)(2,1)}, u32[]{:S(2)}, u32[]{:S(2)}) collective-permute-start(bf16[4,128,1024]{2,1,0:T(8,128)(2,1)} %collective-permute-done.20.rest_2_), channel_id=1, source_target_pairs={{0,1},{1,0},{2,3},{3,2},{4,5},{5,4},{6,7},{7,6},{8,9},{9,8},{10,11... | collective-permute-start | bytes 3145736 | tf_op jit(solution)/shard_map/ppermute | solution.py:91
  230.2 18.0 %all-to-all-start.4 = ((f32[16,24,256]{2,1,0:T(8,128)}), f32[16,24,256]{2,1,0:T(8,128)}, u32[]{:S(2)}, u32[]{:S(2)}) async-start(f32[16,24,256]{2,1,0:T(8,128)} %bitcast.59), calls=%async_computation.4 | async-start | bytes 786432 | tf_op jit(solution)/shard_map/all_to_all | solution.py:535
  248.2 37.3 %all-to-all-start.3 = ((bf16[16,48,512]{2,1,0:T(8,128)(2,1)}), bf16[16,48,512]{2,1,0:T(8,128)(2,1)}, u32[]{:S(2)}, u32[]{:S(2)}) async-start(bf16[16,48,512]{2,1,0:T(8,128)(2,1)} %bitcast.58), calls=%async_computation.3 | async-start | bytes 1572864 | tf_op jit(solution)/shard_map/all_to_all | solution.py:538
  260.6 1.0 copy-start.4
  260.6 1.3 copy-start.5
  260.6 1.6 copy-start.6
  274.0 6.7 %collective-permute-start.24 = (f32[16,1024]{1,0:T(8,128)}, f32[16,1024]{1,0:T(8,128)S(1)}, u32[]{:S(2)}, u32[]{:S(2)}) collective-permute-start(f32[16,1024]{1,0:T(8,128)} %shard_map.110), channel_id=1, source_target_pairs={{0,15},{1,0},{2,1},{3,2},{4,3},{5,4},{6,5},{7,6},{8,7},{9,8},{10,9... | collective-permute-start | bytes 196616 | tf_op jit(solution)/shard_map/ppermute | solution.py:21
  274.3 6.5 %collective-permute-start.25 = (f32[16,1024]{1,0:T(8,128)}, f32[16,1024]{1,0:T(8,128)S(1)}, u32[]{:S(2)}, u32[]{:S(2)}) collective-permute-start(f32[16,1024]{1,0:T(8,128)} %shard_map.110), channel_id=1, source_target_pairs={{0,14},{1,15},{2,0},{3,1},{4,2},{5,3},{6,4},{7,5},{8,6},{9,7},{10,... | collective-permute-start | bytes 196616 | tf_op jit(solution)/shard_map/ppermute | solution.py:21
  278.6 4.2 %collective-permute-start.26 = (f32[16,1024]{1,0:T(8,128)}, f32[16,1024]{1,0:T(8,128)S(1)}, u32[]{:S(2)}, u32[]{:S(2)}) collective-permute-start(f32[16,1024]{1,0:T(8,128)} %shard_map.110), channel_id=1, source_target_pairs={{0,13},{1,14},{2,15},{3,0},{4,1},{5,2},{6,3},{7,4},{8,5},{9,6},{10... | collective-permute-start | bytes 196616 | tf_op jit(solution)/shard_map/ppermute | solution.py:21
  280.2 4.4 %collective-permute-start.27 = (f32[16,1024]{1,0:T(8,128)}, f32[16,1024]{1,0:T(8,128)S(1)}, u32[]{:S(2)}, u32[]{:S(2)}) collective-permute-start(f32[16,1024]{1,0:T(8,128)} %shard_map.110), channel_id=1, source_target_pairs={{0,12},{1,13},{2,14},{3,15},{4,0},{5,1},{6,2},{7,3},{8,4},{9,5},{1... | collective-permute-start | bytes 196616 | tf_op jit(solution)/shard_map/ppermute | solution.py:21
  (6 other events, 5.1 us)

commit v21 on v19

--- a/solution.py
+++ b/solution.py
@@ -436,8 +436,8 @@
     row, place_in = jnp.arange(share, dtype=jnp.int32), jnp.arange(HOPS * rank, dtype=jnp.int32)
     same = row[:, None] % rank == row[None, :] % rank
     same_far = row[:, None] % rank == place_in[None, :] % rank
-    others = lax.rem(device + hops, devices) * resident
-    to_me = lax.div(starts_of(others, start_ids), resident) == device
+    next_ones = lax.rem(device + hops, devices) * resident
+    to_me = lax.div(starts_of(next_ones, start_ids), resident) == device
     home_of = jnp.where(is_local, home_slot, -1)
     home_of = jnp.broadcast_to(home_of[:, None], (resident, rank)).reshape(-1)
     from_own = same & (home_of[:, None] == row[None, :] // rank)
@@ -518,7 +518,10 @@
             out, token = write_quarter(
                 piece, first, group, cot_rows, grad_rows, down_blocks, out
             )
+        others = rest_of_pieces(token)
         place_all = after(place_all, token)
+    else:
+        others = rest_of_pieces(place_all)
 
     starts = start_ids[:, None]
     hidden_call, down_call = feature_calls(
@@ -540,14 +543,15 @@
 
     exact = lax.Precision.HIGHEST
     tail = jnp.dot(remote.astype(jnp.float32), up_all, precision=exact)
+    if tiled:
+        tail = after(tail, *others[1])
     tails = jnp.concatenate([moved(tail, -step) for step in range(1, HOPS + 1)], axis=0)
     up_grads = jnp.dot(to_own.astype(jnp.float32), up_all, precision=exact)
     up_grads = up_grads + jnp.dot(from_tails.astype(jnp.float32), tails, precision=exact)
     up_map_gradient = (adapter_scale * up_grads).reshape(resident, rank, out_width)
 
-    others = rest_of_pieces(shares)
     if tiled:
-        late = after(grad_rows, down_f)
+        late = after(grad_rows, down_f, tail)
         for piece, first in zip(others, firsts[2:]):
             out, _ = write_quarter(piece, first, group, cot_rows, late, down_blocks, out)
     else:

time: 315 us -> 281 us (0.89)
  waiting for transfers between devices: 97.1 us -> 73.9 us
  starting transfers between devices: 123 us -> 106 us
    all_to_all x1, waiting for transfers between devices: 32.5 us -> 3.48 us  [local(): received = lax.all_to_all(received, 'blk', split_axis=0, concat_axis=0)]
    ppermute x10, waiting for transfers between devices: 0.03 us -> 19.3 us  [over(): return lax.ppermute(piece, 'blk', [(i, i ^ bit) for i in range(count)])]
    ppermute x14, starting transfers between devices: 51.2 us -> 38.8 us  [moved(): lax.ppermute(value, 'blk', [(i, (i + steps) % count) for i in range(count)])]
    ppermute x4, waiting for transfers between devices: 33.1 us -> 21.1 us  [groups(): return lax.ppermute(piece, 'groups', [(0, 1), (1, 0)])]
    ppermute x10, starting transfers between devices: 11.1 us -> 6.32 us  [over(): return lax.ppermute(piece, 'blk', [(i, i ^ bit) for i in range(count)])]
    ppermute x14, waiting for transfers between devices: 19.5 us -> 15.7 us  [moved(): lax.ppermute(value, 'blk', [(i, (i + steps) % count) for i in range(count)])]
    unnamed x34 -> x44, local copies, waits for them, and re-layouts: 4.49 us -> 6.76 us
  transfers between devices with their start and end apart: 33 -> 33, of which waited for: 11 -> 8; matrix products, arithmetic and copies ran while one was open for 10% -> 12% of each run, Pallas kernels for 14% -> 18%
where the time goes in v21:
time: 281 us; the launch traced here: 279 us
  starting transfers between devices  106 us (38%)
  waiting for transfers between devices  73.9 us (26%)
  Pallas kernels  51.2 us (18%)
  local copies, waits for them, and re-layouts  22.1 us (8%)
  other arithmetic  13.1 us (5%)
  matrix products  8.42 us (3%)
  between operations  4.42 us (2%)
    ppermute x14, starting transfers between devices, moved(): lax.ppermute(value, 'blk', [(i, (i + steps) % count) for i in range(count)])  38.8 us
    pallas_call x4, Pallas kernels, write_quarter(): pl.pallas_call(quarter_kernel, grid_spec=pltpu.PrefetchScalarGridSpec(num...  28.5 us
    all_to_all x1, starting transfers between devices, local(): got_rows = lax.all_to_all(sent_rows, 'blk', split_axis=0, concat_axis=0)  21.4 us
    ppermute x4, waiting for transfers between devices, groups(): return lax.ppermute(piece, 'groups', [(0, 1), (1, 0)])  21.1 us
    ppermute x10, waiting for transfers between devices, over(): return lax.ppermute(piece, 'blk', [(i, i ^ bit) for i in range(count)])  19.3 us
    all_to_all x1, starting transfers between devices, to_all(): return lax.all_to_all(copies, 'blk', split_axis=0, concat_axis=0)  18.2 us
    ppermute x14, waiting for transfers between devices, moved(): lax.ppermute(value, 'blk', [(i, (i + steps) % count) for i in range(count)])  15.7 us
    all_to_all x1, waiting for transfers between devices, local(): got_rows = lax.all_to_all(sent_rows, 'blk', split_axis=0, concat_axis=0)  11.5 us
  transfers between devices with their start and end apart: 33, of which 8 were waited for; matrix products, arithmetic and copies ran while one was open for 12% of the time, Pallas kernels for 18%

profile of v21, /device:TPU:1, one launch (start us, length us, event | category | flops | bytes accessed | tf_op | source)
XLA Modules:
  0.0 279.2 jit_solution(12131651203884330353)
XLA Ops:
  0.7 1.1 constant_dynamic-slice_fusion
  1.8 2.2 collective-permute-start.3
  3.9 2.3 collective-permute-start.4
  6.3 1.1 collective-permute-start.5
  7.8 1.4 fusion.84
  12.6 1.0 dynamic-slice_bitcast_fusion
  14.3 3.2 %collective-permute-start.6 = (bf16[16,9216]{1,0:T(8,128)(2,1)S(1)}, bf16[16,9216]{1,0:T(8,128)(2,1)S(1)}, u32[]{:S(2)}, u32[]{:S(2)}) collective-permute-start(bf16[16,9216]{1,0:T(8,128)(2,1)S(1)} %pad_maximum_fusion.3), channel_id=1, source_target_pairs={{0,1},{1,2},{2,3},{3,4},{4,5},{5,6},{6,7},{7,8},{8,9},{9,10},{10,1... | collective-permute-start | bytes 884744 | tf_op jit(solution)/shard_map/ppermute | solution.py:21
  17.4 7.3 %collective-permute-done.4 = bf16[128,1024]{1,0:T(8,128)(2,1)S(1)} collective-permute-done((bf16[128,1024]{1,0:T(8,128)(2,1)S(1)}, bf16[128,1024]{1,0:T(8,128)(2,1)S(1)}, u32[]{:S(2)}, u32[]{:S(2)}) %collective-permute-start.4) | collective-permute-done | bytes 262176 | tf_op jit(solution)/shard_map/ppermute | solution.py:21
  24.7 1.5 collective-permute-start.7
  26.2 21.8 %collective-permute-start.8 = (bf16[16,9216]{1,0:T(8,128)(2,1)S(1)}, bf16[16,9216]{1,0:T(8,128)(2,1)S(1)}, u32[]{:S(2)}, u32[]{:S(2)}) collective-permute-start(bf16[16,9216]{1,0:T(8,128)(2,1)S(1)} %pad_maximum_fusion.3), channel_id=1, source_target_pairs={{0,3},{1,4},{2,5},{3,6},{4,7},{5,8},{6,9},{7,10},{8,11},{9,12},{10... | collective-permute-start | bytes 884744 | tf_op jit(solution)/shard_map/ppermute | solution.py:21
  48.0 8.1 %collective-permute-done.1 = bf16[128,1024]{1,0:T(8,128)(2,1)} collective-permute-done((bf16[128,1024]{1,0:T(8,128)(2,1)S(1)}, bf16[128,1024]{1,0:T(8,128)(2,1)}, u32[]{:S(2)}, u32[]{:S(2)}) %collective-permute-start.1) | collective-permute-done | bytes 262176 | tf_op jit(solution)/shard_map/ppermute | solution.py:21
  57.3 2.6 shard_map.94.refs_0_
  59.9 1.2 pad_maximum_fusion.1.refs_2_.rest_1_
  61.4 2.1 pad_maximum_fusion.refs_1_.rest_0_
  65.2 21.4 %all-to-all-start = ((bf16[16,64,512]{2,1,0:T(8,128)(2,1)}), bf16[16,64,512]{2,1,0:T(8,128)(2,1)S(1)}, u32[]{:S(2)}, u32[]{:S(2)}) async-start(bf16[16,64,512]{2,1,0:T(8,128)(2,1)} %shard_map.95), calls=%async_computation | async-start | bytes 2097152 | tf_op jit(solution)/shard_map/all_to_all | solution.py:473
  87.7 4.6 %shard_map.96.refs_0_ = bf16[16,240,512]{2,1,0:T(8,128)(2,1)} custom-call(bf16[192,8192]{1,0:T(8,128)(2,1)} %act.1, bf16[48,8192]{1,0:T(8,128)(2,1)} %bitcast.50), custom_call_target="tpu_custom_call" | custom-call | bytes 7864320 | tf_op jit(solution)/shard_map/pallas_call | solution.py:275
  94.4 1.3 collective-permute-start.14
  96.6 1.6 collective-permute-start.18
  98.2 11.5 %all-to-all-done.refs_1_ = bf16[16,64,512]{2,1,0:T(8,128)(2,1)S(1)} async-done(((bf16[16,64,512]{2,1,0:T(8,128)(2,1)}), bf16[16,64,512]{2,1,0:T(8,128)(2,1)S(1)}, u32[]{:S(2)}, u32[]{:S(2)}) %all-to-all-start) | async-done | bytes 1048608 | tf_op jit(solution)/shard_map/all_to_all | solution.py:473
  110.7 6.9 %all-to-all-start.1 = ((bf16[16,240,512]{2,1,0:T(8,128)(2,1)}), bf16[16,240,512]{2,1,0:T(8,128)(2,1)}, u32[]{:S(2)}, u32[]{:S(2)}) async-start(bf16[16,240,512]{2,1,0:T(8,128)(2,1)} %shard_map.97), calls=%async_computation.1 | async-start | bytes 7864320 | tf_op jit(solution)/shard_map/all_to_all | solution.py:502
  118.8 1.3 fusion.down
  120.8 21.1 %collective-permute-done.12.rest_2_ = bf16[4,128,1024]{2,1,0:T(8,128)(2,1)} collective-permute-done((bf16[4,128,1024]{2,1,0:T(8,128)(2,1)}, bf16[4,128,1024]{2,1,0:T(8,128)(2,1)}, u32[]{:S(2)}, u32[]{:S(2)}) %collective-permute-start.12) | collective-permute-done | bytes 1048608 | tf_op jit(solution)/shard_map/ppermute | solution.py:94
  144.2 1.4 collective-permute-start.16
  147.7 1.0 pad_maximum_fusion.2.cot
  148.7 7.1 %shard_map.99 = (bf16[384,8192]{1,0:T(8,128)(2,1)}, f32[8,128]{1,0:T(8,128)}) custom-call(s32[5]{0:T(128)} %pad_add_fusion.2.where, bf16[384,1024]{1,0:T(8,128)(2,1)} %pad_maximum_fusion.2.cot, bf16[384,16]{1,0:T(8,128)(2,1)} %copy.44.grad.refs_0_, bf16[48,8192]{1,0:T(8,128)(2,1)} %fusion.down, bf16[4,128,1024]{2,1,0:T(8,128)(2,1)} %pad_maximum_fusion.refs_1_.rest_0_, ...), custom_call_target="tpu_custom_call" | custom-call | flops 1610612736 | bytes 5767168 | tf_op jit(solution)/shard_map/pallas_call | solution.py:158
  156.8 7.1 %shard_map.100 = (bf16[384,8192]{1,0:T(8,128)(2,1)}, f32[8,128]{1,0:T(8,128)}) custom-call(s32[5]{0:T(128)} %pad_add_fusion.1.where, bf16[384,1024]{1,0:T(8,128)(2,1)} %pad_maximum_fusion.2.cot, bf16[384,16]{1,0:T(8,128)(2,1)} %copy.44.grad.refs_0_, bf16[48,8192]{1,0:T(8,128)(2,1)} %fusion.down, ...), custom_call_target="tpu_custom_call", output_to_operand_aliasing={{0}: (8, {})} | custom-call | flops 1610612736 | bytes 5767168 | tf_op jit(solution)/shard_map/pallas_call | solution.py:158
  163.9 1.2 collective-permute-start.22
  165.2 19.3 %collective-permute-done.16.refs_0_ = bf16[4,128,1024]{2,1,0:T(8,128)(2,1)S(1)} collective-permute-done((bf16[4,128,1024]{2,1,0:T(8,128)(2,1)}, bf16[4,128,1024]{2,1,0:T(8,128)(2,1)S(1)}, u32[]{:S(2)}, u32[]{:S(2)}) %collective-permute-start.16) | collective-permute-done | bytes 1048608 | tf_op jit(solution)/shard_map/ppermute | solution.py:91
  185.5 1.2 collective-permute-start.20
  187.7 3.5 %all-to-all-done.1.refs_1_.act.maps = bf16[16,240,512]{2,1,0:T(8,128)(2,1)} async-done(((bf16[16,240,512]{2,1,0:T(8,128)(2,1)}), bf16[16,240,512]{2,1,0:T(8,128)(2,1)}, u32[]{:S(2)}, u32[]{:S(2)}) %all-to-all-start.1) | async-done | bytes 3932192 | tf_op jit(solution)/shard_map/all_to_all | solution.py:502
  191.2 1.4 broadcast_in_dim.124
  192.6 18.2 %all-to-all-start.2 = ((bf16[16,24,256]{2,1,0:T(8,128)(2,1)}), bf16[16,24,256]{2,1,0:T(8,128)(2,1)S(1)}, u32[]{:S(2)}, u32[]{:S(2)}) async-start(bf16[16,24,256]{2,1,0:T(8,128)(2,1)} %broadcast_in_dim.124), calls=%async_computation.2 | async-start | bytes 393216 | tf_op jit(solution)/shard_map/all_to_all | solution.py:27
  213.5 8.7 %shard_map.102.refs_1_ = f32[256,384]{1,0:T(8,128)} custom-call(bf16[16,240,512]{2,1,0:T(8,128)(2,1)} %all-to-all-done.1.refs_1_.act.maps, bf16[16,240,512]{2,1,0:T(8,128)(2,1)} %all-to-all-done.1.refs_1_.act.maps, s32[1,3072]{1,0:T(1,128)} %reshape.374.rows.refs_0_, s32[1,3072]{1,0:T(1,128)} %shard_map.101.spots, s32[32,1]{1,0:T(8,128)} %copy.49.starts), custom_call_target="tpu_custom_call" | custom-call | flops 2415919104 | bytes 3145728 | tf_op jit(solution)/shard_map/pallas_call | solution.py:530
  222.2 2.0 copy.51
  224.2 6.0 %all-to-all-start.3 = ((f32[16,24,256]{2,1,0:T(8,128)}), f32[16,24,256]{2,1,0:T(8,128)}, u32[]{:S(2)}, u32[]{:S(2)}) async-start(f32[16,24,256]{2,1,0:T(8,128)} %bitcast.23), calls=%async_computation.3 | async-start | bytes 786432 | tf_op jit(solution)/shard_map/all_to_all | solution.py:534
  232.8 6.8 %shard_map.104.refs_1_ = bf16[768,512]{1,0:T(8,128)(2,1)} custom-call(bf16[16,240,512]{2,1,0:T(8,128)(2,1)} %all-to-all-done.1.refs_1_.act.maps, bf16[256,384]{1,0:T(8,128)(2,1)} %bitcast.69, s32[1,3072]{1,0:T(1,128)} %shard_map.103.rows, s32[1,3072]{1,0:T(1,128)} %shard_map.101.spots, s32[32,1]{1,0:T(8,128)} %copy.49.starts), custom_call_target="tpu_custom_call" | custom-call | flops 2415919104 | bytes 3145728 | tf_op jit(solution)/shard_map/pallas_call | solution.py:532
  239.6 2.7 all-to-all-done.3
  242.3 4.4 %all-to-all-start.4 = ((bf16[16,48,512]{2,1,0:T(8,128)(2,1)}), bf16[16,48,512]{2,1,0:T(8,128)(2,1)}, u32[]{:S(2)}, u32[]{:S(2)}) async-start(bf16[16,48,512]{2,1,0:T(8,128)(2,1)} %bitcast.58), calls=%async_computation.4 | async-start | bytes 1572864 | tf_op jit(solution)/shard_map/all_to_all | solution.py:537
  247.5 1.0 reduce_sum.19
  248.9 1.2 fusion.79
  250.1 1.2 fusion.78
  253.8 4.3 %collective-permute-start.25 = (f32[16,1024]{1,0:T(8,128)}, f32[16,1024]{1,0:T(8,128)S(1)}, u32[]{:S(2)}, u32[]{:S(2)}) collective-permute-start(f32[16,1024]{1,0:T(8,128)} %shard_map.107.refs_2_), channel_id=1, source_target_pairs={{0,14},{1,15},{2,0},{3,1},{4,2},{5,3},{6,4},{7,5},{8,6},{9,7},{10,... | collective-permute-start | bytes 196616 | tf_op jit(solution)/shard_map/ppermute | solution.py:21
  258.1 1.6 collective-permute-start.26
  260.0 7.1 %shard_map.109 = (bf16[384,8192]{1,0:T(8,128)(2,1)}, f32[8,128]{1,0:T(8,128)}) custom-call(s32[5]{0:T(128)} %pad_add_fusion.3.where, bf16[384,1024]{1,0:T(8,128)(2,1)} %pad_maximum_fusion.2.cot, bf16[384,16]{1,0:T(8,128)(2,1)} %shard_map.108.grad, bf16[48,8192]{1,0:T(8,128)(2,1)} %fusion.down, ...), custom_call_target="tpu_custom_call", output_to_operand_aliasing={{0}: (8, {})} | custom-call | flops 1610612736 | bytes 5767168 | tf_op jit(solution)/shard_map/pallas_call | solution.py:158
  267.4 7.1 %shard_map.110 = (bf16[384,8192]{1,0:T(8,128)(2,1)}, f32[8,128]{1,0:T(8,128)}) custom-call(s32[5]{0:T(128)} %pad_add_fusion.where, bf16[384,1024]{1,0:T(8,128)(2,1)} %pad_maximum_fusion.2.cot, bf16[384,16]{1,0:T(8,128)(2,1)} %shard_map.108.grad, bf16[48,8192]{1,0:T(8,128)(2,1)} %fusion.down, ...), custom_call_target="tpu_custom_call", output_to_operand_aliasing={{0}: (8, {})} | custom-call | flops 1610612736 | bytes 5767168 | tf_op jit(solution)/shard_map/pallas_call | solution.py:158
  274.6 1.0 fusion.1
  275.5 1.3 convert_bitcast_fusion
  277.8 1.4 reshape.373
  (158 shorter events, 28.8 us)
Async XLA Ops:
  0.6 12.9 %copy-start = (bf16[3,16,1024]{2,1,0:T(8,128)(2,1)S(1)}, bf16[3,16,1024]{2,1,0:T(8,128)(2,1)}, u32[]{:S(2)}) copy-start(bf16[3,16,1024]{2,1,0:T(8,128)(2,1)} %param.13) | copy-start | bytes 294916
  0.6 55.4 %copy-start.19 = (s32[192]{0:T(256)S(1)}, s32[192]{0:T(256)}, u32[]{:S(2)}) copy-start(s32[192]{0:T(256)} %param.9) | copy-start | bytes 2308
  1.8 12.5 %collective-permute-start.3 = (bf16[128,1024]{1,0:T(8,128)(2,1)S(1)}, bf16[128,1024]{1,0:T(8,128)(2,1)S(1)}, u32[]{:S(2)}, u32[]{:S(2)}) collective-permute-start(bf16[128,1024]{1,0:T(8,128)(2,1)S(1)} %get-tuple-element.25), channel_id=1, source_target_pairs={{0,4},{1,5},{2,6},{3,7},{4,8},{5,9},{6,10},{7,11},{8,12},{9,13},{1... | collective-permute-start | bytes 786440 | tf_op jit(solution)/shard_map/ppermute | solution.py:21
  3.9 20.8 %collective-permute-start.4 = (bf16[128,1024]{1,0:T(8,128)(2,1)S(1)}, bf16[128,1024]{1,0:T(8,128)(2,1)S(1)}, u32[]{:S(2)}, u32[]{:S(2)}) collective-permute-start(bf16[128,1024]{1,0:T(8,128)(2,1)S(1)} %get-tuple-element.25), channel_id=1, source_target_pairs={{0,8},{1,9},{2,10},{3,11},{4,12},{5,13},{6,14},{7,15},{8,0},{9,1},... | collective-permute-start | bytes 786440 | tf_op jit(solution)/shard_map/ppermute | solution.py:21
  6.3 19.9 %collective-permute-start.5 = (bf16[128,1024]{1,0:T(8,128)(2,1)S(1)}, bf16[128,1024]{1,0:T(8,128)(2,1)S(1)}, u32[]{:S(2)}, u32[]{:S(2)}) collective-permute-start(bf16[128,1024]{1,0:T(8,128)(2,1)S(1)} %get-tuple-element.25), channel_id=1, source_target_pairs={{0,12},{1,13},{2,14},{3,15},{4,0},{5,1},{6,2},{7,3},{8,4},{9,5},{1... | collective-permute-start | bytes 786440 | tf_op jit(solution)/shard_map/ppermute | solution.py:21
  7.3 40.6 %collective-permute-start = (bf16[128,1024]{1,0:T(8,128)(2,1)S(1)}, bf16[128,1024]{1,0:T(8,128)(2,1)S(1)}, u32[]{:S(2)}, u32[]{:S(2)}) collective-permute-start(bf16[128,1024]{1,0:T(8,128)(2,1)S(1)} %get-tuple-element.26), channel_id=1, source_target_pairs={{0,4},{1,5},{2,6},{3,7},{4,8},{5,9},{6,10},{7,11},{8,12},{9,13},{1... | collective-permute-start | bytes 786440 | tf_op jit(solution)/shard_map/ppermute | solution.py:21
  7.7 48.4 %collective-permute-start.1 = (bf16[128,1024]{1,0:T(8,128)(2,1)S(1)}, bf16[128,1024]{1,0:T(8,128)(2,1)}, u32[]{:S(2)}, u32[]{:S(2)}) collective-permute-start(bf16[128,1024]{1,0:T(8,128)(2,1)S(1)} %get-tuple-element.26), channel_id=1, source_target_pairs={{0,8},{1,9},{2,10},{3,11},{4,12},{5,13},{6,14},{7,15},{8,0},{9,1},... | collective-permute-start | bytes 786440 | tf_op jit(solution)/shard_map/ppermute | solution.py:21
  14.3 49.3 %collective-permute-start.6 = (bf16[16,9216]{1,0:T(8,128)(2,1)S(1)}, bf16[16,9216]{1,0:T(8,128)(2,1)S(1)}, u32[]{:S(2)}, u32[]{:S(2)}) collective-permute-start(bf16[16,9216]{1,0:T(8,128)(2,1)S(1)} %pad_maximum_fusion.3), channel_id=1, source_target_pairs={{0,1},{1,2},{2,3},{3,4},{4,5},{5,6},{6,7},{7,8},{8,9},{9,10},{10,1... | collective-permute-start | bytes 884744 | tf_op jit(solution)/shard_map/ppermute | solution.py:21
  24.7 38.8 %collective-permute-start.7 = (bf16[16,9216]{1,0:T(8,128)(2,1)S(1)}, bf16[16,9216]{1,0:T(8,128)(2,1)S(1)}, u32[]{:S(2)}, u32[]{:S(2)}) collective-permute-start(bf16[16,9216]{1,0:T(8,128)(2,1)S(1)} %pad_maximum_fusion.3), channel_id=1, source_target_pairs={{0,2},{1,3},{2,4},{3,5},{4,6},{5,7},{6,8},{7,9},{8,10},{9,11},{10,... | collective-permute-start | bytes 884744 | tf_op jit(solution)/shard_map/ppermute | solution.py:21
  26.2 37.4 %collective-permute-start.8 = (bf16[16,9216]{1,0:T(8,128)(2,1)S(1)}, bf16[16,9216]{1,0:T(8,128)(2,1)S(1)}, u32[]{:S(2)}, u32[]{:S(2)}) collective-permute-start(bf16[16,9216]{1,0:T(8,128)(2,1)S(1)} %pad_maximum_fusion.3), channel_id=1, source_target_pairs={{0,3},{1,4},{2,5},{3,6},{4,7},{5,8},{6,9},{7,10},{8,11},{9,12},{10... | collective-permute-start | bytes 884744 | tf_op jit(solution)/shard_map/ppermute | solution.py:21
  47.9 15.6 %collective-permute-start.9 = (bf16[16,9216]{1,0:T(8,128)(2,1)S(1)}, bf16[16,9216]{1,0:T(8,128)(2,1)S(1)}, u32[]{:S(2)}, u32[]{:S(2)}) collective-permute-start(bf16[16,9216]{1,0:T(8,128)(2,1)S(1)} %pad_maximum_fusion.3), channel_id=1, source_target_pairs={{0,4},{1,5},{2,6},{3,7},{4,8},{5,9},{6,10},{7,11},{8,12},{9,13},{1... | collective-permute-start | bytes 884744 | tf_op jit(solution)/shard_map/ppermute | solution.py:21
  56.1 5.3 %collective-permute-start.2 = (bf16[128,1024]{1,0:T(8,128)(2,1)S(1)}, bf16[128,1024]{1,0:T(8,128)(2,1)}, u32[]{:S(2)}, u32[]{:S(2)}) collective-permute-start(bf16[128,1024]{1,0:T(8,128)(2,1)S(1)} %get-tuple-element.26), channel_id=1, source_target_pairs={{0,12},{1,13},{2,14},{3,15},{4,0},{5,1},{6,2},{7,3},{8,4},{9,5},{1... | collective-permute-start | bytes 786440 | tf_op jit(solution)/shard_map/ppermute | solution.py:21
  65.2 44.5 %all-to-all-start = ((bf16[16,64,512]{2,1,0:T(8,128)(2,1)}), bf16[16,64,512]{2,1,0:T(8,128)(2,1)S(1)}, u32[]{:S(2)}, u32[]{:S(2)}) async-start(bf16[16,64,512]{2,1,0:T(8,128)(2,1)} %shard_map.95), calls=%async_computation | async-start | bytes 2097152 | tf_op jit(solution)/shard_map/all_to_all | solution.py:473
  87.7 6.2 %copy-start.3 = (bf16[3,16,8192]{2,1,0:T(8,128)(2,1)S(1)}, bf16[3,16,8192]{2,1,0:T(8,128)(2,1)}, u32[]{:S(2)}) copy-start(bf16[3,16,8192]{2,1,0:T(8,128)(2,1)} %param.12) | copy-start | bytes 2359300
  94.4 25.7 %collective-permute-start.14 = (bf16[4,128,1024]{2,1,0:T(8,128)(2,1)}, bf16[4,128,1024]{2,1,0:T(8,128)(2,1)}, u32[]{:S(2)}, u32[]{:S(2)}) collective-permute-start(bf16[4,128,1024]{2,1,0:T(8,128)(2,1)} %pad_maximum_fusion.1.refs_2_.rest_1_), channel_id=1, source_target_pairs={{0,16},{16,0},{1,17},{17,1},{2,18},{18,2},{3,19},{19,3},{4,20},{20... | collective-permute-start | bytes 3145736 | tf_op jit(solution)/shard_map/ppermute | solution.py:94
  95.7 46.2 %collective-permute-start.12 = (bf16[4,128,1024]{2,1,0:T(8,128)(2,1)}, bf16[4,128,1024]{2,1,0:T(8,128)(2,1)}, u32[]{:S(2)}, u32[]{:S(2)}) collective-permute-start(bf16[4,128,1024]{2,1,0:T(8,128)(2,1)} %pad_maximum_fusion.refs_1_.rest_0_), channel_id=1, source_target_pairs={{0,16},{16,0},{1,17},{17,1},{2,18},{18,2},{3,19},{19,3},{4,20},{20... | collective-permute-start | bytes 3145736 | tf_op jit(solution)/shard_map/ppermute | solution.py:94
  95.9 48.3 %collective-permute-start.11 = (bf16[4,128,1024]{2,1,0:T(8,128)(2,1)}, bf16[4,128,1024]{2,1,0:T(8,128)(2,1)}, u32[]{:S(2)}, u32[]{:S(2)}) collective-permute-start(bf16[4,128,1024]{2,1,0:T(8,128)(2,1)} %pad_maximum_fusion.1.refs_2_.rest_1_), channel_id=1, source_target_pairs={{0,1},{1,0},{2,3},{3,2},{4,5},{5,4},{6,7},{7,6},{8,9},{9,8},{10,11... | collective-permute-start | bytes 3145736 | tf_op jit(solution)/shard_map/ppermute | solution.py:91
  96.5 59.3 %collective-permute-start.10 = (bf16[4,128,1024]{2,1,0:T(8,128)(2,1)}, bf16[4,128,1024]{2,1,0:T(8,128)(2,1)}, u32[]{:S(2)}, u32[]{:S(2)}) collective-permute-start(bf16[4,128,1024]{2,1,0:T(8,128)(2,1)} %pad_maximum_fusion.refs_1_.rest_0_), channel_id=1, source_target_pairs={{0,1},{1,0},{2,3},{3,2},{4,5},{5,4},{6,7},{7,6},{8,9},{9,8},{10,11... | collective-permute-start | bytes 3145736 | tf_op jit(solution)/shard_map/ppermute | solution.py:91
  96.6 67.4 %collective-permute-start.18 = (bf16[4,128,1024]{2,1,0:T(8,128)(2,1)}, bf16[4,128,1024]{2,1,0:T(8,128)(2,1)}, u32[]{:S(2)}, u32[]{:S(2)}) collective-permute-start(bf16[4,128,1024]{2,1,0:T(8,128)(2,1)} %pad_maximum_fusion.1.refs_2_.rest_1_), channel_id=1, source_target_pairs={{0,2},{1,3},{2,0},{3,1},{4,6},{5,7},{6,4},{7,5},{8,10},{9,11},{10,... | collective-permute-start | bytes 3145736 | tf_op jit(solution)/shard_map/ppermute | solution.py:91
  109.7 1.0 copy-start.1
  110.7 6.9 %copy-start.11 = (bf16[16,9216]{1,0:T(8,128)(2,1)S(1)}, bf16[16,9216]{1,0:T(8,128)(2,1)}, u32[]{:S(2)}) copy-start(bf16[16,9216]{1,0:T(8,128)(2,1)} %copy-done.10) | copy-start | bytes 884740
  110.7 6.9 %copy-start.13 = (bf16[16,9216]{1,0:T(8,128)(2,1)S(1)}, bf16[16,9216]{1,0:T(8,128)(2,1)}, u32[]{:S(2)}) copy-start(bf16[16,9216]{1,0:T(8,128)(2,1)} %copy-done.12) | copy-start | bytes 884740
  110.7 7.0 %copy-start.15 = (bf16[16,9216]{1,0:T(8,128)(2,1)S(1)}, bf16[16,9216]{1,0:T(8,128)(2,1)}, u32[]{:S(2)}) copy-start(bf16[16,9216]{1,0:T(8,128)(2,1)} %copy-done.14) | copy-start | bytes 884740
  110.7 80.5 %all-to-all-start.1 = ((bf16[16,240,512]{2,1,0:T(8,128)(2,1)}), bf16[16,240,512]{2,1,0:T(8,128)(2,1)}, u32[]{:S(2)}, u32[]{:S(2)}) async-start(bf16[16,240,512]{2,1,0:T(8,128)(2,1)} %shard_map.97), calls=%async_computation.1 | async-start | bytes 7864320 | tf_op jit(solution)/shard_map/all_to_all | solution.py:502
  118.8 24.0 %copy-start.2 = (bf16[16,64,512]{2,1,0:T(8,128)(2,1)S(1)}, bf16[16,64,512]{2,1,0:T(8,128)(2,1)}, u32[]{:S(2)}) copy-start(bf16[16,64,512]{2,1,0:T(8,128)(2,1)} %copy-done.1) | copy-start | bytes 3145732
  120.1 35.7 %collective-permute-start.15 = (bf16[4,128,1024]{2,1,0:T(8,128)(2,1)}, bf16[4,128,1024]{2,1,0:T(8,128)(2,1)S(1)}, u32[]{:S(2)}, u32[]{:S(2)}) collective-permute-start(bf16[4,128,1024]{2,1,0:T(8,128)(2,1)} %collective-permute-done.14.rest_3_), channel_id=1, source_target_pairs={{0,1},{1,0},{2,3},{3,2},{4,5},{5,4},{6,7},{7,6},{8,9},{9,8},{10,11... | collective-permute-start | bytes 3145736 | tf_op jit(solution)/shard_map/ppermute | solution.py:91
  141.9 13.9 %collective-permute-start.13 = (bf16[4,128,1024]{2,1,0:T(8,128)(2,1)}, bf16[4,128,1024]{2,1,0:T(8,128)(2,1)}, u32[]{:S(2)}, u32[]{:S(2)}) collective-permute-start(bf16[4,128,1024]{2,1,0:T(8,128)(2,1)} %collective-permute-done.12.rest_2_), channel_id=1, source_target_pairs={{0,1},{1,0},{2,3},{3,2},{4,5},{5,4},{6,7},{7,6},{8,9},{9,8},{10,11... | collective-permute-start | bytes 3145736 | tf_op jit(solution)/shard_map/ppermute | solution.py:91
  143.6 5.1 %copy-start.8 = (bf16[16,24,512]{2,1,0:T(8,128)(2,1)}, bf16[16,24,512]{2,1,0:T(8,128)(2,1)S(1)}, u32[]{:S(2)}) copy-start(bf16[16,24,512]{2,1,0:T(8,128)(2,1)S(1)} %get-tuple-element.21) | copy-start | bytes 1179652
  143.7 5.0 %copy-start.9 = (bf16[16,24,512]{2,1,0:T(8,128)(2,1)}, bf16[16,24,512]{2,1,0:T(8,128)(2,1)S(1)}, u32[]{:S(2)}) copy-start(bf16[16,24,512]{2,1,0:T(8,128)(2,1)S(1)} %get-tuple-element.22) | copy-start | bytes 1179652
  144.2 40.3 %collective-permute-start.16 = (bf16[4,128,1024]{2,1,0:T(8,128)(2,1)}, bf16[4,128,1024]{2,1,0:T(8,128)(2,1)S(1)}, u32[]{:S(2)}, u32[]{:S(2)}) collective-permute-start(bf16[4,128,1024]{2,1,0:T(8,128)(2,1)} %pad_maximum_fusion.refs_1_.rest_0_), channel_id=1, source_target_pairs={{0,2},{1,3},{2,0},{3,1},{4,6},{5,7},{6,4},{7,5},{8,10},{9,11},{10,... | collective-permute-start | bytes 3145736 | tf_op jit(solution)/shard_map/ppermute | solution.py:91
  155.8 1.0 copy-start.18
  163.9 67.5 %collective-permute-start.22 = (bf16[4,128,1024]{2,1,0:T(8,128)(2,1)}, bf16[4,128,1024]{2,1,0:T(8,128)(2,1)}, u32[]{:S(2)}, u32[]{:S(2)}) collective-permute-start(bf16[4,128,1024]{2,1,0:T(8,128)(2,1)} %shard_map.106.rest_1_), channel_id=1, source_target_pairs={{0,16},{16,0},{1,17},{17,1},{2,18},{18,2},{3,19},{19,3},{4,20},{20... | collective-permute-start | bytes 3145736 | tf_op jit(solution)/shard_map/ppermute | solution.py:94
  184.5 1.0 copy-start.4
  185.5 46.2 %collective-permute-start.20 = (bf16[4,128,1024]{2,1,0:T(8,128)(2,1)}, bf16[4,128,1024]{2,1,0:T(8,128)(2,1)}, u32[]{:S(2)}, u32[]{:S(2)}) collective-permute-start(bf16[4,128,1024]{2,1,0:T(8,128)(2,1)} %shard_map.105.rest_0_), channel_id=1, source_target_pairs={{0,16},{16,0},{1,17},{17,1},{2,18},{18,2},{3,19},{19,3},{4,20},{20... | collective-permute-start | bytes 3145736 | tf_op jit(solution)/shard_map/ppermute | solution.py:94
  192.6 31.6 %all-to-all-start.2 = ((bf16[16,24,256]{2,1,0:T(8,128)(2,1)}), bf16[16,24,256]{2,1,0:T(8,128)(2,1)S(1)}, u32[]{:S(2)}, u32[]{:S(2)}) async-start(bf16[16,24,256]{2,1,0:T(8,128)(2,1)} %broadcast_in_dim.124), calls=%async_computation.2 | async-start | bytes 393216 | tf_op jit(solution)/shard_map/all_to_all | solution.py:27
  222.2 8.9 %copy-start.5 = (bf16[4,128,1024]{2,1,0:T(8,128)(2,1)S(1)}, bf16[4,128,1024]{2,1,0:T(8,128)(2,1)}, u32[]{:S(2)}) copy-start(bf16[4,128,1024]{2,1,0:T(8,128)(2,1)} %shard_map.105.rest_0_) | copy-start | bytes 3145732
  224.2 18.0 %all-to-all-start.3 = ((f32[16,24,256]{2,1,0:T(8,128)}), f32[16,24,256]{2,1,0:T(8,128)}, u32[]{:S(2)}, u32[]{:S(2)}) async-start(f32[16,24,256]{2,1,0:T(8,128)} %bitcast.23), calls=%async_computation.3 | async-start | bytes 786432 | tf_op jit(solution)/shard_map/all_to_all | solution.py:534
  230.9 21.2 %collective-permute-start.19 = (bf16[4,128,1024]{2,1,0:T(8,128)(2,1)}, bf16[4,128,1024]{2,1,0:T(8,128)(2,1)S(1)}, u32[]{:S(2)}, u32[]{:S(2)}) collective-permute-start(bf16[4,128,1024]{2,1,0:T(8,128)(2,1)} %shard_map.106.rest_1_), channel_id=1, source_target_pairs={{0,1},{1,0},{2,3},{3,2},{4,5},{5,4},{6,7},{7,6},{8,9},{9,8},{10,11... | collective-permute-start | bytes 3145736 | tf_op jit(solution)/shard_map/ppermute | solution.py:91
  231.1 21.1 %collective-permute-start.17 = (bf16[4,128,1024]{2,1,0:T(8,128)(2,1)S(1)}, bf16[4,128,1024]{2,1,0:T(8,128)(2,1)S(1)}, u32[]{:S(2)}, u32[]{:S(2)}) collective-permute-start(bf16[4,128,1024]{2,1,0:T(8,128)(2,1)S(1)} %copy-done.5), channel_id=1, source_target_pairs={{0,1},{1,0},{2,3},{3,2},{4,5},{5,4},{6,7},{7,6},{8,9},{9,8},{10,11... | collective-permute-start | bytes 3145736 | tf_op jit(solution)/shard_map/ppermute | solution.py:91
  231.5 20.7 %collective-permute-start.23 = (bf16[4,128,1024]{2,1,0:T(8,128)(2,1)}, bf16[4,128,1024]{2,1,0:T(8,128)(2,1)}, u32[]{:S(2)}, u32[]{:S(2)}) collective-permute-start(bf16[4,128,1024]{2,1,0:T(8,128)(2,1)} %collective-permute-done.22.rest_3_), channel_id=1, source_target_pairs={{0,1},{1,0},{2,3},{3,2},{4,5},{5,4},{6,7},{7,6},{8,9},{9,8},{10,11... | collective-permute-start | bytes 3145736 | tf_op jit(solution)/shard_map/ppermute | solution.py:91
  231.6 20.6 %collective-permute-start.21 = (bf16[4,128,1024]{2,1,0:T(8,128)(2,1)}, bf16[4,128,1024]{2,1,0:T(8,128)(2,1)}, u32[]{:S(2)}, u32[]{:S(2)}) collective-permute-start(bf16[4,128,1024]{2,1,0:T(8,128)(2,1)} %collective-permute-done.20.rest_2_), channel_id=1, source_target_pairs={{0,1},{1,0},{2,3},{3,2},{4,5},{5,4},{6,7},{7,6},{8,9},{9,8},{10,11... | collective-permute-start | bytes 3145736 | tf_op jit(solution)/shard_map/ppermute | solution.py:91
  242.3 33.2 %all-to-all-start.4 = ((bf16[16,48,512]{2,1,0:T(8,128)(2,1)}), bf16[16,48,512]{2,1,0:T(8,128)(2,1)}, u32[]{:S(2)}, u32[]{:S(2)}) async-start(bf16[16,48,512]{2,1,0:T(8,128)(2,1)} %bitcast.58), calls=%async_computation.4 | async-start | bytes 1572864 | tf_op jit(solution)/shard_map/all_to_all | solution.py:537
  252.2 1.0 copy-start.6
  252.2 1.3 copy-start.7
  253.5 21.0 %collective-permute-start.24 = (f32[16,1024]{1,0:T(8,128)}, f32[16,1024]{1,0:T(8,128)S(1)}, u32[]{:S(2)}, u32[]{:S(2)}) collective-permute-start(f32[16,1024]{1,0:T(8,128)} %shard_map.107.refs_2_), channel_id=1, source_target_pairs={{0,15},{1,0},{2,1},{3,2},{4,3},{5,4},{6,5},{7,6},{8,7},{9,8},{10,9... | collective-permute-start | bytes 196616 | tf_op jit(solution)/shard_map/ppermute | solution.py:21
  253.8 20.7 %collective-permute-start.25 = (f32[16,1024]{1,0:T(8,128)}, f32[16,1024]{1,0:T(8,128)S(1)}, u32[]{:S(2)}, u32[]{:S(2)}) collective-permute-start(f32[16,1024]{1,0:T(8,128)} %shard_map.107.refs_2_), channel_id=1, source_target_pairs={{0,14},{1,15},{2,0},{3,1},{4,2},{5,3},{6,4},{7,5},{8,6},{9,7},{10,... | collective-permute-start | bytes 196616 | tf_op jit(solution)/shard_map/ppermute | solution.py:21
  258.1 16.5 %collective-permute-start.26 = (f32[16,1024]{1,0:T(8,128)}, f32[16,1024]{1,0:T(8,128)S(1)}, u32[]{:S(2)}, u32[]{:S(2)}) collective-permute-start(f32[16,1024]{1,0:T(8,128)} %shard_map.107.refs_2_), channel_id=1, source_target_pairs={{0,13},{1,14},{2,15},{3,0},{4,1},{5,2},{6,3},{7,4},{8,5},{9,6},{10... | collective-permute-start | bytes 196616 | tf_op jit(solution)/shard_map/ppermute | solution.py:21
  259.7 14.8 %collective-permute-start.27 = (f32[16,1024]{1,0:T(8,128)}, f32[16,1024]{1,0:T(8,128)S(1)}, u32[]{:S(2)}, u32[]{:S(2)}) collective-permute-start(f32[16,1024]{1,0:T(8,128)} %shard_map.107.refs_2_), channel_id=1, source_target_pairs={{0,12},{1,13},{2,14},{3,15},{4,0},{5,1},{6,2},{7,3},{8,4},{9,5},{1... | collective-permute-start | bytes 196616 | tf_op jit(solution)/shard_map/ppermute | solution.py:21
  (5 other events, 4.1 us)

commit v22 on v21

--- a/solution.py
+++ b/solution.py
@@ -469,7 +469,6 @@
 
     sent_rows = pack_rows(token_layout_row, cotangent, devices, cap, features)
     own = pieces[0]
-    sent_rows = after(sent_rows, *own[:CHUNKS], *carried)
     got_rows = lax.all_to_all(sent_rows, "blk", split_axis=0, concat_axis=0)
     recv_cot = [
         got_rows[:, k * cap : (k + 1) * cap].reshape(resident_rows, features)

time: 281 us -> 275 us (0.979)
  starting transfers between devices: 106 us -> 87.7 us
  waiting for transfers between devices: 73.9 us -> 81.2 us
    ppermute x10, waiting for transfers between devices: 19.3 us -> 41.6 us  [over(): return lax.ppermute(piece, 'blk', [(i, i ^ bit) for i in range(count)])]
    all_to_all x1, starting transfers between devices: 6.89 us -> 27 us  [local(): received = lax.all_to_all(received, 'blk', split_axis=0, concat_axis=0)]
    all_to_all x1, starting transfers between devices: 21.4 us -> 6.03 us  [local(): got_rows = lax.all_to_all(sent_rows, 'blk', split_axis=0, concat_axis=0)]
    all_to_all x1, starting transfers between devices: 18.2 us -> 5.71 us  [to_all(): return lax.all_to_all(copies, 'blk', split_axis=0, concat_axis=0)]
    all_to_all x1, waiting for transfers between devices: 11.5 us -> 0.01 us  [local(): got_rows = lax.all_to_all(sent_rows, 'blk', split_axis=0, concat_axis=0)]
    ppermute x14, starting transfers between devices: 38.8 us -> 30.2 us  [moved(): lax.ppermute(value, 'blk', [(i, (i + steps) % count) for i in range(count)])]
    all_to_all x1, waiting for transfers between devices: 3.48 us -> 0.01 us  [local(): received = lax.all_to_all(received, 'blk', split_axis=0, concat_axis=0)]
    ppermute x14, waiting for transfers between devices: 15.7 us -> 19.1 us  [moved(): lax.ppermute(value, 'blk', [(i, (i + steps) % count) for i in range(count)])]
  transfers between devices with their start and end apart: 33 -> 33, of which waited for: 8 -> 5; matrix products, arithmetic and copies ran while one was open for 12% -> 14% of each run, Pallas kernels for 18% -> 19%
where the time goes in v22:
time: 275 us; the launch traced here: 273 us
  starting transfers between devices  87.7 us (32%)
  waiting for transfers between devices  81.2 us (30%)
  Pallas kernels  51.1 us (19%)
  local copies, waits for them, and re-layouts  24.4 us (9%)
  other arithmetic  15.7 us (6%)
  matrix products  8.42 us (3%)
  between operations  4.44 us (2%)
    ppermute x10, waiting for transfers between devices, over(): return lax.ppermute(piece, 'blk', [(i, i ^ bit) for i in range(count)])  41.6 us
    ppermute x14, starting transfers between devices, moved(): lax.ppermute(value, 'blk', [(i, (i + steps) % count) for i in range(count)])  30.2 us
    pallas_call x4, Pallas kernels, write_quarter(): pl.pallas_call(quarter_kernel, grid_spec=pltpu.PrefetchScalarGridSpec(num...  28.5 us
    all_to_all x1, starting transfers between devices, local(): received = lax.all_to_all(received, 'blk', split_axis=0, concat_axis=0)  27 us
    ppermute x14, waiting for transfers between devices, moved(): lax.ppermute(value, 'blk', [(i, (i + steps) % count) for i in range(count)])  19.1 us
    ppermute x4, waiting for transfers between devices, groups(): return lax.ppermute(piece, 'groups', [(0, 1), (1, 0)])  17.8 us
    pallas_call x1, Pallas kernels, local(): shares = hidden_call(received, received, rows_all, place_all, starts)  8.73 us
    pallas_call x1, Pallas kernels, local(): down_f = down_call(received, grad_all, rows_all, place_all, starts)  6.77 us
  transfers between devices with their start and end apart: 33, of which 5 were waited for; matrix products, arithmetic and copies ran while one was open for 14% of the time, Pallas kernels for 19%

profile of v22, /device:TPU:1, one launch (start us, length us, event | category | flops | bytes accessed | tf_op | source)
XLA Modules:
  0.0 273.0 jit_solution(3029823458198270539)
XLA Ops:
  0.7 1.9 constant_dynamic-slice_fusion
  2.6 2.1 collective-permute-start.4
  4.7 2.3 collective-permute-start.5
  7.0 1.3 collective-permute-start.9
  8.3 1.9 collective-permute-start.10
  10.3 1.3 concatenate.34
  11.5 2.6 shard_map.94
  14.2 6.0 %all-to-all-start = ((bf16[16,64,512]{2,1,0:T(8,128)(2,1)}), bf16[16,64,512]{2,1,0:T(8,128)(2,1)S(1)}, u32[]{:S(2)}, u32[]{:S(2)}) async-start(bf16[16,64,512]{2,1,0:T(8,128)(2,1)} %shard_map.94), calls=%async_computation | async-start | bytes 2097152 | tf_op jit(solution)/shard_map/all_to_all | solution.py:472
  27.9 1.2 fusion.70
  30.1 3.2 %collective-permute-start.6 = (bf16[128,1024]{1,0:T(8,128)(2,1)}, bf16[128,1024]{1,0:T(8,128)(2,1)}, u32[]{:S(2)}, u32[]{:S(2)}) collective-permute-start(bf16[128,1024]{1,0:T(8,128)(2,1)} %get-tuple-element.22), channel_id=1, source_target_pairs={{0,12},{1,13},{2,14},{3,15},{4,0},{5,1},{6,2},{7,3},{8,4},{9,5},{1... | collective-permute-start | bytes 786440 | tf_op jit(solution)/shard_map/ppermute | solution.py:21
  34.0 19.1 %collective-permute-done.9 = bf16[128,1024]{1,0:T(8,128)(2,1)} collective-permute-done((bf16[128,1024]{1,0:T(8,128)(2,1)}, bf16[128,1024]{1,0:T(8,128)(2,1)}, u32[]{:S(2)}, u32[]{:S(2)}) %collective-permute-start.9) | collective-permute-done | bytes 262176 | tf_op jit(solution)/shard_map/ppermute | solution.py:21
  53.1 1.8 collective-permute-start
  56.2 4.5 %shard_map.95.refs_0_ = bf16[16,240,512]{2,1,0:T(8,128)(2,1)} custom-call(bf16[192,8192]{1,0:T(8,128)(2,1)} %act.1, bf16[48,8192]{1,0:T(8,128)(2,1)} %bitcast.50), custom_call_target="tpu_custom_call" | custom-call | bytes 7864320 | tf_op jit(solution)/shard_map/pallas_call | solution.py:275
  60.8 10.7 %collective-permute-start.1 = (bf16[16,9216]{1,0:T(8,128)(2,1)S(1)}, bf16[16,9216]{1,0:T(8,128)(2,1)}, u32[]{:S(2)}, u32[]{:S(2)}) collective-permute-start(bf16[16,9216]{1,0:T(8,128)(2,1)S(1)} %pad_maximum_fusion.3), channel_id=1, source_target_pairs={{0,2},{1,3},{2,4},{3,5},{4,6},{5,7},{6,8},{7,9},{8,10},{9,11},{10,... | collective-permute-start | bytes 884744 | tf_op jit(solution)/shard_map/ppermute | solution.py:21
  71.5 2.4 pad_maximum_fusion.1.rest_1_
  74.2 1.3 collective-permute-start.14
  75.5 2.3 pad_maximum_fusion.rest_0_
  78.8 27.0 %all-to-all-start.1 = ((bf16[16,240,512]{2,1,0:T(8,128)(2,1)}), bf16[16,240,512]{2,1,0:T(8,128)(2,1)}, u32[]{:S(2)}, u32[]{:S(2)}) async-start(bf16[16,240,512]{2,1,0:T(8,128)(2,1)} %shard_map.96), calls=%async_computation.1 | async-start | bytes 7864320 | tf_op jit(solution)/shard_map/all_to_all | solution.py:501
  106.3 1.0 constant_dynamic-update-slice_fusion.2
  108.0 1.0 constant_dynamic-update-slice_fusion.1
  109.0 1.5 collective-permute-start.18
  110.5 1.0 constant_dynamic-update-slice_fusion
  111.7 1.3 fusion.down
  113.0 17.8 %collective-permute-done.12.rest_2_ = bf16[4,128,1024]{2,1,0:T(8,128)(2,1)} collective-permute-done((bf16[4,128,1024]{2,1,0:T(8,128)(2,1)}, bf16[4,128,1024]{2,1,0:T(8,128)(2,1)}, u32[]{:S(2)}, u32[]{:S(2)}) %collective-permute-start.12) | collective-permute-done | bytes 1048608 | tf_op jit(solution)/shard_map/ppermute | solution.py:94
  130.8 1.2 collective-permute-start.13
  133.4 1.7 collective-permute-start.16
  137.1 1.0 pad_maximum_fusion.2.cot
  138.2 7.1 %shard_map.98 = (bf16[384,8192]{1,0:T(8,128)(2,1)}, f32[8,128]{1,0:T(8,128)}) custom-call(s32[5]{0:T(128)} %pad_add_fusion.2.where, bf16[384,1024]{1,0:T(8,128)(2,1)} %pad_maximum_fusion.2.cot, bf16[384,16]{1,0:T(8,128)(2,1)} %copy.43.grad.refs_0_, bf16[48,8192]{1,0:T(8,128)(2,1)} %fusion.down, bf16[4,128,1024]{2,1,0:T(8,128)(2,1)} %pad_maximum_fusion.rest_0_, ...), custom_call_target="tpu_custom_call" | custom-call | flops 1610612736 | bytes 5767168 | tf_op jit(solution)/shard_map/pallas_call | solution.py:158
  146.3 7.1 %shard_map.99 = (bf16[384,8192]{1,0:T(8,128)(2,1)}, f32[8,128]{1,0:T(8,128)}) custom-call(s32[5]{0:T(128)} %pad_add_fusion.1.where, bf16[384,1024]{1,0:T(8,128)(2,1)} %pad_maximum_fusion.2.cot, bf16[384,16]{1,0:T(8,128)(2,1)} %copy.43.grad.refs_0_, bf16[48,8192]{1,0:T(8,128)(2,1)} %fusion.down, ...), custom_call_target="tpu_custom_call", output_to_operand_aliasing={{0}: (8, {})} | custom-call | flops 1610612736 | bytes 5767168 | tf_op jit(solution)/shard_map/pallas_call | solution.py:158
  153.4 12.3 %collective-permute-done.18.refs_0_ = bf16[4,128,1024]{2,1,0:T(8,128)(2,1)} collective-permute-done((bf16[4,128,1024]{2,1,0:T(8,128)(2,1)}, bf16[4,128,1024]{2,1,0:T(8,128)(2,1)}, u32[]{:S(2)}, u32[]{:S(2)}) %collective-permute-start.18) | collective-permute-done | bytes 1048608 | tf_op jit(solution)/shard_map/ppermute | solution.py:91
  165.9 29.3 %collective-permute-done.16.refs_0_ = bf16[4,128,1024]{2,1,0:T(8,128)(2,1)S(1)} collective-permute-done((bf16[4,128,1024]{2,1,0:T(8,128)(2,1)}, bf16[4,128,1024]{2,1,0:T(8,128)(2,1)S(1)}, u32[]{:S(2)}, u32[]{:S(2)}) %collective-permute-start.16) | collective-permute-done | bytes 1048608 | tf_op jit(solution)/shard_map/ppermute | solution.py:91
  197.5 1.4 broadcast_in_dim.124
  198.9 5.7 %all-to-all-start.2 = ((bf16[16,24,256]{2,1,0:T(8,128)(2,1)}), bf16[16,24,256]{2,1,0:T(8,128)(2,1)S(1)}, u32[]{:S(2)}, u32[]{:S(2)}) async-start(bf16[16,24,256]{2,1,0:T(8,128)(2,1)} %broadcast_in_dim.124), calls=%async_computation.2 | async-start | bytes 393216 | tf_op jit(solution)/shard_map/all_to_all | solution.py:27
  207.3 8.7 %shard_map.101.refs_1_ = f32[256,384]{1,0:T(8,128)} custom-call(bf16[16,240,512]{2,1,0:T(8,128)(2,1)} %all-to-all-done.1.refs_1_.act.maps, bf16[16,240,512]{2,1,0:T(8,128)(2,1)} %all-to-all-done.1.refs_1_.act.maps, s32[1,3072]{1,0:T(1,128)} %reshape.374.rows.refs_0_, s32[1,3072]{1,0:T(1,128)} %shard_map.100.spots, s32[32,1]{1,0:T(8,128)} %copy.48.starts), custom_call_target="tpu_custom_call" | custom-call | flops 2415919104 | bytes 3145728 | tf_op jit(solution)/shard_map/pallas_call | solution.py:529
  216.0 2.0 copy.50
  218.0 6.0 %all-to-all-start.3 = ((f32[16,24,256]{2,1,0:T(8,128)}), f32[16,24,256]{2,1,0:T(8,128)}, u32[]{:S(2)}, u32[]{:S(2)}) async-start(f32[16,24,256]{2,1,0:T(8,128)} %bitcast.23), calls=%async_computation.3 | async-start | bytes 786432 | tf_op jit(solution)/shard_map/all_to_all | solution.py:533
  226.7 6.8 %shard_map.103.refs_1_ = bf16[768,512]{1,0:T(8,128)(2,1)} custom-call(bf16[16,240,512]{2,1,0:T(8,128)(2,1)} %all-to-all-done.1.refs_1_.act.maps, bf16[256,384]{1,0:T(8,128)(2,1)} %bitcast.63, s32[1,3072]{1,0:T(1,128)} %shard_map.102.rows, s32[1,3072]{1,0:T(1,128)} %shard_map.100.spots, s32[32,1]{1,0:T(8,128)} %copy.48.starts), custom_call_target="tpu_custom_call" | custom-call | flops 2415919104 | bytes 3145728 | tf_op jit(solution)/shard_map/pallas_call | solution.py:531
  233.4 2.6 all-to-all-done.3
  236.1 4.4 %all-to-all-start.4 = ((bf16[16,48,512]{2,1,0:T(8,128)(2,1)}), bf16[16,48,512]{2,1,0:T(8,128)(2,1)}, u32[]{:S(2)}, u32[]{:S(2)}) async-start(bf16[16,48,512]{2,1,0:T(8,128)(2,1)} %bitcast.58), calls=%async_computation.4 | async-start | bytes 1572864 | tf_op jit(solution)/shard_map/all_to_all | solution.py:536
  241.3 1.0 reduce_sum.19
  242.7 1.2 fusion.79
  243.9 1.2 fusion.78
  247.6 4.3 %collective-permute-start.25 = (f32[16,1024]{1,0:T(8,128)}, f32[16,1024]{1,0:T(8,128)S(1)}, u32[]{:S(2)}, u32[]{:S(2)}) collective-permute-start(f32[16,1024]{1,0:T(8,128)} %shard_map.106.refs_2_), channel_id=1, source_target_pairs={{0,14},{1,15},{2,0},{3,1},{4,2},{5,3},{6,4},{7,5},{8,6},{9,7},{10,... | collective-permute-start | bytes 196616 | tf_op jit(solution)/shard_map/ppermute | solution.py:21
  251.9 1.6 collective-permute-start.26
  253.8 7.1 %shard_map.108 = (bf16[384,8192]{1,0:T(8,128)(2,1)}, f32[8,128]{1,0:T(8,128)}) custom-call(s32[5]{0:T(128)} %pad_add_fusion.3.where, bf16[384,1024]{1,0:T(8,128)(2,1)} %pad_maximum_fusion.2.cot, bf16[384,16]{1,0:T(8,128)(2,1)} %shard_map.107.grad, bf16[48,8192]{1,0:T(8,128)(2,1)} %fusion.down, ...), custom_call_target="tpu_custom_call", output_to_operand_aliasing={{0}: (8, {})} | custom-call | flops 1610612736 | bytes 5767168 | tf_op jit(solution)/shard_map/pallas_call | solution.py:158
  261.2 7.1 %shard_map.109 = (bf16[384,8192]{1,0:T(8,128)(2,1)}, f32[8,128]{1,0:T(8,128)}) custom-call(s32[5]{0:T(128)} %pad_add_fusion.where, bf16[384,1024]{1,0:T(8,128)(2,1)} %pad_maximum_fusion.2.cot, bf16[384,16]{1,0:T(8,128)(2,1)} %shard_map.107.grad, bf16[48,8192]{1,0:T(8,128)(2,1)} %fusion.down, ...), custom_call_target="tpu_custom_call", output_to_operand_aliasing={{0}: (8, {})} | custom-call | flops 1610612736 | bytes 5767168 | tf_op jit(solution)/shard_map/pallas_call | solution.py:158
  269.3 1.3 convert_bitcast_fusion
  271.6 1.4 reshape.373
  (149 shorter events, 28.2 us)
Async XLA Ops:
  0.6 25.0 %copy-start = (bf16[3,16,1024]{2,1,0:T(8,128)(2,1)S(1)}, bf16[3,16,1024]{2,1,0:T(8,128)(2,1)}, u32[]{:S(2)}) copy-start(bf16[3,16,1024]{2,1,0:T(8,128)(2,1)} %param.13) | copy-start | bytes 294916
  2.6 71.3 %collective-permute-start.4 = (bf16[128,1024]{1,0:T(8,128)(2,1)}, bf16[128,1024]{1,0:T(8,128)(2,1)}, u32[]{:S(2)}, u32[]{:S(2)}) collective-permute-start(bf16[128,1024]{1,0:T(8,128)(2,1)} %get-tuple-element.22), channel_id=1, source_target_pairs={{0,4},{1,5},{2,6},{3,7},{4,8},{5,9},{6,10},{7,11},{8,12},{9,13},{1... | collective-permute-start | bytes 786440 | tf_op jit(solution)/shard_map/ppermute | solution.py:21
  4.7 69.5 %collective-permute-start.5 = (bf16[128,1024]{1,0:T(8,128)(2,1)}, bf16[128,1024]{1,0:T(8,128)(2,1)}, u32[]{:S(2)}, u32[]{:S(2)}) collective-permute-start(bf16[128,1024]{1,0:T(8,128)(2,1)} %get-tuple-element.22), channel_id=1, source_target_pairs={{0,8},{1,9},{2,10},{3,11},{4,12},{5,13},{6,14},{7,15},{8,0},{9,1},... | collective-permute-start | bytes 786440 | tf_op jit(solution)/shard_map/ppermute | solution.py:21
  7.0 23.1 %collective-permute-start.8 = (bf16[128,1024]{1,0:T(8,128)(2,1)}, bf16[128,1024]{1,0:T(8,128)(2,1)}, u32[]{:S(2)}, u32[]{:S(2)}) collective-permute-start(bf16[128,1024]{1,0:T(8,128)(2,1)} %get-tuple-element.21), channel_id=1, source_target_pairs={{0,4},{1,5},{2,6},{3,7},{4,8},{5,9},{6,10},{7,11},{8,12},{9,13},{1... | collective-permute-start | bytes 786440 | tf_op jit(solution)/shard_map/ppermute | solution.py:21
  7.0 46.1 %collective-permute-start.9 = (bf16[128,1024]{1,0:T(8,128)(2,1)}, bf16[128,1024]{1,0:T(8,128)(2,1)}, u32[]{:S(2)}, u32[]{:S(2)}) collective-permute-start(bf16[128,1024]{1,0:T(8,128)(2,1)} %get-tuple-element.21), channel_id=1, source_target_pairs={{0,8},{1,9},{2,10},{3,11},{4,12},{5,13},{6,14},{7,15},{8,0},{9,1},... | collective-permute-start | bytes 786440 | tf_op jit(solution)/shard_map/ppermute | solution.py:21
  8.3 52.4 %collective-permute-start.10 = (bf16[128,1024]{1,0:T(8,128)(2,1)}, bf16[128,1024]{1,0:T(8,128)(2,1)}, u32[]{:S(2)}, u32[]{:S(2)}) collective-permute-start(bf16[128,1024]{1,0:T(8,128)(2,1)} %get-tuple-element.21), channel_id=1, source_target_pairs={{0,12},{1,13},{2,14},{3,15},{4,0},{5,1},{6,2},{7,3},{8,4},{9,5},{1... | collective-permute-start | bytes 786440 | tf_op jit(solution)/shard_map/ppermute | solution.py:21
  11.5 8.7 %copy-start.15 = (s32[32]{0:T(128)S(1)}, s32[32]{0:T(128)}, u32[]{:S(2)}) copy-start(s32[32]{0:T(128)} %param.10) | copy-start | bytes 388
  11.5 13.4 %copy-start.3 = (bf16[3,16,8192]{2,1,0:T(8,128)(2,1)S(1)}, bf16[3,16,8192]{2,1,0:T(8,128)(2,1)}, u32[]{:S(2)}) copy-start(bf16[3,16,8192]{2,1,0:T(8,128)(2,1)} %param.12) | copy-start | bytes 2359300
  14.2 63.7 %all-to-all-start = ((bf16[16,64,512]{2,1,0:T(8,128)(2,1)}), bf16[16,64,512]{2,1,0:T(8,128)(2,1)S(1)}, u32[]{:S(2)}, u32[]{:S(2)}) async-start(bf16[16,64,512]{2,1,0:T(8,128)(2,1)} %shard_map.94), calls=%async_computation | async-start | bytes 2097152 | tf_op jit(solution)/shard_map/all_to_all | solution.py:472
  20.8 5.7 %copy-start.13 = (s32[32]{0:T(128)}, s32[32]{0:T(128)S(1)}, u32[]{:S(2)}) copy-start(s32[32]{0:T(128)S(1)} %get-tuple-element.20) | copy-start | bytes 388
  30.1 44.1 %collective-permute-start.6 = (bf16[128,1024]{1,0:T(8,128)(2,1)}, bf16[128,1024]{1,0:T(8,128)(2,1)}, u32[]{:S(2)}, u32[]{:S(2)}) collective-permute-start(bf16[128,1024]{1,0:T(8,128)(2,1)} %get-tuple-element.22), channel_id=1, source_target_pairs={{0,12},{1,13},{2,14},{3,15},{4,0},{5,1},{6,2},{7,3},{8,4},{9,5},{1... | collective-permute-start | bytes 786440 | tf_op jit(solution)/shard_map/ppermute | solution.py:21
  53.1 52.7 %collective-permute-start = (bf16[16,9216]{1,0:T(8,128)(2,1)S(1)}, bf16[16,9216]{1,0:T(8,128)(2,1)S(1)}, u32[]{:S(2)}, u32[]{:S(2)}) collective-permute-start(bf16[16,9216]{1,0:T(8,128)(2,1)S(1)} %pad_maximum_fusion.3), channel_id=1, source_target_pairs={{0,1},{1,2},{2,3},{3,4},{4,5},{5,6},{6,7},{7,8},{8,9},{9,10},{10,1... | collective-permute-start | bytes 884744 | tf_op jit(solution)/shard_map/ppermute | solution.py:21
  60.8 45.3 %collective-permute-start.1 = (bf16[16,9216]{1,0:T(8,128)(2,1)S(1)}, bf16[16,9216]{1,0:T(8,128)(2,1)}, u32[]{:S(2)}, u32[]{:S(2)}) collective-permute-start(bf16[16,9216]{1,0:T(8,128)(2,1)S(1)} %pad_maximum_fusion.3), channel_id=1, source_target_pairs={{0,2},{1,3},{2,4},{3,5},{4,6},{5,7},{6,8},{7,9},{8,10},{9,11},{10,... | collective-permute-start | bytes 884744 | tf_op jit(solution)/shard_map/ppermute | solution.py:21
  73.9 33.4 %collective-permute-start.2 = (bf16[16,9216]{1,0:T(8,128)(2,1)S(1)}, bf16[16,9216]{1,0:T(8,128)(2,1)}, u32[]{:S(2)}, u32[]{:S(2)}) collective-permute-start(bf16[16,9216]{1,0:T(8,128)(2,1)S(1)} %pad_maximum_fusion.3), channel_id=1, source_target_pairs={{0,3},{1,4},{2,5},{3,6},{4,7},{5,8},{6,9},{7,10},{8,11},{9,12},{10... | collective-permute-start | bytes 884744 | tf_op jit(solution)/shard_map/ppermute | solution.py:21
  74.2 34.8 %collective-permute-start.3 = (bf16[16,9216]{1,0:T(8,128)(2,1)S(1)}, bf16[16,9216]{1,0:T(8,128)(2,1)}, u32[]{:S(2)}, u32[]{:S(2)}) collective-permute-start(bf16[16,9216]{1,0:T(8,128)(2,1)S(1)} %pad_maximum_fusion.3), channel_id=1, source_target_pairs={{0,4},{1,5},{2,6},{3,7},{4,8},{5,9},{6,10},{7,11},{8,12},{9,13},{1... | collective-permute-start | bytes 884744 | tf_op jit(solution)/shard_map/ppermute | solution.py:21
  74.2 57.8 %collective-permute-start.14 = (bf16[4,128,1024]{2,1,0:T(8,128)(2,1)}, bf16[4,128,1024]{2,1,0:T(8,128)(2,1)}, u32[]{:S(2)}, u32[]{:S(2)}) collective-permute-start(bf16[4,128,1024]{2,1,0:T(8,128)(2,1)} %pad_maximum_fusion.1.rest_1_), channel_id=1, source_target_pairs={{0,16},{16,0},{1,17},{17,1},{2,18},{18,2},{3,19},{19,3},{4,20},{20... | collective-permute-start | bytes 3145736 | tf_op jit(solution)/shard_map/ppermute | solution.py:94
  77.8 1.0 copy-start.1
  78.8 118.7 %all-to-all-start.1 = ((bf16[16,240,512]{2,1,0:T(8,128)(2,1)}), bf16[16,240,512]{2,1,0:T(8,128)(2,1)}, u32[]{:S(2)}, u32[]{:S(2)}) async-start(bf16[16,240,512]{2,1,0:T(8,128)(2,1)} %shard_map.96), calls=%async_computation.1 | async-start | bytes 7864320 | tf_op jit(solution)/shard_map/all_to_all | solution.py:501
  105.8 5.7 %copy-start.11 = (pred[48]{0:T(512)(128)(4,1)S(1)}, pred[48]{0:T(512)(128)(4,1)}, u32[]{:S(2)}) copy-start(pred[48]{0:T(512)(128)(4,1)} %broadcast_compare_fusion.2) | copy-start | bytes 148
  105.8 27.6 %collective-permute-start.11 = (bf16[4,128,1024]{2,1,0:T(8,128)(2,1)}, bf16[4,128,1024]{2,1,0:T(8,128)(2,1)}, u32[]{:S(2)}, u32[]{:S(2)}) collective-permute-start(bf16[4,128,1024]{2,1,0:T(8,128)(2,1)} %pad_maximum_fusion.1.rest_1_), channel_id=1, source_target_pairs={{0,1},{1,0},{2,3},{3,2},{4,5},{5,4},{6,7},{7,6},{8,9},{9,8},{10,11... | collective-permute-start | bytes 3145736 | tf_op jit(solution)/shard_map/ppermute | solution.py:91
  106.1 24.8 %collective-permute-start.12 = (bf16[4,128,1024]{2,1,0:T(8,128)(2,1)}, bf16[4,128,1024]{2,1,0:T(8,128)(2,1)}, u32[]{:S(2)}, u32[]{:S(2)}) collective-permute-start(bf16[4,128,1024]{2,1,0:T(8,128)(2,1)} %pad_maximum_fusion.rest_0_), channel_id=1, source_target_pairs={{0,16},{16,0},{1,17},{17,1},{2,18},{18,2},{3,19},{19,3},{4,20},{20... | collective-permute-start | bytes 3145736 | tf_op jit(solution)/shard_map/ppermute | solution.py:94
  107.3 37.9 %collective-permute-start.7 = (bf16[4,128,1024]{2,1,0:T(8,128)(2,1)}, bf16[4,128,1024]{2,1,0:T(8,128)(2,1)}, u32[]{:S(2)}, u32[]{:S(2)}) collective-permute-start(bf16[4,128,1024]{2,1,0:T(8,128)(2,1)} %pad_maximum_fusion.rest_0_), channel_id=1, source_target_pairs={{0,1},{1,0},{2,3},{3,2},{4,5},{5,4},{6,7},{7,6},{8,9},{9,8},{10,11... | collective-permute-start | bytes 3145736 | tf_op jit(solution)/shard_map/ppermute | solution.py:91
  109.0 56.7 %collective-permute-start.18 = (bf16[4,128,1024]{2,1,0:T(8,128)(2,1)}, bf16[4,128,1024]{2,1,0:T(8,128)(2,1)}, u32[]{:S(2)}, u32[]{:S(2)}) collective-permute-start(bf16[4,128,1024]{2,1,0:T(8,128)(2,1)} %pad_maximum_fusion.1.rest_1_), channel_id=1, source_target_pairs={{0,2},{1,3},{2,0},{3,1},{4,6},{5,7},{6,4},{7,5},{8,10},{9,11},{10,... | collective-permute-start | bytes 3145736 | tf_op jit(solution)/shard_map/ppermute | solution.py:91
  111.7 20.3 %copy-start.2 = (bf16[16,64,512]{2,1,0:T(8,128)(2,1)S(1)}, bf16[16,64,512]{2,1,0:T(8,128)(2,1)}, u32[]{:S(2)}) copy-start(bf16[16,64,512]{2,1,0:T(8,128)(2,1)} %copy-done.1) | copy-start | bytes 3145732
  130.8 14.5 %collective-permute-start.13 = (bf16[4,128,1024]{2,1,0:T(8,128)(2,1)}, bf16[4,128,1024]{2,1,0:T(8,128)(2,1)S(1)}, u32[]{:S(2)}, u32[]{:S(2)}) collective-permute-start(bf16[4,128,1024]{2,1,0:T(8,128)(2,1)} %collective-permute-done.12.rest_2_), channel_id=1, source_target_pairs={{0,1},{1,0},{2,3},{3,2},{4,5},{5,4},{6,7},{7,6},{8,9},{9,8},{10,11... | collective-permute-start | bytes 3145736 | tf_op jit(solution)/shard_map/ppermute | solution.py:91
  132.0 13.3 %collective-permute-start.15 = (bf16[4,128,1024]{2,1,0:T(8,128)(2,1)}, bf16[4,128,1024]{2,1,0:T(8,128)(2,1)}, u32[]{:S(2)}, u32[]{:S(2)}) collective-permute-start(bf16[4,128,1024]{2,1,0:T(8,128)(2,1)} %collective-permute-done.14.rest_3_), channel_id=1, source_target_pairs={{0,1},{1,0},{2,3},{3,2},{4,5},{5,4},{6,7},{7,6},{8,9},{9,8},{10,11... | collective-permute-start | bytes 3145736 | tf_op jit(solution)/shard_map/ppermute | solution.py:91
  132.9 5.3 %copy-start.8 = (bf16[16,24,512]{2,1,0:T(8,128)(2,1)}, bf16[16,24,512]{2,1,0:T(8,128)(2,1)S(1)}, u32[]{:S(2)}) copy-start(bf16[16,24,512]{2,1,0:T(8,128)(2,1)S(1)} %get-tuple-element.24) | copy-start | bytes 1179652
  132.9 5.3 %copy-start.9 = (bf16[16,24,512]{2,1,0:T(8,128)(2,1)}, bf16[16,24,512]{2,1,0:T(8,128)(2,1)S(1)}, u32[]{:S(2)}) copy-start(bf16[16,24,512]{2,1,0:T(8,128)(2,1)S(1)} %get-tuple-element.23) | copy-start | bytes 1179652
  133.4 61.8 %collective-permute-start.16 = (bf16[4,128,1024]{2,1,0:T(8,128)(2,1)}, bf16[4,128,1024]{2,1,0:T(8,128)(2,1)S(1)}, u32[]{:S(2)}, u32[]{:S(2)}) collective-permute-start(bf16[4,128,1024]{2,1,0:T(8,128)(2,1)} %pad_maximum_fusion.rest_0_), channel_id=1, source_target_pairs={{0,2},{1,3},{2,0},{3,1},{4,6},{5,7},{6,4},{7,5},{8,10},{9,11},{10,... | collective-permute-start | bytes 3145736 | tf_op jit(solution)/shard_map/ppermute | solution.py:91
  145.3 1.0 copy-start.10
  165.7 59.6 %collective-permute-start.22 = (bf16[4,128,1024]{2,1,0:T(8,128)(2,1)}, bf16[4,128,1024]{2,1,0:T(8,128)(2,1)}, u32[]{:S(2)}, u32[]{:S(2)}) collective-permute-start(bf16[4,128,1024]{2,1,0:T(8,128)(2,1)} %shard_map.105.rest_1_), channel_id=1, source_target_pairs={{0,16},{16,0},{1,17},{17,1},{2,18},{18,2},{3,19},{19,3},{4,20},{20... | collective-permute-start | bytes 3145736 | tf_op jit(solution)/shard_map/ppermute | solution.py:94
  196.2 29.3 %collective-permute-start.20 = (bf16[4,128,1024]{2,1,0:T(8,128)(2,1)}, bf16[4,128,1024]{2,1,0:T(8,128)(2,1)}, u32[]{:S(2)}, u32[]{:S(2)}) collective-permute-start(bf16[4,128,1024]{2,1,0:T(8,128)(2,1)} %shard_map.104.rest_0_), channel_id=1, source_target_pairs={{0,16},{16,0},{1,17},{17,1},{2,18},{18,2},{3,19},{19,3},{4,20},{20... | collective-permute-start | bytes 3145736 | tf_op jit(solution)/shard_map/ppermute | solution.py:94
  197.4 7.1 %copy-start.14 = (s32[32]{0:T(128)S(1)}, s32[32]{0:T(128)}, u32[]{:S(2)}) copy-start(s32[32]{0:T(128)} %copy-done.13) | copy-start | bytes 388
  198.9 19.2 %all-to-all-start.2 = ((bf16[16,24,256]{2,1,0:T(8,128)(2,1)}), bf16[16,24,256]{2,1,0:T(8,128)(2,1)S(1)}, u32[]{:S(2)}, u32[]{:S(2)}) async-start(bf16[16,24,256]{2,1,0:T(8,128)(2,1)} %broadcast_in_dim.124), calls=%async_computation.2 | async-start | bytes 393216 | tf_op jit(solution)/shard_map/all_to_all | solution.py:27
  216.0 8.9 %copy-start.5 = (bf16[4,128,1024]{2,1,0:T(8,128)(2,1)S(1)}, bf16[4,128,1024]{2,1,0:T(8,128)(2,1)}, u32[]{:S(2)}) copy-start(bf16[4,128,1024]{2,1,0:T(8,128)(2,1)} %shard_map.104.rest_0_) | copy-start | bytes 3145732
  218.0 18.0 %all-to-all-start.3 = ((f32[16,24,256]{2,1,0:T(8,128)}), f32[16,24,256]{2,1,0:T(8,128)}, u32[]{:S(2)}, u32[]{:S(2)}) async-start(f32[16,24,256]{2,1,0:T(8,128)} %bitcast.23), calls=%async_computation.3 | async-start | bytes 786432 | tf_op jit(solution)/shard_map/all_to_all | solution.py:533
  224.8 21.2 %collective-permute-start.19 = (bf16[4,128,1024]{2,1,0:T(8,128)(2,1)}, bf16[4,128,1024]{2,1,0:T(8,128)(2,1)S(1)}, u32[]{:S(2)}, u32[]{:S(2)}) collective-permute-start(bf16[4,128,1024]{2,1,0:T(8,128)(2,1)} %shard_map.105.rest_1_), channel_id=1, source_target_pairs={{0,1},{1,0},{2,3},{3,2},{4,5},{5,4},{6,7},{7,6},{8,9},{9,8},{10,11... | collective-permute-start | bytes 3145736 | tf_op jit(solution)/shard_map/ppermute | solution.py:91
  225.0 21.0 %collective-permute-start.17 = (bf16[4,128,1024]{2,1,0:T(8,128)(2,1)S(1)}, bf16[4,128,1024]{2,1,0:T(8,128)(2,1)S(1)}, u32[]{:S(2)}, u32[]{:S(2)}) collective-permute-start(bf16[4,128,1024]{2,1,0:T(8,128)(2,1)S(1)} %copy-done.5), channel_id=1, source_target_pairs={{0,1},{1,0},{2,3},{3,2},{4,5},{5,4},{6,7},{7,6},{8,9},{9,8},{10,11... | collective-permute-start | bytes 3145736 | tf_op jit(solution)/shard_map/ppermute | solution.py:91
  225.3 20.7 %collective-permute-start.23 = (bf16[4,128,1024]{2,1,0:T(8,128)(2,1)}, bf16[4,128,1024]{2,1,0:T(8,128)(2,1)}, u32[]{:S(2)}, u32[]{:S(2)}) collective-permute-start(bf16[4,128,1024]{2,1,0:T(8,128)(2,1)} %collective-permute-done.22.rest_3_), channel_id=1, source_target_pairs={{0,1},{1,0},{2,3},{3,2},{4,5},{5,4},{6,7},{7,6},{8,9},{9,8},{10,11... | collective-permute-start | bytes 3145736 | tf_op jit(solution)/shard_map/ppermute | solution.py:91
  225.5 20.5 %collective-permute-start.21 = (bf16[4,128,1024]{2,1,0:T(8,128)(2,1)}, bf16[4,128,1024]{2,1,0:T(8,128)(2,1)}, u32[]{:S(2)}, u32[]{:S(2)}) collective-permute-start(bf16[4,128,1024]{2,1,0:T(8,128)(2,1)} %collective-permute-done.20.rest_2_), channel_id=1, source_target_pairs={{0,1},{1,0},{2,3},{3,2},{4,5},{5,4},{6,7},{7,6},{8,9},{9,8},{10,11... | collective-permute-start | bytes 3145736 | tf_op jit(solution)/shard_map/ppermute | solution.py:91
  233.4 7.7 %copy-start.12 = (pred[4]{0:T(512)(128)(4,1)S(1)}, pred[4]{0:T(512)(128)(4,1)}, u32[]{:S(2)}) copy-start(pred[4]{0:T(512)(128)(4,1)} %get-tuple-element.30) | copy-start | bytes 16
  236.1 33.2 %all-to-all-start.4 = ((bf16[16,48,512]{2,1,0:T(8,128)(2,1)}), bf16[16,48,512]{2,1,0:T(8,128)(2,1)}, u32[]{:S(2)}, u32[]{:S(2)}) async-start(bf16[16,48,512]{2,1,0:T(8,128)(2,1)} %bitcast.58), calls=%async_computation.4 | async-start | bytes 1572864 | tf_op jit(solution)/shard_map/all_to_all | solution.py:536
  246.0 1.0 copy-start.6
  246.0 1.4 copy-start.7
  247.3 21.0 %collective-permute-start.24 = (f32[16,1024]{1,0:T(8,128)}, f32[16,1024]{1,0:T(8,128)S(1)}, u32[]{:S(2)}, u32[]{:S(2)}) collective-permute-start(f32[16,1024]{1,0:T(8,128)} %shard_map.106.refs_2_), channel_id=1, source_target_pairs={{0,15},{1,0},{2,1},{3,2},{4,3},{5,4},{6,5},{7,6},{8,7},{9,8},{10,9... | collective-permute-start | bytes 196616 | tf_op jit(solution)/shard_map/ppermute | solution.py:21
  247.6 20.7 %collective-permute-start.25 = (f32[16,1024]{1,0:T(8,128)}, f32[16,1024]{1,0:T(8,128)S(1)}, u32[]{:S(2)}, u32[]{:S(2)}) collective-permute-start(f32[16,1024]{1,0:T(8,128)} %shard_map.106.refs_2_), channel_id=1, source_target_pairs={{0,14},{1,15},{2,0},{3,1},{4,2},{5,3},{6,4},{7,5},{8,6},{9,7},{10,... | collective-permute-start | bytes 196616 | tf_op jit(solution)/shard_map/ppermute | solution.py:21
  251.9 16.4 %collective-permute-start.26 = (f32[16,1024]{1,0:T(8,128)}, f32[16,1024]{1,0:T(8,128)S(1)}, u32[]{:S(2)}, u32[]{:S(2)}) collective-permute-start(f32[16,1024]{1,0:T(8,128)} %shard_map.106.refs_2_), channel_id=1, source_target_pairs={{0,13},{1,14},{2,15},{3,0},{4,1},{5,2},{6,3},{7,4},{8,5},{9,6},{10... | collective-permute-start | bytes 196616 | tf_op jit(solution)/shard_map/ppermute | solution.py:21
  253.5 14.8 %collective-permute-start.27 = (f32[16,1024]{1,0:T(8,128)}, f32[16,1024]{1,0:T(8,128)S(1)}, u32[]{:S(2)}, u32[]{:S(2)}) collective-permute-start(f32[16,1024]{1,0:T(8,128)} %shard_map.106.refs_2_), channel_id=1, source_target_pairs={{0,12},{1,13},{2,14},{3,15},{4,0},{5,1},{6,2},{7,3},{8,4},{9,5},{1... | collective-permute-start | bytes 196616 | tf_op jit(solution)/shard_map/ppermute | solution.py:21
  (1 other events, 1.0 us)
